TPU v7x, 32 devices: a whole 2x2x4 slice. The times are simulated.
32 devices in a mesh: song: 4 (over y, x), seq: 8 (over z, core).
Axes of the slice: x: 2, y: 2, z: 4, core: 2. Of those that a mesh axis runs over, the one named last changes fastest.
Arguments:
- queries: bfloat16 [4, 1024, 2048], P('song', 'seq'), may hold values from -64 to 64
- keys: bfloat16 [4, 1024, 2048], P('song', 'seq'), may hold values from -64 to 64
- values: bfloat16 [4, 1024, 2048], P('song', 'seq'), may hold values from -6 to 6
- lyric_keys: bfloat16 [4, 384, 2048], P('song', 'seq'), may hold values from -64 to 64
- lyric_values: bfloat16 [4, 384, 2048], P('song', 'seq'), may hold values from -6 to 6
- q_gain: float32 [128], replicated, may hold values from 0.5 to 1.5
- k_gain: float32 [128], replicated, may hold values from 0.5 to 1.5
- cotangent: bfloat16 [4, 1024, 2048], P('song', 'seq'), may hold values from -12 to 12
- alignment: int32 [4, 8, 2], P('song', 'seq'), may hold values from -1 to 2, as said below
- lyric_len: int32 [4], P('song'), may hold values from 192 to 384
Outputs:
- attn_out: bfloat16 [4, 1024, 2048], P('song', 'seq')
- grad_queries: bfloat16 [4, 1024, 2048], P('song', 'seq')
- grad_keys: bfloat16 [4, 1024, 2048], P('song', 'seq')
- grad_values: bfloat16 [4, 1024, 2048], P('song', 'seq')
- grad_lyric_keys: bfloat16 [4, 384, 2048], P('song', 'seq')
- grad_lyric_values: bfloat16 [4, 384, 2048], P('song', 'seq')
- grad_q_gain: float32 [128], replicated
- grad_k_gain: float32 [128], replicated
Inputs may be any that keep to these rules, and one draw needn't show every extreme that they name: `alignment`: in each row the entries that are not -1 are distinct.
All inputs are finite; a program needn't handle non-finite values.
Results may differ from a plain program's by a relative error of at most 0.01.
Values may be sent and summed in bfloat16 or wider, within the bound.
No kernel may reach another device: no remote copies, remote signals or barrier semaphores. Data moves between devices by JAX's collectives and lax.ppermute only.
A program may use at most 128 MiB of HBM per device.

v0:
```python
import jax
import jax.numpy as jnp
from jax import lax
from jax.sharding import PartitionSpec as P

BLK = 128
WIN = 1
TILES = 2


NORM_EPS = 1e-06


def extended_2(block, sides, width):
    for axis, dim in sides:
        count = lax.axis_size(axis)
        forward = [(i, i + 1) for i in range(count - 1)]
        backward = [(target, source) for source, target in forward]
        low = lax.ppermute(
            lax.slice_in_dim(block, block.shape[dim] - width, None, axis=dim), axis, forward
        )
        high = lax.ppermute(lax.slice_in_dim(block, 0, width, axis=dim), axis, backward)
        block = jnp.concatenate([low, block, high], axis=dim)
    return block


def norm_heads(inputs, norm_gain):
    row_values = inputs.astype(jnp.float32).reshape(inputs.shape[0], -1, norm_gain.shape[0])
    inverse = lax.rsqrt(jnp.mean(row_values * row_values, axis=-1, keepdims=True) + NORM_EPS)
    return (row_values * inverse * norm_gain, inverse)


def norm_back(inputs, inverse, norm_gain, grad_out):
    row_values = inputs.astype(jnp.float32).reshape(grad_out.shape)
    scaled = grad_out * norm_gain
    grad_input = inverse * scaled - row_values * inverse * inverse * inverse * jnp.mean(
        scaled * row_values, axis=-1, keepdims=True
    )
    grad_gain = jnp.sum(grad_out * row_values * inverse, axis=(0, 1))
    return (grad_input.reshape(inputs.shape), grad_gain)


def block_pass(query_rows, key_rows, value_rows, keep_mask, grad_rows, score_scale):
    scores = (
        jnp.einsum("qhd,khd->hqk", query_rows, key_rows, preferred_element_type=jnp.float32)
        * score_scale
    )
    exp_scores = jnp.where(keep_mask[None, None, :], jnp.exp(scores), 0.0)
    totals = jnp.sum(exp_scores, axis=2)
    prob_full = exp_scores / totals[:, :, None]
    prob_low = prob_full.astype(jnp.bfloat16)
    block_output = jnp.einsum(
        "hqk,khd->qhd", prob_low, value_rows, preferred_element_type=jnp.float32
    ).astype(jnp.bfloat16)
    delta_rows = jnp.sum(grad_rows.astype(jnp.float32) * block_output.astype(jnp.float32), axis=2).T
    grad_prob = jnp.einsum(
        "qhd,khd->hqk", grad_rows, value_rows, preferred_element_type=jnp.float32
    )
    grad_score = (prob_full * (grad_prob - delta_rows[:, :, None])).astype(jnp.bfloat16)
    query_gradient = (
        jnp.einsum("hqk,khd->qhd", grad_score, key_rows, preferred_element_type=jnp.float32)
        * score_scale
    )
    grad_key = (
        jnp.einsum("hqk,qhd->khd", grad_score, query_rows, preferred_element_type=jnp.float32)
        * score_scale
    )
    value_gradient = jnp.einsum(
        "hqk,qhd->khd", prob_low, grad_rows, preferred_element_type=jnp.float32
    )
    return (block_output, query_gradient, grad_key, value_gradient, totals, delta_rows)


def body(
    queries, keys, values, lyric_keys, lyric_values, q_gain, k_gain, cotangent, alignment, lyric_len
):
    head_size = q_gain.shape[0]
    model_width = queries.shape[2]
    head_count = model_width // head_size
    frames = queries.shape[1]
    lyric_local = lyric_keys.shape[1]
    blocks = frames // BLK
    border_rows = WIN * BLK
    window_extent = (2 * WIN + 1) * BLK
    score_scale = head_size ** (-0.5)
    total_frames = frames * lax.axis_size("seq")
    first_frame = lax.axis_index("seq") * frames
    query_raw = queries[0]
    key_raw = keys[0]
    query_full, query_inv = norm_heads(query_raw, q_gain)
    key_full, key_inv = norm_heads(key_raw, k_gain)
    lyric_full, lyric_inv = norm_heads(lyric_keys[0], k_gain)
    query_norm = query_full.astype(jnp.bfloat16)
    key_norm = key_full.astype(jnp.bfloat16)
    lyric_norm = lyric_full.astype(jnp.bfloat16)
    lyric_key_all, lyric_val_all = (
        lax.all_gather(lyric_norm.reshape(lyric_local, model_width), "seq", axis=0, tiled=True),
        lax.all_gather(lyric_values[0], "seq", axis=0, tiled=True),
    )
    lyric_total = lyric_key_all.shape[0]
    lyric_key_all = lyric_key_all.reshape(lyric_total, head_count, head_size)
    lyric_val_all = lyric_val_all.reshape(lyric_total, head_count, head_size)
    stacked = jnp.stack([key_norm.reshape(frames, model_width), values[0]])
    extended = extended_2(stacked, (("seq", 1),), border_rows)
    ext_keys = extended[0].reshape(frames + 2 * border_rows, head_count, head_size)
    ext_vals = extended[1].reshape(frames + 2 * border_rows, head_count, head_size)
    grad_heads = cotangent[0].reshape(frames, head_count, head_size)
    length = lyric_len[0]

    def one_block(block_id):
        start_offset = block_id * BLK
        position = (
            first_frame + start_offset - border_rows + jnp.arange(window_extent, dtype=jnp.int32)
        )
        audio_mask = (position >= 0) & (position < total_frames)
        tile_ids = alignment[0, block_id]
        row_grid = (jnp.maximum(tile_ids, 0) * BLK)[:, None] + jnp.arange(BLK, dtype=jnp.int32)[
            None, :
        ]
        lyric_mask = ((tile_ids >= 0)[:, None] & (row_grid < length)).reshape(-1)
        row_index = row_grid.reshape(-1)
        all_keys = jnp.concatenate([ext_keys, jnp.take(lyric_key_all, row_index, axis=0)], axis=0)
        all_vals = jnp.concatenate([ext_vals, jnp.take(lyric_val_all, row_index, axis=0)], axis=0)
        keep_mask = jnp.concatenate([audio_mask, lyric_mask], axis=0)
        results = block_pass(query_norm, all_keys, all_vals, keep_mask, grad_heads, score_scale)
        return results + (row_index,)

    output_list, grad_qn, grad_key, value_gradient, totals, delta_rows, row_index = lax.map(
        one_block, jnp.arange(blocks, dtype=jnp.int32)
    )
    audio_cols = grad_key.shape[1] - TILES * BLK
    flat_rows = row_index.reshape(-1)
    lyric_grad_key = (
        jnp.zeros((lyric_total, head_count, head_size), jnp.float32)
        .at[flat_rows]
        .add(grad_key[:, audio_cols:].reshape(-1, head_count, head_size))
    )
    lyric_grad_val = (
        jnp.zeros((lyric_total, head_count, head_size), jnp.float32)
        .at[flat_rows]
        .add(value_gradient[:, audio_cols:].reshape(-1, head_count, head_size))
    )
    ext_grad_key = jnp.zeros((frames + 2 * border_rows, head_count, head_size), jnp.float32)
    ext_grad_val = jnp.zeros((frames + 2 * border_rows, head_count, head_size), jnp.float32)
    block_id = 0
    lower = block_id * BLK
    ext_grad_key = ext_grad_key.at[lower : lower + window_extent].add(
        grad_key[block_id, :window_extent]
    )
    ext_grad_val = ext_grad_val.at[lower : lower + window_extent].add(
        value_gradient[block_id, :window_extent]
    )
    own_grad_key = ext_grad_key[border_rows : border_rows + frames]
    own_grad_val = ext_grad_val[border_rows : border_rows + frames]
    rims = jnp.stack(
        [
            jnp.concatenate(
                [ext_grad_key[:border_rows], ext_grad_key[border_rows + frames :]], axis=0
            ).reshape(2 * border_rows, model_width),
            jnp.concatenate(
                [ext_grad_val[:border_rows], ext_grad_val[border_rows + frames :]], axis=0
            ).reshape(2 * border_rows, model_width),
        ]
    )
    received = extended_2(rims.astype(jnp.bfloat16), (("seq", 1),), border_rows).astype(rims.dtype)
    from_left = received[:, :border_rows].reshape(2, border_rows, head_count, head_size)
    from_right = received[:, 3 * border_rows :].reshape(2, border_rows, head_count, head_size)
    own_grad_key = (
        own_grad_key.at[:border_rows]
        .add(from_left[0])
        .at[frames - border_rows :]
        .add(from_right[0])
    )
    own_grad_val = (
        own_grad_val.at[:border_rows]
        .add(from_left[1])
        .at[frames - border_rows :]
        .add(from_right[1])
    )
    unnormed_query_gradient, query_gain_vector = norm_back(
        query_raw, query_inv, q_gain, grad_qn.reshape(frames, head_count, head_size)
    )
    unnormed_key_gradient, key_gain_vector = norm_back(key_raw, key_inv, k_gain, own_grad_key)
    summed_key, summed_val = (
        lax.psum_scatter(
            lyric_grad_key.reshape(lyric_total, model_width), "seq", scatter_dimension=0, tiled=True
        ),
        lax.psum_scatter(
            lyric_grad_val.reshape(lyric_total, model_width), "seq", scatter_dimension=0, tiled=True
        ),
    )
    unnormed_lyric_gradient, lyric_gain_vector = norm_back(
        lyric_keys[0], lyric_inv, k_gain, summed_key.reshape(lyric_local, head_count, head_size)
    )
    total_query_gain, total_key_gain = lax.psum(
        (query_gain_vector, key_gain_vector + lyric_gain_vector), ("song", "seq")
    )
    return (
        output_list.reshape(1, frames, model_width),
        unnormed_query_gradient.astype(jnp.bfloat16)[None],
        unnormed_key_gradient.astype(jnp.bfloat16)[None],
        own_grad_val.reshape(1, frames, model_width).astype(jnp.bfloat16),
        unnormed_lyric_gradient.astype(jnp.bfloat16)[None],
        summed_val.astype(jnp.bfloat16)[None],
        total_query_gain,
        total_key_gain,
    )


def solution(mesh):
    in_specs = (
        P("song", "seq", None),
        P("song", "seq", None),
        P("song", "seq", None),
        P("song", "seq", None),
        P("song", "seq", None),
        P(),
        P(),
        P("song", "seq", None),
        P("song", "seq", None),
        P("song"),
    )
    out_specs = (
        P("song", "seq", None),
        P("song", "seq", None),
        P("song", "seq", None),
        P("song", "seq", None),
        P("song", "seq", None),
        P("song", "seq", None),
        P(),
        P(),
    )
    return jax.shard_map(body, mesh=mesh, in_specs=in_specs, out_specs=out_specs, check_vma=False)
```

profile of v0, /device:TPU:0, one launch (start us, length us, event | category | flops | bytes accessed | tf_op | source)
XLA Modules:
  0.0 260.1 jit_solution(15222059618123675038)
XLA Ops:
  7.2 1.0 convert_bitcast_fusion
  9.1 0.7 broadcast_bitcast_fusion
  9.9 1.7 fusion.31
  11.7 0.7 all-gather.6.cloned.1.call-update
  13.1 1.1 multiply_reduce_fusion.2
  14.7 1.3 collective-permute-start.1
  16.0 4.0 %collective-permute-start = (bf16[2,128,2048]{1,2,0:T(8,128)(2,1)S(1)}, bf16[2,128,2048]{1,2,0:T(8,128)(2,1)}, u32[]{:S(2)}, u32[]{:S(2)}) collective-permute-start(bf16[2,128,2048]{1,2,0:T(8,128)(2,1)S(1)} %pad_maximum_fusion.9), channel_id=1, source_target_pairs={{0,1},{1,2},{2,3},{3,4},{4,5},{5,6},{6,7},{8,9},{9,10},{10,11},{11... | collective-permute-start | bytes 3145736 | tf_op jit(solution)/shard_map/ppermute | solution.py:19
  20.7 0.7 multiply_bitcast_fusion.1
  21.3 0.7 compare_bitcast_fusion
  22.0 0.6 compare_and_fusion
  23.1 1.0 copy.64
  24.1 1.2 copy.60
  25.4 1.3 pad_add_fusion
  26.7 1.3 pad_clamp_fusion
  28.1 0.7 iota_add_fusion.1
  28.8 0.6 compare_select_fusion
  29.4 0.6 add_rsqrt_fusion.1
  30.0 1.8 pad_maximum_fusion
  31.8 1.5 fusion.47
  33.2 1.7 copy.62
  34.9 8.9 %all-gather.4.cloned.1.call-done = bf16[384,2048]{1,0:T(8,128)(2,1)} async-done(((bf16[48,2048]{1,0:T(8,128)(2,1)}), bf16[384,2048]{1,0:T(8,128)(2,1)}) %all-gather.4.cloned.1.call-update) | async-done | bytes 1572880 | tf_op jit(solution)/shard_map/all_gather | solution.py:97
  43.8 1.8 copy.83
  45.7 26.3 %all-gather.6.cloned.1.call-done = bf16[1,384,2048]{2,1,0:T(8,128)(2,1)} async-done(((bf16[1,48,2048]{2,1,0:T(8,128)(2,1)}), bf16[1,384,2048]{2,1,0:T(8,128)(2,1)}) %all-gather.6.cloned.1.call-update) | async-done | bytes 1572880 | tf_op jit(solution)/shard_map/all_gather | solution.py:98
  72.0 3.0 %copy.80 = bf16[48,8,16,128]{3,2,1,0:T(8,128)(2,1)} copy(bf16[48,8,16,128]{3,1,2,0:T(8,128)(2,1)} %bitcast.213) | data formatting | bytes 3145728
  75.0 1.9 gather_fusion.1
  76.9 3.4 %gather_fusion = bf16[256,16,128]{2,1,0:T(8,128)(2,1)} fusion(bf16[384,16,128]{2,1,0:T(8,128)(2,1)} %bitcast.206, s32[1024]{0:T(1024)} %pad_clamp_fusion), kind=kCustom, calls=%fused_computation.clone | custom fusion | bytes 2098176 | tf_op jit(solution)/shard_map/while/body/eval_jaxpr/jit(_take)/gather | solution.py:123
  80.3 1.6 copy.59
  82.0 1.0 copy_select_fusion
  83.0 0.8 broadcast_select_fusion
  83.9 1.6 fusion.2
  85.5 2.5 multiply_reduce_fusion
  88.0 1.9 fusion
  89.9 2.4 fusion.52
  92.4 2.3 copy-done
  94.9 2.0 copy.69
  97.1 20.4 %scatter_fusion = f32[384,16,128]{2,1,0:T(8,128)S(1)} fusion(f32[384,16,128]{2,1,0:T(8,128)S(1)} %broadcast.403.clone, s32[256]{0:T(256)} %bitcast.222, f32[256,16,128]{2,1,0:T(8,128)} %copy.69), kind=kCustom, calls=%fused_computation.2 | custom fusion | flops 524288 | bytes 6292480 | tf_op jit(solution)/shard_map/scatter-add | solution.py:136
  117.4 3.2 %copy.100 = f32[48,8,16,128]{3,1,2,0:T(8,128)} copy(f32[48,8,16,128]{3,2,1,0:T(8,128)S(1)} %bitcast.181) | data formatting | bytes 6291456
  120.9 0.8 copy-done.24
  121.7 5.3 %fusion.51 = (bf16[1,640,16,128]{1,3,2,0:T(8,128)(2,1)}, f32[1,640,16,128]{1,3,2,0:T(8,128)S(1)}) fusion(bf16[128,16,128]{0,2,1:T(8,128)(2,1)S(1)} %bitcast.220, f32[16,128]{1,0:T(8,128)S(1)} %copy-done.40, f32[16,128,640]{2,1,0:T(8,128)} %copy-done.38, pred[640]{0:T(1024)(128)(4,1)S(1)} %copy-done.32), kind=kOutput, calls=%fused_computation.116 | convolution fusion | flops 342097920 | bytes 13640320 | tf_op jit(solution)/shard_map/while/body/eval_jaxpr/hqk,qhd->khd/dot_general | solution.py:68
  127.0 2.4 copy-done.15
  129.6 2.0 copy.70
  131.8 20.4 %scatter_fusion.1 = f32[384,16,128]{2,1,0:T(8,128)S(1)} fusion(f32[384,16,128]{2,1,0:T(8,128)S(1)} %broadcast.403.clone.1, s32[256]{0:T(256)} %bitcast.223, f32[256,16,128]{2,1,0:T(8,128)} %copy.70), kind=kCustom, calls=%fused_computation.3 | custom fusion | flops 524288 | bytes 6292480 | tf_op jit(solution)/shard_map/scatter-add | solution.py:141
  152.2 3.0 %copy.99 = f32[48,8,16,128]{3,1,2,0:T(8,128)} copy(f32[48,8,16,128]{3,2,1,0:T(8,128)S(1)} %bitcast.180) | data formatting | bytes 6291456
  155.2 1.3 fusion.49
  156.5 1.5 fusion.48
  158.3 1.7 fusion.50
  160.0 1.4 collective-permute-start.3
  161.5 4.0 %collective-permute-start.2 = (bf16[2,128,2048]{1,2,0:T(8,128)(2,1)}, bf16[2,128,2048]{1,2,0:T(8,128)(2,1)}, u32[]{:S(2)}, u32[]{:S(2)}) collective-permute-start(bf16[2,128,2048]{1,2,0:T(8,128)(2,1)} %get-tuple-element.215), channel_id=1, source_target_pairs={{0,1},{1,2},{2,3},{3,4},{4,5},{5,6},{6,7},{8,9},{9,10},{10,11},{11... | collective-permute-start | bytes 3145736 | tf_op jit(solution)/shard_map/ppermute | solution.py:19
  166.0 1.3 slice.221
  167.3 2.4 slice.228
  169.7 1.0 copy.71
  170.7 4.3 %fusion.18 = (f32[128]{0:T(128)}, f32[128,16]{0,1:T(8,128)S(1)}, f32[16,128,128]{2,1,0:T(8,128)S(1)}) fusion(f32[128,16,128]{0,2,1:T(8,128)S(1)} %bitcast.185, f32[128,16]{0,1:T(8,128)} %add_rsqrt_fusion.1, f32[128]{0:T(128)} %broadcast_multiply_fusion.3, bf16[16,128,640]{2,1,0:T(8,128)(2,1)} %copy-done.14, bf16[256,16,128]{2,0,1:T(8,128)(2,1)} %copy-done.19, ...), kind=kOutput, calls=%fused_computation.40 | convolution fusion | flops 342620032 | bytes 7357440 | tf_op jit(solution)/shard_map/while/body/eval_jaxpr/hqk,khd->qhd/dot_general | solution.py:61
  175.0 1.1 fusion.25
  176.1 2.0 copy.72
  178.2 2.4 fusion.14
  180.6 1.6 fusion.22
  182.2 1.2 fusion.12
  183.5 2.0 copy.73
  185.5 1.7 fusion.16
  187.3 1.0 copy.74
  188.3 1.1 copy.85
  189.8 2.0 fusion.33
  191.9 60.0 %all-reduce = (f32[128]{0:T(128)}, f32[128]{0:T(128)}) all-reduce(f32[128]{0:T(128)S(1)} %copy-done.37, f32[128]{0:T(128)S(1)} %add.202), channel_id=1, replica_groups=mesh['song'=4,'seq'=8] {'song','seq'}, use_global_device_ids=true, to_apply=%region_13.15 | all-reduce | flops 256 | bytes 2048 | tf_op jit(solution)/shard_map/psum | solution.py:195
  251.9 1.7 convert_bitcast_fusion.2
  (117 shorter events, 5.0 us)
Async XLA Ops:
  7.2 5.3 %copy-start.20 = (bf16[1,128,2048]{2,1,0:T(8,128)(2,1)S(1)}, bf16[1,128,2048]{2,1,0:T(8,128)(2,1)}, u32[]{:S(2)}) copy-start(bf16[1,128,2048]{2,1,0:T(8,128)(2,1)} %param.38) | copy-start | bytes 1572868
  7.2 5.6 %copy-start.21 = (bf16[1,128,2048]{2,1,0:T(8,128)(2,1)S(1)}, bf16[1,128,2048]{2,1,0:T(8,128)(2,1)}, u32[]{:S(2)}) copy-start(bf16[1,128,2048]{2,1,0:T(8,128)(2,1)} %param.37) | copy-start | bytes 1572868
  7.2 36.7 %all-gather.4.cloned.1.call-start = ((), (), s32[]{:S(2)}) async-start(), calls=%async_computation.2 | async-start | bytes 1769472 | tf_op jit(solution)/shard_map/all_gather | solution.py:97
  8.3 0.7 copy-start.12
  11.7 60.3 %all-gather.6.cloned.1.call-start = ((), (), s32[]{:S(2)}) async-start(), calls=%async_computation.5 | async-start | bytes 1769472 | tf_op jit(solution)/shard_map/all_gather | solution.py:98
  12.4 175.9 %reduce-scatter.3.cloned.1.call-start = ((), (), s32[]{:S(2)}) async-start(), calls=%async_computation.3 | async-start | bytes 3538944 | tf_op jit(solution)/shard_map/reduce_scatter | solution.py:185
  13.1 10.1 %copy-start.3 = (bf16[1,128,2048]{1,2,0:T(8,128)(2,1)}, bf16[1,128,2048]{1,2,0:T(8,128)(2,1)S(1)}, u32[]{:S(2)}) copy-start(bf16[1,128,2048]{1,2,0:T(8,128)(2,1)S(1)} %copy.57) | copy-start | bytes 1572868
  13.1 10.1 %copy-start.22 = (bf16[1,128,2048]{2,1,0:T(8,128)(2,1)S(1)}, bf16[1,128,2048]{2,1,0:T(8,128)(2,1)}, u32[]{:S(2)}) copy-start(bf16[1,128,2048]{2,1,0:T(8,128)(2,1)} %param.43) | copy-start | bytes 1572868
  14.7 15.3 %collective-permute-start.1 = (bf16[2,128,2048]{1,2,0:T(8,128)(2,1)S(1)}, bf16[2,128,2048]{1,2,0:T(8,128)(2,1)}, u32[]{:S(2)}, u32[]{:S(2)}) collective-permute-start(bf16[2,128,2048]{1,2,0:T(8,128)(2,1)S(1)} %pad_maximum_fusion.9), channel_id=1, source_target_pairs={{1,0},{2,1},{3,2},{4,3},{5,4},{6,5},{7,6},{9,8},{10,9},{11,10},{12... | collective-permute-start | bytes 3145736 | tf_op jit(solution)/shard_map/ppermute | solution.py:22
  16.0 14.0 %collective-permute-start = (bf16[2,128,2048]{1,2,0:T(8,128)(2,1)S(1)}, bf16[2,128,2048]{1,2,0:T(8,128)(2,1)}, u32[]{:S(2)}, u32[]{:S(2)}) collective-permute-start(bf16[2,128,2048]{1,2,0:T(8,128)(2,1)S(1)} %pad_maximum_fusion.9), channel_id=1, source_target_pairs={{0,1},{1,2},{2,3},{3,4},{4,5},{5,6},{6,7},{8,9},{9,10},{10,11},{11... | collective-permute-start | bytes 3145736 | tf_op jit(solution)/shard_map/ppermute | solution.py:19
  21.3 0.7 copy-start.35
  25.4 64.5 %copy-start.1 = (f32[1,128,2048]{1,2,0:T(8,128)}, f32[1,128,2048]{1,2,0:T(8,128)S(1)}, u32[]{:S(2)}) copy-start(f32[1,128,2048]{1,2,0:T(8,128)S(1)} %copy.60) | copy-start | bytes 3145732
  76.9 5.1 %copy-start.11 = (bf16[256,16,128]{2,1,0:T(8,128)(2,1)S(1)}, bf16[256,16,128]{2,1,0:T(8,128)(2,1)}, u32[]{:S(2)}) copy-start(bf16[256,16,128]{2,1,0:T(8,128)(2,1)} %gather_fusion.1) | copy-start | bytes 3145732
  81.9 1.9 copy-start.17
  81.9 1.9 copy-start.26
  81.9 1.9 copy-start.31
  81.9 1.9 copy-start.33
  83.0 2.4 copy-start.19
  83.8 1.6 copy-start.18
  83.8 1.6 copy-start.23
  85.4 2.5 copy-start.38
  85.5 2.5 copy-start.39
  89.9 2.4 copy-start.14
  92.4 2.3 copy-start
  120.6 1.0 copy-start.24
  120.6 1.0 copy-start.32
  120.6 1.0 copy-start.40
  120.7 131.2 %reduce-scatter.5.cloned.1.call-start = ((), (), s32[]{:S(2)}) async-start(), calls=%async_computation.4 | async-start | bytes 3538944 | tf_op jit(solution)/shard_map/reduce_scatter | solution.py:188
  127.0 2.4 copy-start.15
  156.5 1.8 copy-start.5
  158.0 2.0 copy-start.7
  158.1 2.0 copy-start.9
  158.3 7.2 %copy-start.34 = (f32[128]{0:T(128)S(1)}, f32[128]{0:T(128)}, u32[]{:S(2)}) copy-start(f32[128]{0:T(128)} %param.41) | copy-start | bytes 1540
  160.0 9.7 %copy-start.25 = (bf16[16,128,128]{2,1,0:T(8,128)(2,1)S(1)}, bf16[16,128,128]{2,1,0:T(8,128)(2,1)}, u32[]{:S(2)}) copy-start(bf16[16,128,128]{2,1,0:T(8,128)(2,1)} %get-tuple-element.223) | copy-start | bytes 1572868
  160.0 10.7 %copy-start.2 = (f32[1,128,2048]{1,2,0:T(8,128)S(1)}, f32[1,128,2048]{1,2,0:T(8,128)}, u32[]{:S(2)}) copy-start(f32[1,128,2048]{1,2,0:T(8,128)} %copy-done.1) | copy-start | bytes 3145732
  160.0 18.2 %collective-permute-start.3 = (bf16[2,128,2048]{1,2,0:T(8,128)(2,1)}, bf16[2,128,2048]{1,2,0:T(8,128)(2,1)}, u32[]{:S(2)}, u32[]{:S(2)}) collective-permute-start(bf16[2,128,2048]{1,2,0:T(8,128)(2,1)} %get-tuple-element.216), channel_id=1, source_target_pairs={{1,0},{2,1},{3,2},{4,3},{5,4},{6,5},{7,6},{9,8},{10,9},{11,10},{12... | collective-permute-start | bytes 3145736 | tf_op jit(solution)/shard_map/ppermute | solution.py:22
  161.5 16.7 %collective-permute-start.2 = (bf16[2,128,2048]{1,2,0:T(8,128)(2,1)}, bf16[2,128,2048]{1,2,0:T(8,128)(2,1)}, u32[]{:S(2)}, u32[]{:S(2)}) collective-permute-start(bf16[2,128,2048]{1,2,0:T(8,128)(2,1)} %get-tuple-element.215), channel_id=1, source_target_pairs={{0,1},{1,2},{2,3},{3,4},{4,5},{5,6},{6,7},{8,9},{9,10},{10,11},{11... | collective-permute-start | bytes 3145736 | tf_op jit(solution)/shard_map/ppermute | solution.py:19
  170.7 4.3 %copy-start.27 = (f32[128,16]{0,1:T(8,128)S(1)}, f32[128,16]{0,1:T(8,128)}, u32[]{:S(2)}) copy-start(f32[128,16]{0,1:T(8,128)} %add_rsqrt_fusion.1) | copy-start | bytes 24580
  170.7 4.3 %copy-start.36 = (f32[128]{0:T(128)S(1)}, f32[128]{0:T(128)}, u32[]{:S(2)}) copy-start(f32[128]{0:T(128)} %broadcast_multiply_fusion.3) | copy-start | bytes 1540
  175.0 3.2 %copy-start.4 = (bf16[1,128,2048]{1,2,0:T(8,128)(2,1)S(1)}, bf16[1,128,2048]{1,2,0:T(8,128)(2,1)}, u32[]{:S(2)}) copy-start(bf16[1,128,2048]{1,2,0:T(8,128)(2,1)} %copy-done.3) | copy-start | bytes 1572868
  178.2 2.4 copy-start.10
  178.2 2.4 copy-start.29
  182.2 3.3 %copy-start.6 = (bf16[1,128,16,128]{1,3,2,0:T(8,128)(2,1)S(1)}, bf16[1,128,16,128]{1,3,2,0:T(8,128)(2,1)}, u32[]{:S(2)}) copy-start(bf16[1,128,16,128]{1,3,2,0:T(8,128)(2,1)} %copy-done.5) | copy-start | bytes 1572868
  182.2 3.3 %copy-start.8 = (bf16[1,128,16,128]{1,3,2,0:T(8,128)(2,1)S(1)}, bf16[1,128,16,128]{1,3,2,0:T(8,128)(2,1)}, u32[]{:S(2)}) copy-start(bf16[1,128,16,128]{1,3,2,0:T(8,128)(2,1)} %copy-done.7) | copy-start | bytes 1572868
  185.5 3.9 %copy-start.30 = (f32[128]{0:T(128)S(1)}, f32[128]{0:T(128)}, u32[]{:S(2)}) copy-start(f32[128]{0:T(128)} %param.42) | copy-start | bytes 1540
  185.5 3.9 %copy-start.13 = (f32[6,8,16,128]{3,2,1,0:T(8,128)S(1)}, f32[6,8,16,128]{3,2,1,0:T(8,128)}, u32[]{:S(2)}) copy-start(f32[6,8,16,128]{3,2,1,0:T(8,128)} %copy-done.12) | copy-start | bytes 1179652
  187.3 2.5 copy-start.16
  187.3 4.6 %copy-start.28 = (f32[2048]{0:T(1024)S(1)}, f32[2048]{0:T(1024)}, u32[]{:S(2)}) copy-start(f32[2048]{0:T(1024)} %get-tuple-element.202) | copy-start | bytes 24580
  187.3 4.6 %copy-start.37 = (f32[128]{0:T(128)S(1)}, f32[128]{0:T(128)}, u32[]{:S(2)}) copy-start(f32[128]{0:T(128)} %get-tuple-element.198) | copy-start | bytes 1540
Sparse Core Ops, SparseCore 0:
  11.8 31.9 all-gather.3
  45.5 26.4 all-gather.5
  120.8 39.8 reduce-scatter.2
  162.8 47.3 reduce-scatter.4
where the time goes:
time: 262 us; the launch traced here: 260 us
  other arithmetic  68.8 us (26%)
  blocking collectives  60 us (23%)
  local copies, waits for them, and re-layouts  51.2 us (20%)
  waiting for transfers between devices  36 us (14%)
  matrix products  18 us (7%)
  between operations  15 us (6%)
  starting transfers between devices  11.1 us (4%)
    psum x1, blocking collectives, body(): lax.psum((query_gain_vector, key_gain_vector + lyric_gain_vector), ('song...  60 us
    all_gather x1, waiting for transfers between devices, body(): lax.all_gather(lyric_values[0], 'seq', axis=0, tiled=True)  26.3 us
    unnamed x95, local copies, waits for them, and re-layouts  26 us
    scatter-add x1, other arithmetic, body(): lyric_grad_val = jnp.zeros((lyric_total, head_count, head_size), jnp.floa...  20.4 us
    scatter-add x1, other arithmetic, body(): lyric_grad_key = jnp.zeros((lyric_total, head_count, head_size), jnp.floa...  20.4 us
    all_gather x1, waiting for transfers between devices, body(): lax.all_gather(lyric_norm.reshape(lyric_local, model_width), 'seq', axis=...  8.94 us
    ppermute x2, starting transfers between devices, extended_2(): lax.ppermute(lax.slice_in_dim(block, block.shape[dim] - width, None, axis...  8.06 us
    dot_general x1, matrix products, block_pass(): jnp.einsum('hqk,qhd->khd', prob_low, grad_rows, preferred_element_type=jn...  5.35 us
  transfers between devices with their start and end apart: 8, of which 2 were waited for; matrix products, arithmetic and copies ran while one was open for 31% of the time, Pallas kernels for 0%

commit v1 on v0

v1 whole, which is shorter than its diff:
```python
import functools

import jax
import jax.numpy as jnp
from jax import lax
from jax.experimental import pallas as pl
from jax.experimental.pallas import tpu as pltpu
from jax.sharding import PartitionSpec as P

BLK = 128
TILES = 2
NORM_EPS = 1e-06
HEADS_PER_STEP = 2
VMEM_LIMIT = 48 * 1024 * 1024


def dot(lhs, rhs, lhs_dim, rhs_dim):
    return lax.dot_general(
        lhs, rhs, (((lhs_dim,), (rhs_dim,)), ((), ())), preferred_element_type=jnp.float32
    )


def attention_kernel(
    piece_rows, head_size, score_scale, meta_ref, gain_ref, query_ref, grad_ref, key_ref,
    value_ref, left_ref, right_ref, *refs
):
    pieces = len(piece_rows)
    piece_refs = refs[:pieces]
    out_ref, grad_query_ref, own_key_ref, own_value_ref, to_left_ref, to_right_ref = refs[
        pieces : pieces + 6
    ]
    lyric_refs = refs[pieces + 6 : 2 * pieces + 6]
    gain_grad_ref, mask_ref = refs[2 * pieces + 6 :]
    frames = query_ref.shape[0]

    @pl.when(pl.program_id(0) == 0)
    def _():
        gain_grad_ref[...] = jnp.zeros_like(gain_grad_ref)
        mask_ref[0:frames, :] = jnp.full((frames, frames), meta_ref[3], jnp.int32).astype(
            jnp.float32
        )
        mask_ref[frames : 2 * frames, :] = jnp.ones((frames, frames), jnp.float32)
        mask_ref[2 * frames : 3 * frames, :] = jnp.full(
            (frames, frames), meta_ref[4], jnp.int32
        ).astype(jnp.float32)
        start = 3 * frames
        for index, rows in enumerate(piece_rows):
            row = lax.broadcasted_iota(jnp.int32, (rows, frames), 0) + meta_ref[5 + index]
            keep = jnp.zeros((rows, frames), jnp.float32)
            for slot in range(TILES):
                tile = meta_ref[slot]
                lower = tile * BLK
                upper = jnp.minimum(lower + BLK, meta_ref[2])
                inside = (row >= lower) & (row < upper) & (lower >= 0)
                keep = jnp.where(inside, 1.0, keep)
            mask_ref[start : start + rows, :] = keep
            start += rows

    q_gain = gain_ref[0:1, :]
    k_gain = gain_ref[1:2, :]
    for head in range(query_ref.shape[1] // head_size):
        cols = slice(head * head_size, (head + 1) * head_size)
        query = query_ref[:, cols].astype(jnp.float32)
        cot = grad_ref[:, cols]
        raw_keys = jnp.concatenate(
            [left_ref[0:frames, cols], key_ref[:, cols], right_ref[0:frames, cols]]
            + [ref[0:rows, cols] for ref, rows in zip(piece_refs, piece_rows)],
            axis=0,
        ).astype(jnp.float32)
        value = jnp.concatenate(
            [left_ref[frames:, cols], value_ref[:, cols], right_ref[frames:, cols]]
            + [ref[rows:, cols] for ref, rows in zip(piece_refs, piece_rows)],
            axis=0,
        )
        query_inv = lax.rsqrt(jnp.mean(query * query, axis=1, keepdims=True) + NORM_EPS)
        key_inv = lax.rsqrt(jnp.mean(raw_keys * raw_keys, axis=1, keepdims=True) + NORM_EPS)
        query_hat = query * query_inv
        query_low = (query_hat * (q_gain * score_scale)).astype(jnp.bfloat16)
        key_hat = raw_keys * key_inv
        key_low = (key_hat * k_gain).astype(jnp.bfloat16)
        scores = dot(key_low, query_low, 1, 1)
        grad_prob = dot(value, cot, 1, 1)
        exp_scores = jnp.exp(scores) * mask_ref[...]
        prob = exp_scores * (1.0 / jnp.sum(exp_scores, axis=0, keepdims=True))
        prob_low = prob.astype(jnp.bfloat16)
        weighted = prob * grad_prob
        delta = jnp.sum(weighted, axis=0, keepdims=True)
        grad_score = (weighted - prob * delta).astype(jnp.bfloat16)
        out_ref[:, cols] = dot(prob_low, value, 0, 0).astype(jnp.bfloat16)
        grad_qn = dot(grad_score, key_low, 0, 0) * score_scale
        grad_keys = dot(grad_score, query_low, 1, 0)
        grad_values = dot(prob_low, cot, 1, 0)
        scaled = grad_qn * q_gain
        grad_query_ref[:, cols] = (
            query_inv * scaled
            - query_hat
            * (query_inv * query_inv)
            * jnp.mean(scaled * query, axis=1, keepdims=True)
        ).astype(jnp.bfloat16)
        gain_grad_ref[0:1, :] += jnp.sum(grad_qn * query_hat, axis=0, keepdims=True)
        gain_grad_ref[1:2, :] += jnp.sum(grad_keys * key_hat, axis=0, keepdims=True)
        own = slice(frames, 2 * frames)
        own_key_ref[:, cols] = grad_keys[own]
        own_value_ref[:, cols] = grad_values[own]
        for ref, rows in ((to_left_ref, slice(0, frames)), (to_right_ref, slice(2 * frames, 3 * frames))):
            ref[0:frames, cols] = grad_keys[rows].astype(jnp.bfloat16)
            ref[frames:, cols] = grad_values[rows].astype(jnp.bfloat16)
        start = 3 * frames
        for ref, rows in zip(lyric_refs, piece_rows):
            ref[0:rows, cols] = grad_keys[start : start + rows].astype(jnp.bfloat16)
            ref[rows:, cols] = grad_values[start : start + rows].astype(jnp.bfloat16)
            start += rows


def attention(meta, gains, query, cot, key, value, left, right, lyric_pieces):
    frames, width = query.shape
    head_size = gains.shape[1]
    step = HEADS_PER_STEP * head_size
    piece_rows = tuple(piece.shape[0] // 2 for piece in lyric_pieces)
    key_rows = 3 * frames + sum(piece_rows)

    def columns(rows):
        return pl.BlockSpec((rows, step), lambda i: (0, i))

    def rows_out(rows, dtype):
        return jax.ShapeDtypeStruct((rows, width), dtype)

    bf16, f32 = jnp.bfloat16, jnp.float32
    out_shape = (
        [rows_out(frames, bf16)] * 2
        + [rows_out(frames, f32)] * 2
        + [rows_out(2 * frames, bf16)] * 2
        + [rows_out(2 * rows, bf16) for rows in piece_rows]
        + [jax.ShapeDtypeStruct((8, head_size), f32)]
    )
    return pl.pallas_call(
        functools.partial(attention_kernel, piece_rows, head_size, head_size ** (-0.5)),
        grid=(width // step,),
        in_specs=[
            pl.BlockSpec(memory_space=pltpu.SMEM),
            pl.BlockSpec(gains.shape, lambda i: (0, 0)),
        ]
        + [columns(frames)] * 4
        + [columns(2 * frames)] * 2
        + [columns(2 * rows) for rows in piece_rows],
        out_specs=[columns(frames)] * 4
        + [columns(2 * frames)] * 2
        + [columns(2 * rows) for rows in piece_rows]
        + [pl.BlockSpec((8, head_size), lambda i: (0, 0))],
        out_shape=out_shape,
        scratch_shapes=[pltpu.VMEM((key_rows, frames), f32)],
        compiler_params=pltpu.CompilerParams(
            dimension_semantics=("arbitrary",), vmem_limit_bytes=VMEM_LIMIT
        ),
        cost_estimate=pl.CostEstimate(
            flops=12 * key_rows * frames * width,
            bytes_accessed=16 * 1024 * 1024,
            transcendentals=key_rows * frames * (width // head_size),
        ),
        name="attention",
    )(meta, gains, query, cot, key, value, left, right, *lyric_pieces)


def finish_kernel(terms, head_size, gain_ref, raw_ref, *refs):
    rows = raw_ref.shape[0]
    key_parts, value_parts = refs[:terms], refs[terms : 2 * terms]
    grad_key_ref, grad_value_ref = refs[2 * terms :]
    k_gain = gain_ref[1:2, :]
    total = value_parts[0][...].astype(jnp.float32)
    for part in value_parts[1:]:
        total = total + part[...].astype(jnp.float32)
    grad_value_ref[...] = total.astype(jnp.bfloat16)
    for head in range(raw_ref.shape[1] // head_size):
        cols = slice(head * head_size, (head + 1) * head_size)
        raw = raw_ref[:, cols].astype(jnp.float32)
        inverse = lax.rsqrt(jnp.mean(raw * raw, axis=1, keepdims=True) + NORM_EPS)
        grad = key_parts[0][:, cols].astype(jnp.float32)
        for part in key_parts[1:]:
            grad = grad + part[:, cols].astype(jnp.float32)
        scaled = grad * k_gain
        grad_key_ref[:, cols] = (
            inverse * scaled
            - raw
            * (inverse * inverse * inverse)
            * jnp.mean(scaled * raw, axis=1, keepdims=True)
        ).astype(jnp.bfloat16)


def finish(gains, raw, key_parts, value_parts, name):
    rows, width = raw.shape
    head_size = gains.shape[1]
    step = min(width, 4 * head_size)

    def columns(block):
        return pl.BlockSpec((rows, step), lambda i: (block, i))

    parts = list(key_parts) + list(value_parts)
    return pl.pallas_call(
        functools.partial(finish_kernel, len(key_parts), head_size),
        grid=(width // step,),
        in_specs=[pl.BlockSpec(gains.shape, lambda i: (0, 0)), columns(0)]
        + [columns(block) for _, block in parts],
        out_specs=[columns(0)] * 2,
        out_shape=[jax.ShapeDtypeStruct((rows, width), jnp.bfloat16)] * 2,
        compiler_params=pltpu.CompilerParams(
            dimension_semantics=("arbitrary",), vmem_limit_bytes=VMEM_LIMIT
        ),
        cost_estimate=pl.CostEstimate(
            flops=20 * rows * width,
            bytes_accessed=2 * rows * width * (3 + len(parts)),
            transcendentals=rows * (width // head_size),
        ),
        name=name,
    )(gains, raw, *[array for array, _ in parts])


def add_kernel(*refs):
    half = len(refs) // 3
    for first, second, total in zip(refs[:half], refs[half : 2 * half], refs[2 * half :]):
        total[...] = (
            first[...].astype(jnp.float32) + second[...].astype(jnp.float32)
        ).astype(total.dtype)


def add_pieces(first, second):
    rows, width = first[0].shape
    step = width // 4
    spec = pl.BlockSpec((rows, step), lambda i: (0, i))
    count = len(first)
    return pl.pallas_call(
        add_kernel,
        grid=(width // step,),
        in_specs=[spec] * (2 * count),
        out_specs=[spec] * count,
        out_shape=[jax.ShapeDtypeStruct((rows, width), jnp.bfloat16)] * count,
        compiler_params=pltpu.CompilerParams(
            dimension_semantics=("arbitrary",), vmem_limit_bytes=VMEM_LIMIT
        ),
        cost_estimate=pl.CostEstimate(
            flops=count * rows * width,
            bytes_accessed=6 * count * rows * width,
            transcendentals=0,
        ),
        name="add_pieces",
    )(*first, *second)


def sum_over(total, axis):
    count = lax.axis_size(axis)
    if count & (count - 1):
        return lax.psum(total, axis)
    bit = 1
    while bit < count:
        total = total + lax.ppermute(total, axis, [(i, i ^ bit) for i in range(count)])
        bit *= 2
    return total


def shift_chips(block, count, chips):
    return lax.ppermute(block, "seq", [(i, (i + 2 * chips) % count) for i in range(count)])


def swap_cores(block, count):
    return lax.ppermute(block, "seq", [(i, i ^ 1) for i in range(count)])


def body(
    queries, keys, values, lyric_keys, lyric_values, q_gain, k_gain, cotangent, alignment, lyric_len
):
    frames = queries.shape[1]
    lyric_local = lyric_keys.shape[1]
    count = lax.axis_size("seq")
    me = lax.axis_index("seq")
    forward = [(i, i + 1) for i in range(count - 1)]
    backward = [(i + 1, i) for i in range(count - 1)]
    gains = jnp.stack([q_gain, k_gain])

    paired = count % 2 == 0 and count <= 8 and lyric_local % 16 == 0
    own_lyric = jnp.concatenate([lyric_keys[0], lyric_values[0]], axis=0)
    own_window = jnp.concatenate([keys[0], values[0]], axis=0)
    left = lax.ppermute(own_window, "seq", forward)
    right = lax.ppermute(own_window, "seq", backward)
    if paired:
        chips = count // 2
        same = [own_lyric] + [shift_chips(own_lyric, count, -j) for j in range(1, chips)]
        other = [swap_cores(piece, count) for piece in same]
        pieces = same + other
        owners = [(me + 2 * j) % count for j in range(chips)]
        owners = owners + [owner ^ 1 for owner in owners]
        first_rows = [owner * lyric_local for owner in owners]
    else:
        pieces = [
            jnp.concatenate(
                [
                    lax.all_gather(lyric_keys[0], "seq", axis=0, tiled=True),
                    lax.all_gather(lyric_values[0], "seq", axis=0, tiled=True),
                ],
                axis=0,
            )
        ]
        first_rows = [jnp.int32(0)]
    meta = jnp.stack(
        [alignment[0, 0, slot] for slot in range(TILES)]
        + [lyric_len[0], (me > 0).astype(jnp.int32), (me < count - 1).astype(jnp.int32)]
        + [row.astype(jnp.int32) for row in first_rows]
    )
    results = attention(
        meta, gains, queries[0], cotangent[0], keys[0], values[0], left, right, pieces
    )
    output, grad_queries, own_key, own_value, to_left, to_right = results[:6]
    lyric_parts, gain_part = results[6:-1], results[-1]

    if paired:
        from_other = [swap_cores(part, count) for part in lyric_parts[chips:]]
        sums = add_pieces(lyric_parts[:chips], from_other)
        arrived = [sums[0]] + [shift_chips(sums[j], count, j) for j in range(1, chips)]
        lyric_key_parts = [(part, 0) for part in arrived]
        lyric_value_parts = [(part, 1) for part in arrived]
    else:
        total_rows = lyric_local * count
        scattered = [
            lax.psum_scatter(
                half.astype(jnp.float32), "seq", scatter_dimension=0, tiled=True
            )
            for half in (lyric_parts[0][:total_rows], lyric_parts[0][total_rows:])
        ]
        lyric_key_parts = [(scattered[0], 0)]
        lyric_value_parts = [(scattered[1], 0)]
    from_right = lax.ppermute(to_left, "seq", backward)
    from_left = lax.ppermute(to_right, "seq", forward)
    gain_total = sum_over(sum_over(gain_part, "seq"), "song")
    grad_keys, grad_values = finish(
        gains,
        keys[0],
        [(own_key, 0), (from_left, 0), (from_right, 0)],
        [(own_value, 0), (from_left, 1), (from_right, 1)],
        "finish_audio",
    )
    grad_lyric_keys, grad_lyric_values = finish(
        gains, lyric_keys[0], lyric_key_parts, lyric_value_parts, "finish_lyric"
    )
    return (
        output[None],
        grad_queries[None],
        grad_keys[None],
        grad_values[None],
        grad_lyric_keys[None],
        grad_lyric_values[None],
        gain_total[0],
        gain_total[1],
    )


def solution(mesh):
    split = P("song", "seq", None)
    return jax.shard_map(
        body,
        mesh=mesh,
        in_specs=(split, split, split, split, split, P(), P(), split, split, P("song")),
        out_specs=(split, split, split, split, split, split, P(), P()),
        check_vma=False,
    )
```

time: 262 us -> 148 us (0.56)
  the two profiles are of different devices: /device:TPU:0 before, /device:TPU:12 now
where the time goes in v1:
time: 148 us
  starting transfers between devices  63.3 us (43%)
  waiting for transfers between devices  56 us (38%)
  Pallas kernels  20.2 us (14%)
  other arithmetic  3.29 us (2%)
  local copies, waits for them, and re-layouts  3.24 us (2%)
  between operations  1.5 us (1%)
    ppermute x6, waiting for transfers between devices, shift_chips(): lax.ppermute(block, 'seq', [(i, (i + 2 * chips) % count) for i in range(c...  39.1 us
    ppermute x8, starting transfers between devices, swap_cores(): return lax.ppermute(block, 'seq', [(i, i ^ 1) for i in range(count)])  36.5 us
    ppermute x5, waiting for transfers between devices, sum_over(): lax.ppermute(total, axis, [(i, i ^ bit) for i in range(count)])  15.6 us
    pallas_call x1, Pallas kernels, attention(): pl.pallas_call(functools.partial(attention_kernel, piece_rows, head_size,...  15.1 us
    ppermute x6, starting transfers between devices, shift_chips(): lax.ppermute(block, 'seq', [(i, (i + 2 * chips) % count) for i in range(c...  11.1 us
    ppermute x5, starting transfers between devices, sum_over(): lax.ppermute(total, axis, [(i, i ^ bit) for i in range(count)])  5.87 us
    pallas_call x2, Pallas kernels, finish(): pl.pallas_call(functools.partial(finish_kernel, len(key_parts), head_size...  4.24 us
    ppermute x1, starting transfers between devices, body(): from_right = lax.ppermute(to_left, 'seq', backward)  3.63 us
  transfers between devices with their start and end apart: 23, of which 10 were waited for; matrix products, arithmetic and copies ran while one was open for 3% of the time, Pallas kernels for 2%

profile of v1, /device:TPU:12, one launch (start us, length us, event | category | flops | bytes accessed | tf_op | source)
XLA Modules:
  0.0 147.6 jit_solution(12627677493691742902)
XLA Ops:
  0.6 0.0 copy-start
  0.6 1.1 pad_maximum_fusion.1.refs_0_
  1.8 0.1 collective-permute-start.5
  1.8 0.0 copy-done
  1.9 2.2 %pad_maximum_fusion = bf16[256,2048]{1,0:T(8,128)(2,1)} fusion(bf16[128,2048]{1,0:T(8,128)(2,1)} %bitcast.35, bf16[128,2048]{1,0:T(8,128)(2,1)S(1)} %bitcast.31), kind=kLoop, calls=%fused_computation | loop fusion | flops 2097152 | bytes 2097152 | tf_op jit(solution)/shard_map/concatenate | solution.py:280
  4.0 2.4 %collective-permute-start.1 = (bf16[256,2048]{1,0:T(8,128)(2,1)}, bf16[256,2048]{1,0:T(8,128)(2,1)}, u32[]{:S(2)}, u32[]{:S(2)}) collective-permute-start(bf16[256,2048]{1,0:T(8,128)(2,1)} %pad_maximum_fusion), channel_id=1, source_target_pairs={{1,0},{2,1},{3,2},{4,3},{5,4},{6,5},{7,6},{9,8},{10,9},{11,10},{12... | collective-permute-start | bytes 3145736 | tf_op jit(solution)/shard_map/ppermute | solution.py:282
  6.5 1.9 %collective-permute-start = (bf16[256,2048]{1,0:T(8,128)(2,1)}, bf16[256,2048]{1,0:T(8,128)(2,1)}, u32[]{:S(2)}, u32[]{:S(2)}) collective-permute-start(bf16[256,2048]{1,0:T(8,128)(2,1)} %pad_maximum_fusion), channel_id=1, source_target_pairs={{0,1},{1,2},{2,3},{3,4},{4,5},{5,6},{6,7},{8,9},{9,10},{10,11},{11... | collective-permute-start | bytes 3145736 | tf_op jit(solution)/shard_map/ppermute | solution.py:281
  8.4 1.6 %collective-permute-start.4 = (bf16[96,2048]{1,0:T(8,128)(2,1)S(1)}, bf16[96,2048]{1,0:T(8,128)(2,1)S(1)}, u32[]{:S(2)}, u32[]{:S(2)}) collective-permute-start(bf16[96,2048]{1,0:T(8,128)(2,1)S(1)} %pad_maximum_fusion.1.refs_0_), channel_id=1, source_target_pairs={{0,2},{1,3},{2,4},{3,5},{4,6},{5,7},{6,0},{7,1},{8,10},{9,11},{10,... | collective-permute-start | bytes 1179656 | tf_op jit(solution)/shard_map/ppermute | solution.py:260
  10.0 2.1 %collective-permute-start.3 = (bf16[96,2048]{1,0:T(8,128)(2,1)S(1)}, bf16[96,2048]{1,0:T(8,128)(2,1)S(1)}, u32[]{:S(2)}, u32[]{:S(2)}) collective-permute-start(bf16[96,2048]{1,0:T(8,128)(2,1)S(1)} %pad_maximum_fusion.1.refs_0_), channel_id=1, source_target_pairs={{0,4},{1,5},{2,6},{3,7},{4,0},{5,1},{6,2},{7,3},{8,12},{9,13},{10,... | collective-permute-start | bytes 1179656 | tf_op jit(solution)/shard_map/ppermute | solution.py:260
  12.2 0.0 collective-permute-done.5.refs_4_
  12.2 1.8 %collective-permute-start.2 = (bf16[96,2048]{1,0:T(8,128)(2,1)S(1)}, bf16[96,2048]{1,0:T(8,128)(2,1)S(1)}, u32[]{:S(2)}, u32[]{:S(2)}) collective-permute-start(bf16[96,2048]{1,0:T(8,128)(2,1)S(1)} %pad_maximum_fusion.1.refs_0_), channel_id=1, source_target_pairs={{0,6},{1,7},{2,0},{3,1},{4,2},{5,3},{6,4},{7,5},{8,14},{9,15},{10,... | collective-permute-start | bytes 1179656 | tf_op jit(solution)/shard_map/ppermute | solution.py:260
  14.0 6.4 %collective-permute-done.4.refs_3_ = bf16[96,2048]{1,0:T(8,128)(2,1)S(1)} collective-permute-done((bf16[96,2048]{1,0:T(8,128)(2,1)S(1)}, bf16[96,2048]{1,0:T(8,128)(2,1)S(1)}, u32[]{:S(2)}, u32[]{:S(2)}) %collective-permute-start.4) | collective-permute-done | bytes 393248 | tf_op jit(solution)/shard_map/ppermute | solution.py:260
  20.4 31.1 %collective-permute-start.8 = (bf16[96,2048]{1,0:T(8,128)(2,1)S(1)}, bf16[96,2048]{1,0:T(8,128)(2,1)S(1)}, u32[]{:S(2)}, u32[]{:S(2)}) collective-permute-start(bf16[96,2048]{1,0:T(8,128)(2,1)S(1)} %collective-permute-done.4.refs_3_), channel_id=1, source_target_pairs={{0,1},{1,0},{2,3},{3,2},{4,5},{5,4},{6,7},{7,6},{8,9},{9,8},{10,11... | collective-permute-start | bytes 1179656 | tf_op jit(solution)/shard_map/ppermute | solution.py:264
  51.5 0.0 collective-permute-done.3.refs_2_
  51.5 4.2 %collective-permute-start.7 = (bf16[96,2048]{1,0:T(8,128)(2,1)S(1)}, bf16[96,2048]{1,0:T(8,128)(2,1)S(1)}, u32[]{:S(2)}, u32[]{:S(2)}) collective-permute-start(bf16[96,2048]{1,0:T(8,128)(2,1)S(1)} %collective-permute-done.3.refs_2_), channel_id=1, source_target_pairs={{0,1},{1,0},{2,3},{3,2},{4,5},{5,4},{6,7},{7,6},{8,9},{9,8},{10,11... | collective-permute-start | bytes 1179656 | tf_op jit(solution)/shard_map/ppermute | solution.py:264
  55.7 0.0 collective-permute-done.2.refs_1_
  55.7 0.0 collective-permute-start.6
  56.4 0.0 copy-done.5
  56.4 0.6 fusion
  57.0 1.4 stack.60.meta_ref
  58.4 0.0 collective-permute-done.8.refs_7_
  58.4 0.0 copy-start.8
  58.4 0.0 collective-permute-done.7.refs_6_
  58.4 0.0 collective-permute-done.6.refs_5_
  58.4 0.0 collective-permute-done.1.right_ref
  58.4 0.0 collective-permute-done.left_ref
  58.4 0.7 copy-done.8
  59.1 15.1 %attention.1 = (bf16[128,2048]{1,0:T(8,128)(2,1)}, bf16[128,2048]{1,0:T(8,128)(2,1)}, f32[128,2048]{1,0:T(8,128)}, f32[128,2048]{1,0:T(8,128)}, bf16[256,2048]{1...) custom-call(s32[13]{0:T(128)S(1)} %stack.60.meta_ref, ...), custom_call_target="tpu_custom_call" | custom-call | flops 2415919104 | bytes 16777216 | tf_op jit(solution)/shard_map/attention/pallas_call | solution.py:136
  74.3 0.6 collective-permute-start.11
  74.9 1.9 %collective-permute-start.9 = (bf16[256,2048]{1,0:T(8,128)(2,1)}, bf16[256,2048]{1,0:T(8,128)(2,1)S(1)}, u32[]{:S(2)}, u32[]{:S(2)}) collective-permute-start(bf16[256,2048]{1,0:T(8,128)(2,1)} %get-tuple-element.34), channel_id=1, source_target_pairs={{0,1},{1,2},{2,3},{3,4},{4,5},{5,6},{6,7},{8,9},{9,10},{10,11},{11... | collective-permute-start | bytes 3145736 | tf_op jit(solution)/shard_map/ppermute | solution.py:330
  76.8 3.6 %collective-permute-start.10 = (bf16[256,2048]{1,0:T(8,128)(2,1)}, bf16[256,2048]{1,0:T(8,128)(2,1)S(1)}, u32[]{:S(2)}, u32[]{:S(2)}) collective-permute-start(bf16[256,2048]{1,0:T(8,128)(2,1)} %get-tuple-element.35), channel_id=1, source_target_pairs={{1,0},{2,1},{3,2},{4,3},{5,4},{6,5},{7,6},{9,8},{10,9},{11,10},{12... | collective-permute-start | bytes 3145736 | tf_op jit(solution)/shard_map/ppermute | solution.py:329
  80.4 0.1 collective-permute-start.18
  80.5 1.2 collective-permute-done.18
  81.7 0.8 collective-permute-start.19
  82.4 10.7 %collective-permute-done.19 = f32[8,128]{1,0:T(8,128)S(1)} collective-permute-done((f32[8,128]{1,0:T(8,128)S(1)}, f32[8,128]{1,0:T(8,128)S(1)}, u32[]{:S(2)}, u32[]{:S(2)}) %collective-permute-start.19) | collective-permute-done | bytes 4128 | tf_op jit(solution)/shard_map/ppermute | solution.py:254
  93.2 3.1 %collective-permute-start.20 = (f32[8,128]{1,0:T(8,128)S(1)}, f32[8,128]{1,0:T(8,128)S(1)}, u32[]{:S(2)}, u32[]{:S(2)}) collective-permute-start(f32[8,128]{1,0:T(8,128)S(1)} %add.45), channel_id=1, source_target_pairs={{0,4},{1,5},{2,6},{3,7},{4,0},{5,1},{6,2},{7,3},{8,12},{9,13},{10,... | collective-permute-start | bytes 12296 | tf_op jit(solution)/shard_map/ppermute | solution.py:254
  96.2 1.6 %collective-permute-done.20 = f32[8,128]{1,0:T(8,128)S(1)} collective-permute-done((f32[8,128]{1,0:T(8,128)S(1)}, f32[8,128]{1,0:T(8,128)S(1)}, u32[]{:S(2)}, u32[]{:S(2)}) %collective-permute-start.20) | collective-permute-done | bytes 4128 | tf_op jit(solution)/shard_map/ppermute | solution.py:254
  97.8 1.5 %collective-permute-start.21 = (f32[8,128]{1,0:T(8,128)S(1)}, f32[8,128]{1,0:T(8,128)S(1)}, u32[]{:S(2)}, u32[]{:S(2)}) collective-permute-start(f32[8,128]{1,0:T(8,128)S(1)} %add.46), channel_id=1, source_target_pairs={{0,8},{8,0},{16,24},{24,16},{1,9},{9,1},{17,25},{25,17},{2,10},{10... | collective-permute-start | bytes 12296 | tf_op jit(solution)/shard_map/ppermute | solution.py:254
  99.3 0.0 collective-permute-start.12
  99.3 2.1 %collective-permute-done.21 = f32[8,128]{1,0:T(8,128)S(1)} collective-permute-done((f32[8,128]{1,0:T(8,128)S(1)}, f32[8,128]{1,0:T(8,128)S(1)}, u32[]{:S(2)}, u32[]{:S(2)}) %collective-permute-start.21) | collective-permute-done | bytes 4128 | tf_op jit(solution)/shard_map/ppermute | solution.py:254
  101.4 0.0 collective-permute-start.13
  101.4 0.0 collective-permute-done.11.refs_4_
  101.4 0.5 collective-permute-start.14
  101.9 0.0 collective-permute-done.12.refs_5_
  101.9 0.5 collective-permute-start.22
  102.4 0.7 collective-permute-done.13.refs_6_
  103.1 0.6 collective-permute-done.14.refs_7_
  103.7 0.8 add_pieces.1
  104.5 3.9 %collective-permute-start.15 = (bf16[96,2048]{1,0:T(8,128)(2,1)S(1)}, bf16[96,2048]{1,0:T(8,128)(2,1)S(1)}, u32[]{:S(2)}, u32[]{:S(2)}) collective-permute-start(bf16[96,2048]{1,0:T(8,128)(2,1)S(1)} %get-tuple-element.48), channel_id=1, source_target_pairs={{0,2},{1,3},{2,4},{3,5},{4,6},{5,7},{6,0},{7,1},{8,10},{9,11},{10,... | collective-permute-start | bytes 1179656 | tf_op jit(solution)/shard_map/ppermute | solution.py:260
  108.4 0.9 collective-permute-start.16
  109.4 0.0 collective-permute-done.22
  109.4 0.6 collective-permute-start.17
  110.0 0.5 slice_bitcast_fusion
  110.5 24.3 %collective-permute-done.15.refs_1_.refs_5_ = bf16[96,2048]{1,0:T(8,128)(2,1)S(1)} collective-permute-done((bf16[96,2048]{1,0:T(8,128)(2,1)S(1)}, bf16[96,2048]{1,0:T(8,128)(2,1)S(1)}, u32[]{:S(2)}, u32[]{:S(2)}) %collective-permute-start.15) | collective-permute-done | bytes 393248 | tf_op jit(solution)/shard_map/ppermute | solution.py:260
  134.8 7.6 %collective-permute-done.16.refs_2_.refs_6_ = bf16[96,2048]{1,0:T(8,128)(2,1)S(1)} collective-permute-done((bf16[96,2048]{1,0:T(8,128)(2,1)S(1)}, bf16[96,2048]{1,0:T(8,128)(2,1)S(1)}, u32[]{:S(2)}, u32[]{:S(2)}) %collective-permute-start.16) | collective-permute-done | bytes 393248 | tf_op jit(solution)/shard_map/ppermute | solution.py:260
  142.4 0.9 collective-permute-done.17.refs_3_.refs_7_
  143.3 0.0 copy-done.4
  143.3 1.8 %finish_lyric.1 = (bf16[48,2048]{1,0:T(8,128)(2,1)}, bf16[48,2048]{1,0:T(8,128)(2,1)}) custom-call(f32[2,128]{1,0:T(2,128)S(1)} %pad_maximum_fusion.2.gain_ref, bf16[48,2048]{1,0:T(8,128)(2,1)S(1)} %bitcast.34, bf16[96,2048]{1,0:T(8,128)(2,1)S(1)} %get-tuple-element.47.refs_0_.refs_4_, bf16[96,2048]{1,0:T(8,128)(2,1)S(1)} %collective-permute-done.15.refs_1_.refs_5_, ...), custom_call_target="tpu_custom_call" | custom-call | flops 1966080 | bytes 2162688 | tf_op jit(solution)/shard_map/finish_lyric/pallas_call | solution.py:198
  145.1 0.0 collective-permute-done.9.refs_1_.refs_4_
  145.1 0.0 collective-permute-done.10.refs_2_.refs_5_
  145.1 0.0 copy-done.1
  145.1 0.0 copy-done.2
  145.1 0.0 copy-done.3
  145.2 2.4 %finish_audio.1 = (bf16[128,2048]{1,0:T(8,128)(2,1)}, bf16[128,2048]{1,0:T(8,128)(2,1)}) custom-call(f32[2,128]{1,0:T(2,128)S(1)} %pad_maximum_fusion.2.gain_ref, bf16[128,2048]{1,0:T(8,128)(2,1)S(1)} %bitcast.32, f32[128,2048]{1,0:T(8,128)S(1)} %copy-done.2, bf16[256,2048]{1,0:T(8,128)(2,1)S(1)} %collective-permute-done.9.refs_1_.refs_4_, ...), custom_call_target="tpu_custom_call" | custom-call | flops 5242880 | bytes 4718592 | tf_op jit(solution)/shard_map/finish_audio/pallas_call | solution.py:198
  (15 shorter events, 0.0 us)
Async XLA Ops:
  0.6 1.2 copy-start
  1.8 10.4 %collective-permute-start.5 = (bf16[96,2048]{1,0:T(8,128)(2,1)S(1)}, bf16[96,2048]{1,0:T(8,128)(2,1)S(1)}, u32[]{:S(2)}, u32[]{:S(2)}) collective-permute-start(bf16[96,2048]{1,0:T(8,128)(2,1)S(1)} %pad_maximum_fusion.1.refs_0_), channel_id=1, source_target_pairs={{0,1},{1,0},{2,3},{3,2},{4,5},{5,4},{6,7},{7,6},{8,9},{9,8},{10,11... | collective-permute-start | bytes 1179656 | tf_op jit(solution)/shard_map/ppermute | solution.py:264
  1.9 54.5 %copy-start.5 = (s32[1,1,2]{2,1,0:T(1,128)S(1)}, s32[1,1,2]{2,1,0:T(1,128)}, u32[]{:S(2)}) copy-start(s32[1,1,2]{2,1,0:T(1,128)} %param.18) | copy-start | bytes 28
  1.9 56.5 %copy-start.6 = (f32[128]{0:T(128)S(1)}, f32[128]{0:T(128)}, u32[]{:S(2)}) copy-start(f32[128]{0:T(128)} %param.16) | copy-start | bytes 1540
  1.9 56.5 %copy-start.7 = (f32[128]{0:T(128)S(1)}, f32[128]{0:T(128)}, u32[]{:S(2)}) copy-start(f32[128]{0:T(128)} %param.15) | copy-start | bytes 1540
  4.0 54.4 %collective-permute-start.1 = (bf16[256,2048]{1,0:T(8,128)(2,1)}, bf16[256,2048]{1,0:T(8,128)(2,1)}, u32[]{:S(2)}, u32[]{:S(2)}) collective-permute-start(bf16[256,2048]{1,0:T(8,128)(2,1)} %pad_maximum_fusion), channel_id=1, source_target_pairs={{1,0},{2,1},{3,2},{4,3},{5,4},{6,5},{7,6},{9,8},{10,9},{11,10},{12... | collective-permute-start | bytes 3145736 | tf_op jit(solution)/shard_map/ppermute | solution.py:282
  6.5 52.0 %collective-permute-start = (bf16[256,2048]{1,0:T(8,128)(2,1)}, bf16[256,2048]{1,0:T(8,128)(2,1)}, u32[]{:S(2)}, u32[]{:S(2)}) collective-permute-start(bf16[256,2048]{1,0:T(8,128)(2,1)} %pad_maximum_fusion), channel_id=1, source_target_pairs={{0,1},{1,2},{2,3},{3,4},{4,5},{5,6},{6,7},{8,9},{9,10},{10,11},{11... | collective-permute-start | bytes 3145736 | tf_op jit(solution)/shard_map/ppermute | solution.py:281
  8.4 12.0 %collective-permute-start.4 = (bf16[96,2048]{1,0:T(8,128)(2,1)S(1)}, bf16[96,2048]{1,0:T(8,128)(2,1)S(1)}, u32[]{:S(2)}, u32[]{:S(2)}) collective-permute-start(bf16[96,2048]{1,0:T(8,128)(2,1)S(1)} %pad_maximum_fusion.1.refs_0_), channel_id=1, source_target_pairs={{0,2},{1,3},{2,4},{3,5},{4,6},{5,7},{6,0},{7,1},{8,10},{9,11},{10,... | collective-permute-start | bytes 1179656 | tf_op jit(solution)/shard_map/ppermute | solution.py:260
  10.0 41.5 %collective-permute-start.3 = (bf16[96,2048]{1,0:T(8,128)(2,1)S(1)}, bf16[96,2048]{1,0:T(8,128)(2,1)S(1)}, u32[]{:S(2)}, u32[]{:S(2)}) collective-permute-start(bf16[96,2048]{1,0:T(8,128)(2,1)S(1)} %pad_maximum_fusion.1.refs_0_), channel_id=1, source_target_pairs={{0,4},{1,5},{2,6},{3,7},{4,0},{5,1},{6,2},{7,3},{8,12},{9,13},{10,... | collective-permute-start | bytes 1179656 | tf_op jit(solution)/shard_map/ppermute | solution.py:260
  12.2 43.6 %collective-permute-start.2 = (bf16[96,2048]{1,0:T(8,128)(2,1)S(1)}, bf16[96,2048]{1,0:T(8,128)(2,1)S(1)}, u32[]{:S(2)}, u32[]{:S(2)}) collective-permute-start(bf16[96,2048]{1,0:T(8,128)(2,1)S(1)} %pad_maximum_fusion.1.refs_0_), channel_id=1, source_target_pairs={{0,6},{1,7},{2,0},{3,1},{4,2},{5,3},{6,4},{7,5},{8,14},{9,15},{10,... | collective-permute-start | bytes 1179656 | tf_op jit(solution)/shard_map/ppermute | solution.py:260
  20.4 38.0 %collective-permute-start.8 = (bf16[96,2048]{1,0:T(8,128)(2,1)S(1)}, bf16[96,2048]{1,0:T(8,128)(2,1)S(1)}, u32[]{:S(2)}, u32[]{:S(2)}) collective-permute-start(bf16[96,2048]{1,0:T(8,128)(2,1)S(1)} %collective-permute-done.4.refs_3_), channel_id=1, source_target_pairs={{0,1},{1,0},{2,3},{3,2},{4,5},{5,4},{6,7},{7,6},{8,9},{9,8},{10,11... | collective-permute-start | bytes 1179656 | tf_op jit(solution)/shard_map/ppermute | solution.py:264
  51.5 6.9 %collective-permute-start.7 = (bf16[96,2048]{1,0:T(8,128)(2,1)S(1)}, bf16[96,2048]{1,0:T(8,128)(2,1)S(1)}, u32[]{:S(2)}, u32[]{:S(2)}) collective-permute-start(bf16[96,2048]{1,0:T(8,128)(2,1)S(1)} %collective-permute-done.3.refs_2_), channel_id=1, source_target_pairs={{0,1},{1,0},{2,3},{3,2},{4,5},{5,4},{6,7},{7,6},{8,9},{9,8},{10,11... | collective-permute-start | bytes 1179656 | tf_op jit(solution)/shard_map/ppermute | solution.py:264
  55.7 2.7 %collective-permute-start.6 = (bf16[96,2048]{1,0:T(8,128)(2,1)S(1)}, bf16[96,2048]{1,0:T(8,128)(2,1)S(1)}, u32[]{:S(2)}, u32[]{:S(2)}) collective-permute-start(bf16[96,2048]{1,0:T(8,128)(2,1)S(1)} %collective-permute-done.2.refs_1_), channel_id=1, source_target_pairs={{0,1},{1,0},{2,3},{3,2},{4,5},{5,4},{6,7},{7,6},{8,9},{9,8},{10,11... | collective-permute-start | bytes 1179656 | tf_op jit(solution)/shard_map/ppermute | solution.py:264
  58.4 0.7 copy-start.8
  74.3 27.1 %collective-permute-start.11 = (bf16[96,2048]{1,0:T(8,128)(2,1)S(1)}, bf16[96,2048]{1,0:T(8,128)(2,1)S(1)}, u32[]{:S(2)}, u32[]{:S(2)}) collective-permute-start(bf16[96,2048]{1,0:T(8,128)(2,1)S(1)} %get-tuple-element.43), channel_id=1, source_target_pairs={{0,1},{1,0},{2,3},{3,2},{4,5},{5,4},{6,7},{7,6},{8,9},{9,8},{10,11... | collective-permute-start | bytes 1179656 | tf_op jit(solution)/shard_map/ppermute | solution.py:264
  74.9 70.3 %collective-permute-start.9 = (bf16[256,2048]{1,0:T(8,128)(2,1)}, bf16[256,2048]{1,0:T(8,128)(2,1)S(1)}, u32[]{:S(2)}, u32[]{:S(2)}) collective-permute-start(bf16[256,2048]{1,0:T(8,128)(2,1)} %get-tuple-element.34), channel_id=1, source_target_pairs={{0,1},{1,2},{2,3},{3,4},{4,5},{5,6},{6,7},{8,9},{9,10},{10,11},{11... | collective-permute-start | bytes 3145736 | tf_op jit(solution)/shard_map/ppermute | solution.py:330
  76.8 68.3 %collective-permute-start.10 = (bf16[256,2048]{1,0:T(8,128)(2,1)}, bf16[256,2048]{1,0:T(8,128)(2,1)S(1)}, u32[]{:S(2)}, u32[]{:S(2)}) collective-permute-start(bf16[256,2048]{1,0:T(8,128)(2,1)} %get-tuple-element.35), channel_id=1, source_target_pairs={{1,0},{2,1},{3,2},{4,3},{5,4},{6,5},{7,6},{9,8},{10,9},{11,10},{12... | collective-permute-start | bytes 3145736 | tf_op jit(solution)/shard_map/ppermute | solution.py:329
  80.4 1.2 collective-permute-start.18
  81.7 11.5 %collective-permute-start.19 = (f32[8,128]{1,0:T(8,128)S(1)}, f32[8,128]{1,0:T(8,128)S(1)}, u32[]{:S(2)}, u32[]{:S(2)}) collective-permute-start(f32[8,128]{1,0:T(8,128)S(1)} %add.44), channel_id=1, source_target_pairs={{0,2},{1,3},{2,0},{3,1},{4,6},{5,7},{6,4},{7,5},{8,10},{9,11},{10,... | collective-permute-start | bytes 12296 | tf_op jit(solution)/shard_map/ppermute | solution.py:254
  93.2 4.6 %collective-permute-start.20 = (f32[8,128]{1,0:T(8,128)S(1)}, f32[8,128]{1,0:T(8,128)S(1)}, u32[]{:S(2)}, u32[]{:S(2)}) collective-permute-start(f32[8,128]{1,0:T(8,128)S(1)} %add.45), channel_id=1, source_target_pairs={{0,4},{1,5},{2,6},{3,7},{4,0},{5,1},{6,2},{7,3},{8,12},{9,13},{10,... | collective-permute-start | bytes 12296 | tf_op jit(solution)/shard_map/ppermute | solution.py:254
  97.8 3.6 %collective-permute-start.21 = (f32[8,128]{1,0:T(8,128)S(1)}, f32[8,128]{1,0:T(8,128)S(1)}, u32[]{:S(2)}, u32[]{:S(2)}) collective-permute-start(f32[8,128]{1,0:T(8,128)S(1)} %add.46), channel_id=1, source_target_pairs={{0,8},{8,0},{16,24},{24,16},{1,9},{9,1},{17,25},{25,17},{2,10},{10... | collective-permute-start | bytes 12296 | tf_op jit(solution)/shard_map/ppermute | solution.py:254
  99.3 2.6 %collective-permute-start.12 = (bf16[96,2048]{1,0:T(8,128)(2,1)S(1)}, bf16[96,2048]{1,0:T(8,128)(2,1)S(1)}, u32[]{:S(2)}, u32[]{:S(2)}) collective-permute-start(bf16[96,2048]{1,0:T(8,128)(2,1)S(1)} %get-tuple-element.44), channel_id=1, source_target_pairs={{0,1},{1,0},{2,3},{3,2},{4,5},{5,4},{6,7},{7,6},{8,9},{9,8},{10,11... | collective-permute-start | bytes 1179656 | tf_op jit(solution)/shard_map/ppermute | solution.py:264
  101.4 1.7 %collective-permute-start.13 = (bf16[96,2048]{1,0:T(8,128)(2,1)S(1)}, bf16[96,2048]{1,0:T(8,128)(2,1)S(1)}, u32[]{:S(2)}, u32[]{:S(2)}) collective-permute-start(bf16[96,2048]{1,0:T(8,128)(2,1)S(1)} %get-tuple-element.45), channel_id=1, source_target_pairs={{0,1},{1,0},{2,3},{3,2},{4,5},{5,4},{6,7},{7,6},{8,9},{9,8},{10,11... | collective-permute-start | bytes 1179656 | tf_op jit(solution)/shard_map/ppermute | solution.py:264
  101.4 2.3 %collective-permute-start.14 = (bf16[96,2048]{1,0:T(8,128)(2,1)S(1)}, bf16[96,2048]{1,0:T(8,128)(2,1)S(1)}, u32[]{:S(2)}, u32[]{:S(2)}) collective-permute-start(bf16[96,2048]{1,0:T(8,128)(2,1)S(1)} %get-tuple-element.46), channel_id=1, source_target_pairs={{0,1},{1,0},{2,3},{3,2},{4,5},{5,4},{6,7},{7,6},{8,9},{9,8},{10,11... | collective-permute-start | bytes 1179656 | tf_op jit(solution)/shard_map/ppermute | solution.py:264
  101.9 7.4 %collective-permute-start.22 = (f32[8,128]{1,0:T(8,128)S(1)}, f32[8,128]{1,0:T(8,128)S(1)}, u32[]{:S(2)}, u32[]{:S(2)}) collective-permute-start(f32[8,128]{1,0:T(8,128)S(1)} %add.47), channel_id=1, source_target_pairs={{0,16},{8,24},{16,0},{24,8},{1,17},{9,25},{17,1},{25,9},{2,18},{10... | collective-permute-start | bytes 12296 | tf_op jit(solution)/shard_map/ppermute | solution.py:254
  103.7 39.6 %copy-start.4 = (bf16[1,48,2048]{2,1,0:T(8,128)(2,1)S(1)}, bf16[1,48,2048]{2,1,0:T(8,128)(2,1)}, u32[]{:S(2)}) copy-start(bf16[1,48,2048]{2,1,0:T(8,128)(2,1)} %param.13) | copy-start | bytes 589828
  104.5 30.3 %collective-permute-start.15 = (bf16[96,2048]{1,0:T(8,128)(2,1)S(1)}, bf16[96,2048]{1,0:T(8,128)(2,1)S(1)}, u32[]{:S(2)}, u32[]{:S(2)}) collective-permute-start(bf16[96,2048]{1,0:T(8,128)(2,1)S(1)} %get-tuple-element.48), channel_id=1, source_target_pairs={{0,2},{1,3},{2,4},{3,5},{4,6},{5,7},{6,0},{7,1},{8,10},{9,11},{10,... | collective-permute-start | bytes 1179656 | tf_op jit(solution)/shard_map/ppermute | solution.py:260
  108.4 34.0 %collective-permute-start.16 = (bf16[96,2048]{1,0:T(8,128)(2,1)S(1)}, bf16[96,2048]{1,0:T(8,128)(2,1)S(1)}, u32[]{:S(2)}, u32[]{:S(2)}) collective-permute-start(bf16[96,2048]{1,0:T(8,128)(2,1)S(1)} %get-tuple-element.49), channel_id=1, source_target_pairs={{0,4},{1,5},{2,6},{3,7},{4,0},{5,1},{6,2},{7,3},{8,12},{9,13},{10,... | collective-permute-start | bytes 1179656 | tf_op jit(solution)/shard_map/ppermute | solution.py:260
  109.4 33.9 %collective-permute-start.17 = (bf16[96,2048]{1,0:T(8,128)(2,1)S(1)}, bf16[96,2048]{1,0:T(8,128)(2,1)S(1)}, u32[]{:S(2)}, u32[]{:S(2)}) collective-permute-start(bf16[96,2048]{1,0:T(8,128)(2,1)S(1)} %get-tuple-element.50), channel_id=1, source_target_pairs={{0,6},{1,7},{2,0},{3,1},{4,2},{5,3},{6,4},{7,5},{8,14},{9,15},{10,... | collective-permute-start | bytes 1179656 | tf_op jit(solution)/shard_map/ppermute | solution.py:260
  143.3 1.9 %copy-start.1 = (bf16[1,128,2048]{2,1,0:T(8,128)(2,1)S(1)}, bf16[1,128,2048]{2,1,0:T(8,128)(2,1)}, u32[]{:S(2)}) copy-start(bf16[1,128,2048]{2,1,0:T(8,128)(2,1)} %param.11) | copy-start | bytes 1572868
  143.3 1.9 %copy-start.2 = (f32[128,2048]{1,0:T(8,128)S(1)}, f32[128,2048]{1,0:T(8,128)}, u32[]{:S(2)}) copy-start(f32[128,2048]{1,0:T(8,128)} %get-tuple-element.33.refs_0_) | copy-start | bytes 3145732
  143.3 1.9 %copy-start.3 = (f32[128,2048]{1,0:T(8,128)S(1)}, f32[128,2048]{1,0:T(8,128)}, u32[]{:S(2)}) copy-start(f32[128,2048]{1,0:T(8,128)} %get-tuple-element.36.refs_3_) | copy-start | bytes 3145732

commit v2 on v1

v2 whole, which is shorter than its diff:
```python
import functools

import jax
import jax.numpy as jnp
from jax import lax
from jax.experimental import pallas as pl
from jax.experimental.pallas import tpu as pltpu
from jax.sharding import PartitionSpec as P

BLK = 128
TILES = 2
NORM_EPS = 1e-06
HEADS_PER_STEP = 1
VMEM_LIMIT = 32 * 1024 * 1024


def dot(lhs, rhs, lhs_dim, rhs_dim):
    return lax.dot_general(
        lhs, rhs, (((lhs_dim,), (rhs_dim,)), ((), ())), preferred_element_type=jnp.float32
    )


def params():
    return pltpu.CompilerParams(
        dimension_semantics=("arbitrary",), vmem_limit_bytes=VMEM_LIMIT
    )


def pack_kernel(
    core_ref, query, cot, key_other, value_other, key_own, value_own, lkey_other, lvalue_other,
    lkey_own, lvalue_own, mate_ref, near_ref, far_ref, lyric_ref,
):
    frames, lyric = query.shape[0], lkey_own.shape[0]
    start = 0
    for ref in (query, cot, key_other, value_other, lkey_other, lvalue_other):
        mate_ref[start : start + ref.shape[0], :] = ref[...]
        start += ref.shape[0]
    near_ref[0:frames, :] = key_other[...]
    near_ref[frames:, :] = value_other[...]
    far_ref[0:frames, :] = key_own[...]
    far_ref[frames:, :] = value_own[...]
    lyric_ref[0:lyric, :] = lkey_own[...]
    lyric_ref[lyric:, :] = lvalue_own[...]


def pack(core, query, cot, key, value, lyric_key, lyric_value):
    frames, width = query.shape
    lyric = lyric_key.shape[0]
    half = width // 2
    step = half // 4

    def other(rows):
        return pl.BlockSpec((rows, step), lambda i, core: (0, (1 - core[0]) * 4 + i))

    def own(rows):
        return pl.BlockSpec((rows, step), lambda i, core: (0, core[0] * 4 + i))

    out_rows = (4 * frames + 2 * lyric, 2 * frames, 2 * frames, 2 * lyric)
    return pl.pallas_call(
        pack_kernel,
        grid_spec=pltpu.PrefetchScalarGridSpec(
            num_scalar_prefetch=1,
            grid=(4,),
            in_specs=[other(frames)] * 4
            + [own(frames)] * 2
            + [other(lyric)] * 2
            + [own(lyric)] * 2,
            out_specs=[pl.BlockSpec((rows, step), lambda i, core: (0, i)) for rows in out_rows],
        ),
        out_shape=[jax.ShapeDtypeStruct((rows, half), jnp.bfloat16) for rows in out_rows],
        compiler_params=params(),
        cost_estimate=pl.CostEstimate(flops=0, bytes_accessed=5 * 1024 * 1024, transcendentals=0),
        name="pack",
    )(core, query, cot, key, value, key, value, lyric_key, lyric_value, lyric_key, lyric_value)


def attention_kernel(
    groups, head_size, score_scale, meta_ref, gain_ref, query_ref, grad_ref, key_ref, value_ref,
    mate_ref, near_ref, far_ref, *refs
):
    frames = query_ref.shape[0]
    arrays = len(groups)
    lyric_in = refs[:arrays]
    out_ref, grad_query_ref, own_key_ref, own_value_ref, to_mate_ref, to_near_ref, to_far_ref = (
        refs[arrays : arrays + 7]
    )
    lyric_out = refs[arrays + 7 : 2 * arrays + 7]
    gain_grad_ref, mask_ref = refs[2 * arrays + 7 :]
    runs = [(index, run) for index, group in enumerate(groups) for run in group]
    main = 2 * frames + sum(run[2] for _, run in runs)
    lanes = 2 * frames

    @pl.when(pl.program_id(0) == 0)
    def _():
        gain_grad_ref[...] = jnp.zeros_like(gain_grad_ref)
        start = 0
        for number, (_, (_, _, rows)) in enumerate(runs):
            row = lax.broadcasted_iota(jnp.int32, (rows, lanes), 0) + meta_ref[8 + number]
            lane = lax.broadcasted_iota(jnp.int32, (rows, lanes), 1)
            keep = jnp.zeros((rows, lanes), jnp.float32)
            for slot in range(TILES):
                lower = jnp.where(lane < frames, meta_ref[1 + slot], meta_ref[3 + slot]) * BLK
                upper = jnp.minimum(lower + BLK, meta_ref[5])
                inside = (row >= lower) & (row < upper) & (lower >= 0)
                keep = jnp.where(inside, 1.0, keep)
            mask_ref[start : start + rows, :] = keep
            start += rows
        lane = lax.broadcasted_iota(jnp.int32, (frames, lanes), 1)
        mask_ref[start : start + frames, :] = jnp.where(
            lane < frames, meta_ref[6], meta_ref[7]
        ).astype(jnp.float32)

    q_gain = gain_ref[0:1, :]
    k_gain = gain_ref[1:2, :]
    for head in range(query_ref.shape[1] // head_size):
        cols = slice(head * head_size, (head + 1) * head_size)
        query = jnp.concatenate([query_ref[:, cols], mate_ref[0:frames, cols]], axis=0)
        query = query.astype(jnp.float32)
        cot = jnp.concatenate([grad_ref[:, cols], mate_ref[frames : 2 * frames, cols]], axis=0)
        raw_keys = jnp.concatenate(
            [key_ref[:, cols], mate_ref[2 * frames : 3 * frames, cols]]
            + [lyric_in[index][run[0] : run[0] + run[2], cols] for index, run in runs]
            + [near_ref[0:frames, cols], far_ref[0:frames, cols]],
            axis=0,
        ).astype(jnp.float32)
        value = jnp.concatenate(
            [value_ref[:, cols], mate_ref[3 * frames : 4 * frames, cols]]
            + [lyric_in[index][run[1] : run[1] + run[2], cols] for index, run in runs]
            + [near_ref[frames:, cols], far_ref[frames:, cols]],
            axis=0,
        )
        query_inv = lax.rsqrt(jnp.mean(query * query, axis=1, keepdims=True) + NORM_EPS)
        key_inv = lax.rsqrt(jnp.mean(raw_keys * raw_keys, axis=1, keepdims=True) + NORM_EPS)
        query_hat = query * query_inv
        query_low = (query_hat * (q_gain * score_scale)).astype(jnp.bfloat16)
        key_hat = raw_keys * key_inv
        key_low = (key_hat * k_gain).astype(jnp.bfloat16)

        near, far = slice(main, main + frames), slice(main + frames, main + 2 * frames)

        def against(rows, columns):
            return jnp.concatenate(
                [
                    dot(rows[:main], columns, 1, 1),
                    jnp.concatenate(
                        [
                            dot(rows[near], columns[:frames], 1, 1),
                            dot(rows[far], columns[frames:], 1, 1),
                        ],
                        axis=1,
                    ),
                ],
                axis=0,
            )

        def over_keys(weights, rows):
            return dot(weights[:main], rows[:main], 0, 0) + jnp.concatenate(
                [
                    dot(weights[main:, :frames], rows[near], 0, 0),
                    dot(weights[main:, frames:], rows[far], 0, 0),
                ],
                axis=0,
            )

        def over_queries(weights, columns):
            return jnp.concatenate(
                [
                    dot(weights[:main], columns, 1, 0),
                    dot(weights[main:, :frames], columns[:frames], 1, 0),
                    dot(weights[main:, frames:], columns[frames:], 1, 0),
                ],
                axis=0,
            )

        exp_scores = jnp.exp(against(key_low, query_low))
        exp_scores = jnp.concatenate(
            [exp_scores[: 2 * frames], exp_scores[2 * frames :] * mask_ref[...]], axis=0
        )
        grad_prob = against(value, cot)
        prob = exp_scores * (1.0 / jnp.sum(exp_scores, axis=0, keepdims=True))
        prob_low = prob.astype(jnp.bfloat16)
        weighted = prob * grad_prob
        delta = jnp.sum(weighted, axis=0, keepdims=True)
        grad_score = (weighted - prob * delta).astype(jnp.bfloat16)
        output = over_keys(prob_low, value).astype(jnp.bfloat16)
        grad_qn = over_keys(grad_score, key_low) * score_scale
        grad_keys = over_queries(grad_score, query_low)
        grad_values = over_queries(prob_low, cot)
        scaled = grad_qn * q_gain
        grad_query = (
            query_inv * scaled
            - query_hat
            * (query_inv * query_inv)
            * jnp.mean(scaled * query, axis=1, keepdims=True)
        ).astype(jnp.bfloat16)
        gain_grad_ref[0:1, :] += jnp.sum(grad_qn * query_hat, axis=0, keepdims=True)
        gain_grad_ref[1:2, :] += jnp.sum(grad_keys * key_hat, axis=0, keepdims=True)

        out_ref[:, cols] = output[:frames]
        grad_query_ref[:, cols] = grad_query[:frames]
        own_key_ref[:, cols] = grad_keys[:frames]
        own_value_ref[:, cols] = grad_values[:frames]
        to_mate_ref[0:frames, cols] = output[frames:]
        to_mate_ref[frames : 2 * frames, cols] = grad_query[frames:]
        mate = slice(frames, 2 * frames)
        to_mate_ref[2 * frames : 3 * frames, cols] = grad_keys[mate].astype(jnp.bfloat16)
        to_mate_ref[3 * frames :, cols] = grad_values[mate].astype(jnp.bfloat16)
        for ref, rows in ((to_near_ref, near), (to_far_ref, far)):
            ref[0:frames, cols] = grad_keys[rows].astype(jnp.bfloat16)
            ref[frames:, cols] = grad_values[rows].astype(jnp.bfloat16)
        start = 2 * frames
        for index, (key_row, value_row, rows) in runs:
            part = slice(start, start + rows)
            lyric_out[index][key_row : key_row + rows, cols] = grad_keys[part].astype(jnp.bfloat16)
            lyric_out[index][value_row : value_row + rows, cols] = grad_values[part].astype(
                jnp.bfloat16
            )
            start += rows


def attention(meta, gains, query, cot, key, value, mate, near, far, lyrics, groups):
    frames, width = query.shape
    head_size = gains.shape[1]
    half = width // 2
    step = HEADS_PER_STEP * head_size
    steps = half // step
    lyric_rows = sum(run[2] for group in groups for run in group)
    lanes = 2 * frames
    key_rows = 3 * frames + lyric_rows

    def own(rows):
        return pl.BlockSpec((rows, step), lambda i, meta: (0, meta[0] * steps + i))

    def columns(rows):
        return pl.BlockSpec((rows, step), lambda i, meta: (0, i))

    def either(array):
        return own(array.shape[0]) if array.shape[1] == width else columns(array.shape[0])

    whole = lambda i, meta: (0, 0)
    bf16, f32 = jnp.bfloat16, jnp.float32
    return pl.pallas_call(
        functools.partial(attention_kernel, groups, head_size, head_size ** (-0.5)),
        grid_spec=pltpu.PrefetchScalarGridSpec(
            num_scalar_prefetch=1,
            grid=(steps,),
            in_specs=[pl.BlockSpec(gains.shape, whole)]
            + [own(frames)] * 4
            + [columns(mate.shape[0]), columns(2 * frames), columns(2 * frames)]
            + [either(array) for array in lyrics],
            out_specs=[own(frames)] * 2
            + [columns(frames)] * 2
            + [columns(4 * frames), columns(2 * frames), columns(2 * frames)]
            + [columns(array.shape[0]) for array in lyrics]
            + [pl.BlockSpec((8, head_size), whole)],
            scratch_shapes=[pltpu.VMEM((frames + lyric_rows, lanes), f32)],
        ),
        out_shape=[jax.ShapeDtypeStruct((frames, width), bf16)] * 2
        + [jax.ShapeDtypeStruct((frames, half), f32)] * 2
        + [
            jax.ShapeDtypeStruct((4 * frames, half), bf16),
            jax.ShapeDtypeStruct((2 * frames, half), bf16),
            jax.ShapeDtypeStruct((2 * frames, half), bf16),
        ]
        + [jax.ShapeDtypeStruct((array.shape[0], half), bf16) for array in lyrics]
        + [jax.ShapeDtypeStruct((8, head_size), f32)],
        compiler_params=params(),
        cost_estimate=pl.CostEstimate(
            flops=12 * key_rows * lanes * half,
            bytes_accessed=16 * 1024 * 1024,
            transcendentals=key_rows * lanes * (half // head_size),
        ),
        name="attention",
    )(meta, gains, query, cot, key, value, mate, near, far, *lyrics)


def fill_kernel(core_ref, first_ref, second_ref, *refs):
    refs[-2][...] = first_ref[...]
    refs[-1][...] = second_ref[...]


def fill_other(core, output, grad_query, mate):
    frames, width = output.shape
    step = width // 8
    spec = pl.BlockSpec((frames, step), lambda i, core: (0, (1 - core[0]) * 4 + i))
    return pl.pallas_call(
        fill_kernel,
        grid_spec=pltpu.PrefetchScalarGridSpec(
            num_scalar_prefetch=1,
            grid=(4,),
            in_specs=[
                pl.BlockSpec((frames, step), lambda i, core: (0, i)),
                pl.BlockSpec((frames, step), lambda i, core: (1, i)),
                pl.BlockSpec(memory_space=pl.ANY),
                pl.BlockSpec(memory_space=pl.ANY),
            ],
            out_specs=[spec] * 2,
        ),
        out_shape=[jax.ShapeDtypeStruct(output.shape, output.dtype)] * 2,
        input_output_aliases={3: 0, 4: 1},
        compiler_params=params(),
        name="fill_other",
    )(core, mate, mate, output, grad_query)


def through_norm(raw, grad, k_gain):
    raw = raw.astype(jnp.float32)
    inverse = lax.rsqrt(jnp.mean(raw * raw, axis=1, keepdims=True) + NORM_EPS)
    scaled = grad * k_gain
    return (
        inverse * scaled
        - raw * (inverse * inverse * inverse) * jnp.mean(scaled * raw, axis=1, keepdims=True)
    ).astype(jnp.bfloat16)


def finish_audio_kernel(
    head_size, core_ref, gain_ref, raw_ref, own_key, own_value, far_key, far_value, mate_key,
    mate_value, near_key, near_value, grad_key_ref, grad_value_ref,
):
    k_gain = gain_ref[1:2, :]

    def finish(keys, values):
        total = values[0][...].astype(jnp.float32) + values[1][...].astype(jnp.float32)
        grad_value_ref[...] = total.astype(jnp.bfloat16)
        for head in range(raw_ref.shape[1] // head_size):
            cols = slice(head * head_size, (head + 1) * head_size)
            grad = keys[0][:, cols].astype(jnp.float32) + keys[1][:, cols].astype(jnp.float32)
            grad_key_ref[:, cols] = through_norm(raw_ref[:, cols], grad, k_gain)

    @pl.when(pl.program_id(0) == 0)
    def _():
        finish((own_key, far_key), (own_value, far_value))

    @pl.when(pl.program_id(0) == 1)
    def _():
        finish((mate_key, near_key), (mate_value, near_value))


def finish_audio(core, gains, raw, own_key, own_value, from_far, mate, from_near):
    frames, width = raw.shape
    head_size = gains.shape[1]
    parts = 2
    step = width // 2 // parts

    def first(block):
        return pl.BlockSpec(
            (frames, step), lambda h, i, core: (block, jnp.where(h == 0, i, parts - 1))
        )

    def second(block):
        return pl.BlockSpec((frames, step), lambda h, i, core: (block, jnp.where(h == 0, 0, i)))

    both = pl.BlockSpec(
        (frames, step),
        lambda h, i, core: (0, jnp.where(h == 0, core[0], 1 - core[0]) * parts + i),
    )
    return pl.pallas_call(
        functools.partial(finish_audio_kernel, head_size),
        grid_spec=pltpu.PrefetchScalarGridSpec(
            num_scalar_prefetch=1,
            grid=(2, parts),
            in_specs=[pl.BlockSpec(gains.shape, lambda h, i, core: (0, 0)), both]
            + [first(0), first(0), first(0), first(1)]
            + [second(2), second(3), second(0), second(1)],
            out_specs=[both] * 2,
        ),
        out_shape=[jax.ShapeDtypeStruct((frames, width), jnp.bfloat16)] * 2,
        compiler_params=pltpu.CompilerParams(
            dimension_semantics=("arbitrary", "arbitrary"), vmem_limit_bytes=VMEM_LIMIT
        ),
        name="finish_audio",
    )(core, gains, raw, own_key, own_value, from_far, from_far, mate, mate, from_near, from_near)


def finish_lyric_kernel(head_size, gain_ref, raw_ref, *refs):
    rows = raw_ref.shape[0] // 4
    parts, out_refs = refs[:-2], refs[-2:]
    k_gain = gain_ref[1:2, :]
    for head in range(raw_ref.shape[1] // head_size):
        cols = slice(head * head_size, (head + 1) * head_size)
        total = parts[0][:, cols].astype(jnp.float32)
        for part in parts[1:]:
            total = total + part[:, cols].astype(jnp.float32)
        for index, ref in enumerate(out_refs):
            base = 2 * rows * index
            ref[0:rows, cols] = through_norm(
                raw_ref[base : base + rows, cols], total[base : base + rows], k_gain
            )
            ref[rows:, cols] = total[base + rows : base + 2 * rows].astype(jnp.bfloat16)


def finish_lyric(gains, raw, parts):
    rows, half = raw.shape
    head_size = gains.shape[1]
    step = half // 2
    spec = pl.BlockSpec((rows, step), lambda i: (0, i))
    out = pl.BlockSpec((rows // 2, step), lambda i: (0, i))
    return pl.pallas_call(
        functools.partial(finish_lyric_kernel, head_size),
        grid=(2,),
        in_specs=[pl.BlockSpec(gains.shape, lambda i: (0, 0)), spec] + [spec] * len(parts),
        out_specs=[out] * 2,
        out_shape=[jax.ShapeDtypeStruct((rows // 2, half), jnp.bfloat16)] * 2,
        compiler_params=params(),
        name="finish_lyric",
    )(gains, raw, *parts)


def join_kernel(core_ref, own_ref, mate_ref, grad_key_ref, grad_value_ref):
    rows, half = grad_key_ref.shape[0], own_ref.shape[1]
    for part, ref in ((core_ref[0], own_ref), (1 - core_ref[0], mate_ref)):
        cols = pl.ds(pl.multiple_of(part * half, half), half)
        grad_key_ref[:, cols] = ref[0:rows, :]
        grad_value_ref[:, cols] = ref[rows:, :]


def join_lyric(core, own, mate):
    rows, half = own.shape
    return pl.pallas_call(
        join_kernel,
        grid_spec=pltpu.PrefetchScalarGridSpec(
            num_scalar_prefetch=1,
            grid=(1,),
            in_specs=[pl.BlockSpec((rows, half), lambda i, core: (0, 0))] * 2,
            out_specs=[pl.BlockSpec((rows // 2, 2 * half), lambda i, core: (0, 0))] * 2,
        ),
        out_shape=[jax.ShapeDtypeStruct((rows // 2, 2 * half), jnp.bfloat16)] * 2,
        compiler_params=params(),
        name="join_lyric",
    )(core, own, mate)


def norm_lyric_kernel(head_size, gain_ref, raw_ref, grad_ref, out_ref):
    for head in range(raw_ref.shape[1] // head_size):
        cols = slice(head * head_size, (head + 1) * head_size)
        out_ref[:, cols] = through_norm(raw_ref[:, cols], grad_ref[:, cols], gain_ref[1:2, :])


def norm_lyric(gains, raw, grad):
    return pl.pallas_call(
        functools.partial(norm_lyric_kernel, gains.shape[1]),
        out_shape=jax.ShapeDtypeStruct(raw.shape, jnp.bfloat16),
        name="norm_lyric",
    )(gains, raw, grad)


def body(
    queries, keys, values, lyric_keys, lyric_values, q_gain, k_gain, cotangent, alignment, lyric_len
):
    frames = queries.shape[1]
    lyric_local, width = lyric_keys.shape[1:]
    count = lax.axis_size("seq")
    me = lax.axis_index("seq")
    core = me % 2
    chips = count // 2
    chip = me // 2
    core_array = core.astype(jnp.int32).reshape(1)
    gains = jnp.stack([q_gain, k_gain])

    swap = [(i, i ^ 1) for i in range(count)]
    near_pairs = [(i, i + 1) for i in range(1, count - 1, 2)]
    near_pairs += [(i, i - 1) for i in range(2, count, 2)]
    far_pairs = [(i, i + 2) for i in range(1, count - 2, 2)]
    far_pairs += [(i, i - 2) for i in range(2, count, 2)]

    def shift(block, steps):
        return lax.ppermute(
            block, "seq", [(i, (i + 2 * steps) % count) for i in range(count)]
        )

    def back(pairs):
        return [(target, source) for source, target in pairs]

    mate_align = lax.ppermute(alignment, "seq", swap)
    to_mate, to_near, to_far, own_lyric = pack(
        core_array, queries[0], cotangent[0], keys[0], values[0], lyric_keys[0], lyric_values[0]
    )
    near = lax.ppermute(to_near, "seq", near_pairs)
    far = lax.ppermute(to_far, "seq", far_pairs)
    mate = lax.ppermute(to_mate, "seq", swap)

    paired = chips <= 4 and lyric_local % 16 == 0
    if paired:
        pair_lyric = jnp.concatenate([own_lyric, mate[4 * frames :]], axis=0)
        lyrics = [pair_lyric] + [shift(pair_lyric, -j) for j in range(1, chips)]
        run = ((0, lyric_local, lyric_local), (2 * lyric_local, 3 * lyric_local, lyric_local))
        groups = (run,) * chips
        first_rows = []
        for j in range(chips):
            owner = 2 * ((chip + j) % chips)
            first_rows += [(owner + core) * lyric_local, (owner + 1 - core) * lyric_local]
    else:
        total_rows = lyric_local * count
        lyrics = [
            jnp.concatenate(
                [
                    lax.all_gather(lyric_keys[0], "seq", axis=0, tiled=True),
                    lax.all_gather(lyric_values[0], "seq", axis=0, tiled=True),
                ],
                axis=0,
            )
        ]
        groups = (((0, total_rows, total_rows),),)
        first_rows = [0]

    has_near = jnp.where(core == 0, me > 0, me < count - 1)
    has_far = jnp.where(core == 0, me + 1 < count - 1, me - 1 > 0)
    meta = jnp.stack(
        [
            jnp.asarray(value, jnp.int32)
            for value in [core]
            + [alignment[0, 0, slot] for slot in range(TILES)]
            + [mate_align[0, 0, slot] for slot in range(TILES)]
            + [lyric_len[0], has_near, has_far]
            + first_rows
        ]
    )
    results = attention(
        meta, gains, queries[0], cotangent[0], keys[0], values[0], mate, near, far, lyrics, groups
    )
    output, grad_queries, own_key, own_value, for_mate, for_near, for_far = results[:7]
    lyric_parts, gain_part = results[7:-1], results[-1]

    from_mate = lax.ppermute(for_mate, "seq", swap)
    if paired:
        lyric_sums = [lyric_parts[0]] + [shift(lyric_parts[j], j) for j in range(1, chips)]
        own_half, mate_half = finish_lyric(gains, pair_lyric, lyric_sums)
        grad_lyric_keys, grad_lyric_values = join_lyric(
            core_array, own_half, lax.ppermute(mate_half, "seq", swap)
        )
    else:
        spread = lax.dynamic_update_slice(
            jnp.zeros((2 * total_rows, width), jnp.float32),
            lyric_parts[0].astype(jnp.float32),
            (0, core * (width // 2)),
        )
        lyric_key_sum, grad_lyric_values = [
            lax.psum_scatter(part, "seq", scatter_dimension=0, tiled=True)
            for part in (spread[:total_rows], spread[total_rows:])
        ]
        grad_lyric_keys = norm_lyric(gains, lyric_keys[0], lyric_key_sum)
        grad_lyric_values = grad_lyric_values.astype(jnp.bfloat16)
    from_near = lax.ppermute(for_near, "seq", back(near_pairs))
    from_far = lax.ppermute(for_far, "seq", back(far_pairs))
    gain_total = jnp.sum(lax.all_gather(gain_part, ("song", "seq")), axis=0)
    output, grad_queries = fill_other(core_array, output, grad_queries, from_mate)
    grad_keys, grad_values = finish_audio(
        core_array, gains, keys[0], own_key, own_value, from_far, from_mate, from_near
    )
    return (
        output[None],
        grad_queries[None],
        grad_keys[None],
        grad_values[None],
        grad_lyric_keys[None],
        grad_lyric_values[None],
        gain_total[0],
        gain_total[1],
    )


def solution(mesh):
    split = P("song", "seq", None)
    return jax.shard_map(
        body,
        mesh=mesh,
        in_specs=(split, split, split, split, split, P(), P(), split, split, P("song")),
        out_specs=(split, split, split, split, split, split, P(), P()),
        check_vma=False,
    )
```

time: 148 us -> 163 us (1.10)
  the two profiles are of different devices: /device:TPU:12 before, /device:TPU:0 now
where the time goes in v2:
time: 163 us; the launch traced here: 162 us
  blocking collectives  64.9 us (40%)
  waiting for transfers between devices  36.1 us (22%)
  starting transfers between devices  24.4 us (15%)
  Pallas kernels  22 us (13%)
  local copies, waits for them, and re-layouts  12.8 us (8%)
    all_gather x1, blocking collectives, body(): gain_total = jnp.sum(lax.all_gather(gain_part, ('song', 'seq')), axis=0)  64.9 us
    ppermute x6, waiting for transfers between devices, shift(): lax.ppermute(block, 'seq', [(i, (i + 2 * steps) % count) for i in range(c...  23.2 us
    pallas_call x1, Pallas kernels, attention(): pl.pallas_call(functools.partial(attention_kernel, groups, head_size, hea...  14.3 us
    ppermute x1, waiting for transfers between devices, body(): far = lax.ppermute(to_far, 'seq', far_pairs)  12.3 us
    ppermute x6, starting transfers between devices, shift(): lax.ppermute(block, 'seq', [(i, (i + 2 * steps) % count) for i in range(c...  11.5 us
    unnamed x28, local copies, waits for them, and re-layouts  8.39 us
    ppermute x1, starting transfers between devices, body(): mate_align = lax.ppermute(alignment, 'seq', swap)  6.06 us
  transfers between devices with their start and end apart: 14, of which 5 were waited for; matrix products, arithmetic and copies ran while one was open for 3% of the time, Pallas kernels for 2%

profile of v2, /device:TPU:0, one launch (start us, length us, event | category | flops | bytes accessed | tf_op | source)
XLA Modules:
  0.0 162.4 jit_solution(13376613272809863565)
XLA Ops:
  0.6 0.0 copy-start
  0.7 1.0 copy-done
  1.7 0.0 copy-start.2
  1.7 1.0 copy-done.2
  2.7 0.0 copy-start.4
  2.7 0.9 copy-done.4
  3.7 0.0 copy-start.5
  3.7 0.9 copy-done.5
  4.6 0.0 copy-start.6
  4.6 1.0 copy-done.6
  5.6 0.0 copy-start.8
  5.6 1.0 copy-done.8
  6.7 0.0 copy-start.12
  6.7 0.0 copy-start.7
  6.7 2.2 %pack.1 = (bf16[608,1024]{1,0:T(8,128)(2,1)S(1)}, bf16[256,1024]{1,0:T(8,128)(2,1)}, bf16[256,1024]{1,0:T(8,128)(2,1)}, bf16[96,1024]{1,0:T(8,128)(2,1)S(1)}) custom-call(s32[1]{0:T(128)} %bitcast.core_ref, bf16[128,2048]{1,0:T(8,128)(2,1)S(1)} %bitcast.46, bf16[128,2048]{1,0:T(8,128)(2,1)S(1)} %bitcast.48, bf16[128,2048]{1,0:T(8,128)(2,1)S(1)} %bitcast.35, ...), custom_call_target="tpu_custom_call" | custom-call | bytes 5242880 | tf_op jit(solution)/shard_map/pack/pallas_call | solution.py:59
  8.9 0.5 collective-permute-start.1
  9.4 0.7 collective-permute-start.2
  10.1 1.3 collective-permute-start.3
  11.4 0.0 copy-done.12
  11.4 6.1 %collective-permute-start = (s32[1,1,2]{2,1,0:T(1,128)S(1)}, s32[1,1,2]{2,1,0:T(1,128)S(1)}, u32[]{:S(2)}, u32[]{:S(2)}) collective-permute-start(s32[1,1,2]{2,1,0:T(1,128)S(1)} %copy-done.12), channel_id=1, source_target_pairs={{0,1},{1,0},{2,3},{3,2},{4,5},{5,4},{6,7},{7,6},{8,9},{9,8},{10,11... | collective-permute-start | bytes 32 | tf_op jit(solution)/shard_map/ppermute | solution.py:474
  17.5 0.0 collective-permute-done.1.mate_ref
  17.5 0.0 copy-start.10
  17.5 1.1 copy-done.10
  18.6 1.6 collective-permute-start.6
  20.2 0.5 collective-permute-start.5
  20.7 0.0 collective-permute-done
  20.7 2.1 %collective-permute-start.4 = (bf16[192,1024]{1,0:T(8,128)(2,1)S(1)}, bf16[192,1024]{1,0:T(8,128)(2,1)}, u32[]{:S(2)}, u32[]{:S(2)}) collective-permute-start(bf16[192,1024]{1,0:T(8,128)(2,1)S(1)} %pad_maximum_fusion.refs_0_.raw_ref), channel_id=1, source_target_pairs={{0,6},{1,7},{2,0},{3,1},{4,2},{5,3},{6,4},{7,5},{8,14},{9,15},{10,... | collective-permute-start | bytes 1179656 | tf_op jit(solution)/shard_map/ppermute | solution.py:467
  23.5 0.0 copy-done.13
  23.5 0.7 pad_maximum_fusion.1.gain_ref
  24.2 0.6 fusion.1
  24.7 0.6 fusion
  25.3 2.7 %stack.61.meta_ref = s32[16]{0:T(128)S(1)} concatenate(s32[1]{0:T(128)} %bitcast.core_ref, s32[1]{0:T(128)} %bitcast.1, s32[1]{0:T(128)} %bitcast.2, s32[1]{0:T(128)} %bitcast.3, s32[1]{0:T(128)} %bitcast.4, s32[1]{0:T(128)S(6)} %copy.22, s32[1]{0:T(128)} %bitcast.5, s32[1]{0:T(128)} %bitcast.6, s32[1]{0:T(128)} %bitcast.7, s32[1]{0:T(128)} %bitcast.8, s32[1]{0:T(128)} %bitcast.9, ...), dimensions={0} | concatenate | bytes 128 | tf_op jit(solution)/shard_map/stack | solution.py:508
  28.0 0.0 collective-permute-done.2.near_ref
  28.0 12.3 %collective-permute-done.3.far_ref = bf16[256,1024]{1,0:T(8,128)(2,1)S(1)} collective-permute-done((bf16[256,1024]{1,0:T(8,128)(2,1)}, bf16[256,1024]{1,0:T(8,128)(2,1)S(1)}, u32[]{:S(2)}, u32[]{:S(2)}) %collective-permute-start.3) | collective-permute-done | bytes 524320 | tf_op jit(solution)/shard_map/ppermute | solution.py:479
  40.4 3.9 %collective-permute-done.6.refs_3_ = bf16[192,1024]{1,0:T(8,128)(2,1)} collective-permute-done((bf16[192,1024]{1,0:T(8,128)(2,1)S(1)}, bf16[192,1024]{1,0:T(8,128)(2,1)}, u32[]{:S(2)}, u32[]{:S(2)}) %collective-permute-start.6) | collective-permute-done | bytes 393248 | tf_op jit(solution)/shard_map/ppermute | solution.py:467
  44.3 13.7 %collective-permute-done.5.refs_2_ = bf16[192,1024]{1,0:T(8,128)(2,1)} collective-permute-done((bf16[192,1024]{1,0:T(8,128)(2,1)S(1)}, bf16[192,1024]{1,0:T(8,128)(2,1)}, u32[]{:S(2)}, u32[]{:S(2)}) %collective-permute-start.5) | collective-permute-done | bytes 393248 | tf_op jit(solution)/shard_map/ppermute | solution.py:467
  58.0 0.0 collective-permute-done.4.refs_1_
  58.0 0.0 copy-done.7
  58.0 0.0 copy-done.9
  58.0 0.0 copy-done.1
  58.0 0.0 copy-done.3
  58.0 0.0 copy-start.11
  58.0 1.3 copy-done.11
  59.3 14.3 %attention.1 = (bf16[128,2048]{1,0:T(8,128)(2,1)}, bf16[128,2048]{1,0:T(8,128)(2,1)}, f32[128,1024]{1,0:T(8,128)S(1)}, f32[128,1024]{1,0:T(8,128)S(1)}, bf16[512...) custom-call(s32[16]{0:T(128)S(1)} %stack.61.meta_ref, ...), custom_call_target="tpu_custom_call" | custom-call | flops 2415919104 | bytes 16777216 | tf_op jit(solution)/shard_map/attention/pallas_call | solution.py:242
  73.7 0.0 collective-permute-start.7
  73.7 4.8 %collective-permute-start.10 = (bf16[192,1024]{1,0:T(8,128)(2,1)S(1)}, bf16[192,1024]{1,0:T(8,128)(2,1)S(1)}, u32[]{:S(2)}, u32[]{:S(2)}) collective-permute-start(bf16[192,1024]{1,0:T(8,128)(2,1)S(1)} %get-tuple-element.48), channel_id=1, source_target_pairs={{0,2},{1,3},{2,4},{3,5},{4,6},{5,7},{6,0},{7,1},{8,10},{9,11},{10,... | collective-permute-start | bytes 1179656 | tf_op jit(solution)/shard_map/ppermute | solution.py:467
  78.5 1.7 %collective-permute-start.11 = (bf16[192,1024]{1,0:T(8,128)(2,1)S(1)}, bf16[192,1024]{1,0:T(8,128)(2,1)S(1)}, u32[]{:S(2)}, u32[]{:S(2)}) collective-permute-start(bf16[192,1024]{1,0:T(8,128)(2,1)S(1)} %get-tuple-element.49), channel_id=1, source_target_pairs={{0,4},{1,5},{2,6},{3,7},{4,0},{5,1},{6,2},{7,3},{8,12},{9,13},{10,... | collective-permute-start | bytes 1179656 | tf_op jit(solution)/shard_map/ppermute | solution.py:467
  80.2 0.7 collective-permute-start.12
  81.0 3.2 %collective-permute-start.8 = (bf16[256,1024]{1,0:T(8,128)(2,1)S(1)}, bf16[256,1024]{1,0:T(8,128)(2,1)S(1)}, u32[]{:S(2)}, u32[]{:S(2)}) collective-permute-start(bf16[256,1024]{1,0:T(8,128)(2,1)S(1)} %get-tuple-element.43), channel_id=1, source_target_pairs={{3,1},{5,3},{7,5},{0,2},{2,4},{4,6},{11,9},{13,11},{15,13},{8,10},... | collective-permute-start | bytes 1572872 | tf_op jit(solution)/shard_map/ppermute | solution.py:544
  84.2 5.5 %collective-permute-done.10.refs_1_ = bf16[192,1024]{1,0:T(8,128)(2,1)S(1)} collective-permute-done((bf16[192,1024]{1,0:T(8,128)(2,1)S(1)}, bf16[192,1024]{1,0:T(8,128)(2,1)S(1)}, u32[]{:S(2)}, u32[]{:S(2)}) %collective-permute-start.10) | collective-permute-done | bytes 393248 | tf_op jit(solution)/shard_map/ppermute | solution.py:467
  89.7 0.7 collective-permute-start.9
  90.4 64.9 %all-gather = f32[256,128]{1,0:T(8,128)S(1)} all-gather(f32[8,128]{1,0:T(8,128)S(1)} %get-tuple-element.55), channel_id=2, replica_groups=mesh['song'=4,'seq'=8] {'song','seq'}, dimensions={0}, use_global_device_ids=true | all-gather | bytes 135168 | tf_op jit(solution)/shard_map/all_gather | solution.py:545
  155.3 0.0 collective-permute-done.11.refs_2_
  155.4 0.0 collective-permute-done.12.refs_3_
  155.4 0.7 finish_lyric.1
  156.0 0.4 collective-permute-start.13
  156.4 0.5 slice_bitcast_fusion
  157.0 0.6 collective-permute-done.13.mate_ref
  157.5 0.8 join_lyric.1
  158.3 0.0 collective-permute-done.7.first_ref.second_ref.mate_key.mate_value
  158.3 1.5 fill_other.1
  159.8 0.0 collective-permute-done.8.far_key.far_value
  159.8 0.0 collective-permute-done.9.near_key.near_value
  159.8 2.6 %finish_audio.1 = (bf16[128,2048]{1,0:T(8,128)(2,1)}, bf16[128,2048]{1,0:T(8,128)(2,1)}) custom-call(s32[1]{0:T(128)} %bitcast.core_ref, f32[2,128]{1,0:T(2,128)S(1)} %pad_maximum_fusion.1.gain_ref, bf16[128,2048]{1,0:T(8,128)(2,1)S(1)} %bitcast.38, f32[128,1024]{1,0:T(8,128)S(1)} %get-tuple-element.41.own_key, f32[128,1024]{1,0:T(8,128)S(1)} %get-tuple-element.42.own_value, ...), custom_call_target="tpu_custom_call" | custom-call | tf_op jit(solution)/shard_map/finish_audio/pallas_call | solution.py:357
  (7 shorter events, 0.1 us)
Async XLA Ops:
  0.6 1.0 copy-start
  1.7 1.0 copy-start.2
  2.7 0.9 copy-start.4
  3.7 0.9 copy-start.5
  4.6 1.0 copy-start.6
  5.6 1.0 copy-start.8
  6.7 4.7 %copy-start.12 = (s32[1,1,2]{2,1,0:T(1,128)S(1)}, s32[1,1,2]{2,1,0:T(1,128)}, u32[]{:S(2)}) copy-start(s32[1,1,2]{2,1,0:T(1,128)} %param.18) | copy-start | bytes 28
  6.7 51.3 %copy-start.7 = (bf16[1,128,2048]{2,1,0:T(8,128)(2,1)S(1)}, bf16[1,128,2048]{2,1,0:T(8,128)(2,1)}, u32[]{:S(2)}) copy-start(bf16[1,128,2048]{2,1,0:T(8,128)(2,1)} %param.10) | copy-start | bytes 1572868
  6.7 51.3 %copy-start.9 = (bf16[1,128,2048]{2,1,0:T(8,128)(2,1)S(1)}, bf16[1,128,2048]{2,1,0:T(8,128)(2,1)}, u32[]{:S(2)}) copy-start(bf16[1,128,2048]{2,1,0:T(8,128)(2,1)} %param.17) | copy-start | bytes 1572868
  8.9 14.6 %copy-start.13 = (f32[128]{0:T(128)S(1)}, f32[128]{0:T(128)}, u32[]{:S(2)}) copy-start(f32[128]{0:T(128)} %param.16) | copy-start | bytes 1540
  8.9 49.1 %copy-start.1 = (bf16[1,128,2048]{2,1,0:T(8,128)(2,1)S(1)}, bf16[1,128,2048]{2,1,0:T(8,128)(2,1)}, u32[]{:S(2)}) copy-start(bf16[1,128,2048]{2,1,0:T(8,128)(2,1)} %param.11) | copy-start | bytes 1572868
  8.9 49.1 %copy-start.3 = (bf16[1,128,2048]{2,1,0:T(8,128)(2,1)S(1)}, bf16[1,128,2048]{2,1,0:T(8,128)(2,1)}, u32[]{:S(2)}) copy-start(bf16[1,128,2048]{2,1,0:T(8,128)(2,1)} %param.12) | copy-start | bytes 1572868
  8.9 8.6 %collective-permute-start.1 = (bf16[608,1024]{1,0:T(8,128)(2,1)S(1)}, bf16[608,1024]{1,0:T(8,128)(2,1)S(1)}, u32[]{:S(2)}, u32[]{:S(2)}) collective-permute-start(bf16[608,1024]{1,0:T(8,128)(2,1)S(1)} %get-tuple-element.32), channel_id=1, source_target_pairs={{0,1},{1,0},{2,3},{3,2},{4,5},{5,4},{6,7},{7,6},{8,9},{9,8},{10,11... | collective-permute-start | bytes 3735560 | tf_op jit(solution)/shard_map/ppermute | solution.py:480
  9.4 18.6 %collective-permute-start.2 = (bf16[256,1024]{1,0:T(8,128)(2,1)}, bf16[256,1024]{1,0:T(8,128)(2,1)S(1)}, u32[]{:S(2)}, u32[]{:S(2)}) collective-permute-start(bf16[256,1024]{1,0:T(8,128)(2,1)} %get-tuple-element.33), channel_id=1, source_target_pairs={{1,2},{3,4},{5,6},{2,1},{4,3},{6,5},{9,10},{11,12},{13,14},{10,9},... | collective-permute-start | bytes 1572872 | tf_op jit(solution)/shard_map/ppermute | solution.py:478
  10.1 30.3 %collective-permute-start.3 = (bf16[256,1024]{1,0:T(8,128)(2,1)}, bf16[256,1024]{1,0:T(8,128)(2,1)S(1)}, u32[]{:S(2)}, u32[]{:S(2)}) collective-permute-start(bf16[256,1024]{1,0:T(8,128)(2,1)} %get-tuple-element.34), channel_id=1, source_target_pairs={{1,3},{3,5},{5,7},{2,0},{4,2},{6,4},{9,11},{11,13},{13,15},{10,8},... | collective-permute-start | bytes 1572872 | tf_op jit(solution)/shard_map/ppermute | solution.py:479
  11.4 9.3 %collective-permute-start = (s32[1,1,2]{2,1,0:T(1,128)S(1)}, s32[1,1,2]{2,1,0:T(1,128)S(1)}, u32[]{:S(2)}, u32[]{:S(2)}) collective-permute-start(s32[1,1,2]{2,1,0:T(1,128)S(1)} %copy-done.12), channel_id=1, source_target_pairs={{0,1},{1,0},{2,3},{3,2},{4,5},{5,4},{6,7},{7,6},{8,9},{9,8},{10,11... | collective-permute-start | bytes 32 | tf_op jit(solution)/shard_map/ppermute | solution.py:474
  17.5 1.1 copy-start.10
  18.6 25.7 %collective-permute-start.6 = (bf16[192,1024]{1,0:T(8,128)(2,1)S(1)}, bf16[192,1024]{1,0:T(8,128)(2,1)}, u32[]{:S(2)}, u32[]{:S(2)}) collective-permute-start(bf16[192,1024]{1,0:T(8,128)(2,1)S(1)} %pad_maximum_fusion.refs_0_.raw_ref), channel_id=1, source_target_pairs={{0,2},{1,3},{2,4},{3,5},{4,6},{5,7},{6,0},{7,1},{8,10},{9,11},{10,... | collective-permute-start | bytes 1179656 | tf_op jit(solution)/shard_map/ppermute | solution.py:467
  20.2 37.8 %collective-permute-start.5 = (bf16[192,1024]{1,0:T(8,128)(2,1)S(1)}, bf16[192,1024]{1,0:T(8,128)(2,1)}, u32[]{:S(2)}, u32[]{:S(2)}) collective-permute-start(bf16[192,1024]{1,0:T(8,128)(2,1)S(1)} %pad_maximum_fusion.refs_0_.raw_ref), channel_id=1, source_target_pairs={{0,4},{1,5},{2,6},{3,7},{4,0},{5,1},{6,2},{7,3},{8,12},{9,13},{10,... | collective-permute-start | bytes 1179656 | tf_op jit(solution)/shard_map/ppermute | solution.py:467
  20.7 37.3 %collective-permute-start.4 = (bf16[192,1024]{1,0:T(8,128)(2,1)S(1)}, bf16[192,1024]{1,0:T(8,128)(2,1)}, u32[]{:S(2)}, u32[]{:S(2)}) collective-permute-start(bf16[192,1024]{1,0:T(8,128)(2,1)S(1)} %pad_maximum_fusion.refs_0_.raw_ref), channel_id=1, source_target_pairs={{0,6},{1,7},{2,0},{3,1},{4,2},{5,3},{6,4},{7,5},{8,14},{9,15},{10,... | collective-permute-start | bytes 1179656 | tf_op jit(solution)/shard_map/ppermute | solution.py:467
  58.0 1.3 copy-start.11
  73.7 84.6 %collective-permute-start.7 = (bf16[512,1024]{1,0:T(8,128)(2,1)S(1)}, bf16[512,1024]{1,0:T(8,128)(2,1)S(1)}, u32[]{:S(2)}, u32[]{:S(2)}) collective-permute-start(bf16[512,1024]{1,0:T(8,128)(2,1)S(1)} %get-tuple-element.36), channel_id=1, source_target_pairs={{0,1},{1,0},{2,3},{3,2},{4,5},{5,4},{6,7},{7,6},{8,9},{9,8},{10,11... | collective-permute-start | bytes 3145736 | tf_op jit(solution)/shard_map/ppermute | solution.py:524
  73.7 16.0 %collective-permute-start.10 = (bf16[192,1024]{1,0:T(8,128)(2,1)S(1)}, bf16[192,1024]{1,0:T(8,128)(2,1)S(1)}, u32[]{:S(2)}, u32[]{:S(2)}) collective-permute-start(bf16[192,1024]{1,0:T(8,128)(2,1)S(1)} %get-tuple-element.48), channel_id=1, source_target_pairs={{0,2},{1,3},{2,4},{3,5},{4,6},{5,7},{6,0},{7,1},{8,10},{9,11},{10,... | collective-permute-start | bytes 1179656 | tf_op jit(solution)/shard_map/ppermute | solution.py:467
  78.5 76.9 %collective-permute-start.11 = (bf16[192,1024]{1,0:T(8,128)(2,1)S(1)}, bf16[192,1024]{1,0:T(8,128)(2,1)S(1)}, u32[]{:S(2)}, u32[]{:S(2)}) collective-permute-start(bf16[192,1024]{1,0:T(8,128)(2,1)S(1)} %get-tuple-element.49), channel_id=1, source_target_pairs={{0,4},{1,5},{2,6},{3,7},{4,0},{5,1},{6,2},{7,3},{8,12},{9,13},{10,... | collective-permute-start | bytes 1179656 | tf_op jit(solution)/shard_map/ppermute | solution.py:467
  80.2 75.1 %collective-permute-start.12 = (bf16[192,1024]{1,0:T(8,128)(2,1)S(1)}, bf16[192,1024]{1,0:T(8,128)(2,1)S(1)}, u32[]{:S(2)}, u32[]{:S(2)}) collective-permute-start(bf16[192,1024]{1,0:T(8,128)(2,1)S(1)} %get-tuple-element.50), channel_id=1, source_target_pairs={{0,6},{1,7},{2,0},{3,1},{4,2},{5,3},{6,4},{7,5},{8,14},{9,15},{10,... | collective-permute-start | bytes 1179656 | tf_op jit(solution)/shard_map/ppermute | solution.py:467
  81.0 78.8 %collective-permute-start.8 = (bf16[256,1024]{1,0:T(8,128)(2,1)S(1)}, bf16[256,1024]{1,0:T(8,128)(2,1)S(1)}, u32[]{:S(2)}, u32[]{:S(2)}) collective-permute-start(bf16[256,1024]{1,0:T(8,128)(2,1)S(1)} %get-tuple-element.43), channel_id=1, source_target_pairs={{3,1},{5,3},{7,5},{0,2},{2,4},{4,6},{11,9},{13,11},{15,13},{8,10},... | collective-permute-start | bytes 1572872 | tf_op jit(solution)/shard_map/ppermute | solution.py:544
  89.7 70.1 %collective-permute-start.9 = (bf16[256,1024]{1,0:T(8,128)(2,1)S(1)}, bf16[256,1024]{1,0:T(8,128)(2,1)S(1)}, u32[]{:S(2)}, u32[]{:S(2)}) collective-permute-start(bf16[256,1024]{1,0:T(8,128)(2,1)S(1)} %get-tuple-element.44), channel_id=1, source_target_pairs={{2,1},{4,3},{6,5},{1,2},{3,4},{5,6},{10,9},{12,11},{14,13},{9,10},... | collective-permute-start | bytes 1572872 | tf_op jit(solution)/shard_map/ppermute | solution.py:543
  156.0 1.5 collective-permute-start.13

commit v3 on v2

v3 whole, which is shorter than its diff:
```python
import functools

import jax
import jax.numpy as jnp
from jax import lax
from jax.experimental import pallas as pl
from jax.experimental.pallas import tpu as pltpu
from jax.sharding import PartitionSpec as P

BLK = 128
TILES = 2
NORM_EPS = 1e-06
HEADS_PER_STEP = 1
CHUNKS = 2
VMEM_LIMIT = 32 * 1024 * 1024


def dot(lhs, rhs, lhs_dim, rhs_dim):
    return lax.dot_general(
        lhs, rhs, (((lhs_dim,), (rhs_dim,)), ((), ())), preferred_element_type=jnp.float32
    )


def params():
    return pltpu.CompilerParams(
        dimension_semantics=("arbitrary",), vmem_limit_bytes=VMEM_LIMIT
    )


def pack_kernel(core_ref, *refs):
    out_ref = refs[-1]
    start = 0
    for ref in refs[:-1]:
        out_ref[start : start + ref.shape[0], :] = ref[...]
        start += ref.shape[0]


def pack(core, chunk, arrays):
    width = arrays[0].shape[1]
    size = width // 2 // CHUNKS
    step = size // 2
    rows = sum(array.shape[0] for array in arrays)
    return pl.pallas_call(
        pack_kernel,
        grid_spec=pltpu.PrefetchScalarGridSpec(
            num_scalar_prefetch=1,
            grid=(2,),
            in_specs=[
                pl.BlockSpec(
                    (array.shape[0], step),
                    lambda i, core: (0, ((1 - core[0]) * CHUNKS + chunk) * 2 + i),
                )
                for array in arrays
            ],
            out_specs=pl.BlockSpec((rows, step), lambda i, core: (0, i)),
        ),
        out_shape=jax.ShapeDtypeStruct((rows, size), jnp.bfloat16),
        compiler_params=params(),
        cost_estimate=pl.CostEstimate(
            flops=0, bytes_accessed=4 * rows * size, transcendentals=0
        ),
        name="pack",
    )(core, *arrays)


def merge_kernel(lyric, core_ref, key_ref, value_ref, lkey_ref, lvalue_ref, mate_ref, *refs):
    up_ref, down_ref = refs[-2:]
    frames = key_ref.shape[0]
    first = mate_ref.shape[0] - 2 * frames
    for ref, owner in ((up_ref, 1), (down_ref, 0)):
        if lyric:
            ref[0:lyric, :] = lkey_ref[...]
            ref[lyric : 2 * lyric, :] = lvalue_ref[...]
            ref[2 * lyric : 4 * lyric, :] = mate_ref[0 : 2 * lyric, :]
        mine = core_ref[0] == owner
        ref[4 * lyric : 4 * lyric + frames, :] = jnp.where(
            mine, key_ref[...], mate_ref[first : first + frames, :]
        )
        ref[4 * lyric + frames :, :] = jnp.where(
            mine, value_ref[...], mate_ref[first + frames :, :]
        )


def merge(core, chunk, key, value, lyric_key, lyric_value, mate, with_lyric, after):
    frames, width = key.shape
    lyric = lyric_key.shape[0]
    size = width // 2 // CHUNKS
    step = size // 2
    rows = 2 * frames + (4 * lyric if with_lyric else 0)

    def own(array):
        return pl.BlockSpec(
            (array.shape[0], step), lambda i, core: (0, (core[0] * CHUNKS + chunk) * 2 + i)
        )

    def columns(count):
        return pl.BlockSpec((count, step), lambda i, core: (0, i))

    return pl.pallas_call(
        functools.partial(merge_kernel, lyric if with_lyric else 0),
        grid_spec=pltpu.PrefetchScalarGridSpec(
            num_scalar_prefetch=1,
            grid=(2,),
            in_specs=[own(key), own(value), own(lyric_key), own(lyric_value)]
            + [columns(mate.shape[0])]
            + [pl.BlockSpec(memory_space=pl.ANY)] * len(after),
            out_specs=[columns(rows)] * 2,
        ),
        out_shape=[jax.ShapeDtypeStruct((rows, size), jnp.bfloat16)] * 2,
        compiler_params=params(),
        cost_estimate=pl.CostEstimate(
            flops=0, bytes_accessed=8 * rows * size, transcendentals=0
        ),
        name="merge",
    )(core, key, value, lyric_key, lyric_value, mate, *after)


def attention_kernel(
    groups, chained, head_size, score_scale, meta_ref, gain_ref, query_ref, grad_ref, key_ref, value_ref,
    mate_ref, up_ref, down_ref, *refs
):
    frames = query_ref.shape[0]
    arrays = len(groups)
    inputs = 4 if arrays == 4 else arrays
    lyric_in, refs = refs[:inputs], refs[inputs + 2 * chained :]
    window = up_ref.shape[0] - 2 * frames
    out_ref, grad_query_ref, to_mate_ref, key_grad_ref, value_grad_ref = refs[:5]
    to_left_ref, to_right_ref = refs[5:7]
    lyric_out = refs[7 : arrays + 7]
    gain_grad_ref, mask_ref = refs[arrays + 7 :]
    runs = [(index, run) for index, group in enumerate(groups) for run in group]
    main = 2 * frames + sum(run[2] for _, run in runs)
    lanes = 2 * frames

    @pl.when(pl.program_id(0) == 0)
    def _():
        gain_grad_ref[...] = jnp.zeros_like(gain_grad_ref)
        start = 0
        for number, (_, (_, _, rows)) in enumerate(runs):
            row = lax.broadcasted_iota(jnp.int32, (rows, lanes), 0) + meta_ref[9 + number]
            lane = lax.broadcasted_iota(jnp.int32, (rows, lanes), 1)
            keep = jnp.zeros((rows, lanes), jnp.float32)
            for slot in range(TILES):
                lower = jnp.where(lane < frames, meta_ref[1 + slot], meta_ref[3 + slot]) * BLK
                upper = jnp.minimum(lower + BLK, meta_ref[5])
                inside = (row >= lower) & (row < upper) & (lower >= 0)
                keep = jnp.where(inside, 1.0, keep)
            mask_ref[start : start + rows, :] = keep
            start += rows
        lane = lax.broadcasted_iota(jnp.int32, (frames, lanes), 1)
        mask_ref[start : start + frames, :] = jnp.where(
            lane < frames, meta_ref[6], meta_ref[7]
        ).astype(jnp.float32)

    q_gain = gain_ref[0:1, :]
    k_gain = gain_ref[1:2, :]
    for head in range(query_ref.shape[1] // head_size):
        cols = slice(head * head_size, (head + 1) * head_size)
        if arrays == 4:
            pair, up_two, down_two, far_end = [ref[:, cols] for ref in lyric_in]
            up_one, down_one = up_ref[0:window, cols], down_ref[0:window, cols]
            chip = meta_ref[8]
            lyric = [
                pair,
                jnp.where(chip == 0, far_end, up_one),
                jnp.where(chip == 3, far_end, down_one),
                jnp.where(chip <= 1, down_two, up_two),
            ]
        else:
            lyric = [ref[:, cols] for ref in lyric_in]
        left, right = up_ref[window:, cols], down_ref[window:, cols]
        near_rows = jnp.where(meta_ref[0] == 0, left, right)
        far_rows = jnp.where(meta_ref[0] == 0, right, left)
        first = mate_ref.shape[0] - 4 * frames

        def from_mate(number):
            return mate_ref[first + number * frames : first + (number + 1) * frames, cols]

        query = jnp.concatenate([query_ref[:, cols], from_mate(0)], axis=0)
        query = query.astype(jnp.float32)
        cot = jnp.concatenate([grad_ref[:, cols], from_mate(1)], axis=0)
        raw_keys = jnp.concatenate(
            [key_ref[:, cols], from_mate(2)]
            + [lyric[index][run[0] : run[0] + run[2]] for index, run in runs]
            + [near_rows[:frames], far_rows[:frames]],
            axis=0,
        ).astype(jnp.float32)
        value = jnp.concatenate(
            [value_ref[:, cols], from_mate(3)]
            + [lyric[index][run[1] : run[1] + run[2]] for index, run in runs]
            + [near_rows[frames:], far_rows[frames:]],
            axis=0,
        )
        query_inv = lax.rsqrt(jnp.mean(query * query, axis=1, keepdims=True) + NORM_EPS)
        key_inv = lax.rsqrt(jnp.mean(raw_keys * raw_keys, axis=1, keepdims=True) + NORM_EPS)
        query_hat = query * query_inv
        query_low = (query_hat * (q_gain * score_scale)).astype(jnp.bfloat16)
        key_hat = raw_keys * key_inv
        key_low = (key_hat * k_gain).astype(jnp.bfloat16)

        near, far = slice(main, main + frames), slice(main + frames, main + 2 * frames)

        def against(rows, columns):
            return jnp.concatenate(
                [
                    dot(rows[:main], columns, 1, 1),
                    jnp.concatenate(
                        [
                            dot(rows[near], columns[:frames], 1, 1),
                            dot(rows[far], columns[frames:], 1, 1),
                        ],
                        axis=1,
                    ),
                ],
                axis=0,
            )

        def over_keys(weights, rows):
            return dot(weights[:main], rows[:main], 0, 0) + jnp.concatenate(
                [
                    dot(weights[main:, :frames], rows[near], 0, 0),
                    dot(weights[main:, frames:], rows[far], 0, 0),
                ],
                axis=0,
            )

        def over_queries(weights, columns):
            return jnp.concatenate(
                [
                    dot(weights[:main], columns, 1, 0),
                    dot(weights[main:, :frames], columns[:frames], 1, 0),
                    dot(weights[main:, frames:], columns[frames:], 1, 0),
                ],
                axis=0,
            )

        exp_scores = jnp.exp(against(key_low, query_low))
        exp_scores = jnp.concatenate(
            [exp_scores[: 2 * frames], exp_scores[2 * frames :] * mask_ref[...]], axis=0
        )
        grad_prob = against(value, cot)
        prob = exp_scores * (1.0 / jnp.sum(exp_scores, axis=0, keepdims=True))
        prob_low = prob.astype(jnp.bfloat16)
        weighted = prob * grad_prob
        delta = jnp.sum(weighted, axis=0, keepdims=True)
        grad_score = (weighted - prob * delta).astype(jnp.bfloat16)
        output = over_keys(prob_low, value).astype(jnp.bfloat16)
        grad_qn = over_keys(grad_score, key_low) * score_scale
        grad_keys = over_queries(grad_score, query_low)
        grad_values = over_queries(prob_low, cot)
        scaled = grad_qn * q_gain
        grad_query = (
            query_inv * scaled
            - query_hat
            * (query_inv * query_inv)
            * jnp.mean(scaled * query, axis=1, keepdims=True)
        ).astype(jnp.bfloat16)
        gain_grad_ref[0:1, :] += jnp.sum(grad_qn * query_hat, axis=0, keepdims=True)
        gain_grad_ref[1:2, :] += jnp.sum(grad_keys * key_hat, axis=0, keepdims=True)

        out_ref[:, cols] = output[:frames]
        grad_query_ref[:, cols] = grad_query[:frames]
        to_mate_ref[0:frames, cols] = output[frames:]
        to_mate_ref[frames:, cols] = grad_query[frames:]
        key_grad_ref[:, cols] = grad_keys[: 2 * frames]
        value_grad_ref[:, cols] = grad_values[: 2 * frames]
        for grads, part in (
            (grad_keys.astype(jnp.bfloat16), slice(0, frames)),
            (grad_values.astype(jnp.bfloat16), slice(frames, 2 * frames)),
        ):
            to_left_ref[part, cols] = jnp.where(meta_ref[0] == 0, grads[near], grads[far])
            to_right_ref[part, cols] = jnp.where(meta_ref[0] == 0, grads[far], grads[near])
        start = 2 * frames
        for index, (key_row, value_row, rows) in runs:
            part = slice(start, start + rows)
            lyric_out[index][key_row : key_row + rows, cols] = grad_keys[part].astype(jnp.bfloat16)
            lyric_out[index][value_row : value_row + rows, cols] = grad_values[part].astype(
                jnp.bfloat16
            )
            start += rows


def attention(chunk, meta, gains, query, cot, key, value, mate, up, down, lyrics, groups, carried):
    frames, width = query.shape
    head_size = gains.shape[1]
    size = width // 2 // CHUNKS
    step = HEADS_PER_STEP * head_size
    steps = size // step
    lyric_rows = sum(run[2] for group in groups for run in group)
    lanes = 2 * frames
    key_rows = 3 * frames + lyric_rows

    def own(rows):
        return pl.BlockSpec(
            (rows, step), lambda i, meta: (0, (meta[0] * CHUNKS + chunk) * steps + i)
        )

    def columns(rows):
        return pl.BlockSpec((rows, step), lambda i, meta: (0, i))

    slot = sum(2 * run[2] for run in groups[0])

    def either(array):
        return own(slot) if array.shape[1] == width else columns(slot)

    whole = lambda i, meta: (0, 0)
    bf16, f32 = jnp.bfloat16, jnp.float32
    slot_rows = [slot] * len(groups)
    return pl.pallas_call(
        functools.partial(
            attention_kernel, groups, len(carried) // 2, head_size, head_size ** (-0.5)
        ),
        grid_spec=pltpu.PrefetchScalarGridSpec(
            num_scalar_prefetch=1,
            grid=(steps,),
            in_specs=[pl.BlockSpec(gains.shape, whole)]
            + [own(frames)] * 4
            + [columns(mate.shape[0]), columns(up.shape[0]), columns(down.shape[0])]
            + [either(array) for array in lyrics]
            + [pl.BlockSpec(memory_space=pl.ANY)] * len(carried),
            out_specs=[own(frames)] * 2
            + [columns(2 * frames)] * 5
            + [columns(rows) for rows in slot_rows]
            + [pl.BlockSpec((8, head_size), whole)],
            scratch_shapes=[pltpu.VMEM((frames + lyric_rows, lanes), f32)],
        ),
        out_shape=[jax.ShapeDtypeStruct((frames, width), bf16)] * 2
        + [jax.ShapeDtypeStruct((2 * frames, size), dtype) for dtype in (bf16, f32, f32, bf16, bf16)]
        + [jax.ShapeDtypeStruct((rows, size), bf16) for rows in slot_rows]
        + [jax.ShapeDtypeStruct((8, head_size), f32)],
        input_output_aliases={9 + len(lyrics) + i: i for i in range(len(carried))},
        compiler_params=params(),
        cost_estimate=pl.CostEstimate(
            flops=12 * key_rows * lanes * size,
            bytes_accessed=16 * 1024 * 1024 // CHUNKS,
            transcendentals=key_rows * lanes * (size // head_size),
        ),
        name="attention",
    )(meta, gains, query, cot, key, value, mate, up, down, *lyrics, *carried)


def fill_kernel(count, core_ref, mate_ref, *refs):
    rows = mate_ref.shape[0] // count
    for index, ref in enumerate(refs[-count:]):
        ref[...] = mate_ref[index * rows : (index + 1) * rows, :]


def fill_other(core, chunk, arrays, mate):
    frames, width = arrays[0].shape
    count = len(arrays)
    size = width // 2 // CHUNKS
    step = size // 2
    spec = pl.BlockSpec(
        (frames, step), lambda i, core: (0, ((1 - core[0]) * CHUNKS + chunk) * 2 + i)
    )
    return pl.pallas_call(
        functools.partial(fill_kernel, count),
        grid_spec=pltpu.PrefetchScalarGridSpec(
            num_scalar_prefetch=1,
            grid=(2,),
            in_specs=[pl.BlockSpec((count * frames, step), lambda i, core: (0, i))]
            + [pl.BlockSpec(memory_space=pl.ANY)] * count,
            out_specs=[spec] * count,
        ),
        out_shape=[jax.ShapeDtypeStruct(array.shape, array.dtype) for array in arrays],
        input_output_aliases={2 + i: i for i in range(count)},
        compiler_params=params(),
        cost_estimate=pl.CostEstimate(
            flops=0, bytes_accessed=4 * count * frames * size, transcendentals=0
        ),
        name="fill_other",
    )(core, mate, *arrays)


def through_norm(raw, grad, k_gain):
    raw = raw.astype(jnp.float32)
    inverse = lax.rsqrt(jnp.mean(raw * raw, axis=1, keepdims=True) + NORM_EPS)
    scaled = grad * k_gain
    return (
        inverse * scaled
        - raw * (inverse * inverse * inverse) * jnp.mean(scaled * raw, axis=1, keepdims=True)
    ).astype(jnp.bfloat16)


def finish_audio_kernel(
    head_size, core_ref, gain_ref, raw_ref, mate_ref, key_grad_ref, value_grad_ref, up_ref,
    down_ref, ready_ref, *refs,
):
    k_gain = gain_ref[1:2, :]
    grad_key_ref, grad_value_ref, to_mate_ref = refs[-3:]
    frames = raw_ref.shape[0]
    own, mate = slice(0, frames), slice(frames, 2 * frames)
    first = up_ref.shape[0] - 2 * frames
    mate_keys = mate_ref.shape[0] - 2 * frames
    to_mate_ref[0 : 2 * frames, :] = ready_ref[...]
    for head in range(raw_ref.shape[1] // head_size):
        cols = slice(head * head_size, (head + 1) * head_size)
        up = up_ref[first:, cols].astype(jnp.float32)
        down = down_ref[first:, cols].astype(jnp.float32)
        for_own = jnp.where(core_ref[0] == 0, up, down)
        for_mate = jnp.where(core_ref[0] == 0, down, up)
        grad_key_ref[:, cols] = through_norm(
            raw_ref[:, cols], key_grad_ref[own, cols] + for_own[:frames], k_gain
        )
        grad_value_ref[:, cols] = (value_grad_ref[own, cols] + for_own[frames:]).astype(
            jnp.bfloat16
        )
        to_mate_ref[2 * frames : 3 * frames, cols] = through_norm(
            mate_ref[mate_keys : mate_keys + frames, cols],
            key_grad_ref[mate, cols] + for_mate[:frames],
            k_gain,
        )
        to_mate_ref[3 * frames :, cols] = (
            value_grad_ref[mate, cols] + for_mate[frames:]
        ).astype(jnp.bfloat16)


def finish_audio(core, chunk, gains, raw, mate, key_grad, value_grad, up, down, ready, carried):
    frames, width = raw.shape
    head_size = gains.shape[1]
    size = width // 2 // CHUNKS
    step = size // 2

    def columns(array):
        return pl.BlockSpec((array.shape[0], step), lambda i, core: (0, i))

    own = pl.BlockSpec((frames, step), lambda i, core: (0, (core[0] * CHUNKS + chunk) * 2 + i))
    arrays = (mate, key_grad, value_grad, up, down, ready)
    return pl.pallas_call(
        functools.partial(finish_audio_kernel, head_size),
        grid_spec=pltpu.PrefetchScalarGridSpec(
            num_scalar_prefetch=1,
            grid=(2,),
            in_specs=[pl.BlockSpec(gains.shape, lambda i, core: (0, 0)), own]
            + [columns(array) for array in arrays]
            + [pl.BlockSpec(memory_space=pl.ANY)] * len(carried),
            out_specs=[own] * 2 + [pl.BlockSpec((4 * frames, step), lambda i, core: (0, i))],
        ),
        out_shape=[jax.ShapeDtypeStruct((frames, width), jnp.bfloat16)] * 2
        + [jax.ShapeDtypeStruct((4 * frames, size), jnp.bfloat16)],
        input_output_aliases={9 + i: i for i in range(len(carried))},
        compiler_params=params(),
        cost_estimate=pl.CostEstimate(
            flops=40 * frames * size, bytes_accessed=40 * frames * size, transcendentals=0
        ),
        name="finish_audio",
    )(core, gains, raw, *arrays, *carried)


def relay_kernel(third_ref, sum_ref, left_ref, right_ref, up_ref, down_ref):
    rows = third_ref.shape[0]
    total = (third_ref[...].astype(jnp.float32) + sum_ref[...].astype(jnp.float32)).astype(
        jnp.bfloat16
    )
    up_ref[0:rows, :] = total
    up_ref[rows:, :] = right_ref[...]
    down_ref[0:rows, :] = total
    down_ref[rows:, :] = left_ref[...]


def relay(third, far_sum, to_left, to_right):
    rows, size = third.shape
    step = size // 2
    out_rows = rows + to_left.shape[0]

    def columns(count):
        return pl.BlockSpec((count, step), lambda i: (0, i))

    return pl.pallas_call(
        relay_kernel,
        grid=(2,),
        in_specs=[columns(rows)] * 2 + [columns(to_left.shape[0])] * 2,
        out_specs=[columns(out_rows)] * 2,
        out_shape=[jax.ShapeDtypeStruct((out_rows, size), jnp.bfloat16)] * 2,
        compiler_params=params(),
        cost_estimate=pl.CostEstimate(
            flops=rows * size, bytes_accessed=8 * out_rows * size, transcendentals=0
        ),
        name="relay",
    )(third, far_sum, to_left, to_right)


def finish_lyric_kernel(head_size, gain_ref, raw_ref, *refs):
    rows = raw_ref.shape[0] // 4
    parts, out_refs = refs[:-2], refs[-2:]
    k_gain = gain_ref[1:2, :]
    for head in range(raw_ref.shape[1] // head_size):
        cols = slice(head * head_size, (head + 1) * head_size)
        total = parts[0][:, cols].astype(jnp.float32)
        for part in parts[1:]:
            total = total + part[:, cols].astype(jnp.float32)
        for index, ref in enumerate(out_refs):
            base = 2 * rows * index
            ref[0:rows, cols] = through_norm(
                raw_ref[base : base + rows, cols], total[base : base + rows], k_gain
            )
            ref[rows:, cols] = total[base + rows : base + 2 * rows].astype(jnp.bfloat16)


def finish_lyric(gains, raw, parts):
    rows, size = parts[0].shape
    head_size = gains.shape[1]
    step = size // 2
    spec = pl.BlockSpec((rows, step), lambda i: (0, i))
    out = pl.BlockSpec((rows // 2, step), lambda i: (0, i))
    return pl.pallas_call(
        functools.partial(finish_lyric_kernel, head_size),
        grid=(2,),
        in_specs=[pl.BlockSpec(gains.shape, lambda i: (0, 0)), spec] + [spec] * len(parts),
        out_specs=[out] * 2,
        out_shape=[jax.ShapeDtypeStruct((rows // 2, size), jnp.bfloat16)] * 2,
        compiler_params=params(),
        cost_estimate=pl.CostEstimate(
            flops=20 * rows * size, bytes_accessed=10 * rows * size, transcendentals=0
        ),
        name="finish_lyric",
    )(gains, raw, *parts)


def join_kernel(core_ref, *refs):
    grad_key_ref, grad_value_ref = refs[-2:]
    chunks = len(refs) // 2 - 1
    rows, size = grad_key_ref.shape[0], refs[0].shape[1]
    for part, parts in ((core_ref[0], refs[:chunks]), (1 - core_ref[0], refs[chunks:-2])):
        for chunk, ref in enumerate(parts):
            cols = pl.ds(pl.multiple_of((part * chunks + chunk) * size, size), size)
            grad_key_ref[:, cols] = ref[0:rows, :]
            grad_value_ref[:, cols] = ref[rows:, :]


def join_lyric(core, own, mate):
    rows, size = own[0].shape
    width = 2 * len(own) * size
    return pl.pallas_call(
        join_kernel,
        grid_spec=pltpu.PrefetchScalarGridSpec(
            num_scalar_prefetch=1,
            grid=(1,),
            in_specs=[pl.BlockSpec((rows, size), lambda i, core: (0, 0))] * (2 * len(own)),
            out_specs=[pl.BlockSpec((rows // 2, width), lambda i, core: (0, 0))] * 2,
        ),
        out_shape=[jax.ShapeDtypeStruct((rows // 2, width), jnp.bfloat16)] * 2,
        compiler_params=params(),
        name="join_lyric",
    )(core, *own, *mate)


def norm_lyric_kernel(head_size, gain_ref, raw_ref, grad_ref, out_ref):
    for head in range(raw_ref.shape[1] // head_size):
        cols = slice(head * head_size, (head + 1) * head_size)
        out_ref[:, cols] = through_norm(raw_ref[:, cols], grad_ref[:, cols], gain_ref[1:2, :])


def norm_lyric(gains, raw, grad):
    return pl.pallas_call(
        functools.partial(norm_lyric_kernel, gains.shape[1]),
        out_shape=jax.ShapeDtypeStruct(raw.shape, jnp.bfloat16),
        name="norm_lyric",
    )(gains, raw, grad)


def sum_over(total, axis, bits):
    count = lax.axis_size(axis)
    for bit in bits:
        total = total + lax.ppermute(total, axis, [(i, i ^ bit) for i in range(count)])
    return total


def tie_kernel(block_ref, *refs):
    refs[-1][...] = block_ref[...]


def tie(block, after):
    return pl.pallas_call(
        tie_kernel,
        in_specs=[pl.BlockSpec(memory_space=pltpu.VMEM)]
        + [pl.BlockSpec(memory_space=pl.ANY)] * len(after),
        out_shape=jax.ShapeDtypeStruct(block.shape, block.dtype),
        name="tie",
    )(block, *after)


def bits_of(count):
    return [1 << bit for bit in range(count.bit_length() - 1)]


def body(
    queries, keys, values, lyric_keys, lyric_values, q_gain, k_gain, cotangent, alignment, lyric_len
):
    frames = queries.shape[1]
    lyric_local, width = lyric_keys.shape[1:]
    count = lax.axis_size("seq")
    songs = lax.axis_size("song")
    me = lax.axis_index("seq")
    core = me % 2
    chips = count // 2
    chip = me // 2
    core_array = core.astype(jnp.int32).reshape(1)
    gains = jnp.stack([q_gain, k_gain])

    swap = [(i, i ^ 1) for i in range(count)]
    above = [(a, a + 1) for a in range(chips - 1)]
    below = [(a + 1, a) for a in range(chips - 1)]

    def hop(block, moves):
        pairs = [(2 * a + c, 2 * b + c) for a, b in moves for c in (0, 1)]
        return lax.ppermute(block, "seq", pairs)

    hops = chips == 4 and lyric_local % 16 == 0
    total_rows = lyric_local * count
    mate_align = lax.ppermute(alignment, "seq", swap)
    if hops:
        run = ((0, lyric_local, lyric_local), (2 * lyric_local, 3 * lyric_local, lyric_local))
        groups = (run,) * 4
        owners = [
            chip,
            jnp.where(chip == 0, 3, chip - 1),
            jnp.where(chip == 3, 0, chip + 1),
            jnp.where(chip <= 1, chip + 2, chip - 2),
        ]
        first_rows = []
        for owner in owners:
            first_rows += [
                (2 * owner + core) * lyric_local,
                (2 * owner + 1 - core) * lyric_local,
            ]
    else:
        gathered = jnp.concatenate(
            [
                lax.all_gather(lyric_keys[0], "seq", axis=0, tiled=True),
                lax.all_gather(lyric_values[0], "seq", axis=0, tiled=True),
            ],
            axis=0,
        )
        groups = (((0, total_rows, total_rows),),)
        first_rows = [0]
    has_left, has_right = chip > 0, chip < chips - 1
    has_near = jnp.where(core == 0, has_left, has_right)
    has_far = jnp.where(core == 0, has_right, has_left)
    meta = jnp.stack(
        [
            jnp.asarray(value, jnp.int32)
            for value in [core]
            + [alignment[0, 0, slot] for slot in range(TILES)]
            + [mate_align[0, 0, slot] for slot in range(TILES)]
            + [lyric_len[0], has_near, has_far, chip]
            + first_rows
        ]
    )

    rows = 4 * lyric_local
    attended = []
    carried = []
    after = []
    for chunk in range(CHUNKS):
        to_mate = pack(
            core_array,
            chunk,
            [lyric_keys[0], lyric_values[0], queries[0], cotangent[0], keys[0], values[0]],
        )
        mate = lax.ppermute(to_mate, "seq", swap)
        up, down = merge(
            core_array, chunk, keys[0], values[0], lyric_keys[0], lyric_values[0], mate, hops,
            after,
        )
        up_one, down_one = hop(up, above), hop(down, below)
        after = [up_one, down_one]
        if hops:
            up_two = hop(up_one[:rows], [(1, 2), (2, 3)])
            down_two = hop(down_one[:rows], [(1, 0), (2, 1)])
            far_end = hop(jnp.where(chip == 2, up_two, down_two), [(2, 3), (1, 0)])
            lyrics = [up, up_two, down_two, far_end]
        else:
            lyrics = [gathered]
        results = attention(
            chunk, meta, gains, queries[0], cotangent[0], keys[0], values[0], mate, up_one,
            down_one, lyrics, groups, carried,
        )
        carried = results[:2]
        attended.append((results[2:], lyrics, mate))
    output, grad_queries = carried

    grads = []
    own_halves, mate_halves, lyric_cols, from_mates = [], [], [], []
    for chunk, (results, lyrics, mate) in enumerate(attended):
        for_mate, key_grad, value_grad, to_left, to_right = results[:5]
        parts = results[5:-1]
        if hops:
            held, first, second, third = parts
            far_sum = hop(jnp.where(chip == 0, first, second), [(0, 1), (3, 2)])
            to_up, to_down = relay(third, far_sum, to_left, to_right)
        else:
            to_up, to_down = to_right, to_left
        up_two, down_two = hop(to_up, above), hop(to_down, below)
        sent = to_up
        if hops:
            to_up, to_down = second + up_two[:rows], first + down_two[:rows]
            up_one, down_one = hop(to_up, above), hop(to_down, below)
            own_half, mate_half = finish_lyric(gains, lyrics[0], [held, up_one, down_one])
            own_halves.append(own_half)
            mate_halves.append(lax.ppermute(mate_half, "seq", swap))
        else:
            lyric_cols.append(parts[0])
        *grads, for_mate = finish_audio(
            core_array, chunk, gains, keys[0], mate, key_grad, value_grad, up_two, down_two,
            for_mate, grads,
        )
        from_mates.append(lax.ppermute(for_mate, "seq", swap))
    filled = [output, grad_queries, *grads]
    for chunk, from_mate in enumerate(from_mates):
        filled = fill_other(core_array, chunk, filled, from_mate)
    output, grad_queries, grad_keys, grad_values = filled
    gain_total = sum(results[-1] for results, _, _ in attended)
    if (count & (count - 1)) or (songs & (songs - 1)):
        gain_total = lax.psum(gain_total, ("song", "seq"))
    else:
        gain_total = sum_over(tie(gain_total, [sent]), "song", bits_of(songs))
        gain_total = sum_over(tie(gain_total, [to_up, to_down]), "seq", bits_of(count))
    if hops:
        grad_lyric_keys, grad_lyric_values = join_lyric(core_array, own_halves, mate_halves)
    else:
        spread = lax.dynamic_update_slice(
            jnp.zeros((2 * total_rows, width), jnp.float32),
            jnp.concatenate(lyric_cols, axis=1).astype(jnp.float32),
            (0, core * (width // 2)),
        )
        lyric_key_sum, grad_lyric_values = [
            lax.psum_scatter(part, "seq", scatter_dimension=0, tiled=True)
            for part in (spread[:total_rows], spread[total_rows:])
        ]
        grad_lyric_keys = norm_lyric(gains, lyric_keys[0], lyric_key_sum)
        grad_lyric_values = grad_lyric_values.astype(jnp.bfloat16)
    return (
        output[None],
        grad_queries[None],
        grad_keys[None],
        grad_values[None],
        grad_lyric_keys[None],
        grad_lyric_values[None],
        gain_total[0],
        gain_total[1],
    )


def solution(mesh):
    split = P("song", "seq", None)
    return jax.shard_map(
        body,
        mesh=mesh,
        in_specs=(split, split, split, split, split, P(), P(), split, split, P("song")),
        out_specs=(split, split, split, split, split, split, P(), P()),
        check_vma=False,
    )
```

time: 163 us -> 163 us (level)
  blocking collectives: 64.9 us -> 0 us
  starting transfers between devices: 24.4 us -> 66.3 us
  local copies, waits for them, and re-layouts: 12.8 us -> 28.5 us
  Pallas kernels: 22 us -> 33 us
  waiting for transfers between devices: 36.1 us -> 26.5 us
  other arithmetic: 0.73 us -> 5.74 us
    all_gather x1 -> x0, blocking collectives: 64.9 us -> none  [body(): gain_total = jnp.sum(lax.all_gather(gain_part, ('song', 'seq')), axis=0)]
    ppermute x12 -> x29, starting transfers between devices: 17.8 us -> 65.8 us  [the longest x20 57.2 us: hop(): return lax.ppermute(block, 'seq', pairs)]
    unnamed x28 -> x100, local copies, waits for them, and re-layouts: 8.39 us -> 20.6 us
    ppermute x12 -> x29, waiting for transfers between devices: 36.1 us -> 24.8 us  [the longest x20 18.9 us: hop(): return lax.ppermute(block, 'seq', pairs)]
    pallas_call x2 -> x10, Pallas kernels: 15.8 us -> 24.5 us  [the longest x2 15.8 us: attention(): pl.pallas_call(functools.partial(attention_kernel, groups, len(carried) /...]
    ppermute x1, starting transfers between devices: 6.06 us -> 0.01 us  [body(): mate_align = lax.ppermute(alignment, 'seq', swap)]
    add x0 -> x10, other arithmetic: none -> 4.96 us  [the longest x4 3.07 us: body(): to_up, to_down = (second + up_two[:rows], first + down_two[:rows])]
    slice x1 -> x4, local copies, waits for them, and re-layouts: 0.01 us -> 3.5 us  [the longest x2 1.87 us: body(): down_two = hop(down_one[:rows], [(1, 0), (2, 1)])]
  transfers between devices with their start and end apart: 14 -> 32, of which waited for: 5 -> 7; matrix products, arithmetic and copies ran while one was open for 3% -> 8% of each run, Pallas kernels for 2% -> 19%
where the time goes in v3:
time: 163 us; the launch traced here: 162 us
  starting transfers between devices  66.3 us (41%)
  Pallas kernels  33 us (20%)
  local copies, waits for them, and re-layouts  28.5 us (17%)
  waiting for transfers between devices  26.5 us (16%)
  other arithmetic  5.74 us (4%)
  between operations  1.75 us (1%)
    ppermute x20, starting transfers between devices, hop(): return lax.ppermute(block, 'seq', pairs)  57.2 us
    unnamed x100, local copies, waits for them, and re-layouts  20.6 us
    ppermute x20, waiting for transfers between devices, hop(): return lax.ppermute(block, 'seq', pairs)  18.9 us
    pallas_call x2, Pallas kernels, attention(): pl.pallas_call(functools.partial(attention_kernel, groups, len(carried) /...  15.8 us
    ppermute x5, starting transfers between devices, sum_over(): lax.ppermute(total, axis, [(i, i ^ bit) for i in range(count)])  7.99 us
    ppermute x5, waiting for transfers between devices, sum_over(): lax.ppermute(total, axis, [(i, i ^ bit) for i in range(count)])  5.91 us
    pallas_call x2, Pallas kernels, finish_audio(): pl.pallas_call(functools.partial(finish_audio_kernel, head_size), grid_sp...  3.79 us
  transfers between devices with their start and end apart: 32, of which 7 were waited for; matrix products, arithmetic and copies ran while one was open for 8% of the time, Pallas kernels for 19%

profile of v3, /device:TPU:0, one launch (start us, length us, event | category | flops | bytes accessed | tf_op | source)
XLA Modules:
  0.0 161.8 jit_solution(10291350984255736358)
XLA Ops:
  0.7 1.0 copy-done
  1.7 1.0 copy-done.2
  2.7 1.0 copy-done.4
  3.8 1.0 copy-done.6
  4.8 0.9 copy-done.8
  5.7 0.9 copy-done.10
  7.5 1.7 %collective-permute-done.2.mate_ref = bf16[608,512]{1,0:T(8,128)(2,1)S(1)} collective-permute-done((bf16[608,512]{1,0:T(8,128)(2,1)S(1)}, bf16[608,512]{1,0:T(8,128)(2,1)S(1)}, u32[]{:S(2)}, u32[]{:S(2)}) %collective-permute-start.2) | collective-permute-done | bytes 622624 | tf_op jit(solution)/shard_map/ppermute | solution.py:661
  9.6 1.3 collective-permute-start.4
  10.9 5.5 %collective-permute-start.3 = (bf16[448,512]{1,0:T(8,128)(2,1)S(1)}, bf16[448,512]{1,0:T(8,128)(2,1)S(1)}, u32[]{:S(2)}, u32[]{:S(2)}) collective-permute-start(bf16[448,512]{1,0:T(8,128)(2,1)S(1)} %get-tuple-element.60.refs_0_.raw_ref), channel_id=1, source_target_pairs={{0,2},{1,3},{2,4},{3,5},{4,6},{5,7},{8,10},{9,11},{10,12},{11,13},... | collective-permute-start | bytes 1376264 | tf_op jit(solution)/shard_map/ppermute | solution.py:607
  16.4 1.1 pack.2
  17.5 7.7 %collective-permute-done.4.refs_1_.down_ref = bf16[448,512]{1,0:T(8,128)(2,1)S(1)} collective-permute-done((bf16[448,512]{1,0:T(8,128)(2,1)S(1)}, bf16[448,512]{1,0:T(8,128)(2,1)S(1)}, u32[]{:S(2)}, u32[]{:S(2)}) %collective-permute-start.4) | collective-permute-done | bytes 458784 | tf_op jit(solution)/shard_map/ppermute | solution.py:607
  26.7 1.4 collective-permute-start.11
  29.6 1.3 collective-permute-start.10
  32.2 1.0 copy-done.13
  33.3 1.0 copy-done.16
  34.3 1.1 merge.3
  35.4 1.4 collective-permute-start.6
  36.8 8.9 %collective-permute-start.5 = (bf16[448,512]{1,0:T(8,128)(2,1)}, bf16[448,512]{1,0:T(8,128)(2,1)}, u32[]{:S(2)}, u32[]{:S(2)}) collective-permute-start(bf16[448,512]{1,0:T(8,128)(2,1)} %get-tuple-element.62.refs_0_.raw_ref), channel_id=1, source_target_pairs={{0,2},{1,3},{2,4},{3,5},{4,6},{5,7},{8,10},{9,11},{10,12},{11,13},... | collective-permute-start | bytes 1376264 | tf_op jit(solution)/shard_map/ppermute | solution.py:607
  46.5 1.3 collective-permute-start.12
  49.1 2.7 %stack.68.meta_ref = s32[17]{0:T(128)S(1)} concatenate(s32[1]{0:T(128)} %bitcast.core_ref, s32[1]{0:T(128)} %bitcast.9, s32[1]{0:T(128)} %bitcast.10, s32[1]{0:T(128)} %bitcast.11, s32[1]{0:T(128)} %bitcast.12, s32[1]{0:T(128)S(6)} %copy.42, s32[1]{0:T(128)} %bitcast.13, s32[1]{0:T(128)} %bitcast.14, s32[1]{0:T(128)} %bitcast.15, s32[1]{0:T(128)} %bitcast.16, s32[1]{0:T(128)} %bitcast.17, ...), dimensions={0} | concatenate | bytes 136 | tf_op jit(solution)/shard_map/stack | solution.py:640
  51.7 7.1 %collective-permute-done.12.refs_3_ = bf16[192,512]{1,0:T(8,128)(2,1)} collective-permute-done((bf16[192,512]{1,0:T(8,128)(2,1)}, bf16[192,512]{1,0:T(8,128)(2,1)}, u32[]{:S(2)}, u32[]{:S(2)}) %collective-permute-start.12) | collective-permute-done | bytes 196640 | tf_op jit(solution)/shard_map/ppermute | solution.py:607
  58.8 1.0 copy-done.14
  59.8 1.0 copy-done.17
  60.8 1.0 copy-done.19
  61.9 7.9 %attention.2 = (bf16[128,2048]{1,0:T(8,128)(2,1)}, bf16[128,2048]{1,0:T(8,128)(2,1)}, bf16[256,512]{1,0:T(8,128)(2,1)S(1)}, f32[256,512]{1,0:T(8,128)S(1)}, f32[...) custom-call(s32[17]{0:T(128)S(1)} %stack.68.meta_ref, ...), custom_call_target="tpu_custom_call" | custom-call | flops 1207959552 | bytes 8388608 | tf_op jit(solution)/shard_map/attention/pallas_call | solution.py:309
  69.7 0.8 copy-done.33
  71.9 1.2 slice.57
  73.1 1.3 collective-permute-start.8
  74.4 0.9 slice.56
  76.1 6.4 %collective-permute-start.16 = (bf16[192,512]{1,0:T(8,128)(2,1)S(1)}, bf16[192,512]{1,0:T(8,128)(2,1)S(1)}, u32[]{:S(2)}, u32[]{:S(2)}) collective-permute-start(bf16[192,512]{1,0:T(8,128)(2,1)S(1)} %broadcast_select_fusion), channel_id=1, source_target_pairs={{0,2},{1,3},{6,4},{7,5},{8,10},{9,11},{14,12},{15,13},{16,18},{17,... | collective-permute-start | bytes 589832 | tf_op jit(solution)/shard_map/ppermute | solution.py:607
  82.5 1.3 collective-permute-start.9
  83.8 2.2 %collective-permute-done.16.sum_ref = bf16[192,512]{1,0:T(8,128)(2,1)S(1)} collective-permute-done((bf16[192,512]{1,0:T(8,128)(2,1)S(1)}, bf16[192,512]{1,0:T(8,128)(2,1)S(1)}, u32[]{:S(2)}, u32[]{:S(2)}) %collective-permute-start.16) | collective-permute-done | bytes 196640 | tf_op jit(solution)/shard_map/ppermute | solution.py:607
  86.0 1.0 relay.3
  87.0 5.2 %collective-permute-start.17 = (bf16[448,512]{1,0:T(8,128)(2,1)}, bf16[448,512]{1,0:T(8,128)(2,1)}, u32[]{:S(2)}, u32[]{:S(2)}) collective-permute-start(bf16[448,512]{1,0:T(8,128)(2,1)} %get-tuple-element.83), channel_id=1, source_target_pairs={{0,2},{1,3},{2,4},{3,5},{4,6},{5,7},{8,10},{9,11},{10,12},{11,13},... | collective-permute-start | bytes 1376264 | tf_op jit(solution)/shard_map/ppermute | solution.py:607
  92.2 7.9 %attention.3 = (bf16[128,2048]{1,0:T(8,128)(2,1)}, bf16[128,2048]{1,0:T(8,128)(2,1)}, bf16[256,512]{1,0:T(8,128)(2,1)S(1)}, f32[256,512]{1,0:T(8,128)S(1)}, f32[...) custom-call(s32[17]{0:T(128)S(1)} %stack.68.meta_ref, ...), custom_call_target="tpu_custom_call", output_to_operand_aliasing={{0}: (13, {}), {1}: (14, {})} | custom-call | flops 1207959552 | bytes 8388608 | tf_op jit(solution)/shard_map/attention/pallas_call | solution.py:309
  102.2 3.3 %collective-permute-start.13 = (bf16[192,512]{1,0:T(8,128)(2,1)S(1)}, bf16[192,512]{1,0:T(8,128)(2,1)S(1)}, u32[]{:S(2)}, u32[]{:S(2)}) collective-permute-start(bf16[192,512]{1,0:T(8,128)(2,1)S(1)} %broadcast_select_fusion.1), channel_id=1, source_target_pairs={{0,2},{1,3},{6,4},{7,5},{8,10},{9,11},{14,12},{15,13},{16,18},{17,... | collective-permute-start | bytes 589832 | tf_op jit(solution)/shard_map/ppermute | solution.py:607
  105.5 1.3 collective-permute-start.18
  106.8 1.9 %collective-permute-done.13.sum_ref = bf16[192,512]{1,0:T(8,128)(2,1)S(1)} collective-permute-done((bf16[192,512]{1,0:T(8,128)(2,1)S(1)}, bf16[192,512]{1,0:T(8,128)(2,1)S(1)}, u32[]{:S(2)}, u32[]{:S(2)}) %collective-permute-start.13) | collective-permute-done | bytes 196640 | tf_op jit(solution)/shard_map/ppermute | solution.py:607
  108.6 0.9 relay.2
  109.6 1.3 collective-permute-start.15
  111.5 1.3 tie.2
  112.8 1.5 collective-permute-start.27
  114.3 5.0 %collective-permute-start.14 = (bf16[448,512]{1,0:T(8,128)(2,1)}, bf16[448,512]{1,0:T(8,128)(2,1)S(1)}, u32[]{:S(2)}, u32[]{:S(2)}) collective-permute-start(bf16[448,512]{1,0:T(8,128)(2,1)} %copy-done.35), channel_id=1, source_target_pairs={{0,2},{1,3},{2,4},{3,5},{4,6},{5,7},{8,10},{9,11},{10,12},{11,13},... | collective-permute-start | bytes 1376264 | tf_op jit(solution)/shard_map/ppermute | solution.py:607
  120.0 1.5 collective-permute-start.28
  121.5 1.6 %slice_add_fusion.3 = bf16[192,512]{1,0:T(8,128)(2,1)} fusion(bf16[192,512]{1,0:T(8,128)(2,1)S(1)} %copy-done.24, bf16[448,512]{1,0:T(8,128)(2,1)} %collective-permute-done.17.up_ref), kind=kLoop, calls=%fused_computation.3 | loop fusion | flops 98304 | bytes 589824 | tf_op jit(solution)/shard_map/add | solution.py:697
  123.2 6.2 %collective-permute-start.21 = (bf16[192,512]{1,0:T(8,128)(2,1)}, bf16[192,512]{1,0:T(8,128)(2,1)}, u32[]{:S(2)}, u32[]{:S(2)}) collective-permute-start(bf16[192,512]{1,0:T(8,128)(2,1)} %slice_add_fusion.3), channel_id=1, source_target_pairs={{0,2},{1,3},{2,4},{3,5},{4,6},{5,7},{8,10},{9,11},{10,12},{11,13},... | collective-permute-start | bytes 589832 | tf_op jit(solution)/shard_map/ppermute | solution.py:607
  129.4 1.0 copy-done.34
  130.4 0.9 copy-done.39
  131.3 2.3 %finish_audio.2 = (bf16[128,2048]{1,0:T(8,128)(2,1)}, bf16[128,2048]{1,0:T(8,128)(2,1)}, bf16[512,512]{1,0:T(8,128)(2,1)}) custom-call(s32[1]{0:T(128)} %bitcast.core_ref, f32[2,128]{1,0:T(2,128)S(1)} %pad_maximum_fusion.gain_ref, bf16[128,2048]{1,0:T(8,128)(2,1)S(1)} %bitcast.40, bf16[608,512]{1,0:T(8,128)(2,1)S(1)} %collective-permute-done.2.mate_ref, ...), custom_call_target="tpu_custom_call" | custom-call | flops 2621440 | bytes 2621440 | tf_op jit(solution)/shard_map/finish_audio/pallas_call | solution.py:429
  135.7 1.3 tie.3
  137.5 1.0 copy-done.30
  138.6 1.5 finish_audio.3
  140.1 1.4 collective-permute-start.22
  141.6 2.7 %collective-permute-start.30 = (f32[8,128]{1,0:T(8,128)S(1)}, f32[8,128]{1,0:T(8,128)S(1)}, u32[]{:S(2)}, u32[]{:S(2)}) collective-permute-start(f32[8,128]{1,0:T(8,128)S(1)} %add.85), channel_id=1, source_target_pairs={{0,2},{1,3},{2,0},{3,1},{4,6},{5,7},{6,4},{7,5},{8,10},{9,11},{10,... | collective-permute-start | bytes 12296 | tf_op jit(solution)/shard_map/ppermute | solution.py:565
  144.3 1.3 collective-permute-start.24
  145.6 4.4 %collective-permute-done.30 = f32[8,128]{1,0:T(8,128)S(1)} collective-permute-done((f32[8,128]{1,0:T(8,128)S(1)}, f32[8,128]{1,0:T(8,128)S(1)}, u32[]{:S(2)}, u32[]{:S(2)}) %collective-permute-start.30) | collective-permute-done | bytes 4128 | tf_op jit(solution)/shard_map/ppermute | solution.py:565
  149.9 1.4 collective-permute-start.23
  151.4 1.8 %collective-permute-start.31 = (f32[8,128]{1,0:T(8,128)S(1)}, f32[8,128]{1,0:T(8,128)S(1)}, u32[]{:S(2)}, u32[]{:S(2)}) collective-permute-start(f32[8,128]{1,0:T(8,128)S(1)} %add.86), channel_id=1, source_target_pairs={{0,4},{1,5},{2,6},{3,7},{4,0},{5,1},{6,2},{7,3},{8,12},{9,13},{10,... | collective-permute-start | bytes 12296 | tf_op jit(solution)/shard_map/ppermute | solution.py:565
  153.2 1.3 finish_lyric.2
  154.5 1.5 collective-permute-done.31
  156.0 1.2 finish_lyric.3
  158.3 1.8 %fill_other.2 = (bf16[128,2048]{1,0:T(8,128)(2,1)}, bf16[128,2048]{1,0:T(8,128)(2,1)}, bf16[128,2048]{1,0:T(8,128)(2,1)}, bf16[128,2048]{1,0:T(8,128)(2,1)}) custom-call(s32[1]{0:T(128)} %bitcast.core_ref, bf16[512,512]{1,0:T(8,128)(2,1)} %collective-permute-done.20.mate_ref, ...), custom_call_target="tpu_custom_call", output_to_operand_aliasing={{0}: (2, {}), {1}: (3, {}), {2}: (4, {}), {3}: (5, {})} | custom-call | bytes 1048576 | tf_op jit(solution)/shard_map/fill_other/pallas_call | solution.py:356
  160.1 0.8 join_lyric.1
  160.9 0.9 fill_other.3
  (140 shorter events, 16.0 us)
Async XLA Ops:
  0.6 1.0 copy-start
  1.7 1.0 copy-start.2
  2.7 1.0 copy-start.4
  3.8 1.0 copy-start.6
  6.7 2.6 %copy-start.1 = (bf16[1,128,2048]{2,1,0:T(8,128)(2,1)S(1)}, bf16[1,128,2048]{2,1,0:T(8,128)(2,1)}, u32[]{:S(2)}) copy-start(bf16[1,128,2048]{2,1,0:T(8,128)(2,1)} %param.11) | copy-start | bytes 1572868
  6.7 2.6 %copy-start.3 = (bf16[1,128,2048]{2,1,0:T(8,128)(2,1)S(1)}, bf16[1,128,2048]{2,1,0:T(8,128)(2,1)}, u32[]{:S(2)}) copy-start(bf16[1,128,2048]{2,1,0:T(8,128)(2,1)} %param.12) | copy-start | bytes 1572868
  7.0 2.2 %collective-permute-start.2 = (bf16[608,512]{1,0:T(8,128)(2,1)S(1)}, bf16[608,512]{1,0:T(8,128)(2,1)S(1)}, u32[]{:S(2)}, u32[]{:S(2)}) collective-permute-start(bf16[608,512]{1,0:T(8,128)(2,1)S(1)} %pack.3), channel_id=1, source_target_pairs={{0,1},{1,0},{2,3},{3,2},{4,5},{5,4},{6,7},{7,6},{8,9},{9,8},{10,11... | collective-permute-start | bytes 1867784 | tf_op jit(solution)/shard_map/ppermute | solution.py:661
  9.6 7.9 %copy-start.18 = (bf16[448,512]{1,0:T(8,128)(2,1)}, bf16[448,512]{1,0:T(8,128)(2,1)S(1)}, u32[]{:S(2)}) copy-start(bf16[448,512]{1,0:T(8,128)(2,1)S(1)} %get-tuple-element.60.refs_0_.raw_ref) | copy-start | bytes 1376260
  9.6 15.7 %collective-permute-start.4 = (bf16[448,512]{1,0:T(8,128)(2,1)S(1)}, bf16[448,512]{1,0:T(8,128)(2,1)S(1)}, u32[]{:S(2)}, u32[]{:S(2)}) collective-permute-start(bf16[448,512]{1,0:T(8,128)(2,1)S(1)} %get-tuple-element.61), channel_id=1, source_target_pairs={{2,0},{3,1},{4,2},{5,3},{6,4},{7,5},{10,8},{11,9},{12,10},{13,11},... | collective-permute-start | bytes 1376264 | tf_op jit(solution)/shard_map/ppermute | solution.py:607
  10.9 17.3 %collective-permute-start.3 = (bf16[448,512]{1,0:T(8,128)(2,1)S(1)}, bf16[448,512]{1,0:T(8,128)(2,1)S(1)}, u32[]{:S(2)}, u32[]{:S(2)}) collective-permute-start(bf16[448,512]{1,0:T(8,128)(2,1)S(1)} %get-tuple-element.60.refs_0_.raw_ref), channel_id=1, source_target_pairs={{0,2},{1,3},{2,4},{3,5},{4,6},{5,7},{8,10},{9,11},{10,12},{11,13},... | collective-permute-start | bytes 1376264 | tf_op jit(solution)/shard_map/ppermute | solution.py:607
  17.5 14.7 %collective-permute-start = (bf16[608,512]{1,0:T(8,128)(2,1)}, bf16[608,512]{1,0:T(8,128)(2,1)S(1)}, u32[]{:S(2)}, u32[]{:S(2)}) collective-permute-start(bf16[608,512]{1,0:T(8,128)(2,1)} %pack.2), channel_id=1, source_target_pairs={{0,1},{1,0},{2,3},{3,2},{4,5},{5,4},{6,7},{7,6},{8,9},{9,8},{10,11... | collective-permute-start | bytes 1867784 | tf_op jit(solution)/shard_map/ppermute | solution.py:661
  25.3 5.7 %copy-start.47 = (s32[1,1,2]{2,1,0:T(1,128)S(1)}, s32[1,1,2]{2,1,0:T(1,128)}, u32[]{:S(2)}) copy-start(s32[1,1,2]{2,1,0:T(1,128)} %param.18) | copy-start | bytes 28
  26.7 5.5 %copy-start.9 = (bf16[1,48,2048]{2,1,0:T(8,128)(2,1)S(1)}, bf16[1,48,2048]{2,1,0:T(8,128)(2,1)}, u32[]{:S(2)}) copy-start(bf16[1,48,2048]{2,1,0:T(8,128)(2,1)} %param.13) | copy-start | bytes 589828
  26.7 5.5 %copy-start.11 = (bf16[1,48,2048]{2,1,0:T(8,128)(2,1)S(1)}, bf16[1,48,2048]{2,1,0:T(8,128)(2,1)}, u32[]{:S(2)}) copy-start(bf16[1,48,2048]{2,1,0:T(8,128)(2,1)} %param.14) | copy-start | bytes 589828
  26.7 19.1 %collective-permute-start.11 = (bf16[192,512]{1,0:T(8,128)(2,1)}, bf16[192,512]{1,0:T(8,128)(2,1)S(1)}, u32[]{:S(2)}, u32[]{:S(2)}) collective-permute-start(bf16[192,512]{1,0:T(8,128)(2,1)} %slice.59), channel_id=1, source_target_pairs={{2,0},{3,1},{4,2},{5,3},{10,8},{11,9},{12,10},{13,11},{18,16},{19,... | collective-permute-start | bytes 589832 | tf_op jit(solution)/shard_map/ppermute | solution.py:607
  29.6 16.2 %collective-permute-start.10 = (bf16[192,512]{1,0:T(8,128)(2,1)}, bf16[192,512]{1,0:T(8,128)(2,1)}, u32[]{:S(2)}, u32[]{:S(2)}) collective-permute-start(bf16[192,512]{1,0:T(8,128)(2,1)} %slice.58), channel_id=1, source_target_pairs={{2,4},{3,5},{4,6},{5,7},{10,12},{11,13},{12,14},{13,15},{18,20},{1... | collective-permute-start | bytes 589832 | tf_op jit(solution)/shard_map/ppermute | solution.py:607
  31.0 17.5 %collective-permute-start.1 = (s32[1,1,2]{2,1,0:T(1,128)S(1)}, s32[1,1,2]{2,1,0:T(1,128)S(1)}, u32[]{:S(2)}, u32[]{:S(2)}) collective-permute-start(s32[1,1,2]{2,1,0:T(1,128)S(1)} %copy-done.47), channel_id=1, source_target_pairs={{0,1},{1,0},{2,3},{3,2},{4,5},{5,4},{6,7},{7,6},{8,9},{9,8},{10,11... | collective-permute-start | bytes 32 | tf_op jit(solution)/shard_map/ppermute | solution.py:611
  34.3 24.5 %copy-start.7 = (bf16[1,128,2048]{2,1,0:T(8,128)(2,1)S(1)}, bf16[1,128,2048]{2,1,0:T(8,128)(2,1)}, u32[]{:S(2)}) copy-start(bf16[1,128,2048]{2,1,0:T(8,128)(2,1)} %param.17) | copy-start | bytes 1572868
  35.4 23.4 %copy-start.5 = (bf16[1,128,2048]{2,1,0:T(8,128)(2,1)S(1)}, bf16[1,128,2048]{2,1,0:T(8,128)(2,1)}, u32[]{:S(2)}) copy-start(bf16[1,128,2048]{2,1,0:T(8,128)(2,1)} %param.10) | copy-start | bytes 1572868
  35.4 36.5 %collective-permute-start.6 = (bf16[448,512]{1,0:T(8,128)(2,1)}, bf16[448,512]{1,0:T(8,128)(2,1)}, u32[]{:S(2)}, u32[]{:S(2)}) collective-permute-start(bf16[448,512]{1,0:T(8,128)(2,1)} %get-tuple-element.63), channel_id=1, source_target_pairs={{2,0},{3,1},{4,2},{5,3},{6,4},{7,5},{10,8},{11,9},{12,10},{13,11},... | collective-permute-start | bytes 1376264 | tf_op jit(solution)/shard_map/ppermute | solution.py:607
  36.8 37.6 %collective-permute-start.5 = (bf16[448,512]{1,0:T(8,128)(2,1)}, bf16[448,512]{1,0:T(8,128)(2,1)}, u32[]{:S(2)}, u32[]{:S(2)}) collective-permute-start(bf16[448,512]{1,0:T(8,128)(2,1)} %get-tuple-element.62.refs_0_.raw_ref), channel_id=1, source_target_pairs={{0,2},{1,3},{2,4},{3,5},{4,6},{5,7},{8,10},{9,11},{10,12},{11,13},... | collective-permute-start | bytes 1376264 | tf_op jit(solution)/shard_map/ppermute | solution.py:607
  46.5 12.3 %collective-permute-start.12 = (bf16[192,512]{1,0:T(8,128)(2,1)}, bf16[192,512]{1,0:T(8,128)(2,1)}, u32[]{:S(2)}, u32[]{:S(2)}) collective-permute-start(bf16[192,512]{1,0:T(8,128)(2,1)} %broadcast_select_fusion.2), channel_id=1, source_target_pairs={{4,6},{5,7},{2,0},{3,1},{12,14},{13,15},{10,8},{11,9},{20,22},{21,... | collective-permute-start | bytes 589832 | tf_op jit(solution)/shard_map/ppermute | solution.py:607
  71.9 4.1 %copy-start.21 = (bf16[192,512]{1,0:T(8,128)(2,1)}, bf16[192,512]{1,0:T(8,128)(2,1)S(1)}, u32[]{:S(2)}) copy-start(bf16[192,512]{1,0:T(8,128)(2,1)S(1)} %get-tuple-element.79) | copy-start | bytes 589828
  71.9 4.1 %copy-start.23 = (bf16[192,512]{1,0:T(8,128)(2,1)}, bf16[192,512]{1,0:T(8,128)(2,1)S(1)}, u32[]{:S(2)}) copy-start(bf16[192,512]{1,0:T(8,128)(2,1)S(1)} %get-tuple-element.80) | copy-start | bytes 589828
  71.9 4.2 %copy-start.31 = (f32[256,512]{1,0:T(8,128)}, f32[256,512]{1,0:T(8,128)S(1)}, u32[]{:S(2)}) copy-start(f32[256,512]{1,0:T(8,128)S(1)} %get-tuple-element.76.key_grad_ref) | copy-start | bytes 1572868
  73.1 9.4 %collective-permute-start.8 = (bf16[192,512]{1,0:T(8,128)(2,1)S(1)}, bf16[192,512]{1,0:T(8,128)(2,1)S(1)}, u32[]{:S(2)}, u32[]{:S(2)}) collective-permute-start(bf16[192,512]{1,0:T(8,128)(2,1)S(1)} %slice.57), channel_id=1, source_target_pairs={{2,0},{3,1},{4,2},{5,3},{10,8},{11,9},{12,10},{13,11},{18,16},{19,... | collective-permute-start | bytes 589832 | tf_op jit(solution)/shard_map/ppermute | solution.py:607
  75.4 7.1 %collective-permute-start.7 = (bf16[192,512]{1,0:T(8,128)(2,1)S(1)}, bf16[192,512]{1,0:T(8,128)(2,1)S(1)}, u32[]{:S(2)}, u32[]{:S(2)}) collective-permute-start(bf16[192,512]{1,0:T(8,128)(2,1)S(1)} %slice.56), channel_id=1, source_target_pairs={{2,4},{3,5},{4,6},{5,7},{10,12},{11,13},{12,14},{13,15},{18,20},{1... | collective-permute-start | bytes 589832 | tf_op jit(solution)/shard_map/ppermute | solution.py:607
  76.1 9.9 %collective-permute-start.16 = (bf16[192,512]{1,0:T(8,128)(2,1)S(1)}, bf16[192,512]{1,0:T(8,128)(2,1)S(1)}, u32[]{:S(2)}, u32[]{:S(2)}) collective-permute-start(bf16[192,512]{1,0:T(8,128)(2,1)S(1)} %broadcast_select_fusion), channel_id=1, source_target_pairs={{0,2},{1,3},{6,4},{7,5},{8,10},{9,11},{14,12},{15,13},{16,18},{17,... | collective-permute-start | bytes 589832 | tf_op jit(solution)/shard_map/ppermute | solution.py:607
  82.5 9.7 %collective-permute-start.9 = (bf16[192,512]{1,0:T(8,128)(2,1)S(1)}, bf16[192,512]{1,0:T(8,128)(2,1)S(1)}, u32[]{:S(2)}, u32[]{:S(2)}) collective-permute-start(bf16[192,512]{1,0:T(8,128)(2,1)S(1)} %broadcast_select_fusion.3), channel_id=1, source_target_pairs={{4,6},{5,7},{2,0},{3,1},{12,14},{13,15},{10,8},{11,9},{20,22},{21,... | collective-permute-start | bytes 589832 | tf_op jit(solution)/shard_map/ppermute | solution.py:607
  87.0 34.5 %collective-permute-start.17 = (bf16[448,512]{1,0:T(8,128)(2,1)}, bf16[448,512]{1,0:T(8,128)(2,1)}, u32[]{:S(2)}, u32[]{:S(2)}) collective-permute-start(bf16[448,512]{1,0:T(8,128)(2,1)} %get-tuple-element.83), channel_id=1, source_target_pairs={{0,2},{1,3},{2,4},{3,5},{4,6},{5,7},{8,10},{9,11},{10,12},{11,13},... | collective-permute-start | bytes 1376264 | tf_op jit(solution)/shard_map/ppermute | solution.py:607
  101.5 8.1 %copy-start.27 = (f32[256,512]{1,0:T(8,128)}, f32[256,512]{1,0:T(8,128)S(1)}, u32[]{:S(2)}) copy-start(f32[256,512]{1,0:T(8,128)S(1)} %get-tuple-element.66.key_grad_ref) | copy-start | bytes 1572868
  101.5 8.1 %copy-start.29 = (f32[256,512]{1,0:T(8,128)}, f32[256,512]{1,0:T(8,128)S(1)}, u32[]{:S(2)}) copy-start(f32[256,512]{1,0:T(8,128)S(1)} %get-tuple-element.67.value_grad_ref) | copy-start | bytes 1572868
  102.2 6.5 %collective-permute-start.13 = (bf16[192,512]{1,0:T(8,128)(2,1)S(1)}, bf16[192,512]{1,0:T(8,128)(2,1)S(1)}, u32[]{:S(2)}, u32[]{:S(2)}) collective-permute-start(bf16[192,512]{1,0:T(8,128)(2,1)S(1)} %broadcast_select_fusion.1), channel_id=1, source_target_pairs={{0,2},{1,3},{6,4},{7,5},{8,10},{9,11},{14,12},{15,13},{16,18},{17,... | collective-permute-start | bytes 589832 | tf_op jit(solution)/shard_map/ppermute | solution.py:607
  105.5 23.9 %collective-permute-start.18 = (bf16[448,512]{1,0:T(8,128)(2,1)}, bf16[448,512]{1,0:T(8,128)(2,1)S(1)}, u32[]{:S(2)}, u32[]{:S(2)}) collective-permute-start(bf16[448,512]{1,0:T(8,128)(2,1)} %get-tuple-element.84), channel_id=1, source_target_pairs={{2,0},{3,1},{4,2},{5,3},{6,4},{7,5},{10,8},{11,9},{12,10},{13,11},... | collective-permute-start | bytes 1376264 | tf_op jit(solution)/shard_map/ppermute | solution.py:607
  109.6 1.9 %copy-start.35 = (bf16[448,512]{1,0:T(8,128)(2,1)}, bf16[448,512]{1,0:T(8,128)(2,1)S(1)}, u32[]{:S(2)}) copy-start(bf16[448,512]{1,0:T(8,128)(2,1)S(1)} %get-tuple-element.73.refs_0_) | copy-start | bytes 1376260
  109.6 24.7 %collective-permute-start.15 = (bf16[448,512]{1,0:T(8,128)(2,1)}, bf16[448,512]{1,0:T(8,128)(2,1)S(1)}, u32[]{:S(2)}, u32[]{:S(2)}) collective-permute-start(bf16[448,512]{1,0:T(8,128)(2,1)} %get-tuple-element.74), channel_id=1, source_target_pairs={{2,0},{3,1},{4,2},{5,3},{6,4},{7,5},{10,8},{11,9},{12,10},{13,11},... | collective-permute-start | bytes 1376264 | tf_op jit(solution)/shard_map/ppermute | solution.py:607
  111.5 10.1 %copy-start.24 = (bf16[192,512]{1,0:T(8,128)(2,1)S(1)}, bf16[192,512]{1,0:T(8,128)(2,1)}, u32[]{:S(2)}) copy-start(bf16[192,512]{1,0:T(8,128)(2,1)} %copy-done.23) | copy-start | bytes 589828
  112.8 16.6 %copy-start.32 = (f32[256,512]{1,0:T(8,128)S(1)}, f32[256,512]{1,0:T(8,128)}, u32[]{:S(2)}) copy-start(f32[256,512]{1,0:T(8,128)} %copy-done.31) | copy-start | bytes 1572868
  112.8 6.5 %collective-permute-start.27 = (f32[8,128]{1,0:T(8,128)}, f32[8,128]{1,0:T(8,128)S(1)}, u32[]{:S(2)}, u32[]{:S(2)}) collective-permute-start(f32[8,128]{1,0:T(8,128)} %tie.2), channel_id=1, source_target_pairs={{0,8},{8,0},{16,24},{24,16},{1,9},{9,1},{17,25},{25,17},{2,10},{10... | collective-permute-start | bytes 12296 | tf_op jit(solution)/shard_map/ppermute | solution.py:565
  114.3 20.7 %collective-permute-start.14 = (bf16[448,512]{1,0:T(8,128)(2,1)}, bf16[448,512]{1,0:T(8,128)(2,1)S(1)}, u32[]{:S(2)}, u32[]{:S(2)}) collective-permute-start(bf16[448,512]{1,0:T(8,128)(2,1)} %copy-done.35), channel_id=1, source_target_pairs={{0,2},{1,3},{2,4},{3,5},{4,6},{5,7},{8,10},{9,11},{10,12},{11,13},... | collective-permute-start | bytes 1376264 | tf_op jit(solution)/shard_map/ppermute | solution.py:607
  120.0 13.7 %collective-permute-start.28 = (f32[8,128]{1,0:T(8,128)S(1)}, f32[8,128]{1,0:T(8,128)S(1)}, u32[]{:S(2)}, u32[]{:S(2)}) collective-permute-start(f32[8,128]{1,0:T(8,128)S(1)} %add.83), channel_id=1, source_target_pairs={{0,16},{8,24},{16,0},{24,8},{1,17},{9,25},{17,1},{25,9},{2,18},{10... | collective-permute-start | bytes 12296 | tf_op jit(solution)/shard_map/ppermute | solution.py:565
  123.2 21.1 %collective-permute-start.21 = (bf16[192,512]{1,0:T(8,128)(2,1)}, bf16[192,512]{1,0:T(8,128)(2,1)}, u32[]{:S(2)}, u32[]{:S(2)}) collective-permute-start(bf16[192,512]{1,0:T(8,128)(2,1)} %slice_add_fusion.3), channel_id=1, source_target_pairs={{0,2},{1,3},{2,4},{3,5},{4,6},{5,7},{8,10},{9,11},{10,12},{11,13},... | collective-permute-start | bytes 589832 | tf_op jit(solution)/shard_map/ppermute | solution.py:607
  129.4 1.0 copy-start.34
  131.3 2.9 %copy-start.26 = (bf16[192,512]{1,0:T(8,128)(2,1)S(1)}, bf16[192,512]{1,0:T(8,128)(2,1)}, u32[]{:S(2)}) copy-start(bf16[192,512]{1,0:T(8,128)(2,1)} %copy-done.25) | copy-start | bytes 589828
  133.7 24.7 %collective-permute-start.20 = (bf16[512,512]{1,0:T(8,128)(2,1)}, bf16[512,512]{1,0:T(8,128)(2,1)}, u32[]{:S(2)}, u32[]{:S(2)}) collective-permute-start(bf16[512,512]{1,0:T(8,128)(2,1)} %get-tuple-element.89), channel_id=1, source_target_pairs={{0,1},{1,0},{2,3},{3,2},{4,5},{5,4},{6,7},{7,6},{8,9},{9,8},{10,11... | collective-permute-start | bytes 1572872 | tf_op jit(solution)/shard_map/ppermute | solution.py:708
  135.0 2.5 %copy-start.28 = (f32[256,512]{1,0:T(8,128)S(1)}, f32[256,512]{1,0:T(8,128)}, u32[]{:S(2)}) copy-start(f32[256,512]{1,0:T(8,128)} %copy-done.27) | copy-start | bytes 1572868
  135.7 1.8 %copy-start.37 = (bf16[256,512]{1,0:T(8,128)(2,1)S(1)}, bf16[256,512]{1,0:T(8,128)(2,1)}, u32[]{:S(2)}) copy-start(bf16[256,512]{1,0:T(8,128)(2,1)} %copy-done.36) | copy-start | bytes 786436
  137.0 4.5 %collective-permute-start.29 = (f32[8,128]{1,0:T(8,128)}, f32[8,128]{1,0:T(8,128)S(1)}, u32[]{:S(2)}, u32[]{:S(2)}) collective-permute-start(f32[8,128]{1,0:T(8,128)} %tie.3), channel_id=1, source_target_pairs={{0,1},{1,0},{2,3},{3,2},{4,5},{5,4},{6,7},{7,6},{8,9},{9,8},{10,11... | collective-permute-start | bytes 12296 | tf_op jit(solution)/shard_map/ppermute | solution.py:565
  137.5 1.0 copy-start.30
  138.5 1.5 copy-start.22
  138.6 5.7 %copy-start.44 = (bf16[192,512]{1,0:T(8,128)(2,1)S(1)}, bf16[192,512]{1,0:T(8,128)(2,1)}, u32[]{:S(2)}) copy-start(bf16[192,512]{1,0:T(8,128)(2,1)} %slice_add_fusion.refs_1_) | copy-start | bytes 589828
  138.6 11.4 %copy-start.45 = (bf16[192,512]{1,0:T(8,128)(2,1)S(1)}, bf16[192,512]{1,0:T(8,128)(2,1)}, u32[]{:S(2)}) copy-start(bf16[192,512]{1,0:T(8,128)(2,1)} %slice_add_fusion.1.refs_0_) | copy-start | bytes 589828
  138.6 14.6 %copy-start.41 = (bf16[192,512]{1,0:T(8,128)(2,1)S(1)}, bf16[192,512]{1,0:T(8,128)(2,1)}, u32[]{:S(2)}) copy-start(bf16[192,512]{1,0:T(8,128)(2,1)} %copy-done.40) | copy-start | bytes 589828
  140.1 13.1 %copy-start.20 = (bf16[448,512]{1,0:T(8,128)(2,1)S(1)}, bf16[448,512]{1,0:T(8,128)(2,1)}, u32[]{:S(2)}) copy-start(bf16[448,512]{1,0:T(8,128)(2,1)} %copy-done.18) | copy-start | bytes 1376260
  140.1 1.5 copy-start.46
  140.1 20.9 %collective-permute-start.19 = (bf16[512,512]{1,0:T(8,128)(2,1)S(1)}, bf16[512,512]{1,0:T(8,128)(2,1)S(1)}, u32[]{:S(2)}, u32[]{:S(2)}) collective-permute-start(bf16[512,512]{1,0:T(8,128)(2,1)S(1)} %get-tuple-element.88), channel_id=1, source_target_pairs={{0,1},{1,0},{2,3},{3,2},{4,5},{5,4},{6,7},{7,6},{8,9},{9,8},{10,11... | collective-permute-start | bytes 1572872 | tf_op jit(solution)/shard_map/ppermute | solution.py:708
  140.1 11.3 %collective-permute-start.22 = (bf16[192,512]{1,0:T(8,128)(2,1)S(1)}, bf16[192,512]{1,0:T(8,128)(2,1)S(1)}, u32[]{:S(2)}, u32[]{:S(2)}) collective-permute-start(bf16[192,512]{1,0:T(8,128)(2,1)S(1)} %slice_add_fusion.2), channel_id=1, source_target_pairs={{2,0},{3,1},{4,2},{5,3},{6,4},{7,5},{10,8},{11,9},{12,10},{13,11},... | collective-permute-start | bytes 589832 | tf_op jit(solution)/shard_map/ppermute | solution.py:607
  141.6 8.4 %collective-permute-start.30 = (f32[8,128]{1,0:T(8,128)S(1)}, f32[8,128]{1,0:T(8,128)S(1)}, u32[]{:S(2)}, u32[]{:S(2)}) collective-permute-start(f32[8,128]{1,0:T(8,128)S(1)} %add.85), channel_id=1, source_target_pairs={{0,2},{1,3},{2,0},{3,1},{4,6},{5,7},{6,4},{7,5},{8,10},{9,11},{10,... | collective-permute-start | bytes 12296 | tf_op jit(solution)/shard_map/ppermute | solution.py:565
  144.3 11.7 %collective-permute-start.24 = (bf16[192,512]{1,0:T(8,128)(2,1)S(1)}, bf16[192,512]{1,0:T(8,128)(2,1)S(1)}, u32[]{:S(2)}, u32[]{:S(2)}) collective-permute-start(bf16[192,512]{1,0:T(8,128)(2,1)S(1)} %copy-done.44), channel_id=1, source_target_pairs={{2,0},{3,1},{4,2},{5,3},{6,4},{7,5},{10,8},{11,9},{12,10},{13,11},... | collective-permute-start | bytes 589832 | tf_op jit(solution)/shard_map/ppermute | solution.py:607
  149.9 6.1 %collective-permute-start.23 = (bf16[192,512]{1,0:T(8,128)(2,1)S(1)}, bf16[192,512]{1,0:T(8,128)(2,1)S(1)}, u32[]{:S(2)}, u32[]{:S(2)}) collective-permute-start(bf16[192,512]{1,0:T(8,128)(2,1)S(1)} %copy-done.45), channel_id=1, source_target_pairs={{0,2},{1,3},{2,4},{3,5},{4,6},{5,7},{8,10},{9,11},{10,12},{11,13},... | collective-permute-start | bytes 589832 | tf_op jit(solution)/shard_map/ppermute | solution.py:607
  151.4 4.6 %collective-permute-start.31 = (f32[8,128]{1,0:T(8,128)S(1)}, f32[8,128]{1,0:T(8,128)S(1)}, u32[]{:S(2)}, u32[]{:S(2)}) collective-permute-start(f32[8,128]{1,0:T(8,128)S(1)} %add.86), channel_id=1, source_target_pairs={{0,4},{1,5},{2,6},{3,7},{4,0},{5,1},{6,2},{7,3},{8,12},{9,13},{10,... | collective-permute-start | bytes 12296 | tf_op jit(solution)/shard_map/ppermute | solution.py:565
  153.2 2.8 %copy-start.43 = (bf16[192,512]{1,0:T(8,128)(2,1)S(1)}, bf16[192,512]{1,0:T(8,128)(2,1)}, u32[]{:S(2)}) copy-start(bf16[192,512]{1,0:T(8,128)(2,1)} %copy-done.42) | copy-start | bytes 589828
  156.0 4.1 %collective-permute-start.25 = (bf16[96,512]{1,0:T(8,128)(2,1)S(1)}, bf16[96,512]{1,0:T(8,128)(2,1)S(1)}, u32[]{:S(2)}, u32[]{:S(2)}) collective-permute-start(bf16[96,512]{1,0:T(8,128)(2,1)S(1)} %get-tuple-element.106), channel_id=1, source_target_pairs={{0,1},{1,0},{2,3},{3,2},{4,5},{5,4},{6,7},{7,6},{8,9},{9,8},{10,11... | collective-permute-start | bytes 294920 | tf_op jit(solution)/shard_map/ppermute | solution.py:701
  157.3 2.9 %collective-permute-start.26 = (bf16[96,512]{1,0:T(8,128)(2,1)S(1)}, bf16[96,512]{1,0:T(8,128)(2,1)S(1)}, u32[]{:S(2)}, u32[]{:S(2)}) collective-permute-start(bf16[96,512]{1,0:T(8,128)(2,1)S(1)} %get-tuple-element.107), channel_id=1, source_target_pairs={{0,1},{1,0},{2,3},{3,2},{4,5},{5,4},{6,7},{7,6},{8,9},{9,8},{10,11... | collective-permute-start | bytes 294920 | tf_op jit(solution)/shard_map/ppermute | solution.py:701
  (18 other events, 15.0 us)

commit v4 on v3

v4 whole, which is shorter than its diff:
```python
import functools

import jax
import jax.numpy as jnp
from jax import lax
from jax.experimental import pallas as pl
from jax.experimental.pallas import tpu as pltpu
from jax.sharding import PartitionSpec as P

BLK = 128
TILES = 2
NORM_EPS = 1e-06
HEADS_PER_STEP = 1
CHUNKS = 1
VMEM_LIMIT = 8 * 1024 * 1024
ATTENTION_VMEM_LIMIT = 24 * 1024 * 1024
GAIN_ROWS = 32
SMALL = pl.CostEstimate(flops=1, bytes_accessed=1, transcendentals=0)


def dot(lhs, rhs, lhs_dim, rhs_dim):
    return lax.dot_general(
        lhs, rhs, (((lhs_dim,), (rhs_dim,)), ((), ())), preferred_element_type=jnp.float32
    )


def params(limit=VMEM_LIMIT):
    return pltpu.CompilerParams(dimension_semantics=("arbitrary",), vmem_limit_bytes=limit)


def split_rows(sums):
    high = sums.astype(jnp.bfloat16).astype(jnp.float32)
    rest = sums - high
    middle = rest.astype(jnp.bfloat16).astype(jnp.float32)
    low = rest - middle
    return jnp.concatenate([high, middle, low, jnp.zeros_like(high)], axis=0).astype(jnp.bfloat16)


def joined_rows(rows):
    rows = rows.astype(jnp.float32)
    return (rows[16:24] + rows[8:16]) + rows[0:8]


def pack_kernel(state_ref, align_ref, *refs):
    ins, out_ref = refs[:-1], refs[-1]
    start = 0
    for ref in ins[:-4]:
        out_ref[start : start + ref.shape[0], :] = ref[...]
        start += ref.shape[0]
    row = lax.broadcasted_iota(jnp.int32, (16, out_ref.shape[1]), 0)
    tiles = jnp.zeros((16, out_ref.shape[1]), jnp.int32)
    for slot in range(TILES):
        tiles = jnp.where(row == slot, align_ref[slot], tiles)
    out_ref[start : start + 16, :] = tiles.astype(jnp.float32).astype(jnp.bfloat16)
    start += 16
    for ref in ins[-4:]:
        out_ref[start : start + ref.shape[0], :] = ref[...]
        start += ref.shape[0]


def pack(state, align, arrays):
    width = arrays[0].shape[1]
    half = width // 2
    step = half // 4
    rows = sum(array.shape[0] for array in arrays) + 16
    return pl.pallas_call(
        pack_kernel,
        grid_spec=pltpu.PrefetchScalarGridSpec(
            num_scalar_prefetch=2,
            grid=(4,),
            in_specs=[
                pl.BlockSpec(
                    (array.shape[0], step), lambda i, state, _: (0, (1 - state[0]) * 4 + i)
                )
                for array in arrays
            ],
            out_specs=pl.BlockSpec((rows, step), lambda i, state, _: (0, i)),
        ),
        out_shape=jax.ShapeDtypeStruct((rows, half), jnp.bfloat16),
        compiler_params=params(),
        cost_estimate=SMALL,
        name="pack",
    )(state, align, *arrays)


def merge_kernel(lyric, state_ref, key_ref, value_ref, lkey_ref, lvalue_ref, mate_ref, *refs):
    frames = key_ref.shape[0]
    first = mate_ref.shape[0] - 2 * frames
    one_ref, mid_ref = refs[-2:]
    if lyric:
        pair_ref = refs[-3]
        pair_ref[0:lyric, :] = lkey_ref[...]
        pair_ref[lyric : 2 * lyric, :] = lvalue_ref[...]
        pair_ref[2 * lyric :, :] = mate_ref[0 : 2 * lyric, :]
        one_ref[0 : 4 * lyric, :] = pair_ref[...]
    for ref, start, touching in ((one_ref, 4 * lyric, 1), (mid_ref, 0, 0)):
        mine = state_ref[1] == touching
        ref[start : start + frames, :] = jnp.where(
            mine, key_ref[...], mate_ref[first : first + frames, :]
        )
        ref[start + frames :, :] = jnp.where(
            mine, value_ref[...], mate_ref[first + frames :, :]
        )


def merge(state, chunk, key, value, lyric_key, lyric_value, mate, with_lyric, after):
    frames, width = key.shape
    lyric = lyric_key.shape[0] if with_lyric else 0
    size = width // 2 // CHUNKS
    step = size // 2
    out_rows = ([4 * lyric] if lyric else []) + [2 * frames + 4 * lyric, 2 * frames]

    def own(array):
        return pl.BlockSpec(
            (array.shape[0], step), lambda i, state: (0, (state[0] * CHUNKS + chunk) * 2 + i)
        )

    return pl.pallas_call(
        functools.partial(merge_kernel, lyric),
        grid_spec=pltpu.PrefetchScalarGridSpec(
            num_scalar_prefetch=1,
            grid=(2,),
            in_specs=[own(key), own(value), own(lyric_key), own(lyric_value)]
            + [pl.BlockSpec((mate.shape[0], step), lambda i, state: (0, chunk * 2 + i))]
            + [pl.BlockSpec(memory_space=pl.ANY)] * len(after),
            out_specs=[pl.BlockSpec((rows, step), lambda i, state: (0, i)) for rows in out_rows],
        ),
        out_shape=[jax.ShapeDtypeStruct((rows, size), jnp.bfloat16) for rows in out_rows],
        compiler_params=params(),
        cost_estimate=SMALL,
        name="merge",
    )(state, key, value, lyric_key, lyric_value, mate, *after)


def attention_kernel(
    groups, chained, head_size, score_scale, meta_ref, gain_ref, query_ref, grad_ref, key_ref,
    value_ref, mate_ref, one_ref, mid_ref, *refs
):
    frames = query_ref.shape[0]
    exchanged = len(groups) == 4
    inputs = 3 if exchanged else 1
    lyric_in, refs = refs[:inputs], refs[inputs:]
    window = one_ref.shape[0] - 2 * frames
    if chained:
        gain_before_ref, refs = refs[0], refs[3:]
    out_ref, grad_query_ref, to_mate_ref, key_grad_ref, value_grad_ref = refs[:5]
    to_one_ref, to_mid_ref, gain_grad_ref = refs[5:8]
    lyric_out, mask_ref = refs[8:-1], refs[-1]
    runs = [(index, run) for index, group in enumerate(groups) for run in group]
    main = 2 * frames + sum(run[2] for _, run in runs)
    lanes = 2 * frames
    first = mate_ref.shape[0] - 4 * frames
    touching = meta_ref[1] == 1

    @pl.when(pl.program_id(0) == 0)
    def _():
        if chained:
            gain_grad_ref[...] = gain_before_ref[...]
        else:
            gain_grad_ref[...] = jnp.zeros_like(gain_grad_ref)
        mate_tiles = mate_ref[first - 16 : first, 0:frames].astype(jnp.float32).astype(jnp.int32)
        start = 0
        for number, (_, (_, _, rows)) in enumerate(runs):
            row = lax.broadcasted_iota(jnp.int32, (rows, lanes), 0) + meta_ref[7 + number]
            keep = jnp.zeros((rows, lanes), jnp.float32)
            for slot in range(TILES):
                tile = jnp.concatenate(
                    [
                        jnp.full((1, frames), meta_ref[2 + slot], jnp.int32),
                        mate_tiles[slot : slot + 1],
                    ],
                    axis=1,
                )
                lower = tile * BLK
                upper = jnp.minimum(lower + BLK, meta_ref[4])
                inside = (row >= lower) & (row < upper) & (lower >= 0)
                keep = jnp.where(inside, 1.0, keep)
            mask_ref[start : start + rows, :] = keep
            start += rows
        lane = lax.broadcasted_iota(jnp.int32, (frames, lanes), 1)
        mask_ref[start : start + frames, :] = jnp.where(
            lane < frames, meta_ref[5], meta_ref[6]
        ).astype(jnp.float32)

    q_gain = gain_ref[0:1, :]
    k_gain = gain_ref[1:2, :]
    for head in range(query_ref.shape[1] // head_size):
        cols = slice(head * head_size, (head + 1) * head_size)
        lyric = [ref[:, cols] for ref in lyric_in]
        if exchanged:
            lyric = [lyric[0], lyric[1], one_ref[0:window, cols], lyric[2]]
        one_rows, mid_rows = one_ref[window:, cols], mid_ref[:, cols]
        near_rows = jnp.where(touching, one_rows, mid_rows)
        far_rows = jnp.where(touching, mid_rows, one_rows)

        def from_mate(number):
            return mate_ref[first + number * frames : first + (number + 1) * frames, cols]

        query = jnp.concatenate([query_ref[:, cols], from_mate(0)], axis=0)
        query = query.astype(jnp.float32)
        cot = jnp.concatenate([grad_ref[:, cols], from_mate(1)], axis=0)
        raw_keys = jnp.concatenate(
            [key_ref[:, cols], from_mate(2)]
            + [lyric[index][run[0] : run[0] + run[2]] for index, run in runs]
            + [near_rows[:frames], far_rows[:frames]],
            axis=0,
        ).astype(jnp.float32)
        value = jnp.concatenate(
            [value_ref[:, cols], from_mate(3)]
            + [lyric[index][run[1] : run[1] + run[2]] for index, run in runs]
            + [near_rows[frames:], far_rows[frames:]],
            axis=0,
        )
        query_inv = lax.rsqrt(jnp.mean(query * query, axis=1, keepdims=True) + NORM_EPS)
        key_inv = lax.rsqrt(jnp.mean(raw_keys * raw_keys, axis=1, keepdims=True) + NORM_EPS)
        query_hat = query * query_inv
        query_low = (query_hat * (q_gain * score_scale)).astype(jnp.bfloat16)
        key_hat = raw_keys * key_inv
        key_low = (key_hat * k_gain).astype(jnp.bfloat16)

        near, far = slice(main, main + frames), slice(main + frames, main + 2 * frames)

        def against(rows, columns):
            return jnp.concatenate(
                [
                    dot(rows[:main], columns, 1, 1),
                    jnp.concatenate(
                        [
                            dot(rows[near], columns[:frames], 1, 1),
                            dot(rows[far], columns[frames:], 1, 1),
                        ],
                        axis=1,
                    ),
                ],
                axis=0,
            )

        def over_keys(weights, rows):
            return dot(weights[:main], rows[:main], 0, 0) + jnp.concatenate(
                [
                    dot(weights[main:, :frames], rows[near], 0, 0),
                    dot(weights[main:, frames:], rows[far], 0, 0),
                ],
                axis=0,
            )

        def over_queries(weights, columns):
            return jnp.concatenate(
                [
                    dot(weights[:main], columns, 1, 0),
                    dot(weights[main:, :frames], columns[:frames], 1, 0),
                    dot(weights[main:, frames:], columns[frames:], 1, 0),
                ],
                axis=0,
            )

        exp_scores = jnp.exp(against(key_low, query_low))
        exp_scores = jnp.concatenate(
            [exp_scores[: 2 * frames], exp_scores[2 * frames :] * mask_ref[...]], axis=0
        )
        grad_prob = against(value, cot)
        prob = exp_scores * (1.0 / jnp.sum(exp_scores, axis=0, keepdims=True))
        prob_low = prob.astype(jnp.bfloat16)
        weighted = prob * grad_prob
        delta = jnp.sum(weighted, axis=0, keepdims=True)
        grad_score = (weighted - prob * delta).astype(jnp.bfloat16)
        output = over_keys(prob_low, value).astype(jnp.bfloat16)
        grad_qn = over_keys(grad_score, key_low) * score_scale
        grad_keys = over_queries(grad_score, query_low)
        grad_values = over_queries(prob_low, cot)
        scaled = grad_qn * q_gain
        grad_query = (
            query_inv * scaled
            - query_hat
            * (query_inv * query_inv)
            * jnp.mean(scaled * query, axis=1, keepdims=True)
        ).astype(jnp.bfloat16)
        gain_grad_ref[0:1, :] += jnp.sum(grad_qn * query_hat, axis=0, keepdims=True)
        gain_grad_ref[1:2, :] += jnp.sum(grad_keys * key_hat, axis=0, keepdims=True)

        out_ref[:, cols] = output[:frames]
        grad_query_ref[:, cols] = grad_query[:frames]
        to_mate_ref[0:frames, cols] = output[frames:]
        to_mate_ref[frames:, cols] = grad_query[frames:]
        key_grad_ref[:, cols] = grad_keys[: 2 * frames]
        value_grad_ref[:, cols] = grad_values[: 2 * frames]
        for grads, part in (
            (grad_keys.astype(jnp.bfloat16), 0),
            (grad_values.astype(jnp.bfloat16), frames),
        ):
            to_one_ref[window + part : window + part + frames, cols] = jnp.where(
                touching, grads[near], grads[far]
            )
            to_mid_ref[part : part + frames, cols] = jnp.where(touching, grads[far], grads[near])
        if exchanged:
            held_ref, two_ref, to_two_ref = lyric_out
            outs = (held_ref, two_ref, to_one_ref, to_two_ref)
        else:
            outs = lyric_out
        start = 2 * frames
        for index, (key_row, value_row, rows) in runs:
            part = slice(start, start + rows)
            outs[index][key_row : key_row + rows, cols] = grad_keys[part].astype(jnp.bfloat16)
            outs[index][value_row : value_row + rows, cols] = grad_values[part].astype(
                jnp.bfloat16
            )
            start += rows


def attention(chunk, meta, gains, query, cot, key, value, mate, one, mid, lyrics, groups, carried):
    frames, width = query.shape
    head_size = gains.shape[1]
    size = width // 2 // CHUNKS
    step = HEADS_PER_STEP * head_size
    steps = size // step
    lyric_rows = sum(run[2] for group in groups for run in group)
    lanes = 2 * frames
    key_rows = 3 * frames + lyric_rows
    exchanged = len(groups) == 4

    def own(rows):
        return pl.BlockSpec(
            (rows, step), lambda i, meta: (0, (meta[0] * CHUNKS + chunk) * steps + i)
        )

    def columns(rows):
        return pl.BlockSpec((rows, step), lambda i, meta: (0, i))

    def either(array):
        return own(array.shape[0]) if array.shape[1] == width else columns(array.shape[0])

    whole = lambda i, meta: (0, 0)
    bf16, f32 = jnp.bfloat16, jnp.float32
    out_rows = [(2 * frames, bf16), (2 * frames, f32), (2 * frames, f32)]
    out_rows += [(one.shape[0], bf16), (2 * frames, bf16)]
    slot = sum(2 * run[2] for run in groups[0])
    extra_rows = [slot] * (3 if exchanged else 1)
    return pl.pallas_call(
        functools.partial(
            attention_kernel, groups, bool(carried), head_size, head_size ** (-0.5)
        ),
        grid_spec=pltpu.PrefetchScalarGridSpec(
            num_scalar_prefetch=1,
            grid=(steps,),
            in_specs=[pl.BlockSpec(gains.shape, whole)]
            + [own(frames)] * 4
            + [
                pl.BlockSpec((mate.shape[0], step), lambda i, meta: (0, chunk * steps + i)),
                columns(one.shape[0]),
                columns(mid.shape[0]),
            ]
            + [either(array) for array in lyrics]
            + [pl.BlockSpec((8, head_size), whole)] * bool(carried)
            + [pl.BlockSpec(memory_space=pl.ANY)] * len(carried[1:]),
            out_specs=[own(frames)] * 2
            + [columns(rows) for rows, _ in out_rows]
            + [pl.BlockSpec((8, head_size), whole)]
            + [columns(rows) for rows in extra_rows],
            scratch_shapes=[pltpu.VMEM((frames + lyric_rows, lanes), f32)],
        ),
        out_shape=[jax.ShapeDtypeStruct((frames, width), bf16)] * 2
        + [jax.ShapeDtypeStruct((rows, size), dtype) for rows, dtype in out_rows]
        + [jax.ShapeDtypeStruct((8, head_size), f32)]
        + [jax.ShapeDtypeStruct((rows, size), bf16) for rows in extra_rows],
        input_output_aliases={10 + len(lyrics) + i: i for i in range(len(carried[1:]))},
        compiler_params=params(ATTENTION_VMEM_LIMIT),
        cost_estimate=pl.CostEstimate(
            flops=12 * key_rows * lanes * size,
            bytes_accessed=16 * 1024 * 1024 // CHUNKS,
            transcendentals=key_rows * lanes * (size // head_size),
        ),
        name="attention",
    )(meta, gains, query, cot, key, value, mate, one, mid, *lyrics, *carried)


def fill_kernel(count, core_ref, mate_ref, *refs):
    for index, ref in enumerate(refs[-count:]):
        rows = ref.shape[0]
        ref[...] = mate_ref[index * rows : (index + 1) * rows, :]


def fill_other(core, chunk, arrays, mate):
    frames, width = arrays[0].shape
    count = len(arrays)
    size = width // 2 // CHUNKS
    step = size // 2
    spec = pl.BlockSpec(
        (frames, step), lambda i, core: (0, ((1 - core[0]) * CHUNKS + chunk) * 2 + i)
    )
    return pl.pallas_call(
        functools.partial(fill_kernel, count),
        grid_spec=pltpu.PrefetchScalarGridSpec(
            num_scalar_prefetch=1,
            grid=(2,),
            in_specs=[pl.BlockSpec((mate.shape[0], step), lambda i, core: (0, i))]
            + [pl.BlockSpec(memory_space=pl.ANY)] * count,
            out_specs=[spec] * count,
        ),
        out_shape=[jax.ShapeDtypeStruct(array.shape, array.dtype) for array in arrays],
        input_output_aliases={2 + i: i for i in range(count)},
        compiler_params=params(),
        cost_estimate=SMALL,
        name="fill_other",
    )(core, mate, *arrays)


def through_norm(raw, grad, k_gain):
    raw = raw.astype(jnp.float32)
    inverse = lax.rsqrt(jnp.mean(raw * raw, axis=1, keepdims=True) + NORM_EPS)
    scaled = grad * k_gain
    return (
        inverse * scaled
        - raw * (inverse * inverse * inverse) * jnp.mean(scaled * raw, axis=1, keepdims=True)
    ).astype(jnp.bfloat16)


def finish_audio_kernel(
    head_size, state_ref, gain_ref, raw_ref, mate_ref, key_grad_ref, value_grad_ref, one_ref,
    mid_ref, ready_ref, *refs,
):
    k_gain = gain_ref[1:2, :]
    grad_key_ref, grad_value_ref, to_mate_ref = refs[-3:]
    frames = raw_ref.shape[0]
    own, mate = slice(0, frames), slice(frames, 2 * frames)
    first = one_ref.shape[0] - 2 * frames
    touching = state_ref[1] == 1
    mate_keys = mate_ref.shape[0] - 2 * frames
    to_mate_ref[0 : 2 * frames, :] = ready_ref[...]
    for head in range(raw_ref.shape[1] // head_size):
        cols = slice(head * head_size, (head + 1) * head_size)
        one = one_ref[first:, cols].astype(jnp.float32)
        mid = mid_ref[:, cols].astype(jnp.float32)
        for_own = jnp.where(touching, one, mid)
        for_mate = jnp.where(touching, mid, one)
        grad_key_ref[:, cols] = through_norm(
            raw_ref[:, cols], key_grad_ref[own, cols] + for_own[:frames], k_gain
        )
        grad_value_ref[:, cols] = (value_grad_ref[own, cols] + for_own[frames:]).astype(
            jnp.bfloat16
        )
        to_mate_ref[2 * frames : 3 * frames, cols] = through_norm(
            mate_ref[mate_keys : mate_keys + frames, cols],
            key_grad_ref[mate, cols] + for_mate[:frames],
            k_gain,
        )
        to_mate_ref[3 * frames : 4 * frames, cols] = (
            value_grad_ref[mate, cols] + for_mate[frames:]
        ).astype(jnp.bfloat16)


def finish_audio(state, chunk, gains, raw, mate, key_grad, value_grad, one, mid, ready, carried):
    frames, width = raw.shape
    head_size = gains.shape[1]
    size = width // 2 // CHUNKS
    step = size // 2

    def columns(array):
        return pl.BlockSpec((array.shape[0], step), lambda i, core: (0, i))

    own = pl.BlockSpec((frames, step), lambda i, core: (0, (core[0] * CHUNKS + chunk) * 2 + i))
    arrays = (key_grad, value_grad, one, mid, ready)
    return pl.pallas_call(
        functools.partial(finish_audio_kernel, head_size),
        grid_spec=pltpu.PrefetchScalarGridSpec(
            num_scalar_prefetch=1,
            grid=(2,),
            in_specs=[pl.BlockSpec(gains.shape, lambda i, core: (0, 0)), own]
            + [pl.BlockSpec((mate.shape[0], step), lambda i, core: (0, chunk * 2 + i))]
            + [columns(array) for array in arrays]
            + [pl.BlockSpec(memory_space=pl.ANY)] * len(carried),
            out_specs=[own] * 2 + [pl.BlockSpec((4 * frames, step), lambda i, core: (0, i))],
        ),
        out_shape=[jax.ShapeDtypeStruct((frames, width), jnp.bfloat16)] * 2
        + [jax.ShapeDtypeStruct((5 * frames, size), jnp.bfloat16)],
        input_output_aliases={9 + i: i for i in range(len(carried))},
        compiler_params=params(),
        cost_estimate=SMALL,
        name="finish_audio",
    )(state, gains, raw, mate, *arrays, *carried)


def relay_kernel(head_size, part_ref, arrived_ref, *refs):
    out_ref = refs[-1]
    rows = part_ref.shape[0]
    out_ref[0:rows, :] = (
        part_ref[...].astype(jnp.float32) + arrived_ref[...].astype(jnp.float32)
    ).astype(jnp.bfloat16)
    if len(refs) == 2:
        out_ref[rows:, 0:head_size] = split_rows(refs[0][...])
        out_ref[rows:, head_size:] = jnp.zeros_like(out_ref[rows:, head_size:])


def relay(part, arrived, sums):
    rows, size = part.shape
    step = size // 2
    out_rows = rows + GAIN_ROWS * len(sums)
    spec = pl.BlockSpec((rows, step), lambda i: (0, i))
    return pl.pallas_call(
        functools.partial(relay_kernel, sums[0].shape[1] if sums else 0),
        grid=(2,),
        in_specs=[spec] * 2 + [pl.BlockSpec(total.shape, lambda i: (0, 0)) for total in sums],
        out_specs=pl.BlockSpec((out_rows, step), lambda i: (0, i)),
        out_shape=jax.ShapeDtypeStruct((out_rows, size), jnp.bfloat16),
        compiler_params=params(),
        cost_estimate=SMALL,
        name="relay",
    )(part, arrived, *sums)


def finish_lyric_kernel(head_size, gain_ref, raw_ref, held_ref, one_ref, two_ref, *refs):
    lyric_rows = raw_ref.shape[0]
    rows = lyric_rows // 4
    own_ref, to_mate_ref, total_ref = refs[-3:]
    k_gain = gain_ref[1:2, :]
    if len(refs) == 5:
        total_ref[...] = refs[0][...] + joined_rows(two_ref[lyric_rows:, 0:head_size])
    else:
        total_ref[...] = jnp.zeros_like(total_ref)
    for head in range(raw_ref.shape[1] // head_size):
        cols = slice(head * head_size, (head + 1) * head_size)
        total = held_ref[:, cols].astype(jnp.float32)
        for part in (one_ref, two_ref):
            total = total + part[0:lyric_rows, cols].astype(jnp.float32)
        for index, ref in enumerate((own_ref, to_mate_ref)):
            base = 2 * rows * index
            ref[0:rows, cols] = through_norm(
                raw_ref[base : base + rows, cols], total[base : base + rows], k_gain
            )
            ref[rows : 2 * rows, cols] = total[base + rows : base + 2 * rows].astype(jnp.bfloat16)
        to_mate_ref[2 * rows :, cols] = split_rows(total_ref[...])


def finish_lyric(gains, raw, held, one, two, sums, to_mate):
    rows, size = raw.shape
    head_size = gains.shape[1]
    step = size // 2
    tail = rows // 2 + GAIN_ROWS
    last = to_mate.shape[0] // tail - 1
    spec = pl.BlockSpec((rows, step), lambda i: (0, i))
    whole = pl.BlockSpec((8, head_size), lambda i: (0, 0))
    return pl.pallas_call(
        functools.partial(finish_lyric_kernel, head_size),
        grid=(2,),
        in_specs=[pl.BlockSpec(gains.shape, lambda i: (0, 0)), spec, spec, spec]
        + [pl.BlockSpec((two.shape[0], step), lambda i: (0, i))]
        + [whole] * len(sums)
        + [pl.BlockSpec(memory_space=pl.ANY)],
        out_specs=[
            pl.BlockSpec((rows // 2, step), lambda i: (0, i)),
            pl.BlockSpec((tail, step), lambda i: (last, i)),
            whole,
        ],
        out_shape=[
            jax.ShapeDtypeStruct((rows // 2, size), jnp.bfloat16),
            jax.ShapeDtypeStruct(to_mate.shape, jnp.bfloat16),
            jax.ShapeDtypeStruct((8, head_size), jnp.float32),
        ],
        input_output_aliases={5 + len(sums): 1},
        compiler_params=params(),
        cost_estimate=SMALL,
        name="finish_lyric",
    )(gains, raw, held, one, two, *sums, to_mate)


def join_kernel(count, chunks, state_ref, gain_ref, *refs):
    owns, mates, outs = refs[:chunks], refs[chunks : 2 * chunks], refs[-count - 3 :]
    grad_key_ref, grad_value_ref, total_ref = outs[count:]
    rows, size = grad_key_ref.shape[0], owns[0].shape[1]
    frames = outs[0].shape[0]
    for index, ref in enumerate(outs[:count]):
        ref[...] = mates[-1][index * frames : (index + 1) * frames, :]
    for part, parts, first in (
        (state_ref[0], owns, 0),
        (1 - state_ref[0], mates, count * frames),
    ):
        for chunk, ref in enumerate(parts):
            cols = pl.ds(pl.multiple_of((part * chunks + chunk) * size, size), size)
            grad_key_ref[:, cols] = ref[first : first + rows, :]
            grad_value_ref[:, cols] = ref[first + rows : first + 2 * rows, :]
    sums = mates[-1][mates[-1].shape[0] - GAIN_ROWS :, 0 : gain_ref.shape[1]]
    total_ref[...] = gain_ref[...] + joined_rows(sums)


def join(state, gain, arrays, own, mate):
    rows, size = own[0].shape
    frames, width = arrays[0].shape
    count, chunks = len(arrays), len(own)
    whole = lambda i, state: (0, 0)
    other = pl.BlockSpec(
        (frames, size), lambda i, state: (0, (1 - state[0]) * chunks + chunks - 1)
    )
    return pl.pallas_call(
        functools.partial(join_kernel, count, chunks),
        grid_spec=pltpu.PrefetchScalarGridSpec(
            num_scalar_prefetch=1,
            grid=(1,),
            in_specs=[pl.BlockSpec(array.shape, whole) for array in [gain, *own, *mate]]
            + [pl.BlockSpec(memory_space=pl.ANY)] * count,
            out_specs=[other] * count
            + [pl.BlockSpec((rows // 2, width), whole)] * 2
            + [pl.BlockSpec(gain.shape, whole)],
        ),
        out_shape=[jax.ShapeDtypeStruct(array.shape, array.dtype) for array in arrays]
        + [jax.ShapeDtypeStruct((rows // 2, width), jnp.bfloat16)] * 2
        + [jax.ShapeDtypeStruct(gain.shape, jnp.float32)],
        input_output_aliases={2 + 2 * chunks + i: i for i in range(count)},
        compiler_params=params(),
        cost_estimate=SMALL,
        name="join",
    )(state, gain, *own, *mate, *arrays)


def norm_lyric_kernel(head_size, gain_ref, raw_ref, grad_ref, out_ref):
    for head in range(raw_ref.shape[1] // head_size):
        cols = slice(head * head_size, (head + 1) * head_size)
        out_ref[:, cols] = through_norm(raw_ref[:, cols], grad_ref[:, cols], gain_ref[1:2, :])


def norm_lyric(gains, raw, grad):
    return pl.pallas_call(
        functools.partial(norm_lyric_kernel, gains.shape[1]),
        out_shape=jax.ShapeDtypeStruct(raw.shape, jnp.bfloat16),
        name="norm_lyric",
    )(gains, raw, grad)


def sum_over(total, axis, bits):
    count = lax.axis_size(axis)
    for bit in bits:
        total = total + lax.ppermute(total, axis, [(i, i ^ bit) for i in range(count)])
    return total


def bits_of(count):
    return [1 << bit for bit in range(count.bit_length() - 1)]


def body(
    queries, keys, values, lyric_keys, lyric_values, q_gain, k_gain, cotangent, alignment, lyric_len
):
    frames = queries.shape[1]
    lyric_local, width = lyric_keys.shape[1:]
    count = lax.axis_size("seq")
    songs = lax.axis_size("song")
    me = lax.axis_index("seq")
    core = me % 2
    chips = count // 2
    chip = me // 2
    touching = (chip % 2) ^ core
    state = jnp.stack([core, touching]).astype(jnp.int32)
    gains = jnp.stack([q_gain, k_gain])

    swap = [(i, i ^ 1) for i in range(count)]
    partners = [(a, a ^ 1) for a in range(chips)]
    across = [(a, a ^ 2) for a in range(chips)]
    between = [(a, a + 1) for a in range(1, chips - 1, 2)]
    between += [(b, a) for a, b in between]

    def hop(block, moves):
        pairs = [(2 * a + c, 2 * b + c) for a, b in moves for c in (0, 1)]
        return lax.ppermute(block, "seq", pairs)

    hops = chips == 4 and lyric_local % 16 == 0 and 2 * lyric_local + GAIN_ROWS == frames
    total_rows = lyric_local * count
    if hops:
        run = ((0, lyric_local, lyric_local), (2 * lyric_local, 3 * lyric_local, lyric_local))
        groups = (run,) * 4
        owners = [chip, chip ^ 2, chip ^ 1, chip ^ 3]
        first_rows = []
        for owner in owners:
            first_rows += [
                (2 * owner + core) * lyric_local,
                (2 * owner + 1 - core) * lyric_local,
            ]
    else:
        gathered = jnp.concatenate(
            [
                lax.all_gather(lyric_keys[0], "seq", axis=0, tiled=True),
                lax.all_gather(lyric_values[0], "seq", axis=0, tiled=True),
            ],
            axis=0,
        )
        groups = (((0, total_rows, total_rows),),)
        first_rows = [0]
    has_left, has_right = chip > 0, chip < chips - 1
    has_near = jnp.where(core == 0, has_left, has_right)
    has_far = jnp.where(core == 0, has_right, has_left)
    meta = jnp.stack(
        [
            jnp.asarray(value, jnp.int32)
            for value in [core, touching]
            + [alignment[0, 0, slot] for slot in range(TILES)]
            + [lyric_len[0], has_near, has_far]
            + first_rows
        ]
    )

    rows = 4 * lyric_local
    to_mate = pack(
        state,
        alignment[0, 0],
        ([lyric_keys[0], lyric_values[0]] if hops else [])
        + [queries[0], cotangent[0], keys[0], values[0]],
    )
    mate = lax.ppermute(to_mate, "seq", swap)
    attended = []
    carried = []
    after = []
    for chunk in range(CHUNKS):
        *pair, to_one, to_mid = merge(
            state, chunk, keys[0], values[0], lyric_keys[0], lyric_values[0], mate, hops, after
        )
        if hops:
            two = hop(pair[0], across)
        one = hop(to_one, partners)
        mid = hop(to_mid, between)
        if hops:
            lyrics = [pair[0], two, hop(two, partners)]
            after = [two]
        else:
            lyrics = [gathered]
        results = attention(
            chunk, meta, gains, queries[0], cotangent[0], keys[0], values[0], mate, one, mid,
            lyrics, groups, carried,
        )
        carried = [results[7], *results[:2]]
        attended.append((results[2:], lyrics))
    gain_total, output, grad_queries = carried

    grads = []
    own_halves, lyric_cols, from_mates = [], [], []
    if hops:
        gain_total = sum_over(sum_over(gain_total, "song", bits_of(songs)), "seq", [2])
    for chunk, (results, lyrics) in enumerate(attended):
        for_mate, key_grad, value_grad, to_one, to_mid, _, *parts = results
        one = hop(to_one, partners)
        mid = hop(to_mid, between)
        *grads, for_mate = finish_audio(
            state, chunk, gains, keys[0], mate, key_grad, value_grad, one, mid, for_mate, grads
        )
        if hops:
            held, for_two, to_two = parts
            sums = [gain_total] if chunk == CHUNKS - 1 else []
            two = hop(relay(for_two, hop(to_two, partners), sums), across)
            own_half, for_mate, total = finish_lyric(
                gains, lyrics[0], held, one, two, sums, for_mate
            )
            own_halves.append(own_half)
        else:
            lyric_cols.append(parts[0])
        from_mates.append(lax.ppermute(for_mate, "seq", swap))
    filled = [output, grad_queries, *grads]
    for chunk, from_mate in enumerate(from_mates[: CHUNKS - hops]):
        filled = fill_other(state, chunk, filled, from_mate)
    if hops:
        *filled, grad_lyric_keys, grad_lyric_values, gain_total = join(
            state, total, filled, own_halves, from_mates
        )
    else:
        gain_total = lax.psum(gain_total, ("song", "seq"))
        spread = lax.dynamic_update_slice(
            jnp.zeros((2 * total_rows, width), jnp.float32),
            jnp.concatenate(lyric_cols, axis=1).astype(jnp.float32),
            (0, core * (width // 2)),
        )
        lyric_key_sum, grad_lyric_values = [
            lax.psum_scatter(part, "seq", scatter_dimension=0, tiled=True)
            for part in (spread[:total_rows], spread[total_rows:])
        ]
        grad_lyric_keys = norm_lyric(gains, lyric_keys[0], lyric_key_sum)
        grad_lyric_values = grad_lyric_values.astype(jnp.bfloat16)
    output, grad_queries, grad_keys, grad_values = filled
    return (
        output[None],
        grad_queries[None],
        grad_keys[None],
        grad_values[None],
        grad_lyric_keys[None],
        grad_lyric_values[None],
        gain_total[0],
        gain_total[1],
    )


def solution(mesh):
    split = P("song", "seq", None)
    return jax.shard_map(
        body,
        mesh=mesh,
        in_specs=(split, split, split, split, split, P(), P(), split, split, P("song")),
        out_specs=(split, split, split, split, split, split, P(), P()),
        check_vma=False,
    )
```

time: 163 us -> 130 us (0.80)
  waiting for transfers between devices: 26.5 us -> 72.8 us
  starting transfers between devices: 66.3 us -> 21.8 us
  local copies, waits for them, and re-layouts: 28.5 us -> 10.9 us
  Pallas kernels: 33 us -> 22.4 us
  other arithmetic: 5.74 us -> 0.09 us
    ppermute x20 -> x8, starting transfers between devices: 57.2 us -> 14.6 us  [hop(): return lax.ppermute(block, 'seq', pairs)]
    ppermute x20 -> x8, waiting for transfers between devices: 18.9 us -> 47 us  [hop(): return lax.ppermute(block, 'seq', pairs)]
    ppermute x5 -> x3, waiting for transfers between devices: 5.91 us -> 20.2 us  [sum_over(): lax.ppermute(total, axis, [(i, i ^ bit) for i in range(count)])]
    unnamed x100 -> x34, local copies, waits for them, and re-layouts: 20.6 us -> 8.46 us
    pallas_call x11 -> x4, Pallas kernels: 25.3 us -> 17.9 us  [the longest x1 14 us: attention(): pl.pallas_call(functools.partial(attention_kernel, groups, bool(carried),...]
    slice x5 -> x0, local copies, waits for them, and re-layouts: 4.08 us -> none  [the longest x2 1.87 us: body(): down_two = hop(down_one[:rows], [(1, 0), (2, 1)])]
    add x5 -> x0, other arithmetic: 3.66 us -> none  [the longest x4 3.07 us: body(): to_up, to_down = (second + up_two[:rows], first + down_two[:rows])]
    ppermute x2 -> x1, waiting for transfers between devices: 0.01 us -> 3.02 us  [body(): from_mates.append(lax.ppermute(for_mate, 'seq', swap))]
  transfers between devices with their start and end apart: 32 -> 13, of which waited for: 7 -> 8; matrix products, arithmetic and copies ran while one was open for 8% -> 2% of each run, Pallas kernels for 19% -> 2%
where the time goes in v4:
time: 130 us
  waiting for transfers between devices  72.8 us (56%)
  Pallas kernels  22.4 us (17%)
  starting transfers between devices  21.8 us (17%)
  local copies, waits for them, and re-layouts  10.9 us (8%)
  between operations  1.51 us (1%)
    ppermute x8, waiting for transfers between devices, hop(): return lax.ppermute(block, 'seq', pairs)  47 us
    ppermute x3, waiting for transfers between devices, sum_over(): lax.ppermute(total, axis, [(i, i ^ bit) for i in range(count)])  20.2 us
    ppermute x8, starting transfers between devices, hop(): return lax.ppermute(block, 'seq', pairs)  14.6 us
    pallas_call x1, Pallas kernels, attention(): pl.pallas_call(functools.partial(attention_kernel, groups, bool(carried),...  14 us
    unnamed x34, local copies, waits for them, and re-layouts  8.46 us
    ppermute x3, starting transfers between devices, sum_over(): lax.ppermute(total, axis, [(i, i ^ bit) for i in range(count)])  6.53 us
    ppermute x1, waiting for transfers between devices, body(): from_mates.append(lax.ppermute(for_mate, 'seq', swap))  3.02 us
    pallas_call x1, Pallas kernels, finish_audio(): pl.pallas_call(functools.partial(finish_audio_kernel, head_size), grid_sp...  2.63 us
  transfers between devices with their start and end apart: 13, of which 8 were waited for; matrix products, arithmetic and copies ran while one was open for 2% of the time, Pallas kernels for 2%

profile of v4, /device:TPU:0, one launch (start us, length us, event | category | flops | bytes accessed | tf_op | source)
XLA Modules:
  0.0 129.5 jit_solution(14217954800369085698)
XLA Ops:
  0.7 0.1 pad_add_fusion.state_ref
  0.7 0.0 copy-start
  0.7 1.0 copy-done
  1.8 0.0 copy-start.2
  1.8 1.0 copy-done.2
  2.8 0.9 copy-done.4
  3.8 0.9 copy-done.6
  4.7 1.0 copy-done.7
  5.7 1.0 copy-done.9
  6.8 0.7 copy-done.13
  7.4 1.3 pack.1
  8.7 0.0 copy-start.14
  8.7 0.0 copy-start.15
  8.7 0.0 copy-start.16
  8.7 0.0 copy-start.1
  8.7 0.0 copy-start.3
  8.7 0.0 copy-start.8
  8.8 0.0 copy-start.10
  8.8 0.5 collective-permute-start
  9.3 2.6 %collective-permute-done.mate_ref = bf16[624,1024]{1,0:T(8,128)(2,1)S(1)} collective-permute-done((bf16[624,1024]{1,0:T(8,128)(2,1)S(1)}, bf16[624,1024]{1,0:T(8,128)(2,1)S(1)}, u32[]{:S(2)}, u32[]{:S(2)}) %collective-permute-start) | collective-permute-done | bytes 1277984 | tf_op jit(solution)/shard_map/ppermute | solution.py:705
  11.9 0.0 copy-done.5
  11.9 1.9 %merge.1 = (bf16[192,1024]{1,0:T(8,128)(2,1)S(1)}, bf16[448,1024]{1,0:T(8,128)(2,1)}, bf16[256,1024]{1,0:T(8,128)(2,1)}) custom-call(s32[2]{0:T(128)S(1)} %pad_add_fusion.state_ref, bf16[128,2048]{1,0:T(8,128)(2,1)S(1)} %bitcast.34, bf16[128,2048]{1,0:T(8,128)(2,1)S(1)} %bitcast.38, bf16[48,2048]{1,0:T(8,128)(2,1)S(1)} %bitcast.41, ...), custom_call_target="tpu_custom_call" | custom-call | flops 1 | bytes 1 | tf_op jit(solution)/shard_map/merge/pallas_call | solution.py:118
  13.9 2.9 %collective-permute-start.1 = (bf16[448,1024]{1,0:T(8,128)(2,1)}, bf16[448,1024]{1,0:T(8,128)(2,1)}, u32[]{:S(2)}, u32[]{:S(2)}) collective-permute-start(bf16[448,1024]{1,0:T(8,128)(2,1)} %get-tuple-element.36), channel_id=1, source_target_pairs={{0,2},{1,3},{2,0},{3,1},{4,6},{5,7},{6,4},{7,5},{8,10},{9,11},{10,... | collective-permute-start | bytes 2752520 | tf_op jit(solution)/shard_map/ppermute | solution.py:661
  16.8 2.6 %collective-permute-start.3 = (bf16[192,1024]{1,0:T(8,128)(2,1)S(1)}, bf16[192,1024]{1,0:T(8,128)(2,1)}, u32[]{:S(2)}, u32[]{:S(2)}) collective-permute-start(bf16[192,1024]{1,0:T(8,128)(2,1)S(1)} %get-tuple-element.35.refs_0_.raw_ref), channel_id=1, source_target_pairs={{0,4},{1,5},{2,6},{3,7},{4,0},{5,1},{6,2},{7,3},{8,12},{9,13},{10,... | collective-permute-start | bytes 1179656 | tf_op jit(solution)/shard_map/ppermute | solution.py:661
  19.4 0.7 copy-done.11
  20.1 1.5 %collective-permute-start.2 = (bf16[256,1024]{1,0:T(8,128)(2,1)}, bf16[256,1024]{1,0:T(8,128)(2,1)}, u32[]{:S(2)}, u32[]{:S(2)}) collective-permute-start(bf16[256,1024]{1,0:T(8,128)(2,1)} %get-tuple-element.37), channel_id=1, source_target_pairs={{2,4},{3,5},{4,2},{5,3},{10,12},{11,13},{12,10},{13,11},{18,20},{1... | collective-permute-start | bytes 1572872 | tf_op jit(solution)/shard_map/ppermute | solution.py:661
  21.6 23.8 %collective-permute-done.3.refs_1_ = bf16[192,1024]{1,0:T(8,128)(2,1)} collective-permute-done((bf16[192,1024]{1,0:T(8,128)(2,1)S(1)}, bf16[192,1024]{1,0:T(8,128)(2,1)}, u32[]{:S(2)}, u32[]{:S(2)}) %collective-permute-start.3) | collective-permute-done | bytes 393248 | tf_op jit(solution)/shard_map/ppermute | solution.py:661
  45.4 3.6 %collective-permute-start.4 = (bf16[192,1024]{1,0:T(8,128)(2,1)}, bf16[192,1024]{1,0:T(8,128)(2,1)}, u32[]{:S(2)}, u32[]{:S(2)}) collective-permute-start(bf16[192,1024]{1,0:T(8,128)(2,1)} %collective-permute-done.3.refs_1_), channel_id=1, source_target_pairs={{0,2},{1,3},{2,0},{3,1},{4,6},{5,7},{6,4},{7,5},{8,10},{9,11},{10,... | collective-permute-start | bytes 1179656 | tf_op jit(solution)/shard_map/ppermute | solution.py:661
  49.6 0.0 copy-done.14
  49.6 0.6 fusion
  50.2 1.4 %stack.77.meta_ref = s32[15]{0:T(128)S(1)} concatenate(s32[1]{0:T(128)} %bitcast, s32[1]{0:T(128)} %bitcast.1, s32[1]{0:T(128)} %bitcast.11, s32[1]{0:T(128)} %bitcast.12, s32[1]{0:T(128)S(6)} %copy.28, s32[1]{0:T(128)} %bitcast.13, s32[1]{0:T(128)} %bitcast.14, s32[1]{0:T(128)} %bitcast.15, s32[1]{0:T(128)} %bitcast.16, s32[1]{0:T(128)} %bitcast.17, s32[1]{0:T(128)} %bitcast.18, ...), dimensions={0} | concatenate | bytes 120 | tf_op jit(solution)/shard_map/stack | solution.py:688
  51.6 0.0 copy-done.15
  51.6 0.0 copy-done.16
  51.6 0.0 collective-permute-done.2.mid_ref
  51.6 6.2 %collective-permute-done.4.refs_2_ = bf16[192,1024]{1,0:T(8,128)(2,1)} collective-permute-done((bf16[192,1024]{1,0:T(8,128)(2,1)}, bf16[192,1024]{1,0:T(8,128)(2,1)}, u32[]{:S(2)}, u32[]{:S(2)}) %collective-permute-start.4) | collective-permute-done | bytes 393248 | tf_op jit(solution)/shard_map/ppermute | solution.py:661
  57.9 0.0 collective-permute-done.1.one_ref
  57.9 0.0 copy-done.1
  57.9 0.0 copy-done.3
  57.9 0.0 copy-done.8
  57.9 0.0 copy-done.10
  57.9 0.0 copy-start.12
  57.9 1.0 copy-done.12
  58.9 14.0 %attention.1 = (bf16[128,2048]{1,0:T(8,128)(2,1)}, bf16[128,2048]{1,0:T(8,128)(2,1)}, bf16[256,1024]{1,0:T(8,128)(2,1)S(1)}, f32[256,1024]{1,0:T(8,128)S(1)}, f3...) custom-call(s32[15]{0:T(128)S(1)} %stack.77.meta_ref, ...), custom_call_target="tpu_custom_call" | custom-call | flops 2415919104 | bytes 16777216 | tf_op jit(solution)/shard_map/attention/pallas_call | solution.py:338
  72.9 1.7 %collective-permute-start.5 = (bf16[448,1024]{1,0:T(8,128)(2,1)S(1)}, bf16[448,1024]{1,0:T(8,128)(2,1)S(1)}, u32[]{:S(2)}, u32[]{:S(2)}) collective-permute-start(bf16[448,1024]{1,0:T(8,128)(2,1)S(1)} %get-tuple-element.39), channel_id=1, source_target_pairs={{0,2},{1,3},{2,0},{3,1},{4,6},{5,7},{6,4},{7,5},{8,10},{9,11},{10,... | collective-permute-start | bytes 2752520 | tf_op jit(solution)/shard_map/ppermute | solution.py:661
  74.7 0.3 collective-permute-start.6
  75.0 0.7 collective-permute-start.11
  75.6 1.6 %collective-permute-start.7 = (f32[8,128]{1,0:T(8,128)S(1)}, f32[8,128]{1,0:T(8,128)S(1)}, u32[]{:S(2)}, u32[]{:S(2)}) collective-permute-start(f32[8,128]{1,0:T(8,128)S(1)} %get-tuple-element.42), channel_id=1, source_target_pairs={{0,8},{8,0},{16,24},{24,16},{1,9},{9,1},{17,25},{25,17},{2,10},{10... | collective-permute-start | bytes 12296 | tf_op jit(solution)/shard_map/ppermute | solution.py:630
  77.2 2.1 %collective-permute-done.7 = f32[8,128]{1,0:T(8,128)S(1)} collective-permute-done((f32[8,128]{1,0:T(8,128)S(1)}, f32[8,128]{1,0:T(8,128)S(1)}, u32[]{:S(2)}, u32[]{:S(2)}) %collective-permute-start.7) | collective-permute-done | bytes 4128 | tf_op jit(solution)/shard_map/ppermute | solution.py:630
  79.3 1.5 %collective-permute-start.8 = (f32[8,128]{1,0:T(8,128)S(1)}, f32[8,128]{1,0:T(8,128)S(1)}, u32[]{:S(2)}, u32[]{:S(2)}) collective-permute-start(f32[8,128]{1,0:T(8,128)S(1)} %add.51), channel_id=1, source_target_pairs={{0,16},{8,24},{16,0},{24,8},{1,17},{9,25},{17,1},{25,9},{2,18},{10... | collective-permute-start | bytes 12296 | tf_op jit(solution)/shard_map/ppermute | solution.py:630
  80.8 2.1 %collective-permute-done.8 = f32[8,128]{1,0:T(8,128)S(1)} collective-permute-done((f32[8,128]{1,0:T(8,128)S(1)}, f32[8,128]{1,0:T(8,128)S(1)}, u32[]{:S(2)}, u32[]{:S(2)}) %collective-permute-start.8) | collective-permute-done | bytes 4128 | tf_op jit(solution)/shard_map/ppermute | solution.py:630
  82.9 3.5 %collective-permute-start.9 = (f32[8,128]{1,0:T(8,128)S(1)}, f32[8,128]{1,0:T(8,128)S(1)}, u32[]{:S(2)}, u32[]{:S(2)}) collective-permute-start(f32[8,128]{1,0:T(8,128)S(1)} %add.52), channel_id=1, source_target_pairs={{0,2},{1,3},{2,0},{3,1},{4,6},{5,7},{6,4},{7,5},{8,10},{9,11},{10,... | collective-permute-start | bytes 12296 | tf_op jit(solution)/shard_map/ppermute | solution.py:630
  86.4 16.0 %collective-permute-done.9 = f32[8,128]{1,0:T(8,128)S(1)} collective-permute-done((f32[8,128]{1,0:T(8,128)S(1)}, f32[8,128]{1,0:T(8,128)S(1)}, u32[]{:S(2)}, u32[]{:S(2)}) %collective-permute-start.9) | collective-permute-done | bytes 4128 | tf_op jit(solution)/shard_map/ppermute | solution.py:630
  102.4 0.0 collective-permute-done.6.arrived_ref
  102.4 0.2 relay.1
  102.6 1.4 %collective-permute-start.10 = (bf16[224,1024]{1,0:T(8,128)(2,1)S(1)}, bf16[224,1024]{1,0:T(8,128)(2,1)S(1)}, u32[]{:S(2)}, u32[]{:S(2)}) collective-permute-start(bf16[224,1024]{1,0:T(8,128)(2,1)S(1)} %relay.1), channel_id=1, source_target_pairs={{0,4},{1,5},{2,6},{3,7},{4,0},{5,1},{6,2},{7,3},{8,12},{9,13},{10,... | collective-permute-start | bytes 1376264 | tf_op jit(solution)/shard_map/ppermute | solution.py:661
  104.0 0.0 collective-permute-done.11.mid_ref
  104.0 0.0 collective-permute-done.5.one_ref
  104.0 2.6 %finish_audio.1 = (bf16[128,2048]{1,0:T(8,128)(2,1)}, bf16[128,2048]{1,0:T(8,128)(2,1)}, bf16[640,1024]{1,0:T(8,128)(2,1)S(1)}) custom-call(s32[2]{0:T(128)S(1)} %pad_add_fusion.state_ref, f32[2,128]{1,0:T(2,128)S(1)} %pad_maximum_fusion.gain_ref, bf16[128,2048]{1,0:T(8,128)(2,1)S(1)} %bitcast.36, bf16[624,1024]{1,0:T(8,128)(2,1)S(1)} %collective-permute-done.mate_ref, ...), custom_call_target="tpu_custom_call" | custom-call | flops 1 | bytes 1 | tf_op jit(solution)/shard_map/finish_audio/pallas_call | solution.py:462
  106.6 16.9 %collective-permute-done.10.two_ref = bf16[224,1024]{1,0:T(8,128)(2,1)S(1)} collective-permute-done((bf16[224,1024]{1,0:T(8,128)(2,1)S(1)}, bf16[224,1024]{1,0:T(8,128)(2,1)S(1)}, u32[]{:S(2)}, u32[]{:S(2)}) %collective-permute-start.10) | collective-permute-done | bytes 458784 | tf_op jit(solution)/shard_map/ppermute | solution.py:661
  123.6 0.6 finish_lyric.1
  124.2 0.1 collective-permute-start.12
  124.3 3.0 %collective-permute-done.12.refs_1_ = bf16[640,1024]{1,0:T(8,128)(2,1)S(1)} collective-permute-done((bf16[640,1024]{1,0:T(8,128)(2,1)S(1)}, bf16[640,1024]{1,0:T(8,128)(2,1)S(1)}, u32[]{:S(2)}, u32[]{:S(2)}) %collective-permute-start.12) | collective-permute-done | bytes 1310752 | tf_op jit(solution)/shard_map/ppermute | solution.py:751
  127.3 1.7 %join.1 = (bf16[128,2048]{1,0:T(8,128)(2,1)}, bf16[128,2048]{1,0:T(8,128)(2,1)}, bf16[128,2048]{1,0:T(8,128)(2,1)}, bf16[128,2048]{1,0:T(8,128)(2,1)}, bf16[48,2...) custom-call(s32[2]{0:T(128)S(1)} %pad_add_fusion.state_ref, ...), custom_call_target="tpu_custom_call", output_to_operand_aliasing={{0}: (4, {}), {1}: (5, {}), {2}: (6, {}), {3}: (7, {})} | custom-call | flops 1 | bytes 1 | tf_op jit(solution)/shard_map/join/pallas_call | solution.py:592
  129.0 0.5 slice_bitcast_fusion
  (11 shorter events, 0.0 us)
Async XLA Ops:
  0.7 1.0 copy-start
  1.8 1.0 copy-start.2
  2.8 0.9 copy-start.4
  3.8 0.9 copy-start.6
  4.7 1.0 copy-start.7
  5.7 1.0 copy-start.9
  6.8 0.7 copy-start.13
  7.4 4.5 %copy-start.5 = (bf16[1,48,2048]{2,1,0:T(8,128)(2,1)S(1)}, bf16[1,48,2048]{2,1,0:T(8,128)(2,1)}, u32[]{:S(2)}) copy-start(bf16[1,48,2048]{2,1,0:T(8,128)(2,1)} %param.13) | copy-start | bytes 589828
  8.7 40.9 %copy-start.14 = (s32[1,1,2]{2,1,0:T(1,128)S(1)}, s32[1,1,2]{2,1,0:T(1,128)}, u32[]{:S(2)}) copy-start(s32[1,1,2]{2,1,0:T(1,128)} %param.18) | copy-start | bytes 28
  8.7 42.9 %copy-start.15 = (f32[128]{0:T(128)S(1)}, f32[128]{0:T(128)}, u32[]{:S(2)}) copy-start(f32[128]{0:T(128)} %param.16) | copy-start | bytes 1540
  8.7 42.9 %copy-start.16 = (f32[128]{0:T(128)S(1)}, f32[128]{0:T(128)}, u32[]{:S(2)}) copy-start(f32[128]{0:T(128)} %param.15) | copy-start | bytes 1540
  8.7 49.1 %copy-start.1 = (bf16[1,128,2048]{2,1,0:T(8,128)(2,1)S(1)}, bf16[1,128,2048]{2,1,0:T(8,128)(2,1)}, u32[]{:S(2)}) copy-start(bf16[1,128,2048]{2,1,0:T(8,128)(2,1)} %param.11) | copy-start | bytes 1572868
  8.7 49.1 %copy-start.3 = (bf16[1,128,2048]{2,1,0:T(8,128)(2,1)S(1)}, bf16[1,128,2048]{2,1,0:T(8,128)(2,1)}, u32[]{:S(2)}) copy-start(bf16[1,128,2048]{2,1,0:T(8,128)(2,1)} %param.12) | copy-start | bytes 1572868
  8.7 49.1 %copy-start.8 = (bf16[1,128,2048]{2,1,0:T(8,128)(2,1)S(1)}, bf16[1,128,2048]{2,1,0:T(8,128)(2,1)}, u32[]{:S(2)}) copy-start(bf16[1,128,2048]{2,1,0:T(8,128)(2,1)} %param.10) | copy-start | bytes 1572868
  8.8 49.1 %copy-start.10 = (bf16[1,128,2048]{2,1,0:T(8,128)(2,1)S(1)}, bf16[1,128,2048]{2,1,0:T(8,128)(2,1)}, u32[]{:S(2)}) copy-start(bf16[1,128,2048]{2,1,0:T(8,128)(2,1)} %param.17) | copy-start | bytes 1572868
  8.8 3.1 %collective-permute-start = (bf16[624,1024]{1,0:T(8,128)(2,1)S(1)}, bf16[624,1024]{1,0:T(8,128)(2,1)S(1)}, u32[]{:S(2)}, u32[]{:S(2)}) collective-permute-start(bf16[624,1024]{1,0:T(8,128)(2,1)S(1)} %pack.1), channel_id=1, source_target_pairs={{0,1},{1,0},{2,3},{3,2},{4,5},{5,4},{6,7},{7,6},{8,9},{9,8},{10,11... | collective-permute-start | bytes 3833864 | tf_op jit(solution)/shard_map/ppermute | solution.py:705
  13.9 44.0 %collective-permute-start.1 = (bf16[448,1024]{1,0:T(8,128)(2,1)}, bf16[448,1024]{1,0:T(8,128)(2,1)}, u32[]{:S(2)}, u32[]{:S(2)}) collective-permute-start(bf16[448,1024]{1,0:T(8,128)(2,1)} %get-tuple-element.36), channel_id=1, source_target_pairs={{0,2},{1,3},{2,0},{3,1},{4,6},{5,7},{6,4},{7,5},{8,10},{9,11},{10,... | collective-permute-start | bytes 2752520 | tf_op jit(solution)/shard_map/ppermute | solution.py:661
  16.8 28.6 %collective-permute-start.3 = (bf16[192,1024]{1,0:T(8,128)(2,1)S(1)}, bf16[192,1024]{1,0:T(8,128)(2,1)}, u32[]{:S(2)}, u32[]{:S(2)}) collective-permute-start(bf16[192,1024]{1,0:T(8,128)(2,1)S(1)} %get-tuple-element.35.refs_0_.raw_ref), channel_id=1, source_target_pairs={{0,4},{1,5},{2,6},{3,7},{4,0},{5,1},{6,2},{7,3},{8,12},{9,13},{10,... | collective-permute-start | bytes 1179656 | tf_op jit(solution)/shard_map/ppermute | solution.py:661
  19.4 0.7 copy-start.11
  20.1 31.5 %collective-permute-start.2 = (bf16[256,1024]{1,0:T(8,128)(2,1)}, bf16[256,1024]{1,0:T(8,128)(2,1)}, u32[]{:S(2)}, u32[]{:S(2)}) collective-permute-start(bf16[256,1024]{1,0:T(8,128)(2,1)} %get-tuple-element.37), channel_id=1, source_target_pairs={{2,4},{3,5},{4,2},{5,3},{10,12},{11,13},{12,10},{13,11},{18,20},{1... | collective-permute-start | bytes 1572872 | tf_op jit(solution)/shard_map/ppermute | solution.py:661
  45.4 12.5 %collective-permute-start.4 = (bf16[192,1024]{1,0:T(8,128)(2,1)}, bf16[192,1024]{1,0:T(8,128)(2,1)}, u32[]{:S(2)}, u32[]{:S(2)}) collective-permute-start(bf16[192,1024]{1,0:T(8,128)(2,1)} %collective-permute-done.3.refs_1_), channel_id=1, source_target_pairs={{0,2},{1,3},{2,0},{3,1},{4,6},{5,7},{6,4},{7,5},{8,10},{9,11},{10,... | collective-permute-start | bytes 1179656 | tf_op jit(solution)/shard_map/ppermute | solution.py:661
  57.9 1.0 copy-start.12
  72.9 31.1 %collective-permute-start.5 = (bf16[448,1024]{1,0:T(8,128)(2,1)S(1)}, bf16[448,1024]{1,0:T(8,128)(2,1)S(1)}, u32[]{:S(2)}, u32[]{:S(2)}) collective-permute-start(bf16[448,1024]{1,0:T(8,128)(2,1)S(1)} %get-tuple-element.39), channel_id=1, source_target_pairs={{0,2},{1,3},{2,0},{3,1},{4,6},{5,7},{6,4},{7,5},{8,10},{9,11},{10,... | collective-permute-start | bytes 2752520 | tf_op jit(solution)/shard_map/ppermute | solution.py:661
  74.7 27.7 %collective-permute-start.6 = (bf16[192,1024]{1,0:T(8,128)(2,1)S(1)}, bf16[192,1024]{1,0:T(8,128)(2,1)S(1)}, u32[]{:S(2)}, u32[]{:S(2)}) collective-permute-start(bf16[192,1024]{1,0:T(8,128)(2,1)S(1)} %get-tuple-element.41), channel_id=1, source_target_pairs={{0,2},{1,3},{2,0},{3,1},{4,6},{5,7},{6,4},{7,5},{8,10},{9,11},{10,... | collective-permute-start | bytes 1179656 | tf_op jit(solution)/shard_map/ppermute | solution.py:661
  75.0 29.1 %collective-permute-start.11 = (bf16[256,1024]{1,0:T(8,128)(2,1)S(1)}, bf16[256,1024]{1,0:T(8,128)(2,1)S(1)}, u32[]{:S(2)}, u32[]{:S(2)}) collective-permute-start(bf16[256,1024]{1,0:T(8,128)(2,1)S(1)} %get-tuple-element.45), channel_id=1, source_target_pairs={{2,4},{3,5},{4,2},{5,3},{10,12},{11,13},{12,10},{13,11},{18,20},{1... | collective-permute-start | bytes 1572872 | tf_op jit(solution)/shard_map/ppermute | solution.py:661
  75.6 3.7 %collective-permute-start.7 = (f32[8,128]{1,0:T(8,128)S(1)}, f32[8,128]{1,0:T(8,128)S(1)}, u32[]{:S(2)}, u32[]{:S(2)}) collective-permute-start(f32[8,128]{1,0:T(8,128)S(1)} %get-tuple-element.42), channel_id=1, source_target_pairs={{0,8},{8,0},{16,24},{24,16},{1,9},{9,1},{17,25},{25,17},{2,10},{10... | collective-permute-start | bytes 12296 | tf_op jit(solution)/shard_map/ppermute | solution.py:630
  79.3 3.6 %collective-permute-start.8 = (f32[8,128]{1,0:T(8,128)S(1)}, f32[8,128]{1,0:T(8,128)S(1)}, u32[]{:S(2)}, u32[]{:S(2)}) collective-permute-start(f32[8,128]{1,0:T(8,128)S(1)} %add.51), channel_id=1, source_target_pairs={{0,16},{8,24},{16,0},{24,8},{1,17},{9,25},{17,1},{25,9},{2,18},{10... | collective-permute-start | bytes 12296 | tf_op jit(solution)/shard_map/ppermute | solution.py:630
  82.9 19.4 %collective-permute-start.9 = (f32[8,128]{1,0:T(8,128)S(1)}, f32[8,128]{1,0:T(8,128)S(1)}, u32[]{:S(2)}, u32[]{:S(2)}) collective-permute-start(f32[8,128]{1,0:T(8,128)S(1)} %add.52), channel_id=1, source_target_pairs={{0,2},{1,3},{2,0},{3,1},{4,6},{5,7},{6,4},{7,5},{8,10},{9,11},{10,... | collective-permute-start | bytes 12296 | tf_op jit(solution)/shard_map/ppermute | solution.py:630
  102.6 21.0 %collective-permute-start.10 = (bf16[224,1024]{1,0:T(8,128)(2,1)S(1)}, bf16[224,1024]{1,0:T(8,128)(2,1)S(1)}, u32[]{:S(2)}, u32[]{:S(2)}) collective-permute-start(bf16[224,1024]{1,0:T(8,128)(2,1)S(1)} %relay.1), channel_id=1, source_target_pairs={{0,4},{1,5},{2,6},{3,7},{4,0},{5,1},{6,2},{7,3},{8,12},{9,13},{10,... | collective-permute-start | bytes 1376264 | tf_op jit(solution)/shard_map/ppermute | solution.py:661
  124.2 3.1 %collective-permute-start.12 = (bf16[640,1024]{1,0:T(8,128)(2,1)S(1)}, bf16[640,1024]{1,0:T(8,128)(2,1)S(1)}, u32[]{:S(2)}, u32[]{:S(2)}) collective-permute-start(bf16[640,1024]{1,0:T(8,128)(2,1)S(1)} %get-tuple-element.50), channel_id=1, source_target_pairs={{0,1},{1,0},{2,3},{3,2},{4,5},{5,4},{6,7},{7,6},{8,9},{9,8},{10,11... | collective-permute-start | bytes 3932168 | tf_op jit(solution)/shard_map/ppermute | solution.py:751

commit v5 on v4

--- a/solution.py
+++ b/solution.py
@@ -14,7 +14,9 @@
 CHUNKS = 1
 VMEM_LIMIT = 8 * 1024 * 1024
 ATTENTION_VMEM_LIMIT = 24 * 1024 * 1024
+PACK_VMEM_LIMIT = 60 * 1024 * 1024
 GAIN_ROWS = 32
+ALIGN_ROWS = 32
 SMALL = pl.CostEstimate(flops=1, bytes_accessed=1, transcendentals=0)
 
 
@@ -42,27 +44,23 @@
 
 
 def pack_kernel(state_ref, align_ref, *refs):
-    ins, out_ref = refs[:-1], refs[-1]
+    out_ref = refs[-1]
     start = 0
-    for ref in ins[:-4]:
+    for ref in refs[:-1]:
         out_ref[start : start + ref.shape[0], :] = ref[...]
         start += ref.shape[0]
-    row = lax.broadcasted_iota(jnp.int32, (16, out_ref.shape[1]), 0)
-    tiles = jnp.zeros((16, out_ref.shape[1]), jnp.int32)
+    row = lax.broadcasted_iota(jnp.int32, (ALIGN_ROWS, out_ref.shape[1]), 0)
+    tiles = jnp.zeros((ALIGN_ROWS, out_ref.shape[1]), jnp.int32)
     for slot in range(TILES):
         tiles = jnp.where(row == slot, align_ref[slot], tiles)
-    out_ref[start : start + 16, :] = tiles.astype(jnp.float32).astype(jnp.bfloat16)
-    start += 16
-    for ref in ins[-4:]:
-        out_ref[start : start + ref.shape[0], :] = ref[...]
-        start += ref.shape[0]
+    out_ref[start:, :] = tiles.astype(jnp.float32).astype(jnp.bfloat16)
 
 
 def pack(state, align, arrays):
     width = arrays[0].shape[1]
     half = width // 2
     step = half // 4
-    rows = sum(array.shape[0] for array in arrays) + 16
+    rows = sum(array.shape[0] for array in arrays) + ALIGN_ROWS
     return pl.pallas_call(
         pack_kernel,
         grid_spec=pltpu.PrefetchScalarGridSpec(
@@ -77,59 +75,74 @@
             out_specs=pl.BlockSpec((rows, step), lambda i, state, _: (0, i)),
         ),
         out_shape=jax.ShapeDtypeStruct((rows, half), jnp.bfloat16),
-        compiler_params=params(),
+        compiler_params=params(PACK_VMEM_LIMIT),
         cost_estimate=SMALL,
         name="pack",
     )(state, align, *arrays)
 
 
-def merge_kernel(lyric, state_ref, key_ref, value_ref, lkey_ref, lvalue_ref, mate_ref, *refs):
-    frames = key_ref.shape[0]
-    first = mate_ref.shape[0] - 2 * frames
-    one_ref, mid_ref = refs[-2:]
-    if lyric:
-        pair_ref = refs[-3]
-        pair_ref[0:lyric, :] = lkey_ref[...]
-        pair_ref[lyric : 2 * lyric, :] = lvalue_ref[...]
-        pair_ref[2 * lyric :, :] = mate_ref[0 : 2 * lyric, :]
-        one_ref[0 : 4 * lyric, :] = pair_ref[...]
-    for ref, start, touching in ((one_ref, 4 * lyric, 1), (mid_ref, 0, 0)):
-        mine = state_ref[1] == touching
-        ref[start : start + frames, :] = jnp.where(
-            mine, key_ref[...], mate_ref[first : first + frames, :]
-        )
-        ref[start + frames :, :] = jnp.where(
-            mine, value_ref[...], mate_ref[first + frames :, :]
-        )
-
-
-def merge(state, chunk, key, value, lyric_key, lyric_value, mate, with_lyric, after):
-    frames, width = key.shape
-    lyric = lyric_key.shape[0] if with_lyric else 0
+def pair_kernel(state_ref, lkey_ref, lvalue_ref, mate_ref, pair_ref):
+    lyric = lkey_ref.shape[0]
+    pair_ref[0:lyric, :] = lkey_ref[...]
+    pair_ref[lyric : 2 * lyric, :] = lvalue_ref[...]
+    pair_ref[2 * lyric :, :] = mate_ref[0 : 2 * lyric, :]
+
+
+def pair_lyrics(state, chunk, lyric_key, lyric_value, mate):
+    rows, width = lyric_key.shape
     size = width // 2 // CHUNKS
     step = size // 2
-    out_rows = ([4 * lyric] if lyric else []) + [2 * frames + 4 * lyric, 2 * frames]
-
-    def own(array):
-        return pl.BlockSpec(
-            (array.shape[0], step), lambda i, state: (0, (state[0] * CHUNKS + chunk) * 2 + i)
-        )
-
-    return pl.pallas_call(
-        functools.partial(merge_kernel, lyric),
+    last = mate.shape[0] // BLK - 1
+    own = pl.BlockSpec((rows, step), lambda i, state: (0, (state[0] * CHUNKS + chunk) * 2 + i))
+    return pl.pallas_call(
+        pair_kernel,
         grid_spec=pltpu.PrefetchScalarGridSpec(
             num_scalar_prefetch=1,
             grid=(2,),
-            in_specs=[own(key), own(value), own(lyric_key), own(lyric_value)]
-            + [pl.BlockSpec((mate.shape[0], step), lambda i, state: (0, chunk * 2 + i))]
-            + [pl.BlockSpec(memory_space=pl.ANY)] * len(after),
-            out_specs=[pl.BlockSpec((rows, step), lambda i, state: (0, i)) for rows in out_rows],
+            in_specs=[own, own, pl.BlockSpec((BLK, step), lambda i, state: (last, chunk * 2 + i))],
+            out_specs=pl.BlockSpec((4 * rows, step), lambda i, state: (0, i)),
         ),
-        out_shape=[jax.ShapeDtypeStruct((rows, size), jnp.bfloat16) for rows in out_rows],
+        out_shape=jax.ShapeDtypeStruct((4 * rows, size), jnp.bfloat16),
         compiler_params=params(),
         cost_estimate=SMALL,
-        name="merge",
-    )(state, key, value, lyric_key, lyric_value, mate, *after)
+        name="pair_lyrics",
+    )(state, lyric_key, lyric_value, mate)
+
+
+def edge_kernel(touching, state_ref, key_ref, value_ref, mate_key_ref, mate_value_ref, *refs):
+    out_ref = refs[-1]
+    frames = key_ref.shape[0]
+    first = out_ref.shape[0] - 2 * frames
+    if first:
+        out_ref[0:first, :] = refs[0][...]
+    mine = state_ref[1] == touching
+    out_ref[first : first + frames, :] = jnp.where(mine, key_ref[...], mate_key_ref[...])
+    out_ref[first + frames :, :] = jnp.where(mine, value_ref[...], mate_value_ref[...])
+
+
+def edge(state, chunk, touching, key, value, mate, lead, after):
+    frames, width = key.shape
+    size = width // 2 // CHUNKS
+    step = size // 2
+    rows = sum(array.shape[0] for array in lead) + 2 * frames
+    own = pl.BlockSpec((frames, step), lambda i, state: (0, (state[0] * CHUNKS + chunk) * 2 + i))
+    return pl.pallas_call(
+        functools.partial(edge_kernel, touching),
+        grid_spec=pltpu.PrefetchScalarGridSpec(
+            num_scalar_prefetch=1,
+            grid=(2,),
+            in_specs=[own, own]
+            + [pl.BlockSpec((frames, step), lambda i, state: (2, chunk * 2 + i))]
+            + [pl.BlockSpec((frames, step), lambda i, state: (3, chunk * 2 + i))]
+            + [pl.BlockSpec((array.shape[0], step), lambda i, state: (0, i)) for array in lead]
+            + [pl.BlockSpec(memory_space=pl.ANY)] * len(after),
+            out_specs=pl.BlockSpec((rows, step), lambda i, state: (0, i)),
+        ),
+        out_shape=jax.ShapeDtypeStruct((rows, size), jnp.bfloat16),
+        compiler_params=params(),
+        cost_estimate=SMALL,
+        name="edge",
+    )(state, key, value, mate, mate, *lead, *after)
 
 
 def attention_kernel(
@@ -149,7 +162,7 @@
     runs = [(index, run) for index, group in enumerate(groups) for run in group]
     main = 2 * frames + sum(run[2] for _, run in runs)
     lanes = 2 * frames
-    first = mate_ref.shape[0] - 4 * frames
+    align = mate_ref.shape[0] - ALIGN_ROWS
     touching = meta_ref[1] == 1
 
     @pl.when(pl.program_id(0) == 0)
@@ -158,7 +171,7 @@
             gain_grad_ref[...] = gain_before_ref[...]
         else:
             gain_grad_ref[...] = jnp.zeros_like(gain_grad_ref)
-        mate_tiles = mate_ref[first - 16 : first, 0:frames].astype(jnp.float32).astype(jnp.int32)
+        mate_tiles = mate_ref[align:, 0:frames].astype(jnp.float32).astype(jnp.int32)
         start = 0
         for number, (_, (_, _, rows)) in enumerate(runs):
             row = lax.broadcasted_iota(jnp.int32, (rows, lanes), 0) + meta_ref[7 + number]
@@ -194,7 +207,7 @@
         far_rows = jnp.where(touching, mid_rows, one_rows)
 
         def from_mate(number):
-            return mate_ref[first + number * frames : first + (number + 1) * frames, cols]
+            return mate_ref[number * frames : (number + 1) * frames, cols]
 
         query = jnp.concatenate([query_ref[:, cols], from_mate(0)], axis=0)
         query = query.astype(jnp.float32)
@@ -424,7 +437,6 @@
     own, mate = slice(0, frames), slice(frames, 2 * frames)
     first = one_ref.shape[0] - 2 * frames
     touching = state_ref[1] == 1
-    mate_keys = mate_ref.shape[0] - 2 * frames
     to_mate_ref[0 : 2 * frames, :] = ready_ref[...]
     for head in range(raw_ref.shape[1] // head_size):
         cols = slice(head * head_size, (head + 1) * head_size)
@@ -439,16 +451,16 @@
             jnp.bfloat16
         )
         to_mate_ref[2 * frames : 3 * frames, cols] = through_norm(
-            mate_ref[mate_keys : mate_keys + frames, cols],
-            key_grad_ref[mate, cols] + for_mate[:frames],
-            k_gain,
-        )
-        to_mate_ref[3 * frames : 4 * frames, cols] = (
+            mate_ref[:, cols], key_grad_ref[mate, cols] + for_mate[:frames], k_gain
+        )
+        to_mate_ref[3 * frames :, cols] = (
             value_grad_ref[mate, cols] + for_mate[frames:]
         ).astype(jnp.bfloat16)
 
 
-def finish_audio(state, chunk, gains, raw, mate, key_grad, value_grad, one, mid, ready, carried):
+def finish_audio(
+    state, chunk, gains, raw, mate, key_grad, value_grad, one, mid, ready, carried, to_mate
+):
     frames, width = raw.shape
     head_size = gains.shape[1]
     size = width // 2 // CHUNKS
@@ -459,38 +471,41 @@
 
     own = pl.BlockSpec((frames, step), lambda i, core: (0, (core[0] * CHUNKS + chunk) * 2 + i))
     arrays = (key_grad, value_grad, one, mid, ready)
+    aliases = {9 + i: i for i in range(len(carried))}
+    if to_mate:
+        aliases[9 + len(carried)] = 2
     return pl.pallas_call(
         functools.partial(finish_audio_kernel, head_size),
         grid_spec=pltpu.PrefetchScalarGridSpec(
             num_scalar_prefetch=1,
             grid=(2,),
             in_specs=[pl.BlockSpec(gains.shape, lambda i, core: (0, 0)), own]
-            + [pl.BlockSpec((mate.shape[0], step), lambda i, core: (0, chunk * 2 + i))]
+            + [pl.BlockSpec((frames, step), lambda i, core: (2, chunk * 2 + i))]
             + [columns(array) for array in arrays]
-            + [pl.BlockSpec(memory_space=pl.ANY)] * len(carried),
+            + [pl.BlockSpec(memory_space=pl.ANY)] * len(carried + to_mate),
             out_specs=[own] * 2 + [pl.BlockSpec((4 * frames, step), lambda i, core: (0, i))],
         ),
         out_shape=[jax.ShapeDtypeStruct((frames, width), jnp.bfloat16)] * 2
         + [jax.ShapeDtypeStruct((5 * frames, size), jnp.bfloat16)],
-        input_output_aliases={9 + i: i for i in range(len(carried))},
+        input_output_aliases=aliases,
         compiler_params=params(),
         cost_estimate=SMALL,
         name="finish_audio",
-    )(state, gains, raw, mate, *arrays, *carried)
+    )(state, gains, raw, mate, *arrays, *carried, *to_mate)
 
 
 def relay_kernel(head_size, part_ref, arrived_ref, *refs):
-    out_ref = refs[-1]
+    out_ref = refs[-2]
     rows = part_ref.shape[0]
     out_ref[0:rows, :] = (
         part_ref[...].astype(jnp.float32) + arrived_ref[...].astype(jnp.float32)
     ).astype(jnp.bfloat16)
-    if len(refs) == 2:
+    if head_size:
         out_ref[rows:, 0:head_size] = split_rows(refs[0][...])
         out_ref[rows:, head_size:] = jnp.zeros_like(out_ref[rows:, head_size:])
 
 
-def relay(part, arrived, sums):
+def relay(part, arrived, sums, later):
     rows, size = part.shape
     step = size // 2
     out_rows = rows + GAIN_ROWS * len(sums)
@@ -498,13 +513,22 @@
     return pl.pallas_call(
         functools.partial(relay_kernel, sums[0].shape[1] if sums else 0),
         grid=(2,),
-        in_specs=[spec] * 2 + [pl.BlockSpec(total.shape, lambda i: (0, 0)) for total in sums],
-        out_specs=pl.BlockSpec((out_rows, step), lambda i: (0, i)),
-        out_shape=jax.ShapeDtypeStruct((out_rows, size), jnp.bfloat16),
+        in_specs=[spec] * 2
+        + [pl.BlockSpec(total.shape, lambda i: (0, 0)) for total in sums]
+        + [pl.BlockSpec(memory_space=pl.ANY)],
+        out_specs=[
+            pl.BlockSpec((out_rows, step), lambda i: (0, i)),
+            pl.BlockSpec(memory_space=pl.ANY),
+        ],
+        out_shape=[
+            jax.ShapeDtypeStruct((out_rows, size), jnp.bfloat16),
+            jax.ShapeDtypeStruct(later.shape, later.dtype),
+        ],
+        input_output_aliases={2 + len(sums): 1},
         compiler_params=params(),
         cost_estimate=SMALL,
         name="relay",
-    )(part, arrived, *sums)
+    )(part, arrived, *sums, later)
 
 
 def finish_lyric_kernel(head_size, gain_ref, raw_ref, held_ref, one_ref, two_ref, *refs):
@@ -512,7 +536,7 @@
     rows = lyric_rows // 4
     own_ref, to_mate_ref, total_ref = refs[-3:]
     k_gain = gain_ref[1:2, :]
-    if len(refs) == 5:
+    if len(refs) == 4:
         total_ref[...] = refs[0][...] + joined_rows(two_ref[lyric_rows:, 0:head_size])
     else:
         total_ref[...] = jnp.zeros_like(total_ref)
@@ -530,12 +554,11 @@
         to_mate_ref[2 * rows :, cols] = split_rows(total_ref[...])
 
 
-def finish_lyric(gains, raw, held, one, two, sums, to_mate):
+def finish_lyric(gains, raw, held, one, two, sums, frames):
     rows, size = raw.shape
     head_size = gains.shape[1]
     step = size // 2
     tail = rows // 2 + GAIN_ROWS
-    last = to_mate.shape[0] // tail - 1
     spec = pl.BlockSpec((rows, step), lambda i: (0, i))
     whole = pl.BlockSpec((8, head_size), lambda i: (0, 0))
     return pl.pallas_call(
@@ -543,28 +566,26 @@
         grid=(2,),
         in_specs=[pl.BlockSpec(gains.shape, lambda i: (0, 0)), spec, spec, spec]
         + [pl.BlockSpec((two.shape[0], step), lambda i: (0, i))]
-        + [whole] * len(sums)
-        + [pl.BlockSpec(memory_space=pl.ANY)],
+        + [whole] * len(sums),
         out_specs=[
             pl.BlockSpec((rows // 2, step), lambda i: (0, i)),
-            pl.BlockSpec((tail, step), lambda i: (last, i)),
+            pl.BlockSpec((tail, step), lambda i: (4 * frames // tail, i)),
             whole,
         ],
         out_shape=[
             jax.ShapeDtypeStruct((rows // 2, size), jnp.bfloat16),
-            jax.ShapeDtypeStruct(to_mate.shape, jnp.bfloat16),
+            jax.ShapeDtypeStruct((4 * frames + tail, size), jnp.bfloat16),
             jax.ShapeDtypeStruct((8, head_size), jnp.float32),
         ],
-        input_output_aliases={5 + len(sums): 1},
         compiler_params=params(),
         cost_estimate=SMALL,
         name="finish_lyric",
-    )(gains, raw, held, one, two, *sums, to_mate)
+    )(gains, raw, held, one, two, *sums)
 
 
 def join_kernel(count, chunks, state_ref, gain_ref, *refs):
-    owns, mates, outs = refs[:chunks], refs[chunks : 2 * chunks], refs[-count - 3 :]
-    grad_key_ref, grad_value_ref, total_ref = outs[count:]
+    owns, mates, outs = refs[:chunks], refs[chunks : 2 * chunks], refs[-count - 4 :]
+    grad_key_ref, grad_value_ref, q_total_ref, k_total_ref = outs[count:]
     rows, size = grad_key_ref.shape[0], owns[0].shape[1]
     frames = outs[0].shape[0]
     for index, ref in enumerate(outs[:count]):
@@ -578,7 +599,9 @@
             grad_key_ref[:, cols] = ref[first : first + rows, :]
             grad_value_ref[:, cols] = ref[first + rows : first + 2 * rows, :]
     sums = mates[-1][mates[-1].shape[0] - GAIN_ROWS :, 0 : gain_ref.shape[1]]
-    total_ref[...] = gain_ref[...] + joined_rows(sums)
+    total = gain_ref[...] + joined_rows(sums)
+    q_total_ref[...] = total[0:1]
+    k_total_ref[...] = total[1:2]
 
 
 def join(state, gain, arrays, own, mate):
@@ -598,11 +621,11 @@
             + [pl.BlockSpec(memory_space=pl.ANY)] * count,
             out_specs=[other] * count
             + [pl.BlockSpec((rows // 2, width), whole)] * 2
-            + [pl.BlockSpec(gain.shape, whole)],
+            + [pl.BlockSpec((1, gain.shape[1]), whole)] * 2,
         ),
         out_shape=[jax.ShapeDtypeStruct(array.shape, array.dtype) for array in arrays]
         + [jax.ShapeDtypeStruct((rows // 2, width), jnp.bfloat16)] * 2
-        + [jax.ShapeDtypeStruct(gain.shape, jnp.float32)],
+        + [jax.ShapeDtypeStruct((1, gain.shape[1]), jnp.float32)] * 2,
         input_output_aliases={2 + 2 * chunks + i: i for i in range(count)},
         compiler_params=params(),
         cost_estimate=SMALL,
@@ -695,30 +718,25 @@
         ]
     )
 
-    rows = 4 * lyric_local
     to_mate = pack(
         state,
         alignment[0, 0],
-        ([lyric_keys[0], lyric_values[0]] if hops else [])
-        + [queries[0], cotangent[0], keys[0], values[0]],
+        [queries[0], cotangent[0], keys[0], values[0]]
+        + ([lyric_keys[0], lyric_values[0]] if hops else []),
     )
     mate = lax.ppermute(to_mate, "seq", swap)
     attended = []
     carried = []
-    after = []
     for chunk in range(CHUNKS):
-        *pair, to_one, to_mid = merge(
-            state, chunk, keys[0], values[0], lyric_keys[0], lyric_values[0], mate, hops, after
-        )
         if hops:
-            two = hop(pair[0], across)
-        one = hop(to_one, partners)
-        mid = hop(to_mid, between)
-        if hops:
-            lyrics = [pair[0], two, hop(two, partners)]
-            after = [two]
+            pair = pair_lyrics(state, chunk, lyric_keys[0], lyric_values[0], mate)
+            two = hop(pair, across)
+            lyrics = [pair, two, hop(two, partners)]
+            lead, after = [pair], [two]
         else:
-            lyrics = [gathered]
+            lyrics, lead, after = [gathered], [], []
+        one = hop(edge(state, chunk, 1, keys[0], values[0], mate, lead, []), partners)
+        mid = hop(edge(state, chunk, 0, keys[0], values[0], mate, [], after), between)
         results = attention(
             chunk, meta, gains, queries[0], cotangent[0], keys[0], values[0], mate, one, mid,
             lyrics, groups, carried,
@@ -733,31 +751,36 @@
         gain_total = sum_over(sum_over(gain_total, "song", bits_of(songs)), "seq", [2])
     for chunk, (results, lyrics) in enumerate(attended):
         for_mate, key_grad, value_grad, to_one, to_mid, _, *parts = results
-        one = hop(to_one, partners)
+        to_mate = []
         mid = hop(to_mid, between)
-        *grads, for_mate = finish_audio(
-            state, chunk, gains, keys[0], mate, key_grad, value_grad, one, mid, for_mate, grads
-        )
         if hops:
             held, for_two, to_two = parts
             sums = [gain_total] if chunk == CHUNKS - 1 else []
-            two = hop(relay(for_two, hop(to_two, partners), sums), across)
-            own_half, for_mate, total = finish_lyric(
-                gains, lyrics[0], held, one, two, sums, for_mate
+            to_two, to_one = relay(for_two, hop(to_two, partners), sums, to_one)
+            two, one = hop(to_two, across), hop(to_one, partners)
+            own_half, to_mate, total = finish_lyric(
+                gains, lyrics[0], held, one, two, sums, frames
             )
             own_halves.append(own_half)
+            to_mate = [to_mate]
         else:
+            one = hop(to_one, partners)
             lyric_cols.append(parts[0])
+        *grads, for_mate = finish_audio(
+            state, chunk, gains, keys[0], mate, key_grad, value_grad, one, mid, for_mate, grads,
+            to_mate,
+        )
         from_mates.append(lax.ppermute(for_mate, "seq", swap))
     filled = [output, grad_queries, *grads]
     for chunk, from_mate in enumerate(from_mates[: CHUNKS - hops]):
         filled = fill_other(state, chunk, filled, from_mate)
     if hops:
-        *filled, grad_lyric_keys, grad_lyric_values, gain_total = join(
+        *filled, grad_lyric_keys, grad_lyric_values, q_total, k_total = join(
             state, total, filled, own_halves, from_mates
         )
     else:
         gain_total = lax.psum(gain_total, ("song", "seq"))
+        q_total, k_total = gain_total[0:1], gain_total[1:2]
         spread = lax.dynamic_update_slice(
             jnp.zeros((2 * total_rows, width), jnp.float32),
             jnp.concatenate(lyric_cols, axis=1).astype(jnp.float32),
@@ -777,8 +800,8 @@
         grad_values[None],
         grad_lyric_keys[None],
         grad_lyric_values[None],
-        gain_total[0],
-        gain_total[1],
+        q_total[0],
+        k_total[0],
     )
 
 

time: 130 us -> 123 us (0.946)
  local copies, waits for them, and re-layouts: 10.9 us -> 4.08 us
  Pallas kernels: 22.4 us -> 26.8 us
  starting transfers between devices: 21.8 us -> 19.3 us
  waiting for transfers between devices: 72.8 us -> 70.5 us
    ppermute x3, waiting for transfers between devices: 20.2 us -> 5.75 us  [sum_over(): lax.ppermute(total, axis, [(i, i ^ bit) for i in range(count)])]
    ppermute x8, waiting for transfers between devices: 47 us -> 58.8 us  [hop(): return lax.ppermute(block, 'seq', pairs)]
    unnamed x34 -> x20, local copies, waits for them, and re-layouts: 8.46 us -> 2.11 us
    pallas_call x1, Pallas kernels: 1.25 us -> 4.28 us  [pack(): pl.pallas_call(pack_kernel, grid_spec=pltpu.PrefetchScalarGridSpec(num_sc...]
    ppermute x3, starting transfers between devices: 6.53 us -> 5.13 us  [sum_over(): lax.ppermute(total, axis, [(i, i ^ bit) for i in range(count)])]
    pallas_call x1 -> x3, Pallas kernels: 1.95 us -> 3.28 us  [the longest x2 2.54 us: edge(): pl.pallas_call(functools.partial(edge_kernel, touching), grid_spec=pltpu....]
  transfers between devices with their start and end apart: 13 -> 13, of which waited for: 8 -> 8; matrix products, arithmetic and copies ran while one was open for 2% -> 2% of each run, Pallas kernels for 2% -> 3%
where the time goes in v5:
time: 123 us
  waiting for transfers between devices  70.5 us (57%)
  Pallas kernels  26.8 us (22%)
  starting transfers between devices  19.3 us (16%)
  local copies, waits for them, and re-layouts  4.08 us (3%)
  between operations  1.43 us (1%)
    ppermute x8, waiting for transfers between devices, hop(): return lax.ppermute(block, 'seq', pairs)  58.8 us
    pallas_call x1, Pallas kernels, attention(): pl.pallas_call(functools.partial(attention_kernel, groups, bool(carried),...  14.1 us
    ppermute x8, starting transfers between devices, hop(): return lax.ppermute(block, 'seq', pairs)  13.7 us
    ppermute x3, waiting for transfers between devices, sum_over(): lax.ppermute(total, axis, [(i, i ^ bit) for i in range(count)])  5.75 us
    ppermute x3, starting transfers between devices, sum_over(): lax.ppermute(total, axis, [(i, i ^ bit) for i in range(count)])  5.13 us
    pallas_call x1, Pallas kernels, pack(): pl.pallas_call(pack_kernel, grid_spec=pltpu.PrefetchScalarGridSpec(num_sc...  4.28 us
    ppermute x1, waiting for transfers between devices, body(): from_mates.append(lax.ppermute(for_mate, 'seq', swap))  3.03 us
    ppermute x1, waiting for transfers between devices, body(): mate = lax.ppermute(to_mate, 'seq', swap)  2.87 us
  transfers between devices with their start and end apart: 13, of which 8 were waited for; matrix products, arithmetic and copies ran while one was open for 2% of the time, Pallas kernels for 3%

profile of v5, /device:TPU:0, one launch (start us, length us, event | category | flops | bytes accessed | tf_op | source)
XLA Modules:
  0.0 122.7 jit_solution(10191384205283626)
XLA Ops:
  0.7 0.6 pad_add_fusion.state_ref
  1.3 0.0 copy-start.2
  1.3 0.0 copy-start.3
  1.3 0.0 copy-start.6
  1.3 4.3 %pack.1 = bf16[640,1024]{1,0:T(8,128)(2,1)} custom-call(s32[2]{0:T(128)} %pad_add_fusion.state_ref, s32[2]{0:T(128)} %bitcast.52, bf16[128,2048]{1,0:T(8,128)(2,1)} %bitcast.44, bf16[128,2048]{1,0:T(8,128)(2,1)} %bitcast.46, bf16[128,2048]{1,0:T(8,128)(2,1)} %bitcast.31, bf16[128,2048]{1,0:T(8,128)(2,1)} %bitcast.36, bf16[48,2048]{1,0:T(8,128)(2,1)} %bitcast.40, ...), custom_call_target="tpu_custom_call" | custom-call | flops 1 | bytes 1 | tf_op jit(solution)/shard_map/pack/pallas_call | solution.py:64
  5.5 0.0 copy-start
  5.5 0.0 copy-start.1
  5.6 0.5 collective-permute-start
  6.1 2.9 %collective-permute-done.mate_ref.mate_key_ref.mate_value_ref = bf16[640,1024]{1,0:T(8,128)(2,1)S(1)} collective-permute-done((bf16[640,1024]{1,0:T(8,128)(2,1)}, bf16[640,1024]{1,0:T(8,128)(2,1)S(1)}, u32[]{:S(2)}, u32[]{:S(2)}) %collective-permute-start) | collective-permute-done | bytes 1310752 | tf_op jit(solution)/shard_map/ppermute | solution.py:727
  8.9 0.0 copy-done.2
  8.9 0.0 copy-done.3
  8.9 0.0 copy-done.6
  9.0 0.7 pair_lyrics.1.refs_0_.raw_ref
  9.7 4.0 %collective-permute-start.2 = (bf16[192,1024]{1,0:T(8,128)(2,1)S(1)}, bf16[192,1024]{1,0:T(8,128)(2,1)}, u32[]{:S(2)}, u32[]{:S(2)}) collective-permute-start(bf16[192,1024]{1,0:T(8,128)(2,1)S(1)} %pair_lyrics.1.refs_0_.raw_ref), channel_id=1, source_target_pairs={{0,4},{1,5},{2,6},{3,7},{4,0},{5,1},{6,2},{7,3},{8,12},{9,13},{10,... | collective-permute-start | bytes 1179656 | tf_op jit(solution)/shard_map/ppermute | solution.py:684
  13.7 0.0 copy-done
  13.7 0.0 copy-done.1
  13.7 1.7 %edge.2 = bf16[448,1024]{1,0:T(8,128)(2,1)} custom-call(s32[2]{0:T(128)S(1)} %copy-done.6, bf16[128,2048]{1,0:T(8,128)(2,1)S(1)} %bitcast.32, bf16[128,2048]{1,0:T(8,128)(2,1)S(1)} %bitcast.37, bf16[640,1024]{1,0:T(8,128)(2,1)S(1)} %collective-permute-done.mate_ref.mate_key_ref.mate_value_ref, ...), custom_call_target="tpu_custom_call" | custom-call | flops 1 | bytes 1 | tf_op jit(solution)/shard_map/edge/pallas_call | solution.py:129
  15.5 0.0 copy-start.7
  15.5 0.0 copy-start.8
  15.5 0.0 copy-start.9
  15.5 1.6 %collective-permute-start.1 = (bf16[448,1024]{1,0:T(8,128)(2,1)}, bf16[448,1024]{1,0:T(8,128)(2,1)}, u32[]{:S(2)}, u32[]{:S(2)}) collective-permute-start(bf16[448,1024]{1,0:T(8,128)(2,1)} %edge.2), channel_id=1, source_target_pairs={{0,2},{1,3},{2,0},{3,1},{4,6},{5,7},{6,4},{7,5},{8,10},{9,11},{10,... | collective-permute-start | bytes 2752520 | tf_op jit(solution)/shard_map/ppermute | solution.py:684
  17.0 14.7 %collective-permute-done.2.refs_0_.refs_1_ = bf16[192,1024]{1,0:T(8,128)(2,1)} collective-permute-done((bf16[192,1024]{1,0:T(8,128)(2,1)S(1)}, bf16[192,1024]{1,0:T(8,128)(2,1)}, u32[]{:S(2)}, u32[]{:S(2)}) %collective-permute-start.2) | collective-permute-done | bytes 393248 | tf_op jit(solution)/shard_map/ppermute | solution.py:684
  31.8 0.8 edge.3
  32.6 1.5 %collective-permute-start.3 = (bf16[256,1024]{1,0:T(8,128)(2,1)S(1)}, bf16[256,1024]{1,0:T(8,128)(2,1)}, u32[]{:S(2)}, u32[]{:S(2)}) collective-permute-start(bf16[256,1024]{1,0:T(8,128)(2,1)S(1)} %edge.3), channel_id=1, source_target_pairs={{2,4},{3,5},{4,2},{5,3},{10,12},{11,13},{12,10},{13,11},{18,20},{1... | collective-permute-start | bytes 1572872 | tf_op jit(solution)/shard_map/ppermute | solution.py:684
  34.1 1.1 collective-permute-start.4
  35.8 0.0 copy-done.7
  35.8 0.6 fusion
  36.4 1.4 %stack.77.meta_ref = s32[15]{0:T(128)S(1)} concatenate(s32[1]{0:T(128)} %bitcast, s32[1]{0:T(128)} %bitcast.1, s32[1]{0:T(128)} %bitcast.11, s32[1]{0:T(128)} %bitcast.12, s32[1]{0:T(128)S(6)} %copy.30, s32[1]{0:T(128)} %bitcast.13, s32[1]{0:T(128)} %bitcast.14, s32[1]{0:T(128)} %bitcast.15, s32[1]{0:T(128)} %bitcast.16, s32[1]{0:T(128)} %bitcast.17, s32[1]{0:T(128)} %bitcast.18, ...), dimensions={0} | concatenate | bytes 120 | tf_op jit(solution)/shard_map/stack | solution.py:711
  37.8 0.0 copy-done.8
  37.8 0.0 copy-done.9
  37.8 15.8 %collective-permute-done.4.refs_2_ = bf16[192,1024]{1,0:T(8,128)(2,1)} collective-permute-done((bf16[192,1024]{1,0:T(8,128)(2,1)}, bf16[192,1024]{1,0:T(8,128)(2,1)}, u32[]{:S(2)}, u32[]{:S(2)}) %collective-permute-start.4) | collective-permute-done | bytes 393248 | tf_op jit(solution)/shard_map/ppermute | solution.py:684
  53.6 0.0 collective-permute-done.3.mid_ref
  53.6 0.0 collective-permute-done.1.one_ref
  53.6 0.0 copy-start.4
  53.6 1.0 copy-done.4
  54.6 0.0 copy-start.5
  54.6 1.0 copy-done.5
  55.7 14.1 %attention.1 = (bf16[128,2048]{1,0:T(8,128)(2,1)}, bf16[128,2048]{1,0:T(8,128)(2,1)}, bf16[256,1024]{1,0:T(8,128)(2,1)S(1)}, f32[256,1024]{1,0:T(8,128)S(1)}, f3...) custom-call(s32[15]{0:T(128)S(1)} %stack.77.meta_ref, ...), custom_call_target="tpu_custom_call" | custom-call | flops 2415919104 | bytes 16777216 | tf_op jit(solution)/shard_map/attention/pallas_call | solution.py:351
  69.7 0.0 collective-permute-start.5
  69.7 1.6 %collective-permute-start.6 = (f32[8,128]{1,0:T(8,128)S(1)}, f32[8,128]{1,0:T(8,128)S(1)}, u32[]{:S(2)}, u32[]{:S(2)}) collective-permute-start(f32[8,128]{1,0:T(8,128)S(1)} %get-tuple-element.38), channel_id=1, source_target_pairs={{0,8},{8,0},{16,24},{24,16},{1,9},{9,1},{17,25},{25,17},{2,10},{10... | collective-permute-start | bytes 12296 | tf_op jit(solution)/shard_map/ppermute | solution.py:653
  71.3 2.1 %collective-permute-done.6 = f32[8,128]{1,0:T(8,128)S(1)} collective-permute-done((f32[8,128]{1,0:T(8,128)S(1)}, f32[8,128]{1,0:T(8,128)S(1)}, u32[]{:S(2)}, u32[]{:S(2)}) %collective-permute-start.6) | collective-permute-done | bytes 4128 | tf_op jit(solution)/shard_map/ppermute | solution.py:653
  73.4 1.6 %collective-permute-start.7 = (f32[8,128]{1,0:T(8,128)S(1)}, f32[8,128]{1,0:T(8,128)S(1)}, u32[]{:S(2)}, u32[]{:S(2)}) collective-permute-start(f32[8,128]{1,0:T(8,128)S(1)} %add.51), channel_id=1, source_target_pairs={{0,16},{8,24},{16,0},{24,8},{1,17},{9,25},{17,1},{25,9},{2,18},{10... | collective-permute-start | bytes 12296 | tf_op jit(solution)/shard_map/ppermute | solution.py:653
  75.0 2.0 %collective-permute-done.7 = f32[8,128]{1,0:T(8,128)S(1)} collective-permute-done((f32[8,128]{1,0:T(8,128)S(1)}, f32[8,128]{1,0:T(8,128)S(1)}, u32[]{:S(2)}, u32[]{:S(2)}) %collective-permute-start.7) | collective-permute-done | bytes 4128 | tf_op jit(solution)/shard_map/ppermute | solution.py:653
  77.0 2.0 %collective-permute-start.8 = (f32[8,128]{1,0:T(8,128)S(1)}, f32[8,128]{1,0:T(8,128)S(1)}, u32[]{:S(2)}, u32[]{:S(2)}) collective-permute-start(f32[8,128]{1,0:T(8,128)S(1)} %add.52), channel_id=1, source_target_pairs={{0,2},{1,3},{2,0},{3,1},{4,6},{5,7},{6,4},{7,5},{8,10},{9,11},{10,... | collective-permute-start | bytes 12296 | tf_op jit(solution)/shard_map/ppermute | solution.py:653
  79.0 1.6 %collective-permute-done.8 = f32[8,128]{1,0:T(8,128)S(1)} collective-permute-done((f32[8,128]{1,0:T(8,128)S(1)}, f32[8,128]{1,0:T(8,128)S(1)}, u32[]{:S(2)}, u32[]{:S(2)}) %collective-permute-start.8) | collective-permute-done | bytes 4128 | tf_op jit(solution)/shard_map/ppermute | solution.py:653
  80.6 0.0 collective-permute-done.5.arrived_ref
  80.6 0.2 relay.1
  80.9 2.1 %collective-permute-start.9 = (bf16[448,1024]{1,0:T(8,128)(2,1)S(1)}, bf16[448,1024]{1,0:T(8,128)(2,1)S(1)}, u32[]{:S(2)}, u32[]{:S(2)}) collective-permute-start(bf16[448,1024]{1,0:T(8,128)(2,1)S(1)} %get-tuple-element.40), channel_id=1, source_target_pairs={{0,2},{1,3},{2,0},{3,1},{4,6},{5,7},{6,4},{7,5},{8,10},{9,11},{10,... | collective-permute-start | bytes 2752520 | tf_op jit(solution)/shard_map/ppermute | solution.py:684
  82.9 0.7 collective-permute-start.11
  83.6 2.8 %collective-permute-start.10 = (bf16[224,1024]{1,0:T(8,128)(2,1)S(1)}, bf16[224,1024]{1,0:T(8,128)(2,1)S(1)}, u32[]{:S(2)}, u32[]{:S(2)}) collective-permute-start(bf16[224,1024]{1,0:T(8,128)(2,1)S(1)} %get-tuple-element.41), channel_id=1, source_target_pairs={{0,4},{1,5},{2,6},{3,7},{4,0},{5,1},{6,2},{7,3},{8,12},{9,13},{10,... | collective-permute-start | bytes 1376264 | tf_op jit(solution)/shard_map/ppermute | solution.py:684
  86.4 28.3 %collective-permute-done.10.two_ref = bf16[224,1024]{1,0:T(8,128)(2,1)S(1)} collective-permute-done((bf16[224,1024]{1,0:T(8,128)(2,1)S(1)}, bf16[224,1024]{1,0:T(8,128)(2,1)S(1)}, u32[]{:S(2)}, u32[]{:S(2)}) %collective-permute-start.10) | collective-permute-done | bytes 458784 | tf_op jit(solution)/shard_map/ppermute | solution.py:684
  114.7 0.0 collective-permute-done.9.one_ref
  114.7 0.6 finish_lyric.1
  115.3 0.0 collective-permute-done.11.mid_ref
  115.4 2.6 %finish_audio.1 = (bf16[128,2048]{1,0:T(8,128)(2,1)}, bf16[128,2048]{1,0:T(8,128)(2,1)}, bf16[640,1024]{1,0:T(8,128)(2,1)S(1)}) custom-call(s32[2]{0:T(128)S(1)} %copy-done.6, f32[2,128]{1,0:T(2,128)S(1)} %pad_maximum_fusion.gain_ref, bf16[128,2048]{1,0:T(8,128)(2,1)S(1)} %bitcast.35, ...), custom_call_target="tpu_custom_call", output_to_operand_aliasing={{2}: (9, {})} | custom-call | flops 1 | bytes 1 | tf_op jit(solution)/shard_map/finish_audio/pallas_call | solution.py:477
  117.9 0.0 collective-permute-start.12
  117.9 3.0 %collective-permute-done.12.refs_1_ = bf16[640,1024]{1,0:T(8,128)(2,1)S(1)} collective-permute-done((bf16[640,1024]{1,0:T(8,128)(2,1)S(1)}, bf16[640,1024]{1,0:T(8,128)(2,1)S(1)}, u32[]{:S(2)}, u32[]{:S(2)}) %collective-permute-start.12) | collective-permute-done | bytes 1310752 | tf_op jit(solution)/shard_map/ppermute | solution.py:773
  121.0 1.7 %join.1 = (bf16[128,2048]{1,0:T(8,128)(2,1)}, bf16[128,2048]{1,0:T(8,128)(2,1)}, bf16[128,2048]{1,0:T(8,128)(2,1)}, bf16[128,2048]{1,0:T(8,128)(2,1)}, bf16[48,2...) custom-call(s32[2]{0:T(128)S(1)} %copy-done.6, ...), custom_call_target="tpu_custom_call", output_to_operand_aliasing={{0}: (4, {}), {1}: (5, {}), {2}: (6, {}), {3}: (7, {})} | custom-call | flops 1 | bytes 1 | tf_op jit(solution)/shard_map/join/pallas_call | solution.py:615
  (4 shorter events, 0.0 us)
Async XLA Ops:
  1.3 7.7 %copy-start.2 = (bf16[1,48,2048]{2,1,0:T(8,128)(2,1)S(1)}, bf16[1,48,2048]{2,1,0:T(8,128)(2,1)}, u32[]{:S(2)}) copy-start(bf16[1,48,2048]{2,1,0:T(8,128)(2,1)} %param.13) | copy-start | bytes 589828
  1.3 7.7 %copy-start.3 = (bf16[1,48,2048]{2,1,0:T(8,128)(2,1)S(1)}, bf16[1,48,2048]{2,1,0:T(8,128)(2,1)}, u32[]{:S(2)}) copy-start(bf16[1,48,2048]{2,1,0:T(8,128)(2,1)} %param.14) | copy-start | bytes 589828
  1.3 7.7 %copy-start.6 = (s32[2]{0:T(128)S(1)}, s32[2]{0:T(128)}, u32[]{:S(2)}) copy-start(s32[2]{0:T(128)} %pad_add_fusion.state_ref) | copy-start | bytes 28
  5.5 8.2 %copy-start = (bf16[1,128,2048]{2,1,0:T(8,128)(2,1)S(1)}, bf16[1,128,2048]{2,1,0:T(8,128)(2,1)}, u32[]{:S(2)}) copy-start(bf16[1,128,2048]{2,1,0:T(8,128)(2,1)} %param.11) | copy-start | bytes 1572868
  5.5 8.2 %copy-start.1 = (bf16[1,128,2048]{2,1,0:T(8,128)(2,1)S(1)}, bf16[1,128,2048]{2,1,0:T(8,128)(2,1)}, u32[]{:S(2)}) copy-start(bf16[1,128,2048]{2,1,0:T(8,128)(2,1)} %param.12) | copy-start | bytes 1572868
  5.6 3.4 %collective-permute-start = (bf16[640,1024]{1,0:T(8,128)(2,1)}, bf16[640,1024]{1,0:T(8,128)(2,1)S(1)}, u32[]{:S(2)}, u32[]{:S(2)}) collective-permute-start(bf16[640,1024]{1,0:T(8,128)(2,1)} %pack.1), channel_id=1, source_target_pairs={{0,1},{1,0},{2,3},{3,2},{4,5},{5,4},{6,7},{7,6},{8,9},{9,8},{10,11... | collective-permute-start | bytes 3932168 | tf_op jit(solution)/shard_map/ppermute | solution.py:727
  9.7 22.1 %collective-permute-start.2 = (bf16[192,1024]{1,0:T(8,128)(2,1)S(1)}, bf16[192,1024]{1,0:T(8,128)(2,1)}, u32[]{:S(2)}, u32[]{:S(2)}) collective-permute-start(bf16[192,1024]{1,0:T(8,128)(2,1)S(1)} %pair_lyrics.1.refs_0_.raw_ref), channel_id=1, source_target_pairs={{0,4},{1,5},{2,6},{3,7},{4,0},{5,1},{6,2},{7,3},{8,12},{9,13},{10,... | collective-permute-start | bytes 1179656 | tf_op jit(solution)/shard_map/ppermute | solution.py:684
  15.5 20.3 %copy-start.7 = (s32[1,1,2]{2,1,0:T(1,128)S(1)}, s32[1,1,2]{2,1,0:T(1,128)}, u32[]{:S(2)}) copy-start(s32[1,1,2]{2,1,0:T(1,128)} %param.18) | copy-start | bytes 28
  15.5 22.3 %copy-start.8 = (f32[128]{0:T(128)S(1)}, f32[128]{0:T(128)}, u32[]{:S(2)}) copy-start(f32[128]{0:T(128)} %param.16) | copy-start | bytes 1540
  15.5 22.3 %copy-start.9 = (f32[128]{0:T(128)S(1)}, f32[128]{0:T(128)}, u32[]{:S(2)}) copy-start(f32[128]{0:T(128)} %param.15) | copy-start | bytes 1540
  15.5 38.1 %collective-permute-start.1 = (bf16[448,1024]{1,0:T(8,128)(2,1)}, bf16[448,1024]{1,0:T(8,128)(2,1)}, u32[]{:S(2)}, u32[]{:S(2)}) collective-permute-start(bf16[448,1024]{1,0:T(8,128)(2,1)} %edge.2), channel_id=1, source_target_pairs={{0,2},{1,3},{2,0},{3,1},{4,6},{5,7},{6,4},{7,5},{8,10},{9,11},{10,... | collective-permute-start | bytes 2752520 | tf_op jit(solution)/shard_map/ppermute | solution.py:684
  32.6 21.0 %collective-permute-start.3 = (bf16[256,1024]{1,0:T(8,128)(2,1)S(1)}, bf16[256,1024]{1,0:T(8,128)(2,1)}, u32[]{:S(2)}, u32[]{:S(2)}) collective-permute-start(bf16[256,1024]{1,0:T(8,128)(2,1)S(1)} %edge.3), channel_id=1, source_target_pairs={{2,4},{3,5},{4,2},{5,3},{10,12},{11,13},{12,10},{13,11},{18,20},{1... | collective-permute-start | bytes 1572872 | tf_op jit(solution)/shard_map/ppermute | solution.py:684
  34.1 19.5 %collective-permute-start.4 = (bf16[192,1024]{1,0:T(8,128)(2,1)}, bf16[192,1024]{1,0:T(8,128)(2,1)}, u32[]{:S(2)}, u32[]{:S(2)}) collective-permute-start(bf16[192,1024]{1,0:T(8,128)(2,1)} %collective-permute-done.2.refs_0_.refs_1_), channel_id=1, source_target_pairs={{0,2},{1,3},{2,0},{3,1},{4,6},{5,7},{6,4},{7,5},{8,10},{9,11},{10,... | collective-permute-start | bytes 1179656 | tf_op jit(solution)/shard_map/ppermute | solution.py:684
  53.6 1.0 copy-start.4
  54.6 1.0 copy-start.5
  69.7 10.9 %collective-permute-start.5 = (bf16[192,1024]{1,0:T(8,128)(2,1)S(1)}, bf16[192,1024]{1,0:T(8,128)(2,1)S(1)}, u32[]{:S(2)}, u32[]{:S(2)}) collective-permute-start(bf16[192,1024]{1,0:T(8,128)(2,1)S(1)} %get-tuple-element.37), channel_id=1, source_target_pairs={{0,2},{1,3},{2,0},{3,1},{4,6},{5,7},{6,4},{7,5},{8,10},{9,11},{10,... | collective-permute-start | bytes 1179656 | tf_op jit(solution)/shard_map/ppermute | solution.py:684
  69.7 3.7 %collective-permute-start.6 = (f32[8,128]{1,0:T(8,128)S(1)}, f32[8,128]{1,0:T(8,128)S(1)}, u32[]{:S(2)}, u32[]{:S(2)}) collective-permute-start(f32[8,128]{1,0:T(8,128)S(1)} %get-tuple-element.38), channel_id=1, source_target_pairs={{0,8},{8,0},{16,24},{24,16},{1,9},{9,1},{17,25},{25,17},{2,10},{10... | collective-permute-start | bytes 12296 | tf_op jit(solution)/shard_map/ppermute | solution.py:653
  73.4 3.6 %collective-permute-start.7 = (f32[8,128]{1,0:T(8,128)S(1)}, f32[8,128]{1,0:T(8,128)S(1)}, u32[]{:S(2)}, u32[]{:S(2)}) collective-permute-start(f32[8,128]{1,0:T(8,128)S(1)} %add.51), channel_id=1, source_target_pairs={{0,16},{8,24},{16,0},{24,8},{1,17},{9,25},{17,1},{25,9},{2,18},{10... | collective-permute-start | bytes 12296 | tf_op jit(solution)/shard_map/ppermute | solution.py:653
  77.0 3.6 %collective-permute-start.8 = (f32[8,128]{1,0:T(8,128)S(1)}, f32[8,128]{1,0:T(8,128)S(1)}, u32[]{:S(2)}, u32[]{:S(2)}) collective-permute-start(f32[8,128]{1,0:T(8,128)S(1)} %add.52), channel_id=1, source_target_pairs={{0,2},{1,3},{2,0},{3,1},{4,6},{5,7},{6,4},{7,5},{8,10},{9,11},{10,... | collective-permute-start | bytes 12296 | tf_op jit(solution)/shard_map/ppermute | solution.py:653
  80.9 33.9 %collective-permute-start.9 = (bf16[448,1024]{1,0:T(8,128)(2,1)S(1)}, bf16[448,1024]{1,0:T(8,128)(2,1)S(1)}, u32[]{:S(2)}, u32[]{:S(2)}) collective-permute-start(bf16[448,1024]{1,0:T(8,128)(2,1)S(1)} %get-tuple-element.40), channel_id=1, source_target_pairs={{0,2},{1,3},{2,0},{3,1},{4,6},{5,7},{6,4},{7,5},{8,10},{9,11},{10,... | collective-permute-start | bytes 2752520 | tf_op jit(solution)/shard_map/ppermute | solution.py:684
  82.9 32.4 %collective-permute-start.11 = (bf16[256,1024]{1,0:T(8,128)(2,1)S(1)}, bf16[256,1024]{1,0:T(8,128)(2,1)S(1)}, u32[]{:S(2)}, u32[]{:S(2)}) collective-permute-start(bf16[256,1024]{1,0:T(8,128)(2,1)S(1)} %get-tuple-element.46), channel_id=1, source_target_pairs={{2,4},{3,5},{4,2},{5,3},{10,12},{11,13},{12,10},{13,11},{18,20},{1... | collective-permute-start | bytes 1572872 | tf_op jit(solution)/shard_map/ppermute | solution.py:684
  83.6 31.1 %collective-permute-start.10 = (bf16[224,1024]{1,0:T(8,128)(2,1)S(1)}, bf16[224,1024]{1,0:T(8,128)(2,1)S(1)}, u32[]{:S(2)}, u32[]{:S(2)}) collective-permute-start(bf16[224,1024]{1,0:T(8,128)(2,1)S(1)} %get-tuple-element.41), channel_id=1, source_target_pairs={{0,4},{1,5},{2,6},{3,7},{4,0},{5,1},{6,2},{7,3},{8,12},{9,13},{10,... | collective-permute-start | bytes 1376264 | tf_op jit(solution)/shard_map/ppermute | solution.py:684
  117.9 3.0 %collective-permute-start.12 = (bf16[640,1024]{1,0:T(8,128)(2,1)S(1)}, bf16[640,1024]{1,0:T(8,128)(2,1)S(1)}, u32[]{:S(2)}, u32[]{:S(2)}) collective-permute-start(bf16[640,1024]{1,0:T(8,128)(2,1)S(1)} %get-tuple-element.49), channel_id=1, source_target_pairs={{0,1},{1,0},{2,3},{3,2},{4,5},{5,4},{6,7},{7,6},{8,9},{9,8},{10,11... | collective-permute-start | bytes 3932168 | tf_op jit(solution)/shard_map/ppermute | solution.py:773

commit v6 on v5

--- a/solution.py
+++ b/solution.py
@@ -44,35 +44,50 @@
 
 
 def pack_kernel(state_ref, align_ref, *refs):
-    out_ref = refs[-1]
+    ins, (out_ref, tile_ref, sems) = refs[:-3], refs[-3:]
+    half = out_ref.shape[1]
+    cols = pl.ds(pl.multiple_of((1 - state_ref[0]) * half, half), half)
     start = 0
-    for ref in refs[:-1]:
-        out_ref[start : start + ref.shape[0], :] = ref[...]
-        start += ref.shape[0]
-    row = lax.broadcasted_iota(jnp.int32, (ALIGN_ROWS, out_ref.shape[1]), 0)
-    tiles = jnp.zeros((ALIGN_ROWS, out_ref.shape[1]), jnp.int32)
+    copies = []
+    for index, ref in enumerate(ins):
+        rows = ref.shape[0]
+        copies.append(
+            pltpu.make_async_copy(
+                ref.at[:, cols], out_ref.at[start : start + rows, :], sems.at[index]
+            )
+        )
+        copies[-1].start()
+        start += rows
+    row = lax.broadcasted_iota(jnp.int32, tile_ref.shape, 0)
+    tiles = jnp.zeros(tile_ref.shape, jnp.int32)
     for slot in range(TILES):
         tiles = jnp.where(row == slot, align_ref[slot], tiles)
-    out_ref[start:, :] = tiles.astype(jnp.float32).astype(jnp.bfloat16)
+    tile_ref[...] = tiles.astype(jnp.float32).astype(jnp.bfloat16)
+    copies.append(
+        pltpu.make_async_copy(
+            tile_ref, out_ref.at[start : start + ALIGN_ROWS, :], sems.at[len(ins)]
+        )
+    )
+    copies[-1].start()
+    for copy in copies:
+        copy.wait()
 
 
 def pack(state, align, arrays):
     width = arrays[0].shape[1]
     half = width // 2
-    step = half // 4
     rows = sum(array.shape[0] for array in arrays) + ALIGN_ROWS
     return pl.pallas_call(
         pack_kernel,
         grid_spec=pltpu.PrefetchScalarGridSpec(
             num_scalar_prefetch=2,
-            grid=(4,),
-            in_specs=[
-                pl.BlockSpec(
-                    (array.shape[0], step), lambda i, state, _: (0, (1 - state[0]) * 4 + i)
-                )
-                for array in arrays
+            grid=(1,),
+            in_specs=[pl.BlockSpec(memory_space=pl.ANY)] * len(arrays),
+            out_specs=pl.BlockSpec(memory_space=pl.ANY),
+            scratch_shapes=[
+                pltpu.VMEM((ALIGN_ROWS, half), jnp.bfloat16),
+                pltpu.SemaphoreType.DMA((len(arrays) + 1,)),
             ],
-            out_specs=pl.BlockSpec((rows, step), lambda i, state, _: (0, i)),
         ),
         out_shape=jax.ShapeDtypeStruct((rows, half), jnp.bfloat16),
         compiler_params=params(PACK_VMEM_LIMIT),
@@ -81,14 +96,15 @@
     )(state, align, *arrays)
 
 
-def pair_kernel(state_ref, lkey_ref, lvalue_ref, mate_ref, pair_ref):
-    lyric = lkey_ref.shape[0]
-    pair_ref[0:lyric, :] = lkey_ref[...]
-    pair_ref[lyric : 2 * lyric, :] = lvalue_ref[...]
-    pair_ref[2 * lyric :, :] = mate_ref[0 : 2 * lyric, :]
-
-
-def pair_lyrics(state, chunk, lyric_key, lyric_value, mate):
+def pair_kernel(state_ref, gain_ref, key_ref, value_ref, mate_ref, pair_ref):
+    rows = key_ref.shape[0]
+    norm_columns(pair_ref, slice(0, rows), key_ref[...], gain_ref)
+    pair_ref[rows : 2 * rows, :] = value_ref[...]
+    norm_columns(pair_ref, slice(2 * rows, 3 * rows), mate_ref[0:rows, :], gain_ref)
+    pair_ref[3 * rows :, :] = mate_ref[rows : 2 * rows, :]
+
+
+def pair_lyrics(state, chunk, gains, lyric_key, lyric_value, mate):
     rows, width = lyric_key.shape
     size = width // 2 // CHUNKS
     step = size // 2
@@ -99,28 +115,36 @@
         grid_spec=pltpu.PrefetchScalarGridSpec(
             num_scalar_prefetch=1,
             grid=(2,),
-            in_specs=[own, own, pl.BlockSpec((BLK, step), lambda i, state: (last, chunk * 2 + i))],
+            in_specs=[
+                pl.BlockSpec(gains.shape, lambda i, state: (0, 0)),
+                own,
+                own,
+                pl.BlockSpec((BLK, step), lambda i, state: (last, chunk * 2 + i)),
+            ],
             out_specs=pl.BlockSpec((4 * rows, step), lambda i, state: (0, i)),
         ),
         out_shape=jax.ShapeDtypeStruct((4 * rows, size), jnp.bfloat16),
         compiler_params=params(),
         cost_estimate=SMALL,
         name="pair_lyrics",
-    )(state, lyric_key, lyric_value, mate)
-
-
-def edge_kernel(touching, state_ref, key_ref, value_ref, mate_key_ref, mate_value_ref, *refs):
+    )(state, gains, lyric_key, lyric_value, mate)
+
+
+def edge_kernel(
+    touching, state_ref, gain_ref, key_ref, value_ref, mate_key_ref, mate_value_ref, *refs
+):
     out_ref = refs[-1]
     frames = key_ref.shape[0]
     first = out_ref.shape[0] - 2 * frames
     if first:
         out_ref[0:first, :] = refs[0][...]
     mine = state_ref[1] == touching
-    out_ref[first : first + frames, :] = jnp.where(mine, key_ref[...], mate_key_ref[...])
+    keys = jnp.where(mine, key_ref[...], mate_key_ref[...])
+    norm_columns(out_ref, slice(first, first + frames), keys, gain_ref)
     out_ref[first + frames :, :] = jnp.where(mine, value_ref[...], mate_value_ref[...])
 
 
-def edge(state, chunk, touching, key, value, mate, lead, after):
+def edge(state, chunk, touching, gains, key, value, mate, lead, after):
     frames, width = key.shape
     size = width // 2 // CHUNKS
     step = size // 2
@@ -131,7 +155,7 @@
         grid_spec=pltpu.PrefetchScalarGridSpec(
             num_scalar_prefetch=1,
             grid=(2,),
-            in_specs=[own, own]
+            in_specs=[pl.BlockSpec(gains.shape, lambda i, state: (0, 0)), own, own]
             + [pl.BlockSpec((frames, step), lambda i, state: (2, chunk * 2 + i))]
             + [pl.BlockSpec((frames, step), lambda i, state: (3, chunk * 2 + i))]
             + [pl.BlockSpec((array.shape[0], step), lambda i, state: (0, i)) for array in lead]
@@ -142,12 +166,43 @@
         compiler_params=params(),
         cost_estimate=SMALL,
         name="edge",
-    )(state, key, value, mate, mate, *lead, *after)
+    )(state, gains, key, value, mate, mate, *lead, *after)
+
+
+def prepare_kernel(state_ref, gain_ref, key_ref, mate_ref, *refs):
+    out_ref = refs[-1]
+    frames = key_ref.shape[0]
+    norm_columns(out_ref, slice(0, frames), key_ref[...], gain_ref)
+    norm_columns(out_ref, slice(frames, 2 * frames), mate_ref[...], gain_ref)
+
+
+def prepare_keys(state, gains, key, mate, after):
+    frames, width = key.shape
+    half = width // 2
+    step = half // 2
+    return pl.pallas_call(
+        prepare_kernel,
+        grid_spec=pltpu.PrefetchScalarGridSpec(
+            num_scalar_prefetch=1,
+            grid=(2,),
+            in_specs=[
+                pl.BlockSpec(gains.shape, lambda i, state: (0, 0)),
+                pl.BlockSpec((frames, step), lambda i, state: (0, state[0] * 2 + i)),
+                pl.BlockSpec((frames, step), lambda i, state: (2, i)),
+            ]
+            + [pl.BlockSpec(memory_space=pl.ANY)] * len(after),
+            out_specs=pl.BlockSpec((2 * frames, step), lambda i, state: (0, i)),
+        ),
+        out_shape=jax.ShapeDtypeStruct((2 * frames, half), jnp.bfloat16),
+        compiler_params=params(),
+        cost_estimate=SMALL,
+        name="prepare_keys",
+    )(state, gains, key, mate, *after)
 
 
 def attention_kernel(
-    groups, chained, head_size, score_scale, meta_ref, gain_ref, query_ref, grad_ref, key_ref,
-    value_ref, mate_ref, one_ref, mid_ref, *refs
+    groups, chained, head_size, score_scale, meta_ref, gain_ref, query_ref, grad_ref, value_ref,
+    key_ref, mate_ref, one_ref, mid_ref, *refs
 ):
     frames = query_ref.shape[0]
     exchanged = len(groups) == 4
@@ -212,12 +267,12 @@
         query = jnp.concatenate([query_ref[:, cols], from_mate(0)], axis=0)
         query = query.astype(jnp.float32)
         cot = jnp.concatenate([grad_ref[:, cols], from_mate(1)], axis=0)
-        raw_keys = jnp.concatenate(
-            [key_ref[:, cols], from_mate(2)]
+        key_low = jnp.concatenate(
+            [key_ref[:, cols]]
             + [lyric[index][run[0] : run[0] + run[2]] for index, run in runs]
             + [near_rows[:frames], far_rows[:frames]],
             axis=0,
-        ).astype(jnp.float32)
+        )
         value = jnp.concatenate(
             [value_ref[:, cols], from_mate(3)]
             + [lyric[index][run[1] : run[1] + run[2]] for index, run in runs]
@@ -225,11 +280,8 @@
             axis=0,
         )
         query_inv = lax.rsqrt(jnp.mean(query * query, axis=1, keepdims=True) + NORM_EPS)
-        key_inv = lax.rsqrt(jnp.mean(raw_keys * raw_keys, axis=1, keepdims=True) + NORM_EPS)
         query_hat = query * query_inv
         query_low = (query_hat * (q_gain * score_scale)).astype(jnp.bfloat16)
-        key_hat = raw_keys * key_inv
-        key_low = (key_hat * k_gain).astype(jnp.bfloat16)
 
         near, far = slice(main, main + frames), slice(main + frames, main + 2 * frames)
 
@@ -278,7 +330,8 @@
         delta = jnp.sum(weighted, axis=0, keepdims=True)
         grad_score = (weighted - prob * delta).astype(jnp.bfloat16)
         output = over_keys(prob_low, value).astype(jnp.bfloat16)
-        grad_qn = over_keys(grad_score, key_low) * score_scale
+        grad_low = over_keys(grad_score, key_low)
+        grad_qn = grad_low * score_scale
         grad_keys = over_queries(grad_score, query_low)
         grad_values = over_queries(prob_low, cot)
         scaled = grad_qn * q_gain
@@ -289,7 +342,9 @@
             * jnp.mean(scaled * query, axis=1, keepdims=True)
         ).astype(jnp.bfloat16)
         gain_grad_ref[0:1, :] += jnp.sum(grad_qn * query_hat, axis=0, keepdims=True)
-        gain_grad_ref[1:2, :] += jnp.sum(grad_keys * key_hat, axis=0, keepdims=True)
+        gain_grad_ref[1:2, :] += (
+            jnp.sum(grad_low * query_low.astype(jnp.float32), axis=0, keepdims=True) / k_gain
+        )
 
         out_ref[:, cols] = output[:frames]
         grad_query_ref[:, cols] = grad_query[:frames]
@@ -320,7 +375,7 @@
             start += rows
 
 
-def attention(chunk, meta, gains, query, cot, key, value, mate, one, mid, lyrics, groups, carried):
+def attention(chunk, meta, gains, query, cot, value, key, mate, one, mid, lyrics, groups, carried):
     frames, width = query.shape
     head_size = gains.shape[1]
     size = width // 2 // CHUNKS
@@ -356,8 +411,9 @@
             num_scalar_prefetch=1,
             grid=(steps,),
             in_specs=[pl.BlockSpec(gains.shape, whole)]
-            + [own(frames)] * 4
+            + [own(frames)] * 3
             + [
+                pl.BlockSpec((2 * frames, step), lambda i, meta: (0, chunk * steps + i)),
                 pl.BlockSpec((mate.shape[0], step), lambda i, meta: (0, chunk * steps + i)),
                 columns(one.shape[0]),
                 columns(mid.shape[0]),
@@ -383,7 +439,7 @@
             transcendentals=key_rows * lanes * (size // head_size),
         ),
         name="attention",
-    )(meta, gains, query, cot, key, value, mate, one, mid, *lyrics, *carried)
+    )(meta, gains, query, cot, value, key, mate, one, mid, *lyrics, *carried)
 
 
 def fill_kernel(count, core_ref, mate_ref, *refs):
@@ -415,6 +471,19 @@
         cost_estimate=SMALL,
         name="fill_other",
     )(core, mate, *arrays)
+
+
+def normed(raw, k_gain):
+    raw = raw.astype(jnp.float32)
+    inverse = lax.rsqrt(jnp.mean(raw * raw, axis=1, keepdims=True) + NORM_EPS)
+    return (raw * inverse * k_gain).astype(jnp.bfloat16)
+
+
+def norm_columns(out_ref, rows, raw, gain_ref):
+    head_size = gain_ref.shape[1]
+    for head in range(raw.shape[1] // head_size):
+        cols = slice(head * head_size, (head + 1) * head_size)
+        out_ref[rows, cols] = normed(raw[:, cols], gain_ref[1:2, :])
 
 
 def through_norm(raw, grad, k_gain):
@@ -531,9 +600,11 @@
     )(part, arrived, *sums, later)
 
 
-def finish_lyric_kernel(head_size, gain_ref, raw_ref, held_ref, one_ref, two_ref, *refs):
-    lyric_rows = raw_ref.shape[0]
-    rows = lyric_rows // 4
+def finish_lyric_kernel(
+    head_size, state_ref, gain_ref, raw_ref, mate_ref, held_ref, one_ref, two_ref, *refs
+):
+    rows = raw_ref.shape[0]
+    lyric_rows = 4 * rows
     own_ref, to_mate_ref, total_ref = refs[-3:]
     k_gain = gain_ref[1:2, :]
     if len(refs) == 4:
@@ -545,42 +616,55 @@
         total = held_ref[:, cols].astype(jnp.float32)
         for part in (one_ref, two_ref):
             total = total + part[0:lyric_rows, cols].astype(jnp.float32)
-        for index, ref in enumerate((own_ref, to_mate_ref)):
+        for index, (ref, raw) in enumerate(((own_ref, raw_ref), (to_mate_ref, mate_ref))):
             base = 2 * rows * index
             ref[0:rows, cols] = through_norm(
-                raw_ref[base : base + rows, cols], total[base : base + rows], k_gain
+                raw[0:rows, cols], total[base : base + rows], k_gain
             )
             ref[rows : 2 * rows, cols] = total[base + rows : base + 2 * rows].astype(jnp.bfloat16)
         to_mate_ref[2 * rows :, cols] = split_rows(total_ref[...])
 
 
-def finish_lyric(gains, raw, held, one, two, sums, frames):
-    rows, size = raw.shape
+def finish_lyric(state, chunk, gains, raw, mate, held, one, two, sums, frames):
+    rows = raw.shape[0]
+    size = held.shape[1]
     head_size = gains.shape[1]
     step = size // 2
-    tail = rows // 2 + GAIN_ROWS
-    spec = pl.BlockSpec((rows, step), lambda i: (0, i))
-    whole = pl.BlockSpec((8, head_size), lambda i: (0, 0))
+    tail = 2 * rows + GAIN_ROWS
+    last = mate.shape[0] // BLK - 1
+    spec = pl.BlockSpec((4 * rows, step), lambda i, state: (0, i))
+    whole = pl.BlockSpec((8, head_size), lambda i, state: (0, 0))
     return pl.pallas_call(
         functools.partial(finish_lyric_kernel, head_size),
-        grid=(2,),
-        in_specs=[pl.BlockSpec(gains.shape, lambda i: (0, 0)), spec, spec, spec]
-        + [pl.BlockSpec((two.shape[0], step), lambda i: (0, i))]
-        + [whole] * len(sums),
-        out_specs=[
-            pl.BlockSpec((rows // 2, step), lambda i: (0, i)),
-            pl.BlockSpec((tail, step), lambda i: (4 * frames // tail, i)),
-            whole,
-        ],
+        grid_spec=pltpu.PrefetchScalarGridSpec(
+            num_scalar_prefetch=1,
+            grid=(2,),
+            in_specs=[
+                pl.BlockSpec(gains.shape, lambda i, state: (0, 0)),
+                pl.BlockSpec(
+                    (rows, step), lambda i, state: (0, (state[0] * CHUNKS + chunk) * 2 + i)
+                ),
+                pl.BlockSpec((BLK, step), lambda i, state: (last, chunk * 2 + i)),
+                spec,
+                spec,
+                pl.BlockSpec((two.shape[0], step), lambda i, state: (0, i)),
+            ]
+            + [whole] * len(sums),
+            out_specs=[
+                pl.BlockSpec((2 * rows, step), lambda i, state: (0, i)),
+                pl.BlockSpec((tail, step), lambda i, state: (4 * frames // tail, i)),
+                whole,
+            ],
+        ),
         out_shape=[
-            jax.ShapeDtypeStruct((rows // 2, size), jnp.bfloat16),
+            jax.ShapeDtypeStruct((2 * rows, size), jnp.bfloat16),
             jax.ShapeDtypeStruct((4 * frames + tail, size), jnp.bfloat16),
             jax.ShapeDtypeStruct((8, head_size), jnp.float32),
         ],
         compiler_params=params(),
         cost_estimate=SMALL,
         name="finish_lyric",
-    )(gains, raw, held, one, two, *sums)
+    )(state, gains, raw, mate, held, one, two, *sums)
 
 
 def join_kernel(count, chunks, state_ref, gain_ref, *refs):
@@ -633,6 +717,18 @@
     )(state, gain, *own, *mate, *arrays)
 
 
+def norm_rows_kernel(gain_ref, raw_ref, out_ref):
+    norm_columns(out_ref, slice(0, raw_ref.shape[0]), raw_ref[...], gain_ref)
+
+
+def norm_rows(gains, raw):
+    return pl.pallas_call(
+        norm_rows_kernel,
+        out_shape=jax.ShapeDtypeStruct(raw.shape, raw.dtype),
+        name="norm_rows",
+    )(gains, raw)
+
+
 def norm_lyric_kernel(head_size, gain_ref, raw_ref, grad_ref, out_ref):
     for head in range(raw_ref.shape[1] // head_size):
         cols = slice(head * head_size, (head + 1) * head_size)
@@ -698,7 +794,9 @@
     else:
         gathered = jnp.concatenate(
             [
-                lax.all_gather(lyric_keys[0], "seq", axis=0, tiled=True),
+                lax.all_gather(
+                    norm_rows(gains, lyric_keys[0]), "seq", axis=0, tiled=True
+                ),
                 lax.all_gather(lyric_values[0], "seq", axis=0, tiled=True),
             ],
             axis=0,
@@ -729,16 +827,18 @@
     carried = []
     for chunk in range(CHUNKS):
         if hops:
-            pair = pair_lyrics(state, chunk, lyric_keys[0], lyric_values[0], mate)
+            pair = pair_lyrics(state, chunk, gains, lyric_keys[0], lyric_values[0], mate)
             two = hop(pair, across)
             lyrics = [pair, two, hop(two, partners)]
             lead, after = [pair], [two]
         else:
             lyrics, lead, after = [gathered], [], []
-        one = hop(edge(state, chunk, 1, keys[0], values[0], mate, lead, []), partners)
-        mid = hop(edge(state, chunk, 0, keys[0], values[0], mate, [], after), between)
+        one = hop(edge(state, chunk, 1, gains, keys[0], values[0], mate, lead, []), partners)
+        mid = hop(edge(state, chunk, 0, gains, keys[0], values[0], mate, [], after), between)
+        if chunk == 0:
+            key_low = prepare_keys(state, gains, keys[0], mate, after)
         results = attention(
-            chunk, meta, gains, queries[0], cotangent[0], keys[0], values[0], mate, one, mid,
+            chunk, meta, gains, queries[0], cotangent[0], values[0], key_low, mate, one, mid,
             lyrics, groups, carried,
         )
         carried = [results[7], *results[:2]]
@@ -759,7 +859,7 @@
             to_two, to_one = relay(for_two, hop(to_two, partners), sums, to_one)
             two, one = hop(to_two, across), hop(to_one, partners)
             own_half, to_mate, total = finish_lyric(
-                gains, lyrics[0], held, one, two, sums, frames
+                state, chunk, gains, lyric_keys[0], mate, held, one, two, sums, frames
             )
             own_halves.append(own_half)
             to_mate = [to_mate]

time: 123 us -> 157 us (1.28)
  Pallas kernels: 26.8 us -> 65.3 us
  waiting for transfers between devices: 70.5 us -> 68.4 us
  local copies, waits for them, and re-layouts: 4.08 us -> 2.01 us
    pallas_call x1, Pallas kernels: 4.28 us -> 39.7 us  [pack(): pl.pallas_call(pack_kernel, grid_spec=pltpu.PrefetchScalarGridSpec(num_sc...]
    ppermute x8, waiting for transfers between devices: 58.8 us -> 56.7 us  [hop(): return lax.ppermute(block, 'seq', pairs)]
    unnamed x20, local copies, waits for them, and re-layouts: 2.11 us -> 0.05 us
    pallas_call x1 -> x2, Pallas kernels: 0.6 us -> 2.29 us  [the longest x1 1.16 us: finish_lyric(): pl.pallas_call(functools.partial(finish_lyric_kernel, head_size), grid_sp...]
  transfers between devices with their start and end apart: 13 -> 13, of which waited for: 8 -> 8; matrix products, arithmetic and copies ran while one was open for 2% -> 1% of each run, Pallas kernels for 3% -> 4%
where the time goes in v6:
time: 157 us
  waiting for transfers between devices  68.4 us (44%)
  Pallas kernels  65.3 us (42%)
  starting transfers between devices  19.4 us (12%)
  local copies, waits for them, and re-layouts  2.01 us (1%)
    ppermute x8, waiting for transfers between devices, hop(): return lax.ppermute(block, 'seq', pairs)  56.7 us
    pallas_call x1, Pallas kernels, pack(): pl.pallas_call(pack_kernel, grid_spec=pltpu.PrefetchScalarGridSpec(num_sc...  39.7 us
    pallas_call x1, Pallas kernels, attention(): pl.pallas_call(functools.partial(attention_kernel, groups, bool(carried),...  14.3 us
    ppermute x8, starting transfers between devices, hop(): return lax.ppermute(block, 'seq', pairs)  13.8 us
    ppermute x3, waiting for transfers between devices, sum_over(): lax.ppermute(total, axis, [(i, i ^ bit) for i in range(count)])  5.73 us
    ppermute x3, starting transfers between devices, sum_over(): lax.ppermute(total, axis, [(i, i ^ bit) for i in range(count)])  5.13 us
    pallas_call x2, Pallas kernels, edge(): pl.pallas_call(functools.partial(edge_kernel, touching), grid_spec=pltpu....  3.59 us
  transfers between devices with their start and end apart: 13, of which 8 were waited for; matrix products, arithmetic and copies ran while one was open for 1% of the time, Pallas kernels for 4%

profile of v6, /device:TPU:0, one launch (start us, length us, event | category | flops | bytes accessed | tf_op | source)
XLA Modules:
  0.0 157.2 jit_solution(14589576544264113869)
XLA Ops:
  0.7 0.6 pad_add_fusion.state_ref
  1.3 0.0 copy-start.8
  1.3 0.0 copy-start.9
  1.3 0.0 copy-start.2
  1.3 0.0 copy-start.3
  1.3 0.0 copy-start.6
  1.3 39.7 %pack.1 = bf16[640,1024]{1,0:T(8,128)(2,1)} custom-call(s32[2]{0:T(128)} %pad_add_fusion.state_ref, s32[2]{0:T(128)} %bitcast.53, bf16[128,2048]{1,0:T(8,128)(2,1)} %bitcast.45, bf16[128,2048]{1,0:T(8,128)(2,1)} %bitcast.47, bf16[128,2048]{1,0:T(8,128)(2,1)} %bitcast.31, bf16[128,2048]{1,0:T(8,128)(2,1)} %bitcast.36, bf16[48,2048]{1,0:T(8,128)(2,1)} %bitcast.40, ...), custom_call_target="tpu_custom_call" | custom-call | flops 1 | bytes 1 | tf_op jit(solution)/shard_map/pack/pallas_call | solution.py:80
  41.0 0.0 copy-start
  41.0 0.0 copy-start.1
  41.0 0.5 collective-permute-start
  41.5 0.0 copy-done.8
  41.5 0.0 copy-done.9
  41.5 2.9 %collective-permute-done.mate_ref.mate_key_ref.mate_value_ref = bf16[640,1024]{1,0:T(8,128)(2,1)S(1)} collective-permute-done((bf16[640,1024]{1,0:T(8,128)(2,1)}, bf16[640,1024]{1,0:T(8,128)(2,1)S(1)}, u32[]{:S(2)}, u32[]{:S(2)}) %collective-permute-start) | collective-permute-done | bytes 1310752 | tf_op jit(solution)/shard_map/ppermute | solution.py:825
  44.4 0.0 copy-done.2
  44.4 0.0 copy-done.3
  44.4 0.0 copy-done.6
  44.4 1.0 pair_lyrics.1.refs_0_
  45.4 4.0 %collective-permute-start.1 = (bf16[192,1024]{1,0:T(8,128)(2,1)S(1)}, bf16[192,1024]{1,0:T(8,128)(2,1)S(1)}, u32[]{:S(2)}, u32[]{:S(2)}) collective-permute-start(bf16[192,1024]{1,0:T(8,128)(2,1)S(1)} %pair_lyrics.1.refs_0_), channel_id=1, source_target_pairs={{0,4},{1,5},{2,6},{3,7},{4,0},{5,1},{6,2},{7,3},{8,12},{9,13},{10,... | collective-permute-start | bytes 1179656 | tf_op jit(solution)/shard_map/ppermute | solution.py:780
  49.4 0.0 copy-done
  49.4 0.0 copy-done.1
  49.4 1.9 %edge.2 = bf16[448,1024]{1,0:T(8,128)(2,1)} custom-call(s32[2]{0:T(128)S(1)} %copy-done.6, f32[2,128]{1,0:T(2,128)S(1)} %pad_maximum_fusion.gain_ref, bf16[128,2048]{1,0:T(8,128)(2,1)S(1)} %bitcast.32, bf16[128,2048]{1,0:T(8,128)(2,1)S(1)} %bitcast.37, bf16[640,1024]{1,0:T(8,128)(2,1)S(1)} %collective-permute-done.mate_ref.mate_key_ref.mate_value_ref, ...), custom_call_target="tpu_custom_call" | custom-call | flops 1 | bytes 1 | tf_op jit(solution)/shard_map/edge/pallas_call | solution.py:153
  51.3 0.0 copy-start.7
  51.3 1.6 %collective-permute-start.2 = (bf16[448,1024]{1,0:T(8,128)(2,1)}, bf16[448,1024]{1,0:T(8,128)(2,1)}, u32[]{:S(2)}, u32[]{:S(2)}) collective-permute-start(bf16[448,1024]{1,0:T(8,128)(2,1)} %edge.2), channel_id=1, source_target_pairs={{0,2},{1,3},{2,0},{3,1},{4,6},{5,7},{6,4},{7,5},{8,10},{9,11},{10,... | collective-permute-start | bytes 2752520 | tf_op jit(solution)/shard_map/ppermute | solution.py:780
  52.9 14.5 %collective-permute-done.1.refs_0_.refs_1_ = bf16[192,1024]{1,0:T(8,128)(2,1)S(1)} collective-permute-done((bf16[192,1024]{1,0:T(8,128)(2,1)S(1)}, bf16[192,1024]{1,0:T(8,128)(2,1)S(1)}, u32[]{:S(2)}, u32[]{:S(2)}) %collective-permute-start.1) | collective-permute-done | bytes 393248 | tf_op jit(solution)/shard_map/ppermute | solution.py:780
  67.3 1.7 %edge.3 = bf16[256,1024]{1,0:T(8,128)(2,1)} custom-call(s32[2]{0:T(128)S(1)} %copy-done.6, f32[2,128]{1,0:T(2,128)S(1)} %pad_maximum_fusion.gain_ref, bf16[128,2048]{1,0:T(8,128)(2,1)S(1)} %bitcast.33, bf16[128,2048]{1,0:T(8,128)(2,1)S(1)} %bitcast.38, bf16[640,1024]{1,0:T(8,128)(2,1)S(1)} %collective-permute-done.mate_ref.mate_key_ref.mate_value_ref, ...), custom_call_target="tpu_custom_call" | custom-call | flops 1 | bytes 1 | tf_op jit(solution)/shard_map/edge/pallas_call | solution.py:153
  69.1 1.5 collective-permute-start.3
  70.5 1.2 collective-permute-start.4
  72.4 0.0 copy-done.7
  72.4 0.6 fusion
  73.0 1.4 stack.77.meta_ref
  74.3 0.0 copy-start.4
  74.4 0.0 copy-start.5
  74.4 1.1 prepare_keys.1.key_ref
  75.5 13.9 %collective-permute-done.4.refs_2_ = bf16[192,1024]{1,0:T(8,128)(2,1)} collective-permute-done((bf16[192,1024]{1,0:T(8,128)(2,1)S(1)}, bf16[192,1024]{1,0:T(8,128)(2,1)}, u32[]{:S(2)}, u32[]{:S(2)}) %collective-permute-start.4) | collective-permute-done | bytes 393248 | tf_op jit(solution)/shard_map/ppermute | solution.py:780
  89.4 0.0 collective-permute-done.3.mid_ref
  89.4 0.0 collective-permute-done.2.one_ref
  89.4 0.0 copy-done.4
  89.4 0.0 copy-done.5
  89.4 14.3 %attention.1 = (bf16[128,2048]{1,0:T(8,128)(2,1)}, bf16[128,2048]{1,0:T(8,128)(2,1)}, bf16[256,1024]{1,0:T(8,128)(2,1)S(1)}, f32[256,1024]{1,0:T(8,128)S(1)}, f3...) custom-call(s32[15]{0:T(128)S(1)} %stack.77.meta_ref, ...), custom_call_target="tpu_custom_call" | custom-call | flops 2415919104 | bytes 16777216 | tf_op jit(solution)/shard_map/attention/pallas_call | solution.py:406
  103.7 0.0 collective-permute-start.5
  103.7 1.6 %collective-permute-start.6 = (f32[8,128]{1,0:T(8,128)S(1)}, f32[8,128]{1,0:T(8,128)S(1)}, u32[]{:S(2)}, u32[]{:S(2)}) collective-permute-start(f32[8,128]{1,0:T(8,128)S(1)} %get-tuple-element.38), channel_id=1, source_target_pairs={{0,8},{8,0},{16,24},{24,16},{1,9},{9,1},{17,25},{25,17},{2,10},{10... | collective-permute-start | bytes 12296 | tf_op jit(solution)/shard_map/ppermute | solution.py:749
  105.3 2.1 %collective-permute-done.6 = f32[8,128]{1,0:T(8,128)S(1)} collective-permute-done((f32[8,128]{1,0:T(8,128)S(1)}, f32[8,128]{1,0:T(8,128)S(1)}, u32[]{:S(2)}, u32[]{:S(2)}) %collective-permute-start.6) | collective-permute-done | bytes 4128 | tf_op jit(solution)/shard_map/ppermute | solution.py:749
  107.3 1.6 collective-permute-start.7
  108.9 2.0 %collective-permute-done.7 = f32[8,128]{1,0:T(8,128)S(1)} collective-permute-done((f32[8,128]{1,0:T(8,128)S(1)}, f32[8,128]{1,0:T(8,128)S(1)}, u32[]{:S(2)}, u32[]{:S(2)}) %collective-permute-start.7) | collective-permute-done | bytes 4128 | tf_op jit(solution)/shard_map/ppermute | solution.py:749
  110.9 2.0 %collective-permute-start.8 = (f32[8,128]{1,0:T(8,128)S(1)}, f32[8,128]{1,0:T(8,128)S(1)}, u32[]{:S(2)}, u32[]{:S(2)}) collective-permute-start(f32[8,128]{1,0:T(8,128)S(1)} %add.52), channel_id=1, source_target_pairs={{0,2},{1,3},{2,0},{3,1},{4,6},{5,7},{6,4},{7,5},{8,10},{9,11},{10,... | collective-permute-start | bytes 12296 | tf_op jit(solution)/shard_map/ppermute | solution.py:749
  112.9 1.6 %collective-permute-done.8 = f32[8,128]{1,0:T(8,128)S(1)} collective-permute-done((f32[8,128]{1,0:T(8,128)S(1)}, f32[8,128]{1,0:T(8,128)S(1)}, u32[]{:S(2)}, u32[]{:S(2)}) %collective-permute-start.8) | collective-permute-done | bytes 4128 | tf_op jit(solution)/shard_map/ppermute | solution.py:749
  114.6 0.0 collective-permute-done.5.arrived_ref
  114.6 0.2 relay.1
  114.8 2.1 %collective-permute-start.9 = (bf16[448,1024]{1,0:T(8,128)(2,1)S(1)}, bf16[448,1024]{1,0:T(8,128)(2,1)S(1)}, u32[]{:S(2)}, u32[]{:S(2)}) collective-permute-start(bf16[448,1024]{1,0:T(8,128)(2,1)S(1)} %get-tuple-element.40), channel_id=1, source_target_pairs={{0,2},{1,3},{2,0},{3,1},{4,6},{5,7},{6,4},{7,5},{8,10},{9,11},{10,... | collective-permute-start | bytes 2752520 | tf_op jit(solution)/shard_map/ppermute | solution.py:780
  116.9 0.7 collective-permute-start.11
  117.6 2.8 %collective-permute-start.10 = (bf16[224,1024]{1,0:T(8,128)(2,1)S(1)}, bf16[224,1024]{1,0:T(8,128)(2,1)S(1)}, u32[]{:S(2)}, u32[]{:S(2)}) collective-permute-start(bf16[224,1024]{1,0:T(8,128)(2,1)S(1)} %get-tuple-element.41), channel_id=1, source_target_pairs={{0,4},{1,5},{2,6},{3,7},{4,0},{5,1},{6,2},{7,3},{8,12},{9,13},{10,... | collective-permute-start | bytes 1376264 | tf_op jit(solution)/shard_map/ppermute | solution.py:780
  120.4 28.3 %collective-permute-done.10.two_ref = bf16[224,1024]{1,0:T(8,128)(2,1)S(1)} collective-permute-done((bf16[224,1024]{1,0:T(8,128)(2,1)S(1)}, bf16[224,1024]{1,0:T(8,128)(2,1)S(1)}, u32[]{:S(2)}, u32[]{:S(2)}) %collective-permute-start.10) | collective-permute-done | bytes 458784 | tf_op jit(solution)/shard_map/ppermute | solution.py:780
  148.7 0.0 collective-permute-done.9.one_ref
  148.7 1.2 finish_lyric.1
  149.9 0.0 collective-permute-done.11.mid_ref
  149.9 2.6 %finish_audio.1 = (bf16[128,2048]{1,0:T(8,128)(2,1)}, bf16[128,2048]{1,0:T(8,128)(2,1)}, bf16[640,1024]{1,0:T(8,128)(2,1)S(1)}) custom-call(s32[2]{0:T(128)S(1)} %copy-done.6, f32[2,128]{1,0:T(2,128)S(1)} %pad_maximum_fusion.gain_ref, bf16[128,2048]{1,0:T(8,128)(2,1)S(1)} %bitcast.35, ...), custom_call_target="tpu_custom_call", output_to_operand_aliasing={{2}: (9, {})} | custom-call | flops 1 | bytes 1 | tf_op jit(solution)/shard_map/finish_audio/pallas_call | solution.py:546
  152.5 0.0 collective-permute-start.12
  152.5 3.0 %collective-permute-done.12.refs_1_ = bf16[640,1024]{1,0:T(8,128)(2,1)S(1)} collective-permute-done((bf16[640,1024]{1,0:T(8,128)(2,1)S(1)}, bf16[640,1024]{1,0:T(8,128)(2,1)S(1)}, u32[]{:S(2)}, u32[]{:S(2)}) %collective-permute-start.12) | collective-permute-done | bytes 1310752 | tf_op jit(solution)/shard_map/ppermute | solution.py:873
  155.5 1.7 %join.1 = (bf16[128,2048]{1,0:T(8,128)(2,1)}, bf16[128,2048]{1,0:T(8,128)(2,1)}, bf16[128,2048]{1,0:T(8,128)(2,1)}, bf16[128,2048]{1,0:T(8,128)(2,1)}, bf16[48,2...) custom-call(s32[2]{0:T(128)S(1)} %copy-done.6, ...), custom_call_target="tpu_custom_call", output_to_operand_aliasing={{0}: (4, {}), {1}: (5, {}), {2}: (6, {}), {3}: (7, {})} | custom-call | flops 1 | bytes 1 | tf_op jit(solution)/shard_map/join/pallas_call | solution.py:699
  (4 shorter events, 0.0 us)
Async XLA Ops:
  1.3 40.3 %copy-start.8 = (f32[128]{0:T(128)S(1)}, f32[128]{0:T(128)}, u32[]{:S(2)}) copy-start(f32[128]{0:T(128)} %param.16) | copy-start | bytes 1540
  1.3 40.3 %copy-start.9 = (f32[128]{0:T(128)S(1)}, f32[128]{0:T(128)}, u32[]{:S(2)}) copy-start(f32[128]{0:T(128)} %param.15) | copy-start | bytes 1540
  1.3 43.1 %copy-start.2 = (bf16[1,48,2048]{2,1,0:T(8,128)(2,1)S(1)}, bf16[1,48,2048]{2,1,0:T(8,128)(2,1)}, u32[]{:S(2)}) copy-start(bf16[1,48,2048]{2,1,0:T(8,128)(2,1)} %param.13) | copy-start | bytes 589828
  1.3 43.1 %copy-start.3 = (bf16[1,48,2048]{2,1,0:T(8,128)(2,1)S(1)}, bf16[1,48,2048]{2,1,0:T(8,128)(2,1)}, u32[]{:S(2)}) copy-start(bf16[1,48,2048]{2,1,0:T(8,128)(2,1)} %param.14) | copy-start | bytes 589828
  1.3 43.1 %copy-start.6 = (s32[2]{0:T(128)S(1)}, s32[2]{0:T(128)}, u32[]{:S(2)}) copy-start(s32[2]{0:T(128)} %pad_add_fusion.state_ref) | copy-start | bytes 28
  41.0 8.4 %copy-start = (bf16[1,128,2048]{2,1,0:T(8,128)(2,1)S(1)}, bf16[1,128,2048]{2,1,0:T(8,128)(2,1)}, u32[]{:S(2)}) copy-start(bf16[1,128,2048]{2,1,0:T(8,128)(2,1)} %param.11) | copy-start | bytes 1572868
  41.0 8.4 %copy-start.1 = (bf16[1,128,2048]{2,1,0:T(8,128)(2,1)S(1)}, bf16[1,128,2048]{2,1,0:T(8,128)(2,1)}, u32[]{:S(2)}) copy-start(bf16[1,128,2048]{2,1,0:T(8,128)(2,1)} %param.12) | copy-start | bytes 1572868
  41.0 3.4 %collective-permute-start = (bf16[640,1024]{1,0:T(8,128)(2,1)}, bf16[640,1024]{1,0:T(8,128)(2,1)S(1)}, u32[]{:S(2)}, u32[]{:S(2)}) collective-permute-start(bf16[640,1024]{1,0:T(8,128)(2,1)} %pack.1), channel_id=1, source_target_pairs={{0,1},{1,0},{2,3},{3,2},{4,5},{5,4},{6,7},{7,6},{8,9},{9,8},{10,11... | collective-permute-start | bytes 3932168 | tf_op jit(solution)/shard_map/ppermute | solution.py:825
  45.4 22.0 %collective-permute-start.1 = (bf16[192,1024]{1,0:T(8,128)(2,1)S(1)}, bf16[192,1024]{1,0:T(8,128)(2,1)S(1)}, u32[]{:S(2)}, u32[]{:S(2)}) collective-permute-start(bf16[192,1024]{1,0:T(8,128)(2,1)S(1)} %pair_lyrics.1.refs_0_), channel_id=1, source_target_pairs={{0,4},{1,5},{2,6},{3,7},{4,0},{5,1},{6,2},{7,3},{8,12},{9,13},{10,... | collective-permute-start | bytes 1179656 | tf_op jit(solution)/shard_map/ppermute | solution.py:780
  51.3 21.1 %copy-start.7 = (s32[1,1,2]{2,1,0:T(1,128)S(1)}, s32[1,1,2]{2,1,0:T(1,128)}, u32[]{:S(2)}) copy-start(s32[1,1,2]{2,1,0:T(1,128)} %param.18) | copy-start | bytes 28
  51.3 38.1 %collective-permute-start.2 = (bf16[448,1024]{1,0:T(8,128)(2,1)}, bf16[448,1024]{1,0:T(8,128)(2,1)}, u32[]{:S(2)}, u32[]{:S(2)}) collective-permute-start(bf16[448,1024]{1,0:T(8,128)(2,1)} %edge.2), channel_id=1, source_target_pairs={{0,2},{1,3},{2,0},{3,1},{4,6},{5,7},{6,4},{7,5},{8,10},{9,11},{10,... | collective-permute-start | bytes 2752520 | tf_op jit(solution)/shard_map/ppermute | solution.py:780
  69.1 20.3 %collective-permute-start.3 = (bf16[256,1024]{1,0:T(8,128)(2,1)}, bf16[256,1024]{1,0:T(8,128)(2,1)}, u32[]{:S(2)}, u32[]{:S(2)}) collective-permute-start(bf16[256,1024]{1,0:T(8,128)(2,1)} %edge.3), channel_id=1, source_target_pairs={{2,4},{3,5},{4,2},{5,3},{10,12},{11,13},{12,10},{13,11},{18,20},{1... | collective-permute-start | bytes 1572872 | tf_op jit(solution)/shard_map/ppermute | solution.py:780
  70.5 18.9 %collective-permute-start.4 = (bf16[192,1024]{1,0:T(8,128)(2,1)S(1)}, bf16[192,1024]{1,0:T(8,128)(2,1)}, u32[]{:S(2)}, u32[]{:S(2)}) collective-permute-start(bf16[192,1024]{1,0:T(8,128)(2,1)S(1)} %collective-permute-done.1.refs_0_.refs_1_), channel_id=1, source_target_pairs={{0,2},{1,3},{2,0},{3,1},{4,6},{5,7},{6,4},{7,5},{8,10},{9,11},{10,... | collective-permute-start | bytes 1179656 | tf_op jit(solution)/shard_map/ppermute | solution.py:780
  74.3 15.1 %copy-start.4 = (bf16[1,128,2048]{2,1,0:T(8,128)(2,1)S(1)}, bf16[1,128,2048]{2,1,0:T(8,128)(2,1)}, u32[]{:S(2)}) copy-start(bf16[1,128,2048]{2,1,0:T(8,128)(2,1)} %param.10) | copy-start | bytes 1572868
  74.4 15.1 %copy-start.5 = (bf16[1,128,2048]{2,1,0:T(8,128)(2,1)S(1)}, bf16[1,128,2048]{2,1,0:T(8,128)(2,1)}, u32[]{:S(2)}) copy-start(bf16[1,128,2048]{2,1,0:T(8,128)(2,1)} %param.17) | copy-start | bytes 1572868
  103.7 10.9 %collective-permute-start.5 = (bf16[192,1024]{1,0:T(8,128)(2,1)S(1)}, bf16[192,1024]{1,0:T(8,128)(2,1)S(1)}, u32[]{:S(2)}, u32[]{:S(2)}) collective-permute-start(bf16[192,1024]{1,0:T(8,128)(2,1)S(1)} %get-tuple-element.37), channel_id=1, source_target_pairs={{0,2},{1,3},{2,0},{3,1},{4,6},{5,7},{6,4},{7,5},{8,10},{9,11},{10,... | collective-permute-start | bytes 1179656 | tf_op jit(solution)/shard_map/ppermute | solution.py:780
  103.7 3.6 %collective-permute-start.6 = (f32[8,128]{1,0:T(8,128)S(1)}, f32[8,128]{1,0:T(8,128)S(1)}, u32[]{:S(2)}, u32[]{:S(2)}) collective-permute-start(f32[8,128]{1,0:T(8,128)S(1)} %get-tuple-element.38), channel_id=1, source_target_pairs={{0,8},{8,0},{16,24},{24,16},{1,9},{9,1},{17,25},{25,17},{2,10},{10... | collective-permute-start | bytes 12296 | tf_op jit(solution)/shard_map/ppermute | solution.py:749
  107.3 3.6 %collective-permute-start.7 = (f32[8,128]{1,0:T(8,128)S(1)}, f32[8,128]{1,0:T(8,128)S(1)}, u32[]{:S(2)}, u32[]{:S(2)}) collective-permute-start(f32[8,128]{1,0:T(8,128)S(1)} %add.51), channel_id=1, source_target_pairs={{0,16},{8,24},{16,0},{24,8},{1,17},{9,25},{17,1},{25,9},{2,18},{10... | collective-permute-start | bytes 12296 | tf_op jit(solution)/shard_map/ppermute | solution.py:749
  110.9 3.6 %collective-permute-start.8 = (f32[8,128]{1,0:T(8,128)S(1)}, f32[8,128]{1,0:T(8,128)S(1)}, u32[]{:S(2)}, u32[]{:S(2)}) collective-permute-start(f32[8,128]{1,0:T(8,128)S(1)} %add.52), channel_id=1, source_target_pairs={{0,2},{1,3},{2,0},{3,1},{4,6},{5,7},{6,4},{7,5},{8,10},{9,11},{10,... | collective-permute-start | bytes 12296 | tf_op jit(solution)/shard_map/ppermute | solution.py:749
  114.8 33.9 %collective-permute-start.9 = (bf16[448,1024]{1,0:T(8,128)(2,1)S(1)}, bf16[448,1024]{1,0:T(8,128)(2,1)S(1)}, u32[]{:S(2)}, u32[]{:S(2)}) collective-permute-start(bf16[448,1024]{1,0:T(8,128)(2,1)S(1)} %get-tuple-element.40), channel_id=1, source_target_pairs={{0,2},{1,3},{2,0},{3,1},{4,6},{5,7},{6,4},{7,5},{8,10},{9,11},{10,... | collective-permute-start | bytes 2752520 | tf_op jit(solution)/shard_map/ppermute | solution.py:780
  116.9 33.0 %collective-permute-start.11 = (bf16[256,1024]{1,0:T(8,128)(2,1)S(1)}, bf16[256,1024]{1,0:T(8,128)(2,1)S(1)}, u32[]{:S(2)}, u32[]{:S(2)}) collective-permute-start(bf16[256,1024]{1,0:T(8,128)(2,1)S(1)} %get-tuple-element.46), channel_id=1, source_target_pairs={{2,4},{3,5},{4,2},{5,3},{10,12},{11,13},{12,10},{13,11},{18,20},{1... | collective-permute-start | bytes 1572872 | tf_op jit(solution)/shard_map/ppermute | solution.py:780
  117.6 31.1 %collective-permute-start.10 = (bf16[224,1024]{1,0:T(8,128)(2,1)S(1)}, bf16[224,1024]{1,0:T(8,128)(2,1)S(1)}, u32[]{:S(2)}, u32[]{:S(2)}) collective-permute-start(bf16[224,1024]{1,0:T(8,128)(2,1)S(1)} %get-tuple-element.41), channel_id=1, source_target_pairs={{0,4},{1,5},{2,6},{3,7},{4,0},{5,1},{6,2},{7,3},{8,12},{9,13},{10,... | collective-permute-start | bytes 1376264 | tf_op jit(solution)/shard_map/ppermute | solution.py:780
  152.5 3.0 %collective-permute-start.12 = (bf16[640,1024]{1,0:T(8,128)(2,1)S(1)}, bf16[640,1024]{1,0:T(8,128)(2,1)S(1)}, u32[]{:S(2)}, u32[]{:S(2)}) collective-permute-start(bf16[640,1024]{1,0:T(8,128)(2,1)S(1)} %get-tuple-element.49), channel_id=1, source_target_pairs={{0,1},{1,0},{2,3},{3,2},{4,5},{5,4},{6,7},{7,6},{8,9},{9,8},{10,11... | collective-permute-start | bytes 3932168 | tf_op jit(solution)/shard_map/ppermute | solution.py:873

commit v7 on v5

v7 whole, which is shorter than its diff:
```python
import functools

import jax
import jax.numpy as jnp
from jax import lax
from jax.experimental import pallas as pl
from jax.experimental.pallas import tpu as pltpu
from jax.sharding import PartitionSpec as P

BLK = 128
TILES = 2
NORM_EPS = 1e-06
VMEM_LIMIT = 8 * 1024 * 1024
ATTENTION_VMEM_LIMIT = 24 * 1024 * 1024
PACK_VMEM_LIMIT = 60 * 1024 * 1024
VMEM = pl.BlockSpec(memory_space=pltpu.VMEM)
SMEM = pl.BlockSpec(memory_space=pltpu.SMEM)
HBM = pl.BlockSpec(memory_space=pltpu.HBM)
ANY = pl.BlockSpec(memory_space=pl.ANY)
GAIN_ROWS = 32
ALIGN_ROWS = 32
SMALL = pl.CostEstimate(flops=1, bytes_accessed=1, transcendentals=0)


def dot(lhs, rhs, lhs_dim, rhs_dim):
    return lax.dot_general(
        lhs, rhs, (((lhs_dim,), (rhs_dim,)), ((), ())), preferred_element_type=jnp.float32
    )


def call(kernel, name, in_specs, out_specs, out_shape, limit=VMEM_LIMIT, cost=SMALL, **options):
    return pl.pallas_call(
        kernel,
        in_specs=in_specs,
        out_specs=out_specs,
        out_shape=out_shape,
        compiler_params=pltpu.CompilerParams(vmem_limit_bytes=limit),
        cost_estimate=cost,
        name=name,
        **options,
    )


def shape(rows, cols, dtype=jnp.bfloat16):
    return jax.ShapeDtypeStruct((rows, cols), dtype)


def half_of(ref, core):
    half = ref.shape[1] // 2
    return pl.ds(pl.multiple_of(core * half, half), half)


def split_rows(sums):
    high = sums.astype(jnp.bfloat16).astype(jnp.float32)
    rest = sums - high
    middle = rest.astype(jnp.bfloat16).astype(jnp.float32)
    low = rest - middle
    return jnp.concatenate([high, middle, low, jnp.zeros_like(high)], axis=0).astype(jnp.bfloat16)


def joined_rows(rows):
    rows = rows.astype(jnp.float32)
    return (rows[16:24] + rows[8:16]) + rows[0:8]


def normed(raw, k_gain):
    raw = raw.astype(jnp.float32)
    inverse = lax.rsqrt(jnp.mean(raw * raw, axis=1, keepdims=True) + NORM_EPS)
    return (raw * inverse * k_gain).astype(jnp.bfloat16)


def norm_columns(out_ref, rows, raw, gain_ref):
    head_size = gain_ref.shape[1]
    for head in range(raw.shape[1] // head_size):
        cols = slice(head * head_size, (head + 1) * head_size)
        out_ref[rows, cols] = normed(raw[:, cols], gain_ref[1:2, :])


def through_norm(raw, grad, k_gain):
    raw = raw.astype(jnp.float32)
    inverse = lax.rsqrt(jnp.mean(raw * raw, axis=1, keepdims=True) + NORM_EPS)
    scaled = grad * k_gain
    return (
        inverse * scaled
        - raw * (inverse * inverse * inverse) * jnp.mean(scaled * raw, axis=1, keepdims=True)
    ).astype(jnp.bfloat16)


def pack_kernel(state_ref, align_ref, *refs):
    ins, (out_ref, sems) = refs[:-2], refs[-2:]
    start = 0
    copies = []
    for index, ref in enumerate(ins):
        rows = ref.shape[0]
        copies.append(
            pltpu.make_async_copy(
                ref.at[:, half_of(ref, 1 - state_ref[0])],
                out_ref.at[start : start + rows, :],
                sems.at[index],
            )
        )
        copies[-1].start()
        start += rows
    row = lax.broadcasted_iota(jnp.int32, (ALIGN_ROWS, out_ref.shape[1]), 0)
    tiles = jnp.zeros(row.shape, jnp.int32)
    for slot in range(TILES):
        tiles = jnp.where(row == slot, align_ref[slot], tiles)
    out_ref[start:, :] = tiles.astype(jnp.float32).astype(jnp.bfloat16)
    for copy in copies:
        copy.wait()


def pack(state, align, arrays):
    rows = sum(array.shape[0] for array in arrays) + ALIGN_ROWS
    return call(
        pack_kernel,
        "pack",
        [SMEM, SMEM] + [HBM] * len(arrays),
        VMEM,
        shape(rows, arrays[0].shape[1] // 2),
        scratch_shapes=[pltpu.SemaphoreType.DMA((len(arrays),))],
    )(state, align, *arrays)


def pair_kernel(state_ref, gain_ref, key_ref, value_ref, mate_ref, pair_ref):
    rows = key_ref.shape[0]
    first = mate_ref.shape[0] - ALIGN_ROWS - 2 * rows
    own = half_of(key_ref, state_ref[0])
    norm_columns(pair_ref, slice(0, rows), key_ref[:, own], gain_ref)
    pair_ref[rows : 2 * rows, :] = value_ref[:, own]
    norm_columns(
        pair_ref, slice(2 * rows, 3 * rows), mate_ref[first : first + rows, :], gain_ref
    )
    pair_ref[3 * rows :, :] = mate_ref[first + rows : first + 2 * rows, :]


def pair_lyrics(state, gains, lyric_key, lyric_value, mate):
    rows, width = lyric_key.shape
    return call(
        pair_kernel, "pair_lyrics", [SMEM] + [VMEM] * 4, VMEM, shape(4 * rows, width // 2)
    )(state, gains, lyric_key, lyric_value, mate)


def edge_kernel(touching, leading, state_ref, gain_ref, key_ref, value_ref, mate_ref, *refs):
    out_ref = refs[-1]
    frames = key_ref.shape[0]
    first = out_ref.shape[0] - 2 * frames
    if leading:
        out_ref[0:first, :] = refs[0][...]
    mine = state_ref[1] == touching
    own = half_of(key_ref, state_ref[0])
    keys = jnp.where(mine, key_ref[:, own], mate_ref[2 * frames : 3 * frames, :])
    norm_columns(out_ref, slice(first, first + frames), keys, gain_ref)
    out_ref[first + frames :, :] = jnp.where(
        mine, value_ref[:, own], mate_ref[3 * frames : 4 * frames, :]
    )


def edge(state, touching, gains, key, value, mate, lead, after):
    frames, width = key.shape
    rows = sum(array.shape[0] for array in lead) + 2 * frames
    return call(
        functools.partial(edge_kernel, touching, bool(lead)),
        "edge",
        [SMEM] + [VMEM] * (4 + len(lead)) + [ANY] * len(after),
        VMEM,
        shape(rows, width // 2),
    )(state, gains, key, value, mate, *lead, *after)


def prepare_kernel(state_ref, gain_ref, key_ref, mate_ref, *refs):
    out_ref = refs[-1]
    frames = key_ref.shape[0]
    own = half_of(key_ref, state_ref[0])
    norm_columns(out_ref, slice(0, frames), key_ref[:, own], gain_ref)
    norm_columns(
        out_ref, slice(frames, 2 * frames), mate_ref[2 * frames : 3 * frames, :], gain_ref
    )


def prepare_keys(state, gains, key, mate, after):
    frames, width = key.shape
    return call(
        prepare_kernel,
        "prepare_keys",
        [SMEM] + [VMEM] * 3 + [ANY] * len(after),
        VMEM,
        shape(2 * frames, width // 2),
    )(state, gains, key, mate, *after)


def attention_kernel(
    groups, head_size, score_scale, meta_ref, gain_ref, query_ref, grad_ref, value_ref, key_ref,
    mate_ref, one_ref, mid_ref, *refs
):
    frames = query_ref.shape[0]
    exchanged = len(groups) == 4
    inputs = 3 if exchanged else 1
    lyric_in, refs = refs[:inputs], refs[inputs:]
    window = one_ref.shape[0] - 2 * frames
    out_ref, grad_query_ref, to_mate_ref, key_grad_ref, value_grad_ref = refs[:5]
    to_one_ref, to_mid_ref, gain_grad_ref = refs[5:8]
    lyric_out, mask_ref = refs[8:-1], refs[-1]
    runs = [(index, run) for index, group in enumerate(groups) for run in group]
    main = 2 * frames + sum(run[2] for _, run in runs)
    lanes = 2 * frames
    align = mate_ref.shape[0] - ALIGN_ROWS
    touching = meta_ref[1] == 1

    gain_grad_ref[...] = jnp.zeros_like(gain_grad_ref)
    mate_tiles = mate_ref[align:, 0:frames].astype(jnp.float32).astype(jnp.int32)
    start = 0
    for number, (_, (_, _, rows)) in enumerate(runs):
        row = lax.broadcasted_iota(jnp.int32, (rows, lanes), 0) + meta_ref[7 + number]
        keep = jnp.zeros((rows, lanes), jnp.float32)
        for slot in range(TILES):
            tile = jnp.concatenate(
                [
                    jnp.full((1, frames), meta_ref[2 + slot], jnp.int32),
                    mate_tiles[slot : slot + 1],
                ],
                axis=1,
            )
            lower = tile * BLK
            upper = jnp.minimum(lower + BLK, meta_ref[4])
            inside = (row >= lower) & (row < upper) & (lower >= 0)
            keep = jnp.where(inside, 1.0, keep)
        mask_ref[start : start + rows, :] = keep
        start += rows
    lane = lax.broadcasted_iota(jnp.int32, (frames, lanes), 1)
    mask_ref[start : start + frames, :] = jnp.where(
        lane < frames, meta_ref[5], meta_ref[6]
    ).astype(jnp.float32)

    q_gain = gain_ref[0:1, :]
    k_gain = gain_ref[1:2, :]
    heads = key_ref.shape[1] // head_size

    @pl.loop(0, heads)
    def _(head):
        cols = pl.ds(pl.multiple_of(head * head_size, head_size), head_size)
        own_cols = pl.ds(
            pl.multiple_of((meta_ref[0] * heads + head) * head_size, head_size), head_size
        )
        lyric = [ref[:, cols if exchanged else own_cols] for ref in lyric_in]
        if exchanged:
            lyric = [lyric[0], lyric[1], one_ref[0:window, cols], lyric[2]]
        one_rows, mid_rows = one_ref[window:, cols], mid_ref[:, cols]
        near_rows = jnp.where(touching, one_rows, mid_rows)
        far_rows = jnp.where(touching, mid_rows, one_rows)

        def from_mate(number):
            return mate_ref[number * frames : (number + 1) * frames, cols]

        query = jnp.concatenate([query_ref[:, own_cols], from_mate(0)], axis=0)
        query = query.astype(jnp.float32)
        cot = jnp.concatenate([grad_ref[:, own_cols], from_mate(1)], axis=0)
        key_low = jnp.concatenate(
            [key_ref[:, cols]]
            + [lyric[index][run[0] : run[0] + run[2]] for index, run in runs]
            + [near_rows[:frames], far_rows[:frames]],
            axis=0,
        )
        value = jnp.concatenate(
            [value_ref[:, own_cols], from_mate(3)]
            + [lyric[index][run[1] : run[1] + run[2]] for index, run in runs]
            + [near_rows[frames:], far_rows[frames:]],
            axis=0,
        )
        query_inv = lax.rsqrt(jnp.mean(query * query, axis=1, keepdims=True) + NORM_EPS)
        query_hat = query * query_inv
        query_low = (query_hat * (q_gain * score_scale)).astype(jnp.bfloat16)

        near, far = slice(main, main + frames), slice(main + frames, main + 2 * frames)

        def against(rows, columns):
            return jnp.concatenate(
                [
                    dot(rows[:main], columns, 1, 1),
                    jnp.concatenate(
                        [
                            dot(rows[near], columns[:frames], 1, 1),
                            dot(rows[far], columns[frames:], 1, 1),
                        ],
                        axis=1,
                    ),
                ],
                axis=0,
            )

        def over_keys(weights, rows):
            return dot(weights[:main], rows[:main], 0, 0) + jnp.concatenate(
                [
                    dot(weights[main:, :frames], rows[near], 0, 0),
                    dot(weights[main:, frames:], rows[far], 0, 0),
                ],
                axis=0,
            )

        def over_queries(weights, columns):
            return jnp.concatenate(
                [
                    dot(weights[:main], columns, 1, 0),
                    dot(weights[main:, :frames], columns[:frames], 1, 0),
                    dot(weights[main:, frames:], columns[frames:], 1, 0),
                ],
                axis=0,
            )

        exp_scores = jnp.exp(against(key_low, query_low))
        exp_scores = jnp.concatenate(
            [exp_scores[: 2 * frames], exp_scores[2 * frames :] * mask_ref[...]], axis=0
        )
        grad_prob = against(value, cot)
        prob = exp_scores * (1.0 / jnp.sum(exp_scores, axis=0, keepdims=True))
        prob_low = prob.astype(jnp.bfloat16)
        weighted = prob * grad_prob
        delta = jnp.sum(weighted, axis=0, keepdims=True)
        grad_score = (weighted - prob * delta).astype(jnp.bfloat16)
        output = over_keys(prob_low, value).astype(jnp.bfloat16)
        grad_low = over_keys(grad_score, key_low)
        grad_qn = grad_low * score_scale
        grad_keys = over_queries(grad_score, query_low)
        grad_values = over_queries(prob_low, cot)
        scaled = grad_qn * q_gain
        grad_query = (
            query_inv * scaled
            - query_hat
            * (query_inv * query_inv)
            * jnp.mean(scaled * query, axis=1, keepdims=True)
        ).astype(jnp.bfloat16)
        gain_grad_ref[0:1, :] += jnp.sum(grad_qn * query_hat, axis=0, keepdims=True)
        gain_grad_ref[1:2, :] += (
            jnp.sum(grad_low * query_low.astype(jnp.float32), axis=0, keepdims=True) / k_gain
        )

        out_ref[:, cols] = output[:frames]
        grad_query_ref[:, cols] = grad_query[:frames]
        to_mate_ref[0:frames, cols] = output[frames:]
        to_mate_ref[frames:, cols] = grad_query[frames:]
        key_grad_ref[:, cols] = grad_keys[: 2 * frames]
        value_grad_ref[:, cols] = grad_values[: 2 * frames]
        for grads, part in (
            (grad_keys.astype(jnp.bfloat16), 0),
            (grad_values.astype(jnp.bfloat16), frames),
        ):
            to_one_ref[window + part : window + part + frames, cols] = jnp.where(
                touching, grads[near], grads[far]
            )
            to_mid_ref[part : part + frames, cols] = jnp.where(touching, grads[far], grads[near])
        if exchanged:
            held_ref, two_ref, to_two_ref = lyric_out
            outs = (held_ref, two_ref, to_one_ref, to_two_ref)
        else:
            outs = lyric_out
        start = 2 * frames
        for index, (key_row, value_row, rows) in runs:
            part = slice(start, start + rows)
            outs[index][key_row : key_row + rows, cols] = grad_keys[part].astype(jnp.bfloat16)
            outs[index][value_row : value_row + rows, cols] = grad_values[part].astype(
                jnp.bfloat16
            )
            start += rows


def attention(meta, gains, query, cot, value, key, mate, one, mid, lyrics, groups):
    frames, width = query.shape
    head_size = gains.shape[1]
    half = width // 2
    lyric_rows = sum(run[2] for group in groups for run in group)
    key_rows = 3 * frames + lyric_rows
    bf16, f32 = jnp.bfloat16, jnp.float32
    slot = sum(2 * run[2] for run in groups[0])
    out_shape = [shape(frames, half)] * 2
    out_shape += [shape(2 * frames, half, dtype) for dtype in (bf16, f32, f32)]
    out_shape += [shape(one.shape[0], half), shape(2 * frames, half), shape(8, head_size, f32)]
    out_shape += [shape(slot, half)] * len(lyrics)
    return call(
        functools.partial(attention_kernel, groups, head_size, head_size ** (-0.5)),
        "attention",
        [SMEM] + [VMEM] * (8 + len(lyrics)),
        [VMEM] * len(out_shape),
        out_shape,
        limit=ATTENTION_VMEM_LIMIT,
        cost=pl.CostEstimate(
            flops=24 * key_rows * frames * half,
            bytes_accessed=16 * 1024 * 1024,
            transcendentals=2 * key_rows * frames * (half // head_size),
        ),
        scratch_shapes=[pltpu.VMEM((frames + lyric_rows, 2 * frames), f32)],
    )(meta, gains, query, cot, value, key, mate, one, mid, *lyrics)


def finish_audio_kernel(
    aliased, state_ref, gain_ref, raw_ref, mate_ref, key_grad_ref, value_grad_ref, one_ref,
    mid_ref, ready_ref, out_own_ref, query_own_ref, *refs,
):
    refs = refs[aliased:]
    outs, to_mate_ref, key_ref, value_ref, sems = refs[:4], *refs[4:]
    head_size = gain_ref.shape[1]
    k_gain = gain_ref[1:2, :]
    frames = raw_ref.shape[0]
    own, mate = slice(0, frames), slice(frames, 2 * frames)
    first = one_ref.shape[0] - 2 * frames
    touching = state_ref[1] == 1
    copies = [
        pltpu.make_async_copy(source, out.at[:, half_of(out, state_ref[0])], sems.at[index])
        for index, (source, out) in enumerate(
            zip((out_own_ref, query_own_ref, key_ref, value_ref), outs)
        )
    ]
    copies[0].start()
    copies[1].start()
    to_mate_ref[0 : 2 * frames, :] = ready_ref[...]
    raw_keys = raw_ref[:, half_of(raw_ref, state_ref[0])]
    for head in range(key_ref.shape[1] // head_size):
        cols = slice(head * head_size, (head + 1) * head_size)
        one = one_ref[first:, cols].astype(jnp.float32)
        mid = mid_ref[:, cols].astype(jnp.float32)
        for_own = jnp.where(touching, one, mid)
        for_mate = jnp.where(touching, mid, one)
        key_ref[:, cols] = through_norm(
            raw_keys[:, cols], key_grad_ref[own, cols] + for_own[:frames], k_gain
        )
        value_ref[:, cols] = (value_grad_ref[own, cols] + for_own[frames:]).astype(jnp.bfloat16)
        to_mate_ref[2 * frames : 3 * frames, cols] = through_norm(
            mate_ref[2 * frames : 3 * frames, cols],
            key_grad_ref[mate, cols] + for_mate[:frames],
            k_gain,
        )
        to_mate_ref[3 * frames : 4 * frames, cols] = (
            value_grad_ref[mate, cols] + for_mate[frames:]
        ).astype(jnp.bfloat16)
    copies[2].start()
    copies[3].start()
    for copy in copies:
        copy.wait()


def finish_audio(state, gains, raw, mate, key_grad, value_grad, one, mid, ready, owns, to_mate):
    frames, width = raw.shape
    half = width // 2
    return call(
        functools.partial(finish_audio_kernel, len(to_mate)),
        "finish_audio",
        [SMEM] + [VMEM] * (10 + len(to_mate)),
        [HBM] * 4 + [VMEM],
        [shape(frames, width)] * 4 + [shape(5 * frames, half)],
        input_output_aliases={11: 4} if to_mate else {},
        scratch_shapes=[pltpu.VMEM((frames, half), jnp.bfloat16)] * 2
        + [pltpu.SemaphoreType.DMA((4,))],
    )(state, gains, raw, mate, key_grad, value_grad, one, mid, ready, *owns, *to_mate)


def relay_kernel(head_size, part_ref, arrived_ref, total_ref, later_ref, out_ref, handed_ref):
    rows = part_ref.shape[0]
    out_ref[0:rows, :] = (
        part_ref[...].astype(jnp.float32) + arrived_ref[...].astype(jnp.float32)
    ).astype(jnp.bfloat16)
    out_ref[rows:, 0:head_size] = split_rows(total_ref[...])
    out_ref[rows:, head_size:] = jnp.zeros_like(out_ref[rows:, head_size:])


def relay(part, arrived, total, later):
    rows, half = part.shape
    return call(
        functools.partial(relay_kernel, total.shape[1]),
        "relay",
        [VMEM] * 3 + [ANY],
        [VMEM, ANY],
        [shape(rows + GAIN_ROWS, half), shape(*later.shape)],
        input_output_aliases={3: 1},
    )(part, arrived, total, later)


def finish_lyric_kernel(
    state_ref, gain_ref, raw_ref, mate_ref, held_ref, one_ref, two_ref, sum_ref, own_ref,
    to_mate_ref, total_ref,
):
    rows = raw_ref.shape[0]
    head_size = gain_ref.shape[1]
    k_gain = gain_ref[1:2, :]
    first = mate_ref.shape[0] - ALIGN_ROWS - 2 * rows
    end = to_mate_ref.shape[0] - GAIN_ROWS
    total_ref[...] = sum_ref[...] + joined_rows(two_ref[4 * rows :, 0:head_size])
    to_mate_ref[end:, 0:head_size] = split_rows(total_ref[...])
    to_mate_ref[end:, head_size:] = jnp.zeros_like(to_mate_ref[end:, head_size:])
    raw_keys = raw_ref[:, half_of(raw_ref, state_ref[0])]
    for head in range(own_ref.shape[1] // head_size):
        cols = slice(head * head_size, (head + 1) * head_size)
        total = held_ref[:, cols].astype(jnp.float32)
        for part in (one_ref, two_ref):
            total = total + part[0 : 4 * rows, cols].astype(jnp.float32)
        mate_keys = mate_ref[first : first + rows, cols]
        for ref, start, base, raw in (
            (own_ref, 0, 0, raw_keys[:, cols]),
            (to_mate_ref, end - 2 * rows, 2 * rows, mate_keys),
        ):
            ref[start : start + rows, cols] = through_norm(raw, total[base : base + rows], k_gain)
            ref[start + rows : start + 2 * rows, cols] = total[
                base + rows : base + 2 * rows
            ].astype(jnp.bfloat16)


def finish_lyric(state, gains, raw, mate, held, one, two, total, frames):
    rows = raw.shape[0]
    half = held.shape[1]
    return call(
        finish_lyric_kernel,
        "finish_lyric",
        [SMEM] + [VMEM] * 7,
        [VMEM] * 3,
        [
            shape(2 * rows, half),
            shape(4 * frames + 2 * rows + GAIN_ROWS, half),
            shape(*total.shape, jnp.float32),
        ],
    )(state, gains, raw, mate, held, one, two, total)


def join_kernel(count, state_ref, gain_ref, own_ref, mate_ref, *refs):
    outs, (q_total_ref, k_total_ref, sems) = refs[count:-3], refs[-3:]
    frames = outs[0].shape[0]
    rows = own_ref.shape[0] // 2
    pieces = [
        (mate_ref.at[index * frames : (index + 1) * frames, :], out, 1 - state_ref[0])
        for index, out in enumerate(outs[:count])
    ]
    for ref, first, core in ((own_ref, 0, state_ref[0]), (mate_ref, count * frames, 1 - state_ref[0])):
        for index, out in enumerate(outs[count:]):
            start = first + index * rows
            pieces.append((ref.at[start : start + rows, :], out, core))
    copies = [
        pltpu.make_async_copy(source, out.at[:, half_of(out, core)], sems.at[index])
        for index, (source, out, core) in enumerate(pieces)
    ]
    for copy in copies:
        copy.start()
    sums = mate_ref[mate_ref.shape[0] - GAIN_ROWS :, 0 : gain_ref.shape[1]]
    total = gain_ref[...] + joined_rows(sums)
    q_total_ref[...] = total[0:1]
    k_total_ref[...] = total[1:2]
    for copy in copies:
        copy.wait()


def join(state, gain, arrays, own, mate):
    rows, half = own.shape
    count = len(arrays)
    return call(
        functools.partial(join_kernel, count),
        "join",
        [SMEM] + [VMEM] * 3 + [HBM] * count,
        [HBM] * (count + 2) + [VMEM] * 2,
        [shape(*array.shape) for array in arrays]
        + [shape(rows // 2, 2 * half)] * 2
        + [shape(1, gain.shape[1], jnp.float32)] * 2,
        input_output_aliases={4 + i: i for i in range(count)},
        scratch_shapes=[pltpu.SemaphoreType.DMA((count + 4,))],
    )(state, gain, own, mate, *arrays)


def fill_kernel(count, state_ref, mate_ref, *refs):
    outs, sems = refs[count:-1], refs[-1]
    frames = outs[0].shape[0]
    copies = [
        pltpu.make_async_copy(
            mate_ref.at[index * frames : (index + 1) * frames, :],
            out.at[:, half_of(out, 1 - state_ref[0])],
            sems.at[index],
        )
        for index, out in enumerate(outs)
    ]
    for copy in copies:
        copy.start()
    for copy in copies:
        copy.wait()


def fill_other(state, arrays, mate):
    count = len(arrays)
    return call(
        functools.partial(fill_kernel, count),
        "fill_other",
        [SMEM, VMEM] + [HBM] * count,
        [HBM] * count,
        [shape(*array.shape) for array in arrays],
        input_output_aliases={2 + i: i for i in range(count)},
        scratch_shapes=[pltpu.SemaphoreType.DMA((count,))],
    )(state, mate, *arrays)


def norm_rows_kernel(gain_ref, raw_ref, out_ref):
    norm_columns(out_ref, slice(0, raw_ref.shape[0]), raw_ref[...], gain_ref)


def norm_rows(gains, raw):
    return pl.pallas_call(
        norm_rows_kernel,
        out_shape=jax.ShapeDtypeStruct(raw.shape, raw.dtype),
        name="norm_rows",
    )(gains, raw)


def norm_lyric_kernel(head_size, gain_ref, raw_ref, grad_ref, out_ref):
    for head in range(raw_ref.shape[1] // head_size):
        cols = slice(head * head_size, (head + 1) * head_size)
        out_ref[:, cols] = through_norm(raw_ref[:, cols], grad_ref[:, cols], gain_ref[1:2, :])


def norm_lyric(gains, raw, grad):
    return pl.pallas_call(
        functools.partial(norm_lyric_kernel, gains.shape[1]),
        out_shape=jax.ShapeDtypeStruct(raw.shape, jnp.bfloat16),
        name="norm_lyric",
    )(gains, raw, grad)


def sum_over(total, axis, bits):
    count = lax.axis_size(axis)
    for bit in bits:
        total = total + lax.ppermute(total, axis, [(i, i ^ bit) for i in range(count)])
    return total


def bits_of(count):
    return [1 << bit for bit in range(count.bit_length() - 1)]


def body(
    queries, keys, values, lyric_keys, lyric_values, q_gain, k_gain, cotangent, alignment, lyric_len
):
    frames = queries.shape[1]
    lyric_local, width = lyric_keys.shape[1:]
    count = lax.axis_size("seq")
    songs = lax.axis_size("song")
    me = lax.axis_index("seq")
    core = me % 2
    chips = count // 2
    chip = me // 2
    touching = (chip % 2) ^ core
    state = jnp.stack([core, touching]).astype(jnp.int32)
    gains = jnp.stack([q_gain, k_gain])

    swap = [(i, i ^ 1) for i in range(count)]
    partners = [(a, a ^ 1) for a in range(chips)]
    across = [(a, a ^ 2) for a in range(chips)]
    between = [(a, a + 1) for a in range(1, chips - 1, 2)]
    between += [(b, a) for a, b in between]

    def hop(block, moves):
        pairs = [(2 * a + c, 2 * b + c) for a, b in moves for c in (0, 1)]
        return lax.ppermute(block, "seq", pairs)

    hops = chips == 4 and lyric_local % 16 == 0 and 2 * lyric_local + GAIN_ROWS == frames
    total_rows = lyric_local * count
    if hops:
        run = ((0, lyric_local, lyric_local), (2 * lyric_local, 3 * lyric_local, lyric_local))
        groups = (run,) * 4
        owners = [chip, chip ^ 2, chip ^ 1, chip ^ 3]
        first_rows = []
        for owner in owners:
            first_rows += [
                (2 * owner + core) * lyric_local,
                (2 * owner + 1 - core) * lyric_local,
            ]
    else:
        gathered = jnp.concatenate(
            [
                lax.all_gather(
                    norm_rows(gains, lyric_keys[0]), "seq", axis=0, tiled=True
                ),
                lax.all_gather(lyric_values[0], "seq", axis=0, tiled=True),
            ],
            axis=0,
        )
        groups = (((0, total_rows, total_rows),),)
        first_rows = [0]
    has_left, has_right = chip > 0, chip < chips - 1
    has_near = jnp.where(core == 0, has_left, has_right)
    has_far = jnp.where(core == 0, has_right, has_left)
    meta = jnp.stack(
        [
            jnp.asarray(value, jnp.int32)
            for value in [core, touching]
            + [alignment[0, 0, slot] for slot in range(TILES)]
            + [lyric_len[0], has_near, has_far]
            + first_rows
        ]
    )

    to_mate = pack(
        state,
        alignment[0, 0],
        [queries[0], cotangent[0], keys[0], values[0]]
        + ([lyric_keys[0], lyric_values[0]] if hops else []),
    )
    mate = lax.ppermute(to_mate, "seq", swap)
    if hops:
        pair = pair_lyrics(state, gains, lyric_keys[0], lyric_values[0], mate)
        two = hop(pair, across)
        lyrics = [pair, two, hop(two, partners)]
        lead, after = [pair], [two]
    else:
        lyrics, lead, after = [gathered], [], []
    one = hop(edge(state, 1, gains, keys[0], values[0], mate, lead, []), partners)
    mid = hop(edge(state, 0, gains, keys[0], values[0], mate, [], after), between)
    key_low = prepare_keys(state, gains, keys[0], mate, after)
    output, grad_queries, for_mate, key_grad, value_grad, to_one, to_mid, gain_part, *parts = (
        attention(
            meta, gains, queries[0], cotangent[0], values[0], key_low, mate, one, mid, lyrics,
            groups,
        )
    )

    to_mate = []
    mid = hop(to_mid, between)
    if hops:
        held, for_two, to_two = parts
        gain_total = sum_over(sum_over(gain_part, "song", bits_of(songs)), "seq", [2])
        to_two, to_one = relay(for_two, hop(to_two, partners), gain_total, to_one)
        two, one = hop(to_two, across), hop(to_one, partners)
        own_half, part_to_mate, gain_total = finish_lyric(
            state, gains, lyric_keys[0], mate, held, one, two, gain_total, frames
        )
        to_mate = [part_to_mate]
    else:
        one = hop(to_one, partners)
    *filled, to_mate = finish_audio(
        state, gains, keys[0], mate, key_grad, value_grad, one, mid, for_mate,
        [output, grad_queries], to_mate,
    )
    from_mate = lax.ppermute(to_mate, "seq", swap)
    if hops:
        *filled, grad_lyric_keys, grad_lyric_values, q_total, k_total = join(
            state, gain_total, filled, own_half, from_mate
        )
    else:
        filled = fill_other(state, filled, from_mate)
        gain_total = lax.psum(gain_part, ("song", "seq"))
        q_total, k_total = gain_total[0:1], gain_total[1:2]
        spread = lax.dynamic_update_slice(
            jnp.zeros((2 * total_rows, width), jnp.float32),
            parts[0].astype(jnp.float32),
            (0, core * (width // 2)),
        )
        lyric_key_sum, grad_lyric_values = [
            lax.psum_scatter(part, "seq", scatter_dimension=0, tiled=True)
            for part in (spread[:total_rows], spread[total_rows:])
        ]
        grad_lyric_keys = norm_lyric(gains, lyric_keys[0], lyric_key_sum)
        grad_lyric_values = grad_lyric_values.astype(jnp.bfloat16)
    output, grad_queries, grad_keys, grad_values = filled
    return (
        output[None],
        grad_queries[None],
        grad_keys[None],
        grad_values[None],
        grad_lyric_keys[None],
        grad_lyric_values[None],
        q_total[0],
        k_total[0],
    )


def solution(mesh):
    split = P("song", "seq", None)
    return jax.shard_map(
        body,
        mesh=mesh,
        in_specs=(split, split, split, split, split, P(), P(), split, split, P("song")),
        out_specs=(split, split, split, split, split, split, P(), P()),
        check_vma=False,
    )
```

time: 123 us -> 121 us (0.984)
  local copies, waits for them, and re-layouts: 4.08 us -> 8.68 us
  Pallas kernels: 26.8 us -> 22.4 us
  waiting for transfers between devices: 70.5 us -> 68.5 us
    unnamed x20 -> x32, local copies, waits for them, and re-layouts: 2.11 us -> 6.72 us
    pallas_call x9 -> x10, Pallas kernels: 26.8 us -> 22.4 us  [the longest x1 11.2 us: attention(): call(functools.partial(attention_kernel, groups, head_size, head_size **...]
    ppermute x8, waiting for transfers between devices: 58.8 us -> 57.1 us  [hop(): return lax.ppermute(block, 'seq', pairs)]
  transfers between devices with their start and end apart: 13 -> 13, of which waited for: 8 -> 8; matrix products, arithmetic and copies ran while one was open for 2% -> 2% of each run, Pallas kernels for 3% -> 4%
where the time goes in v7:
time: 121 us
  waiting for transfers between devices  68.5 us (57%)
  Pallas kernels  22.4 us (19%)
  starting transfers between devices  19.6 us (16%)
  local copies, waits for them, and re-layouts  8.68 us (7%)
  between operations  1.5 us (1%)
    ppermute x8, waiting for transfers between devices, hop(): return lax.ppermute(block, 'seq', pairs)  57.1 us
    ppermute x8, starting transfers between devices, hop(): return lax.ppermute(block, 'seq', pairs)  13.8 us
    pallas_call x1, Pallas kernels, attention(): call(functools.partial(attention_kernel, groups, head_size, head_size **...  11.2 us
    unnamed x32, local copies, waits for them, and re-layouts  6.72 us
    ppermute x3, waiting for transfers between devices, sum_over(): lax.ppermute(total, axis, [(i, i ^ bit) for i in range(count)])  5.76 us
    ppermute x3, starting transfers between devices, sum_over(): lax.ppermute(total, axis, [(i, i ^ bit) for i in range(count)])  5.12 us
    pallas_call x2, Pallas kernels, edge(): call(functools.partial(edge_kernel, touching, bool(lead)), 'edge', [SMEM]...  3.29 us
    ppermute x1, waiting for transfers between devices, body(): from_mate = lax.ppermute(to_mate, 'seq', swap)  3.02 us
  transfers between devices with their start and end apart: 13, of which 8 were waited for; matrix products, arithmetic and copies ran while one was open for 2% of the time, Pallas kernels for 4%

profile of v7, /device:TPU:0, one launch (start us, length us, event | category | flops | bytes accessed | tf_op | source)
XLA Modules:
  0.0 120.7 jit_solution(16931704538213864592)
XLA Ops:
  0.7 0.1 pad_add_fusion.state_ref
  0.7 0.0 copy-start
  0.7 1.0 copy-done
  1.8 0.0 copy-start.2
  1.8 1.0 copy-done.2
  2.8 0.0 copy-start.4
  2.8 0.9 copy-done.4
  3.8 0.0 copy-start.6
  3.8 0.9 copy-done.6
  4.7 0.0 copy-start.8
  4.7 1.0 copy-done.8
  5.7 1.0 copy-done.10
  6.8 0.7 copy-done.12
  7.4 0.8 pack.1
  8.2 0.0 copy-start.1
  8.2 0.0 copy-start.3
  8.2 0.5 collective-permute-start
  8.8 0.0 copy-done.14
  8.8 0.0 copy-done.15
  8.8 2.6 %collective-permute-done.mate_ref = bf16[640,1024]{1,0:T(8,128)(2,1)S(1)} collective-permute-done((bf16[640,1024]{1,0:T(8,128)(2,1)S(1)}, bf16[640,1024]{1,0:T(8,128)(2,1)S(1)}, u32[]{:S(2)}, u32[]{:S(2)}) %collective-permute-start) | collective-permute-done | bytes 1310752 | tf_op jit(solution)/shard_map/ppermute | solution.py:698
  11.4 0.0 copy-done.5
  11.4 0.0 copy-done.7
  11.4 0.7 pair_lyrics.1.refs_0_
  12.2 4.0 %collective-permute-start.1 = (bf16[192,1024]{1,0:T(8,128)(2,1)S(1)}, bf16[192,1024]{1,0:T(8,128)(2,1)S(1)}, u32[]{:S(2)}, u32[]{:S(2)}) collective-permute-start(bf16[192,1024]{1,0:T(8,128)(2,1)S(1)} %pair_lyrics.1.refs_0_), channel_id=1, source_target_pairs={{0,4},{1,5},{2,6},{3,7},{4,0},{5,1},{6,2},{7,3},{8,12},{9,13},{10,... | collective-permute-start | bytes 1179656 | tf_op jit(solution)/shard_map/ppermute | solution.py:653
  16.2 0.0 copy-done.1
  16.2 0.0 copy-done.3
  16.2 1.7 %edge.2 = bf16[448,1024]{1,0:T(8,128)(2,1)} custom-call(s32[2]{0:T(128)S(1)} %pad_add_fusion.state_ref, f32[2,128]{1,0:T(2,128)S(1)} %pad_maximum_fusion.gain_ref, bf16[128,2048]{1,0:T(8,128)(2,1)S(1)} %bitcast.32, bf16[128,2048]{1,0:T(8,128)(2,1)S(1)} %bitcast.37, bf16[640,1024]{1,0:T(8,128)(2,1)S(1)} %collective-permute-done.mate_ref, ...), custom_call_target="tpu_custom_call" | custom-call | flops 1 | bytes 1 | tf_op jit(solution)/shard_map/edge/pallas_call | solution.py:162
  17.9 1.6 %collective-permute-start.2 = (bf16[448,1024]{1,0:T(8,128)(2,1)}, bf16[448,1024]{1,0:T(8,128)(2,1)}, u32[]{:S(2)}, u32[]{:S(2)}) collective-permute-start(bf16[448,1024]{1,0:T(8,128)(2,1)} %edge.2), channel_id=1, source_target_pairs={{0,2},{1,3},{2,0},{3,1},{4,6},{5,7},{6,4},{7,5},{8,10},{9,11},{10,... | collective-permute-start | bytes 2752520 | tf_op jit(solution)/shard_map/ppermute | solution.py:653
  19.5 14.6 %collective-permute-done.1.refs_0_.refs_1_ = bf16[192,1024]{1,0:T(8,128)(2,1)S(1)} collective-permute-done((bf16[192,1024]{1,0:T(8,128)(2,1)S(1)}, bf16[192,1024]{1,0:T(8,128)(2,1)S(1)}, u32[]{:S(2)}, u32[]{:S(2)}) %collective-permute-start.1) | collective-permute-done | bytes 393248 | tf_op jit(solution)/shard_map/ppermute | solution.py:653
  34.1 1.6 %edge.3 = bf16[256,1024]{1,0:T(8,128)(2,1)} custom-call(s32[2]{0:T(128)S(1)} %pad_add_fusion.state_ref, f32[2,128]{1,0:T(2,128)S(1)} %pad_maximum_fusion.gain_ref, bf16[128,2048]{1,0:T(8,128)(2,1)S(1)} %bitcast.33, bf16[128,2048]{1,0:T(8,128)(2,1)S(1)} %bitcast.38, bf16[640,1024]{1,0:T(8,128)(2,1)S(1)} %collective-permute-done.mate_ref, ...), custom_call_target="tpu_custom_call" | custom-call | flops 1 | bytes 1 | tf_op jit(solution)/shard_map/edge/pallas_call | solution.py:162
  35.7 1.5 %collective-permute-start.3 = (bf16[256,1024]{1,0:T(8,128)(2,1)}, bf16[256,1024]{1,0:T(8,128)(2,1)}, u32[]{:S(2)}, u32[]{:S(2)}) collective-permute-start(bf16[256,1024]{1,0:T(8,128)(2,1)} %edge.3), channel_id=1, source_target_pairs={{2,4},{3,5},{4,2},{5,3},{10,12},{11,13},{12,10},{13,11},{18,20},{1... | collective-permute-start | bytes 1572872 | tf_op jit(solution)/shard_map/ppermute | solution.py:653
  37.2 1.2 collective-permute-start.4
  39.0 0.0 copy-done.13
  39.0 0.6 fusion
  39.6 1.4 %stack.77.meta_ref = s32[15]{0:T(128)S(1)} concatenate(s32[1]{0:T(128)} %bitcast, s32[1]{0:T(128)} %bitcast.1, s32[1]{0:T(128)} %bitcast.11, s32[1]{0:T(128)} %bitcast.12, s32[1]{0:T(128)S(6)} %copy.30, s32[1]{0:T(128)} %bitcast.13, s32[1]{0:T(128)} %bitcast.14, s32[1]{0:T(128)} %bitcast.15, s32[1]{0:T(128)} %bitcast.16, s32[1]{0:T(128)} %bitcast.17, s32[1]{0:T(128)} %bitcast.18, ...), dimensions={0} | concatenate | bytes 120 | tf_op jit(solution)/shard_map/stack | solution.py:682
  41.0 0.0 copy-start.9
  41.0 0.0 copy-start.11
  41.0 0.9 prepare_keys.1.key_ref
  41.9 14.1 %collective-permute-done.4.refs_2_ = bf16[192,1024]{1,0:T(8,128)(2,1)} collective-permute-done((bf16[192,1024]{1,0:T(8,128)(2,1)S(1)}, bf16[192,1024]{1,0:T(8,128)(2,1)}, u32[]{:S(2)}, u32[]{:S(2)}) %collective-permute-start.4) | collective-permute-done | bytes 393248 | tf_op jit(solution)/shard_map/ppermute | solution.py:653
  56.0 0.0 collective-permute-done.2.one_ref
  56.0 0.0 collective-permute-done.3.mid_ref
  56.0 0.0 copy-done.9
  56.0 0.0 copy-done.11
  56.1 11.2 %attention.1 = (bf16[128,1024]{1,0:T(8,128)(2,1)S(1)}, bf16[128,1024]{1,0:T(8,128)(2,1)S(1)}, bf16[256,1024]{1,0:T(8,128)(2,1)S(1)}, f32[256,1024]{1,0:T(8,128)S...) custom-call(s32[15]{0:T(128)S(1)} %stack.77.meta_ref, ...), custom_call_target="tpu_custom_call" | custom-call | flops 2415919104 | bytes 16777216 | tf_op jit(solution)/shard_map/attention/pallas_call | solution.py:378
  67.3 0.1 collective-permute-start.5
  67.3 1.6 %collective-permute-start.6 = (f32[8,128]{1,0:T(8,128)S(1)}, f32[8,128]{1,0:T(8,128)S(1)}, u32[]{:S(2)}, u32[]{:S(2)}) collective-permute-start(f32[8,128]{1,0:T(8,128)S(1)} %get-tuple-element.40), channel_id=1, source_target_pairs={{0,8},{8,0},{16,24},{24,16},{1,9},{9,1},{17,25},{25,17},{2,10},{10... | collective-permute-start | bytes 12296 | tf_op jit(solution)/shard_map/ppermute | solution.py:622
  68.9 2.1 %collective-permute-done.6 = f32[8,128]{1,0:T(8,128)S(1)} collective-permute-done((f32[8,128]{1,0:T(8,128)S(1)}, f32[8,128]{1,0:T(8,128)S(1)}, u32[]{:S(2)}, u32[]{:S(2)}) %collective-permute-start.6) | collective-permute-done | bytes 4128 | tf_op jit(solution)/shard_map/ppermute | solution.py:622
  71.0 1.6 %collective-permute-start.7 = (f32[8,128]{1,0:T(8,128)S(1)}, f32[8,128]{1,0:T(8,128)S(1)}, u32[]{:S(2)}, u32[]{:S(2)}) collective-permute-start(f32[8,128]{1,0:T(8,128)S(1)} %add.51), channel_id=1, source_target_pairs={{0,16},{8,24},{16,0},{24,8},{1,17},{9,25},{17,1},{25,9},{2,18},{10... | collective-permute-start | bytes 12296 | tf_op jit(solution)/shard_map/ppermute | solution.py:622
  72.6 2.0 %collective-permute-done.7 = f32[8,128]{1,0:T(8,128)S(1)} collective-permute-done((f32[8,128]{1,0:T(8,128)S(1)}, f32[8,128]{1,0:T(8,128)S(1)}, u32[]{:S(2)}, u32[]{:S(2)}) %collective-permute-start.7) | collective-permute-done | bytes 4128 | tf_op jit(solution)/shard_map/ppermute | solution.py:622
  74.6 1.9 %collective-permute-start.8 = (f32[8,128]{1,0:T(8,128)S(1)}, f32[8,128]{1,0:T(8,128)S(1)}, u32[]{:S(2)}, u32[]{:S(2)}) collective-permute-start(f32[8,128]{1,0:T(8,128)S(1)} %add.52), channel_id=1, source_target_pairs={{0,2},{1,3},{2,0},{3,1},{4,6},{5,7},{6,4},{7,5},{8,10},{9,11},{10,... | collective-permute-start | bytes 12296 | tf_op jit(solution)/shard_map/ppermute | solution.py:622
  76.6 1.7 %collective-permute-done.8 = f32[8,128]{1,0:T(8,128)S(1)} collective-permute-done((f32[8,128]{1,0:T(8,128)S(1)}, f32[8,128]{1,0:T(8,128)S(1)}, u32[]{:S(2)}, u32[]{:S(2)}) %collective-permute-start.8) | collective-permute-done | bytes 4128 | tf_op jit(solution)/shard_map/ppermute | solution.py:622
  78.2 0.0 collective-permute-done.5.arrived_ref
  78.2 0.1 relay.1
  78.3 2.1 %collective-permute-start.9 = (bf16[448,1024]{1,0:T(8,128)(2,1)S(1)}, bf16[448,1024]{1,0:T(8,128)(2,1)S(1)}, u32[]{:S(2)}, u32[]{:S(2)}) collective-permute-start(bf16[448,1024]{1,0:T(8,128)(2,1)S(1)} %get-tuple-element.42), channel_id=1, source_target_pairs={{0,2},{1,3},{2,0},{3,1},{4,6},{5,7},{6,4},{7,5},{8,10},{9,11},{10,... | collective-permute-start | bytes 2752520 | tf_op jit(solution)/shard_map/ppermute | solution.py:653
  80.4 0.7 collective-permute-start.11
  81.1 2.8 %collective-permute-start.10 = (bf16[224,1024]{1,0:T(8,128)(2,1)S(1)}, bf16[224,1024]{1,0:T(8,128)(2,1)S(1)}, u32[]{:S(2)}, u32[]{:S(2)}) collective-permute-start(bf16[224,1024]{1,0:T(8,128)(2,1)S(1)} %get-tuple-element.43), channel_id=1, source_target_pairs={{0,4},{1,5},{2,6},{3,7},{4,0},{5,1},{6,2},{7,3},{8,12},{9,13},{10,... | collective-permute-start | bytes 1376264 | tf_op jit(solution)/shard_map/ppermute | solution.py:653
  83.9 28.3 %collective-permute-done.10.two_ref = bf16[224,1024]{1,0:T(8,128)(2,1)S(1)} collective-permute-done((bf16[224,1024]{1,0:T(8,128)(2,1)S(1)}, bf16[224,1024]{1,0:T(8,128)(2,1)S(1)}, u32[]{:S(2)}, u32[]{:S(2)}) %collective-permute-start.10) | collective-permute-done | bytes 458784 | tf_op jit(solution)/shard_map/ppermute | solution.py:653
  112.2 0.0 collective-permute-done.9.one_ref
  112.2 0.9 finish_lyric.1
  113.1 0.0 collective-permute-done.11.mid_ref
  113.1 2.2 %finish_audio.1 = (bf16[128,2048]{1,0:T(8,128)(2,1)}, bf16[128,2048]{1,0:T(8,128)(2,1)}, bf16[128,2048]{1,0:T(8,128)(2,1)}, bf16[128,2048]{1,0:T(8,128)(2,1)}, bf16[640,1024]{1,0:T(8,128)(2,1)S(1)}) custom-call(s32[2]{0:T(128)S(1)} %pad_add_fusion.state_ref, f32[2,128]{1,0:T(2,128)S(1)} %pad_maximum_fusion.gain_ref, ...), custom_call_target="tpu_custom_call", output_to_operand_aliasing={{4}: (11, {})} | custom-call | flops 1 | bytes 1 | tf_op jit(solution)/shard_map/finish_audio/pallas_call | solution.py:443
  115.4 0.1 collective-permute-start.12
  115.5 3.0 %collective-permute-done.12.mate_ref = bf16[640,1024]{1,0:T(8,128)(2,1)S(1)} collective-permute-done((bf16[640,1024]{1,0:T(8,128)(2,1)S(1)}, bf16[640,1024]{1,0:T(8,128)(2,1)S(1)}, u32[]{:S(2)}, u32[]{:S(2)}) %collective-permute-start.12) | collective-permute-done | bytes 1310752 | tf_op jit(solution)/shard_map/ppermute | solution.py:733
  118.5 2.2 %join.1 = (bf16[128,2048]{1,0:T(8,128)(2,1)}, bf16[128,2048]{1,0:T(8,128)(2,1)}, bf16[128,2048]{1,0:T(8,128)(2,1)}, bf16[128,2048]{1,0:T(8,128)(2,1)}, bf16[48,2...) custom-call(s32[2]{0:T(128)S(1)} %pad_add_fusion.state_ref, ...), custom_call_target="tpu_custom_call", output_to_operand_aliasing={{0}: (4, {}), {1}: (5, {}), {2}: (6, {}), {3}: (7, {})} | custom-call | flops 1 | bytes 1 | tf_op jit(solution)/shard_map/join/pallas_call | solution.py:550
  (11 shorter events, 0.0 us)
Async XLA Ops:
  0.7 1.0 copy-start
  1.8 1.0 copy-start.2
  2.8 0.9 copy-start.4
  3.8 0.9 copy-start.6
  4.7 1.0 copy-start.8
  5.7 1.0 copy-start.10
  6.8 0.7 copy-start.12
  7.4 1.3 %copy-start.14 = (f32[128]{0:T(128)S(1)}, f32[128]{0:T(128)}, u32[]{:S(2)}) copy-start(f32[128]{0:T(128)} %param.16) | copy-start | bytes 1540
  7.4 1.3 %copy-start.15 = (f32[128]{0:T(128)S(1)}, f32[128]{0:T(128)}, u32[]{:S(2)}) copy-start(f32[128]{0:T(128)} %param.15) | copy-start | bytes 1540
  7.4 4.0 %copy-start.5 = (bf16[1,48,2048]{2,1,0:T(8,128)(2,1)S(1)}, bf16[1,48,2048]{2,1,0:T(8,128)(2,1)}, u32[]{:S(2)}) copy-start(bf16[1,48,2048]{2,1,0:T(8,128)(2,1)} %param.13) | copy-start | bytes 589828
  7.4 4.0 %copy-start.7 = (bf16[1,48,2048]{2,1,0:T(8,128)(2,1)S(1)}, bf16[1,48,2048]{2,1,0:T(8,128)(2,1)}, u32[]{:S(2)}) copy-start(bf16[1,48,2048]{2,1,0:T(8,128)(2,1)} %param.14) | copy-start | bytes 589828
  8.2 8.0 %copy-start.1 = (bf16[1,128,2048]{2,1,0:T(8,128)(2,1)S(1)}, bf16[1,128,2048]{2,1,0:T(8,128)(2,1)}, u32[]{:S(2)}) copy-start(bf16[1,128,2048]{2,1,0:T(8,128)(2,1)} %param.11) | copy-start | bytes 1572868
  8.2 8.0 %copy-start.3 = (bf16[1,128,2048]{2,1,0:T(8,128)(2,1)S(1)}, bf16[1,128,2048]{2,1,0:T(8,128)(2,1)}, u32[]{:S(2)}) copy-start(bf16[1,128,2048]{2,1,0:T(8,128)(2,1)} %param.12) | copy-start | bytes 1572868
  8.2 3.2 %collective-permute-start = (bf16[640,1024]{1,0:T(8,128)(2,1)S(1)}, bf16[640,1024]{1,0:T(8,128)(2,1)S(1)}, u32[]{:S(2)}, u32[]{:S(2)}) collective-permute-start(bf16[640,1024]{1,0:T(8,128)(2,1)S(1)} %pack.1), channel_id=1, source_target_pairs={{0,1},{1,0},{2,3},{3,2},{4,5},{5,4},{6,7},{7,6},{8,9},{9,8},{10,11... | collective-permute-start | bytes 3932168 | tf_op jit(solution)/shard_map/ppermute | solution.py:698
  12.2 22.0 %collective-permute-start.1 = (bf16[192,1024]{1,0:T(8,128)(2,1)S(1)}, bf16[192,1024]{1,0:T(8,128)(2,1)S(1)}, u32[]{:S(2)}, u32[]{:S(2)}) collective-permute-start(bf16[192,1024]{1,0:T(8,128)(2,1)S(1)} %pair_lyrics.1.refs_0_), channel_id=1, source_target_pairs={{0,4},{1,5},{2,6},{3,7},{4,0},{5,1},{6,2},{7,3},{8,12},{9,13},{10,... | collective-permute-start | bytes 1179656 | tf_op jit(solution)/shard_map/ppermute | solution.py:653
  17.9 21.1 %copy-start.13 = (s32[1,1,2]{2,1,0:T(1,128)S(1)}, s32[1,1,2]{2,1,0:T(1,128)}, u32[]{:S(2)}) copy-start(s32[1,1,2]{2,1,0:T(1,128)} %param.18) | copy-start | bytes 28
  17.9 38.1 %collective-permute-start.2 = (bf16[448,1024]{1,0:T(8,128)(2,1)}, bf16[448,1024]{1,0:T(8,128)(2,1)}, u32[]{:S(2)}, u32[]{:S(2)}) collective-permute-start(bf16[448,1024]{1,0:T(8,128)(2,1)} %edge.2), channel_id=1, source_target_pairs={{0,2},{1,3},{2,0},{3,1},{4,6},{5,7},{6,4},{7,5},{8,10},{9,11},{10,... | collective-permute-start | bytes 2752520 | tf_op jit(solution)/shard_map/ppermute | solution.py:653
  35.7 20.3 %collective-permute-start.3 = (bf16[256,1024]{1,0:T(8,128)(2,1)}, bf16[256,1024]{1,0:T(8,128)(2,1)}, u32[]{:S(2)}, u32[]{:S(2)}) collective-permute-start(bf16[256,1024]{1,0:T(8,128)(2,1)} %edge.3), channel_id=1, source_target_pairs={{2,4},{3,5},{4,2},{5,3},{10,12},{11,13},{12,10},{13,11},{18,20},{1... | collective-permute-start | bytes 1572872 | tf_op jit(solution)/shard_map/ppermute | solution.py:653
  37.2 18.9 %collective-permute-start.4 = (bf16[192,1024]{1,0:T(8,128)(2,1)S(1)}, bf16[192,1024]{1,0:T(8,128)(2,1)}, u32[]{:S(2)}, u32[]{:S(2)}) collective-permute-start(bf16[192,1024]{1,0:T(8,128)(2,1)S(1)} %collective-permute-done.1.refs_0_.refs_1_), channel_id=1, source_target_pairs={{0,2},{1,3},{2,0},{3,1},{4,6},{5,7},{6,4},{7,5},{8,10},{9,11},{10,... | collective-permute-start | bytes 1179656 | tf_op jit(solution)/shard_map/ppermute | solution.py:653
  41.0 15.1 %copy-start.9 = (bf16[1,128,2048]{2,1,0:T(8,128)(2,1)S(1)}, bf16[1,128,2048]{2,1,0:T(8,128)(2,1)}, u32[]{:S(2)}) copy-start(bf16[1,128,2048]{2,1,0:T(8,128)(2,1)} %param.10) | copy-start | bytes 1572868
  41.0 15.0 %copy-start.11 = (bf16[1,128,2048]{2,1,0:T(8,128)(2,1)S(1)}, bf16[1,128,2048]{2,1,0:T(8,128)(2,1)}, u32[]{:S(2)}) copy-start(bf16[1,128,2048]{2,1,0:T(8,128)(2,1)} %param.17) | copy-start | bytes 1572868
  67.3 11.0 %collective-permute-start.5 = (bf16[192,1024]{1,0:T(8,128)(2,1)S(1)}, bf16[192,1024]{1,0:T(8,128)(2,1)S(1)}, u32[]{:S(2)}, u32[]{:S(2)}) collective-permute-start(bf16[192,1024]{1,0:T(8,128)(2,1)S(1)} %get-tuple-element.39), channel_id=1, source_target_pairs={{0,2},{1,3},{2,0},{3,1},{4,6},{5,7},{6,4},{7,5},{8,10},{9,11},{10,... | collective-permute-start | bytes 1179656 | tf_op jit(solution)/shard_map/ppermute | solution.py:653
  67.3 3.7 %collective-permute-start.6 = (f32[8,128]{1,0:T(8,128)S(1)}, f32[8,128]{1,0:T(8,128)S(1)}, u32[]{:S(2)}, u32[]{:S(2)}) collective-permute-start(f32[8,128]{1,0:T(8,128)S(1)} %get-tuple-element.40), channel_id=1, source_target_pairs={{0,8},{8,0},{16,24},{24,16},{1,9},{9,1},{17,25},{25,17},{2,10},{10... | collective-permute-start | bytes 12296 | tf_op jit(solution)/shard_map/ppermute | solution.py:622
  71.0 3.6 %collective-permute-start.7 = (f32[8,128]{1,0:T(8,128)S(1)}, f32[8,128]{1,0:T(8,128)S(1)}, u32[]{:S(2)}, u32[]{:S(2)}) collective-permute-start(f32[8,128]{1,0:T(8,128)S(1)} %add.51), channel_id=1, source_target_pairs={{0,16},{8,24},{16,0},{24,8},{1,17},{9,25},{17,1},{25,9},{2,18},{10... | collective-permute-start | bytes 12296 | tf_op jit(solution)/shard_map/ppermute | solution.py:622
  74.6 3.6 %collective-permute-start.8 = (f32[8,128]{1,0:T(8,128)S(1)}, f32[8,128]{1,0:T(8,128)S(1)}, u32[]{:S(2)}, u32[]{:S(2)}) collective-permute-start(f32[8,128]{1,0:T(8,128)S(1)} %add.52), channel_id=1, source_target_pairs={{0,2},{1,3},{2,0},{3,1},{4,6},{5,7},{6,4},{7,5},{8,10},{9,11},{10,... | collective-permute-start | bytes 12296 | tf_op jit(solution)/shard_map/ppermute | solution.py:622
  78.3 33.9 %collective-permute-start.9 = (bf16[448,1024]{1,0:T(8,128)(2,1)S(1)}, bf16[448,1024]{1,0:T(8,128)(2,1)S(1)}, u32[]{:S(2)}, u32[]{:S(2)}) collective-permute-start(bf16[448,1024]{1,0:T(8,128)(2,1)S(1)} %get-tuple-element.42), channel_id=1, source_target_pairs={{0,2},{1,3},{2,0},{3,1},{4,6},{5,7},{6,4},{7,5},{8,10},{9,11},{10,... | collective-permute-start | bytes 2752520 | tf_op jit(solution)/shard_map/ppermute | solution.py:653
  80.4 32.7 %collective-permute-start.11 = (bf16[256,1024]{1,0:T(8,128)(2,1)S(1)}, bf16[256,1024]{1,0:T(8,128)(2,1)S(1)}, u32[]{:S(2)}, u32[]{:S(2)}) collective-permute-start(bf16[256,1024]{1,0:T(8,128)(2,1)S(1)} %get-tuple-element.48), channel_id=1, source_target_pairs={{2,4},{3,5},{4,2},{5,3},{10,12},{11,13},{12,10},{13,11},{18,20},{1... | collective-permute-start | bytes 1572872 | tf_op jit(solution)/shard_map/ppermute | solution.py:653
  81.1 31.1 %collective-permute-start.10 = (bf16[224,1024]{1,0:T(8,128)(2,1)S(1)}, bf16[224,1024]{1,0:T(8,128)(2,1)S(1)}, u32[]{:S(2)}, u32[]{:S(2)}) collective-permute-start(bf16[224,1024]{1,0:T(8,128)(2,1)S(1)} %get-tuple-element.43), channel_id=1, source_target_pairs={{0,4},{1,5},{2,6},{3,7},{4,0},{5,1},{6,2},{7,3},{8,12},{9,13},{10,... | collective-permute-start | bytes 1376264 | tf_op jit(solution)/shard_map/ppermute | solution.py:653
  115.4 3.1 %collective-permute-start.12 = (bf16[640,1024]{1,0:T(8,128)(2,1)S(1)}, bf16[640,1024]{1,0:T(8,128)(2,1)S(1)}, u32[]{:S(2)}, u32[]{:S(2)}) collective-permute-start(bf16[640,1024]{1,0:T(8,128)(2,1)S(1)} %get-tuple-element.53), channel_id=1, source_target_pairs={{0,1},{1,0},{2,3},{3,2},{4,5},{5,4},{6,7},{7,6},{8,9},{9,8},{10,11... | collective-permute-start | bytes 3932168 | tf_op jit(solution)/shard_map/ppermute | solution.py:733

commit v8 on v7

--- a/solution.py
+++ b/solution.py
@@ -17,7 +17,8 @@
 SMEM = pl.BlockSpec(memory_space=pltpu.SMEM)
 HBM = pl.BlockSpec(memory_space=pltpu.HBM)
 ANY = pl.BlockSpec(memory_space=pl.ANY)
-GAIN_ROWS = 32
+GAIN_ROWS = 16
+HEADS_PER_STEP = 2
 ALIGN_ROWS = 32
 SMALL = pl.CostEstimate(flops=1, bytes_accessed=1, transcendentals=0)
 
@@ -50,17 +51,19 @@
     return pl.ds(pl.multiple_of(core * half, half), half)
 
 
-def split_rows(sums):
+def split_rows(sums, cols):
     high = sums.astype(jnp.bfloat16).astype(jnp.float32)
     rest = sums - high
     middle = rest.astype(jnp.bfloat16).astype(jnp.float32)
     low = rest - middle
-    return jnp.concatenate([high, middle, low, jnp.zeros_like(high)], axis=0).astype(jnp.bfloat16)
-
-
-def joined_rows(rows):
-    rows = rows.astype(jnp.float32)
-    return (rows[16:24] + rows[8:16]) + rows[0:8]
+    empty = jnp.zeros((sums.shape[0], cols - 3 * sums.shape[1]), jnp.float32)
+    rows = jnp.concatenate([high, middle, low, empty], axis=1)
+    return jnp.concatenate([rows, jnp.zeros_like(rows)], axis=0).astype(jnp.bfloat16)
+
+
+def joined_rows(rows, size):
+    rows = rows.astype(jnp.float32)[0:8]
+    return (rows[:, 2 * size : 3 * size] + rows[:, size : 2 * size]) + rows[:, 0:size]
 
 
 def normed(raw, k_gain):
@@ -118,6 +121,7 @@
         [SMEM, SMEM] + [HBM] * len(arrays),
         VMEM,
         shape(rows, arrays[0].shape[1] // 2),
+        limit=PACK_VMEM_LIMIT,
         scratch_shapes=[pltpu.SemaphoreType.DMA((len(arrays),))],
     )(state, align, *arrays)
 
@@ -236,8 +240,7 @@
     k_gain = gain_ref[1:2, :]
     heads = key_ref.shape[1] // head_size
 
-    @pl.loop(0, heads)
-    def _(head):
+    def one_head(head):
         cols = pl.ds(pl.multiple_of(head * head_size, head_size), head_size)
         own_cols = pl.ds(
             pl.multiple_of((meta_ref[0] * heads + head) * head_size, head_size), head_size
@@ -362,6 +365,11 @@
             )
             start += rows
 
+    @pl.loop(0, heads // HEADS_PER_STEP)
+    def _(step):
+        for number in range(HEADS_PER_STEP):
+            one_head(step * HEADS_PER_STEP + number)
+
 
 def attention(meta, gains, query, cot, value, key, mate, one, mid, lyrics, groups):
     frames, width = query.shape
@@ -445,26 +453,26 @@
         "finish_audio",
         [SMEM] + [VMEM] * (10 + len(to_mate)),
         [HBM] * 4 + [VMEM],
-        [shape(frames, width)] * 4 + [shape(5 * frames, half)],
+        [shape(frames, width)] * 4
+        + [shape(*array.shape) for array in to_mate or [shape(4 * frames, half)]],
         input_output_aliases={11: 4} if to_mate else {},
         scratch_shapes=[pltpu.VMEM((frames, half), jnp.bfloat16)] * 2
         + [pltpu.SemaphoreType.DMA((4,))],
     )(state, gains, raw, mate, key_grad, value_grad, one, mid, ready, *owns, *to_mate)
 
 
-def relay_kernel(head_size, part_ref, arrived_ref, total_ref, later_ref, out_ref, handed_ref):
+def relay_kernel(part_ref, arrived_ref, total_ref, later_ref, out_ref, handed_ref):
     rows = part_ref.shape[0]
     out_ref[0:rows, :] = (
         part_ref[...].astype(jnp.float32) + arrived_ref[...].astype(jnp.float32)
     ).astype(jnp.bfloat16)
-    out_ref[rows:, 0:head_size] = split_rows(total_ref[...])
-    out_ref[rows:, head_size:] = jnp.zeros_like(out_ref[rows:, head_size:])
+    out_ref[rows:, :] = split_rows(total_ref[...], out_ref.shape[1])
 
 
 def relay(part, arrived, total, later):
     rows, half = part.shape
     return call(
-        functools.partial(relay_kernel, total.shape[1]),
+        relay_kernel,
         "relay",
         [VMEM] * 3 + [ANY],
         [VMEM, ANY],
@@ -482,9 +490,8 @@
     k_gain = gain_ref[1:2, :]
     first = mate_ref.shape[0] - ALIGN_ROWS - 2 * rows
     end = to_mate_ref.shape[0] - GAIN_ROWS
-    total_ref[...] = sum_ref[...] + joined_rows(two_ref[4 * rows :, 0:head_size])
-    to_mate_ref[end:, 0:head_size] = split_rows(total_ref[...])
-    to_mate_ref[end:, head_size:] = jnp.zeros_like(to_mate_ref[end:, head_size:])
+    total_ref[...] = sum_ref[...] + joined_rows(two_ref[4 * rows :, :], head_size)
+    to_mate_ref[end:, :] = split_rows(total_ref[...], to_mate_ref.shape[1])
     raw_keys = raw_ref[:, half_of(raw_ref, state_ref[0])]
     for head in range(own_ref.shape[1] // head_size):
         cols = slice(head * head_size, (head + 1) * head_size)
@@ -536,8 +543,8 @@
     ]
     for copy in copies:
         copy.start()
-    sums = mate_ref[mate_ref.shape[0] - GAIN_ROWS :, 0 : gain_ref.shape[1]]
-    total = gain_ref[...] + joined_rows(sums)
+    sums = mate_ref[mate_ref.shape[0] - GAIN_ROWS :, :]
+    total = gain_ref[...] + joined_rows(sums, gain_ref.shape[1])
     q_total_ref[...] = total[0:1]
     k_total_ref[...] = total[1:2]
     for copy in copies:
@@ -652,7 +659,7 @@
         pairs = [(2 * a + c, 2 * b + c) for a, b in moves for c in (0, 1)]
         return lax.ppermute(block, "seq", pairs)
 
-    hops = chips == 4 and lyric_local % 16 == 0 and 2 * lyric_local + GAIN_ROWS == frames
+    hops = chips == 4 and lyric_local % 16 == 0
     total_rows = lyric_local * count
     if hops:
         run = ((0, lyric_local, lyric_local), (2 * lyric_local, 3 * lyric_local, lyric_local))

time: 121 us -> 115 us (0.950)
  local copies, waits for them, and re-layouts: 8.68 us -> 2.01 us
  Pallas kernels: 22.4 us -> 23.9 us
    unnamed x32 -> x20, local copies, waits for them, and re-layouts: 6.72 us -> 0.05 us
    pallas_call x1, Pallas kernels: 0.77 us -> 3.18 us  [pack(): call(pack_kernel, 'pack', [SMEM, SMEM] + [HBM] * len(arrays), VMEM, shape...]
    ppermute x8, waiting for transfers between devices: 57.1 us -> 55.7 us  [hop(): return lax.ppermute(block, 'seq', pairs)]
where the time goes in v8:
time: 115 us
  waiting for transfers between devices  67.3 us (59%)
  Pallas kernels  23.9 us (21%)
  starting transfers between devices  19.6 us (17%)
  local copies, waits for them, and re-layouts  2.01 us (2%)
  between operations  1.5 us (1%)
    ppermute x8, waiting for transfers between devices, hop(): return lax.ppermute(block, 'seq', pairs)  55.7 us
    ppermute x8, starting transfers between devices, hop(): return lax.ppermute(block, 'seq', pairs)  13.8 us
    pallas_call x1, Pallas kernels, attention(): call(functools.partial(attention_kernel, groups, head_size, head_size **...  10.3 us
    ppermute x3, waiting for transfers between devices, sum_over(): lax.ppermute(total, axis, [(i, i ^ bit) for i in range(count)])  5.76 us
    ppermute x3, starting transfers between devices, sum_over(): lax.ppermute(total, axis, [(i, i ^ bit) for i in range(count)])  5.12 us
    pallas_call x2, Pallas kernels, edge(): call(functools.partial(edge_kernel, touching, bool(lead)), 'edge', [SMEM]...  3.31 us
    pallas_call x1, Pallas kernels, pack(): call(pack_kernel, 'pack', [SMEM, SMEM] + [HBM] * len(arrays), VMEM, shape...  3.18 us
    ppermute x1, waiting for transfers between devices, body(): from_mate = lax.ppermute(to_mate, 'seq', swap)  2.97 us
  transfers between devices with their start and end apart: 13, of which 8 were waited for; matrix products, arithmetic and copies ran while one was open for 2% of the time, Pallas kernels for 4%

profile of v8, /device:TPU:0, one launch (start us, length us, event | category | flops | bytes accessed | tf_op | source)
XLA Modules:
  0.0 114.9 jit_solution(16584512351436075753)
XLA Ops:
  0.7 0.6 pad_add_fusion.state_ref
  1.3 0.0 copy-start.8
  1.3 0.0 copy-start.9
  1.3 0.0 copy-start.2
  1.3 0.0 copy-start.3
  1.3 0.0 copy-start.6
  1.3 3.2 %pack.1 = bf16[640,1024]{1,0:T(8,128)(2,1)} custom-call(s32[2]{0:T(128)} %pad_add_fusion.state_ref, s32[2]{0:T(128)} %bitcast.53, bf16[128,2048]{1,0:T(8,128)(2,1)} %bitcast.45, bf16[128,2048]{1,0:T(8,128)(2,1)} %bitcast.47, bf16[128,2048]{1,0:T(8,128)(2,1)} %bitcast.31, bf16[128,2048]{1,0:T(8,128)(2,1)} %bitcast.36, bf16[48,2048]{1,0:T(8,128)(2,1)} %bitcast.40, ...), custom_call_target="tpu_custom_call" | custom-call | flops 1 | bytes 1 | tf_op jit(solution)/shard_map/pack/pallas_call | solution.py:118
  4.5 0.0 copy-start
  4.5 0.0 copy-start.1
  4.5 0.5 collective-permute-start
  5.0 0.0 copy-done.8
  5.0 0.0 copy-done.9
  5.0 2.9 %collective-permute-done.mate_ref = bf16[640,1024]{1,0:T(8,128)(2,1)S(1)} collective-permute-done((bf16[640,1024]{1,0:T(8,128)(2,1)}, bf16[640,1024]{1,0:T(8,128)(2,1)S(1)}, u32[]{:S(2)}, u32[]{:S(2)}) %collective-permute-start) | collective-permute-done | bytes 1310752 | tf_op jit(solution)/shard_map/ppermute | solution.py:705
  7.9 0.0 copy-done.2
  7.9 0.0 copy-done.3
  7.9 0.0 copy-done.6
  7.9 0.7 pair_lyrics.1.refs_0_
  8.6 4.0 %collective-permute-start.1 = (bf16[192,1024]{1,0:T(8,128)(2,1)S(1)}, bf16[192,1024]{1,0:T(8,128)(2,1)S(1)}, u32[]{:S(2)}, u32[]{:S(2)}) collective-permute-start(bf16[192,1024]{1,0:T(8,128)(2,1)S(1)} %pair_lyrics.1.refs_0_), channel_id=1, source_target_pairs={{0,4},{1,5},{2,6},{3,7},{4,0},{5,1},{6,2},{7,3},{8,12},{9,13},{10,... | collective-permute-start | bytes 1179656 | tf_op jit(solution)/shard_map/ppermute | solution.py:660
  12.7 0.0 copy-done
  12.7 0.0 copy-done.1
  12.7 1.7 %edge.2 = bf16[448,1024]{1,0:T(8,128)(2,1)} custom-call(s32[2]{0:T(128)S(1)} %copy-done.6, f32[2,128]{1,0:T(2,128)S(1)} %pad_maximum_fusion.gain_ref, bf16[128,2048]{1,0:T(8,128)(2,1)S(1)} %bitcast.32, bf16[128,2048]{1,0:T(8,128)(2,1)S(1)} %bitcast.37, bf16[640,1024]{1,0:T(8,128)(2,1)S(1)} %collective-permute-done.mate_ref, ...), custom_call_target="tpu_custom_call" | custom-call | flops 1 | bytes 1 | tf_op jit(solution)/shard_map/edge/pallas_call | solution.py:166
  14.4 0.0 copy-start.7
  14.4 1.6 %collective-permute-start.2 = (bf16[448,1024]{1,0:T(8,128)(2,1)}, bf16[448,1024]{1,0:T(8,128)(2,1)}, u32[]{:S(2)}, u32[]{:S(2)}) collective-permute-start(bf16[448,1024]{1,0:T(8,128)(2,1)} %edge.2), channel_id=1, source_target_pairs={{0,2},{1,3},{2,0},{3,1},{4,6},{5,7},{6,4},{7,5},{8,10},{9,11},{10,... | collective-permute-start | bytes 2752520 | tf_op jit(solution)/shard_map/ppermute | solution.py:660
  16.0 14.6 %collective-permute-done.1.refs_0_.refs_1_ = bf16[192,1024]{1,0:T(8,128)(2,1)S(1)} collective-permute-done((bf16[192,1024]{1,0:T(8,128)(2,1)S(1)}, bf16[192,1024]{1,0:T(8,128)(2,1)S(1)}, u32[]{:S(2)}, u32[]{:S(2)}) %collective-permute-start.1) | collective-permute-done | bytes 393248 | tf_op jit(solution)/shard_map/ppermute | solution.py:660
  30.6 1.6 %edge.3 = bf16[256,1024]{1,0:T(8,128)(2,1)} custom-call(s32[2]{0:T(128)S(1)} %copy-done.6, f32[2,128]{1,0:T(2,128)S(1)} %pad_maximum_fusion.gain_ref, bf16[128,2048]{1,0:T(8,128)(2,1)S(1)} %bitcast.33, bf16[128,2048]{1,0:T(8,128)(2,1)S(1)} %bitcast.38, bf16[640,1024]{1,0:T(8,128)(2,1)S(1)} %collective-permute-done.mate_ref, ...), custom_call_target="tpu_custom_call" | custom-call | flops 1 | bytes 1 | tf_op jit(solution)/shard_map/edge/pallas_call | solution.py:166
  32.2 1.5 %collective-permute-start.3 = (bf16[256,1024]{1,0:T(8,128)(2,1)}, bf16[256,1024]{1,0:T(8,128)(2,1)}, u32[]{:S(2)}, u32[]{:S(2)}) collective-permute-start(bf16[256,1024]{1,0:T(8,128)(2,1)} %edge.3), channel_id=1, source_target_pairs={{2,4},{3,5},{4,2},{5,3},{10,12},{11,13},{12,10},{13,11},{18,20},{1... | collective-permute-start | bytes 1572872 | tf_op jit(solution)/shard_map/ppermute | solution.py:660
  33.6 1.2 %collective-permute-start.4 = (bf16[192,1024]{1,0:T(8,128)(2,1)S(1)}, bf16[192,1024]{1,0:T(8,128)(2,1)}, u32[]{:S(2)}, u32[]{:S(2)}) collective-permute-start(bf16[192,1024]{1,0:T(8,128)(2,1)S(1)} %collective-permute-done.1.refs_0_.refs_1_), channel_id=1, source_target_pairs={{0,2},{1,3},{2,0},{3,1},{4,6},{5,7},{6,4},{7,5},{8,10},{9,11},{10,... | collective-permute-start | bytes 1179656 | tf_op jit(solution)/shard_map/ppermute | solution.py:660
  35.5 0.0 copy-done.7
  35.5 0.6 fusion
  36.1 1.4 %stack.77.meta_ref = s32[15]{0:T(128)S(1)} concatenate(s32[1]{0:T(128)} %bitcast, s32[1]{0:T(128)} %bitcast.1, s32[1]{0:T(128)} %bitcast.11, s32[1]{0:T(128)} %bitcast.12, s32[1]{0:T(128)S(6)} %copy.30, s32[1]{0:T(128)} %bitcast.13, s32[1]{0:T(128)} %bitcast.14, s32[1]{0:T(128)} %bitcast.15, s32[1]{0:T(128)} %bitcast.16, s32[1]{0:T(128)} %bitcast.17, s32[1]{0:T(128)} %bitcast.18, ...), dimensions={0} | concatenate | bytes 120 | tf_op jit(solution)/shard_map/stack | solution.py:689
  37.5 0.0 copy-start.4
  37.5 0.0 copy-start.5
  37.5 0.9 prepare_keys.1.key_ref
  38.4 14.1 %collective-permute-done.4.refs_2_ = bf16[192,1024]{1,0:T(8,128)(2,1)} collective-permute-done((bf16[192,1024]{1,0:T(8,128)(2,1)S(1)}, bf16[192,1024]{1,0:T(8,128)(2,1)}, u32[]{:S(2)}, u32[]{:S(2)}) %collective-permute-start.4) | collective-permute-done | bytes 393248 | tf_op jit(solution)/shard_map/ppermute | solution.py:660
  52.5 0.0 collective-permute-done.2.one_ref
  52.5 0.0 collective-permute-done.3.mid_ref
  52.5 0.0 copy-done.4
  52.5 0.0 copy-done.5
  52.5 10.3 %attention.1 = (bf16[128,1024]{1,0:T(8,128)(2,1)S(1)}, bf16[128,1024]{1,0:T(8,128)(2,1)S(1)}, bf16[256,1024]{1,0:T(8,128)(2,1)S(1)}, f32[256,1024]{1,0:T(8,128)S...) custom-call(s32[15]{0:T(128)S(1)} %stack.77.meta_ref, ...), custom_call_target="tpu_custom_call" | custom-call | flops 2415919104 | bytes 16777216 | tf_op jit(solution)/shard_map/attention/pallas_call | solution.py:386
  62.8 0.1 collective-permute-start.5
  62.9 1.6 %collective-permute-start.6 = (f32[8,128]{1,0:T(8,128)S(1)}, f32[8,128]{1,0:T(8,128)S(1)}, u32[]{:S(2)}, u32[]{:S(2)}) collective-permute-start(f32[8,128]{1,0:T(8,128)S(1)} %get-tuple-element.40), channel_id=1, source_target_pairs={{0,8},{8,0},{16,24},{24,16},{1,9},{9,1},{17,25},{25,17},{2,10},{10... | collective-permute-start | bytes 12296 | tf_op jit(solution)/shard_map/ppermute | solution.py:629
  64.5 2.1 %collective-permute-done.6 = f32[8,128]{1,0:T(8,128)S(1)} collective-permute-done((f32[8,128]{1,0:T(8,128)S(1)}, f32[8,128]{1,0:T(8,128)S(1)}, u32[]{:S(2)}, u32[]{:S(2)}) %collective-permute-start.6) | collective-permute-done | bytes 4128 | tf_op jit(solution)/shard_map/ppermute | solution.py:629
  66.6 1.6 %collective-permute-start.7 = (f32[8,128]{1,0:T(8,128)S(1)}, f32[8,128]{1,0:T(8,128)S(1)}, u32[]{:S(2)}, u32[]{:S(2)}) collective-permute-start(f32[8,128]{1,0:T(8,128)S(1)} %add.51), channel_id=1, source_target_pairs={{0,16},{8,24},{16,0},{24,8},{1,17},{9,25},{17,1},{25,9},{2,18},{10... | collective-permute-start | bytes 12296 | tf_op jit(solution)/shard_map/ppermute | solution.py:629
  68.2 2.0 %collective-permute-done.7 = f32[8,128]{1,0:T(8,128)S(1)} collective-permute-done((f32[8,128]{1,0:T(8,128)S(1)}, f32[8,128]{1,0:T(8,128)S(1)}, u32[]{:S(2)}, u32[]{:S(2)}) %collective-permute-start.7) | collective-permute-done | bytes 4128 | tf_op jit(solution)/shard_map/ppermute | solution.py:629
  70.2 1.9 %collective-permute-start.8 = (f32[8,128]{1,0:T(8,128)S(1)}, f32[8,128]{1,0:T(8,128)S(1)}, u32[]{:S(2)}, u32[]{:S(2)}) collective-permute-start(f32[8,128]{1,0:T(8,128)S(1)} %add.52), channel_id=1, source_target_pairs={{0,2},{1,3},{2,0},{3,1},{4,6},{5,7},{6,4},{7,5},{8,10},{9,11},{10,... | collective-permute-start | bytes 12296 | tf_op jit(solution)/shard_map/ppermute | solution.py:629
  72.2 1.7 %collective-permute-done.8 = f32[8,128]{1,0:T(8,128)S(1)} collective-permute-done((f32[8,128]{1,0:T(8,128)S(1)}, f32[8,128]{1,0:T(8,128)S(1)}, u32[]{:S(2)}, u32[]{:S(2)}) %collective-permute-start.8) | collective-permute-done | bytes 4128 | tf_op jit(solution)/shard_map/ppermute | solution.py:629
  73.8 0.0 collective-permute-done.5.arrived_ref
  73.8 0.1 relay.1
  73.9 2.1 %collective-permute-start.9 = (bf16[448,1024]{1,0:T(8,128)(2,1)S(1)}, bf16[448,1024]{1,0:T(8,128)(2,1)S(1)}, u32[]{:S(2)}, u32[]{:S(2)}) collective-permute-start(bf16[448,1024]{1,0:T(8,128)(2,1)S(1)} %get-tuple-element.42), channel_id=1, source_target_pairs={{0,2},{1,3},{2,0},{3,1},{4,6},{5,7},{6,4},{7,5},{8,10},{9,11},{10,... | collective-permute-start | bytes 2752520 | tf_op jit(solution)/shard_map/ppermute | solution.py:660
  76.0 0.7 collective-permute-start.11
  76.7 2.8 %collective-permute-start.10 = (bf16[208,1024]{1,0:T(8,128)(2,1)S(1)}, bf16[208,1024]{1,0:T(8,128)(2,1)S(1)}, u32[]{:S(2)}, u32[]{:S(2)}) collective-permute-start(bf16[208,1024]{1,0:T(8,128)(2,1)S(1)} %get-tuple-element.43), channel_id=1, source_target_pairs={{0,4},{1,5},{2,6},{3,7},{4,0},{5,1},{6,2},{7,3},{8,12},{9,13},{10,... | collective-permute-start | bytes 1277960 | tf_op jit(solution)/shard_map/ppermute | solution.py:660
  79.5 26.9 %collective-permute-done.10.two_ref = bf16[208,1024]{1,0:T(8,128)(2,1)S(1)} collective-permute-done((bf16[208,1024]{1,0:T(8,128)(2,1)S(1)}, bf16[208,1024]{1,0:T(8,128)(2,1)S(1)}, u32[]{:S(2)}, u32[]{:S(2)}) %collective-permute-start.10) | collective-permute-done | bytes 426016 | tf_op jit(solution)/shard_map/ppermute | solution.py:660
  106.4 0.0 collective-permute-done.9.one_ref
  106.4 0.9 finish_lyric.1
  107.3 0.0 collective-permute-done.11.mid_ref
  107.4 2.3 %finish_audio.1 = (bf16[128,2048]{1,0:T(8,128)(2,1)}, bf16[128,2048]{1,0:T(8,128)(2,1)}, bf16[128,2048]{1,0:T(8,128)(2,1)}, bf16[128,2048]{1,0:T(8,128)(2,1)}, bf16[624,1024]{1,0:T(8,128)(2,1)S(1)}) custom-call(s32[2]{0:T(128)S(1)} %copy-done.6, f32[2,128]{1,0:T(2,128)S(1)} %pad_maximum_fusion.gain_ref, ...), custom_call_target="tpu_custom_call", output_to_operand_aliasing={{4}: (11, {})} | custom-call | flops 1 | bytes 1 | tf_op jit(solution)/shard_map/finish_audio/pallas_call | solution.py:451
  109.6 0.1 collective-permute-start.12
  109.7 3.0 %collective-permute-done.12.mate_ref = bf16[624,1024]{1,0:T(8,128)(2,1)S(1)} collective-permute-done((bf16[624,1024]{1,0:T(8,128)(2,1)S(1)}, bf16[624,1024]{1,0:T(8,128)(2,1)S(1)}, u32[]{:S(2)}, u32[]{:S(2)}) %collective-permute-start.12) | collective-permute-done | bytes 1277984 | tf_op jit(solution)/shard_map/ppermute | solution.py:740
  112.7 2.2 %join.1 = (bf16[128,2048]{1,0:T(8,128)(2,1)}, bf16[128,2048]{1,0:T(8,128)(2,1)}, bf16[128,2048]{1,0:T(8,128)(2,1)}, bf16[128,2048]{1,0:T(8,128)(2,1)}, bf16[48,2...) custom-call(s32[2]{0:T(128)S(1)} %copy-done.6, ...), custom_call_target="tpu_custom_call", output_to_operand_aliasing={{0}: (4, {}), {1}: (5, {}), {2}: (6, {}), {3}: (7, {})} | custom-call | flops 1 | bytes 1 | tf_op jit(solution)/shard_map/join/pallas_call | solution.py:557
  (4 shorter events, 0.0 us)
Async XLA Ops:
  1.3 3.8 %copy-start.8 = (f32[128]{0:T(128)S(1)}, f32[128]{0:T(128)}, u32[]{:S(2)}) copy-start(f32[128]{0:T(128)} %param.16) | copy-start | bytes 1540
  1.3 3.8 %copy-start.9 = (f32[128]{0:T(128)S(1)}, f32[128]{0:T(128)}, u32[]{:S(2)}) copy-start(f32[128]{0:T(128)} %param.15) | copy-start | bytes 1540
  1.3 6.6 %copy-start.2 = (bf16[1,48,2048]{2,1,0:T(8,128)(2,1)S(1)}, bf16[1,48,2048]{2,1,0:T(8,128)(2,1)}, u32[]{:S(2)}) copy-start(bf16[1,48,2048]{2,1,0:T(8,128)(2,1)} %param.13) | copy-start | bytes 589828
  1.3 6.6 %copy-start.3 = (bf16[1,48,2048]{2,1,0:T(8,128)(2,1)S(1)}, bf16[1,48,2048]{2,1,0:T(8,128)(2,1)}, u32[]{:S(2)}) copy-start(bf16[1,48,2048]{2,1,0:T(8,128)(2,1)} %param.14) | copy-start | bytes 589828
  1.3 6.6 %copy-start.6 = (s32[2]{0:T(128)S(1)}, s32[2]{0:T(128)}, u32[]{:S(2)}) copy-start(s32[2]{0:T(128)} %pad_add_fusion.state_ref) | copy-start | bytes 28
  4.5 8.2 %copy-start = (bf16[1,128,2048]{2,1,0:T(8,128)(2,1)S(1)}, bf16[1,128,2048]{2,1,0:T(8,128)(2,1)}, u32[]{:S(2)}) copy-start(bf16[1,128,2048]{2,1,0:T(8,128)(2,1)} %param.11) | copy-start | bytes 1572868
  4.5 8.2 %copy-start.1 = (bf16[1,128,2048]{2,1,0:T(8,128)(2,1)S(1)}, bf16[1,128,2048]{2,1,0:T(8,128)(2,1)}, u32[]{:S(2)}) copy-start(bf16[1,128,2048]{2,1,0:T(8,128)(2,1)} %param.12) | copy-start | bytes 1572868
  4.5 3.4 %collective-permute-start = (bf16[640,1024]{1,0:T(8,128)(2,1)}, bf16[640,1024]{1,0:T(8,128)(2,1)S(1)}, u32[]{:S(2)}, u32[]{:S(2)}) collective-permute-start(bf16[640,1024]{1,0:T(8,128)(2,1)} %pack.1), channel_id=1, source_target_pairs={{0,1},{1,0},{2,3},{3,2},{4,5},{5,4},{6,7},{7,6},{8,9},{9,8},{10,11... | collective-permute-start | bytes 3932168 | tf_op jit(solution)/shard_map/ppermute | solution.py:705
  8.6 22.0 %collective-permute-start.1 = (bf16[192,1024]{1,0:T(8,128)(2,1)S(1)}, bf16[192,1024]{1,0:T(8,128)(2,1)S(1)}, u32[]{:S(2)}, u32[]{:S(2)}) collective-permute-start(bf16[192,1024]{1,0:T(8,128)(2,1)S(1)} %pair_lyrics.1.refs_0_), channel_id=1, source_target_pairs={{0,4},{1,5},{2,6},{3,7},{4,0},{5,1},{6,2},{7,3},{8,12},{9,13},{10,... | collective-permute-start | bytes 1179656 | tf_op jit(solution)/shard_map/ppermute | solution.py:660
  14.4 21.1 %copy-start.7 = (s32[1,1,2]{2,1,0:T(1,128)S(1)}, s32[1,1,2]{2,1,0:T(1,128)}, u32[]{:S(2)}) copy-start(s32[1,1,2]{2,1,0:T(1,128)} %param.18) | copy-start | bytes 28
  14.4 38.1 %collective-permute-start.2 = (bf16[448,1024]{1,0:T(8,128)(2,1)}, bf16[448,1024]{1,0:T(8,128)(2,1)}, u32[]{:S(2)}, u32[]{:S(2)}) collective-permute-start(bf16[448,1024]{1,0:T(8,128)(2,1)} %edge.2), channel_id=1, source_target_pairs={{0,2},{1,3},{2,0},{3,1},{4,6},{5,7},{6,4},{7,5},{8,10},{9,11},{10,... | collective-permute-start | bytes 2752520 | tf_op jit(solution)/shard_map/ppermute | solution.py:660
  32.2 20.4 %collective-permute-start.3 = (bf16[256,1024]{1,0:T(8,128)(2,1)}, bf16[256,1024]{1,0:T(8,128)(2,1)}, u32[]{:S(2)}, u32[]{:S(2)}) collective-permute-start(bf16[256,1024]{1,0:T(8,128)(2,1)} %edge.3), channel_id=1, source_target_pairs={{2,4},{3,5},{4,2},{5,3},{10,12},{11,13},{12,10},{13,11},{18,20},{1... | collective-permute-start | bytes 1572872 | tf_op jit(solution)/shard_map/ppermute | solution.py:660
  33.6 18.9 %collective-permute-start.4 = (bf16[192,1024]{1,0:T(8,128)(2,1)S(1)}, bf16[192,1024]{1,0:T(8,128)(2,1)}, u32[]{:S(2)}, u32[]{:S(2)}) collective-permute-start(bf16[192,1024]{1,0:T(8,128)(2,1)S(1)} %collective-permute-done.1.refs_0_.refs_1_), channel_id=1, source_target_pairs={{0,2},{1,3},{2,0},{3,1},{4,6},{5,7},{6,4},{7,5},{8,10},{9,11},{10,... | collective-permute-start | bytes 1179656 | tf_op jit(solution)/shard_map/ppermute | solution.py:660
  37.5 15.1 %copy-start.4 = (bf16[1,128,2048]{2,1,0:T(8,128)(2,1)S(1)}, bf16[1,128,2048]{2,1,0:T(8,128)(2,1)}, u32[]{:S(2)}) copy-start(bf16[1,128,2048]{2,1,0:T(8,128)(2,1)} %param.10) | copy-start | bytes 1572868
  37.5 15.1 %copy-start.5 = (bf16[1,128,2048]{2,1,0:T(8,128)(2,1)S(1)}, bf16[1,128,2048]{2,1,0:T(8,128)(2,1)}, u32[]{:S(2)}) copy-start(bf16[1,128,2048]{2,1,0:T(8,128)(2,1)} %param.17) | copy-start | bytes 1572868
  62.8 11.0 %collective-permute-start.5 = (bf16[192,1024]{1,0:T(8,128)(2,1)S(1)}, bf16[192,1024]{1,0:T(8,128)(2,1)S(1)}, u32[]{:S(2)}, u32[]{:S(2)}) collective-permute-start(bf16[192,1024]{1,0:T(8,128)(2,1)S(1)} %get-tuple-element.39), channel_id=1, source_target_pairs={{0,2},{1,3},{2,0},{3,1},{4,6},{5,7},{6,4},{7,5},{8,10},{9,11},{10,... | collective-permute-start | bytes 1179656 | tf_op jit(solution)/shard_map/ppermute | solution.py:660
  62.9 3.7 %collective-permute-start.6 = (f32[8,128]{1,0:T(8,128)S(1)}, f32[8,128]{1,0:T(8,128)S(1)}, u32[]{:S(2)}, u32[]{:S(2)}) collective-permute-start(f32[8,128]{1,0:T(8,128)S(1)} %get-tuple-element.40), channel_id=1, source_target_pairs={{0,8},{8,0},{16,24},{24,16},{1,9},{9,1},{17,25},{25,17},{2,10},{10... | collective-permute-start | bytes 12296 | tf_op jit(solution)/shard_map/ppermute | solution.py:629
  66.6 3.6 %collective-permute-start.7 = (f32[8,128]{1,0:T(8,128)S(1)}, f32[8,128]{1,0:T(8,128)S(1)}, u32[]{:S(2)}, u32[]{:S(2)}) collective-permute-start(f32[8,128]{1,0:T(8,128)S(1)} %add.51), channel_id=1, source_target_pairs={{0,16},{8,24},{16,0},{24,8},{1,17},{9,25},{17,1},{25,9},{2,18},{10... | collective-permute-start | bytes 12296 | tf_op jit(solution)/shard_map/ppermute | solution.py:629
  70.2 3.6 %collective-permute-start.8 = (f32[8,128]{1,0:T(8,128)S(1)}, f32[8,128]{1,0:T(8,128)S(1)}, u32[]{:S(2)}, u32[]{:S(2)}) collective-permute-start(f32[8,128]{1,0:T(8,128)S(1)} %add.52), channel_id=1, source_target_pairs={{0,2},{1,3},{2,0},{3,1},{4,6},{5,7},{6,4},{7,5},{8,10},{9,11},{10,... | collective-permute-start | bytes 12296 | tf_op jit(solution)/shard_map/ppermute | solution.py:629
  73.9 32.5 %collective-permute-start.9 = (bf16[448,1024]{1,0:T(8,128)(2,1)S(1)}, bf16[448,1024]{1,0:T(8,128)(2,1)S(1)}, u32[]{:S(2)}, u32[]{:S(2)}) collective-permute-start(bf16[448,1024]{1,0:T(8,128)(2,1)S(1)} %get-tuple-element.42), channel_id=1, source_target_pairs={{0,2},{1,3},{2,0},{3,1},{4,6},{5,7},{6,4},{7,5},{8,10},{9,11},{10,... | collective-permute-start | bytes 2752520 | tf_op jit(solution)/shard_map/ppermute | solution.py:660
  76.0 31.3 %collective-permute-start.11 = (bf16[256,1024]{1,0:T(8,128)(2,1)S(1)}, bf16[256,1024]{1,0:T(8,128)(2,1)S(1)}, u32[]{:S(2)}, u32[]{:S(2)}) collective-permute-start(bf16[256,1024]{1,0:T(8,128)(2,1)S(1)} %get-tuple-element.48), channel_id=1, source_target_pairs={{2,4},{3,5},{4,2},{5,3},{10,12},{11,13},{12,10},{13,11},{18,20},{1... | collective-permute-start | bytes 1572872 | tf_op jit(solution)/shard_map/ppermute | solution.py:660
  76.7 29.7 %collective-permute-start.10 = (bf16[208,1024]{1,0:T(8,128)(2,1)S(1)}, bf16[208,1024]{1,0:T(8,128)(2,1)S(1)}, u32[]{:S(2)}, u32[]{:S(2)}) collective-permute-start(bf16[208,1024]{1,0:T(8,128)(2,1)S(1)} %get-tuple-element.43), channel_id=1, source_target_pairs={{0,4},{1,5},{2,6},{3,7},{4,0},{5,1},{6,2},{7,3},{8,12},{9,13},{10,... | collective-permute-start | bytes 1277960 | tf_op jit(solution)/shard_map/ppermute | solution.py:660
  109.6 3.1 %collective-permute-start.12 = (bf16[624,1024]{1,0:T(8,128)(2,1)S(1)}, bf16[624,1024]{1,0:T(8,128)(2,1)S(1)}, u32[]{:S(2)}, u32[]{:S(2)}) collective-permute-start(bf16[624,1024]{1,0:T(8,128)(2,1)S(1)} %get-tuple-element.53), channel_id=1, source_target_pairs={{0,1},{1,0},{2,3},{3,2},{4,5},{5,4},{6,7},{7,6},{8,9},{9,8},{10,11... | collective-permute-start | bytes 3833864 | tf_op jit(solution)/shard_map/ppermute | solution.py:740

commit v9 on v8

--- a/solution.py
+++ b/solution.py
@@ -19,6 +19,7 @@
 ANY = pl.BlockSpec(memory_space=pl.ANY)
 GAIN_ROWS = 16
 HEADS_PER_STEP = 2
+CHUNKS = 2
 ALIGN_ROWS = 32
 SMALL = pl.CostEstimate(flops=1, bytes_accessed=1, transcendentals=0)
 
@@ -49,6 +50,15 @@
 def half_of(ref, core):
     half = ref.shape[1] // 2
     return pl.ds(pl.multiple_of(core * half, half), half)
+
+
+def chunk_of(ref, core, chunk):
+    size = ref.shape[1] // 2 // CHUNKS
+    return pl.ds(pl.multiple_of((core * CHUNKS + chunk) * size, size), size)
+
+
+def chunk_cols(chunk, size):
+    return slice(chunk * size, (chunk + 1) * size)
 
 
 def split_rows(sums, cols):
@@ -126,49 +136,57 @@
     )(state, align, *arrays)
 
 
-def pair_kernel(state_ref, gain_ref, key_ref, value_ref, mate_ref, pair_ref):
+def pair_kernel(chunk, state_ref, gain_ref, key_ref, value_ref, mate_ref, pair_ref):
     rows = key_ref.shape[0]
     first = mate_ref.shape[0] - ALIGN_ROWS - 2 * rows
-    own = half_of(key_ref, state_ref[0])
+    own = chunk_of(key_ref, state_ref[0], chunk)
+    cols = chunk_cols(chunk, pair_ref.shape[1])
     norm_columns(pair_ref, slice(0, rows), key_ref[:, own], gain_ref)
     pair_ref[rows : 2 * rows, :] = value_ref[:, own]
     norm_columns(
-        pair_ref, slice(2 * rows, 3 * rows), mate_ref[first : first + rows, :], gain_ref
+        pair_ref, slice(2 * rows, 3 * rows), mate_ref[first : first + rows, cols], gain_ref
     )
-    pair_ref[3 * rows :, :] = mate_ref[first + rows : first + 2 * rows, :]
-
-
-def pair_lyrics(state, gains, lyric_key, lyric_value, mate):
+    pair_ref[3 * rows :, :] = mate_ref[first + rows : first + 2 * rows, cols]
+
+
+def pair_lyrics(state, chunk, gains, lyric_key, lyric_value, mate):
     rows, width = lyric_key.shape
     return call(
-        pair_kernel, "pair_lyrics", [SMEM] + [VMEM] * 4, VMEM, shape(4 * rows, width // 2)
+        functools.partial(pair_kernel, chunk),
+        "pair_lyrics",
+        [SMEM] + [VMEM] * 4,
+        VMEM,
+        shape(4 * rows, width // 2 // CHUNKS),
     )(state, gains, lyric_key, lyric_value, mate)
 
 
-def edge_kernel(touching, leading, state_ref, gain_ref, key_ref, value_ref, mate_ref, *refs):
+def edge_kernel(
+    chunk, touching, leading, state_ref, gain_ref, key_ref, value_ref, mate_ref, *refs
+):
     out_ref = refs[-1]
     frames = key_ref.shape[0]
     first = out_ref.shape[0] - 2 * frames
     if leading:
         out_ref[0:first, :] = refs[0][...]
     mine = state_ref[1] == touching
-    own = half_of(key_ref, state_ref[0])
-    keys = jnp.where(mine, key_ref[:, own], mate_ref[2 * frames : 3 * frames, :])
+    own = chunk_of(key_ref, state_ref[0], chunk)
+    cols = chunk_cols(chunk, out_ref.shape[1])
+    keys = jnp.where(mine, key_ref[:, own], mate_ref[2 * frames : 3 * frames, cols])
     norm_columns(out_ref, slice(first, first + frames), keys, gain_ref)
     out_ref[first + frames :, :] = jnp.where(
-        mine, value_ref[:, own], mate_ref[3 * frames : 4 * frames, :]
+        mine, value_ref[:, own], mate_ref[3 * frames : 4 * frames, cols]
     )
 
 
-def edge(state, touching, gains, key, value, mate, lead, after):
+def edge(state, chunk, touching, gains, key, value, mate, lead, after):
     frames, width = key.shape
     rows = sum(array.shape[0] for array in lead) + 2 * frames
     return call(
-        functools.partial(edge_kernel, touching, bool(lead)),
+        functools.partial(edge_kernel, chunk, touching, bool(lead)),
         "edge",
         [SMEM] + [VMEM] * (4 + len(lead)) + [ANY] * len(after),
         VMEM,
-        shape(rows, width // 2),
+        shape(rows, width // 2 // CHUNKS),
     )(state, gains, key, value, mate, *lead, *after)
 
 
@@ -194,13 +212,14 @@
 
 
 def attention_kernel(
-    groups, head_size, score_scale, meta_ref, gain_ref, query_ref, grad_ref, value_ref, key_ref,
+    chunk, groups, head_size, score_scale, meta_ref, gain_ref, query_ref, grad_ref, value_ref, key_ref,
     mate_ref, one_ref, mid_ref, *refs
 ):
     frames = query_ref.shape[0]
     exchanged = len(groups) == 4
     inputs = 3 if exchanged else 1
     lyric_in, refs = refs[:inputs], refs[inputs:]
+    earlier, refs = refs[: 3 * chunk], refs[3 * chunk :]
     window = one_ref.shape[0] - 2 * frames
     out_ref, grad_query_ref, to_mate_ref, key_grad_ref, value_grad_ref = refs[:5]
     to_one_ref, to_mid_ref, gain_grad_ref = refs[5:8]
@@ -211,7 +230,12 @@
     align = mate_ref.shape[0] - ALIGN_ROWS
     touching = meta_ref[1] == 1
 
-    gain_grad_ref[...] = jnp.zeros_like(gain_grad_ref)
+    size = out_ref.shape[1]
+    for index in range(chunk):
+        for ref, part_ref in zip((to_one_ref, to_mid_ref), earlier[3 * index :]):
+            if ref.shape[1] > size:
+                ref[:, chunk_cols(index, size)] = part_ref[...]
+    gain_grad_ref[...] = earlier[-1][...] if chunk else jnp.zeros_like(gain_grad_ref)
     mate_tiles = mate_ref[align:, 0:frames].astype(jnp.float32).astype(jnp.int32)
     start = 0
     for number, (_, (_, _, rows)) in enumerate(runs):
@@ -238,13 +262,21 @@
 
     q_gain = gain_ref[0:1, :]
     k_gain = gain_ref[1:2, :]
-    heads = key_ref.shape[1] // head_size
+    heads = size // head_size
+    sent = to_one_ref.shape[1] // size > 1
 
     def one_head(head):
         cols = pl.ds(pl.multiple_of(head * head_size, head_size), head_size)
+        half_cols = pl.ds(
+            pl.multiple_of((chunk * heads + head) * head_size, head_size), head_size
+        )
         own_cols = pl.ds(
-            pl.multiple_of((meta_ref[0] * heads + head) * head_size, head_size), head_size
-        )
+            pl.multiple_of(
+                ((meta_ref[0] * CHUNKS + chunk) * heads + head) * head_size, head_size
+            ),
+            head_size,
+        )
+        sent_cols = half_cols if sent else cols
         lyric = [ref[:, cols if exchanged else own_cols] for ref in lyric_in]
         if exchanged:
             lyric = [lyric[0], lyric[1], one_ref[0:window, cols], lyric[2]]
@@ -253,13 +285,13 @@
         far_rows = jnp.where(touching, mid_rows, one_rows)
 
         def from_mate(number):
-            return mate_ref[number * frames : (number + 1) * frames, cols]
+            return mate_ref[number * frames : (number + 1) * frames, half_cols]
 
         query = jnp.concatenate([query_ref[:, own_cols], from_mate(0)], axis=0)
         query = query.astype(jnp.float32)
         cot = jnp.concatenate([grad_ref[:, own_cols], from_mate(1)], axis=0)
         key_low = jnp.concatenate(
-            [key_ref[:, cols]]
+            [key_ref[:, half_cols]]
             + [lyric[index][run[0] : run[0] + run[2]] for index, run in runs]
             + [near_rows[:frames], far_rows[:frames]],
             axis=0,
@@ -347,10 +379,10 @@
             (grad_keys.astype(jnp.bfloat16), 0),
             (grad_values.astype(jnp.bfloat16), frames),
         ):
-            to_one_ref[window + part : window + part + frames, cols] = jnp.where(
+            to_one_ref[window + part : window + part + frames, sent_cols] = jnp.where(
                 touching, grads[near], grads[far]
             )
-            to_mid_ref[part : part + frames, cols] = jnp.where(touching, grads[far], grads[near])
+            to_mid_ref[part : part + frames, sent_cols] = jnp.where(touching, grads[far], grads[near])
         if exchanged:
             held_ref, two_ref, to_two_ref = lyric_out
             outs = (held_ref, two_ref, to_one_ref, to_two_ref)
@@ -359,8 +391,9 @@
         start = 2 * frames
         for index, (key_row, value_row, rows) in runs:
             part = slice(start, start + rows)
-            outs[index][key_row : key_row + rows, cols] = grad_keys[part].astype(jnp.bfloat16)
-            outs[index][value_row : value_row + rows, cols] = grad_values[part].astype(
+            put = sent_cols if outs[index] is to_one_ref else cols
+            outs[index][key_row : key_row + rows, put] = grad_keys[part].astype(jnp.bfloat16)
+            outs[index][value_row : value_row + rows, put] = grad_values[part].astype(
                 jnp.bfloat16
             )
             start += rows
@@ -371,158 +404,176 @@
             one_head(step * HEADS_PER_STEP + number)
 
 
-def attention(meta, gains, query, cot, value, key, mate, one, mid, lyrics, groups):
+def attention(
+    chunk, meta, gains, query, cot, value, key, mate, one, mid, lyrics, groups, earlier
+):
     frames, width = query.shape
     head_size = gains.shape[1]
-    half = width // 2
+    size = width // 2 // CHUNKS
+    sent = size if chunk < CHUNKS - 1 else width // 2
     lyric_rows = sum(run[2] for group in groups for run in group)
     key_rows = 3 * frames + lyric_rows
     bf16, f32 = jnp.bfloat16, jnp.float32
     slot = sum(2 * run[2] for run in groups[0])
-    out_shape = [shape(frames, half)] * 2
-    out_shape += [shape(2 * frames, half, dtype) for dtype in (bf16, f32, f32)]
-    out_shape += [shape(one.shape[0], half), shape(2 * frames, half), shape(8, head_size, f32)]
-    out_shape += [shape(slot, half)] * len(lyrics)
-    return call(
-        functools.partial(attention_kernel, groups, head_size, head_size ** (-0.5)),
+    out_shape = [shape(frames, size)] * 2
+    out_shape += [shape(2 * frames, size, dtype) for dtype in (bf16, f32, f32)]
+    out_shape += [shape(one.shape[0], sent), shape(2 * frames, sent), shape(8, head_size, f32)]
+    out_shape += [shape(slot, size)] * len(lyrics)
+    return call(
+        functools.partial(attention_kernel, chunk, groups, head_size, head_size ** (-0.5)),
         "attention",
-        [SMEM] + [VMEM] * (8 + len(lyrics)),
+        [SMEM] + [VMEM] * (8 + len(lyrics) + len(earlier)),
         [VMEM] * len(out_shape),
         out_shape,
         limit=ATTENTION_VMEM_LIMIT,
         cost=pl.CostEstimate(
-            flops=24 * key_rows * frames * half,
-            bytes_accessed=16 * 1024 * 1024,
-            transcendentals=2 * key_rows * frames * (half // head_size),
+            flops=24 * key_rows * frames * size,
+            bytes_accessed=8 * 1024 * 1024,
+            transcendentals=2 * key_rows * frames * (size // head_size),
         ),
         scratch_shapes=[pltpu.VMEM((frames + lyric_rows, 2 * frames), f32)],
-    )(meta, gains, query, cot, value, key, mate, one, mid, *lyrics)
+    )(meta, gains, query, cot, value, key, mate, one, mid, *lyrics, *earlier)
 
 
 def finish_audio_kernel(
-    aliased, state_ref, gain_ref, raw_ref, mate_ref, key_grad_ref, value_grad_ref, one_ref,
-    mid_ref, ready_ref, out_own_ref, query_own_ref, *refs,
+    state_ref, gain_ref, raw_ref, mate_ref, one_ref, mid_ref, *refs
 ):
-    refs = refs[aliased:]
-    outs, to_mate_ref, key_ref, value_ref, sems = refs[:4], *refs[4:]
+    chunk_refs, refs = refs[: 5 * CHUNKS], refs[5 * CHUNKS :]
+    *lyric, out, query_out, key_out, value_out, to_mate_ref, key_ref, value_ref, sems = refs
     head_size = gain_ref.shape[1]
     k_gain = gain_ref[1:2, :]
-    frames = raw_ref.shape[0]
+    frames, half = key_ref.shape
+    size = half // CHUNKS
     own, mate = slice(0, frames), slice(frames, 2 * frames)
     first = one_ref.shape[0] - 2 * frames
     touching = state_ref[1] == 1
-    copies = [
-        pltpu.make_async_copy(source, out.at[:, half_of(out, state_ref[0])], sems.at[index])
-        for index, (source, out) in enumerate(
-            zip((out_own_ref, query_own_ref, key_ref, value_ref), outs)
-        )
-    ]
-    copies[0].start()
-    copies[1].start()
-    to_mate_ref[0 : 2 * frames, :] = ready_ref[...]
+    copies = []
+    for chunk in range(CHUNKS):
+        out_own_ref, query_own_ref, ready_ref = chunk_refs[5 * chunk : 5 * chunk + 3]
+        for source, target in ((out_own_ref, out), (query_own_ref, query_out)):
+            copies.append(
+                pltpu.make_async_copy(
+                    source,
+                    target.at[:, chunk_of(target, state_ref[0], chunk)],
+                    sems.at[len(copies)],
+                )
+            )
+            copies[-1].start()
+        to_mate_ref[0 : 2 * frames, chunk_cols(chunk, size)] = ready_ref[...]
+    for ref in lyric:
+        to_mate_ref[4 * frames :, :] = ref[...]
     raw_keys = raw_ref[:, half_of(raw_ref, state_ref[0])]
-    for head in range(key_ref.shape[1] // head_size):
+    for head in range(half // head_size):
         cols = slice(head * head_size, (head + 1) * head_size)
+        chunk = head * head_size // size
+        part = slice(head * head_size - chunk * size, (head + 1) * head_size - chunk * size)
+        key_grad_ref, value_grad_ref = chunk_refs[5 * chunk + 3 : 5 * chunk + 5]
         one = one_ref[first:, cols].astype(jnp.float32)
         mid = mid_ref[:, cols].astype(jnp.float32)
         for_own = jnp.where(touching, one, mid)
         for_mate = jnp.where(touching, mid, one)
         key_ref[:, cols] = through_norm(
-            raw_keys[:, cols], key_grad_ref[own, cols] + for_own[:frames], k_gain
-        )
-        value_ref[:, cols] = (value_grad_ref[own, cols] + for_own[frames:]).astype(jnp.bfloat16)
+            raw_keys[:, cols], key_grad_ref[own, part] + for_own[:frames], k_gain
+        )
+        value_ref[:, cols] = (value_grad_ref[own, part] + for_own[frames:]).astype(jnp.bfloat16)
         to_mate_ref[2 * frames : 3 * frames, cols] = through_norm(
             mate_ref[2 * frames : 3 * frames, cols],
-            key_grad_ref[mate, cols] + for_mate[:frames],
+            key_grad_ref[mate, part] + for_mate[:frames],
             k_gain,
         )
         to_mate_ref[3 * frames : 4 * frames, cols] = (
-            value_grad_ref[mate, cols] + for_mate[frames:]
+            value_grad_ref[mate, part] + for_mate[frames:]
         ).astype(jnp.bfloat16)
-    copies[2].start()
-    copies[3].start()
+    for source, target in ((key_ref, key_out), (value_ref, value_out)):
+        copies.append(
+            pltpu.make_async_copy(
+                source, target.at[:, half_of(target, state_ref[0])], sems.at[len(copies)]
+            )
+        )
+        copies[-1].start()
     for copy in copies:
         copy.wait()
 
 
-def finish_audio(state, gains, raw, mate, key_grad, value_grad, one, mid, ready, owns, to_mate):
+def finish_audio(state, gains, raw, mate, one, mid, chunks, lyric):
     frames, width = raw.shape
     half = width // 2
-    return call(
-        functools.partial(finish_audio_kernel, len(to_mate)),
+    rows = 4 * frames + sum(array.shape[0] for array in lyric)
+    return call(
+        finish_audio_kernel,
         "finish_audio",
-        [SMEM] + [VMEM] * (10 + len(to_mate)),
+        [SMEM] + [VMEM] * (5 + len(chunks) + len(lyric)),
         [HBM] * 4 + [VMEM],
-        [shape(frames, width)] * 4
-        + [shape(*array.shape) for array in to_mate or [shape(4 * frames, half)]],
-        input_output_aliases={11: 4} if to_mate else {},
+        [shape(frames, width)] * 4 + [shape(rows, half)],
         scratch_shapes=[pltpu.VMEM((frames, half), jnp.bfloat16)] * 2
-        + [pltpu.SemaphoreType.DMA((4,))],
-    )(state, gains, raw, mate, key_grad, value_grad, one, mid, ready, *owns, *to_mate)
-
-
-def relay_kernel(part_ref, arrived_ref, total_ref, later_ref, out_ref, handed_ref):
-    rows = part_ref.shape[0]
-    out_ref[0:rows, :] = (
-        part_ref[...].astype(jnp.float32) + arrived_ref[...].astype(jnp.float32)
-    ).astype(jnp.bfloat16)
+        + [pltpu.SemaphoreType.DMA((2 * CHUNKS + 2,))],
+    )(state, gains, raw, mate, one, mid, *chunks, *lyric)
+
+
+def relay_kernel(total_ref, later_ref, *refs):
+    parts, arrived, (out_ref, _) = refs[:CHUNKS], refs[CHUNKS : 2 * CHUNKS], refs[2 * CHUNKS :]
+    rows, size = parts[0].shape
+    for chunk, (part_ref, arrived_ref) in enumerate(zip(parts, arrived)):
+        out_ref[0:rows, chunk_cols(chunk, size)] = (
+            part_ref[...].astype(jnp.float32) + arrived_ref[...].astype(jnp.float32)
+        ).astype(jnp.bfloat16)
     out_ref[rows:, :] = split_rows(total_ref[...], out_ref.shape[1])
 
 
-def relay(part, arrived, total, later):
-    rows, half = part.shape
+def relay(parts, arrived, total, later):
+    rows, size = parts[0].shape
     return call(
         relay_kernel,
         "relay",
-        [VMEM] * 3 + [ANY],
+        [VMEM, ANY] + [VMEM] * (2 * CHUNKS),
         [VMEM, ANY],
-        [shape(rows + GAIN_ROWS, half), shape(*later.shape)],
-        input_output_aliases={3: 1},
-    )(part, arrived, total, later)
+        [shape(rows + GAIN_ROWS, CHUNKS * size), shape(*later.shape)],
+        input_output_aliases={1: 1},
+    )(total, later, *parts, *arrived)
 
 
 def finish_lyric_kernel(
-    state_ref, gain_ref, raw_ref, mate_ref, held_ref, one_ref, two_ref, sum_ref, own_ref,
-    to_mate_ref, total_ref,
+    state_ref, gain_ref, raw_ref, mate_ref, one_ref, two_ref, sum_ref, *refs
 ):
+    held_refs, (own_ref, to_mate_ref, total_ref) = refs[:CHUNKS], refs[CHUNKS:]
     rows = raw_ref.shape[0]
     head_size = gain_ref.shape[1]
     k_gain = gain_ref[1:2, :]
+    size = held_refs[0].shape[1]
     first = mate_ref.shape[0] - ALIGN_ROWS - 2 * rows
-    end = to_mate_ref.shape[0] - GAIN_ROWS
     total_ref[...] = sum_ref[...] + joined_rows(two_ref[4 * rows :, :], head_size)
-    to_mate_ref[end:, :] = split_rows(total_ref[...], to_mate_ref.shape[1])
+    to_mate_ref[2 * rows :, :] = split_rows(total_ref[...], to_mate_ref.shape[1])
     raw_keys = raw_ref[:, half_of(raw_ref, state_ref[0])]
     for head in range(own_ref.shape[1] // head_size):
         cols = slice(head * head_size, (head + 1) * head_size)
-        total = held_ref[:, cols].astype(jnp.float32)
-        for part in (one_ref, two_ref):
-            total = total + part[0 : 4 * rows, cols].astype(jnp.float32)
+        chunk = head * head_size // size
+        part = slice(head * head_size - chunk * size, (head + 1) * head_size - chunk * size)
+        total = held_refs[chunk][:, part].astype(jnp.float32)
+        for ref in (one_ref, two_ref):
+            total = total + ref[0 : 4 * rows, cols].astype(jnp.float32)
         mate_keys = mate_ref[first : first + rows, cols]
-        for ref, start, base, raw in (
-            (own_ref, 0, 0, raw_keys[:, cols]),
-            (to_mate_ref, end - 2 * rows, 2 * rows, mate_keys),
+        for ref, base, raw in (
+            (own_ref, 0, raw_keys[:, cols]),
+            (to_mate_ref, 2 * rows, mate_keys),
         ):
-            ref[start : start + rows, cols] = through_norm(raw, total[base : base + rows], k_gain)
-            ref[start + rows : start + 2 * rows, cols] = total[
-                base + rows : base + 2 * rows
-            ].astype(jnp.bfloat16)
-
-
-def finish_lyric(state, gains, raw, mate, held, one, two, total, frames):
-    rows = raw.shape[0]
-    half = held.shape[1]
+            ref[0:rows, cols] = through_norm(raw, total[base : base + rows], k_gain)
+            ref[rows : 2 * rows, cols] = total[base + rows : base + 2 * rows].astype(jnp.bfloat16)
+
+
+def finish_lyric(state, gains, raw, mate, held, one, two, total):
+    rows, width = raw.shape
+    half = width // 2
     return call(
         finish_lyric_kernel,
         "finish_lyric",
-        [SMEM] + [VMEM] * 7,
+        [SMEM] + [VMEM] * (6 + len(held)),
         [VMEM] * 3,
         [
             shape(2 * rows, half),
-            shape(4 * frames + 2 * rows + GAIN_ROWS, half),
+            shape(2 * rows + GAIN_ROWS, half),
             shape(*total.shape, jnp.float32),
         ],
-    )(state, gains, raw, mate, held, one, two, total)
+    )(state, gains, raw, mate, one, two, total, *held)
 
 
 def join_kernel(count, state_ref, gain_ref, own_ref, mate_ref, *refs):
@@ -703,40 +754,45 @@
         + ([lyric_keys[0], lyric_values[0]] if hops else []),
     )
     mate = lax.ppermute(to_mate, "seq", swap)
+    chunks, parts, earlier, arrived = [], [], [], []
+    after = []
+    for chunk in range(CHUNKS):
+        before = after
+        if hops:
+            pair = pair_lyrics(state, chunk, gains, lyric_keys[0], lyric_values[0], mate)
+            two = hop(pair, across)
+            lyrics = [pair, two, hop(two, partners)]
+            lead, after = [pair], [two]
+        else:
+            lyrics, lead = [gathered], []
+        one = hop(edge(state, chunk, 1, gains, keys[0], values[0], mate, lead, before), partners)
+        mid = hop(edge(state, chunk, 0, gains, keys[0], values[0], mate, [], after), between)
+        if not chunk:
+            key_low = prepare_keys(state, gains, keys[0], mate, after)
+        results = attention(
+            chunk, meta, gains, queries[0], cotangent[0], values[0], key_low, mate, one, mid,
+            lyrics, groups, earlier,
+        )
+        chunks += results[:5]
+        earlier = [*earlier, *results[5:8]]
+        parts.append(results[8:])
+        if hops:
+            arrived.append(hop(results[-1], partners))
+    to_one, to_mid, gain_part = earlier[-3:]
+
+    mid = hop(to_mid, between)
+    to_mate = []
     if hops:
-        pair = pair_lyrics(state, gains, lyric_keys[0], lyric_values[0], mate)
-        two = hop(pair, across)
-        lyrics = [pair, two, hop(two, partners)]
-        lead, after = [pair], [two]
-    else:
-        lyrics, lead, after = [gathered], [], []
-    one = hop(edge(state, 1, gains, keys[0], values[0], mate, lead, []), partners)
-    mid = hop(edge(state, 0, gains, keys[0], values[0], mate, [], after), between)
-    key_low = prepare_keys(state, gains, keys[0], mate, after)
-    output, grad_queries, for_mate, key_grad, value_grad, to_one, to_mid, gain_part, *parts = (
-        attention(
-            meta, gains, queries[0], cotangent[0], values[0], key_low, mate, one, mid, lyrics,
-            groups,
-        )
-    )
-
-    to_mate = []
-    mid = hop(to_mid, between)
-    if hops:
-        held, for_two, to_two = parts
         gain_total = sum_over(sum_over(gain_part, "song", bits_of(songs)), "seq", [2])
-        to_two, to_one = relay(for_two, hop(to_two, partners), gain_total, to_one)
+        to_two, to_one = relay([part[1] for part in parts], arrived, gain_total, to_one)
         two, one = hop(to_two, across), hop(to_one, partners)
         own_half, part_to_mate, gain_total = finish_lyric(
-            state, gains, lyric_keys[0], mate, held, one, two, gain_total, frames
+            state, gains, lyric_keys[0], mate, [part[0] for part in parts], one, two, gain_total
         )
         to_mate = [part_to_mate]
     else:
         one = hop(to_one, partners)
-    *filled, to_mate = finish_audio(
-        state, gains, keys[0], mate, key_grad, value_grad, one, mid, for_mate,
-        [output, grad_queries], to_mate,
-    )
+    *filled, to_mate = finish_audio(state, gains, keys[0], mate, one, mid, chunks, to_mate)
     from_mate = lax.ppermute(to_mate, "seq", swap)
     if hops:
         *filled, grad_lyric_keys, grad_lyric_values, q_total, k_total = join(
@@ -748,7 +804,7 @@
         q_total, k_total = gain_total[0:1], gain_total[1:2]
         spread = lax.dynamic_update_slice(
             jnp.zeros((2 * total_rows, width), jnp.float32),
-            parts[0].astype(jnp.float32),
+            jnp.concatenate([part[0] for part in parts], axis=1).astype(jnp.float32),
             (0, core * (width // 2)),
         )
         lyric_key_sum, grad_lyric_values = [

time: 115 us -> 115 us (level)
  waiting for transfers between devices: 67.3 us -> 58 us
  starting transfers between devices: 19.6 us -> 24.3 us
  Pallas kernels: 23.9 us -> 28.3 us
    ppermute x8 -> x13, waiting for transfers between devices: 55.7 us -> 46.3 us  [hop(): return lax.ppermute(block, 'seq', pairs)]
    ppermute x8 -> x13, starting transfers between devices: 13.8 us -> 18.6 us  [hop(): return lax.ppermute(block, 'seq', pairs)]
    pallas_call x7 -> x11, Pallas kernels: 17.6 us -> 22 us  [the longest x2 11.6 us: attention(): call(functools.partial(attention_kernel, chunk, groups, head_size, head_s...]
  transfers between devices with their start and end apart: 13 -> 18, of which waited for: 8 -> 9; matrix products, arithmetic and copies ran while one was open for 2% -> 2% of each run, Pallas kernels for 4% -> 17%
where the time goes in v9:
time: 115 us
  waiting for transfers between devices  58 us (50%)
  Pallas kernels  28.3 us (25%)
  starting transfers between devices  24.3 us (21%)
  local copies, waits for them, and re-layouts  2.01 us (2%)
  between operations  1.61 us (1%)
    ppermute x13, waiting for transfers between devices, hop(): return lax.ppermute(block, 'seq', pairs)  46.3 us
    ppermute x13, starting transfers between devices, hop(): return lax.ppermute(block, 'seq', pairs)  18.6 us
    pallas_call x2, Pallas kernels, attention(): call(functools.partial(attention_kernel, chunk, groups, head_size, head_s...  11.6 us
    ppermute x3, waiting for transfers between devices, sum_over(): lax.ppermute(total, axis, [(i, i ^ bit) for i in range(count)])  5.87 us
    pallas_call x4, Pallas kernels, edge(): call(functools.partial(edge_kernel, chunk, touching, bool(lead)), 'edge',...  5.77 us
    ppermute x3, starting transfers between devices, sum_over(): lax.ppermute(total, axis, [(i, i ^ bit) for i in range(count)])  5.1 us
    pallas_call x1, Pallas kernels, pack(): call(pack_kernel, 'pack', [SMEM, SMEM] + [HBM] * len(arrays), VMEM, shape...  3.19 us
    ppermute x1, waiting for transfers between devices, body(): from_mate = lax.ppermute(to_mate, 'seq', swap)  2.97 us
  transfers between devices with their start and end apart: 18, of which 9 were waited for; matrix products, arithmetic and copies ran while one was open for 2% of the time, Pallas kernels for 17%

profile of v9, /device:TPU:0, one launch (start us, length us, event | category | flops | bytes accessed | tf_op | source)
XLA Modules:
  0.0 114.8 jit_solution(8244362766082901059)
XLA Ops:
  0.7 0.6 pad_add_fusion.state_ref
  1.3 0.0 copy-start.13
  1.3 3.2 %pack.1 = bf16[640,1024]{1,0:T(8,128)(2,1)} custom-call(s32[2]{0:T(128)} %pad_add_fusion.state_ref, s32[2]{0:T(128)} %bitcast.62, bf16[128,2048]{1,0:T(8,128)(2,1)} %bitcast.45, bf16[128,2048]{1,0:T(8,128)(2,1)} %bitcast.48, bf16[128,2048]{1,0:T(8,128)(2,1)} %bitcast.31, bf16[128,2048]{1,0:T(8,128)(2,1)} %bitcast.38, bf16[48,2048]{1,0:T(8,128)(2,1)} %bitcast.51, ...), custom_call_target="tpu_custom_call" | custom-call | flops 1 | bytes 1 | tf_op jit(solution)/shard_map/pack/pallas_call | solution.py:128
  4.5 0.0 copy-start
  4.5 0.0 copy-start.1
  4.5 0.5 collective-permute-start
  5.0 0.0 copy-done.15
  5.0 2.9 %collective-permute-done.mate_ref = bf16[640,1024]{1,0:T(8,128)(2,1)S(1)} collective-permute-done((bf16[640,1024]{1,0:T(8,128)(2,1)}, bf16[640,1024]{1,0:T(8,128)(2,1)S(1)}, u32[]{:S(2)}, u32[]{:S(2)}) %collective-permute-start) | collective-permute-done | bytes 1310752 | tf_op jit(solution)/shard_map/ppermute | solution.py:756
  7.9 0.7 pair_lyrics.2.refs_0_
  8.6 4.0 %collective-permute-start.1 = (bf16[192,512]{1,0:T(8,128)(2,1)S(1)}, bf16[192,512]{1,0:T(8,128)(2,1)}, u32[]{:S(2)}, u32[]{:S(2)}) collective-permute-start(bf16[192,512]{1,0:T(8,128)(2,1)S(1)} %pair_lyrics.2.refs_0_), channel_id=1, source_target_pairs={{0,4},{1,5},{2,6},{3,7},{4,0},{5,1},{6,2},{7,3},{8,12},{9,13},{10,... | collective-permute-start | bytes 589832 | tf_op jit(solution)/shard_map/ppermute | solution.py:711
  12.6 0.0 copy-done.1
  12.6 1.5 %edge.6 = bf16[448,512]{1,0:T(8,128)(2,1)} custom-call(s32[2]{0:T(128)S(1)} %copy-done.13, f32[2,128]{1,0:T(2,128)S(1)} %pad_maximum_fusion.gain_ref, bf16[128,2048]{1,0:T(8,128)(2,1)S(1)} %bitcast.32, bf16[128,2048]{1,0:T(8,128)(2,1)S(1)} %bitcast.39, bf16[640,1024]{1,0:T(8,128)(2,1)S(1)} %collective-permute-done.mate_ref, ...), custom_call_target="tpu_custom_call" | custom-call | flops 1 | bytes 1 | tf_op jit(solution)/shard_map/edge/pallas_call | solution.py:184
  14.1 1.6 %collective-permute-start.6 = (bf16[448,512]{1,0:T(8,128)(2,1)}, bf16[448,512]{1,0:T(8,128)(2,1)}, u32[]{:S(2)}, u32[]{:S(2)}) collective-permute-start(bf16[448,512]{1,0:T(8,128)(2,1)} %edge.6), channel_id=1, source_target_pairs={{0,2},{1,3},{2,0},{3,1},{4,6},{5,7},{6,4},{7,5},{8,10},{9,11},{10,... | collective-permute-start | bytes 1376264 | tf_op jit(solution)/shard_map/ppermute | solution.py:711
  15.7 0.7 pair_lyrics.3.refs_0_
  16.4 0.0 copy-start.7
  16.4 0.4 collective-permute-start.3
  16.8 5.9 %collective-permute-done.1.refs_0_.refs_1_ = bf16[192,512]{1,0:T(8,128)(2,1)} collective-permute-done((bf16[192,512]{1,0:T(8,128)(2,1)S(1)}, bf16[192,512]{1,0:T(8,128)(2,1)}, u32[]{:S(2)}, u32[]{:S(2)}) %collective-permute-start.1) | collective-permute-done | bytes 196640 | tf_op jit(solution)/shard_map/ppermute | solution.py:711
  22.7 1.5 %edge.4 = bf16[448,512]{1,0:T(8,128)(2,1)} custom-call(s32[2]{0:T(128)S(1)} %copy-done.13, f32[2,128]{1,0:T(2,128)S(1)} %pad_maximum_fusion.gain_ref, bf16[128,2048]{1,0:T(8,128)(2,1)S(1)} %bitcast.33, bf16[128,2048]{1,0:T(8,128)(2,1)S(1)} %bitcast.40, bf16[640,1024]{1,0:T(8,128)(2,1)S(1)} %collective-permute-done.mate_ref, ...), custom_call_target="tpu_custom_call" | custom-call | flops 1 | bytes 1 | tf_op jit(solution)/shard_map/edge/pallas_call | solution.py:184
  24.2 0.1 collective-permute-start.2
  24.4 1.9 %collective-permute-start.8 = (bf16[192,512]{1,0:T(8,128)(2,1)}, bf16[192,512]{1,0:T(8,128)(2,1)}, u32[]{:S(2)}, u32[]{:S(2)}) collective-permute-start(bf16[192,512]{1,0:T(8,128)(2,1)} %collective-permute-done.1.refs_0_.refs_1_), channel_id=1, source_target_pairs={{0,2},{1,3},{2,0},{3,1},{4,6},{5,7},{6,4},{7,5},{8,10},{9,11},{10,... | collective-permute-start | bytes 589832 | tf_op jit(solution)/shard_map/ppermute | solution.py:711
  26.2 1.4 %edge.7 = bf16[256,512]{1,0:T(8,128)(2,1)} custom-call(s32[2]{0:T(128)S(1)} %copy-done.13, f32[2,128]{1,0:T(2,128)S(1)} %pad_maximum_fusion.gain_ref, bf16[128,2048]{1,0:T(8,128)(2,1)S(1)} %bitcast.34, bf16[128,2048]{1,0:T(8,128)(2,1)S(1)} %bitcast.41, bf16[640,1024]{1,0:T(8,128)(2,1)S(1)} %collective-permute-done.mate_ref, ...), custom_call_target="tpu_custom_call" | custom-call | flops 1 | bytes 1 | tf_op jit(solution)/shard_map/edge/pallas_call | solution.py:184
  27.7 1.5 %collective-permute-start.7 = (bf16[256,512]{1,0:T(8,128)(2,1)}, bf16[256,512]{1,0:T(8,128)(2,1)}, u32[]{:S(2)}, u32[]{:S(2)}) collective-permute-start(bf16[256,512]{1,0:T(8,128)(2,1)} %edge.7), channel_id=1, source_target_pairs={{2,4},{3,5},{4,2},{5,3},{10,12},{11,13},{12,10},{13,11},{18,20},{1... | collective-permute-start | bytes 786440 | tf_op jit(solution)/shard_map/ppermute | solution.py:711
  29.1 2.8 %collective-permute-done.3.refs_0_.refs_1_ = bf16[192,512]{1,0:T(8,128)(2,1)S(1)} collective-permute-done((bf16[192,512]{1,0:T(8,128)(2,1)S(1)}, bf16[192,512]{1,0:T(8,128)(2,1)S(1)}, u32[]{:S(2)}, u32[]{:S(2)}) %collective-permute-start.3) | collective-permute-done | bytes 196640 | tf_op jit(solution)/shard_map/ppermute | solution.py:711
  32.0 1.4 %edge.5 = bf16[256,512]{1,0:T(8,128)(2,1)} custom-call(s32[2]{0:T(128)S(1)} %copy-done.13, f32[2,128]{1,0:T(2,128)S(1)} %pad_maximum_fusion.gain_ref, bf16[128,2048]{1,0:T(8,128)(2,1)S(1)} %bitcast.35, bf16[128,2048]{1,0:T(8,128)(2,1)S(1)} %bitcast.42, bf16[640,1024]{1,0:T(8,128)(2,1)S(1)} %collective-permute-done.mate_ref, ...), custom_call_target="tpu_custom_call" | custom-call | flops 1 | bytes 1 | tf_op jit(solution)/shard_map/edge/pallas_call | solution.py:184
  33.4 1.4 %collective-permute-start.4 = (bf16[256,512]{1,0:T(8,128)(2,1)}, bf16[256,512]{1,0:T(8,128)(2,1)}, u32[]{:S(2)}, u32[]{:S(2)}) collective-permute-start(bf16[256,512]{1,0:T(8,128)(2,1)} %edge.5), channel_id=1, source_target_pairs={{2,4},{3,5},{4,2},{5,3},{10,12},{11,13},{12,10},{13,11},{18,20},{1... | collective-permute-start | bytes 786440 | tf_op jit(solution)/shard_map/ppermute | solution.py:711
  35.4 0.0 copy-start.2
  35.4 0.0 copy-start.3
  35.4 12.6 %collective-permute-done.8.refs_2_ = bf16[192,512]{1,0:T(8,128)(2,1)} collective-permute-done((bf16[192,512]{1,0:T(8,128)(2,1)}, bf16[192,512]{1,0:T(8,128)(2,1)}, u32[]{:S(2)}, u32[]{:S(2)}) %collective-permute-start.8) | collective-permute-done | bytes 196640 | tf_op jit(solution)/shard_map/ppermute | solution.py:711
  48.0 0.0 collective-permute-start.5
  48.0 0.6 fusion
  48.6 1.3 %stack.77.meta_ref = s32[15]{0:T(128)S(1)} concatenate(s32[1]{0:T(128)} %bitcast, s32[1]{0:T(128)} %bitcast.1, s32[1]{0:T(128)} %bitcast.11, s32[1]{0:T(128)} %bitcast.12, s32[1]{0:T(128)S(6)} %copy.28, s32[1]{0:T(128)} %bitcast.13, s32[1]{0:T(128)} %bitcast.14, s32[1]{0:T(128)} %bitcast.15, s32[1]{0:T(128)} %bitcast.16, s32[1]{0:T(128)} %bitcast.17, s32[1]{0:T(128)} %bitcast.18, ...), dimensions={0} | concatenate | bytes 120 | tf_op jit(solution)/shard_map/stack | solution.py:740
  50.0 0.9 prepare_keys.1.key_ref
  50.9 0.0 copy-start.8
  50.9 0.0 copy-start.12
  50.9 0.0 collective-permute-done.6.one_ref
  50.9 0.0 collective-permute-done.7.mid_ref
  50.9 5.8 %attention.2 = (bf16[128,512]{1,0:T(8,128)(2,1)S(1)}, bf16[128,512]{1,0:T(8,128)(2,1)S(1)}, bf16[256,512]{1,0:T(8,128)(2,1)S(1)}, f32[256,512]{1,0:T(8,128)S(1)}...) custom-call(s32[15]{0:T(128)S(1)} %stack.77.meta_ref, ...), custom_call_target="tpu_custom_call" | custom-call | flops 1207959552 | bytes 8388608 | tf_op jit(solution)/shard_map/attention/pallas_call | solution.py:422
  56.8 2.1 %collective-permute-start.12 = (bf16[192,512]{1,0:T(8,128)(2,1)S(1)}, bf16[192,512]{1,0:T(8,128)(2,1)S(1)}, u32[]{:S(2)}, u32[]{:S(2)}) collective-permute-start(bf16[192,512]{1,0:T(8,128)(2,1)S(1)} %get-tuple-element.55), channel_id=1, source_target_pairs={{0,2},{1,3},{2,0},{3,1},{4,6},{5,7},{6,4},{7,5},{8,10},{9,11},{10,... | collective-permute-start | bytes 589832 | tf_op jit(solution)/shard_map/ppermute | solution.py:711
  58.9 0.0 collective-permute-done.5.refs_2_
  58.9 0.0 collective-permute-done.4.mid_ref
  58.9 0.0 collective-permute-done.2.one_ref
  58.9 5.7 %attention.3 = (bf16[128,512]{1,0:T(8,128)(2,1)S(1)}, bf16[128,512]{1,0:T(8,128)(2,1)S(1)}, bf16[256,512]{1,0:T(8,128)(2,1)S(1)}, f32[256,512]{1,0:T(8,128)S(1)}...) custom-call(s32[15]{0:T(128)S(1)} %stack.77.meta_ref, ...), custom_call_target="tpu_custom_call" | custom-call | flops 1207959552 | bytes 8388608 | tf_op jit(solution)/shard_map/attention/pallas_call | solution.py:422
  64.6 0.0 copy-start.5
  64.6 0.1 collective-permute-start.13
  64.7 1.6 %collective-permute-start.9 = (f32[8,128]{1,0:T(8,128)S(1)}, f32[8,128]{1,0:T(8,128)S(1)}, u32[]{:S(2)}, u32[]{:S(2)}) collective-permute-start(f32[8,128]{1,0:T(8,128)S(1)} %get-tuple-element.51), channel_id=1, source_target_pairs={{0,8},{8,0},{16,24},{24,16},{1,9},{9,1},{17,25},{25,17},{2,10},{10... | collective-permute-start | bytes 12296 | tf_op jit(solution)/shard_map/ppermute | solution.py:680
  66.3 2.1 %collective-permute-done.9 = f32[8,128]{1,0:T(8,128)S(1)} collective-permute-done((f32[8,128]{1,0:T(8,128)S(1)}, f32[8,128]{1,0:T(8,128)S(1)}, u32[]{:S(2)}, u32[]{:S(2)}) %collective-permute-start.9) | collective-permute-done | bytes 4128 | tf_op jit(solution)/shard_map/ppermute | solution.py:680
  68.4 1.6 %collective-permute-start.10 = (f32[8,128]{1,0:T(8,128)S(1)}, f32[8,128]{1,0:T(8,128)S(1)}, u32[]{:S(2)}, u32[]{:S(2)}) collective-permute-start(f32[8,128]{1,0:T(8,128)S(1)} %add.51), channel_id=1, source_target_pairs={{0,16},{8,24},{16,0},{24,8},{1,17},{9,25},{17,1},{25,9},{2,18},{10... | collective-permute-start | bytes 12296 | tf_op jit(solution)/shard_map/ppermute | solution.py:680
  70.0 2.0 %collective-permute-done.10 = f32[8,128]{1,0:T(8,128)S(1)} collective-permute-done((f32[8,128]{1,0:T(8,128)S(1)}, f32[8,128]{1,0:T(8,128)S(1)}, u32[]{:S(2)}, u32[]{:S(2)}) %collective-permute-start.10) | collective-permute-done | bytes 4128 | tf_op jit(solution)/shard_map/ppermute | solution.py:680
  72.0 1.9 %collective-permute-start.11 = (f32[8,128]{1,0:T(8,128)S(1)}, f32[8,128]{1,0:T(8,128)S(1)}, u32[]{:S(2)}, u32[]{:S(2)}) collective-permute-start(f32[8,128]{1,0:T(8,128)S(1)} %add.52), channel_id=1, source_target_pairs={{0,2},{1,3},{2,0},{3,1},{4,6},{5,7},{6,4},{7,5},{8,10},{9,11},{10,... | collective-permute-start | bytes 12296 | tf_op jit(solution)/shard_map/ppermute | solution.py:680
  74.0 1.8 %collective-permute-done.11 = f32[8,128]{1,0:T(8,128)S(1)} collective-permute-done((f32[8,128]{1,0:T(8,128)S(1)}, f32[8,128]{1,0:T(8,128)S(1)}, u32[]{:S(2)}, u32[]{:S(2)}) %collective-permute-start.11) | collective-permute-done | bytes 4128 | tf_op jit(solution)/shard_map/ppermute | solution.py:680
  75.7 0.0 collective-permute-done.12.refs_2_
  75.7 0.0 collective-permute-done.13.refs_3_
  75.7 0.1 relay.1
  75.8 2.0 %collective-permute-start.14 = (bf16[448,1024]{1,0:T(8,128)(2,1)S(1)}, bf16[448,1024]{1,0:T(8,128)(2,1)S(1)}, u32[]{:S(2)}, u32[]{:S(2)}) collective-permute-start(bf16[448,1024]{1,0:T(8,128)(2,1)S(1)} %get-tuple-element.57), channel_id=1, source_target_pairs={{0,2},{1,3},{2,0},{3,1},{4,6},{5,7},{6,4},{7,5},{8,10},{9,11},{10,... | collective-permute-start | bytes 2752520 | tf_op jit(solution)/shard_map/ppermute | solution.py:711
  77.9 0.7 collective-permute-start.16
  78.5 2.8 %collective-permute-start.15 = (bf16[208,1024]{1,0:T(8,128)(2,1)S(1)}, bf16[208,1024]{1,0:T(8,128)(2,1)S(1)}, u32[]{:S(2)}, u32[]{:S(2)}) collective-permute-start(bf16[208,1024]{1,0:T(8,128)(2,1)S(1)} %get-tuple-element.58), channel_id=1, source_target_pairs={{0,4},{1,5},{2,6},{3,7},{4,0},{5,1},{6,2},{7,3},{8,12},{9,13},{10,... | collective-permute-start | bytes 1277960 | tf_op jit(solution)/shard_map/ppermute | solution.py:711
  81.4 24.9 %collective-permute-done.15.two_ref = bf16[208,1024]{1,0:T(8,128)(2,1)S(1)} collective-permute-done((bf16[208,1024]{1,0:T(8,128)(2,1)S(1)}, bf16[208,1024]{1,0:T(8,128)(2,1)S(1)}, u32[]{:S(2)}, u32[]{:S(2)}) %collective-permute-start.15) | collective-permute-done | bytes 426016 | tf_op jit(solution)/shard_map/ppermute | solution.py:711
  106.3 0.0 collective-permute-done.14.one_ref
  106.3 0.9 finish_lyric.1
  107.2 0.0 collective-permute-done.16.mid_ref
  107.2 2.3 %finish_audio.1 = (bf16[128,2048]{1,0:T(8,128)(2,1)}, bf16[128,2048]{1,0:T(8,128)(2,1)}, bf16[128,2048]{1,0:T(8,128)(2,1)}, bf16[128,2048]{1,0:T(8,128)(2,1)}, bf16[624,1024]{1,0:T(8,128)(2,1)S(1)}) custom-call(s32[2]{0:T(128)S(1)} %copy-done.13, f32[2,128]{1,0:T(2,128)S(1)} %pad_maximum_fusion.gain_ref, bf16[128,2048]{1,0:T(8,128)(2,1)S(1)} %bitcast.37, ...), custom_call_target="tpu_custom_call" | custom-call | flops 1 | bytes 1 | tf_op jit(solution)/shard_map/finish_audio/pallas_call | solution.py:502
  109.5 0.1 collective-permute-start.17
  109.6 3.0 %collective-permute-done.17.mate_ref = bf16[624,1024]{1,0:T(8,128)(2,1)S(1)} collective-permute-done((bf16[624,1024]{1,0:T(8,128)(2,1)S(1)}, bf16[624,1024]{1,0:T(8,128)(2,1)S(1)}, u32[]{:S(2)}, u32[]{:S(2)}) %collective-permute-start.17) | collective-permute-done | bytes 1277984 | tf_op jit(solution)/shard_map/ppermute | solution.py:796
  112.6 2.2 %join.1 = (bf16[128,2048]{1,0:T(8,128)(2,1)}, bf16[128,2048]{1,0:T(8,128)(2,1)}, bf16[128,2048]{1,0:T(8,128)(2,1)}, bf16[128,2048]{1,0:T(8,128)(2,1)}, bf16[48,2...) custom-call(s32[2]{0:T(128)S(1)} %copy-done.13, ...), custom_call_target="tpu_custom_call", output_to_operand_aliasing={{0}: (4, {}), {1}: (5, {}), {2}: (6, {}), {3}: (7, {})} | custom-call | flops 1 | bytes 1 | tf_op jit(solution)/shard_map/join/pallas_call | solution.py:608
  (27 shorter events, 0.1 us)
Async XLA Ops:
  1.3 3.8 %copy-start.15 = (f32[128]{0:T(128)S(1)}, f32[128]{0:T(128)}, u32[]{:S(2)}) copy-start(f32[128]{0:T(128)} %param.16) | copy-start | bytes 1540
  1.3 3.8 %copy-start.16 = (f32[128]{0:T(128)S(1)}, f32[128]{0:T(128)}, u32[]{:S(2)}) copy-start(f32[128]{0:T(128)} %param.15) | copy-start | bytes 1540
  1.3 6.6 %copy-start.4 = (bf16[1,48,2048]{2,1,0:T(8,128)(2,1)S(1)}, bf16[1,48,2048]{2,1,0:T(8,128)(2,1)}, u32[]{:S(2)}) copy-start(bf16[1,48,2048]{2,1,0:T(8,128)(2,1)} %param.13) | copy-start | bytes 589828
  1.3 6.6 %copy-start.6 = (bf16[1,48,2048]{2,1,0:T(8,128)(2,1)S(1)}, bf16[1,48,2048]{2,1,0:T(8,128)(2,1)}, u32[]{:S(2)}) copy-start(bf16[1,48,2048]{2,1,0:T(8,128)(2,1)} %param.14) | copy-start | bytes 589828
  1.3 6.6 %copy-start.13 = (s32[2]{0:T(128)S(1)}, s32[2]{0:T(128)}, u32[]{:S(2)}) copy-start(s32[2]{0:T(128)} %pad_add_fusion.state_ref) | copy-start | bytes 28
  4.5 8.2 %copy-start = (bf16[1,128,2048]{2,1,0:T(8,128)(2,1)S(1)}, bf16[1,128,2048]{2,1,0:T(8,128)(2,1)}, u32[]{:S(2)}) copy-start(bf16[1,128,2048]{2,1,0:T(8,128)(2,1)} %param.11) | copy-start | bytes 1572868
  4.5 8.1 %copy-start.1 = (bf16[1,128,2048]{2,1,0:T(8,128)(2,1)S(1)}, bf16[1,128,2048]{2,1,0:T(8,128)(2,1)}, u32[]{:S(2)}) copy-start(bf16[1,128,2048]{2,1,0:T(8,128)(2,1)} %param.12) | copy-start | bytes 1572868
  4.5 3.4 %collective-permute-start = (bf16[640,1024]{1,0:T(8,128)(2,1)}, bf16[640,1024]{1,0:T(8,128)(2,1)S(1)}, u32[]{:S(2)}, u32[]{:S(2)}) collective-permute-start(bf16[640,1024]{1,0:T(8,128)(2,1)} %pack.1), channel_id=1, source_target_pairs={{0,1},{1,0},{2,3},{3,2},{4,5},{5,4},{6,7},{7,6},{8,9},{9,8},{10,11... | collective-permute-start | bytes 3932168 | tf_op jit(solution)/shard_map/ppermute | solution.py:756
  8.6 5.5 %copy-start.9 = (bf16[192,512]{1,0:T(8,128)(2,1)}, bf16[192,512]{1,0:T(8,128)(2,1)S(1)}, u32[]{:S(2)}) copy-start(bf16[192,512]{1,0:T(8,128)(2,1)S(1)} %pair_lyrics.2.refs_0_) | copy-start | bytes 589828
  8.6 14.1 %collective-permute-start.1 = (bf16[192,512]{1,0:T(8,128)(2,1)S(1)}, bf16[192,512]{1,0:T(8,128)(2,1)}, u32[]{:S(2)}, u32[]{:S(2)}) collective-permute-start(bf16[192,512]{1,0:T(8,128)(2,1)S(1)} %pair_lyrics.2.refs_0_), channel_id=1, source_target_pairs={{0,4},{1,5},{2,6},{3,7},{4,0},{5,1},{6,2},{7,3},{8,12},{9,13},{10,... | collective-permute-start | bytes 589832 | tf_op jit(solution)/shard_map/ppermute | solution.py:711
  14.1 36.8 %collective-permute-start.6 = (bf16[448,512]{1,0:T(8,128)(2,1)}, bf16[448,512]{1,0:T(8,128)(2,1)}, u32[]{:S(2)}, u32[]{:S(2)}) collective-permute-start(bf16[448,512]{1,0:T(8,128)(2,1)} %edge.6), channel_id=1, source_target_pairs={{0,2},{1,3},{2,0},{3,1},{4,6},{5,7},{6,4},{7,5},{8,10},{9,11},{10,... | collective-permute-start | bytes 1376264 | tf_op jit(solution)/shard_map/ppermute | solution.py:711
  16.4 7.8 %copy-start.7 = (bf16[192,512]{1,0:T(8,128)(2,1)}, bf16[192,512]{1,0:T(8,128)(2,1)S(1)}, u32[]{:S(2)}) copy-start(bf16[192,512]{1,0:T(8,128)(2,1)S(1)} %pair_lyrics.3.refs_0_) | copy-start | bytes 589828
  16.4 15.6 %collective-permute-start.3 = (bf16[192,512]{1,0:T(8,128)(2,1)S(1)}, bf16[192,512]{1,0:T(8,128)(2,1)S(1)}, u32[]{:S(2)}, u32[]{:S(2)}) collective-permute-start(bf16[192,512]{1,0:T(8,128)(2,1)S(1)} %pair_lyrics.3.refs_0_), channel_id=1, source_target_pairs={{0,4},{1,5},{2,6},{3,7},{4,0},{5,1},{6,2},{7,3},{8,12},{9,13},{10,... | collective-permute-start | bytes 589832 | tf_op jit(solution)/shard_map/ppermute | solution.py:711
  24.2 34.6 %collective-permute-start.2 = (bf16[448,512]{1,0:T(8,128)(2,1)}, bf16[448,512]{1,0:T(8,128)(2,1)}, u32[]{:S(2)}, u32[]{:S(2)}) collective-permute-start(bf16[448,512]{1,0:T(8,128)(2,1)} %edge.4), channel_id=1, source_target_pairs={{0,2},{1,3},{2,0},{3,1},{4,6},{5,7},{6,4},{7,5},{8,10},{9,11},{10,... | collective-permute-start | bytes 1376264 | tf_op jit(solution)/shard_map/ppermute | solution.py:711
  24.4 23.6 %collective-permute-start.8 = (bf16[192,512]{1,0:T(8,128)(2,1)}, bf16[192,512]{1,0:T(8,128)(2,1)}, u32[]{:S(2)}, u32[]{:S(2)}) collective-permute-start(bf16[192,512]{1,0:T(8,128)(2,1)} %collective-permute-done.1.refs_0_.refs_1_), channel_id=1, source_target_pairs={{0,2},{1,3},{2,0},{3,1},{4,6},{5,7},{6,4},{7,5},{8,10},{9,11},{10,... | collective-permute-start | bytes 589832 | tf_op jit(solution)/shard_map/ppermute | solution.py:711
  27.6 20.4 %copy-start.14 = (s32[1,1,2]{2,1,0:T(1,128)S(1)}, s32[1,1,2]{2,1,0:T(1,128)}, u32[]{:S(2)}) copy-start(s32[1,1,2]{2,1,0:T(1,128)} %param.18) | copy-start | bytes 28
  27.7 23.3 %collective-permute-start.7 = (bf16[256,512]{1,0:T(8,128)(2,1)}, bf16[256,512]{1,0:T(8,128)(2,1)}, u32[]{:S(2)}, u32[]{:S(2)}) collective-permute-start(bf16[256,512]{1,0:T(8,128)(2,1)} %edge.7), channel_id=1, source_target_pairs={{2,4},{3,5},{4,2},{5,3},{10,12},{11,13},{12,10},{13,11},{18,20},{1... | collective-permute-start | bytes 786440 | tf_op jit(solution)/shard_map/ppermute | solution.py:711
  32.0 1.4 %copy-start.11 = (bf16[192,512]{1,0:T(8,128)(2,1)}, bf16[192,512]{1,0:T(8,128)(2,1)S(1)}, u32[]{:S(2)}) copy-start(bf16[192,512]{1,0:T(8,128)(2,1)S(1)} %collective-permute-done.3.refs_0_.refs_1_) | copy-start | bytes 589828
  33.4 25.5 %collective-permute-start.4 = (bf16[256,512]{1,0:T(8,128)(2,1)}, bf16[256,512]{1,0:T(8,128)(2,1)}, u32[]{:S(2)}, u32[]{:S(2)}) collective-permute-start(bf16[256,512]{1,0:T(8,128)(2,1)} %edge.5), channel_id=1, source_target_pairs={{2,4},{3,5},{4,2},{5,3},{10,12},{11,13},{12,10},{13,11},{18,20},{1... | collective-permute-start | bytes 786440 | tf_op jit(solution)/shard_map/ppermute | solution.py:711
  35.4 15.5 %copy-start.2 = (bf16[1,128,2048]{2,1,0:T(8,128)(2,1)S(1)}, bf16[1,128,2048]{2,1,0:T(8,128)(2,1)}, u32[]{:S(2)}) copy-start(bf16[1,128,2048]{2,1,0:T(8,128)(2,1)} %param.10) | copy-start | bytes 1572868
  35.4 15.5 %copy-start.3 = (bf16[1,128,2048]{2,1,0:T(8,128)(2,1)S(1)}, bf16[1,128,2048]{2,1,0:T(8,128)(2,1)}, u32[]{:S(2)}) copy-start(bf16[1,128,2048]{2,1,0:T(8,128)(2,1)} %param.17) | copy-start | bytes 1572868
  48.0 10.8 %collective-permute-start.5 = (bf16[192,512]{1,0:T(8,128)(2,1)}, bf16[192,512]{1,0:T(8,128)(2,1)}, u32[]{:S(2)}, u32[]{:S(2)}) collective-permute-start(bf16[192,512]{1,0:T(8,128)(2,1)} %copy-done.11), channel_id=1, source_target_pairs={{0,2},{1,3},{2,0},{3,1},{4,6},{5,7},{6,4},{7,5},{8,10},{9,11},{10,... | collective-permute-start | bytes 589832 | tf_op jit(solution)/shard_map/ppermute | solution.py:711
  49.9 1.0 copy-start.10
  50.9 8.0 %copy-start.8 = (bf16[192,512]{1,0:T(8,128)(2,1)S(1)}, bf16[192,512]{1,0:T(8,128)(2,1)}, u32[]{:S(2)}) copy-start(bf16[192,512]{1,0:T(8,128)(2,1)} %copy-done.7) | copy-start | bytes 589828
  50.9 8.0 %copy-start.12 = (bf16[192,512]{1,0:T(8,128)(2,1)S(1)}, bf16[192,512]{1,0:T(8,128)(2,1)}, u32[]{:S(2)}) copy-start(bf16[192,512]{1,0:T(8,128)(2,1)} %copy-done.11) | copy-start | bytes 589828
  56.8 19.0 %collective-permute-start.12 = (bf16[192,512]{1,0:T(8,128)(2,1)S(1)}, bf16[192,512]{1,0:T(8,128)(2,1)S(1)}, u32[]{:S(2)}, u32[]{:S(2)}) collective-permute-start(bf16[192,512]{1,0:T(8,128)(2,1)S(1)} %get-tuple-element.55), channel_id=1, source_target_pairs={{0,2},{1,3},{2,0},{3,1},{4,6},{5,7},{6,4},{7,5},{8,10},{9,11},{10,... | collective-permute-start | bytes 589832 | tf_op jit(solution)/shard_map/ppermute | solution.py:711
  64.6 41.6 %copy-start.5 = (bf16[1,48,2048]{2,1,0:T(8,128)(2,1)S(1)}, bf16[1,48,2048]{2,1,0:T(8,128)(2,1)}, u32[]{:S(2)}) copy-start(bf16[1,48,2048]{2,1,0:T(8,128)(2,1)} %param.13) | copy-start | bytes 589828
  64.6 11.1 %collective-permute-start.13 = (bf16[192,512]{1,0:T(8,128)(2,1)S(1)}, bf16[192,512]{1,0:T(8,128)(2,1)S(1)}, u32[]{:S(2)}, u32[]{:S(2)}) collective-permute-start(bf16[192,512]{1,0:T(8,128)(2,1)S(1)} %get-tuple-element.56), channel_id=1, source_target_pairs={{0,2},{1,3},{2,0},{3,1},{4,6},{5,7},{6,4},{7,5},{8,10},{9,11},{10,... | collective-permute-start | bytes 589832 | tf_op jit(solution)/shard_map/ppermute | solution.py:711
  64.7 3.6 %collective-permute-start.9 = (f32[8,128]{1,0:T(8,128)S(1)}, f32[8,128]{1,0:T(8,128)S(1)}, u32[]{:S(2)}, u32[]{:S(2)}) collective-permute-start(f32[8,128]{1,0:T(8,128)S(1)} %get-tuple-element.51), channel_id=1, source_target_pairs={{0,8},{8,0},{16,24},{24,16},{1,9},{9,1},{17,25},{25,17},{2,10},{10... | collective-permute-start | bytes 12296 | tf_op jit(solution)/shard_map/ppermute | solution.py:680
  68.4 3.6 %collective-permute-start.10 = (f32[8,128]{1,0:T(8,128)S(1)}, f32[8,128]{1,0:T(8,128)S(1)}, u32[]{:S(2)}, u32[]{:S(2)}) collective-permute-start(f32[8,128]{1,0:T(8,128)S(1)} %add.51), channel_id=1, source_target_pairs={{0,16},{8,24},{16,0},{24,8},{1,17},{9,25},{17,1},{25,9},{2,18},{10... | collective-permute-start | bytes 12296 | tf_op jit(solution)/shard_map/ppermute | solution.py:680
  72.0 3.7 %collective-permute-start.11 = (f32[8,128]{1,0:T(8,128)S(1)}, f32[8,128]{1,0:T(8,128)S(1)}, u32[]{:S(2)}, u32[]{:S(2)}) collective-permute-start(f32[8,128]{1,0:T(8,128)S(1)} %add.52), channel_id=1, source_target_pairs={{0,2},{1,3},{2,0},{3,1},{4,6},{5,7},{6,4},{7,5},{8,10},{9,11},{10,... | collective-permute-start | bytes 12296 | tf_op jit(solution)/shard_map/ppermute | solution.py:680
  75.8 30.4 %collective-permute-start.14 = (bf16[448,1024]{1,0:T(8,128)(2,1)S(1)}, bf16[448,1024]{1,0:T(8,128)(2,1)S(1)}, u32[]{:S(2)}, u32[]{:S(2)}) collective-permute-start(bf16[448,1024]{1,0:T(8,128)(2,1)S(1)} %get-tuple-element.57), channel_id=1, source_target_pairs={{0,2},{1,3},{2,0},{3,1},{4,6},{5,7},{6,4},{7,5},{8,10},{9,11},{10,... | collective-permute-start | bytes 2752520 | tf_op jit(solution)/shard_map/ppermute | solution.py:711
  77.9 29.3 %collective-permute-start.16 = (bf16[256,1024]{1,0:T(8,128)(2,1)S(1)}, bf16[256,1024]{1,0:T(8,128)(2,1)S(1)}, u32[]{:S(2)}, u32[]{:S(2)}) collective-permute-start(bf16[256,1024]{1,0:T(8,128)(2,1)S(1)} %get-tuple-element.63), channel_id=1, source_target_pairs={{2,4},{3,5},{4,2},{5,3},{10,12},{11,13},{12,10},{13,11},{18,20},{1... | collective-permute-start | bytes 1572872 | tf_op jit(solution)/shard_map/ppermute | solution.py:711
  78.5 27.7 %collective-permute-start.15 = (bf16[208,1024]{1,0:T(8,128)(2,1)S(1)}, bf16[208,1024]{1,0:T(8,128)(2,1)S(1)}, u32[]{:S(2)}, u32[]{:S(2)}) collective-permute-start(bf16[208,1024]{1,0:T(8,128)(2,1)S(1)} %get-tuple-element.58), channel_id=1, source_target_pairs={{0,4},{1,5},{2,6},{3,7},{4,0},{5,1},{6,2},{7,3},{8,12},{9,13},{10,... | collective-permute-start | bytes 1277960 | tf_op jit(solution)/shard_map/ppermute | solution.py:711
  109.5 3.1 %collective-permute-start.17 = (bf16[624,1024]{1,0:T(8,128)(2,1)S(1)}, bf16[624,1024]{1,0:T(8,128)(2,1)S(1)}, u32[]{:S(2)}, u32[]{:S(2)}) collective-permute-start(bf16[624,1024]{1,0:T(8,128)(2,1)S(1)} %get-tuple-element.75), channel_id=1, source_target_pairs={{0,1},{1,0},{2,3},{3,2},{4,5},{5,4},{6,7},{7,6},{8,9},{9,8},{10,11... | collective-permute-start | bytes 3833864 | tf_op jit(solution)/shard_map/ppermute | solution.py:796

commit v10 on v9

--- a/solution.py
+++ b/solution.py
@@ -136,7 +136,8 @@
     )(state, align, *arrays)
 
 
-def pair_kernel(chunk, state_ref, gain_ref, key_ref, value_ref, mate_ref, pair_ref):
+def pair_kernel(chunk, state_ref, gain_ref, key_ref, value_ref, mate_ref, *refs):
+    pair_ref = refs[-1]
     rows = key_ref.shape[0]
     first = mate_ref.shape[0] - ALIGN_ROWS - 2 * rows
     own = chunk_of(key_ref, state_ref[0], chunk)
@@ -149,15 +150,15 @@
     pair_ref[3 * rows :, :] = mate_ref[first + rows : first + 2 * rows, cols]
 
 
-def pair_lyrics(state, chunk, gains, lyric_key, lyric_value, mate):
+def pair_lyrics(state, chunk, gains, lyric_key, lyric_value, mate, after):
     rows, width = lyric_key.shape
     return call(
         functools.partial(pair_kernel, chunk),
         "pair_lyrics",
-        [SMEM] + [VMEM] * 4,
+        [SMEM] + [VMEM] * 4 + [ANY] * len(after),
         VMEM,
         shape(4 * rows, width // 2 // CHUNKS),
-    )(state, gains, lyric_key, lyric_value, mate)
+    )(state, gains, lyric_key, lyric_value, mate, *after)
 
 
 def edge_kernel(
@@ -219,7 +220,7 @@
     exchanged = len(groups) == 4
     inputs = 3 if exchanged else 1
     lyric_in, refs = refs[:inputs], refs[inputs:]
-    earlier, refs = refs[: 3 * chunk], refs[3 * chunk :]
+    earlier, refs = refs[: 3 * chunk], refs[3 * chunk + (chunk if exchanged else 0) :]
     window = one_ref.shape[0] - 2 * frames
     out_ref, grad_query_ref, to_mate_ref, key_grad_ref, value_grad_ref = refs[:5]
     to_one_ref, to_mid_ref, gain_grad_ref = refs[5:8]
@@ -403,9 +404,13 @@
         for number in range(HEADS_PER_STEP):
             one_head(step * HEADS_PER_STEP + number)
 
+    if exchanged and sent:
+        to_two_ref = lyric_out[2]
+        to_two_ref[window:, :] = split_rows(gain_grad_ref[...], size)
+
 
 def attention(
-    chunk, meta, gains, query, cot, value, key, mate, one, mid, lyrics, groups, earlier
+    chunk, meta, gains, query, cot, value, key, mate, one, mid, lyrics, groups, earlier, after
 ):
     frames, width = query.shape
     head_size = gains.shape[1]
@@ -419,10 +424,12 @@
     out_shape += [shape(2 * frames, size, dtype) for dtype in (bf16, f32, f32)]
     out_shape += [shape(one.shape[0], sent), shape(2 * frames, sent), shape(8, head_size, f32)]
     out_shape += [shape(slot, size)] * len(lyrics)
+    if len(lyrics) > 1 and chunk == CHUNKS - 1:
+        out_shape[-1] = shape(slot + GAIN_ROWS, size)
     return call(
         functools.partial(attention_kernel, chunk, groups, head_size, head_size ** (-0.5)),
         "attention",
-        [SMEM] + [VMEM] * (8 + len(lyrics) + len(earlier)),
+        [SMEM] + [VMEM] * (8 + len(lyrics) + len(earlier)) + [ANY] * len(after),
         [VMEM] * len(out_shape),
         out_shape,
         limit=ATTENTION_VMEM_LIMIT,
@@ -432,7 +439,7 @@
             transcendentals=2 * key_rows * frames * (size // head_size),
         ),
         scratch_shapes=[pltpu.VMEM((frames + lyric_rows, 2 * frames), f32)],
-    )(meta, gains, query, cot, value, key, mate, one, mid, *lyrics, *earlier)
+    )(meta, gains, query, cot, value, key, mate, one, mid, *lyrics, *earlier, *after)
 
 
 def finish_audio_kernel(
@@ -510,39 +517,46 @@
     )(state, gains, raw, mate, one, mid, *chunks, *lyric)
 
 
-def relay_kernel(total_ref, later_ref, *refs):
-    parts, arrived, (out_ref, _) = refs[:CHUNKS], refs[CHUNKS : 2 * CHUNKS], refs[2 * CHUNKS :]
+def relay_kernel(gain_ref, later_ref, *refs):
+    parts, arrived, (out_ref, _, total_ref) = (
+        refs[:CHUNKS],
+        refs[CHUNKS : 2 * CHUNKS],
+        refs[2 * CHUNKS :],
+    )
     rows, size = parts[0].shape
     for chunk, (part_ref, arrived_ref) in enumerate(zip(parts, arrived)):
-        out_ref[0:rows, chunk_cols(chunk, size)] = (
-            part_ref[...].astype(jnp.float32) + arrived_ref[...].astype(jnp.float32)
+        out_ref[:, chunk_cols(chunk, size)] = (
+            part_ref[...].astype(jnp.float32) + arrived_ref[0:rows, :].astype(jnp.float32)
         ).astype(jnp.bfloat16)
-    out_ref[rows:, :] = split_rows(total_ref[...], out_ref.shape[1])
-
-
-def relay(parts, arrived, total, later):
+    total_ref[...] = gain_ref[...] + joined_rows(arrived[-1][rows:, :], gain_ref.shape[1])
+
+
+def relay(parts, arrived, gain, later):
     rows, size = parts[0].shape
     return call(
         relay_kernel,
         "relay",
         [VMEM, ANY] + [VMEM] * (2 * CHUNKS),
-        [VMEM, ANY],
-        [shape(rows + GAIN_ROWS, CHUNKS * size), shape(*later.shape)],
+        [VMEM, ANY, VMEM],
+        [
+            shape(rows, CHUNKS * size),
+            shape(*later.shape),
+            shape(*gain.shape, jnp.float32),
+        ],
         input_output_aliases={1: 1},
-    )(total, later, *parts, *arrived)
+    )(gain, later, *parts, *arrived)
 
 
 def finish_lyric_kernel(
     state_ref, gain_ref, raw_ref, mate_ref, one_ref, two_ref, sum_ref, *refs
 ):
-    held_refs, (own_ref, to_mate_ref, total_ref) = refs[:CHUNKS], refs[CHUNKS:]
+    held_refs, (own_ref, to_mate_ref) = refs[:CHUNKS], refs[CHUNKS:]
     rows = raw_ref.shape[0]
     head_size = gain_ref.shape[1]
     k_gain = gain_ref[1:2, :]
     size = held_refs[0].shape[1]
     first = mate_ref.shape[0] - ALIGN_ROWS - 2 * rows
-    total_ref[...] = sum_ref[...] + joined_rows(two_ref[4 * rows :, :], head_size)
-    to_mate_ref[2 * rows :, :] = split_rows(total_ref[...], to_mate_ref.shape[1])
+    to_mate_ref[2 * rows :, :] = split_rows(sum_ref[...], to_mate_ref.shape[1])
     raw_keys = raw_ref[:, half_of(raw_ref, state_ref[0])]
     for head in range(own_ref.shape[1] // head_size):
         cols = slice(head * head_size, (head + 1) * head_size)
@@ -567,12 +581,8 @@
         finish_lyric_kernel,
         "finish_lyric",
         [SMEM] + [VMEM] * (6 + len(held)),
-        [VMEM] * 3,
-        [
-            shape(2 * rows, half),
-            shape(2 * rows + GAIN_ROWS, half),
-            shape(*total.shape, jnp.float32),
-        ],
+        [VMEM] * 2,
+        [shape(2 * rows, half), shape(2 * rows + GAIN_ROWS, half)],
     )(state, gains, raw, mate, one, two, total, *held)
 
 
@@ -757,21 +767,21 @@
     chunks, parts, earlier, arrived = [], [], [], []
     after = []
     for chunk in range(CHUNKS):
-        before = after
+        before, one_before = after, lyrics[2:] if chunk else []
         if hops:
-            pair = pair_lyrics(state, chunk, gains, lyric_keys[0], lyric_values[0], mate)
+            pair = pair_lyrics(state, chunk, gains, lyric_keys[0], lyric_values[0], mate, before)
             two = hop(pair, across)
             lyrics = [pair, two, hop(two, partners)]
             lead, after = [pair], [two]
         else:
             lyrics, lead = [gathered], []
-        one = hop(edge(state, chunk, 1, gains, keys[0], values[0], mate, lead, before), partners)
+        one = hop(edge(state, chunk, 1, gains, keys[0], values[0], mate, lead, one_before), partners)
         mid = hop(edge(state, chunk, 0, gains, keys[0], values[0], mate, [], after), between)
         if not chunk:
             key_low = prepare_keys(state, gains, keys[0], mate, after)
         results = attention(
             chunk, meta, gains, queries[0], cotangent[0], values[0], key_low, mate, one, mid,
-            lyrics, groups, earlier,
+            lyrics, groups, earlier, arrived,
         )
         chunks += results[:5]
         earlier = [*earlier, *results[5:8]]
@@ -783,10 +793,12 @@
     mid = hop(to_mid, between)
     to_mate = []
     if hops:
-        gain_total = sum_over(sum_over(gain_part, "song", bits_of(songs)), "seq", [2])
-        to_two, to_one = relay([part[1] for part in parts], arrived, gain_total, to_one)
+        to_two, to_one, gain_total = relay(
+            [part[1] for part in parts], arrived, gain_part, to_one
+        )
+        gain_total = sum_over(sum_over(gain_total, "song", bits_of(songs)), "seq", [4])
         two, one = hop(to_two, across), hop(to_one, partners)
-        own_half, part_to_mate, gain_total = finish_lyric(
+        own_half, part_to_mate = finish_lyric(
             state, gains, lyric_keys[0], mate, [part[0] for part in parts], one, two, gain_total
         )
         to_mate = [part_to_mate]

time: 115 us -> 112 us (0.974)
  waiting for transfers between devices: 58 us -> 56 us
    ppermute x13, waiting for transfers between devices: 46.3 us -> 26.9 us  [hop(): return lax.ppermute(block, 'seq', pairs)]
    ppermute x3, waiting for transfers between devices: 5.87 us -> 23.3 us  [sum_over(): lax.ppermute(total, axis, [(i, i ^ bit) for i in range(count)])]
    ppermute x13, starting transfers between devices: 18.6 us -> 20.7 us  [hop(): return lax.ppermute(block, 'seq', pairs)]
    ppermute x3, starting transfers between devices: 5.1 us -> 3.08 us  [sum_over(): lax.ppermute(total, axis, [(i, i ^ bit) for i in range(count)])]
  transfers between devices with their start and end apart: 18 -> 18, of which waited for: 9 -> 11; matrix products, arithmetic and copies ran while one was open for 2% -> 2% of each run, Pallas kernels for 17% -> 12%
where the time goes in v10:
time: 112 us
  waiting for transfers between devices  56 us (50%)
  Pallas kernels  27.2 us (24%)
  starting transfers between devices  24.4 us (22%)
  local copies, waits for them, and re-layouts  2.02 us (2%)
  between operations  1.54 us (1%)
    ppermute x13, waiting for transfers between devices, hop(): return lax.ppermute(block, 'seq', pairs)  26.9 us
    ppermute x3, waiting for transfers between devices, sum_over(): lax.ppermute(total, axis, [(i, i ^ bit) for i in range(count)])  23.3 us
    ppermute x13, starting transfers between devices, hop(): return lax.ppermute(block, 'seq', pairs)  20.7 us
    pallas_call x2, Pallas kernels, attention(): call(functools.partial(attention_kernel, chunk, groups, head_size, head_s...  11.2 us
    pallas_call x4, Pallas kernels, edge(): call(functools.partial(edge_kernel, chunk, touching, bool(lead)), 'edge',...  5.08 us
    pallas_call x1, Pallas kernels, pack(): call(pack_kernel, 'pack', [SMEM, SMEM] + [HBM] * len(arrays), VMEM, shape...  3.18 us
    ppermute x3, starting transfers between devices, sum_over(): lax.ppermute(total, axis, [(i, i ^ bit) for i in range(count)])  3.08 us
    ppermute x1, waiting for transfers between devices, body(): from_mate = lax.ppermute(to_mate, 'seq', swap)  2.97 us
  transfers between devices with their start and end apart: 18, of which 11 were waited for; matrix products, arithmetic and copies ran while one was open for 2% of the time, Pallas kernels for 12%

profile of v10, /device:TPU:0, one launch (start us, length us, event | category | flops | bytes accessed | tf_op | source)
XLA Modules:
  0.0 111.8 jit_solution(14961094121330953160)
XLA Ops:
  0.7 0.6 pad_add_fusion.state_ref
  1.3 0.0 copy-start.6
  1.3 3.2 %pack.1 = bf16[640,1024]{1,0:T(8,128)(2,1)} custom-call(s32[2]{0:T(128)} %pad_add_fusion.state_ref, s32[2]{0:T(128)} %bitcast.62, bf16[128,2048]{1,0:T(8,128)(2,1)} %bitcast.45, bf16[128,2048]{1,0:T(8,128)(2,1)} %bitcast.48, bf16[128,2048]{1,0:T(8,128)(2,1)} %bitcast.31, bf16[128,2048]{1,0:T(8,128)(2,1)} %bitcast.38, bf16[48,2048]{1,0:T(8,128)(2,1)} %bitcast.51, ...), custom_call_target="tpu_custom_call" | custom-call | flops 1 | bytes 1 | tf_op jit(solution)/shard_map/pack/pallas_call | solution.py:128
  4.5 0.0 copy-start
  4.5 0.0 copy-start.1
  4.5 0.5 collective-permute-start
  5.0 0.0 copy-done.8
  5.0 0.0 copy-done.9
  5.0 2.9 %collective-permute-done.mate_ref = bf16[640,1024]{1,0:T(8,128)(2,1)S(1)} collective-permute-done((bf16[640,1024]{1,0:T(8,128)(2,1)}, bf16[640,1024]{1,0:T(8,128)(2,1)S(1)}, u32[]{:S(2)}, u32[]{:S(2)}) %collective-permute-start) | collective-permute-done | bytes 1310752 | tf_op jit(solution)/shard_map/ppermute | solution.py:766
  7.9 0.0 copy-done.4
  7.9 0.0 copy-done.5
  7.9 0.0 copy-done.6
  7.9 0.7 pair_lyrics.2.refs_0_
  8.6 4.0 %collective-permute-start.1 = (bf16[192,512]{1,0:T(8,128)(2,1)S(1)}, bf16[192,512]{1,0:T(8,128)(2,1)S(1)}, u32[]{:S(2)}, u32[]{:S(2)}) collective-permute-start(bf16[192,512]{1,0:T(8,128)(2,1)S(1)} %pair_lyrics.2.refs_0_), channel_id=1, source_target_pairs={{0,4},{1,5},{2,6},{3,7},{4,0},{5,1},{6,2},{7,3},{8,12},{9,13},{10,... | collective-permute-start | bytes 589832 | tf_op jit(solution)/shard_map/ppermute | solution.py:721
  12.6 1.5 %edge.6 = bf16[448,512]{1,0:T(8,128)(2,1)} custom-call(s32[2]{0:T(128)S(1)} %copy-done.6, f32[2,128]{1,0:T(2,128)S(1)} %pad_maximum_fusion.gain_ref, bf16[128,2048]{1,0:T(8,128)(2,1)S(1)} %bitcast.32, bf16[128,2048]{1,0:T(8,128)(2,1)S(1)} %bitcast.39, bf16[640,1024]{1,0:T(8,128)(2,1)S(1)} %collective-permute-done.mate_ref, ...), custom_call_target="tpu_custom_call" | custom-call | flops 1 | bytes 1 | tf_op jit(solution)/shard_map/edge/pallas_call | solution.py:185
  14.1 1.6 %collective-permute-start.7 = (bf16[448,512]{1,0:T(8,128)(2,1)}, bf16[448,512]{1,0:T(8,128)(2,1)}, u32[]{:S(2)}, u32[]{:S(2)}) collective-permute-start(bf16[448,512]{1,0:T(8,128)(2,1)} %edge.6), channel_id=1, source_target_pairs={{0,2},{1,3},{2,0},{3,1},{4,6},{5,7},{6,4},{7,5},{8,10},{9,11},{10,... | collective-permute-start | bytes 1376264 | tf_op jit(solution)/shard_map/ppermute | solution.py:721
  15.7 6.5 %collective-permute-done.1.refs_0_.refs_1_ = bf16[192,512]{1,0:T(8,128)(2,1)S(1)} collective-permute-done((bf16[192,512]{1,0:T(8,128)(2,1)S(1)}, bf16[192,512]{1,0:T(8,128)(2,1)S(1)}, u32[]{:S(2)}, u32[]{:S(2)}) %collective-permute-start.1) | collective-permute-done | bytes 196640 | tf_op jit(solution)/shard_map/ppermute | solution.py:721
  22.1 0.7 collective-permute-start.2
  22.8 1.4 %edge.7 = bf16[256,512]{1,0:T(8,128)(2,1)} custom-call(s32[2]{0:T(128)S(1)} %copy-done.6, f32[2,128]{1,0:T(2,128)S(1)} %pad_maximum_fusion.gain_ref, bf16[128,2048]{1,0:T(8,128)(2,1)S(1)} %bitcast.33, bf16[128,2048]{1,0:T(8,128)(2,1)S(1)} %bitcast.40, bf16[640,1024]{1,0:T(8,128)(2,1)S(1)} %collective-permute-done.mate_ref, ...), custom_call_target="tpu_custom_call" | custom-call | flops 1 | bytes 1 | tf_op jit(solution)/shard_map/edge/pallas_call | solution.py:185
  24.2 1.4 %collective-permute-start.8 = (bf16[256,512]{1,0:T(8,128)(2,1)}, bf16[256,512]{1,0:T(8,128)(2,1)}, u32[]{:S(2)}, u32[]{:S(2)}) collective-permute-start(bf16[256,512]{1,0:T(8,128)(2,1)} %edge.7), channel_id=1, source_target_pairs={{2,4},{3,5},{4,2},{5,3},{10,12},{11,13},{12,10},{13,11},{18,20},{1... | collective-permute-start | bytes 786440 | tf_op jit(solution)/shard_map/ppermute | solution.py:721
  25.6 0.7 pair_lyrics.3.refs_0_
  26.2 0.0 copy-start.7
  26.3 4.1 %collective-permute-start.4 = (bf16[192,512]{1,0:T(8,128)(2,1)S(1)}, bf16[192,512]{1,0:T(8,128)(2,1)S(1)}, u32[]{:S(2)}, u32[]{:S(2)}) collective-permute-start(bf16[192,512]{1,0:T(8,128)(2,1)S(1)} %pair_lyrics.3.refs_0_), channel_id=1, source_target_pairs={{0,4},{1,5},{2,6},{3,7},{4,0},{5,1},{6,2},{7,3},{8,12},{9,13},{10,... | collective-permute-start | bytes 589832 | tf_op jit(solution)/shard_map/ppermute | solution.py:721
  30.3 3.5 %collective-permute-done.2.refs_1_.refs_2_ = bf16[192,512]{1,0:T(8,128)(2,1)S(1)} collective-permute-done((bf16[192,512]{1,0:T(8,128)(2,1)S(1)}, bf16[192,512]{1,0:T(8,128)(2,1)S(1)}, u32[]{:S(2)}, u32[]{:S(2)}) %collective-permute-start.2) | collective-permute-done | bytes 196640 | tf_op jit(solution)/shard_map/ppermute | solution.py:721
  33.8 1.5 %edge.4 = bf16[448,512]{1,0:T(8,128)(2,1)} custom-call(s32[2]{0:T(128)S(1)} %copy-done.6, f32[2,128]{1,0:T(2,128)S(1)} %pad_maximum_fusion.gain_ref, bf16[128,2048]{1,0:T(8,128)(2,1)S(1)} %bitcast.34, bf16[128,2048]{1,0:T(8,128)(2,1)S(1)} %bitcast.41, bf16[640,1024]{1,0:T(8,128)(2,1)S(1)} %collective-permute-done.mate_ref, ...), custom_call_target="tpu_custom_call" | custom-call | flops 1 | bytes 1 | tf_op jit(solution)/shard_map/edge/pallas_call | solution.py:185
  35.3 0.6 collective-permute-start.3
  36.6 0.6 fusion
  37.2 1.4 %stack.74.meta_ref = s32[15]{0:T(128)S(1)} concatenate(s32[1]{0:T(128)} %bitcast, s32[1]{0:T(128)} %bitcast.1, s32[1]{0:T(128)} %bitcast.2, s32[1]{0:T(128)} %bitcast.3, s32[1]{0:T(128)S(6)} %copy.28, s32[1]{0:T(128)} %bitcast.4, s32[1]{0:T(128)} %bitcast.5, s32[1]{0:T(128)} %bitcast.6, s32[1]{0:T(128)} %bitcast.7, s32[1]{0:T(128)} %bitcast.8, s32[1]{0:T(128)} %bitcast.9, ...), dimensions={0} | concatenate | bytes 120 | tf_op jit(solution)/shard_map/stack | solution.py:750
  38.6 0.9 prepare_keys.1.key_ref
  39.5 0.0 copy-start.2
  39.5 0.0 copy-start.3
  39.5 4.9 %collective-permute-done.4.refs_0_.refs_1_ = bf16[192,512]{1,0:T(8,128)(2,1)S(1)} collective-permute-done((bf16[192,512]{1,0:T(8,128)(2,1)S(1)}, bf16[192,512]{1,0:T(8,128)(2,1)S(1)}, u32[]{:S(2)}, u32[]{:S(2)}) %collective-permute-start.4) | collective-permute-done | bytes 196640 | tf_op jit(solution)/shard_map/ppermute | solution.py:721
  44.4 0.7 edge.5
  45.2 0.7 collective-permute-start.5
  45.8 1.3 %collective-permute-start.6 = (bf16[192,512]{1,0:T(8,128)(2,1)S(1)}, bf16[192,512]{1,0:T(8,128)(2,1)S(1)}, u32[]{:S(2)}, u32[]{:S(2)}) collective-permute-start(bf16[192,512]{1,0:T(8,128)(2,1)S(1)} %collective-permute-done.4.refs_0_.refs_1_), channel_id=1, source_target_pairs={{0,2},{1,3},{2,0},{3,1},{4,6},{5,7},{6,4},{7,5},{8,10},{9,11},{10,... | collective-permute-start | bytes 589832 | tf_op jit(solution)/shard_map/ppermute | solution.py:721
  47.2 0.0 collective-permute-done.7.one_ref
  47.2 0.0 collective-permute-done.8.mid_ref
  47.2 5.6 %attention.2 = (bf16[128,512]{1,0:T(8,128)(2,1)S(1)}, bf16[128,512]{1,0:T(8,128)(2,1)S(1)}, bf16[256,512]{1,0:T(8,128)(2,1)S(1)}, f32[256,512]{1,0:T(8,128)S(1)}...) custom-call(s32[15]{0:T(128)S(1)} %stack.74.meta_ref, ...), custom_call_target="tpu_custom_call" | custom-call | flops 1207959552 | bytes 8388608 | tf_op jit(solution)/shard_map/attention/pallas_call | solution.py:429
  52.8 0.8 collective-permute-start.9
  53.6 2.9 %collective-permute-done.6.refs_2_ = bf16[192,512]{1,0:T(8,128)(2,1)S(1)} collective-permute-done((bf16[192,512]{1,0:T(8,128)(2,1)S(1)}, bf16[192,512]{1,0:T(8,128)(2,1)S(1)}, u32[]{:S(2)}, u32[]{:S(2)}) %collective-permute-start.6) | collective-permute-done | bytes 196640 | tf_op jit(solution)/shard_map/ppermute | solution.py:721
  56.6 0.0 collective-permute-done.5.mid_ref
  56.6 3.0 %collective-permute-done.9.refs_6_.refs_2_ = bf16[192,512]{1,0:T(8,128)(2,1)S(1)} collective-permute-done((bf16[192,512]{1,0:T(8,128)(2,1)S(1)}, bf16[192,512]{1,0:T(8,128)(2,1)S(1)}, u32[]{:S(2)}, u32[]{:S(2)}) %collective-permute-start.9) | collective-permute-done | bytes 196640 | tf_op jit(solution)/shard_map/ppermute | solution.py:721
  59.6 0.0 collective-permute-done.3.one_ref
  59.6 5.5 %attention.3 = (bf16[128,512]{1,0:T(8,128)(2,1)S(1)}, bf16[128,512]{1,0:T(8,128)(2,1)S(1)}, bf16[256,512]{1,0:T(8,128)(2,1)S(1)}, f32[256,512]{1,0:T(8,128)S(1)}...) custom-call(s32[15]{0:T(128)S(1)} %stack.74.meta_ref, ...), custom_call_target="tpu_custom_call" | custom-call | flops 1207959552 | bytes 8388608 | tf_op jit(solution)/shard_map/attention/pallas_call | solution.py:429
  65.1 0.1 collective-permute-start.10
  65.2 6.0 %collective-permute-done.10.refs_3_ = bf16[208,512]{1,0:T(8,128)(2,1)S(1)} collective-permute-done((bf16[208,512]{1,0:T(8,128)(2,1)S(1)}, bf16[208,512]{1,0:T(8,128)(2,1)S(1)}, u32[]{:S(2)}, u32[]{:S(2)}) %collective-permute-start.10) | collective-permute-done | bytes 213024 | tf_op jit(solution)/shard_map/ppermute | solution.py:721
  71.2 0.1 relay.1
  71.3 0.4 collective-permute-start.14
  71.7 0.7 collective-permute-start.16
  72.4 4.5 %collective-permute-start.15 = (bf16[192,1024]{1,0:T(8,128)(2,1)S(1)}, bf16[192,1024]{1,0:T(8,128)(2,1)S(1)}, u32[]{:S(2)}, u32[]{:S(2)}) collective-permute-start(bf16[192,1024]{1,0:T(8,128)(2,1)S(1)} %get-tuple-element.59), channel_id=1, source_target_pairs={{0,4},{1,5},{2,6},{3,7},{4,0},{5,1},{6,2},{7,3},{8,12},{9,13},{10,... | collective-permute-start | bytes 1179656 | tf_op jit(solution)/shard_map/ppermute | solution.py:721
  76.8 1.5 %collective-permute-start.11 = (f32[8,128]{1,0:T(8,128)S(1)}, f32[8,128]{1,0:T(8,128)S(1)}, u32[]{:S(2)}, u32[]{:S(2)}) collective-permute-start(f32[8,128]{1,0:T(8,128)S(1)} %get-tuple-element.57), channel_id=1, source_target_pairs={{0,8},{8,0},{16,24},{24,16},{1,9},{9,1},{17,25},{25,17},{2,10},{10... | collective-permute-start | bytes 12296 | tf_op jit(solution)/shard_map/ppermute | solution.py:690
  78.3 2.1 %collective-permute-done.11 = f32[8,128]{1,0:T(8,128)S(1)} collective-permute-done((f32[8,128]{1,0:T(8,128)S(1)}, f32[8,128]{1,0:T(8,128)S(1)}, u32[]{:S(2)}, u32[]{:S(2)}) %collective-permute-start.11) | collective-permute-done | bytes 4128 | tf_op jit(solution)/shard_map/ppermute | solution.py:690
  80.5 1.5 %collective-permute-start.12 = (f32[8,128]{1,0:T(8,128)S(1)}, f32[8,128]{1,0:T(8,128)S(1)}, u32[]{:S(2)}, u32[]{:S(2)}) collective-permute-start(f32[8,128]{1,0:T(8,128)S(1)} %add.51), channel_id=1, source_target_pairs={{0,16},{8,24},{16,0},{24,8},{1,17},{9,25},{17,1},{25,9},{2,18},{10... | collective-permute-start | bytes 12296 | tf_op jit(solution)/shard_map/ppermute | solution.py:690
  82.0 2.1 %collective-permute-done.12 = f32[8,128]{1,0:T(8,128)S(1)} collective-permute-done((f32[8,128]{1,0:T(8,128)S(1)}, f32[8,128]{1,0:T(8,128)S(1)}, u32[]{:S(2)}, u32[]{:S(2)}) %collective-permute-start.12) | collective-permute-done | bytes 4128 | tf_op jit(solution)/shard_map/ppermute | solution.py:690
  84.1 0.1 collective-permute-start.13
  84.1 19.1 %collective-permute-done.13 = f32[8,128]{1,0:T(8,128)S(1)} collective-permute-done((f32[8,128]{1,0:T(8,128)S(1)}, f32[8,128]{1,0:T(8,128)S(1)}, u32[]{:S(2)}, u32[]{:S(2)}) %collective-permute-start.13) | collective-permute-done | bytes 4128 | tf_op jit(solution)/shard_map/ppermute | solution.py:690
  103.3 0.0 collective-permute-done.15.two_ref
  103.3 0.0 collective-permute-done.14.one_ref
  103.3 0.9 finish_lyric.1
  104.2 0.0 collective-permute-done.16.mid_ref
  104.2 2.3 %finish_audio.1 = (bf16[128,2048]{1,0:T(8,128)(2,1)}, bf16[128,2048]{1,0:T(8,128)(2,1)}, bf16[128,2048]{1,0:T(8,128)(2,1)}, bf16[128,2048]{1,0:T(8,128)(2,1)}, bf16[624,1024]{1,0:T(8,128)(2,1)S(1)}) custom-call(s32[2]{0:T(128)S(1)} %copy-done.6, f32[2,128]{1,0:T(2,128)S(1)} %pad_maximum_fusion.gain_ref, bf16[128,2048]{1,0:T(8,128)(2,1)S(1)} %bitcast.37, ...), custom_call_target="tpu_custom_call" | custom-call | flops 1 | bytes 1 | tf_op jit(solution)/shard_map/finish_audio/pallas_call | solution.py:509
  106.5 0.1 collective-permute-start.17
  106.6 3.0 %collective-permute-done.17.mate_ref = bf16[624,1024]{1,0:T(8,128)(2,1)S(1)} collective-permute-done((bf16[624,1024]{1,0:T(8,128)(2,1)S(1)}, bf16[624,1024]{1,0:T(8,128)(2,1)S(1)}, u32[]{:S(2)}, u32[]{:S(2)}) %collective-permute-start.17) | collective-permute-done | bytes 1277984 | tf_op jit(solution)/shard_map/ppermute | solution.py:808
  109.6 2.2 %join.1 = (bf16[128,2048]{1,0:T(8,128)(2,1)}, bf16[128,2048]{1,0:T(8,128)(2,1)}, bf16[128,2048]{1,0:T(8,128)(2,1)}, bf16[128,2048]{1,0:T(8,128)(2,1)}, bf16[48,2...) custom-call(s32[2]{0:T(128)S(1)} %copy-done.6, ...), custom_call_target="tpu_custom_call", output_to_operand_aliasing={{0}: (4, {}), {1}: (5, {}), {2}: (6, {}), {3}: (7, {})} | custom-call | flops 1 | bytes 1 | tf_op jit(solution)/shard_map/join/pallas_call | solution.py:618
  (13 shorter events, 0.0 us)
Async XLA Ops:
  1.3 3.8 %copy-start.8 = (f32[128]{0:T(128)S(1)}, f32[128]{0:T(128)}, u32[]{:S(2)}) copy-start(f32[128]{0:T(128)} %param.16) | copy-start | bytes 1540
  1.3 3.8 %copy-start.9 = (f32[128]{0:T(128)S(1)}, f32[128]{0:T(128)}, u32[]{:S(2)}) copy-start(f32[128]{0:T(128)} %param.15) | copy-start | bytes 1540
  1.3 6.6 %copy-start.4 = (bf16[1,48,2048]{2,1,0:T(8,128)(2,1)S(1)}, bf16[1,48,2048]{2,1,0:T(8,128)(2,1)}, u32[]{:S(2)}) copy-start(bf16[1,48,2048]{2,1,0:T(8,128)(2,1)} %param.13) | copy-start | bytes 589828
  1.3 6.6 %copy-start.5 = (bf16[1,48,2048]{2,1,0:T(8,128)(2,1)S(1)}, bf16[1,48,2048]{2,1,0:T(8,128)(2,1)}, u32[]{:S(2)}) copy-start(bf16[1,48,2048]{2,1,0:T(8,128)(2,1)} %param.14) | copy-start | bytes 589828
  1.3 6.6 %copy-start.6 = (s32[2]{0:T(128)S(1)}, s32[2]{0:T(128)}, u32[]{:S(2)}) copy-start(s32[2]{0:T(128)} %pad_add_fusion.state_ref) | copy-start | bytes 28
  4.5 8.1 %copy-start = (bf16[1,128,2048]{2,1,0:T(8,128)(2,1)S(1)}, bf16[1,128,2048]{2,1,0:T(8,128)(2,1)}, u32[]{:S(2)}) copy-start(bf16[1,128,2048]{2,1,0:T(8,128)(2,1)} %param.11) | copy-start | bytes 1572868
  4.5 8.1 %copy-start.1 = (bf16[1,128,2048]{2,1,0:T(8,128)(2,1)S(1)}, bf16[1,128,2048]{2,1,0:T(8,128)(2,1)}, u32[]{:S(2)}) copy-start(bf16[1,128,2048]{2,1,0:T(8,128)(2,1)} %param.12) | copy-start | bytes 1572868
  4.5 3.4 %collective-permute-start = (bf16[640,1024]{1,0:T(8,128)(2,1)}, bf16[640,1024]{1,0:T(8,128)(2,1)S(1)}, u32[]{:S(2)}, u32[]{:S(2)}) collective-permute-start(bf16[640,1024]{1,0:T(8,128)(2,1)} %pack.1), channel_id=1, source_target_pairs={{0,1},{1,0},{2,3},{3,2},{4,5},{5,4},{6,7},{7,6},{8,9},{9,8},{10,11... | collective-permute-start | bytes 3932168 | tf_op jit(solution)/shard_map/ppermute | solution.py:766
  8.6 13.5 %collective-permute-start.1 = (bf16[192,512]{1,0:T(8,128)(2,1)S(1)}, bf16[192,512]{1,0:T(8,128)(2,1)S(1)}, u32[]{:S(2)}, u32[]{:S(2)}) collective-permute-start(bf16[192,512]{1,0:T(8,128)(2,1)S(1)} %pair_lyrics.2.refs_0_), channel_id=1, source_target_pairs={{0,4},{1,5},{2,6},{3,7},{4,0},{5,1},{6,2},{7,3},{8,12},{9,13},{10,... | collective-permute-start | bytes 589832 | tf_op jit(solution)/shard_map/ppermute | solution.py:721
  14.1 33.1 %collective-permute-start.7 = (bf16[448,512]{1,0:T(8,128)(2,1)}, bf16[448,512]{1,0:T(8,128)(2,1)}, u32[]{:S(2)}, u32[]{:S(2)}) collective-permute-start(bf16[448,512]{1,0:T(8,128)(2,1)} %edge.6), channel_id=1, source_target_pairs={{0,2},{1,3},{2,0},{3,1},{4,6},{5,7},{6,4},{7,5},{8,10},{9,11},{10,... | collective-permute-start | bytes 1376264 | tf_op jit(solution)/shard_map/ppermute | solution.py:721
  22.1 11.7 %collective-permute-start.2 = (bf16[192,512]{1,0:T(8,128)(2,1)S(1)}, bf16[192,512]{1,0:T(8,128)(2,1)S(1)}, u32[]{:S(2)}, u32[]{:S(2)}) collective-permute-start(bf16[192,512]{1,0:T(8,128)(2,1)S(1)} %collective-permute-done.1.refs_0_.refs_1_), channel_id=1, source_target_pairs={{0,2},{1,3},{2,0},{3,1},{4,6},{5,7},{6,4},{7,5},{8,10},{9,11},{10,... | collective-permute-start | bytes 589832 | tf_op jit(solution)/shard_map/ppermute | solution.py:721
  24.2 23.0 %collective-permute-start.8 = (bf16[256,512]{1,0:T(8,128)(2,1)}, bf16[256,512]{1,0:T(8,128)(2,1)}, u32[]{:S(2)}, u32[]{:S(2)}) collective-permute-start(bf16[256,512]{1,0:T(8,128)(2,1)} %edge.7), channel_id=1, source_target_pairs={{2,4},{3,5},{4,2},{5,3},{10,12},{11,13},{12,10},{13,11},{18,20},{1... | collective-permute-start | bytes 786440 | tf_op jit(solution)/shard_map/ppermute | solution.py:721
  26.2 10.3 %copy-start.7 = (s32[1,1,2]{2,1,0:T(1,128)S(1)}, s32[1,1,2]{2,1,0:T(1,128)}, u32[]{:S(2)}) copy-start(s32[1,1,2]{2,1,0:T(1,128)} %param.18) | copy-start | bytes 28
  26.3 18.2 %collective-permute-start.4 = (bf16[192,512]{1,0:T(8,128)(2,1)S(1)}, bf16[192,512]{1,0:T(8,128)(2,1)S(1)}, u32[]{:S(2)}, u32[]{:S(2)}) collective-permute-start(bf16[192,512]{1,0:T(8,128)(2,1)S(1)} %pair_lyrics.3.refs_0_), channel_id=1, source_target_pairs={{0,4},{1,5},{2,6},{3,7},{4,0},{5,1},{6,2},{7,3},{8,12},{9,13},{10,... | collective-permute-start | bytes 589832 | tf_op jit(solution)/shard_map/ppermute | solution.py:721
  35.3 24.3 %collective-permute-start.3 = (bf16[448,512]{1,0:T(8,128)(2,1)}, bf16[448,512]{1,0:T(8,128)(2,1)}, u32[]{:S(2)}, u32[]{:S(2)}) collective-permute-start(bf16[448,512]{1,0:T(8,128)(2,1)} %edge.4), channel_id=1, source_target_pairs={{0,2},{1,3},{2,0},{3,1},{4,6},{5,7},{6,4},{7,5},{8,10},{9,11},{10,... | collective-permute-start | bytes 1376264 | tf_op jit(solution)/shard_map/ppermute | solution.py:721
  39.5 7.7 %copy-start.2 = (bf16[1,128,2048]{2,1,0:T(8,128)(2,1)S(1)}, bf16[1,128,2048]{2,1,0:T(8,128)(2,1)}, u32[]{:S(2)}) copy-start(bf16[1,128,2048]{2,1,0:T(8,128)(2,1)} %param.10) | copy-start | bytes 1572868
  39.5 7.7 %copy-start.3 = (bf16[1,128,2048]{2,1,0:T(8,128)(2,1)S(1)}, bf16[1,128,2048]{2,1,0:T(8,128)(2,1)}, u32[]{:S(2)}) copy-start(bf16[1,128,2048]{2,1,0:T(8,128)(2,1)} %param.17) | copy-start | bytes 1572868
  45.2 11.4 %collective-permute-start.5 = (bf16[256,512]{1,0:T(8,128)(2,1)S(1)}, bf16[256,512]{1,0:T(8,128)(2,1)S(1)}, u32[]{:S(2)}, u32[]{:S(2)}) collective-permute-start(bf16[256,512]{1,0:T(8,128)(2,1)S(1)} %edge.5), channel_id=1, source_target_pairs={{2,4},{3,5},{4,2},{5,3},{10,12},{11,13},{12,10},{13,11},{18,20},{1... | collective-permute-start | bytes 786440 | tf_op jit(solution)/shard_map/ppermute | solution.py:721
  45.8 10.7 %collective-permute-start.6 = (bf16[192,512]{1,0:T(8,128)(2,1)S(1)}, bf16[192,512]{1,0:T(8,128)(2,1)S(1)}, u32[]{:S(2)}, u32[]{:S(2)}) collective-permute-start(bf16[192,512]{1,0:T(8,128)(2,1)S(1)} %collective-permute-done.4.refs_0_.refs_1_), channel_id=1, source_target_pairs={{0,2},{1,3},{2,0},{3,1},{4,6},{5,7},{6,4},{7,5},{8,10},{9,11},{10,... | collective-permute-start | bytes 589832 | tf_op jit(solution)/shard_map/ppermute | solution.py:721
  52.8 6.7 %collective-permute-start.9 = (bf16[192,512]{1,0:T(8,128)(2,1)S(1)}, bf16[192,512]{1,0:T(8,128)(2,1)S(1)}, u32[]{:S(2)}, u32[]{:S(2)}) collective-permute-start(bf16[192,512]{1,0:T(8,128)(2,1)S(1)} %get-tuple-element.51), channel_id=1, source_target_pairs={{0,2},{1,3},{2,0},{3,1},{4,6},{5,7},{6,4},{7,5},{8,10},{9,11},{10,... | collective-permute-start | bytes 589832 | tf_op jit(solution)/shard_map/ppermute | solution.py:721
  65.1 6.1 %collective-permute-start.10 = (bf16[208,512]{1,0:T(8,128)(2,1)S(1)}, bf16[208,512]{1,0:T(8,128)(2,1)S(1)}, u32[]{:S(2)}, u32[]{:S(2)}) collective-permute-start(bf16[208,512]{1,0:T(8,128)(2,1)S(1)} %get-tuple-element.56), channel_id=1, source_target_pairs={{0,2},{1,3},{2,0},{3,1},{4,6},{5,7},{6,4},{7,5},{8,10},{9,11},{10,... | collective-permute-start | bytes 638984 | tf_op jit(solution)/shard_map/ppermute | solution.py:721
  71.3 32.0 %collective-permute-start.14 = (bf16[448,1024]{1,0:T(8,128)(2,1)S(1)}, bf16[448,1024]{1,0:T(8,128)(2,1)S(1)}, u32[]{:S(2)}, u32[]{:S(2)}) collective-permute-start(bf16[448,1024]{1,0:T(8,128)(2,1)S(1)} %get-tuple-element.58), channel_id=1, source_target_pairs={{0,2},{1,3},{2,0},{3,1},{4,6},{5,7},{6,4},{7,5},{8,10},{9,11},{10,... | collective-permute-start | bytes 2752520 | tf_op jit(solution)/shard_map/ppermute | solution.py:721
  71.7 32.5 %collective-permute-start.16 = (bf16[256,1024]{1,0:T(8,128)(2,1)S(1)}, bf16[256,1024]{1,0:T(8,128)(2,1)S(1)}, u32[]{:S(2)}, u32[]{:S(2)}) collective-permute-start(bf16[256,1024]{1,0:T(8,128)(2,1)S(1)} %get-tuple-element.63), channel_id=1, source_target_pairs={{2,4},{3,5},{4,2},{5,3},{10,12},{11,13},{12,10},{13,11},{18,20},{1... | collective-permute-start | bytes 1572872 | tf_op jit(solution)/shard_map/ppermute | solution.py:721
  72.4 30.9 %collective-permute-start.15 = (bf16[192,1024]{1,0:T(8,128)(2,1)S(1)}, bf16[192,1024]{1,0:T(8,128)(2,1)S(1)}, u32[]{:S(2)}, u32[]{:S(2)}) collective-permute-start(bf16[192,1024]{1,0:T(8,128)(2,1)S(1)} %get-tuple-element.59), channel_id=1, source_target_pairs={{0,4},{1,5},{2,6},{3,7},{4,0},{5,1},{6,2},{7,3},{8,12},{9,13},{10,... | collective-permute-start | bytes 1179656 | tf_op jit(solution)/shard_map/ppermute | solution.py:721
  76.8 3.6 %collective-permute-start.11 = (f32[8,128]{1,0:T(8,128)S(1)}, f32[8,128]{1,0:T(8,128)S(1)}, u32[]{:S(2)}, u32[]{:S(2)}) collective-permute-start(f32[8,128]{1,0:T(8,128)S(1)} %get-tuple-element.57), channel_id=1, source_target_pairs={{0,8},{8,0},{16,24},{24,16},{1,9},{9,1},{17,25},{25,17},{2,10},{10... | collective-permute-start | bytes 12296 | tf_op jit(solution)/shard_map/ppermute | solution.py:690
  80.5 3.6 %collective-permute-start.12 = (f32[8,128]{1,0:T(8,128)S(1)}, f32[8,128]{1,0:T(8,128)S(1)}, u32[]{:S(2)}, u32[]{:S(2)}) collective-permute-start(f32[8,128]{1,0:T(8,128)S(1)} %add.51), channel_id=1, source_target_pairs={{0,16},{8,24},{16,0},{24,8},{1,17},{9,25},{17,1},{25,9},{2,18},{10... | collective-permute-start | bytes 12296 | tf_op jit(solution)/shard_map/ppermute | solution.py:690
  84.1 19.2 %collective-permute-start.13 = (f32[8,128]{1,0:T(8,128)S(1)}, f32[8,128]{1,0:T(8,128)S(1)}, u32[]{:S(2)}, u32[]{:S(2)}) collective-permute-start(f32[8,128]{1,0:T(8,128)S(1)} %add.52), channel_id=1, source_target_pairs={{0,4},{1,5},{2,6},{3,7},{4,0},{5,1},{6,2},{7,3},{8,12},{9,13},{10,... | collective-permute-start | bytes 12296 | tf_op jit(solution)/shard_map/ppermute | solution.py:690
  106.5 3.1 %collective-permute-start.17 = (bf16[624,1024]{1,0:T(8,128)(2,1)S(1)}, bf16[624,1024]{1,0:T(8,128)(2,1)S(1)}, u32[]{:S(2)}, u32[]{:S(2)}) collective-permute-start(bf16[624,1024]{1,0:T(8,128)(2,1)S(1)} %get-tuple-element.75), channel_id=1, source_target_pairs={{0,1},{1,0},{2,3},{3,2},{4,5},{5,4},{6,7},{7,6},{8,9},{9,8},{10,11... | collective-permute-start | bytes 3833864 | tf_op jit(solution)/shard_map/ppermute | solution.py:808

commit v11 on v10

--- a/solution.py
+++ b/solution.py
@@ -213,14 +213,14 @@
 
 
 def attention_kernel(
-    chunk, groups, head_size, score_scale, meta_ref, gain_ref, query_ref, grad_ref, value_ref, key_ref,
+    chunk, chained, waits, groups, head_size, score_scale, meta_ref, gain_ref, query_ref, grad_ref, value_ref, key_ref,
     mate_ref, one_ref, mid_ref, *refs
 ):
     frames = query_ref.shape[0]
     exchanged = len(groups) == 4
     inputs = 3 if exchanged else 1
     lyric_in, refs = refs[:inputs], refs[inputs:]
-    earlier, refs = refs[: 3 * chunk], refs[3 * chunk + (chunk if exchanged else 0) :]
+    earlier, refs = refs[:chained], refs[chained + waits :]
     window = one_ref.shape[0] - 2 * frames
     out_ref, grad_query_ref, to_mate_ref, key_grad_ref, value_grad_ref = refs[:5]
     to_one_ref, to_mid_ref, gain_grad_ref = refs[5:8]
@@ -232,11 +232,7 @@
     touching = meta_ref[1] == 1
 
     size = out_ref.shape[1]
-    for index in range(chunk):
-        for ref, part_ref in zip((to_one_ref, to_mid_ref), earlier[3 * index :]):
-            if ref.shape[1] > size:
-                ref[:, chunk_cols(index, size)] = part_ref[...]
-    gain_grad_ref[...] = earlier[-1][...] if chunk else jnp.zeros_like(gain_grad_ref)
+    gain_grad_ref[...] = earlier[0][...] if chained else jnp.zeros_like(gain_grad_ref)
     mate_tiles = mate_ref[align:, 0:frames].astype(jnp.float32).astype(jnp.int32)
     start = 0
     for number, (_, (_, _, rows)) in enumerate(runs):
@@ -264,7 +260,6 @@
     q_gain = gain_ref[0:1, :]
     k_gain = gain_ref[1:2, :]
     heads = size // head_size
-    sent = to_one_ref.shape[1] // size > 1
 
     def one_head(head):
         cols = pl.ds(pl.multiple_of(head * head_size, head_size), head_size)
@@ -277,7 +272,6 @@
             ),
             head_size,
         )
-        sent_cols = half_cols if sent else cols
         lyric = [ref[:, cols if exchanged else own_cols] for ref in lyric_in]
         if exchanged:
             lyric = [lyric[0], lyric[1], one_ref[0:window, cols], lyric[2]]
@@ -380,10 +374,10 @@
             (grad_keys.astype(jnp.bfloat16), 0),
             (grad_values.astype(jnp.bfloat16), frames),
         ):
-            to_one_ref[window + part : window + part + frames, sent_cols] = jnp.where(
+            to_one_ref[window + part : window + part + frames, cols] = jnp.where(
                 touching, grads[near], grads[far]
             )
-            to_mid_ref[part : part + frames, sent_cols] = jnp.where(touching, grads[far], grads[near])
+            to_mid_ref[part : part + frames, cols] = jnp.where(touching, grads[far], grads[near])
         if exchanged:
             held_ref, two_ref, to_two_ref = lyric_out
             outs = (held_ref, two_ref, to_one_ref, to_two_ref)
@@ -392,9 +386,8 @@
         start = 2 * frames
         for index, (key_row, value_row, rows) in runs:
             part = slice(start, start + rows)
-            put = sent_cols if outs[index] is to_one_ref else cols
-            outs[index][key_row : key_row + rows, put] = grad_keys[part].astype(jnp.bfloat16)
-            outs[index][value_row : value_row + rows, put] = grad_values[part].astype(
+            outs[index][key_row : key_row + rows, cols] = grad_keys[part].astype(jnp.bfloat16)
+            outs[index][value_row : value_row + rows, cols] = grad_values[part].astype(
                 jnp.bfloat16
             )
             start += rows
@@ -404,7 +397,7 @@
         for number in range(HEADS_PER_STEP):
             one_head(step * HEADS_PER_STEP + number)
 
-    if exchanged and sent:
+    if exchanged and chunk == CHUNKS - 1:
         to_two_ref = lyric_out[2]
         to_two_ref[window:, :] = split_rows(gain_grad_ref[...], size)
 
@@ -415,19 +408,20 @@
     frames, width = query.shape
     head_size = gains.shape[1]
     size = width // 2 // CHUNKS
-    sent = size if chunk < CHUNKS - 1 else width // 2
     lyric_rows = sum(run[2] for group in groups for run in group)
     key_rows = 3 * frames + lyric_rows
     bf16, f32 = jnp.bfloat16, jnp.float32
     slot = sum(2 * run[2] for run in groups[0])
     out_shape = [shape(frames, size)] * 2
     out_shape += [shape(2 * frames, size, dtype) for dtype in (bf16, f32, f32)]
-    out_shape += [shape(one.shape[0], sent), shape(2 * frames, sent), shape(8, head_size, f32)]
+    out_shape += [shape(one.shape[0], size), shape(2 * frames, size), shape(8, head_size, f32)]
     out_shape += [shape(slot, size)] * len(lyrics)
     if len(lyrics) > 1 and chunk == CHUNKS - 1:
         out_shape[-1] = shape(slot + GAIN_ROWS, size)
     return call(
-        functools.partial(attention_kernel, chunk, groups, head_size, head_size ** (-0.5)),
+        functools.partial(
+            attention_kernel, chunk, len(earlier), len(after), groups, head_size, head_size ** (-0.5)
+        ),
         "attention",
         [SMEM] + [VMEM] * (8 + len(lyrics) + len(earlier)) + [ANY] * len(after),
         [VMEM] * len(out_shape),
@@ -442,21 +436,18 @@
     )(meta, gains, query, cot, value, key, mate, one, mid, *lyrics, *earlier, *after)
 
 
-def finish_audio_kernel(
-    state_ref, gain_ref, raw_ref, mate_ref, one_ref, mid_ref, *refs
-):
-    chunk_refs, refs = refs[: 5 * CHUNKS], refs[5 * CHUNKS :]
+def finish_audio_kernel(state_ref, gain_ref, raw_ref, mate_ref, *refs):
+    chunk_refs, refs = refs[: 7 * CHUNKS], refs[7 * CHUNKS :]
     *lyric, out, query_out, key_out, value_out, to_mate_ref, key_ref, value_ref, sems = refs
     head_size = gain_ref.shape[1]
     k_gain = gain_ref[1:2, :]
     frames, half = key_ref.shape
     size = half // CHUNKS
     own, mate = slice(0, frames), slice(frames, 2 * frames)
-    first = one_ref.shape[0] - 2 * frames
     touching = state_ref[1] == 1
     copies = []
     for chunk in range(CHUNKS):
-        out_own_ref, query_own_ref, ready_ref = chunk_refs[5 * chunk : 5 * chunk + 3]
+        out_own_ref, query_own_ref, ready_ref = chunk_refs[7 * chunk : 7 * chunk + 3]
         for source, target in ((out_own_ref, out), (query_own_ref, query_out)):
             copies.append(
                 pltpu.make_async_copy(
@@ -474,9 +465,9 @@
         cols = slice(head * head_size, (head + 1) * head_size)
         chunk = head * head_size // size
         part = slice(head * head_size - chunk * size, (head + 1) * head_size - chunk * size)
-        key_grad_ref, value_grad_ref = chunk_refs[5 * chunk + 3 : 5 * chunk + 5]
-        one = one_ref[first:, cols].astype(jnp.float32)
-        mid = mid_ref[:, cols].astype(jnp.float32)
+        key_grad_ref, value_grad_ref, one_ref, mid_ref = chunk_refs[7 * chunk + 3 : 7 * chunk + 7]
+        one = one_ref[one_ref.shape[0] - 2 * frames :, part].astype(jnp.float32)
+        mid = mid_ref[:, part].astype(jnp.float32)
         for_own = jnp.where(touching, one, mid)
         for_mate = jnp.where(touching, mid, one)
         key_ref[:, cols] = through_norm(
@@ -502,59 +493,55 @@
         copy.wait()
 
 
-def finish_audio(state, gains, raw, mate, one, mid, chunks, lyric):
+def finish_audio(state, gains, raw, mate, chunks, lyric):
     frames, width = raw.shape
     half = width // 2
     rows = 4 * frames + sum(array.shape[0] for array in lyric)
     return call(
         finish_audio_kernel,
         "finish_audio",
-        [SMEM] + [VMEM] * (5 + len(chunks) + len(lyric)),
+        [SMEM] + [VMEM] * (3 + len(chunks) + len(lyric)),
         [HBM] * 4 + [VMEM],
         [shape(frames, width)] * 4 + [shape(rows, half)],
         scratch_shapes=[pltpu.VMEM((frames, half), jnp.bfloat16)] * 2
         + [pltpu.SemaphoreType.DMA((2 * CHUNKS + 2,))],
-    )(state, gains, raw, mate, one, mid, *chunks, *lyric)
-
-
-def relay_kernel(gain_ref, later_ref, *refs):
-    parts, arrived, (out_ref, _, total_ref) = (
-        refs[:CHUNKS],
-        refs[CHUNKS : 2 * CHUNKS],
-        refs[2 * CHUNKS :],
-    )
-    rows, size = parts[0].shape
-    for chunk, (part_ref, arrived_ref) in enumerate(zip(parts, arrived)):
-        out_ref[:, chunk_cols(chunk, size)] = (
-            part_ref[...].astype(jnp.float32) + arrived_ref[0:rows, :].astype(jnp.float32)
-        ).astype(jnp.bfloat16)
-    total_ref[...] = gain_ref[...] + joined_rows(arrived[-1][rows:, :], gain_ref.shape[1])
-
-
-def relay(parts, arrived, gain, later):
-    rows, size = parts[0].shape
+    )(state, gains, raw, mate, *chunks, *lyric)
+
+
+def relay_kernel(part_ref, arrived_ref, *refs):
+    rows = part_ref.shape[0]
+    total = part_ref[...].astype(jnp.float32) + arrived_ref[0:rows, :].astype(jnp.float32)
+    if arrived_ref.shape[0] == rows:
+        refs[0][...] = total.astype(jnp.bfloat16)
+        return
+    gain_ref, (out_ref, total_ref, _) = refs[0], refs[-3:]
+    out_ref[...] = total.astype(jnp.bfloat16)
+    total_ref[...] = gain_ref[...] + joined_rows(arrived_ref[rows:, :], gain_ref.shape[1])
+
+
+def relay(part, arrived):
+    return call(relay_kernel, "relay", [VMEM] * 2, VMEM, shape(*part.shape))(part, arrived)
+
+
+def last_relay(part, arrived, gain, later, after):
     return call(
         relay_kernel,
         "relay",
-        [VMEM, ANY] + [VMEM] * (2 * CHUNKS),
-        [VMEM, ANY, VMEM],
-        [
-            shape(rows, CHUNKS * size),
-            shape(*later.shape),
-            shape(*gain.shape, jnp.float32),
-        ],
-        input_output_aliases={1: 1},
-    )(gain, later, *parts, *arrived)
+        [VMEM] * 3 + [ANY] * (1 + len(after)),
+        [VMEM, VMEM, ANY],
+        [shape(*part.shape), shape(*gain.shape, jnp.float32), shape(*later.shape)],
+        input_output_aliases={3: 2},
+    )(part, arrived, gain, later, *after)
 
 
 def finish_lyric_kernel(
-    state_ref, gain_ref, raw_ref, mate_ref, one_ref, two_ref, sum_ref, *refs
+    state_ref, gain_ref, raw_ref, mate_ref, sum_ref, *refs
 ):
-    held_refs, (own_ref, to_mate_ref) = refs[:CHUNKS], refs[CHUNKS:]
+    chunk_refs, (own_ref, to_mate_ref) = refs[:-2], refs[-2:]
     rows = raw_ref.shape[0]
     head_size = gain_ref.shape[1]
     k_gain = gain_ref[1:2, :]
-    size = held_refs[0].shape[1]
+    size = chunk_refs[0].shape[1]
     first = mate_ref.shape[0] - ALIGN_ROWS - 2 * rows
     to_mate_ref[2 * rows :, :] = split_rows(sum_ref[...], to_mate_ref.shape[1])
     raw_keys = raw_ref[:, half_of(raw_ref, state_ref[0])]
@@ -562,9 +549,9 @@
         cols = slice(head * head_size, (head + 1) * head_size)
         chunk = head * head_size // size
         part = slice(head * head_size - chunk * size, (head + 1) * head_size - chunk * size)
-        total = held_refs[chunk][:, part].astype(jnp.float32)
-        for ref in (one_ref, two_ref):
-            total = total + ref[0 : 4 * rows, cols].astype(jnp.float32)
+        total = chunk_refs[3 * chunk][:, part].astype(jnp.float32)
+        for ref in chunk_refs[3 * chunk + 1 : 3 * chunk + 3]:
+            total = total + ref[0 : 4 * rows, part].astype(jnp.float32)
         mate_keys = mate_ref[first : first + rows, cols]
         for ref, base, raw in (
             (own_ref, 0, raw_keys[:, cols]),
@@ -574,16 +561,16 @@
             ref[rows : 2 * rows, cols] = total[base + rows : base + 2 * rows].astype(jnp.bfloat16)
 
 
-def finish_lyric(state, gains, raw, mate, held, one, two, total):
+def finish_lyric(state, gains, raw, mate, total, chunks):
     rows, width = raw.shape
     half = width // 2
     return call(
         finish_lyric_kernel,
         "finish_lyric",
-        [SMEM] + [VMEM] * (6 + len(held)),
+        [SMEM] + [VMEM] * (4 + len(chunks)),
         [VMEM] * 2,
         [shape(2 * rows, half), shape(2 * rows + GAIN_ROWS, half)],
-    )(state, gains, raw, mate, one, two, total, *held)
+    )(state, gains, raw, mate, total, *chunks)
 
 
 def join_kernel(count, state_ref, gain_ref, own_ref, mate_ref, *refs):
@@ -764,7 +751,7 @@
         + ([lyric_keys[0], lyric_values[0]] if hops else []),
     )
     mate = lax.ppermute(to_mate, "seq", swap)
-    chunks, parts, earlier, arrived = [], [], [], []
+    chunks, lyric_chunks, earlier, relayed, sent = [], [], [], [], []
     after = []
     for chunk in range(CHUNKS):
         before, one_before = after, lyrics[2:] if chunk else []
@@ -781,30 +768,37 @@
             key_low = prepare_keys(state, gains, keys[0], mate, after)
         results = attention(
             chunk, meta, gains, queries[0], cotangent[0], values[0], key_low, mate, one, mid,
-            lyrics, groups, earlier, arrived,
-        )
-        chunks += results[:5]
-        earlier = [*earlier, *results[5:8]]
-        parts.append(results[8:])
+            lyrics, groups, earlier, relayed,
+        )
+        to_one, to_mid, gain_part, *parts = results[5:]
+        earlier = [gain_part]
+        mid_back = hop(to_mid, between)
         if hops:
-            arrived.append(hop(results[-1], partners))
-    to_one, to_mid, gain_part = earlier[-3:]
-
-    mid = hop(to_mid, between)
+            held, for_two, to_two = parts
+            arrived = hop(to_two, partners)
+            if chunk < CHUNKS - 1:
+                relayed = [relay(for_two, arrived)]
+                to_two = relayed[0]
+            else:
+                to_two, gain_total, to_one = last_relay(
+                    for_two, arrived, gain_part, to_one, sent
+                )
+            two_back, one_back = hop(to_two, across), hop(to_one, partners)
+            lyric_chunks += [held, one_back, two_back]
+            sent = [*sent, mid_back, one_back, two_back]
+        else:
+            one_back = hop(to_one, partners)
+            lyric_chunks += parts
+        chunks += [*results[:5], one_back, mid_back]
+
     to_mate = []
     if hops:
-        to_two, to_one, gain_total = relay(
-            [part[1] for part in parts], arrived, gain_part, to_one
-        )
         gain_total = sum_over(sum_over(gain_total, "song", bits_of(songs)), "seq", [4])
-        two, one = hop(to_two, across), hop(to_one, partners)
         own_half, part_to_mate = finish_lyric(
-            state, gains, lyric_keys[0], mate, [part[0] for part in parts], one, two, gain_total
+            state, gains, lyric_keys[0], mate, gain_total, lyric_chunks
         )
         to_mate = [part_to_mate]
-    else:
-        one = hop(to_one, partners)
-    *filled, to_mate = finish_audio(state, gains, keys[0], mate, one, mid, chunks, to_mate)
+    *filled, to_mate = finish_audio(state, gains, keys[0], mate, chunks, to_mate)
     from_mate = lax.ppermute(to_mate, "seq", swap)
     if hops:
         *filled, grad_lyric_keys, grad_lyric_values, q_total, k_total = join(
@@ -816,7 +810,7 @@
         q_total, k_total = gain_total[0:1], gain_total[1:2]
         spread = lax.dynamic_update_slice(
             jnp.zeros((2 * total_rows, width), jnp.float32),
-            jnp.concatenate([part[0] for part in parts], axis=1).astype(jnp.float32),
+            jnp.concatenate(lyric_chunks, axis=1).astype(jnp.float32),
             (0, core * (width // 2)),
         )
         lyric_key_sum, grad_lyric_values = [

time: 112 us -> 107 us (0.955)
  waiting for transfers between devices: 56 us -> 45.2 us
  starting transfers between devices: 24.4 us -> 29.9 us
    ppermute x3, waiting for transfers between devices: 23.3 us -> 8.64 us  [sum_over(): lax.ppermute(total, axis, [(i, i ^ bit) for i in range(count)])]
    ppermute x13 -> x16, starting transfers between devices: 20.7 us -> 26.2 us  [hop(): return lax.ppermute(block, 'seq', pairs)]
    ppermute x13 -> x16, waiting for transfers between devices: 26.9 us -> 30.8 us  [hop(): return lax.ppermute(block, 'seq', pairs)]
    pallas_call x5 -> x6, Pallas kernels: 14.5 us -> 14.5 us  [the longest x2 11.2 us: attention(): call(functools.partial(attention_kernel, chunk, len(earlier), len(after),...]
  transfers between devices with their start and end apart: 18 -> 21, of which waited for: 11 -> 12; matrix products, arithmetic and copies ran while one was open for 2% -> 2% of each run, Pallas kernels for 12% -> 18%
where the time goes in v11:
time: 107 us; the launch traced here: 106 us
  waiting for transfers between devices  45.2 us (42%)
  starting transfers between devices  29.9 us (28%)
  Pallas kernels  27.2 us (25%)
  local copies, waits for them, and re-layouts  2.02 us (2%)
  between operations  1.57 us (1%)
    ppermute x16, waiting for transfers between devices, hop(): return lax.ppermute(block, 'seq', pairs)  30.8 us
    ppermute x16, starting transfers between devices, hop(): return lax.ppermute(block, 'seq', pairs)  26.2 us
    pallas_call x2, Pallas kernels, attention(): call(functools.partial(attention_kernel, chunk, len(earlier), len(after),...  11.2 us
    ppermute x3, waiting for transfers between devices, sum_over(): lax.ppermute(total, axis, [(i, i ^ bit) for i in range(count)])  8.64 us
    pallas_call x4, Pallas kernels, edge(): call(functools.partial(edge_kernel, chunk, touching, bool(lead)), 'edge',...  5.08 us
    pallas_call x1, Pallas kernels, pack(): call(pack_kernel, 'pack', [SMEM, SMEM] + [HBM] * len(arrays), VMEM, shape...  3.17 us
    ppermute x3, starting transfers between devices, sum_over(): lax.ppermute(total, axis, [(i, i ^ bit) for i in range(count)])  3.08 us
    ppermute x1, waiting for transfers between devices, body(): from_mate = lax.ppermute(to_mate, 'seq', swap)  2.97 us
  transfers between devices with their start and end apart: 21, of which 12 were waited for; matrix products, arithmetic and copies ran while one was open for 2% of the time, Pallas kernels for 18%

profile of v11, /device:TPU:0, one launch (start us, length us, event | category | flops | bytes accessed | tf_op | source)
XLA Modules:
  0.0 106.5 jit_solution(8217098943372304304)
XLA Ops:
  0.7 0.6 pad_add_fusion.state_ref
  1.3 0.0 copy-start.6
  1.3 3.2 %pack.1 = bf16[640,1024]{1,0:T(8,128)(2,1)} custom-call(s32[2]{0:T(128)} %pad_add_fusion.state_ref, s32[2]{0:T(128)} %bitcast.62, bf16[128,2048]{1,0:T(8,128)(2,1)} %bitcast.45, bf16[128,2048]{1,0:T(8,128)(2,1)} %bitcast.48, bf16[128,2048]{1,0:T(8,128)(2,1)} %bitcast.38, bf16[128,2048]{1,0:T(8,128)(2,1)} %bitcast.31, bf16[48,2048]{1,0:T(8,128)(2,1)} %bitcast.51, ...), custom_call_target="tpu_custom_call" | custom-call | flops 1 | bytes 1 | tf_op jit(solution)/shard_map/pack/pallas_call | solution.py:128
  4.5 0.0 copy-start
  4.5 0.0 copy-start.1
  4.5 0.5 collective-permute-start
  5.0 2.9 %collective-permute-done.mate_ref = bf16[640,1024]{1,0:T(8,128)(2,1)S(1)} collective-permute-done((bf16[640,1024]{1,0:T(8,128)(2,1)}, bf16[640,1024]{1,0:T(8,128)(2,1)S(1)}, u32[]{:S(2)}, u32[]{:S(2)}) %collective-permute-start) | collective-permute-done | bytes 1310752 | tf_op jit(solution)/shard_map/ppermute | solution.py:753
  7.9 0.7 pair_lyrics.2.refs_0_
  8.6 4.0 %collective-permute-start.1 = (bf16[192,512]{1,0:T(8,128)(2,1)S(1)}, bf16[192,512]{1,0:T(8,128)(2,1)S(1)}, u32[]{:S(2)}, u32[]{:S(2)}) collective-permute-start(bf16[192,512]{1,0:T(8,128)(2,1)S(1)} %pair_lyrics.2.refs_0_), channel_id=1, source_target_pairs={{0,4},{1,5},{2,6},{3,7},{4,0},{5,1},{6,2},{7,3},{8,12},{9,13},{10,... | collective-permute-start | bytes 589832 | tf_op jit(solution)/shard_map/ppermute | solution.py:708
  12.6 1.5 %edge.6 = bf16[448,512]{1,0:T(8,128)(2,1)} custom-call(s32[2]{0:T(128)S(1)} %copy-done.6, f32[2,128]{1,0:T(2,128)S(1)} %pad_maximum_fusion.gain_ref, bf16[128,2048]{1,0:T(8,128)(2,1)S(1)} %bitcast.39, bf16[128,2048]{1,0:T(8,128)(2,1)S(1)} %bitcast.32, bf16[640,1024]{1,0:T(8,128)(2,1)S(1)} %collective-permute-done.mate_ref, ...), custom_call_target="tpu_custom_call" | custom-call | flops 1 | bytes 1 | tf_op jit(solution)/shard_map/edge/pallas_call | solution.py:185
  14.1 1.6 %collective-permute-start.7 = (bf16[448,512]{1,0:T(8,128)(2,1)}, bf16[448,512]{1,0:T(8,128)(2,1)}, u32[]{:S(2)}, u32[]{:S(2)}) collective-permute-start(bf16[448,512]{1,0:T(8,128)(2,1)} %edge.6), channel_id=1, source_target_pairs={{0,2},{1,3},{2,0},{3,1},{4,6},{5,7},{6,4},{7,5},{8,10},{9,11},{10,... | collective-permute-start | bytes 1376264 | tf_op jit(solution)/shard_map/ppermute | solution.py:708
  15.7 6.5 %collective-permute-done.1.refs_0_.refs_1_ = bf16[192,512]{1,0:T(8,128)(2,1)S(1)} collective-permute-done((bf16[192,512]{1,0:T(8,128)(2,1)S(1)}, bf16[192,512]{1,0:T(8,128)(2,1)S(1)}, u32[]{:S(2)}, u32[]{:S(2)}) %collective-permute-start.1) | collective-permute-done | bytes 196640 | tf_op jit(solution)/shard_map/ppermute | solution.py:708
  22.1 0.7 collective-permute-start.2
  22.8 1.4 %edge.7 = bf16[256,512]{1,0:T(8,128)(2,1)} custom-call(s32[2]{0:T(128)S(1)} %copy-done.6, f32[2,128]{1,0:T(2,128)S(1)} %pad_maximum_fusion.gain_ref, bf16[128,2048]{1,0:T(8,128)(2,1)S(1)} %bitcast.40, bf16[128,2048]{1,0:T(8,128)(2,1)S(1)} %bitcast.33, bf16[640,1024]{1,0:T(8,128)(2,1)S(1)} %collective-permute-done.mate_ref, ...), custom_call_target="tpu_custom_call" | custom-call | flops 1 | bytes 1 | tf_op jit(solution)/shard_map/edge/pallas_call | solution.py:185
  24.2 1.4 %collective-permute-start.8 = (bf16[256,512]{1,0:T(8,128)(2,1)}, bf16[256,512]{1,0:T(8,128)(2,1)}, u32[]{:S(2)}, u32[]{:S(2)}) collective-permute-start(bf16[256,512]{1,0:T(8,128)(2,1)} %edge.7), channel_id=1, source_target_pairs={{2,4},{3,5},{4,2},{5,3},{10,12},{11,13},{12,10},{13,11},{18,20},{1... | collective-permute-start | bytes 786440 | tf_op jit(solution)/shard_map/ppermute | solution.py:708
  25.5 0.7 pair_lyrics.3.refs_0_
  26.2 0.0 copy-start.7
  26.2 4.1 %collective-permute-start.4 = (bf16[192,512]{1,0:T(8,128)(2,1)S(1)}, bf16[192,512]{1,0:T(8,128)(2,1)S(1)}, u32[]{:S(2)}, u32[]{:S(2)}) collective-permute-start(bf16[192,512]{1,0:T(8,128)(2,1)S(1)} %pair_lyrics.3.refs_0_), channel_id=1, source_target_pairs={{0,4},{1,5},{2,6},{3,7},{4,0},{5,1},{6,2},{7,3},{8,12},{9,13},{10,... | collective-permute-start | bytes 589832 | tf_op jit(solution)/shard_map/ppermute | solution.py:708
  30.3 3.5 %collective-permute-done.2.refs_1_.refs_2_ = bf16[192,512]{1,0:T(8,128)(2,1)S(1)} collective-permute-done((bf16[192,512]{1,0:T(8,128)(2,1)S(1)}, bf16[192,512]{1,0:T(8,128)(2,1)S(1)}, u32[]{:S(2)}, u32[]{:S(2)}) %collective-permute-start.2) | collective-permute-done | bytes 196640 | tf_op jit(solution)/shard_map/ppermute | solution.py:708
  33.8 1.5 %edge.4 = bf16[448,512]{1,0:T(8,128)(2,1)} custom-call(s32[2]{0:T(128)S(1)} %copy-done.6, f32[2,128]{1,0:T(2,128)S(1)} %pad_maximum_fusion.gain_ref, bf16[128,2048]{1,0:T(8,128)(2,1)S(1)} %bitcast.41, bf16[128,2048]{1,0:T(8,128)(2,1)S(1)} %bitcast.34, bf16[640,1024]{1,0:T(8,128)(2,1)S(1)} %collective-permute-done.mate_ref, ...), custom_call_target="tpu_custom_call" | custom-call | flops 1 | bytes 1 | tf_op jit(solution)/shard_map/edge/pallas_call | solution.py:185
  35.3 0.6 collective-permute-start.3
  36.6 0.6 fusion
  37.2 1.4 %stack.74.meta_ref = s32[15]{0:T(128)S(1)} concatenate(s32[1]{0:T(128)} %bitcast, s32[1]{0:T(128)} %bitcast.1, s32[1]{0:T(128)} %bitcast.2, s32[1]{0:T(128)} %bitcast.3, s32[1]{0:T(128)S(6)} %copy.28, s32[1]{0:T(128)} %bitcast.4, s32[1]{0:T(128)} %bitcast.5, s32[1]{0:T(128)} %bitcast.6, s32[1]{0:T(128)} %bitcast.7, s32[1]{0:T(128)} %bitcast.8, s32[1]{0:T(128)} %bitcast.9, ...), dimensions={0} | concatenate | bytes 120 | tf_op jit(solution)/shard_map/stack | solution.py:737
  38.6 0.9 prepare_keys.1.key_ref
  39.5 0.0 copy-start.2
  39.5 0.0 copy-start.3
  39.5 4.9 %collective-permute-done.4.refs_0_.refs_1_ = bf16[192,512]{1,0:T(8,128)(2,1)S(1)} collective-permute-done((bf16[192,512]{1,0:T(8,128)(2,1)S(1)}, bf16[192,512]{1,0:T(8,128)(2,1)S(1)}, u32[]{:S(2)}, u32[]{:S(2)}) %collective-permute-start.4) | collective-permute-done | bytes 196640 | tf_op jit(solution)/shard_map/ppermute | solution.py:708
  44.4 0.7 edge.5
  45.1 0.7 collective-permute-start.5
  45.8 0.0 collective-permute-done.7.one_ref
  45.8 0.0 collective-permute-done.8.mid_ref
  45.9 5.6 %attention.2 = (bf16[128,512]{1,0:T(8,128)(2,1)S(1)}, bf16[128,512]{1,0:T(8,128)(2,1)S(1)}, bf16[256,512]{1,0:T(8,128)(2,1)S(1)}, f32[256,512]{1,0:T(8,128)S(1)}...) custom-call(s32[15]{0:T(128)S(1)} %stack.74.meta_ref, ...), custom_call_target="tpu_custom_call" | custom-call | flops 1207959552 | bytes 8388608 | tf_op jit(solution)/shard_map/attention/pallas_call | solution.py:421
  51.5 1.3 %collective-permute-start.9 = (bf16[192,512]{1,0:T(8,128)(2,1)S(1)}, bf16[192,512]{1,0:T(8,128)(2,1)S(1)}, u32[]{:S(2)}, u32[]{:S(2)}) collective-permute-start(bf16[192,512]{1,0:T(8,128)(2,1)S(1)} %get-tuple-element.50), channel_id=1, source_target_pairs={{0,2},{1,3},{2,0},{3,1},{4,6},{5,7},{6,4},{7,5},{8,10},{9,11},{10,... | collective-permute-start | bytes 589832 | tf_op jit(solution)/shard_map/ppermute | solution.py:708
  52.8 0.8 collective-permute-start.6
  53.6 1.3 %collective-permute-start.12 = (bf16[448,512]{1,0:T(8,128)(2,1)S(1)}, bf16[448,512]{1,0:T(8,128)(2,1)S(1)}, u32[]{:S(2)}, u32[]{:S(2)}) collective-permute-start(bf16[448,512]{1,0:T(8,128)(2,1)S(1)} %get-tuple-element.56), channel_id=1, source_target_pairs={{0,2},{1,3},{2,0},{3,1},{4,6},{5,7},{6,4},{7,5},{8,10},{9,11},{10,... | collective-permute-start | bytes 1376264 | tf_op jit(solution)/shard_map/ppermute | solution.py:708
  54.9 4.5 %collective-permute-done.9.arrived_ref = bf16[192,512]{1,0:T(8,128)(2,1)S(1)} collective-permute-done((bf16[192,512]{1,0:T(8,128)(2,1)S(1)}, bf16[192,512]{1,0:T(8,128)(2,1)S(1)}, u32[]{:S(2)}, u32[]{:S(2)}) %collective-permute-start.9) | collective-permute-done | bytes 196640 | tf_op jit(solution)/shard_map/ppermute | solution.py:708
  59.4 0.7 collective-permute-start.11
  60.1 3.5 %collective-permute-done.6.refs_2_ = bf16[192,512]{1,0:T(8,128)(2,1)S(1)} collective-permute-done((bf16[192,512]{1,0:T(8,128)(2,1)S(1)}, bf16[192,512]{1,0:T(8,128)(2,1)S(1)}, u32[]{:S(2)}, u32[]{:S(2)}) %collective-permute-start.6) | collective-permute-done | bytes 196640 | tf_op jit(solution)/shard_map/ppermute | solution.py:708
  63.6 0.0 collective-permute-done.5.mid_ref
  63.6 0.0 collective-permute-done.3.one_ref
  63.6 5.5 %attention.3 = (bf16[128,512]{1,0:T(8,128)(2,1)S(1)}, bf16[128,512]{1,0:T(8,128)(2,1)S(1)}, bf16[256,512]{1,0:T(8,128)(2,1)S(1)}, f32[256,512]{1,0:T(8,128)S(1)}...) custom-call(s32[15]{0:T(128)S(1)} %stack.74.meta_ref, ...), custom_call_target="tpu_custom_call" | custom-call | flops 1207959552 | bytes 8388608 | tf_op jit(solution)/shard_map/attention/pallas_call | solution.py:421
  69.2 1.3 %collective-permute-start.10 = (bf16[208,512]{1,0:T(8,128)(2,1)S(1)}, bf16[208,512]{1,0:T(8,128)(2,1)S(1)}, u32[]{:S(2)}, u32[]{:S(2)}) collective-permute-start(bf16[208,512]{1,0:T(8,128)(2,1)S(1)} %get-tuple-element.52), channel_id=1, source_target_pairs={{0,2},{1,3},{2,0},{3,1},{4,6},{5,7},{6,4},{7,5},{8,10},{9,11},{10,... | collective-permute-start | bytes 638984 | tf_op jit(solution)/shard_map/ppermute | solution.py:708
  70.5 1.9 %collective-permute-start.13 = (bf16[192,512]{1,0:T(8,128)(2,1)S(1)}, bf16[192,512]{1,0:T(8,128)(2,1)S(1)}, u32[]{:S(2)}, u32[]{:S(2)}) collective-permute-start(bf16[192,512]{1,0:T(8,128)(2,1)S(1)} %relay.2.refs_4_), channel_id=1, source_target_pairs={{0,4},{1,5},{2,6},{3,7},{4,0},{5,1},{6,2},{7,3},{8,12},{9,13},{10,... | collective-permute-start | bytes 589832 | tf_op jit(solution)/shard_map/ppermute | solution.py:708
  72.4 0.0 collective-permute-done.11.refs_2_.refs_6_
  72.4 6.8 %collective-permute-done.13.refs_4_.refs_2_ = bf16[192,512]{1,0:T(8,128)(2,1)S(1)} collective-permute-done((bf16[192,512]{1,0:T(8,128)(2,1)S(1)}, bf16[192,512]{1,0:T(8,128)(2,1)S(1)}, u32[]{:S(2)}, u32[]{:S(2)}) %collective-permute-start.13) | collective-permute-done | bytes 196640 | tf_op jit(solution)/shard_map/ppermute | solution.py:708
  79.2 0.0 collective-permute-done.12.refs_3_.refs_1_.refs_5_
  79.2 1.0 collective-permute-done.10.arrived_ref
  80.3 2.0 %collective-permute-start.17 = (bf16[448,512]{1,0:T(8,128)(2,1)S(1)}, bf16[448,512]{1,0:T(8,128)(2,1)S(1)}, u32[]{:S(2)}, u32[]{:S(2)}) collective-permute-start(bf16[448,512]{1,0:T(8,128)(2,1)S(1)} %get-tuple-element.60), channel_id=1, source_target_pairs={{0,2},{1,3},{2,0},{3,1},{4,6},{5,7},{6,4},{7,5},{8,10},{9,11},{10,... | collective-permute-start | bytes 1376264 | tf_op jit(solution)/shard_map/ppermute | solution.py:708
  82.3 0.7 collective-permute-start.19
  83.0 3.3 %collective-permute-start.18 = (bf16[192,512]{1,0:T(8,128)(2,1)S(1)}, bf16[192,512]{1,0:T(8,128)(2,1)S(1)}, u32[]{:S(2)}, u32[]{:S(2)}) collective-permute-start(bf16[192,512]{1,0:T(8,128)(2,1)S(1)} %get-tuple-element.61), channel_id=1, source_target_pairs={{0,4},{1,5},{2,6},{3,7},{4,0},{5,1},{6,2},{7,3},{8,12},{9,13},{10,... | collective-permute-start | bytes 589832 | tf_op jit(solution)/shard_map/ppermute | solution.py:708
  86.3 1.5 %collective-permute-start.14 = (f32[8,128]{1,0:T(8,128)S(1)}, f32[8,128]{1,0:T(8,128)S(1)}, u32[]{:S(2)}, u32[]{:S(2)}) collective-permute-start(f32[8,128]{1,0:T(8,128)S(1)} %get-tuple-element.57), channel_id=1, source_target_pairs={{0,8},{8,0},{16,24},{24,16},{1,9},{9,1},{17,25},{25,17},{2,10},{10... | collective-permute-start | bytes 12296 | tf_op jit(solution)/shard_map/ppermute | solution.py:677
  87.7 2.1 %collective-permute-done.14 = f32[8,128]{1,0:T(8,128)S(1)} collective-permute-done((f32[8,128]{1,0:T(8,128)S(1)}, f32[8,128]{1,0:T(8,128)S(1)}, u32[]{:S(2)}, u32[]{:S(2)}) %collective-permute-start.14) | collective-permute-done | bytes 4128 | tf_op jit(solution)/shard_map/ppermute | solution.py:677
  89.9 1.5 %collective-permute-start.15 = (f32[8,128]{1,0:T(8,128)S(1)}, f32[8,128]{1,0:T(8,128)S(1)}, u32[]{:S(2)}, u32[]{:S(2)}) collective-permute-start(f32[8,128]{1,0:T(8,128)S(1)} %add.51), channel_id=1, source_target_pairs={{0,16},{8,24},{16,0},{24,8},{1,17},{9,25},{17,1},{25,9},{2,18},{10... | collective-permute-start | bytes 12296 | tf_op jit(solution)/shard_map/ppermute | solution.py:677
  91.4 2.1 %collective-permute-done.15 = f32[8,128]{1,0:T(8,128)S(1)} collective-permute-done((f32[8,128]{1,0:T(8,128)S(1)}, f32[8,128]{1,0:T(8,128)S(1)}, u32[]{:S(2)}, u32[]{:S(2)}) %collective-permute-start.15) | collective-permute-done | bytes 4128 | tf_op jit(solution)/shard_map/ppermute | solution.py:677
  93.5 0.1 collective-permute-start.16
  93.6 4.4 %collective-permute-done.16 = f32[8,128]{1,0:T(8,128)S(1)} collective-permute-done((f32[8,128]{1,0:T(8,128)S(1)}, f32[8,128]{1,0:T(8,128)S(1)}, u32[]{:S(2)}, u32[]{:S(2)}) %collective-permute-start.16) | collective-permute-done | bytes 4128 | tf_op jit(solution)/shard_map/ppermute | solution.py:677
  98.0 0.0 collective-permute-done.18.refs_5_
  98.0 0.0 collective-permute-done.17.refs_4_.refs_12_
  98.0 0.9 finish_lyric.1
  98.9 0.0 collective-permute-done.19.refs_13_
  98.9 2.3 %finish_audio.1 = (bf16[128,2048]{1,0:T(8,128)(2,1)}, bf16[128,2048]{1,0:T(8,128)(2,1)}, bf16[128,2048]{1,0:T(8,128)(2,1)}, bf16[128,2048]{1,0:T(8,128)(2,1)}, bf16[624,1024]{1,0:T(8,128)(2,1)S(1)}) custom-call(s32[2]{0:T(128)S(1)} %copy-done.6, f32[2,128]{1,0:T(2,128)S(1)} %pad_maximum_fusion.gain_ref, bf16[128,2048]{1,0:T(8,128)(2,1)S(1)} %bitcast.44, ...), custom_call_target="tpu_custom_call" | custom-call | flops 1 | bytes 1 | tf_op jit(solution)/shard_map/finish_audio/pallas_call | solution.py:500
  101.2 0.1 collective-permute-start.20
  101.3 3.0 %collective-permute-done.20.mate_ref = bf16[624,1024]{1,0:T(8,128)(2,1)S(1)} collective-permute-done((bf16[624,1024]{1,0:T(8,128)(2,1)S(1)}, bf16[624,1024]{1,0:T(8,128)(2,1)S(1)}, u32[]{:S(2)}, u32[]{:S(2)}) %collective-permute-start.20) | collective-permute-done | bytes 1277984 | tf_op jit(solution)/shard_map/ppermute | solution.py:802
  104.3 2.2 %join.1 = (bf16[128,2048]{1,0:T(8,128)(2,1)}, bf16[128,2048]{1,0:T(8,128)(2,1)}, bf16[128,2048]{1,0:T(8,128)(2,1)}, bf16[128,2048]{1,0:T(8,128)(2,1)}, bf16[48,2...) custom-call(s32[2]{0:T(128)S(1)} %copy-done.6, ...), custom_call_target="tpu_custom_call", output_to_operand_aliasing={{0}: (4, {}), {1}: (5, {}), {2}: (6, {}), {3}: (7, {})} | custom-call | flops 1 | bytes 1 | tf_op jit(solution)/shard_map/join/pallas_call | solution.py:605
  (20 shorter events, 0.1 us)
Async XLA Ops:
  1.3 3.7 %copy-start.8 = (f32[128]{0:T(128)S(1)}, f32[128]{0:T(128)}, u32[]{:S(2)}) copy-start(f32[128]{0:T(128)} %param.16) | copy-start | bytes 1540
  1.3 3.7 %copy-start.9 = (f32[128]{0:T(128)S(1)}, f32[128]{0:T(128)}, u32[]{:S(2)}) copy-start(f32[128]{0:T(128)} %param.15) | copy-start | bytes 1540
  1.3 6.6 %copy-start.4 = (bf16[1,48,2048]{2,1,0:T(8,128)(2,1)S(1)}, bf16[1,48,2048]{2,1,0:T(8,128)(2,1)}, u32[]{:S(2)}) copy-start(bf16[1,48,2048]{2,1,0:T(8,128)(2,1)} %param.13) | copy-start | bytes 589828
  1.3 6.6 %copy-start.5 = (bf16[1,48,2048]{2,1,0:T(8,128)(2,1)S(1)}, bf16[1,48,2048]{2,1,0:T(8,128)(2,1)}, u32[]{:S(2)}) copy-start(bf16[1,48,2048]{2,1,0:T(8,128)(2,1)} %param.14) | copy-start | bytes 589828
  1.3 6.6 %copy-start.6 = (s32[2]{0:T(128)S(1)}, s32[2]{0:T(128)}, u32[]{:S(2)}) copy-start(s32[2]{0:T(128)} %pad_add_fusion.state_ref) | copy-start | bytes 28
  4.5 8.1 %copy-start = (bf16[1,128,2048]{2,1,0:T(8,128)(2,1)S(1)}, bf16[1,128,2048]{2,1,0:T(8,128)(2,1)}, u32[]{:S(2)}) copy-start(bf16[1,128,2048]{2,1,0:T(8,128)(2,1)} %param.12) | copy-start | bytes 1572868
  4.5 8.1 %copy-start.1 = (bf16[1,128,2048]{2,1,0:T(8,128)(2,1)S(1)}, bf16[1,128,2048]{2,1,0:T(8,128)(2,1)}, u32[]{:S(2)}) copy-start(bf16[1,128,2048]{2,1,0:T(8,128)(2,1)} %param.11) | copy-start | bytes 1572868
  4.5 3.4 %collective-permute-start = (bf16[640,1024]{1,0:T(8,128)(2,1)}, bf16[640,1024]{1,0:T(8,128)(2,1)S(1)}, u32[]{:S(2)}, u32[]{:S(2)}) collective-permute-start(bf16[640,1024]{1,0:T(8,128)(2,1)} %pack.1), channel_id=1, source_target_pairs={{0,1},{1,0},{2,3},{3,2},{4,5},{5,4},{6,7},{7,6},{8,9},{9,8},{10,11... | collective-permute-start | bytes 3932168 | tf_op jit(solution)/shard_map/ppermute | solution.py:753
  8.6 13.5 %collective-permute-start.1 = (bf16[192,512]{1,0:T(8,128)(2,1)S(1)}, bf16[192,512]{1,0:T(8,128)(2,1)S(1)}, u32[]{:S(2)}, u32[]{:S(2)}) collective-permute-start(bf16[192,512]{1,0:T(8,128)(2,1)S(1)} %pair_lyrics.2.refs_0_), channel_id=1, source_target_pairs={{0,4},{1,5},{2,6},{3,7},{4,0},{5,1},{6,2},{7,3},{8,12},{9,13},{10,... | collective-permute-start | bytes 589832 | tf_op jit(solution)/shard_map/ppermute | solution.py:708
  14.1 31.8 %collective-permute-start.7 = (bf16[448,512]{1,0:T(8,128)(2,1)}, bf16[448,512]{1,0:T(8,128)(2,1)}, u32[]{:S(2)}, u32[]{:S(2)}) collective-permute-start(bf16[448,512]{1,0:T(8,128)(2,1)} %edge.6), channel_id=1, source_target_pairs={{0,2},{1,3},{2,0},{3,1},{4,6},{5,7},{6,4},{7,5},{8,10},{9,11},{10,... | collective-permute-start | bytes 1376264 | tf_op jit(solution)/shard_map/ppermute | solution.py:708
  22.1 11.7 %collective-permute-start.2 = (bf16[192,512]{1,0:T(8,128)(2,1)S(1)}, bf16[192,512]{1,0:T(8,128)(2,1)S(1)}, u32[]{:S(2)}, u32[]{:S(2)}) collective-permute-start(bf16[192,512]{1,0:T(8,128)(2,1)S(1)} %collective-permute-done.1.refs_0_.refs_1_), channel_id=1, source_target_pairs={{0,2},{1,3},{2,0},{3,1},{4,6},{5,7},{6,4},{7,5},{8,10},{9,11},{10,... | collective-permute-start | bytes 589832 | tf_op jit(solution)/shard_map/ppermute | solution.py:708
  24.2 21.7 %collective-permute-start.8 = (bf16[256,512]{1,0:T(8,128)(2,1)}, bf16[256,512]{1,0:T(8,128)(2,1)}, u32[]{:S(2)}, u32[]{:S(2)}) collective-permute-start(bf16[256,512]{1,0:T(8,128)(2,1)} %edge.7), channel_id=1, source_target_pairs={{2,4},{3,5},{4,2},{5,3},{10,12},{11,13},{12,10},{13,11},{18,20},{1... | collective-permute-start | bytes 786440 | tf_op jit(solution)/shard_map/ppermute | solution.py:708
  26.2 10.3 %copy-start.7 = (s32[1,1,2]{2,1,0:T(1,128)S(1)}, s32[1,1,2]{2,1,0:T(1,128)}, u32[]{:S(2)}) copy-start(s32[1,1,2]{2,1,0:T(1,128)} %param.18) | copy-start | bytes 28
  26.2 18.2 %collective-permute-start.4 = (bf16[192,512]{1,0:T(8,128)(2,1)S(1)}, bf16[192,512]{1,0:T(8,128)(2,1)S(1)}, u32[]{:S(2)}, u32[]{:S(2)}) collective-permute-start(bf16[192,512]{1,0:T(8,128)(2,1)S(1)} %pair_lyrics.3.refs_0_), channel_id=1, source_target_pairs={{0,4},{1,5},{2,6},{3,7},{4,0},{5,1},{6,2},{7,3},{8,12},{9,13},{10,... | collective-permute-start | bytes 589832 | tf_op jit(solution)/shard_map/ppermute | solution.py:708
  35.3 28.3 %collective-permute-start.3 = (bf16[448,512]{1,0:T(8,128)(2,1)}, bf16[448,512]{1,0:T(8,128)(2,1)}, u32[]{:S(2)}, u32[]{:S(2)}) collective-permute-start(bf16[448,512]{1,0:T(8,128)(2,1)} %edge.4), channel_id=1, source_target_pairs={{0,2},{1,3},{2,0},{3,1},{4,6},{5,7},{6,4},{7,5},{8,10},{9,11},{10,... | collective-permute-start | bytes 1376264 | tf_op jit(solution)/shard_map/ppermute | solution.py:708
  39.5 6.4 %copy-start.2 = (bf16[1,128,2048]{2,1,0:T(8,128)(2,1)S(1)}, bf16[1,128,2048]{2,1,0:T(8,128)(2,1)}, u32[]{:S(2)}) copy-start(bf16[1,128,2048]{2,1,0:T(8,128)(2,1)} %param.10) | copy-start | bytes 1572868
  39.5 6.4 %copy-start.3 = (bf16[1,128,2048]{2,1,0:T(8,128)(2,1)S(1)}, bf16[1,128,2048]{2,1,0:T(8,128)(2,1)}, u32[]{:S(2)}) copy-start(bf16[1,128,2048]{2,1,0:T(8,128)(2,1)} %param.17) | copy-start | bytes 1572868
  45.1 18.5 %collective-permute-start.5 = (bf16[256,512]{1,0:T(8,128)(2,1)S(1)}, bf16[256,512]{1,0:T(8,128)(2,1)S(1)}, u32[]{:S(2)}, u32[]{:S(2)}) collective-permute-start(bf16[256,512]{1,0:T(8,128)(2,1)S(1)} %edge.5), channel_id=1, source_target_pairs={{2,4},{3,5},{4,2},{5,3},{10,12},{11,13},{12,10},{13,11},{18,20},{1... | collective-permute-start | bytes 786440 | tf_op jit(solution)/shard_map/ppermute | solution.py:708
  51.5 7.9 %collective-permute-start.9 = (bf16[192,512]{1,0:T(8,128)(2,1)S(1)}, bf16[192,512]{1,0:T(8,128)(2,1)S(1)}, u32[]{:S(2)}, u32[]{:S(2)}) collective-permute-start(bf16[192,512]{1,0:T(8,128)(2,1)S(1)} %get-tuple-element.50), channel_id=1, source_target_pairs={{0,2},{1,3},{2,0},{3,1},{4,6},{5,7},{6,4},{7,5},{8,10},{9,11},{10,... | collective-permute-start | bytes 589832 | tf_op jit(solution)/shard_map/ppermute | solution.py:708
  52.8 10.8 %collective-permute-start.6 = (bf16[192,512]{1,0:T(8,128)(2,1)S(1)}, bf16[192,512]{1,0:T(8,128)(2,1)S(1)}, u32[]{:S(2)}, u32[]{:S(2)}) collective-permute-start(bf16[192,512]{1,0:T(8,128)(2,1)S(1)} %collective-permute-done.4.refs_0_.refs_1_), channel_id=1, source_target_pairs={{0,2},{1,3},{2,0},{3,1},{4,6},{5,7},{6,4},{7,5},{8,10},{9,11},{10,... | collective-permute-start | bytes 589832 | tf_op jit(solution)/shard_map/ppermute | solution.py:708
  53.6 25.6 %collective-permute-start.12 = (bf16[448,512]{1,0:T(8,128)(2,1)S(1)}, bf16[448,512]{1,0:T(8,128)(2,1)S(1)}, u32[]{:S(2)}, u32[]{:S(2)}) collective-permute-start(bf16[448,512]{1,0:T(8,128)(2,1)S(1)} %get-tuple-element.56), channel_id=1, source_target_pairs={{0,2},{1,3},{2,0},{3,1},{4,6},{5,7},{6,4},{7,5},{8,10},{9,11},{10,... | collective-permute-start | bytes 1376264 | tf_op jit(solution)/shard_map/ppermute | solution.py:708
  59.4 13.0 %collective-permute-start.11 = (bf16[256,512]{1,0:T(8,128)(2,1)S(1)}, bf16[256,512]{1,0:T(8,128)(2,1)S(1)}, u32[]{:S(2)}, u32[]{:S(2)}) collective-permute-start(bf16[256,512]{1,0:T(8,128)(2,1)S(1)} %get-tuple-element.55), channel_id=1, source_target_pairs={{2,4},{3,5},{4,2},{5,3},{10,12},{11,13},{12,10},{13,11},{18,20},{1... | collective-permute-start | bytes 786440 | tf_op jit(solution)/shard_map/ppermute | solution.py:708
  69.2 11.1 %collective-permute-start.10 = (bf16[208,512]{1,0:T(8,128)(2,1)S(1)}, bf16[208,512]{1,0:T(8,128)(2,1)S(1)}, u32[]{:S(2)}, u32[]{:S(2)}) collective-permute-start(bf16[208,512]{1,0:T(8,128)(2,1)S(1)} %get-tuple-element.52), channel_id=1, source_target_pairs={{0,2},{1,3},{2,0},{3,1},{4,6},{5,7},{6,4},{7,5},{8,10},{9,11},{10,... | collective-permute-start | bytes 638984 | tf_op jit(solution)/shard_map/ppermute | solution.py:708
  70.5 8.7 %collective-permute-start.13 = (bf16[192,512]{1,0:T(8,128)(2,1)S(1)}, bf16[192,512]{1,0:T(8,128)(2,1)S(1)}, u32[]{:S(2)}, u32[]{:S(2)}) collective-permute-start(bf16[192,512]{1,0:T(8,128)(2,1)S(1)} %relay.2.refs_4_), channel_id=1, source_target_pairs={{0,4},{1,5},{2,6},{3,7},{4,0},{5,1},{6,2},{7,3},{8,12},{9,13},{10,... | collective-permute-start | bytes 589832 | tf_op jit(solution)/shard_map/ppermute | solution.py:708
  80.3 17.7 %collective-permute-start.17 = (bf16[448,512]{1,0:T(8,128)(2,1)S(1)}, bf16[448,512]{1,0:T(8,128)(2,1)S(1)}, u32[]{:S(2)}, u32[]{:S(2)}) collective-permute-start(bf16[448,512]{1,0:T(8,128)(2,1)S(1)} %get-tuple-element.60), channel_id=1, source_target_pairs={{0,2},{1,3},{2,0},{3,1},{4,6},{5,7},{6,4},{7,5},{8,10},{9,11},{10,... | collective-permute-start | bytes 1376264 | tf_op jit(solution)/shard_map/ppermute | solution.py:708
  82.3 16.6 %collective-permute-start.19 = (bf16[256,512]{1,0:T(8,128)(2,1)S(1)}, bf16[256,512]{1,0:T(8,128)(2,1)S(1)}, u32[]{:S(2)}, u32[]{:S(2)}) collective-permute-start(bf16[256,512]{1,0:T(8,128)(2,1)S(1)} %get-tuple-element.73), channel_id=1, source_target_pairs={{2,4},{3,5},{4,2},{5,3},{10,12},{11,13},{12,10},{13,11},{18,20},{1... | collective-permute-start | bytes 786440 | tf_op jit(solution)/shard_map/ppermute | solution.py:708
  83.0 15.0 %collective-permute-start.18 = (bf16[192,512]{1,0:T(8,128)(2,1)S(1)}, bf16[192,512]{1,0:T(8,128)(2,1)S(1)}, u32[]{:S(2)}, u32[]{:S(2)}) collective-permute-start(bf16[192,512]{1,0:T(8,128)(2,1)S(1)} %get-tuple-element.61), channel_id=1, source_target_pairs={{0,4},{1,5},{2,6},{3,7},{4,0},{5,1},{6,2},{7,3},{8,12},{9,13},{10,... | collective-permute-start | bytes 589832 | tf_op jit(solution)/shard_map/ppermute | solution.py:708
  86.3 3.6 %collective-permute-start.14 = (f32[8,128]{1,0:T(8,128)S(1)}, f32[8,128]{1,0:T(8,128)S(1)}, u32[]{:S(2)}, u32[]{:S(2)}) collective-permute-start(f32[8,128]{1,0:T(8,128)S(1)} %get-tuple-element.57), channel_id=1, source_target_pairs={{0,8},{8,0},{16,24},{24,16},{1,9},{9,1},{17,25},{25,17},{2,10},{10... | collective-permute-start | bytes 12296 | tf_op jit(solution)/shard_map/ppermute | solution.py:677
  89.9 3.6 %collective-permute-start.15 = (f32[8,128]{1,0:T(8,128)S(1)}, f32[8,128]{1,0:T(8,128)S(1)}, u32[]{:S(2)}, u32[]{:S(2)}) collective-permute-start(f32[8,128]{1,0:T(8,128)S(1)} %add.51), channel_id=1, source_target_pairs={{0,16},{8,24},{16,0},{24,8},{1,17},{9,25},{17,1},{25,9},{2,18},{10... | collective-permute-start | bytes 12296 | tf_op jit(solution)/shard_map/ppermute | solution.py:677
  93.5 4.5 %collective-permute-start.16 = (f32[8,128]{1,0:T(8,128)S(1)}, f32[8,128]{1,0:T(8,128)S(1)}, u32[]{:S(2)}, u32[]{:S(2)}) collective-permute-start(f32[8,128]{1,0:T(8,128)S(1)} %add.52), channel_id=1, source_target_pairs={{0,4},{1,5},{2,6},{3,7},{4,0},{5,1},{6,2},{7,3},{8,12},{9,13},{10,... | collective-permute-start | bytes 12296 | tf_op jit(solution)/shard_map/ppermute | solution.py:677
  101.2 3.1 %collective-permute-start.20 = (bf16[624,1024]{1,0:T(8,128)(2,1)S(1)}, bf16[624,1024]{1,0:T(8,128)(2,1)S(1)}, u32[]{:S(2)}, u32[]{:S(2)}) collective-permute-start(bf16[624,1024]{1,0:T(8,128)(2,1)S(1)} %get-tuple-element.75), channel_id=1, source_target_pairs={{0,1},{1,0},{2,3},{3,2},{4,5},{5,4},{6,7},{7,6},{8,9},{9,8},{10,11... | collective-permute-start | bytes 3833864 | tf_op jit(solution)/shard_map/ppermute | solution.py:802

commit v12 on v11

--- a/solution.py
+++ b/solution.py
@@ -114,17 +114,18 @@
         )
         copies[-1].start()
         start += rows
-    row = lax.broadcasted_iota(jnp.int32, (ALIGN_ROWS, out_ref.shape[1]), 0)
-    tiles = jnp.zeros(row.shape, jnp.int32)
-    for slot in range(TILES):
-        tiles = jnp.where(row == slot, align_ref[slot], tiles)
-    out_ref[start:, :] = tiles.astype(jnp.float32).astype(jnp.bfloat16)
+    if out_ref.shape[0] > start:
+        row = lax.broadcasted_iota(jnp.int32, (ALIGN_ROWS, out_ref.shape[1]), 0)
+        tiles = jnp.zeros(row.shape, jnp.int32)
+        for slot in range(TILES):
+            tiles = jnp.where(row == slot, align_ref[slot], tiles)
+        out_ref[start:, :] = tiles.astype(jnp.float32).astype(jnp.bfloat16)
     for copy in copies:
         copy.wait()
 
 
-def pack(state, align, arrays):
-    rows = sum(array.shape[0] for array in arrays) + ALIGN_ROWS
+def pack(state, align, arrays, extra_rows):
+    rows = sum(array.shape[0] for array in arrays) + extra_rows
     return call(
         pack_kernel,
         "pack",
@@ -172,10 +173,10 @@
     mine = state_ref[1] == touching
     own = chunk_of(key_ref, state_ref[0], chunk)
     cols = chunk_cols(chunk, out_ref.shape[1])
-    keys = jnp.where(mine, key_ref[:, own], mate_ref[2 * frames : 3 * frames, cols])
+    keys = jnp.where(mine, key_ref[:, own], mate_ref[0:frames, cols])
     norm_columns(out_ref, slice(first, first + frames), keys, gain_ref)
     out_ref[first + frames :, :] = jnp.where(
-        mine, value_ref[:, own], mate_ref[3 * frames : 4 * frames, cols]
+        mine, value_ref[:, own], mate_ref[frames : 2 * frames, cols]
     )
 
 
@@ -196,9 +197,7 @@
     frames = key_ref.shape[0]
     own = half_of(key_ref, state_ref[0])
     norm_columns(out_ref, slice(0, frames), key_ref[:, own], gain_ref)
-    norm_columns(
-        out_ref, slice(frames, 2 * frames), mate_ref[2 * frames : 3 * frames, :], gain_ref
-    )
+    norm_columns(out_ref, slice(frames, 2 * frames), mate_ref[0:frames, :], gain_ref)
 
 
 def prepare_keys(state, gains, key, mate, after):
@@ -214,7 +213,7 @@
 
 def attention_kernel(
     chunk, chained, waits, groups, head_size, score_scale, meta_ref, gain_ref, query_ref, grad_ref, value_ref, key_ref,
-    mate_ref, one_ref, mid_ref, *refs
+    mate_ref, asked_ref, one_ref, mid_ref, *refs
 ):
     frames = query_ref.shape[0]
     exchanged = len(groups) == 4
@@ -279,12 +278,9 @@
         near_rows = jnp.where(touching, one_rows, mid_rows)
         far_rows = jnp.where(touching, mid_rows, one_rows)
 
-        def from_mate(number):
-            return mate_ref[number * frames : (number + 1) * frames, half_cols]
-
-        query = jnp.concatenate([query_ref[:, own_cols], from_mate(0)], axis=0)
+        query = jnp.concatenate([query_ref[:, own_cols], asked_ref[0:frames, half_cols]], axis=0)
         query = query.astype(jnp.float32)
-        cot = jnp.concatenate([grad_ref[:, own_cols], from_mate(1)], axis=0)
+        cot = jnp.concatenate([grad_ref[:, own_cols], asked_ref[frames:, half_cols]], axis=0)
         key_low = jnp.concatenate(
             [key_ref[:, half_cols]]
             + [lyric[index][run[0] : run[0] + run[2]] for index, run in runs]
@@ -292,7 +288,7 @@
             axis=0,
         )
         value = jnp.concatenate(
-            [value_ref[:, own_cols], from_mate(3)]
+            [value_ref[:, own_cols], mate_ref[frames : 2 * frames, half_cols]]
             + [lyric[index][run[1] : run[1] + run[2]] for index, run in runs]
             + [near_rows[frames:], far_rows[frames:]],
             axis=0,
@@ -403,7 +399,8 @@
 
 
 def attention(
-    chunk, meta, gains, query, cot, value, key, mate, one, mid, lyrics, groups, earlier, after
+    chunk, meta, gains, query, cot, value, key, mate, asked, one, mid, lyrics, groups, earlier,
+    after,
 ):
     frames, width = query.shape
     head_size = gains.shape[1]
@@ -423,7 +420,7 @@
             attention_kernel, chunk, len(earlier), len(after), groups, head_size, head_size ** (-0.5)
         ),
         "attention",
-        [SMEM] + [VMEM] * (8 + len(lyrics) + len(earlier)) + [ANY] * len(after),
+        [SMEM] + [VMEM] * (9 + len(lyrics) + len(earlier)) + [ANY] * len(after),
         [VMEM] * len(out_shape),
         out_shape,
         limit=ATTENTION_VMEM_LIMIT,
@@ -433,79 +430,76 @@
             transcendentals=2 * key_rows * frames * (size // head_size),
         ),
         scratch_shapes=[pltpu.VMEM((frames + lyric_rows, 2 * frames), f32)],
-    )(meta, gains, query, cot, value, key, mate, one, mid, *lyrics, *earlier, *after)
-
-
-def finish_audio_kernel(state_ref, gain_ref, raw_ref, mate_ref, *refs):
-    chunk_refs, refs = refs[: 7 * CHUNKS], refs[7 * CHUNKS :]
-    *lyric, out, query_out, key_out, value_out, to_mate_ref, key_ref, value_ref, sems = refs
+    )(meta, gains, query, cot, value, key, mate, asked, one, mid, *lyrics, *earlier, *after)
+
+
+def finish_audio_kernel(
+    chunk, filled, state_ref, gain_ref, raw_ref, mate_ref, lyric_ref, out_own_ref, query_own_ref,
+    ready_ref, key_grad_ref, value_grad_ref, one_ref, mid_ref, *refs,
+):
+    out, query_out, key_out, value_out, to_mate_ref, key_ref, value_ref, sems = refs[filled:]
     head_size = gain_ref.shape[1]
     k_gain = gain_ref[1:2, :]
-    frames, half = key_ref.shape
-    size = half // CHUNKS
+    frames, size = key_ref.shape
     own, mate = slice(0, frames), slice(frames, 2 * frames)
     touching = state_ref[1] == 1
-    copies = []
-    for chunk in range(CHUNKS):
-        out_own_ref, query_own_ref, ready_ref = chunk_refs[7 * chunk : 7 * chunk + 3]
-        for source, target in ((out_own_ref, out), (query_own_ref, query_out)):
-            copies.append(
-                pltpu.make_async_copy(
-                    source,
-                    target.at[:, chunk_of(target, state_ref[0], chunk)],
-                    sems.at[len(copies)],
-                )
-            )
-            copies[-1].start()
-        to_mate_ref[0 : 2 * frames, chunk_cols(chunk, size)] = ready_ref[...]
-    for ref in lyric:
-        to_mate_ref[4 * frames :, :] = ref[...]
-    raw_keys = raw_ref[:, half_of(raw_ref, state_ref[0])]
-    for head in range(half // head_size):
+    copies = [
+        pltpu.make_async_copy(
+            source, target.at[:, chunk_of(target, state_ref[0], chunk)], sems.at[index]
+        )
+        for index, (source, target) in enumerate(
+            (
+                (out_own_ref, out),
+                (query_own_ref, query_out),
+                (key_ref, key_out),
+                (value_ref, value_out),
+            )
+        )
+    ]
+    copies[0].start()
+    copies[1].start()
+    to_mate_ref[0 : 2 * frames, :] = ready_ref[...]
+    if to_mate_ref.shape[0] > 4 * frames:
+        to_mate_ref[4 * frames :, :] = lyric_ref[...]
+    raw_keys = raw_ref[:, chunk_of(raw_ref, state_ref[0], chunk)]
+    mate_keys = mate_ref[0:frames, chunk_cols(chunk, size)]
+    first = one_ref.shape[0] - 2 * frames
+    for head in range(size // head_size):
         cols = slice(head * head_size, (head + 1) * head_size)
-        chunk = head * head_size // size
-        part = slice(head * head_size - chunk * size, (head + 1) * head_size - chunk * size)
-        key_grad_ref, value_grad_ref, one_ref, mid_ref = chunk_refs[7 * chunk + 3 : 7 * chunk + 7]
-        one = one_ref[one_ref.shape[0] - 2 * frames :, part].astype(jnp.float32)
-        mid = mid_ref[:, part].astype(jnp.float32)
+        one = one_ref[first:, cols].astype(jnp.float32)
+        mid = mid_ref[:, cols].astype(jnp.float32)
         for_own = jnp.where(touching, one, mid)
         for_mate = jnp.where(touching, mid, one)
         key_ref[:, cols] = through_norm(
-            raw_keys[:, cols], key_grad_ref[own, part] + for_own[:frames], k_gain
-        )
-        value_ref[:, cols] = (value_grad_ref[own, part] + for_own[frames:]).astype(jnp.bfloat16)
+            raw_keys[:, cols], key_grad_ref[own, cols] + for_own[:frames], k_gain
+        )
+        value_ref[:, cols] = (value_grad_ref[own, cols] + for_own[frames:]).astype(jnp.bfloat16)
         to_mate_ref[2 * frames : 3 * frames, cols] = through_norm(
-            mate_ref[2 * frames : 3 * frames, cols],
-            key_grad_ref[mate, part] + for_mate[:frames],
-            k_gain,
+            mate_keys[:, cols], key_grad_ref[mate, cols] + for_mate[:frames], k_gain
         )
         to_mate_ref[3 * frames : 4 * frames, cols] = (
-            value_grad_ref[mate, part] + for_mate[frames:]
+            value_grad_ref[mate, cols] + for_mate[frames:]
         ).astype(jnp.bfloat16)
-    for source, target in ((key_ref, key_out), (value_ref, value_out)):
-        copies.append(
-            pltpu.make_async_copy(
-                source, target.at[:, half_of(target, state_ref[0])], sems.at[len(copies)]
-            )
-        )
-        copies[-1].start()
+    copies[2].start()
+    copies[3].start()
     for copy in copies:
         copy.wait()
 
 
-def finish_audio(state, gains, raw, mate, chunks, lyric):
+def finish_audio(state, chunk, gains, raw, mate, lyric, arrays, filled):
     frames, width = raw.shape
-    half = width // 2
-    rows = 4 * frames + sum(array.shape[0] for array in lyric)
-    return call(
-        finish_audio_kernel,
+    size = width // 2 // CHUNKS
+    rows = 4 * frames + (lyric.shape[0] if lyric.shape[1] == size else 0)
+    return call(
+        functools.partial(finish_audio_kernel, chunk, len(filled)),
         "finish_audio",
-        [SMEM] + [VMEM] * (3 + len(chunks) + len(lyric)),
+        [SMEM] + [VMEM] * 11 + [HBM] * len(filled),
         [HBM] * 4 + [VMEM],
-        [shape(frames, width)] * 4 + [shape(rows, half)],
-        scratch_shapes=[pltpu.VMEM((frames, half), jnp.bfloat16)] * 2
-        + [pltpu.SemaphoreType.DMA((2 * CHUNKS + 2,))],
-    )(state, gains, raw, mate, *chunks, *lyric)
+        [shape(frames, width)] * 4 + [shape(rows, size)],
+        input_output_aliases={12 + i: i for i in range(len(filled))},
+        scratch_shapes=[pltpu.VMEM((frames, size), jnp.bfloat16)] * 2
+        + [pltpu.SemaphoreType.DMA((4,))],
+    )(state, gains, raw, mate, lyric, *arrays, *filled)
 
 
 def relay_kernel(part_ref, arrived_ref, *refs):
@@ -535,93 +529,104 @@
 
 
 def finish_lyric_kernel(
-    state_ref, gain_ref, raw_ref, mate_ref, sum_ref, *refs
+    chunk, summed, state_ref, gain_ref, raw_ref, mate_ref, held_ref, one_ref, two_ref, *refs
 ):
-    chunk_refs, (own_ref, to_mate_ref) = refs[:-2], refs[-2:]
+    own_ref, to_mate_ref = refs[-2:]
     rows = raw_ref.shape[0]
     head_size = gain_ref.shape[1]
     k_gain = gain_ref[1:2, :]
-    size = chunk_refs[0].shape[1]
+    size = held_ref.shape[1]
     first = mate_ref.shape[0] - ALIGN_ROWS - 2 * rows
-    to_mate_ref[2 * rows :, :] = split_rows(sum_ref[...], to_mate_ref.shape[1])
-    raw_keys = raw_ref[:, half_of(raw_ref, state_ref[0])]
-    for head in range(own_ref.shape[1] // head_size):
+    if summed:
+        to_mate_ref[2 * rows :, :] = split_rows(refs[0][...], size)
+    raw_keys = raw_ref[:, chunk_of(raw_ref, state_ref[0], chunk)]
+    mate_keys = mate_ref[first : first + rows, chunk_cols(chunk, size)]
+    for head in range(size // head_size):
         cols = slice(head * head_size, (head + 1) * head_size)
-        chunk = head * head_size // size
-        part = slice(head * head_size - chunk * size, (head + 1) * head_size - chunk * size)
-        total = chunk_refs[3 * chunk][:, part].astype(jnp.float32)
-        for ref in chunk_refs[3 * chunk + 1 : 3 * chunk + 3]:
-            total = total + ref[0 : 4 * rows, part].astype(jnp.float32)
-        mate_keys = mate_ref[first : first + rows, cols]
+        total = held_ref[:, cols].astype(jnp.float32)
+        for ref in (one_ref, two_ref):
+            total = total + ref[0 : 4 * rows, cols].astype(jnp.float32)
         for ref, base, raw in (
             (own_ref, 0, raw_keys[:, cols]),
-            (to_mate_ref, 2 * rows, mate_keys),
+            (to_mate_ref, 2 * rows, mate_keys[:, cols]),
         ):
             ref[0:rows, cols] = through_norm(raw, total[base : base + rows], k_gain)
             ref[rows : 2 * rows, cols] = total[base + rows : base + 2 * rows].astype(jnp.bfloat16)
 
 
-def finish_lyric(state, gains, raw, mate, total, chunks):
+def finish_lyric(state, chunk, gains, raw, mate, parts, sums, after):
     rows, width = raw.shape
-    half = width // 2
-    return call(
-        finish_lyric_kernel,
+    size = width // 2 // CHUNKS
+    return call(
+        functools.partial(finish_lyric_kernel, chunk, bool(sums)),
         "finish_lyric",
-        [SMEM] + [VMEM] * (4 + len(chunks)),
+        [SMEM] + [VMEM] * (6 + len(sums)) + [ANY] * len(after),
         [VMEM] * 2,
-        [shape(2 * rows, half), shape(2 * rows + GAIN_ROWS, half)],
-    )(state, gains, raw, mate, total, *chunks)
-
-
-def join_kernel(count, state_ref, gain_ref, own_ref, mate_ref, *refs):
-    outs, (q_total_ref, k_total_ref, sems) = refs[count:-3], refs[-3:]
+        [shape(2 * rows, size), shape(2 * rows + GAIN_ROWS * len(sums), size)],
+    )(state, gains, raw, mate, *parts, *sums, *after)
+
+
+def join_kernel(chunk, count, filled, state_ref, own_ref, mate_ref, *refs):
+    outs, rest = refs[filled : filled + count], refs[filled + count :]
+    sems = rest[-1]
     frames = outs[0].shape[0]
     rows = own_ref.shape[0] // 2
     pieces = [
         (mate_ref.at[index * frames : (index + 1) * frames, :], out, 1 - state_ref[0])
-        for index, out in enumerate(outs[:count])
+        for index, out in enumerate(outs[:4])
     ]
-    for ref, first, core in ((own_ref, 0, state_ref[0]), (mate_ref, count * frames, 1 - state_ref[0])):
-        for index, out in enumerate(outs[count:]):
+    for ref, first, core in ((own_ref, 0, state_ref[0]), (mate_ref, 4 * frames, 1 - state_ref[0])):
+        for index, out in enumerate(outs[4:]):
             start = first + index * rows
             pieces.append((ref.at[start : start + rows, :], out, core))
     copies = [
-        pltpu.make_async_copy(source, out.at[:, half_of(out, core)], sems.at[index])
+        pltpu.make_async_copy(source, out.at[:, chunk_of(out, core, chunk)], sems.at[index])
         for index, (source, out, core) in enumerate(pieces)
     ]
     for copy in copies:
         copy.start()
-    sums = mate_ref[mate_ref.shape[0] - GAIN_ROWS :, :]
-    total = gain_ref[...] + joined_rows(sums, gain_ref.shape[1])
-    q_total_ref[...] = total[0:1]
-    k_total_ref[...] = total[1:2]
+    if len(rest) > 1:
+        gain_ref, (q_total_ref, k_total_ref) = refs[0], rest[:2]
+        sums = mate_ref[mate_ref.shape[0] - GAIN_ROWS :, :]
+        total = gain_ref[...] + joined_rows(sums, gain_ref.shape[1])
+        q_total_ref[...] = total[0:1]
+        k_total_ref[...] = total[1:2]
     for copy in copies:
         copy.wait()
 
 
-def join(state, gain, arrays, own, mate):
-    rows, half = own.shape
-    count = len(arrays)
-    return call(
-        functools.partial(join_kernel, count),
+def join(state, chunk, own, mate, sums, filled, lyric_shape):
+    shapes = [shape(*array.shape) for array in filled[:4]] + [shape(*lyric_shape)] * 2
+    first = len(sums)
+    return call(
+        functools.partial(join_kernel, chunk, 6, first + len(filled)),
         "join",
-        [SMEM] + [VMEM] * 3 + [HBM] * count,
-        [HBM] * (count + 2) + [VMEM] * 2,
-        [shape(*array.shape) for array in arrays]
-        + [shape(rows // 2, 2 * half)] * 2
-        + [shape(1, gain.shape[1], jnp.float32)] * 2,
-        input_output_aliases={4 + i: i for i in range(count)},
-        scratch_shapes=[pltpu.SemaphoreType.DMA((count + 4,))],
-    )(state, gain, own, mate, *arrays)
-
-
-def fill_kernel(count, state_ref, mate_ref, *refs):
-    outs, sems = refs[count:-1], refs[-1]
+        [SMEM] + [VMEM] * (2 + first) + [HBM] * len(filled),
+        [HBM] * 6 + [VMEM] * (2 * first),
+        shapes + [shape(1, total.shape[1], jnp.float32) for total in sums for _ in range(2)],
+        input_output_aliases={3 + first + i: i for i in range(len(filled))},
+        scratch_shapes=[pltpu.SemaphoreType.DMA((8,))],
+    )(state, own, mate, *sums, *filled)
+
+
+def tie(block, after):
+    return call(
+        lambda *refs: None,
+        "tie",
+        [ANY] * (1 + len(after)),
+        ANY,
+        shape(*block.shape, block.dtype),
+        input_output_aliases={0: 0},
+    )(block, *after)
+
+
+def fill_kernel(chunk, state_ref, mate_ref, *refs):
+    outs, sems = refs[4:-1], refs[-1]
     frames = outs[0].shape[0]
     copies = [
         pltpu.make_async_copy(
             mate_ref.at[index * frames : (index + 1) * frames, :],
-            out.at[:, half_of(out, 1 - state_ref[0])],
+            out.at[:, chunk_of(out, 1 - state_ref[0], chunk)],
             sems.at[index],
         )
         for index, out in enumerate(outs)
@@ -632,16 +637,15 @@
         copy.wait()
 
 
-def fill_other(state, arrays, mate):
-    count = len(arrays)
-    return call(
-        functools.partial(fill_kernel, count),
+def fill_other(state, chunk, arrays, mate):
+    return call(
+        functools.partial(fill_kernel, chunk),
         "fill_other",
-        [SMEM, VMEM] + [HBM] * count,
-        [HBM] * count,
+        [SMEM, VMEM] + [HBM] * 4,
+        [HBM] * 4,
         [shape(*array.shape) for array in arrays],
-        input_output_aliases={2 + i: i for i in range(count)},
-        scratch_shapes=[pltpu.SemaphoreType.DMA((count,))],
+        input_output_aliases={2 + i: i for i in range(4)},
+        scratch_shapes=[pltpu.SemaphoreType.DMA((4,))],
     )(state, mate, *arrays)
 
 
@@ -744,13 +748,11 @@
         ]
     )
 
-    to_mate = pack(
-        state,
-        alignment[0, 0],
-        [queries[0], cotangent[0], keys[0], values[0]]
-        + ([lyric_keys[0], lyric_values[0]] if hops else []),
-    )
+    lyric_rows = [lyric_keys[0], lyric_values[0]] if hops else []
+    to_mate = pack(state, alignment[0, 0], [keys[0], values[0], *lyric_rows], ALIGN_ROWS)
     mate = lax.ppermute(to_mate, "seq", swap)
+    asked = pack(state, alignment[0, 0], [queries[0], cotangent[0]], 0)
+    asked = lax.ppermute(asked, "seq", swap)
     chunks, lyric_chunks, earlier, relayed, sent = [], [], [], [], []
     after = []
     for chunk in range(CHUNKS):
@@ -767,8 +769,8 @@
         if not chunk:
             key_low = prepare_keys(state, gains, keys[0], mate, after)
         results = attention(
-            chunk, meta, gains, queries[0], cotangent[0], values[0], key_low, mate, one, mid,
-            lyrics, groups, earlier, relayed,
+            chunk, meta, gains, queries[0], cotangent[0], values[0], key_low, mate, asked, one,
+            mid, lyrics, groups, earlier, relayed,
         )
         to_one, to_mid, gain_part, *parts = results[5:]
         earlier = [gain_part]
@@ -791,21 +793,34 @@
             lyric_chunks += parts
         chunks += [*results[:5], one_back, mid_back]
 
-    to_mate = []
+    filled, lyric_grads, totals = [], [], []
+    for chunk in range(CHUNKS):
+        sums = []
+        if hops and chunk == CHUNKS - 1:
+            gain_total = tie(sum_over(gain_total, "song", bits_of(songs)), lyric_grads)
+            sums = [sum_over(gain_total, "seq", [4])]
+        if hops:
+            own_lyric, lyric = finish_lyric(
+                state, chunk, gains, lyric_keys[0], mate, lyric_chunks[3 * chunk : 3 * chunk + 3],
+                sums, [to_two],
+            )
+        else:
+            lyric = gains
+        *filled, to_mate = finish_audio(
+            state, chunk, gains, keys[0], mate, lyric, chunks[7 * chunk : 7 * chunk + 7], filled
+        )
+        from_mate = lax.ppermute(to_mate, "seq", swap)
+        if hops:
+            results = join(
+                state, chunk, own_lyric, from_mate, sums, [*filled, *lyric_grads],
+                (lyric_local, width),
+            )
+            filled, lyric_grads, totals = results[:4], results[4:6], results[6:]
+        else:
+            filled = fill_other(state, chunk, filled, from_mate)
     if hops:
-        gain_total = sum_over(sum_over(gain_total, "song", bits_of(songs)), "seq", [4])
-        own_half, part_to_mate = finish_lyric(
-            state, gains, lyric_keys[0], mate, gain_total, lyric_chunks
-        )
-        to_mate = [part_to_mate]
-    *filled, to_mate = finish_audio(state, gains, keys[0], mate, chunks, to_mate)
-    from_mate = lax.ppermute(to_mate, "seq", swap)
-    if hops:
-        *filled, grad_lyric_keys, grad_lyric_values, q_total, k_total = join(
-            state, gain_total, filled, own_half, from_mate
-        )
+        (grad_lyric_keys, grad_lyric_values), (q_total, k_total) = lyric_grads, totals
     else:
-        filled = fill_other(state, filled, from_mate)
         gain_total = lax.psum(gain_part, ("song", "seq"))
         q_total, k_total = gain_total[0:1], gain_total[1:2]
         spread = lax.dynamic_update_slice(

time: 107 us -> 112 us (1.047)
  Pallas kernels: 27.2 us -> 32.5 us
  waiting for transfers between devices: 45.2 us -> 42.4 us
  local copies, waits for them, and re-layouts: 2.02 us -> 4.52 us
    pallas_call x3 -> x7, Pallas kernels: 5.41 us -> 8.37 us  [the longest x2 3.44 us: finish_audio(): call(functools.partial(finish_audio_kernel, chunk, len(filled)), 'finish_...]
    unnamed x20 -> x26, local copies, waits for them, and re-layouts: 0.05 us -> 2.56 us
    pallas_call x1 -> x2, Pallas kernels: 3.17 us -> 5.46 us  [pack(): call(pack_kernel, 'pack', [SMEM, SMEM] + [HBM] * len(arrays), VMEM, shape...]
    ppermute x1, waiting for transfers between devices: 2.86 us -> 1.44 us  [body(): mate = lax.ppermute(to_mate, 'seq', swap)]
    ppermute x1 -> x2, waiting for transfers between devices: 2.97 us -> 2.06 us  [body(): from_mate = lax.ppermute(to_mate, 'seq', swap)]
  transfers between devices with their start and end apart: 21 -> 23, of which waited for: 12 -> 11; matrix products, arithmetic and copies ran while one was open for 2% -> 2% of each run, Pallas kernels for 18% -> 20%
where the time goes in v12:
time: 112 us
  waiting for transfers between devices  42.4 us (38%)
  Pallas kernels  32.5 us (29%)
  starting transfers between devices  29.9 us (27%)
  local copies, waits for them, and re-layouts  4.52 us (4%)
  between operations  1.63 us (1%)
    ppermute x16, waiting for transfers between devices, hop(): return lax.ppermute(block, 'seq', pairs)  30.3 us
    ppermute x16, starting transfers between devices, hop(): return lax.ppermute(block, 'seq', pairs)  26.1 us
    pallas_call x2, Pallas kernels, attention(): call(functools.partial(attention_kernel, chunk, len(earlier), len(after),...  11.2 us
    ppermute x3, waiting for transfers between devices, sum_over(): lax.ppermute(total, axis, [(i, i ^ bit) for i in range(count)])  8.62 us
    pallas_call x2, Pallas kernels, pack(): call(pack_kernel, 'pack', [SMEM, SMEM] + [HBM] * len(arrays), VMEM, shape...  5.46 us
    pallas_call x4, Pallas kernels, edge(): call(functools.partial(edge_kernel, chunk, touching, bool(lead)), 'edge',...  5.08 us
    pallas_call x2, Pallas kernels, finish_audio(): call(functools.partial(finish_audio_kernel, chunk, len(filled)), 'finish_...  3.44 us
    pallas_call x2, Pallas kernels, join(): call(functools.partial(join_kernel, chunk, 6, first + len(filled)), 'join...  3.42 us
  transfers between devices with their start and end apart: 23, of which 11 were waited for; matrix products, arithmetic and copies ran while one was open for 2% of the time, Pallas kernels for 20%

profile of v12, /device:TPU:0, one launch (start us, length us, event | category | flops | bytes accessed | tf_op | source)
XLA Modules:
  0.0 111.5 jit_solution(17107096645407081312)
XLA Ops:
  0.7 0.6 pad_add_fusion.state_ref
  1.3 2.8 %pack.2 = bf16[384,1024]{1,0:T(8,128)(2,1)} custom-call(s32[2]{0:T(128)} %pad_add_fusion.state_ref, s32[2]{0:T(128)} %bitcast.66, bf16[128,2048]{1,0:T(8,128)(2,1)} %bitcast.31, bf16[128,2048]{1,0:T(8,128)(2,1)} %bitcast.39, bf16[48,2048]{1,0:T(8,128)(2,1)} %bitcast.46, bf16[48,2048]{1,0:T(8,128)(2,1)} %bitcast.57), custom_call_target="tpu_custom_call" | custom-call | flops 1 | bytes 1 | tf_op jit(solution)/shard_map/pack/pallas_call | solution.py:129
  4.1 0.5 collective-permute-start
  4.6 0.7 copy-done.11
  5.3 0.0 copy-done.12
  5.3 1.4 %collective-permute-done.mate_ref = bf16[384,1024]{1,0:T(8,128)(2,1)S(1)} collective-permute-done((bf16[384,1024]{1,0:T(8,128)(2,1)}, bf16[384,1024]{1,0:T(8,128)(2,1)S(1)}, u32[]{:S(2)}, u32[]{:S(2)}) %collective-permute-start) | collective-permute-done | bytes 786464 | tf_op jit(solution)/shard_map/ppermute | solution.py:753
  6.7 0.7 pair_lyrics.2.refs_0_
  7.4 4.0 %collective-permute-start.1 = (bf16[192,512]{1,0:T(8,128)(2,1)S(1)}, bf16[192,512]{1,0:T(8,128)(2,1)S(1)}, u32[]{:S(2)}, u32[]{:S(2)}) collective-permute-start(bf16[192,512]{1,0:T(8,128)(2,1)S(1)} %pair_lyrics.2.refs_0_), channel_id=1, source_target_pairs={{0,4},{1,5},{2,6},{3,7},{4,0},{5,1},{6,2},{7,3},{8,12},{9,13},{10,... | collective-permute-start | bytes 589832 | tf_op jit(solution)/shard_map/ppermute | solution.py:712
  11.5 2.6 %pack.3 = bf16[256,1024]{1,0:T(8,128)(2,1)} custom-call(s32[2]{0:T(128)} %pad_add_fusion.state_ref, s32[2]{0:T(128)} %bitcast.67, bf16[128,2048]{1,0:T(8,128)(2,1)} %bitcast.51, bf16[128,2048]{1,0:T(8,128)(2,1)} %bitcast.54), custom_call_target="tpu_custom_call" | custom-call | flops 1 | bytes 1 | tf_op jit(solution)/shard_map/pack/pallas_call | solution.py:129
  14.1 0.1 collective-permute-start.2
  14.2 1.5 %edge.6 = bf16[448,512]{1,0:T(8,128)(2,1)} custom-call(s32[2]{0:T(128)S(1)} %copy-done.9, f32[2,128]{1,0:T(2,128)S(1)} %pad_maximum_fusion.gain_ref, bf16[128,2048]{1,0:T(8,128)(2,1)S(1)} %bitcast.32, bf16[128,2048]{1,0:T(8,128)(2,1)S(1)} %bitcast.40, bf16[384,1024]{1,0:T(8,128)(2,1)S(1)} %collective-permute-done.mate_ref, ...), custom_call_target="tpu_custom_call" | custom-call | flops 1 | bytes 1 | tf_op jit(solution)/shard_map/edge/pallas_call | solution.py:186
  15.7 1.6 %collective-permute-start.8 = (bf16[448,512]{1,0:T(8,128)(2,1)}, bf16[448,512]{1,0:T(8,128)(2,1)}, u32[]{:S(2)}, u32[]{:S(2)}) collective-permute-start(bf16[448,512]{1,0:T(8,128)(2,1)} %edge.6), channel_id=1, source_target_pairs={{0,2},{1,3},{2,0},{3,1},{4,6},{5,7},{6,4},{7,5},{8,10},{9,11},{10,... | collective-permute-start | bytes 1376264 | tf_op jit(solution)/shard_map/ppermute | solution.py:712
  17.3 3.7 %collective-permute-done.1.refs_0_.refs_1_ = bf16[192,512]{1,0:T(8,128)(2,1)S(1)} collective-permute-done((bf16[192,512]{1,0:T(8,128)(2,1)S(1)}, bf16[192,512]{1,0:T(8,128)(2,1)S(1)}, u32[]{:S(2)}, u32[]{:S(2)}) %collective-permute-start.1) | collective-permute-done | bytes 196640 | tf_op jit(solution)/shard_map/ppermute | solution.py:712
  21.0 0.7 collective-permute-start.3
  21.6 1.4 %edge.7 = bf16[256,512]{1,0:T(8,128)(2,1)} custom-call(s32[2]{0:T(128)S(1)} %copy-done.9, f32[2,128]{1,0:T(2,128)S(1)} %pad_maximum_fusion.gain_ref, bf16[128,2048]{1,0:T(8,128)(2,1)S(1)} %bitcast.33, bf16[128,2048]{1,0:T(8,128)(2,1)S(1)} %bitcast.41, bf16[384,1024]{1,0:T(8,128)(2,1)S(1)} %collective-permute-done.mate_ref, ...), custom_call_target="tpu_custom_call" | custom-call | flops 1 | bytes 1 | tf_op jit(solution)/shard_map/edge/pallas_call | solution.py:186
  23.0 1.4 %collective-permute-start.9 = (bf16[256,512]{1,0:T(8,128)(2,1)}, bf16[256,512]{1,0:T(8,128)(2,1)}, u32[]{:S(2)}, u32[]{:S(2)}) collective-permute-start(bf16[256,512]{1,0:T(8,128)(2,1)} %edge.7), channel_id=1, source_target_pairs={{2,4},{3,5},{4,2},{5,3},{10,12},{11,13},{12,10},{13,11},{18,20},{1... | collective-permute-start | bytes 786440 | tf_op jit(solution)/shard_map/ppermute | solution.py:712
  24.4 0.7 pair_lyrics.3.refs_0_
  25.1 4.1 %collective-permute-start.5 = (bf16[192,512]{1,0:T(8,128)(2,1)S(1)}, bf16[192,512]{1,0:T(8,128)(2,1)S(1)}, u32[]{:S(2)}, u32[]{:S(2)}) collective-permute-start(bf16[192,512]{1,0:T(8,128)(2,1)S(1)} %pair_lyrics.3.refs_0_), channel_id=1, source_target_pairs={{0,4},{1,5},{2,6},{3,7},{4,0},{5,1},{6,2},{7,3},{8,12},{9,13},{10,... | collective-permute-start | bytes 589832 | tf_op jit(solution)/shard_map/ppermute | solution.py:712
  29.2 5.8 %collective-permute-done.3.refs_1_.refs_2_ = bf16[192,512]{1,0:T(8,128)(2,1)S(1)} collective-permute-done((bf16[192,512]{1,0:T(8,128)(2,1)S(1)}, bf16[192,512]{1,0:T(8,128)(2,1)S(1)}, u32[]{:S(2)}, u32[]{:S(2)}) %collective-permute-start.3) | collective-permute-done | bytes 196640 | tf_op jit(solution)/shard_map/ppermute | solution.py:712
  34.9 1.5 %edge.4 = bf16[448,512]{1,0:T(8,128)(2,1)} custom-call(s32[2]{0:T(128)S(1)} %copy-done.9, f32[2,128]{1,0:T(2,128)S(1)} %pad_maximum_fusion.gain_ref, bf16[128,2048]{1,0:T(8,128)(2,1)S(1)} %bitcast.34, bf16[128,2048]{1,0:T(8,128)(2,1)S(1)} %bitcast.42, bf16[384,1024]{1,0:T(8,128)(2,1)S(1)} %collective-permute-done.mate_ref, ...), custom_call_target="tpu_custom_call" | custom-call | flops 1 | bytes 1 | tf_op jit(solution)/shard_map/edge/pallas_call | solution.py:186
  36.4 0.1 collective-permute-start.4
  37.2 0.6 fusion
  37.8 1.4 %stack.77.meta_ref = s32[15]{0:T(128)S(1)} concatenate(s32[1]{0:T(128)} %bitcast, s32[1]{0:T(128)} %bitcast.1, s32[1]{0:T(128)} %bitcast.9, s32[1]{0:T(128)} %bitcast.10, s32[1]{0:T(128)S(6)} %copy.50, s32[1]{0:T(128)} %bitcast.11, s32[1]{0:T(128)} %bitcast.12, s32[1]{0:T(128)} %bitcast.13, s32[1]{0:T(128)} %bitcast.14, s32[1]{0:T(128)} %bitcast.15, s32[1]{0:T(128)} %bitcast.16, ...), dimensions={0} | concatenate | bytes 120 | tf_op jit(solution)/shard_map/stack | solution.py:741
  39.1 0.9 prepare_keys.1.key_ref
  40.0 0.0 copy-start.3
  40.1 0.0 copy-start.4
  40.1 3.2 %collective-permute-done.5.refs_0_.refs_1_ = bf16[192,512]{1,0:T(8,128)(2,1)S(1)} collective-permute-done((bf16[192,512]{1,0:T(8,128)(2,1)S(1)}, bf16[192,512]{1,0:T(8,128)(2,1)S(1)}, u32[]{:S(2)}, u32[]{:S(2)}) %collective-permute-start.5) | collective-permute-done | bytes 196640 | tf_op jit(solution)/shard_map/ppermute | solution.py:712
  43.3 0.7 edge.5
  44.0 0.7 collective-permute-start.6
  44.7 0.0 collective-permute-done.2.asked_ref
  44.7 0.0 collective-permute-done.8.one_ref
  44.7 5.6 %attention.2 = (bf16[128,512]{1,0:T(8,128)(2,1)S(1)}, bf16[128,512]{1,0:T(8,128)(2,1)S(1)}, bf16[256,512]{1,0:T(8,128)(2,1)S(1)}, f32[256,512]{1,0:T(8,128)S(1)}...) custom-call(s32[15]{0:T(128)S(1)} %stack.77.meta_ref, ...), custom_call_target="tpu_custom_call" | custom-call | flops 1207959552 | bytes 8388608 | tf_op jit(solution)/shard_map/attention/pallas_call | solution.py:418
  50.4 2.9 %collective-permute-start.10 = (bf16[192,512]{1,0:T(8,128)(2,1)S(1)}, bf16[192,512]{1,0:T(8,128)(2,1)S(1)}, u32[]{:S(2)}, u32[]{:S(2)}) collective-permute-start(bf16[192,512]{1,0:T(8,128)(2,1)S(1)} %get-tuple-element.63), channel_id=1, source_target_pairs={{0,2},{1,3},{2,0},{3,1},{4,6},{5,7},{6,4},{7,5},{8,10},{9,11},{10,... | collective-permute-start | bytes 589832 | tf_op jit(solution)/shard_map/ppermute | solution.py:712
  53.3 0.1 collective-permute-start.7
  53.3 1.9 %collective-permute-start.13 = (bf16[448,512]{1,0:T(8,128)(2,1)S(1)}, bf16[448,512]{1,0:T(8,128)(2,1)S(1)}, u32[]{:S(2)}, u32[]{:S(2)}) collective-permute-start(bf16[448,512]{1,0:T(8,128)(2,1)S(1)} %get-tuple-element.70), channel_id=1, source_target_pairs={{0,2},{1,3},{2,0},{3,1},{4,6},{5,7},{6,4},{7,5},{8,10},{9,11},{10,... | collective-permute-start | bytes 1376264 | tf_op jit(solution)/shard_map/ppermute | solution.py:712
  55.3 3.7 %collective-permute-done.10.arrived_ref = bf16[192,512]{1,0:T(8,128)(2,1)S(1)} collective-permute-done((bf16[192,512]{1,0:T(8,128)(2,1)S(1)}, bf16[192,512]{1,0:T(8,128)(2,1)S(1)}, u32[]{:S(2)}, u32[]{:S(2)}) %collective-permute-start.10) | collective-permute-done | bytes 196640 | tf_op jit(solution)/shard_map/ppermute | solution.py:712
  59.0 0.7 collective-permute-start.12
  59.8 3.5 %collective-permute-done.7.refs_2_ = bf16[192,512]{1,0:T(8,128)(2,1)S(1)} collective-permute-done((bf16[192,512]{1,0:T(8,128)(2,1)S(1)}, bf16[192,512]{1,0:T(8,128)(2,1)S(1)}, u32[]{:S(2)}, u32[]{:S(2)}) %collective-permute-start.7) | collective-permute-done | bytes 196640 | tf_op jit(solution)/shard_map/ppermute | solution.py:712
  63.2 5.6 %attention.3 = (bf16[128,512]{1,0:T(8,128)(2,1)S(1)}, bf16[128,512]{1,0:T(8,128)(2,1)S(1)}, bf16[256,512]{1,0:T(8,128)(2,1)S(1)}, f32[256,512]{1,0:T(8,128)S(1)}...) custom-call(s32[15]{0:T(128)S(1)} %stack.77.meta_ref, ...), custom_call_target="tpu_custom_call" | custom-call | flops 1207959552 | bytes 8388608 | tf_op jit(solution)/shard_map/attention/pallas_call | solution.py:418
  68.8 2.1 %collective-permute-start.11 = (bf16[208,512]{1,0:T(8,128)(2,1)S(1)}, bf16[208,512]{1,0:T(8,128)(2,1)S(1)}, u32[]{:S(2)}, u32[]{:S(2)}) collective-permute-start(bf16[208,512]{1,0:T(8,128)(2,1)S(1)} %get-tuple-element.66), channel_id=1, source_target_pairs={{0,2},{1,3},{2,0},{3,1},{4,6},{5,7},{6,4},{7,5},{8,10},{9,11},{10,... | collective-permute-start | bytes 638984 | tf_op jit(solution)/shard_map/ppermute | solution.py:712
  70.9 0.4 collective-permute-start.14
  71.3 10.4 %collective-permute-done.14.refs_4_.two_ref = bf16[192,512]{1,0:T(8,128)(2,1)S(1)} collective-permute-done((bf16[192,512]{1,0:T(8,128)(2,1)S(1)}, bf16[192,512]{1,0:T(8,128)(2,1)S(1)}, u32[]{:S(2)}, u32[]{:S(2)}) %collective-permute-start.14) | collective-permute-done | bytes 196640 | tf_op jit(solution)/shard_map/ppermute | solution.py:712
  81.7 0.1 relay.3
  81.8 0.8 finish_lyric.2
  82.5 1.7 %finish_audio.2 = (bf16[128,2048]{1,0:T(8,128)(2,1)}, bf16[128,2048]{1,0:T(8,128)(2,1)}, bf16[128,2048]{1,0:T(8,128)(2,1)}, bf16[128,2048]{1,0:T(8,128)(2,1)}, bf16[608,512]{1,0:T(8,128)(2,1)S(1)}) custom-call(s32[2]{0:T(128)S(1)} %copy-done.9, f32[2,128]{1,0:T(2,128)S(1)} %pad_maximum_fusion.gain_ref, bf16[128,2048]{1,0:T(8,128)(2,1)S(1)} %bitcast.37, ...), custom_call_target="tpu_custom_call" | custom-call | flops 1 | bytes 1 | tf_op jit(solution)/shard_map/finish_audio/pallas_call | solution.py:493
  84.3 0.1 collective-permute-start.19
  84.3 0.6 collective-permute-start.15
  84.9 0.7 collective-permute-start.21
  85.6 4.3 %collective-permute-start.16 = (bf16[192,512]{1,0:T(8,128)(2,1)S(1)}, bf16[192,512]{1,0:T(8,128)(2,1)S(1)}, u32[]{:S(2)}, u32[]{:S(2)}) collective-permute-start(bf16[192,512]{1,0:T(8,128)(2,1)S(1)} %get-tuple-element.72.refs_0_.refs_1_), channel_id=1, source_target_pairs={{0,4},{1,5},{2,6},{3,7},{4,0},{5,1},{6,2},{7,3},{8,12},{9,13},{10,... | collective-permute-start | bytes 589832 | tf_op jit(solution)/shard_map/ppermute | solution.py:712
  89.9 1.5 %collective-permute-start.17 = (f32[8,128]{1,0:T(8,128)S(1)}, f32[8,128]{1,0:T(8,128)S(1)}, u32[]{:S(2)}, u32[]{:S(2)}) collective-permute-start(f32[8,128]{1,0:T(8,128)S(1)} %get-tuple-element.73), channel_id=1, source_target_pairs={{0,8},{8,0},{16,24},{24,16},{1,9},{9,1},{17,25},{25,17},{2,10},{10... | collective-permute-start | bytes 12296 | tf_op jit(solution)/shard_map/ppermute | solution.py:681
  91.4 2.1 %collective-permute-done.17 = f32[8,128]{1,0:T(8,128)S(1)} collective-permute-done((f32[8,128]{1,0:T(8,128)S(1)}, f32[8,128]{1,0:T(8,128)S(1)}, u32[]{:S(2)}, u32[]{:S(2)}) %collective-permute-start.17) | collective-permute-done | bytes 4128 | tf_op jit(solution)/shard_map/ppermute | solution.py:681
  93.5 1.5 %collective-permute-start.18 = (f32[8,128]{1,0:T(8,128)S(1)}, f32[8,128]{1,0:T(8,128)S(1)}, u32[]{:S(2)}, u32[]{:S(2)}) collective-permute-start(f32[8,128]{1,0:T(8,128)S(1)} %add.51), channel_id=1, source_target_pairs={{0,16},{8,24},{16,0},{24,8},{1,17},{9,25},{17,1},{25,9},{2,18},{10... | collective-permute-start | bytes 12296 | tf_op jit(solution)/shard_map/ppermute | solution.py:681
  95.0 2.1 %collective-permute-done.18 = f32[8,128]{1,0:T(8,128)S(1)} collective-permute-done((f32[8,128]{1,0:T(8,128)S(1)}, f32[8,128]{1,0:T(8,128)S(1)}, u32[]{:S(2)}, u32[]{:S(2)}) %collective-permute-start.18) | collective-permute-done | bytes 4128 | tf_op jit(solution)/shard_map/ppermute | solution.py:681
  97.1 1.5 %join.2 = (bf16[128,2048]{1,0:T(8,128)(2,1)}, bf16[128,2048]{1,0:T(8,128)(2,1)}, bf16[128,2048]{1,0:T(8,128)(2,1)}, bf16[128,2048]{1,0:T(8,128)(2,1)}, bf16[48,2...) custom-call(s32[2]{0:T(128)S(1)} %copy-done.9, ...), custom_call_target="tpu_custom_call", output_to_operand_aliasing={{0}: (3, {}), {1}: (4, {}), {2}: (5, {}), {3}: (6, {})} | custom-call | flops 1 | bytes 1 | tf_op jit(solution)/shard_map/join/pallas_call | solution.py:601
  98.5 0.0 copy-start.6
  98.6 0.9 copy-done.6
  99.5 0.9 copy-done.7
  100.4 0.1 collective-permute-start.20
  100.5 4.4 %collective-permute-done.20 = f32[8,128]{1,0:T(8,128)S(1)} collective-permute-done((f32[8,128]{1,0:T(8,128)S(1)}, f32[8,128]{1,0:T(8,128)S(1)}, u32[]{:S(2)}, u32[]{:S(2)}) %collective-permute-start.20) | collective-permute-done | bytes 4128 | tf_op jit(solution)/shard_map/ppermute | solution.py:681
  104.9 0.8 finish_lyric.3
  105.7 1.7 %finish_audio.3 = (bf16[128,2048]{1,0:T(8,128)(2,1)}, bf16[128,2048]{1,0:T(8,128)(2,1)}, bf16[128,2048]{1,0:T(8,128)(2,1)}, bf16[128,2048]{1,0:T(8,128)(2,1)}, bf16[624,512]{1,0:T(8,128)(2,1)S(1)}) custom-call(s32[2]{0:T(128)S(1)} %copy-done.9, ...), custom_call_target="tpu_custom_call", output_to_operand_aliasing={{0}: (12, {}), {1}: (13, {}), {2}: (14, {}), {3}: (15, {})} | custom-call | flops 1 | bytes 1 | tf_op jit(solution)/shard_map/finish_audio/pallas_call | solution.py:493
  107.4 0.1 collective-permute-start.22
  107.5 2.1 %collective-permute-done.22.mate_ref = bf16[624,512]{1,0:T(8,128)(2,1)S(1)} collective-permute-done((bf16[624,512]{1,0:T(8,128)(2,1)S(1)}, bf16[624,512]{1,0:T(8,128)(2,1)S(1)}, u32[]{:S(2)}, u32[]{:S(2)}) %collective-permute-start.22) | collective-permute-done | bytes 639008 | tf_op jit(solution)/shard_map/ppermute | solution.py:812
  109.6 2.0 %join.3 = (bf16[128,2048]{1,0:T(8,128)(2,1)}, bf16[128,2048]{1,0:T(8,128)(2,1)}, bf16[128,2048]{1,0:T(8,128)(2,1)}, bf16[128,2048]{1,0:T(8,128)(2,1)}, bf16[48,2...) custom-call(s32[2]{0:T(128)S(1)} %copy-done.9, ...), custom_call_target="tpu_custom_call", output_to_operand_aliasing={{0}: (4, {}), {1}: (5, {}), {2}: (6, {}), {3}: (7, {}), {4}... | custom-call | flops 1 | bytes 1 | tf_op jit(solution)/shard_map/join/pallas_call | solution.py:601
  (35 shorter events, 0.1 us)
Async XLA Ops:
  1.3 5.5 %copy-start.2 = (bf16[1,48,2048]{2,1,0:T(8,128)(2,1)S(1)}, bf16[1,48,2048]{2,1,0:T(8,128)(2,1)}, u32[]{:S(2)}) copy-start(bf16[1,48,2048]{2,1,0:T(8,128)(2,1)} %param.13) | copy-start | bytes 589828
  1.3 5.5 %copy-start.5 = (bf16[1,48,2048]{2,1,0:T(8,128)(2,1)S(1)}, bf16[1,48,2048]{2,1,0:T(8,128)(2,1)}, u32[]{:S(2)}) copy-start(bf16[1,48,2048]{2,1,0:T(8,128)(2,1)} %param.14) | copy-start | bytes 589828
  4.1 2.6 %collective-permute-start = (bf16[384,1024]{1,0:T(8,128)(2,1)}, bf16[384,1024]{1,0:T(8,128)(2,1)S(1)}, u32[]{:S(2)}, u32[]{:S(2)}) collective-permute-start(bf16[384,1024]{1,0:T(8,128)(2,1)} %pack.2), channel_id=1, source_target_pairs={{0,1},{1,0},{2,3},{3,2},{4,5},{5,4},{6,7},{7,6},{8,9},{9,8},{10,11... | collective-permute-start | bytes 2359304 | tf_op jit(solution)/shard_map/ppermute | solution.py:753
  4.6 0.7 copy-start.11
  4.6 0.7 copy-start.12
  5.3 1.5 %copy-start.8 = (s32[2]{0:T(128)S(1)}, s32[2]{0:T(128)}, u32[]{:S(2)}) copy-start(s32[2]{0:T(128)} %pad_add_fusion.state_ref) | copy-start | bytes 28
  7.4 13.5 %collective-permute-start.1 = (bf16[192,512]{1,0:T(8,128)(2,1)S(1)}, bf16[192,512]{1,0:T(8,128)(2,1)S(1)}, u32[]{:S(2)}, u32[]{:S(2)}) collective-permute-start(bf16[192,512]{1,0:T(8,128)(2,1)S(1)} %pair_lyrics.2.refs_0_), channel_id=1, source_target_pairs={{0,4},{1,5},{2,6},{3,7},{4,0},{5,1},{6,2},{7,3},{8,12},{9,13},{10,... | collective-permute-start | bytes 589832 | tf_op jit(solution)/shard_map/ppermute | solution.py:712
  11.4 2.7 %copy-start = (bf16[1,128,2048]{2,1,0:T(8,128)(2,1)S(1)}, bf16[1,128,2048]{2,1,0:T(8,128)(2,1)}, u32[]{:S(2)}) copy-start(bf16[1,128,2048]{2,1,0:T(8,128)(2,1)} %param.11) | copy-start | bytes 1572868
  11.5 2.7 %copy-start.1 = (bf16[1,128,2048]{2,1,0:T(8,128)(2,1)S(1)}, bf16[1,128,2048]{2,1,0:T(8,128)(2,1)}, u32[]{:S(2)}) copy-start(bf16[1,128,2048]{2,1,0:T(8,128)(2,1)} %param.12) | copy-start | bytes 1572868
  11.5 2.8 %copy-start.9 = (s32[2]{0:T(128)S(1)}, s32[2]{0:T(128)}, u32[]{:S(2)}) copy-start(s32[2]{0:T(128)} %pad_add_fusion.state_ref) | copy-start | bytes 28
  14.1 30.6 %collective-permute-start.2 = (bf16[256,1024]{1,0:T(8,128)(2,1)}, bf16[256,1024]{1,0:T(8,128)(2,1)S(1)}, u32[]{:S(2)}, u32[]{:S(2)}) collective-permute-start(bf16[256,1024]{1,0:T(8,128)(2,1)} %pack.3), channel_id=1, source_target_pairs={{0,1},{1,0},{2,3},{3,2},{4,5},{5,4},{6,7},{7,6},{8,9},{9,8},{10,11... | collective-permute-start | bytes 1572872 | tf_op jit(solution)/shard_map/ppermute | solution.py:755
  15.7 29.0 %collective-permute-start.8 = (bf16[448,512]{1,0:T(8,128)(2,1)}, bf16[448,512]{1,0:T(8,128)(2,1)}, u32[]{:S(2)}, u32[]{:S(2)}) collective-permute-start(bf16[448,512]{1,0:T(8,128)(2,1)} %edge.6), channel_id=1, source_target_pairs={{0,2},{1,3},{2,0},{3,1},{4,6},{5,7},{6,4},{7,5},{8,10},{9,11},{10,... | collective-permute-start | bytes 1376264 | tf_op jit(solution)/shard_map/ppermute | solution.py:712
  21.0 13.9 %collective-permute-start.3 = (bf16[192,512]{1,0:T(8,128)(2,1)S(1)}, bf16[192,512]{1,0:T(8,128)(2,1)S(1)}, u32[]{:S(2)}, u32[]{:S(2)}) collective-permute-start(bf16[192,512]{1,0:T(8,128)(2,1)S(1)} %collective-permute-done.1.refs_0_.refs_1_), channel_id=1, source_target_pairs={{0,2},{1,3},{2,0},{3,1},{4,6},{5,7},{6,4},{7,5},{8,10},{9,11},{10,... | collective-permute-start | bytes 589832 | tf_op jit(solution)/shard_map/ppermute | solution.py:712
  23.0 21.7 %collective-permute-start.9 = (bf16[256,512]{1,0:T(8,128)(2,1)}, bf16[256,512]{1,0:T(8,128)(2,1)}, u32[]{:S(2)}, u32[]{:S(2)}) collective-permute-start(bf16[256,512]{1,0:T(8,128)(2,1)} %edge.7), channel_id=1, source_target_pairs={{2,4},{3,5},{4,2},{5,3},{10,12},{11,13},{12,10},{13,11},{18,20},{1... | collective-permute-start | bytes 786440 | tf_op jit(solution)/shard_map/ppermute | solution.py:712
  25.1 18.2 %collective-permute-start.5 = (bf16[192,512]{1,0:T(8,128)(2,1)S(1)}, bf16[192,512]{1,0:T(8,128)(2,1)S(1)}, u32[]{:S(2)}, u32[]{:S(2)}) collective-permute-start(bf16[192,512]{1,0:T(8,128)(2,1)S(1)} %pair_lyrics.3.refs_0_), channel_id=1, source_target_pairs={{0,4},{1,5},{2,6},{3,7},{4,0},{5,1},{6,2},{7,3},{8,12},{9,13},{10,... | collective-permute-start | bytes 589832 | tf_op jit(solution)/shard_map/ppermute | solution.py:712
  36.4 26.9 %collective-permute-start.4 = (bf16[448,512]{1,0:T(8,128)(2,1)}, bf16[448,512]{1,0:T(8,128)(2,1)}, u32[]{:S(2)}, u32[]{:S(2)}) collective-permute-start(bf16[448,512]{1,0:T(8,128)(2,1)} %edge.4), channel_id=1, source_target_pairs={{0,2},{1,3},{2,0},{3,1},{4,6},{5,7},{6,4},{7,5},{8,10},{9,11},{10,... | collective-permute-start | bytes 1376264 | tf_op jit(solution)/shard_map/ppermute | solution.py:712
  36.5 0.7 copy-start.10
  40.0 4.7 %copy-start.3 = (bf16[1,128,2048]{2,1,0:T(8,128)(2,1)S(1)}, bf16[1,128,2048]{2,1,0:T(8,128)(2,1)}, u32[]{:S(2)}) copy-start(bf16[1,128,2048]{2,1,0:T(8,128)(2,1)} %param.10) | copy-start | bytes 1572868
  40.1 4.7 %copy-start.4 = (bf16[1,128,2048]{2,1,0:T(8,128)(2,1)S(1)}, bf16[1,128,2048]{2,1,0:T(8,128)(2,1)}, u32[]{:S(2)}) copy-start(bf16[1,128,2048]{2,1,0:T(8,128)(2,1)} %param.17) | copy-start | bytes 1572868
  44.0 19.2 %collective-permute-start.6 = (bf16[256,512]{1,0:T(8,128)(2,1)S(1)}, bf16[256,512]{1,0:T(8,128)(2,1)S(1)}, u32[]{:S(2)}, u32[]{:S(2)}) collective-permute-start(bf16[256,512]{1,0:T(8,128)(2,1)S(1)} %edge.5), channel_id=1, source_target_pairs={{2,4},{3,5},{4,2},{5,3},{10,12},{11,13},{12,10},{13,11},{18,20},{1... | collective-permute-start | bytes 786440 | tf_op jit(solution)/shard_map/ppermute | solution.py:712
  50.4 8.7 %collective-permute-start.10 = (bf16[192,512]{1,0:T(8,128)(2,1)S(1)}, bf16[192,512]{1,0:T(8,128)(2,1)S(1)}, u32[]{:S(2)}, u32[]{:S(2)}) collective-permute-start(bf16[192,512]{1,0:T(8,128)(2,1)S(1)} %get-tuple-element.63), channel_id=1, source_target_pairs={{0,2},{1,3},{2,0},{3,1},{4,6},{5,7},{6,4},{7,5},{8,10},{9,11},{10,... | collective-permute-start | bytes 589832 | tf_op jit(solution)/shard_map/ppermute | solution.py:712
  53.3 10.0 %collective-permute-start.7 = (bf16[192,512]{1,0:T(8,128)(2,1)S(1)}, bf16[192,512]{1,0:T(8,128)(2,1)S(1)}, u32[]{:S(2)}, u32[]{:S(2)}) collective-permute-start(bf16[192,512]{1,0:T(8,128)(2,1)S(1)} %collective-permute-done.5.refs_0_.refs_1_), channel_id=1, source_target_pairs={{0,2},{1,3},{2,0},{3,1},{4,6},{5,7},{6,4},{7,5},{8,10},{9,11},{10,... | collective-permute-start | bytes 589832 | tf_op jit(solution)/shard_map/ppermute | solution.py:712
  53.3 28.4 %collective-permute-start.13 = (bf16[448,512]{1,0:T(8,128)(2,1)S(1)}, bf16[448,512]{1,0:T(8,128)(2,1)S(1)}, u32[]{:S(2)}, u32[]{:S(2)}) collective-permute-start(bf16[448,512]{1,0:T(8,128)(2,1)S(1)} %get-tuple-element.70), channel_id=1, source_target_pairs={{0,2},{1,3},{2,0},{3,1},{4,6},{5,7},{6,4},{7,5},{8,10},{9,11},{10,... | collective-permute-start | bytes 1376264 | tf_op jit(solution)/shard_map/ppermute | solution.py:712
  59.0 12.3 %collective-permute-start.12 = (bf16[256,512]{1,0:T(8,128)(2,1)S(1)}, bf16[256,512]{1,0:T(8,128)(2,1)S(1)}, u32[]{:S(2)}, u32[]{:S(2)}) collective-permute-start(bf16[256,512]{1,0:T(8,128)(2,1)S(1)} %get-tuple-element.69), channel_id=1, source_target_pairs={{2,4},{3,5},{4,2},{5,3},{10,12},{11,13},{12,10},{13,11},{18,20},{1... | collective-permute-start | bytes 786440 | tf_op jit(solution)/shard_map/ppermute | solution.py:712
  68.8 12.9 %collective-permute-start.11 = (bf16[208,512]{1,0:T(8,128)(2,1)S(1)}, bf16[208,512]{1,0:T(8,128)(2,1)S(1)}, u32[]{:S(2)}, u32[]{:S(2)}) collective-permute-start(bf16[208,512]{1,0:T(8,128)(2,1)S(1)} %get-tuple-element.66), channel_id=1, source_target_pairs={{0,2},{1,3},{2,0},{3,1},{4,6},{5,7},{6,4},{7,5},{8,10},{9,11},{10,... | collective-permute-start | bytes 638984 | tf_op jit(solution)/shard_map/ppermute | solution.py:712
  70.9 10.8 %collective-permute-start.14 = (bf16[192,512]{1,0:T(8,128)(2,1)S(1)}, bf16[192,512]{1,0:T(8,128)(2,1)S(1)}, u32[]{:S(2)}, u32[]{:S(2)}) collective-permute-start(bf16[192,512]{1,0:T(8,128)(2,1)S(1)} %relay.2.refs_4_), channel_id=1, source_target_pairs={{0,4},{1,5},{2,6},{3,7},{4,0},{5,1},{6,2},{7,3},{8,12},{9,13},{10,... | collective-permute-start | bytes 589832 | tf_op jit(solution)/shard_map/ppermute | solution.py:712
  84.3 12.8 %collective-permute-start.19 = (bf16[608,512]{1,0:T(8,128)(2,1)S(1)}, bf16[608,512]{1,0:T(8,128)(2,1)S(1)}, u32[]{:S(2)}, u32[]{:S(2)}) collective-permute-start(bf16[608,512]{1,0:T(8,128)(2,1)S(1)} %get-tuple-element.82), channel_id=1, source_target_pairs={{0,1},{1,0},{2,3},{3,2},{4,5},{5,4},{6,7},{7,6},{8,9},{9,8},{10,11... | collective-permute-start | bytes 1867784 | tf_op jit(solution)/shard_map/ppermute | solution.py:812
  84.3 20.6 %collective-permute-start.15 = (bf16[448,512]{1,0:T(8,128)(2,1)S(1)}, bf16[448,512]{1,0:T(8,128)(2,1)S(1)}, u32[]{:S(2)}, u32[]{:S(2)}) collective-permute-start(bf16[448,512]{1,0:T(8,128)(2,1)S(1)} %get-tuple-element.71), channel_id=1, source_target_pairs={{0,2},{1,3},{2,0},{3,1},{4,6},{5,7},{6,4},{7,5},{8,10},{9,11},{10,... | collective-permute-start | bytes 1376264 | tf_op jit(solution)/shard_map/ppermute | solution.py:712
  84.9 20.8 %collective-permute-start.21 = (bf16[256,512]{1,0:T(8,128)(2,1)S(1)}, bf16[256,512]{1,0:T(8,128)(2,1)S(1)}, u32[]{:S(2)}, u32[]{:S(2)}) collective-permute-start(bf16[256,512]{1,0:T(8,128)(2,1)S(1)} %get-tuple-element.96), channel_id=1, source_target_pairs={{2,4},{3,5},{4,2},{5,3},{10,12},{11,13},{12,10},{13,11},{18,20},{1... | collective-permute-start | bytes 786440 | tf_op jit(solution)/shard_map/ppermute | solution.py:712
  85.6 19.3 %collective-permute-start.16 = (bf16[192,512]{1,0:T(8,128)(2,1)S(1)}, bf16[192,512]{1,0:T(8,128)(2,1)S(1)}, u32[]{:S(2)}, u32[]{:S(2)}) collective-permute-start(bf16[192,512]{1,0:T(8,128)(2,1)S(1)} %get-tuple-element.72.refs_0_.refs_1_), channel_id=1, source_target_pairs={{0,4},{1,5},{2,6},{3,7},{4,0},{5,1},{6,2},{7,3},{8,12},{9,13},{10,... | collective-permute-start | bytes 589832 | tf_op jit(solution)/shard_map/ppermute | solution.py:712
  89.9 3.6 %collective-permute-start.17 = (f32[8,128]{1,0:T(8,128)S(1)}, f32[8,128]{1,0:T(8,128)S(1)}, u32[]{:S(2)}, u32[]{:S(2)}) collective-permute-start(f32[8,128]{1,0:T(8,128)S(1)} %get-tuple-element.73), channel_id=1, source_target_pairs={{0,8},{8,0},{16,24},{24,16},{1,9},{9,1},{17,25},{25,17},{2,10},{10... | collective-permute-start | bytes 12296 | tf_op jit(solution)/shard_map/ppermute | solution.py:681
  93.5 3.6 %collective-permute-start.18 = (f32[8,128]{1,0:T(8,128)S(1)}, f32[8,128]{1,0:T(8,128)S(1)}, u32[]{:S(2)}, u32[]{:S(2)}) collective-permute-start(f32[8,128]{1,0:T(8,128)S(1)} %add.51), channel_id=1, source_target_pairs={{0,16},{8,24},{16,0},{24,8},{1,17},{9,25},{17,1},{25,9},{2,18},{10... | collective-permute-start | bytes 12296 | tf_op jit(solution)/shard_map/ppermute | solution.py:681
  98.5 0.9 copy-start.6
  99.5 0.9 copy-start.7
  100.4 4.5 %collective-permute-start.20 = (f32[8,128]{1,0:T(8,128)S(1)}, f32[8,128]{1,0:T(8,128)S(1)}, u32[]{:S(2)}, u32[]{:S(2)}) collective-permute-start(f32[8,128]{1,0:T(8,128)S(1)} %tie.1), channel_id=1, source_target_pairs={{0,4},{1,5},{2,6},{3,7},{4,0},{5,1},{6,2},{7,3},{8,12},{9,13},{10,... | collective-permute-start | bytes 12296 | tf_op jit(solution)/shard_map/ppermute | solution.py:681
  107.4 2.1 %collective-permute-start.22 = (bf16[624,512]{1,0:T(8,128)(2,1)S(1)}, bf16[624,512]{1,0:T(8,128)(2,1)S(1)}, u32[]{:S(2)}, u32[]{:S(2)}) collective-permute-start(bf16[624,512]{1,0:T(8,128)(2,1)S(1)} %get-tuple-element.101), channel_id=1, source_target_pairs={{0,1},{1,0},{2,3},{3,2},{4,5},{5,4},{6,7},{7,6},{8,9},{9,8},{10,11... | collective-permute-start | bytes 1916936 | tf_op jit(solution)/shard_map/ppermute | solution.py:812

commit v13 on v11

--- a/solution.py
+++ b/solution.py
@@ -397,10 +397,6 @@
         for number in range(HEADS_PER_STEP):
             one_head(step * HEADS_PER_STEP + number)
 
-    if exchanged and chunk == CHUNKS - 1:
-        to_two_ref = lyric_out[2]
-        to_two_ref[window:, :] = split_rows(gain_grad_ref[...], size)
-
 
 def attention(
     chunk, meta, gains, query, cot, value, key, mate, one, mid, lyrics, groups, earlier, after
@@ -416,8 +412,6 @@
     out_shape += [shape(2 * frames, size, dtype) for dtype in (bf16, f32, f32)]
     out_shape += [shape(one.shape[0], size), shape(2 * frames, size), shape(8, head_size, f32)]
     out_shape += [shape(slot, size)] * len(lyrics)
-    if len(lyrics) > 1 and chunk == CHUNKS - 1:
-        out_shape[-1] = shape(slot + GAIN_ROWS, size)
     return call(
         functools.partial(
             attention_kernel, chunk, len(earlier), len(after), groups, head_size, head_size ** (-0.5)
@@ -509,29 +503,25 @@
 
 
 def relay_kernel(part_ref, arrived_ref, *refs):
-    rows = part_ref.shape[0]
-    total = part_ref[...].astype(jnp.float32) + arrived_ref[0:rows, :].astype(jnp.float32)
-    if arrived_ref.shape[0] == rows:
-        refs[0][...] = total.astype(jnp.bfloat16)
-        return
-    gain_ref, (out_ref, total_ref, _) = refs[0], refs[-3:]
-    out_ref[...] = total.astype(jnp.bfloat16)
-    total_ref[...] = gain_ref[...] + joined_rows(arrived_ref[rows:, :], gain_ref.shape[1])
+    out_ref = refs[0] if len(refs) == 1 else refs[-2]
+    out_ref[...] = (
+        part_ref[...].astype(jnp.float32) + arrived_ref[...].astype(jnp.float32)
+    ).astype(jnp.bfloat16)
 
 
 def relay(part, arrived):
     return call(relay_kernel, "relay", [VMEM] * 2, VMEM, shape(*part.shape))(part, arrived)
 
 
-def last_relay(part, arrived, gain, later, after):
+def last_relay(part, arrived, later, after):
     return call(
         relay_kernel,
         "relay",
-        [VMEM] * 3 + [ANY] * (1 + len(after)),
-        [VMEM, VMEM, ANY],
-        [shape(*part.shape), shape(*gain.shape, jnp.float32), shape(*later.shape)],
-        input_output_aliases={3: 2},
-    )(part, arrived, gain, later, *after)
+        [VMEM] * 2 + [ANY] * (1 + len(after)),
+        [VMEM, ANY],
+        [shape(*part.shape), shape(*later.shape)],
+        input_output_aliases={2: 1},
+    )(part, arrived, later, *after)
 
 
 def finish_lyric_kernel(
@@ -780,9 +770,8 @@
                 relayed = [relay(for_two, arrived)]
                 to_two = relayed[0]
             else:
-                to_two, gain_total, to_one = last_relay(
-                    for_two, arrived, gain_part, to_one, sent
-                )
+                gain_total = sum_over(gain_part, "song", bits_of(songs))
+                to_two, to_one = last_relay(for_two, arrived, to_one, [*sent, gain_total])
             two_back, one_back = hop(to_two, across), hop(to_one, partners)
             lyric_chunks += [held, one_back, two_back]
             sent = [*sent, mid_back, one_back, two_back]
@@ -793,7 +782,7 @@
 
     to_mate = []
     if hops:
-        gain_total = sum_over(sum_over(gain_total, "song", bits_of(songs)), "seq", [4])
+        gain_total = sum_over(gain_total, "seq", [2, 4])
         own_half, part_to_mate = finish_lyric(
             state, gains, lyric_keys[0], mate, gain_total, lyric_chunks
         )

time: 107 us -> 107 us (level)
  starting transfers between devices: 29.9 us -> 32.4 us
  waiting for transfers between devices: 45.2 us -> 42.7 us
    ppermute x16, waiting for transfers between devices: 30.8 us -> 25.1 us  [hop(): return lax.ppermute(block, 'seq', pairs)]
    ppermute x3 -> x4, waiting for transfers between devices: 8.64 us -> 11.8 us  [sum_over(): lax.ppermute(total, axis, [(i, i ^ bit) for i in range(count)])]
    ppermute x3 -> x4, starting transfers between devices: 3.08 us -> 6.04 us  [sum_over(): lax.ppermute(total, axis, [(i, i ^ bit) for i in range(count)])]
  transfers between devices with their start and end apart: 21 -> 22, of which waited for: 12 -> 11; matrix products, arithmetic and copies ran while one was open for 2% -> 2% of each run, Pallas kernels for 18% -> 18%
where the time goes in v13:
time: 107 us
  waiting for transfers between devices  42.7 us (40%)
  starting transfers between devices  32.4 us (30%)
  Pallas kernels  27.2 us (25%)
  local copies, waits for them, and re-layouts  2.02 us (2%)
  between operations  1.59 us (1%)
    ppermute x16, starting transfers between devices, hop(): return lax.ppermute(block, 'seq', pairs)  25.8 us
    ppermute x16, waiting for transfers between devices, hop(): return lax.ppermute(block, 'seq', pairs)  25.1 us
    ppermute x4, waiting for transfers between devices, sum_over(): lax.ppermute(total, axis, [(i, i ^ bit) for i in range(count)])  11.8 us
    pallas_call x2, Pallas kernels, attention(): call(functools.partial(attention_kernel, chunk, len(earlier), len(after),...  11.2 us
    ppermute x4, starting transfers between devices, sum_over(): lax.ppermute(total, axis, [(i, i ^ bit) for i in range(count)])  6.04 us
    pallas_call x4, Pallas kernels, edge(): call(functools.partial(edge_kernel, chunk, touching, bool(lead)), 'edge',...  5.08 us
    pallas_call x1, Pallas kernels, pack(): call(pack_kernel, 'pack', [SMEM, SMEM] + [HBM] * len(arrays), VMEM, shape...  3.17 us
    ppermute x1, waiting for transfers between devices, body(): from_mate = lax.ppermute(to_mate, 'seq', swap)  2.97 us
  transfers between devices with their start and end apart: 22, of which 11 were waited for; matrix products, arithmetic and copies ran while one was open for 2% of the time, Pallas kernels for 18%

profile of v13, /device:TPU:0, one launch (start us, length us, event | category | flops | bytes accessed | tf_op | source)
XLA Modules:
  0.0 106.5 jit_solution(14803156589695320103)
XLA Ops:
  0.7 0.6 pad_add_fusion.state_ref
  1.3 0.0 copy-start.6
  1.3 3.2 %pack.1 = bf16[640,1024]{1,0:T(8,128)(2,1)} custom-call(s32[2]{0:T(128)} %pad_add_fusion.state_ref, s32[2]{0:T(128)} %bitcast.62, bf16[128,2048]{1,0:T(8,128)(2,1)} %bitcast.45, bf16[128,2048]{1,0:T(8,128)(2,1)} %bitcast.48, bf16[128,2048]{1,0:T(8,128)(2,1)} %bitcast.38, bf16[128,2048]{1,0:T(8,128)(2,1)} %bitcast.31, bf16[48,2048]{1,0:T(8,128)(2,1)} %bitcast.51, ...), custom_call_target="tpu_custom_call" | custom-call | flops 1 | bytes 1 | tf_op jit(solution)/shard_map/pack/pallas_call | solution.py:128
  4.5 0.0 copy-start
  4.5 0.0 copy-start.1
  4.5 0.5 collective-permute-start
  5.0 2.9 %collective-permute-done.mate_ref = bf16[640,1024]{1,0:T(8,128)(2,1)S(1)} collective-permute-done((bf16[640,1024]{1,0:T(8,128)(2,1)}, bf16[640,1024]{1,0:T(8,128)(2,1)S(1)}, u32[]{:S(2)}, u32[]{:S(2)}) %collective-permute-start) | collective-permute-done | bytes 1310752 | tf_op jit(solution)/shard_map/ppermute | solution.py:743
  7.9 0.7 pair_lyrics.2.refs_0_
  8.6 4.0 %collective-permute-start.1 = (bf16[192,512]{1,0:T(8,128)(2,1)S(1)}, bf16[192,512]{1,0:T(8,128)(2,1)S(1)}, u32[]{:S(2)}, u32[]{:S(2)}) collective-permute-start(bf16[192,512]{1,0:T(8,128)(2,1)S(1)} %pair_lyrics.2.refs_0_), channel_id=1, source_target_pairs={{0,4},{1,5},{2,6},{3,7},{4,0},{5,1},{6,2},{7,3},{8,12},{9,13},{10,... | collective-permute-start | bytes 589832 | tf_op jit(solution)/shard_map/ppermute | solution.py:698
  12.6 1.5 %edge.6 = bf16[448,512]{1,0:T(8,128)(2,1)} custom-call(s32[2]{0:T(128)S(1)} %copy-done.6, f32[2,128]{1,0:T(2,128)S(1)} %pad_maximum_fusion.gain_ref, bf16[128,2048]{1,0:T(8,128)(2,1)S(1)} %bitcast.39, bf16[128,2048]{1,0:T(8,128)(2,1)S(1)} %bitcast.32, bf16[640,1024]{1,0:T(8,128)(2,1)S(1)} %collective-permute-done.mate_ref, ...), custom_call_target="tpu_custom_call" | custom-call | flops 1 | bytes 1 | tf_op jit(solution)/shard_map/edge/pallas_call | solution.py:185
  14.1 1.6 %collective-permute-start.7 = (bf16[448,512]{1,0:T(8,128)(2,1)}, bf16[448,512]{1,0:T(8,128)(2,1)}, u32[]{:S(2)}, u32[]{:S(2)}) collective-permute-start(bf16[448,512]{1,0:T(8,128)(2,1)} %edge.6), channel_id=1, source_target_pairs={{0,2},{1,3},{2,0},{3,1},{4,6},{5,7},{6,4},{7,5},{8,10},{9,11},{10,... | collective-permute-start | bytes 1376264 | tf_op jit(solution)/shard_map/ppermute | solution.py:698
  15.7 6.5 %collective-permute-done.1.refs_0_.refs_1_ = bf16[192,512]{1,0:T(8,128)(2,1)S(1)} collective-permute-done((bf16[192,512]{1,0:T(8,128)(2,1)S(1)}, bf16[192,512]{1,0:T(8,128)(2,1)S(1)}, u32[]{:S(2)}, u32[]{:S(2)}) %collective-permute-start.1) | collective-permute-done | bytes 196640 | tf_op jit(solution)/shard_map/ppermute | solution.py:698
  22.1 0.7 collective-permute-start.2
  22.8 1.4 %edge.7 = bf16[256,512]{1,0:T(8,128)(2,1)} custom-call(s32[2]{0:T(128)S(1)} %copy-done.6, f32[2,128]{1,0:T(2,128)S(1)} %pad_maximum_fusion.gain_ref, bf16[128,2048]{1,0:T(8,128)(2,1)S(1)} %bitcast.40, bf16[128,2048]{1,0:T(8,128)(2,1)S(1)} %bitcast.33, bf16[640,1024]{1,0:T(8,128)(2,1)S(1)} %collective-permute-done.mate_ref, ...), custom_call_target="tpu_custom_call" | custom-call | flops 1 | bytes 1 | tf_op jit(solution)/shard_map/edge/pallas_call | solution.py:185
  24.2 1.4 %collective-permute-start.8 = (bf16[256,512]{1,0:T(8,128)(2,1)}, bf16[256,512]{1,0:T(8,128)(2,1)}, u32[]{:S(2)}, u32[]{:S(2)}) collective-permute-start(bf16[256,512]{1,0:T(8,128)(2,1)} %edge.7), channel_id=1, source_target_pairs={{2,4},{3,5},{4,2},{5,3},{10,12},{11,13},{12,10},{13,11},{18,20},{1... | collective-permute-start | bytes 786440 | tf_op jit(solution)/shard_map/ppermute | solution.py:698
  25.5 0.7 pair_lyrics.3.refs_0_
  26.2 0.0 copy-start.7
  26.2 4.1 %collective-permute-start.4 = (bf16[192,512]{1,0:T(8,128)(2,1)S(1)}, bf16[192,512]{1,0:T(8,128)(2,1)S(1)}, u32[]{:S(2)}, u32[]{:S(2)}) collective-permute-start(bf16[192,512]{1,0:T(8,128)(2,1)S(1)} %pair_lyrics.3.refs_0_), channel_id=1, source_target_pairs={{0,4},{1,5},{2,6},{3,7},{4,0},{5,1},{6,2},{7,3},{8,12},{9,13},{10,... | collective-permute-start | bytes 589832 | tf_op jit(solution)/shard_map/ppermute | solution.py:698
  30.3 3.5 %collective-permute-done.2.refs_1_.refs_2_ = bf16[192,512]{1,0:T(8,128)(2,1)S(1)} collective-permute-done((bf16[192,512]{1,0:T(8,128)(2,1)S(1)}, bf16[192,512]{1,0:T(8,128)(2,1)S(1)}, u32[]{:S(2)}, u32[]{:S(2)}) %collective-permute-start.2) | collective-permute-done | bytes 196640 | tf_op jit(solution)/shard_map/ppermute | solution.py:698
  33.8 1.5 %edge.4 = bf16[448,512]{1,0:T(8,128)(2,1)} custom-call(s32[2]{0:T(128)S(1)} %copy-done.6, f32[2,128]{1,0:T(2,128)S(1)} %pad_maximum_fusion.gain_ref, bf16[128,2048]{1,0:T(8,128)(2,1)S(1)} %bitcast.41, bf16[128,2048]{1,0:T(8,128)(2,1)S(1)} %bitcast.34, bf16[640,1024]{1,0:T(8,128)(2,1)S(1)} %collective-permute-done.mate_ref, ...), custom_call_target="tpu_custom_call" | custom-call | flops 1 | bytes 1 | tf_op jit(solution)/shard_map/edge/pallas_call | solution.py:185
  35.3 0.6 collective-permute-start.3
  36.6 0.6 fusion
  37.2 1.4 %stack.74.meta_ref = s32[15]{0:T(128)S(1)} concatenate(s32[1]{0:T(128)} %bitcast, s32[1]{0:T(128)} %bitcast.1, s32[1]{0:T(128)} %bitcast.2, s32[1]{0:T(128)} %bitcast.3, s32[1]{0:T(128)S(6)} %copy.28, s32[1]{0:T(128)} %bitcast.4, s32[1]{0:T(128)} %bitcast.5, s32[1]{0:T(128)} %bitcast.6, s32[1]{0:T(128)} %bitcast.7, s32[1]{0:T(128)} %bitcast.8, s32[1]{0:T(128)} %bitcast.9, ...), dimensions={0} | concatenate | bytes 120 | tf_op jit(solution)/shard_map/stack | solution.py:727
  38.5 0.9 prepare_keys.1.key_ref
  39.5 0.0 copy-start.2
  39.5 0.0 copy-start.3
  39.5 4.9 %collective-permute-done.4.refs_0_.refs_1_ = bf16[192,512]{1,0:T(8,128)(2,1)S(1)} collective-permute-done((bf16[192,512]{1,0:T(8,128)(2,1)S(1)}, bf16[192,512]{1,0:T(8,128)(2,1)S(1)}, u32[]{:S(2)}, u32[]{:S(2)}) %collective-permute-start.4) | collective-permute-done | bytes 196640 | tf_op jit(solution)/shard_map/ppermute | solution.py:698
  44.4 0.7 edge.5
  45.1 0.7 collective-permute-start.5
  45.8 0.0 collective-permute-done.7.one_ref
  45.8 0.0 collective-permute-done.8.mid_ref
  45.9 5.6 %attention.2 = (bf16[128,512]{1,0:T(8,128)(2,1)S(1)}, bf16[128,512]{1,0:T(8,128)(2,1)S(1)}, bf16[256,512]{1,0:T(8,128)(2,1)S(1)}, f32[256,512]{1,0:T(8,128)S(1)}...) custom-call(s32[15]{0:T(128)S(1)} %stack.74.meta_ref, ...), custom_call_target="tpu_custom_call" | custom-call | flops 1207959552 | bytes 8388608 | tf_op jit(solution)/shard_map/attention/pallas_call | solution.py:415
  51.5 1.3 %collective-permute-start.9 = (bf16[192,512]{1,0:T(8,128)(2,1)S(1)}, bf16[192,512]{1,0:T(8,128)(2,1)S(1)}, u32[]{:S(2)}, u32[]{:S(2)}) collective-permute-start(bf16[192,512]{1,0:T(8,128)(2,1)S(1)} %get-tuple-element.49), channel_id=1, source_target_pairs={{0,2},{1,3},{2,0},{3,1},{4,6},{5,7},{6,4},{7,5},{8,10},{9,11},{10,... | collective-permute-start | bytes 589832 | tf_op jit(solution)/shard_map/ppermute | solution.py:698
  52.8 0.7 collective-permute-start.6
  53.6 1.3 %collective-permute-start.14 = (bf16[448,512]{1,0:T(8,128)(2,1)S(1)}, bf16[448,512]{1,0:T(8,128)(2,1)S(1)}, u32[]{:S(2)}, u32[]{:S(2)}) collective-permute-start(bf16[448,512]{1,0:T(8,128)(2,1)S(1)} %get-tuple-element.52), channel_id=1, source_target_pairs={{0,2},{1,3},{2,0},{3,1},{4,6},{5,7},{6,4},{7,5},{8,10},{9,11},{10,... | collective-permute-start | bytes 1376264 | tf_op jit(solution)/shard_map/ppermute | solution.py:698
  54.9 4.5 %collective-permute-done.9.arrived_ref = bf16[192,512]{1,0:T(8,128)(2,1)S(1)} collective-permute-done((bf16[192,512]{1,0:T(8,128)(2,1)S(1)}, bf16[192,512]{1,0:T(8,128)(2,1)S(1)}, u32[]{:S(2)}, u32[]{:S(2)}) %collective-permute-start.9) | collective-permute-done | bytes 196640 | tf_op jit(solution)/shard_map/ppermute | solution.py:698
  59.4 0.7 collective-permute-start.17
  60.1 5.6 %collective-permute-done.6.refs_2_ = bf16[192,512]{1,0:T(8,128)(2,1)S(1)} collective-permute-done((bf16[192,512]{1,0:T(8,128)(2,1)S(1)}, bf16[192,512]{1,0:T(8,128)(2,1)S(1)}, u32[]{:S(2)}, u32[]{:S(2)}) %collective-permute-start.6) | collective-permute-done | bytes 196640 | tf_op jit(solution)/shard_map/ppermute | solution.py:698
  65.7 0.7 collective-permute-start.15
  66.4 0.0 collective-permute-done.5.mid_ref
  66.4 0.0 collective-permute-done.3.one_ref
  66.4 5.5 %attention.3 = (bf16[128,512]{1,0:T(8,128)(2,1)S(1)}, bf16[128,512]{1,0:T(8,128)(2,1)S(1)}, bf16[256,512]{1,0:T(8,128)(2,1)S(1)}, f32[256,512]{1,0:T(8,128)S(1)}...) custom-call(s32[15]{0:T(128)S(1)} %stack.74.meta_ref, ...), custom_call_target="tpu_custom_call" | custom-call | flops 1207959552 | bytes 8388608 | tf_op jit(solution)/shard_map/attention/pallas_call | solution.py:415
  72.0 2.5 %collective-permute-start.16 = (bf16[192,512]{1,0:T(8,128)(2,1)S(1)}, bf16[192,512]{1,0:T(8,128)(2,1)S(1)}, u32[]{:S(2)}, u32[]{:S(2)}) collective-permute-start(bf16[192,512]{1,0:T(8,128)(2,1)S(1)} %get-tuple-element.55), channel_id=1, source_target_pairs={{0,2},{1,3},{2,0},{3,1},{4,6},{5,7},{6,4},{7,5},{8,10},{9,11},{10,... | collective-permute-start | bytes 589832 | tf_op jit(solution)/shard_map/ppermute | solution.py:698
  74.5 1.5 %collective-permute-start.10 = (f32[8,128]{1,0:T(8,128)S(1)}, f32[8,128]{1,0:T(8,128)S(1)}, u32[]{:S(2)}, u32[]{:S(2)}) collective-permute-start(f32[8,128]{1,0:T(8,128)S(1)} %get-tuple-element.50), channel_id=1, source_target_pairs={{0,8},{8,0},{16,24},{24,16},{1,9},{9,1},{17,25},{25,17},{2,10},{10... | collective-permute-start | bytes 12296 | tf_op jit(solution)/shard_map/ppermute | solution.py:667
  76.0 2.1 %collective-permute-done.10 = f32[8,128]{1,0:T(8,128)S(1)} collective-permute-done((f32[8,128]{1,0:T(8,128)S(1)}, f32[8,128]{1,0:T(8,128)S(1)}, u32[]{:S(2)}, u32[]{:S(2)}) %collective-permute-start.10) | collective-permute-done | bytes 4128 | tf_op jit(solution)/shard_map/ppermute | solution.py:667
  78.1 1.5 %collective-permute-start.11 = (f32[8,128]{1,0:T(8,128)S(1)}, f32[8,128]{1,0:T(8,128)S(1)}, u32[]{:S(2)}, u32[]{:S(2)}) collective-permute-start(f32[8,128]{1,0:T(8,128)S(1)} %add.54), channel_id=1, source_target_pairs={{0,16},{8,24},{16,0},{24,8},{1,17},{9,25},{17,1},{25,9},{2,18},{10... | collective-permute-start | bytes 12296 | tf_op jit(solution)/shard_map/ppermute | solution.py:667
  79.7 2.1 %collective-permute-done.11 = f32[8,128]{1,0:T(8,128)S(1)} collective-permute-done((f32[8,128]{1,0:T(8,128)S(1)}, f32[8,128]{1,0:T(8,128)S(1)}, u32[]{:S(2)}, u32[]{:S(2)}) %collective-permute-start.11) | collective-permute-done | bytes 4128 | tf_op jit(solution)/shard_map/ppermute | solution.py:667
  81.8 0.0 collective-permute-done.17.refs_1_.refs_6_
  81.8 0.0 collective-permute-done.15.refs_3_.refs_2_
  81.8 0.0 collective-permute-done.14.refs_2_.refs_1_.refs_5_
  81.8 0.0 collective-permute-done.16.arrived_ref
  81.8 0.1 relay.3
  81.8 0.1 collective-permute-start.18
  82.0 0.7 collective-permute-start.20
  82.7 4.7 %collective-permute-start.19 = (bf16[192,512]{1,0:T(8,128)(2,1)S(1)}, bf16[192,512]{1,0:T(8,128)(2,1)S(1)}, u32[]{:S(2)}, u32[]{:S(2)}) collective-permute-start(bf16[192,512]{1,0:T(8,128)(2,1)S(1)} %get-tuple-element.59), channel_id=1, source_target_pairs={{0,4},{1,5},{2,6},{3,7},{4,0},{5,1},{6,2},{7,3},{8,12},{9,13},{10,... | collective-permute-start | bytes 589832 | tf_op jit(solution)/shard_map/ppermute | solution.py:698
  87.4 5.9 %collective-permute-done.12 = f32[8,128]{1,0:T(8,128)S(1)} collective-permute-done((f32[8,128]{1,0:T(8,128)S(1)}, f32[8,128]{1,0:T(8,128)S(1)}, u32[]{:S(2)}, u32[]{:S(2)}) %collective-permute-start.12) | collective-permute-done | bytes 4128 | tf_op jit(solution)/shard_map/ppermute | solution.py:667
  93.3 3.0 %collective-permute-start.13 = (f32[8,128]{1,0:T(8,128)S(1)}, f32[8,128]{1,0:T(8,128)S(1)}, u32[]{:S(2)}, u32[]{:S(2)}) collective-permute-start(f32[8,128]{1,0:T(8,128)S(1)} %add.56), channel_id=1, source_target_pairs={{0,4},{1,5},{2,6},{3,7},{4,0},{5,1},{6,2},{7,3},{8,12},{9,13},{10,... | collective-permute-start | bytes 12296 | tf_op jit(solution)/shard_map/ppermute | solution.py:667
  96.3 1.7 %collective-permute-done.13 = f32[8,128]{1,0:T(8,128)S(1)} collective-permute-done((f32[8,128]{1,0:T(8,128)S(1)}, f32[8,128]{1,0:T(8,128)S(1)}, u32[]{:S(2)}, u32[]{:S(2)}) %collective-permute-start.13) | collective-permute-done | bytes 4128 | tf_op jit(solution)/shard_map/ppermute | solution.py:667
  98.1 0.9 finish_lyric.1
  99.0 0.0 collective-permute-done.20.refs_13_
  99.0 2.3 %finish_audio.1 = (bf16[128,2048]{1,0:T(8,128)(2,1)}, bf16[128,2048]{1,0:T(8,128)(2,1)}, bf16[128,2048]{1,0:T(8,128)(2,1)}, bf16[128,2048]{1,0:T(8,128)(2,1)}, bf16[624,1024]{1,0:T(8,128)(2,1)S(1)}) custom-call(s32[2]{0:T(128)S(1)} %copy-done.6, f32[2,128]{1,0:T(2,128)S(1)} %pad_maximum_fusion.gain_ref, bf16[128,2048]{1,0:T(8,128)(2,1)S(1)} %bitcast.44, ...), custom_call_target="tpu_custom_call" | custom-call | flops 1 | bytes 1 | tf_op jit(solution)/shard_map/finish_audio/pallas_call | solution.py:494
  101.3 0.1 collective-permute-start.21
  101.4 3.0 %collective-permute-done.21.mate_ref = bf16[624,1024]{1,0:T(8,128)(2,1)S(1)} collective-permute-done((bf16[624,1024]{1,0:T(8,128)(2,1)S(1)}, bf16[624,1024]{1,0:T(8,128)(2,1)S(1)}, u32[]{:S(2)}, u32[]{:S(2)}) %collective-permute-start.21) | collective-permute-done | bytes 1277984 | tf_op jit(solution)/shard_map/ppermute | solution.py:791
  104.3 2.2 %join.1 = (bf16[128,2048]{1,0:T(8,128)(2,1)}, bf16[128,2048]{1,0:T(8,128)(2,1)}, bf16[128,2048]{1,0:T(8,128)(2,1)}, bf16[128,2048]{1,0:T(8,128)(2,1)}, bf16[48,2...) custom-call(s32[2]{0:T(128)S(1)} %copy-done.6, ...), custom_call_target="tpu_custom_call", output_to_operand_aliasing={{0}: (4, {}), {1}: (5, {}), {2}: (6, {}), {3}: (7, {})} | custom-call | flops 1 | bytes 1 | tf_op jit(solution)/shard_map/join/pallas_call | solution.py:595
  (23 shorter events, 0.1 us)
Async XLA Ops:
  1.3 3.7 %copy-start.8 = (f32[128]{0:T(128)S(1)}, f32[128]{0:T(128)}, u32[]{:S(2)}) copy-start(f32[128]{0:T(128)} %param.16) | copy-start | bytes 1540
  1.3 3.7 %copy-start.9 = (f32[128]{0:T(128)S(1)}, f32[128]{0:T(128)}, u32[]{:S(2)}) copy-start(f32[128]{0:T(128)} %param.15) | copy-start | bytes 1540
  1.3 6.6 %copy-start.4 = (bf16[1,48,2048]{2,1,0:T(8,128)(2,1)S(1)}, bf16[1,48,2048]{2,1,0:T(8,128)(2,1)}, u32[]{:S(2)}) copy-start(bf16[1,48,2048]{2,1,0:T(8,128)(2,1)} %param.13) | copy-start | bytes 589828
  1.3 6.6 %copy-start.5 = (bf16[1,48,2048]{2,1,0:T(8,128)(2,1)S(1)}, bf16[1,48,2048]{2,1,0:T(8,128)(2,1)}, u32[]{:S(2)}) copy-start(bf16[1,48,2048]{2,1,0:T(8,128)(2,1)} %param.14) | copy-start | bytes 589828
  1.3 6.6 %copy-start.6 = (s32[2]{0:T(128)S(1)}, s32[2]{0:T(128)}, u32[]{:S(2)}) copy-start(s32[2]{0:T(128)} %pad_add_fusion.state_ref) | copy-start | bytes 28
  4.5 8.1 %copy-start = (bf16[1,128,2048]{2,1,0:T(8,128)(2,1)S(1)}, bf16[1,128,2048]{2,1,0:T(8,128)(2,1)}, u32[]{:S(2)}) copy-start(bf16[1,128,2048]{2,1,0:T(8,128)(2,1)} %param.12) | copy-start | bytes 1572868
  4.5 8.1 %copy-start.1 = (bf16[1,128,2048]{2,1,0:T(8,128)(2,1)S(1)}, bf16[1,128,2048]{2,1,0:T(8,128)(2,1)}, u32[]{:S(2)}) copy-start(bf16[1,128,2048]{2,1,0:T(8,128)(2,1)} %param.11) | copy-start | bytes 1572868
  4.5 3.4 %collective-permute-start = (bf16[640,1024]{1,0:T(8,128)(2,1)}, bf16[640,1024]{1,0:T(8,128)(2,1)S(1)}, u32[]{:S(2)}, u32[]{:S(2)}) collective-permute-start(bf16[640,1024]{1,0:T(8,128)(2,1)} %pack.1), channel_id=1, source_target_pairs={{0,1},{1,0},{2,3},{3,2},{4,5},{5,4},{6,7},{7,6},{8,9},{9,8},{10,11... | collective-permute-start | bytes 3932168 | tf_op jit(solution)/shard_map/ppermute | solution.py:743
  8.6 13.5 %collective-permute-start.1 = (bf16[192,512]{1,0:T(8,128)(2,1)S(1)}, bf16[192,512]{1,0:T(8,128)(2,1)S(1)}, u32[]{:S(2)}, u32[]{:S(2)}) collective-permute-start(bf16[192,512]{1,0:T(8,128)(2,1)S(1)} %pair_lyrics.2.refs_0_), channel_id=1, source_target_pairs={{0,4},{1,5},{2,6},{3,7},{4,0},{5,1},{6,2},{7,3},{8,12},{9,13},{10,... | collective-permute-start | bytes 589832 | tf_op jit(solution)/shard_map/ppermute | solution.py:698
  14.1 31.8 %collective-permute-start.7 = (bf16[448,512]{1,0:T(8,128)(2,1)}, bf16[448,512]{1,0:T(8,128)(2,1)}, u32[]{:S(2)}, u32[]{:S(2)}) collective-permute-start(bf16[448,512]{1,0:T(8,128)(2,1)} %edge.6), channel_id=1, source_target_pairs={{0,2},{1,3},{2,0},{3,1},{4,6},{5,7},{6,4},{7,5},{8,10},{9,11},{10,... | collective-permute-start | bytes 1376264 | tf_op jit(solution)/shard_map/ppermute | solution.py:698
  22.1 11.7 %collective-permute-start.2 = (bf16[192,512]{1,0:T(8,128)(2,1)S(1)}, bf16[192,512]{1,0:T(8,128)(2,1)S(1)}, u32[]{:S(2)}, u32[]{:S(2)}) collective-permute-start(bf16[192,512]{1,0:T(8,128)(2,1)S(1)} %collective-permute-done.1.refs_0_.refs_1_), channel_id=1, source_target_pairs={{0,2},{1,3},{2,0},{3,1},{4,6},{5,7},{6,4},{7,5},{8,10},{9,11},{10,... | collective-permute-start | bytes 589832 | tf_op jit(solution)/shard_map/ppermute | solution.py:698
  24.2 21.7 %collective-permute-start.8 = (bf16[256,512]{1,0:T(8,128)(2,1)}, bf16[256,512]{1,0:T(8,128)(2,1)}, u32[]{:S(2)}, u32[]{:S(2)}) collective-permute-start(bf16[256,512]{1,0:T(8,128)(2,1)} %edge.7), channel_id=1, source_target_pairs={{2,4},{3,5},{4,2},{5,3},{10,12},{11,13},{12,10},{13,11},{18,20},{1... | collective-permute-start | bytes 786440 | tf_op jit(solution)/shard_map/ppermute | solution.py:698
  26.2 10.3 %copy-start.7 = (s32[1,1,2]{2,1,0:T(1,128)S(1)}, s32[1,1,2]{2,1,0:T(1,128)}, u32[]{:S(2)}) copy-start(s32[1,1,2]{2,1,0:T(1,128)} %param.18) | copy-start | bytes 28
  26.2 18.2 %collective-permute-start.4 = (bf16[192,512]{1,0:T(8,128)(2,1)S(1)}, bf16[192,512]{1,0:T(8,128)(2,1)S(1)}, u32[]{:S(2)}, u32[]{:S(2)}) collective-permute-start(bf16[192,512]{1,0:T(8,128)(2,1)S(1)} %pair_lyrics.3.refs_0_), channel_id=1, source_target_pairs={{0,4},{1,5},{2,6},{3,7},{4,0},{5,1},{6,2},{7,3},{8,12},{9,13},{10,... | collective-permute-start | bytes 589832 | tf_op jit(solution)/shard_map/ppermute | solution.py:698
  35.3 31.1 %collective-permute-start.3 = (bf16[448,512]{1,0:T(8,128)(2,1)}, bf16[448,512]{1,0:T(8,128)(2,1)}, u32[]{:S(2)}, u32[]{:S(2)}) collective-permute-start(bf16[448,512]{1,0:T(8,128)(2,1)} %edge.4), channel_id=1, source_target_pairs={{0,2},{1,3},{2,0},{3,1},{4,6},{5,7},{6,4},{7,5},{8,10},{9,11},{10,... | collective-permute-start | bytes 1376264 | tf_op jit(solution)/shard_map/ppermute | solution.py:698
  39.5 6.4 %copy-start.2 = (bf16[1,128,2048]{2,1,0:T(8,128)(2,1)S(1)}, bf16[1,128,2048]{2,1,0:T(8,128)(2,1)}, u32[]{:S(2)}) copy-start(bf16[1,128,2048]{2,1,0:T(8,128)(2,1)} %param.10) | copy-start | bytes 1572868
  39.5 6.4 %copy-start.3 = (bf16[1,128,2048]{2,1,0:T(8,128)(2,1)S(1)}, bf16[1,128,2048]{2,1,0:T(8,128)(2,1)}, u32[]{:S(2)}) copy-start(bf16[1,128,2048]{2,1,0:T(8,128)(2,1)} %param.17) | copy-start | bytes 1572868
  45.1 21.3 %collective-permute-start.5 = (bf16[256,512]{1,0:T(8,128)(2,1)S(1)}, bf16[256,512]{1,0:T(8,128)(2,1)S(1)}, u32[]{:S(2)}, u32[]{:S(2)}) collective-permute-start(bf16[256,512]{1,0:T(8,128)(2,1)S(1)} %edge.5), channel_id=1, source_target_pairs={{2,4},{3,5},{4,2},{5,3},{10,12},{11,13},{12,10},{13,11},{18,20},{1... | collective-permute-start | bytes 786440 | tf_op jit(solution)/shard_map/ppermute | solution.py:698
  51.5 7.9 %collective-permute-start.9 = (bf16[192,512]{1,0:T(8,128)(2,1)S(1)}, bf16[192,512]{1,0:T(8,128)(2,1)S(1)}, u32[]{:S(2)}, u32[]{:S(2)}) collective-permute-start(bf16[192,512]{1,0:T(8,128)(2,1)S(1)} %get-tuple-element.49), channel_id=1, source_target_pairs={{0,2},{1,3},{2,0},{3,1},{4,6},{5,7},{6,4},{7,5},{8,10},{9,11},{10,... | collective-permute-start | bytes 589832 | tf_op jit(solution)/shard_map/ppermute | solution.py:698
  52.8 12.9 %collective-permute-start.6 = (bf16[192,512]{1,0:T(8,128)(2,1)S(1)}, bf16[192,512]{1,0:T(8,128)(2,1)S(1)}, u32[]{:S(2)}, u32[]{:S(2)}) collective-permute-start(bf16[192,512]{1,0:T(8,128)(2,1)S(1)} %collective-permute-done.4.refs_0_.refs_1_), channel_id=1, source_target_pairs={{0,2},{1,3},{2,0},{3,1},{4,6},{5,7},{6,4},{7,5},{8,10},{9,11},{10,... | collective-permute-start | bytes 589832 | tf_op jit(solution)/shard_map/ppermute | solution.py:698
  53.6 28.2 %collective-permute-start.14 = (bf16[448,512]{1,0:T(8,128)(2,1)S(1)}, bf16[448,512]{1,0:T(8,128)(2,1)S(1)}, u32[]{:S(2)}, u32[]{:S(2)}) collective-permute-start(bf16[448,512]{1,0:T(8,128)(2,1)S(1)} %get-tuple-element.52), channel_id=1, source_target_pairs={{0,2},{1,3},{2,0},{3,1},{4,6},{5,7},{6,4},{7,5},{8,10},{9,11},{10,... | collective-permute-start | bytes 1376264 | tf_op jit(solution)/shard_map/ppermute | solution.py:698
  59.4 22.4 %collective-permute-start.17 = (bf16[256,512]{1,0:T(8,128)(2,1)S(1)}, bf16[256,512]{1,0:T(8,128)(2,1)S(1)}, u32[]{:S(2)}, u32[]{:S(2)}) collective-permute-start(bf16[256,512]{1,0:T(8,128)(2,1)S(1)} %get-tuple-element.57), channel_id=1, source_target_pairs={{2,4},{3,5},{4,2},{5,3},{10,12},{11,13},{12,10},{13,11},{18,20},{1... | collective-permute-start | bytes 786440 | tf_op jit(solution)/shard_map/ppermute | solution.py:698
  65.7 16.0 %collective-permute-start.15 = (bf16[192,512]{1,0:T(8,128)(2,1)S(1)}, bf16[192,512]{1,0:T(8,128)(2,1)S(1)}, u32[]{:S(2)}, u32[]{:S(2)}) collective-permute-start(bf16[192,512]{1,0:T(8,128)(2,1)S(1)} %relay.2.refs_4_), channel_id=1, source_target_pairs={{0,4},{1,5},{2,6},{3,7},{4,0},{5,1},{6,2},{7,3},{8,12},{9,13},{10,... | collective-permute-start | bytes 589832 | tf_op jit(solution)/shard_map/ppermute | solution.py:698
  72.0 9.8 %collective-permute-start.16 = (bf16[192,512]{1,0:T(8,128)(2,1)S(1)}, bf16[192,512]{1,0:T(8,128)(2,1)S(1)}, u32[]{:S(2)}, u32[]{:S(2)}) collective-permute-start(bf16[192,512]{1,0:T(8,128)(2,1)S(1)} %get-tuple-element.55), channel_id=1, source_target_pairs={{0,2},{1,3},{2,0},{3,1},{4,6},{5,7},{6,4},{7,5},{8,10},{9,11},{10,... | collective-permute-start | bytes 589832 | tf_op jit(solution)/shard_map/ppermute | solution.py:698
  74.5 3.6 %collective-permute-start.10 = (f32[8,128]{1,0:T(8,128)S(1)}, f32[8,128]{1,0:T(8,128)S(1)}, u32[]{:S(2)}, u32[]{:S(2)}) collective-permute-start(f32[8,128]{1,0:T(8,128)S(1)} %get-tuple-element.50), channel_id=1, source_target_pairs={{0,8},{8,0},{16,24},{24,16},{1,9},{9,1},{17,25},{25,17},{2,10},{10... | collective-permute-start | bytes 12296 | tf_op jit(solution)/shard_map/ppermute | solution.py:667
  78.1 3.6 %collective-permute-start.11 = (f32[8,128]{1,0:T(8,128)S(1)}, f32[8,128]{1,0:T(8,128)S(1)}, u32[]{:S(2)}, u32[]{:S(2)}) collective-permute-start(f32[8,128]{1,0:T(8,128)S(1)} %add.54), channel_id=1, source_target_pairs={{0,16},{8,24},{16,0},{24,8},{1,17},{9,25},{17,1},{25,9},{2,18},{10... | collective-permute-start | bytes 12296 | tf_op jit(solution)/shard_map/ppermute | solution.py:667
  81.8 16.2 %collective-permute-start.18 = (bf16[448,512]{1,0:T(8,128)(2,1)S(1)}, bf16[448,512]{1,0:T(8,128)(2,1)S(1)}, u32[]{:S(2)}, u32[]{:S(2)}) collective-permute-start(bf16[448,512]{1,0:T(8,128)(2,1)S(1)} %get-tuple-element.58), channel_id=1, source_target_pairs={{0,2},{1,3},{2,0},{3,1},{4,6},{5,7},{6,4},{7,5},{8,10},{9,11},{10,... | collective-permute-start | bytes 1376264 | tf_op jit(solution)/shard_map/ppermute | solution.py:698
  82.0 17.0 %collective-permute-start.20 = (bf16[256,512]{1,0:T(8,128)(2,1)S(1)}, bf16[256,512]{1,0:T(8,128)(2,1)S(1)}, u32[]{:S(2)}, u32[]{:S(2)}) collective-permute-start(bf16[256,512]{1,0:T(8,128)(2,1)S(1)} %get-tuple-element.71), channel_id=1, source_target_pairs={{2,4},{3,5},{4,2},{5,3},{10,12},{11,13},{12,10},{13,11},{18,20},{1... | collective-permute-start | bytes 786440 | tf_op jit(solution)/shard_map/ppermute | solution.py:698
  82.7 15.4 %collective-permute-start.19 = (bf16[192,512]{1,0:T(8,128)(2,1)S(1)}, bf16[192,512]{1,0:T(8,128)(2,1)S(1)}, u32[]{:S(2)}, u32[]{:S(2)}) collective-permute-start(bf16[192,512]{1,0:T(8,128)(2,1)S(1)} %get-tuple-element.59), channel_id=1, source_target_pairs={{0,4},{1,5},{2,6},{3,7},{4,0},{5,1},{6,2},{7,3},{8,12},{9,13},{10,... | collective-permute-start | bytes 589832 | tf_op jit(solution)/shard_map/ppermute | solution.py:698
  87.4 5.9 %collective-permute-start.12 = (f32[8,128]{1,0:T(8,128)S(1)}, f32[8,128]{1,0:T(8,128)S(1)}, u32[]{:S(2)}, u32[]{:S(2)}) collective-permute-start(f32[8,128]{1,0:T(8,128)S(1)} %add.55.refs_4_), channel_id=1, source_target_pairs={{0,2},{1,3},{2,0},{3,1},{4,6},{5,7},{6,4},{7,5},{8,10},{9,11},{10,... | collective-permute-start | bytes 12296 | tf_op jit(solution)/shard_map/ppermute | solution.py:667
  93.3 4.7 %collective-permute-start.13 = (f32[8,128]{1,0:T(8,128)S(1)}, f32[8,128]{1,0:T(8,128)S(1)}, u32[]{:S(2)}, u32[]{:S(2)}) collective-permute-start(f32[8,128]{1,0:T(8,128)S(1)} %add.56), channel_id=1, source_target_pairs={{0,4},{1,5},{2,6},{3,7},{4,0},{5,1},{6,2},{7,3},{8,12},{9,13},{10,... | collective-permute-start | bytes 12296 | tf_op jit(solution)/shard_map/ppermute | solution.py:667
  101.3 3.1 %collective-permute-start.21 = (bf16[624,1024]{1,0:T(8,128)(2,1)S(1)}, bf16[624,1024]{1,0:T(8,128)(2,1)S(1)}, u32[]{:S(2)}, u32[]{:S(2)}) collective-permute-start(bf16[624,1024]{1,0:T(8,128)(2,1)S(1)} %get-tuple-element.73), channel_id=1, source_target_pairs={{0,1},{1,0},{2,3},{3,2},{4,5},{5,4},{6,7},{7,6},{8,9},{9,8},{10,11... | collective-permute-start | bytes 3833864 | tf_op jit(solution)/shard_map/ppermute | solution.py:791

commit v14 on v13

--- a/solution.py
+++ b/solution.py
@@ -18,7 +18,7 @@
 HBM = pl.BlockSpec(memory_space=pltpu.HBM)
 ANY = pl.BlockSpec(memory_space=pl.ANY)
 GAIN_ROWS = 16
-HEADS_PER_STEP = 2
+HEADS_PER_STEP = 4
 CHUNKS = 2
 ALIGN_ROWS = 32
 SMALL = pl.CostEstimate(flops=1, bytes_accessed=1, transcendentals=0)

time: 107 us -> 106 us (level)
  transfers between devices with their start and end apart: 22 -> 22, of which waited for: 11 -> 11; matrix products, arithmetic and copies ran while one was open for 2% -> 2% of each run, Pallas kernels for 18% -> 17%
where the time goes in v14:
time: 106 us
  waiting for transfers between devices  43.1 us (41%)
  starting transfers between devices  32.4 us (31%)
  Pallas kernels  26.3 us (25%)
  local copies, waits for them, and re-layouts  2.02 us (2%)
  between operations  1.59 us (2%)
    ppermute x16, starting transfers between devices, hop(): return lax.ppermute(block, 'seq', pairs)  25.8 us
    ppermute x16, waiting for transfers between devices, hop(): return lax.ppermute(block, 'seq', pairs)  25.1 us
    ppermute x4, waiting for transfers between devices, sum_over(): lax.ppermute(total, axis, [(i, i ^ bit) for i in range(count)])  12.3 us
    pallas_call x2, Pallas kernels, attention(): call(functools.partial(attention_kernel, chunk, len(earlier), len(after),...  10.3 us
    ppermute x4, starting transfers between devices, sum_over(): lax.ppermute(total, axis, [(i, i ^ bit) for i in range(count)])  6.01 us
    pallas_call x4, Pallas kernels, edge(): call(functools.partial(edge_kernel, chunk, touching, bool(lead)), 'edge',...  5.08 us
    pallas_call x1, Pallas kernels, pack(): call(pack_kernel, 'pack', [SMEM, SMEM] + [HBM] * len(arrays), VMEM, shape...  3.17 us
    ppermute x1, waiting for transfers between devices, body(): from_mate = lax.ppermute(to_mate, 'seq', swap)  2.97 us
  transfers between devices with their start and end apart: 22, of which 11 were waited for; matrix products, arithmetic and copies ran while one was open for 2% of the time, Pallas kernels for 17%

profile of v14, /device:TPU:0, one launch (start us, length us, event | category | flops | bytes accessed | tf_op | source)
XLA Modules:
  0.0 106.1 jit_solution(17845197110113147354)
XLA Ops:
  0.7 0.6 pad_add_fusion.state_ref
  1.3 0.0 copy-start.6
  1.3 3.2 %pack.1 = bf16[640,1024]{1,0:T(8,128)(2,1)} custom-call(s32[2]{0:T(128)} %pad_add_fusion.state_ref, s32[2]{0:T(128)} %bitcast.62, bf16[128,2048]{1,0:T(8,128)(2,1)} %bitcast.45, bf16[128,2048]{1,0:T(8,128)(2,1)} %bitcast.48, bf16[128,2048]{1,0:T(8,128)(2,1)} %bitcast.38, bf16[128,2048]{1,0:T(8,128)(2,1)} %bitcast.31, bf16[48,2048]{1,0:T(8,128)(2,1)} %bitcast.51, ...), custom_call_target="tpu_custom_call" | custom-call | flops 1 | bytes 1 | tf_op jit(solution)/shard_map/pack/pallas_call | solution.py:128
  4.5 0.0 copy-start
  4.5 0.0 copy-start.1
  4.5 0.5 collective-permute-start
  5.0 2.9 %collective-permute-done.mate_ref = bf16[640,1024]{1,0:T(8,128)(2,1)S(1)} collective-permute-done((bf16[640,1024]{1,0:T(8,128)(2,1)}, bf16[640,1024]{1,0:T(8,128)(2,1)S(1)}, u32[]{:S(2)}, u32[]{:S(2)}) %collective-permute-start) | collective-permute-done | bytes 1310752 | tf_op jit(solution)/shard_map/ppermute | solution.py:743
  7.9 0.7 pair_lyrics.2.refs_0_
  8.6 4.0 %collective-permute-start.1 = (bf16[192,512]{1,0:T(8,128)(2,1)S(1)}, bf16[192,512]{1,0:T(8,128)(2,1)S(1)}, u32[]{:S(2)}, u32[]{:S(2)}) collective-permute-start(bf16[192,512]{1,0:T(8,128)(2,1)S(1)} %pair_lyrics.2.refs_0_), channel_id=1, source_target_pairs={{0,4},{1,5},{2,6},{3,7},{4,0},{5,1},{6,2},{7,3},{8,12},{9,13},{10,... | collective-permute-start | bytes 589832 | tf_op jit(solution)/shard_map/ppermute | solution.py:698
  12.6 1.5 %edge.6 = bf16[448,512]{1,0:T(8,128)(2,1)} custom-call(s32[2]{0:T(128)S(1)} %copy-done.6, f32[2,128]{1,0:T(2,128)S(1)} %pad_maximum_fusion.gain_ref, bf16[128,2048]{1,0:T(8,128)(2,1)S(1)} %bitcast.39, bf16[128,2048]{1,0:T(8,128)(2,1)S(1)} %bitcast.32, bf16[640,1024]{1,0:T(8,128)(2,1)S(1)} %collective-permute-done.mate_ref, ...), custom_call_target="tpu_custom_call" | custom-call | flops 1 | bytes 1 | tf_op jit(solution)/shard_map/edge/pallas_call | solution.py:185
  14.1 1.6 %collective-permute-start.7 = (bf16[448,512]{1,0:T(8,128)(2,1)}, bf16[448,512]{1,0:T(8,128)(2,1)}, u32[]{:S(2)}, u32[]{:S(2)}) collective-permute-start(bf16[448,512]{1,0:T(8,128)(2,1)} %edge.6), channel_id=1, source_target_pairs={{0,2},{1,3},{2,0},{3,1},{4,6},{5,7},{6,4},{7,5},{8,10},{9,11},{10,... | collective-permute-start | bytes 1376264 | tf_op jit(solution)/shard_map/ppermute | solution.py:698
  15.7 6.5 %collective-permute-done.1.refs_0_.refs_1_ = bf16[192,512]{1,0:T(8,128)(2,1)S(1)} collective-permute-done((bf16[192,512]{1,0:T(8,128)(2,1)S(1)}, bf16[192,512]{1,0:T(8,128)(2,1)S(1)}, u32[]{:S(2)}, u32[]{:S(2)}) %collective-permute-start.1) | collective-permute-done | bytes 196640 | tf_op jit(solution)/shard_map/ppermute | solution.py:698
  22.1 0.7 collective-permute-start.2
  22.8 1.4 %edge.7 = bf16[256,512]{1,0:T(8,128)(2,1)} custom-call(s32[2]{0:T(128)S(1)} %copy-done.6, f32[2,128]{1,0:T(2,128)S(1)} %pad_maximum_fusion.gain_ref, bf16[128,2048]{1,0:T(8,128)(2,1)S(1)} %bitcast.40, bf16[128,2048]{1,0:T(8,128)(2,1)S(1)} %bitcast.33, bf16[640,1024]{1,0:T(8,128)(2,1)S(1)} %collective-permute-done.mate_ref, ...), custom_call_target="tpu_custom_call" | custom-call | flops 1 | bytes 1 | tf_op jit(solution)/shard_map/edge/pallas_call | solution.py:185
  24.2 1.4 %collective-permute-start.8 = (bf16[256,512]{1,0:T(8,128)(2,1)}, bf16[256,512]{1,0:T(8,128)(2,1)}, u32[]{:S(2)}, u32[]{:S(2)}) collective-permute-start(bf16[256,512]{1,0:T(8,128)(2,1)} %edge.7), channel_id=1, source_target_pairs={{2,4},{3,5},{4,2},{5,3},{10,12},{11,13},{12,10},{13,11},{18,20},{1... | collective-permute-start | bytes 786440 | tf_op jit(solution)/shard_map/ppermute | solution.py:698
  25.5 0.7 pair_lyrics.3.refs_0_
  26.2 0.0 copy-start.7
  26.2 4.1 %collective-permute-start.4 = (bf16[192,512]{1,0:T(8,128)(2,1)S(1)}, bf16[192,512]{1,0:T(8,128)(2,1)S(1)}, u32[]{:S(2)}, u32[]{:S(2)}) collective-permute-start(bf16[192,512]{1,0:T(8,128)(2,1)S(1)} %pair_lyrics.3.refs_0_), channel_id=1, source_target_pairs={{0,4},{1,5},{2,6},{3,7},{4,0},{5,1},{6,2},{7,3},{8,12},{9,13},{10,... | collective-permute-start | bytes 589832 | tf_op jit(solution)/shard_map/ppermute | solution.py:698
  30.3 3.5 %collective-permute-done.2.refs_1_.refs_2_ = bf16[192,512]{1,0:T(8,128)(2,1)S(1)} collective-permute-done((bf16[192,512]{1,0:T(8,128)(2,1)S(1)}, bf16[192,512]{1,0:T(8,128)(2,1)S(1)}, u32[]{:S(2)}, u32[]{:S(2)}) %collective-permute-start.2) | collective-permute-done | bytes 196640 | tf_op jit(solution)/shard_map/ppermute | solution.py:698
  33.8 1.5 %edge.4 = bf16[448,512]{1,0:T(8,128)(2,1)} custom-call(s32[2]{0:T(128)S(1)} %copy-done.6, f32[2,128]{1,0:T(2,128)S(1)} %pad_maximum_fusion.gain_ref, bf16[128,2048]{1,0:T(8,128)(2,1)S(1)} %bitcast.41, bf16[128,2048]{1,0:T(8,128)(2,1)S(1)} %bitcast.34, bf16[640,1024]{1,0:T(8,128)(2,1)S(1)} %collective-permute-done.mate_ref, ...), custom_call_target="tpu_custom_call" | custom-call | flops 1 | bytes 1 | tf_op jit(solution)/shard_map/edge/pallas_call | solution.py:185
  35.3 0.6 collective-permute-start.3
  36.6 0.6 fusion
  37.2 1.4 %stack.74.meta_ref = s32[15]{0:T(128)S(1)} concatenate(s32[1]{0:T(128)} %bitcast, s32[1]{0:T(128)} %bitcast.1, s32[1]{0:T(128)} %bitcast.2, s32[1]{0:T(128)} %bitcast.3, s32[1]{0:T(128)S(6)} %copy.28, s32[1]{0:T(128)} %bitcast.4, s32[1]{0:T(128)} %bitcast.5, s32[1]{0:T(128)} %bitcast.6, s32[1]{0:T(128)} %bitcast.7, s32[1]{0:T(128)} %bitcast.8, s32[1]{0:T(128)} %bitcast.9, ...), dimensions={0} | concatenate | bytes 120 | tf_op jit(solution)/shard_map/stack | solution.py:727
  38.5 0.9 prepare_keys.1.key_ref
  39.5 0.0 copy-start.2
  39.5 0.0 copy-start.3
  39.5 4.9 %collective-permute-done.4.refs_0_.refs_1_ = bf16[192,512]{1,0:T(8,128)(2,1)S(1)} collective-permute-done((bf16[192,512]{1,0:T(8,128)(2,1)S(1)}, bf16[192,512]{1,0:T(8,128)(2,1)S(1)}, u32[]{:S(2)}, u32[]{:S(2)}) %collective-permute-start.4) | collective-permute-done | bytes 196640 | tf_op jit(solution)/shard_map/ppermute | solution.py:698
  44.4 0.7 edge.5
  45.1 0.7 collective-permute-start.5
  45.8 0.0 collective-permute-done.7.one_ref
  45.8 0.0 collective-permute-done.8.mid_ref
  45.9 5.2 %attention.2 = (bf16[128,512]{1,0:T(8,128)(2,1)S(1)}, bf16[128,512]{1,0:T(8,128)(2,1)S(1)}, bf16[256,512]{1,0:T(8,128)(2,1)S(1)}, f32[256,512]{1,0:T(8,128)S(1)}...) custom-call(s32[15]{0:T(128)S(1)} %stack.74.meta_ref, ...), custom_call_target="tpu_custom_call" | custom-call | flops 1207959552 | bytes 8388608 | tf_op jit(solution)/shard_map/attention/pallas_call | solution.py:415
  51.1 1.3 %collective-permute-start.9 = (bf16[192,512]{1,0:T(8,128)(2,1)S(1)}, bf16[192,512]{1,0:T(8,128)(2,1)S(1)}, u32[]{:S(2)}, u32[]{:S(2)}) collective-permute-start(bf16[192,512]{1,0:T(8,128)(2,1)S(1)} %get-tuple-element.49), channel_id=1, source_target_pairs={{0,2},{1,3},{2,0},{3,1},{4,6},{5,7},{6,4},{7,5},{8,10},{9,11},{10,... | collective-permute-start | bytes 589832 | tf_op jit(solution)/shard_map/ppermute | solution.py:698
  52.4 0.7 collective-permute-start.6
  53.2 1.3 %collective-permute-start.14 = (bf16[448,512]{1,0:T(8,128)(2,1)S(1)}, bf16[448,512]{1,0:T(8,128)(2,1)S(1)}, u32[]{:S(2)}, u32[]{:S(2)}) collective-permute-start(bf16[448,512]{1,0:T(8,128)(2,1)S(1)} %get-tuple-element.52), channel_id=1, source_target_pairs={{0,2},{1,3},{2,0},{3,1},{4,6},{5,7},{6,4},{7,5},{8,10},{9,11},{10,... | collective-permute-start | bytes 1376264 | tf_op jit(solution)/shard_map/ppermute | solution.py:698
  54.4 4.5 %collective-permute-done.9.arrived_ref = bf16[192,512]{1,0:T(8,128)(2,1)S(1)} collective-permute-done((bf16[192,512]{1,0:T(8,128)(2,1)S(1)}, bf16[192,512]{1,0:T(8,128)(2,1)S(1)}, u32[]{:S(2)}, u32[]{:S(2)}) %collective-permute-start.9) | collective-permute-done | bytes 196640 | tf_op jit(solution)/shard_map/ppermute | solution.py:698
  59.0 0.7 collective-permute-start.17
  59.7 5.6 %collective-permute-done.6.refs_2_ = bf16[192,512]{1,0:T(8,128)(2,1)S(1)} collective-permute-done((bf16[192,512]{1,0:T(8,128)(2,1)S(1)}, bf16[192,512]{1,0:T(8,128)(2,1)S(1)}, u32[]{:S(2)}, u32[]{:S(2)}) %collective-permute-start.6) | collective-permute-done | bytes 196640 | tf_op jit(solution)/shard_map/ppermute | solution.py:698
  65.3 0.7 collective-permute-start.15
  66.0 0.0 collective-permute-done.5.mid_ref
  66.0 0.0 collective-permute-done.3.one_ref
  66.0 5.1 %attention.3 = (bf16[128,512]{1,0:T(8,128)(2,1)S(1)}, bf16[128,512]{1,0:T(8,128)(2,1)S(1)}, bf16[256,512]{1,0:T(8,128)(2,1)S(1)}, f32[256,512]{1,0:T(8,128)S(1)}...) custom-call(s32[15]{0:T(128)S(1)} %stack.74.meta_ref, ...), custom_call_target="tpu_custom_call" | custom-call | flops 1207959552 | bytes 8388608 | tf_op jit(solution)/shard_map/attention/pallas_call | solution.py:415
  71.1 2.5 %collective-permute-start.16 = (bf16[192,512]{1,0:T(8,128)(2,1)S(1)}, bf16[192,512]{1,0:T(8,128)(2,1)S(1)}, u32[]{:S(2)}, u32[]{:S(2)}) collective-permute-start(bf16[192,512]{1,0:T(8,128)(2,1)S(1)} %get-tuple-element.55), channel_id=1, source_target_pairs={{0,2},{1,3},{2,0},{3,1},{4,6},{5,7},{6,4},{7,5},{8,10},{9,11},{10,... | collective-permute-start | bytes 589832 | tf_op jit(solution)/shard_map/ppermute | solution.py:698
  73.7 1.5 %collective-permute-start.10 = (f32[8,128]{1,0:T(8,128)S(1)}, f32[8,128]{1,0:T(8,128)S(1)}, u32[]{:S(2)}, u32[]{:S(2)}) collective-permute-start(f32[8,128]{1,0:T(8,128)S(1)} %get-tuple-element.50), channel_id=1, source_target_pairs={{0,8},{8,0},{16,24},{24,16},{1,9},{9,1},{17,25},{25,17},{2,10},{10... | collective-permute-start | bytes 12296 | tf_op jit(solution)/shard_map/ppermute | solution.py:667
  75.2 2.1 %collective-permute-done.10 = f32[8,128]{1,0:T(8,128)S(1)} collective-permute-done((f32[8,128]{1,0:T(8,128)S(1)}, f32[8,128]{1,0:T(8,128)S(1)}, u32[]{:S(2)}, u32[]{:S(2)}) %collective-permute-start.10) | collective-permute-done | bytes 4128 | tf_op jit(solution)/shard_map/ppermute | solution.py:667
  77.3 1.5 %collective-permute-start.11 = (f32[8,128]{1,0:T(8,128)S(1)}, f32[8,128]{1,0:T(8,128)S(1)}, u32[]{:S(2)}, u32[]{:S(2)}) collective-permute-start(f32[8,128]{1,0:T(8,128)S(1)} %add.54), channel_id=1, source_target_pairs={{0,16},{8,24},{16,0},{24,8},{1,17},{9,25},{17,1},{25,9},{2,18},{10... | collective-permute-start | bytes 12296 | tf_op jit(solution)/shard_map/ppermute | solution.py:667
  78.8 2.1 %collective-permute-done.11 = f32[8,128]{1,0:T(8,128)S(1)} collective-permute-done((f32[8,128]{1,0:T(8,128)S(1)}, f32[8,128]{1,0:T(8,128)S(1)}, u32[]{:S(2)}, u32[]{:S(2)}) %collective-permute-start.11) | collective-permute-done | bytes 4128 | tf_op jit(solution)/shard_map/ppermute | solution.py:667
  80.9 0.0 collective-permute-done.17.refs_1_.refs_6_
  80.9 0.0 collective-permute-done.15.refs_3_.refs_2_
  80.9 0.0 collective-permute-done.14.refs_2_.refs_1_.refs_5_
  80.9 0.0 collective-permute-done.16.arrived_ref
  80.9 0.1 relay.3
  81.0 0.1 collective-permute-start.18
  81.1 0.7 collective-permute-start.20
  81.8 4.7 %collective-permute-start.19 = (bf16[192,512]{1,0:T(8,128)(2,1)S(1)}, bf16[192,512]{1,0:T(8,128)(2,1)S(1)}, u32[]{:S(2)}, u32[]{:S(2)}) collective-permute-start(bf16[192,512]{1,0:T(8,128)(2,1)S(1)} %get-tuple-element.59), channel_id=1, source_target_pairs={{0,4},{1,5},{2,6},{3,7},{4,0},{5,1},{6,2},{7,3},{8,12},{9,13},{10,... | collective-permute-start | bytes 589832 | tf_op jit(solution)/shard_map/ppermute | solution.py:698
  86.5 6.4 %collective-permute-done.12 = f32[8,128]{1,0:T(8,128)S(1)} collective-permute-done((f32[8,128]{1,0:T(8,128)S(1)}, f32[8,128]{1,0:T(8,128)S(1)}, u32[]{:S(2)}, u32[]{:S(2)}) %collective-permute-start.12) | collective-permute-done | bytes 4128 | tf_op jit(solution)/shard_map/ppermute | solution.py:667
  92.9 3.0 %collective-permute-start.13 = (f32[8,128]{1,0:T(8,128)S(1)}, f32[8,128]{1,0:T(8,128)S(1)}, u32[]{:S(2)}, u32[]{:S(2)}) collective-permute-start(f32[8,128]{1,0:T(8,128)S(1)} %add.56), channel_id=1, source_target_pairs={{0,4},{1,5},{2,6},{3,7},{4,0},{5,1},{6,2},{7,3},{8,12},{9,13},{10,... | collective-permute-start | bytes 12296 | tf_op jit(solution)/shard_map/ppermute | solution.py:667
  95.9 1.7 %collective-permute-done.13 = f32[8,128]{1,0:T(8,128)S(1)} collective-permute-done((f32[8,128]{1,0:T(8,128)S(1)}, f32[8,128]{1,0:T(8,128)S(1)}, u32[]{:S(2)}, u32[]{:S(2)}) %collective-permute-start.13) | collective-permute-done | bytes 4128 | tf_op jit(solution)/shard_map/ppermute | solution.py:667
  97.6 0.9 finish_lyric.1
  98.5 0.0 collective-permute-done.20.refs_13_
  98.5 2.3 %finish_audio.1 = (bf16[128,2048]{1,0:T(8,128)(2,1)}, bf16[128,2048]{1,0:T(8,128)(2,1)}, bf16[128,2048]{1,0:T(8,128)(2,1)}, bf16[128,2048]{1,0:T(8,128)(2,1)}, bf16[624,1024]{1,0:T(8,128)(2,1)S(1)}) custom-call(s32[2]{0:T(128)S(1)} %copy-done.6, f32[2,128]{1,0:T(2,128)S(1)} %pad_maximum_fusion.gain_ref, bf16[128,2048]{1,0:T(8,128)(2,1)S(1)} %bitcast.44, ...), custom_call_target="tpu_custom_call" | custom-call | flops 1 | bytes 1 | tf_op jit(solution)/shard_map/finish_audio/pallas_call | solution.py:494
  100.8 0.1 collective-permute-start.21
  100.9 3.0 %collective-permute-done.21.mate_ref = bf16[624,1024]{1,0:T(8,128)(2,1)S(1)} collective-permute-done((bf16[624,1024]{1,0:T(8,128)(2,1)S(1)}, bf16[624,1024]{1,0:T(8,128)(2,1)S(1)}, u32[]{:S(2)}, u32[]{:S(2)}) %collective-permute-start.21) | collective-permute-done | bytes 1277984 | tf_op jit(solution)/shard_map/ppermute | solution.py:791
  103.9 2.2 %join.1 = (bf16[128,2048]{1,0:T(8,128)(2,1)}, bf16[128,2048]{1,0:T(8,128)(2,1)}, bf16[128,2048]{1,0:T(8,128)(2,1)}, bf16[128,2048]{1,0:T(8,128)(2,1)}, bf16[48,2...) custom-call(s32[2]{0:T(128)S(1)} %copy-done.6, ...), custom_call_target="tpu_custom_call", output_to_operand_aliasing={{0}: (4, {}), {1}: (5, {}), {2}: (6, {}), {3}: (7, {})} | custom-call | flops 1 | bytes 1 | tf_op jit(solution)/shard_map/join/pallas_call | solution.py:595
  (23 shorter events, 0.1 us)
Async XLA Ops:
  1.3 3.7 %copy-start.8 = (f32[128]{0:T(128)S(1)}, f32[128]{0:T(128)}, u32[]{:S(2)}) copy-start(f32[128]{0:T(128)} %param.16) | copy-start | bytes 1540
  1.3 3.7 %copy-start.9 = (f32[128]{0:T(128)S(1)}, f32[128]{0:T(128)}, u32[]{:S(2)}) copy-start(f32[128]{0:T(128)} %param.15) | copy-start | bytes 1540
  1.3 6.6 %copy-start.4 = (bf16[1,48,2048]{2,1,0:T(8,128)(2,1)S(1)}, bf16[1,48,2048]{2,1,0:T(8,128)(2,1)}, u32[]{:S(2)}) copy-start(bf16[1,48,2048]{2,1,0:T(8,128)(2,1)} %param.13) | copy-start | bytes 589828
  1.3 6.6 %copy-start.5 = (bf16[1,48,2048]{2,1,0:T(8,128)(2,1)S(1)}, bf16[1,48,2048]{2,1,0:T(8,128)(2,1)}, u32[]{:S(2)}) copy-start(bf16[1,48,2048]{2,1,0:T(8,128)(2,1)} %param.14) | copy-start | bytes 589828
  1.3 6.6 %copy-start.6 = (s32[2]{0:T(128)S(1)}, s32[2]{0:T(128)}, u32[]{:S(2)}) copy-start(s32[2]{0:T(128)} %pad_add_fusion.state_ref) | copy-start | bytes 28
  4.5 8.1 %copy-start = (bf16[1,128,2048]{2,1,0:T(8,128)(2,1)S(1)}, bf16[1,128,2048]{2,1,0:T(8,128)(2,1)}, u32[]{:S(2)}) copy-start(bf16[1,128,2048]{2,1,0:T(8,128)(2,1)} %param.12) | copy-start | bytes 1572868
  4.5 8.1 %copy-start.1 = (bf16[1,128,2048]{2,1,0:T(8,128)(2,1)S(1)}, bf16[1,128,2048]{2,1,0:T(8,128)(2,1)}, u32[]{:S(2)}) copy-start(bf16[1,128,2048]{2,1,0:T(8,128)(2,1)} %param.11) | copy-start | bytes 1572868
  4.5 3.4 %collective-permute-start = (bf16[640,1024]{1,0:T(8,128)(2,1)}, bf16[640,1024]{1,0:T(8,128)(2,1)S(1)}, u32[]{:S(2)}, u32[]{:S(2)}) collective-permute-start(bf16[640,1024]{1,0:T(8,128)(2,1)} %pack.1), channel_id=1, source_target_pairs={{0,1},{1,0},{2,3},{3,2},{4,5},{5,4},{6,7},{7,6},{8,9},{9,8},{10,11... | collective-permute-start | bytes 3932168 | tf_op jit(solution)/shard_map/ppermute | solution.py:743
  8.6 13.5 %collective-permute-start.1 = (bf16[192,512]{1,0:T(8,128)(2,1)S(1)}, bf16[192,512]{1,0:T(8,128)(2,1)S(1)}, u32[]{:S(2)}, u32[]{:S(2)}) collective-permute-start(bf16[192,512]{1,0:T(8,128)(2,1)S(1)} %pair_lyrics.2.refs_0_), channel_id=1, source_target_pairs={{0,4},{1,5},{2,6},{3,7},{4,0},{5,1},{6,2},{7,3},{8,12},{9,13},{10,... | collective-permute-start | bytes 589832 | tf_op jit(solution)/shard_map/ppermute | solution.py:698
  14.1 31.8 %collective-permute-start.7 = (bf16[448,512]{1,0:T(8,128)(2,1)}, bf16[448,512]{1,0:T(8,128)(2,1)}, u32[]{:S(2)}, u32[]{:S(2)}) collective-permute-start(bf16[448,512]{1,0:T(8,128)(2,1)} %edge.6), channel_id=1, source_target_pairs={{0,2},{1,3},{2,0},{3,1},{4,6},{5,7},{6,4},{7,5},{8,10},{9,11},{10,... | collective-permute-start | bytes 1376264 | tf_op jit(solution)/shard_map/ppermute | solution.py:698
  22.1 11.7 %collective-permute-start.2 = (bf16[192,512]{1,0:T(8,128)(2,1)S(1)}, bf16[192,512]{1,0:T(8,128)(2,1)S(1)}, u32[]{:S(2)}, u32[]{:S(2)}) collective-permute-start(bf16[192,512]{1,0:T(8,128)(2,1)S(1)} %collective-permute-done.1.refs_0_.refs_1_), channel_id=1, source_target_pairs={{0,2},{1,3},{2,0},{3,1},{4,6},{5,7},{6,4},{7,5},{8,10},{9,11},{10,... | collective-permute-start | bytes 589832 | tf_op jit(solution)/shard_map/ppermute | solution.py:698
  24.2 21.7 %collective-permute-start.8 = (bf16[256,512]{1,0:T(8,128)(2,1)}, bf16[256,512]{1,0:T(8,128)(2,1)}, u32[]{:S(2)}, u32[]{:S(2)}) collective-permute-start(bf16[256,512]{1,0:T(8,128)(2,1)} %edge.7), channel_id=1, source_target_pairs={{2,4},{3,5},{4,2},{5,3},{10,12},{11,13},{12,10},{13,11},{18,20},{1... | collective-permute-start | bytes 786440 | tf_op jit(solution)/shard_map/ppermute | solution.py:698
  26.2 10.3 %copy-start.7 = (s32[1,1,2]{2,1,0:T(1,128)S(1)}, s32[1,1,2]{2,1,0:T(1,128)}, u32[]{:S(2)}) copy-start(s32[1,1,2]{2,1,0:T(1,128)} %param.18) | copy-start | bytes 28
  26.2 18.2 %collective-permute-start.4 = (bf16[192,512]{1,0:T(8,128)(2,1)S(1)}, bf16[192,512]{1,0:T(8,128)(2,1)S(1)}, u32[]{:S(2)}, u32[]{:S(2)}) collective-permute-start(bf16[192,512]{1,0:T(8,128)(2,1)S(1)} %pair_lyrics.3.refs_0_), channel_id=1, source_target_pairs={{0,4},{1,5},{2,6},{3,7},{4,0},{5,1},{6,2},{7,3},{8,12},{9,13},{10,... | collective-permute-start | bytes 589832 | tf_op jit(solution)/shard_map/ppermute | solution.py:698
  35.3 30.7 %collective-permute-start.3 = (bf16[448,512]{1,0:T(8,128)(2,1)}, bf16[448,512]{1,0:T(8,128)(2,1)}, u32[]{:S(2)}, u32[]{:S(2)}) collective-permute-start(bf16[448,512]{1,0:T(8,128)(2,1)} %edge.4), channel_id=1, source_target_pairs={{0,2},{1,3},{2,0},{3,1},{4,6},{5,7},{6,4},{7,5},{8,10},{9,11},{10,... | collective-permute-start | bytes 1376264 | tf_op jit(solution)/shard_map/ppermute | solution.py:698
  39.5 6.4 %copy-start.2 = (bf16[1,128,2048]{2,1,0:T(8,128)(2,1)S(1)}, bf16[1,128,2048]{2,1,0:T(8,128)(2,1)}, u32[]{:S(2)}) copy-start(bf16[1,128,2048]{2,1,0:T(8,128)(2,1)} %param.10) | copy-start | bytes 1572868
  39.5 6.4 %copy-start.3 = (bf16[1,128,2048]{2,1,0:T(8,128)(2,1)S(1)}, bf16[1,128,2048]{2,1,0:T(8,128)(2,1)}, u32[]{:S(2)}) copy-start(bf16[1,128,2048]{2,1,0:T(8,128)(2,1)} %param.17) | copy-start | bytes 1572868
  45.1 20.9 %collective-permute-start.5 = (bf16[256,512]{1,0:T(8,128)(2,1)S(1)}, bf16[256,512]{1,0:T(8,128)(2,1)S(1)}, u32[]{:S(2)}, u32[]{:S(2)}) collective-permute-start(bf16[256,512]{1,0:T(8,128)(2,1)S(1)} %edge.5), channel_id=1, source_target_pairs={{2,4},{3,5},{4,2},{5,3},{10,12},{11,13},{12,10},{13,11},{18,20},{1... | collective-permute-start | bytes 786440 | tf_op jit(solution)/shard_map/ppermute | solution.py:698
  51.1 7.9 %collective-permute-start.9 = (bf16[192,512]{1,0:T(8,128)(2,1)S(1)}, bf16[192,512]{1,0:T(8,128)(2,1)S(1)}, u32[]{:S(2)}, u32[]{:S(2)}) collective-permute-start(bf16[192,512]{1,0:T(8,128)(2,1)S(1)} %get-tuple-element.49), channel_id=1, source_target_pairs={{0,2},{1,3},{2,0},{3,1},{4,6},{5,7},{6,4},{7,5},{8,10},{9,11},{10,... | collective-permute-start | bytes 589832 | tf_op jit(solution)/shard_map/ppermute | solution.py:698
  52.4 12.9 %collective-permute-start.6 = (bf16[192,512]{1,0:T(8,128)(2,1)S(1)}, bf16[192,512]{1,0:T(8,128)(2,1)S(1)}, u32[]{:S(2)}, u32[]{:S(2)}) collective-permute-start(bf16[192,512]{1,0:T(8,128)(2,1)S(1)} %collective-permute-done.4.refs_0_.refs_1_), channel_id=1, source_target_pairs={{0,2},{1,3},{2,0},{3,1},{4,6},{5,7},{6,4},{7,5},{8,10},{9,11},{10,... | collective-permute-start | bytes 589832 | tf_op jit(solution)/shard_map/ppermute | solution.py:698
  53.2 27.8 %collective-permute-start.14 = (bf16[448,512]{1,0:T(8,128)(2,1)S(1)}, bf16[448,512]{1,0:T(8,128)(2,1)S(1)}, u32[]{:S(2)}, u32[]{:S(2)}) collective-permute-start(bf16[448,512]{1,0:T(8,128)(2,1)S(1)} %get-tuple-element.52), channel_id=1, source_target_pairs={{0,2},{1,3},{2,0},{3,1},{4,6},{5,7},{6,4},{7,5},{8,10},{9,11},{10,... | collective-permute-start | bytes 1376264 | tf_op jit(solution)/shard_map/ppermute | solution.py:698
  59.0 21.9 %collective-permute-start.17 = (bf16[256,512]{1,0:T(8,128)(2,1)S(1)}, bf16[256,512]{1,0:T(8,128)(2,1)S(1)}, u32[]{:S(2)}, u32[]{:S(2)}) collective-permute-start(bf16[256,512]{1,0:T(8,128)(2,1)S(1)} %get-tuple-element.57), channel_id=1, source_target_pairs={{2,4},{3,5},{4,2},{5,3},{10,12},{11,13},{12,10},{13,11},{18,20},{1... | collective-permute-start | bytes 786440 | tf_op jit(solution)/shard_map/ppermute | solution.py:698
  65.3 15.6 %collective-permute-start.15 = (bf16[192,512]{1,0:T(8,128)(2,1)S(1)}, bf16[192,512]{1,0:T(8,128)(2,1)S(1)}, u32[]{:S(2)}, u32[]{:S(2)}) collective-permute-start(bf16[192,512]{1,0:T(8,128)(2,1)S(1)} %relay.2.refs_4_), channel_id=1, source_target_pairs={{0,4},{1,5},{2,6},{3,7},{4,0},{5,1},{6,2},{7,3},{8,12},{9,13},{10,... | collective-permute-start | bytes 589832 | tf_op jit(solution)/shard_map/ppermute | solution.py:698
  71.1 9.8 %collective-permute-start.16 = (bf16[192,512]{1,0:T(8,128)(2,1)S(1)}, bf16[192,512]{1,0:T(8,128)(2,1)S(1)}, u32[]{:S(2)}, u32[]{:S(2)}) collective-permute-start(bf16[192,512]{1,0:T(8,128)(2,1)S(1)} %get-tuple-element.55), channel_id=1, source_target_pairs={{0,2},{1,3},{2,0},{3,1},{4,6},{5,7},{6,4},{7,5},{8,10},{9,11},{10,... | collective-permute-start | bytes 589832 | tf_op jit(solution)/shard_map/ppermute | solution.py:698
  73.7 3.6 %collective-permute-start.10 = (f32[8,128]{1,0:T(8,128)S(1)}, f32[8,128]{1,0:T(8,128)S(1)}, u32[]{:S(2)}, u32[]{:S(2)}) collective-permute-start(f32[8,128]{1,0:T(8,128)S(1)} %get-tuple-element.50), channel_id=1, source_target_pairs={{0,8},{8,0},{16,24},{24,16},{1,9},{9,1},{17,25},{25,17},{2,10},{10... | collective-permute-start | bytes 12296 | tf_op jit(solution)/shard_map/ppermute | solution.py:667
  77.3 3.6 %collective-permute-start.11 = (f32[8,128]{1,0:T(8,128)S(1)}, f32[8,128]{1,0:T(8,128)S(1)}, u32[]{:S(2)}, u32[]{:S(2)}) collective-permute-start(f32[8,128]{1,0:T(8,128)S(1)} %add.54), channel_id=1, source_target_pairs={{0,16},{8,24},{16,0},{24,8},{1,17},{9,25},{17,1},{25,9},{2,18},{10... | collective-permute-start | bytes 12296 | tf_op jit(solution)/shard_map/ppermute | solution.py:667
  81.0 16.6 %collective-permute-start.18 = (bf16[448,512]{1,0:T(8,128)(2,1)S(1)}, bf16[448,512]{1,0:T(8,128)(2,1)S(1)}, u32[]{:S(2)}, u32[]{:S(2)}) collective-permute-start(bf16[448,512]{1,0:T(8,128)(2,1)S(1)} %get-tuple-element.58), channel_id=1, source_target_pairs={{0,2},{1,3},{2,0},{3,1},{4,6},{5,7},{6,4},{7,5},{8,10},{9,11},{10,... | collective-permute-start | bytes 1376264 | tf_op jit(solution)/shard_map/ppermute | solution.py:698
  81.1 17.4 %collective-permute-start.20 = (bf16[256,512]{1,0:T(8,128)(2,1)S(1)}, bf16[256,512]{1,0:T(8,128)(2,1)S(1)}, u32[]{:S(2)}, u32[]{:S(2)}) collective-permute-start(bf16[256,512]{1,0:T(8,128)(2,1)S(1)} %get-tuple-element.71), channel_id=1, source_target_pairs={{2,4},{3,5},{4,2},{5,3},{10,12},{11,13},{12,10},{13,11},{18,20},{1... | collective-permute-start | bytes 786440 | tf_op jit(solution)/shard_map/ppermute | solution.py:698
  81.8 15.8 %collective-permute-start.19 = (bf16[192,512]{1,0:T(8,128)(2,1)S(1)}, bf16[192,512]{1,0:T(8,128)(2,1)S(1)}, u32[]{:S(2)}, u32[]{:S(2)}) collective-permute-start(bf16[192,512]{1,0:T(8,128)(2,1)S(1)} %get-tuple-element.59), channel_id=1, source_target_pairs={{0,4},{1,5},{2,6},{3,7},{4,0},{5,1},{6,2},{7,3},{8,12},{9,13},{10,... | collective-permute-start | bytes 589832 | tf_op jit(solution)/shard_map/ppermute | solution.py:698
  86.5 6.4 %collective-permute-start.12 = (f32[8,128]{1,0:T(8,128)S(1)}, f32[8,128]{1,0:T(8,128)S(1)}, u32[]{:S(2)}, u32[]{:S(2)}) collective-permute-start(f32[8,128]{1,0:T(8,128)S(1)} %add.55.refs_4_), channel_id=1, source_target_pairs={{0,2},{1,3},{2,0},{3,1},{4,6},{5,7},{6,4},{7,5},{8,10},{9,11},{10,... | collective-permute-start | bytes 12296 | tf_op jit(solution)/shard_map/ppermute | solution.py:667
  92.9 4.7 %collective-permute-start.13 = (f32[8,128]{1,0:T(8,128)S(1)}, f32[8,128]{1,0:T(8,128)S(1)}, u32[]{:S(2)}, u32[]{:S(2)}) collective-permute-start(f32[8,128]{1,0:T(8,128)S(1)} %add.56), channel_id=1, source_target_pairs={{0,4},{1,5},{2,6},{3,7},{4,0},{5,1},{6,2},{7,3},{8,12},{9,13},{10,... | collective-permute-start | bytes 12296 | tf_op jit(solution)/shard_map/ppermute | solution.py:667
  100.8 3.1 %collective-permute-start.21 = (bf16[624,1024]{1,0:T(8,128)(2,1)S(1)}, bf16[624,1024]{1,0:T(8,128)(2,1)S(1)}, u32[]{:S(2)}, u32[]{:S(2)}) collective-permute-start(bf16[624,1024]{1,0:T(8,128)(2,1)S(1)} %get-tuple-element.73), channel_id=1, source_target_pairs={{0,1},{1,0},{2,3},{3,2},{4,5},{5,4},{6,7},{7,6},{8,9},{9,8},{10,11... | collective-permute-start | bytes 3833864 | tf_op jit(solution)/shard_map/ppermute | solution.py:791

commit v15 on v14

--- a/solution.py
+++ b/solution.py
@@ -770,7 +770,7 @@
                 relayed = [relay(for_two, arrived)]
                 to_two = relayed[0]
             else:
-                gain_total = sum_over(gain_part, "song", bits_of(songs))
+                gain_total = sum_over(gain_part, "song", bits_of(songs)[:1])
                 to_two, to_one = last_relay(for_two, arrived, to_one, [*sent, gain_total])
             two_back, one_back = hop(to_two, across), hop(to_one, partners)
             lyric_chunks += [held, one_back, two_back]
@@ -782,6 +782,7 @@
 
     to_mate = []
     if hops:
+        gain_total = sum_over(gain_total, "song", bits_of(songs)[1:])
         gain_total = sum_over(gain_total, "seq", [2, 4])
         own_half, part_to_mate = finish_lyric(
             state, gains, lyric_keys[0], mate, gain_total, lyric_chunks

time: 106 us -> 106 us (level)
    ppermute x4, waiting for transfers between devices: 12.3 us -> 10.1 us  [sum_over(): lax.ppermute(total, axis, [(i, i ^ bit) for i in range(count)])]
    ppermute x16, waiting for transfers between devices: 25.1 us -> 27.2 us  [hop(): return lax.ppermute(block, 'seq', pairs)]
  transfers between devices with their start and end apart: 22 -> 22, of which waited for: 11 -> 12; matrix products, arithmetic and copies ran while one was open for 2% -> 2% of each run, Pallas kernels for 17% -> 17%
where the time goes in v15:
time: 106 us
  waiting for transfers between devices  43.1 us (41%)
  starting transfers between devices  32.4 us (31%)
  Pallas kernels  26.3 us (25%)
  local copies, waits for them, and re-layouts  2.02 us (2%)
  between operations  1.58 us (1%)
    ppermute x16, waiting for transfers between devices, hop(): return lax.ppermute(block, 'seq', pairs)  27.2 us
    ppermute x16, starting transfers between devices, hop(): return lax.ppermute(block, 'seq', pairs)  25.8 us
    pallas_call x2, Pallas kernels, attention(): call(functools.partial(attention_kernel, chunk, len(earlier), len(after),...  10.3 us
    ppermute x4, waiting for transfers between devices, sum_over(): lax.ppermute(total, axis, [(i, i ^ bit) for i in range(count)])  10.1 us
    ppermute x4, starting transfers between devices, sum_over(): lax.ppermute(total, axis, [(i, i ^ bit) for i in range(count)])  6.02 us
    pallas_call x4, Pallas kernels, edge(): call(functools.partial(edge_kernel, chunk, touching, bool(lead)), 'edge',...  5.08 us
    pallas_call x1, Pallas kernels, pack(): call(pack_kernel, 'pack', [SMEM, SMEM] + [HBM] * len(arrays), VMEM, shape...  3.17 us
    ppermute x1, waiting for transfers between devices, body(): from_mate = lax.ppermute(to_mate, 'seq', swap)  2.97 us
  transfers between devices with their start and end apart: 22, of which 12 were waited for; matrix products, arithmetic and copies ran while one was open for 2% of the time, Pallas kernels for 17%

profile of v15, /device:TPU:0, one launch (start us, length us, event | category | flops | bytes accessed | tf_op | source)
XLA Modules:
  0.0 106.0 jit_solution(13162309619766096063)
XLA Ops:
  0.7 0.6 pad_add_fusion.state_ref
  1.3 0.0 copy-start.6
  1.3 3.2 %pack.1 = bf16[640,1024]{1,0:T(8,128)(2,1)} custom-call(s32[2]{0:T(128)} %pad_add_fusion.state_ref, s32[2]{0:T(128)} %bitcast.62, bf16[128,2048]{1,0:T(8,128)(2,1)} %bitcast.45, bf16[128,2048]{1,0:T(8,128)(2,1)} %bitcast.48, bf16[128,2048]{1,0:T(8,128)(2,1)} %bitcast.38, bf16[128,2048]{1,0:T(8,128)(2,1)} %bitcast.31, bf16[48,2048]{1,0:T(8,128)(2,1)} %bitcast.51, ...), custom_call_target="tpu_custom_call" | custom-call | flops 1 | bytes 1 | tf_op jit(solution)/shard_map/pack/pallas_call | solution.py:128
  4.5 0.0 copy-start
  4.5 0.0 copy-start.1
  4.5 0.5 collective-permute-start
  5.0 2.9 %collective-permute-done.mate_ref = bf16[640,1024]{1,0:T(8,128)(2,1)S(1)} collective-permute-done((bf16[640,1024]{1,0:T(8,128)(2,1)}, bf16[640,1024]{1,0:T(8,128)(2,1)S(1)}, u32[]{:S(2)}, u32[]{:S(2)}) %collective-permute-start) | collective-permute-done | bytes 1310752 | tf_op jit(solution)/shard_map/ppermute | solution.py:743
  7.9 0.7 pair_lyrics.2.refs_0_
  8.6 4.0 %collective-permute-start.1 = (bf16[192,512]{1,0:T(8,128)(2,1)S(1)}, bf16[192,512]{1,0:T(8,128)(2,1)S(1)}, u32[]{:S(2)}, u32[]{:S(2)}) collective-permute-start(bf16[192,512]{1,0:T(8,128)(2,1)S(1)} %pair_lyrics.2.refs_0_), channel_id=1, source_target_pairs={{0,4},{1,5},{2,6},{3,7},{4,0},{5,1},{6,2},{7,3},{8,12},{9,13},{10,... | collective-permute-start | bytes 589832 | tf_op jit(solution)/shard_map/ppermute | solution.py:698
  12.6 1.5 %edge.6 = bf16[448,512]{1,0:T(8,128)(2,1)} custom-call(s32[2]{0:T(128)S(1)} %copy-done.6, f32[2,128]{1,0:T(2,128)S(1)} %pad_maximum_fusion.gain_ref, bf16[128,2048]{1,0:T(8,128)(2,1)S(1)} %bitcast.39, bf16[128,2048]{1,0:T(8,128)(2,1)S(1)} %bitcast.32, bf16[640,1024]{1,0:T(8,128)(2,1)S(1)} %collective-permute-done.mate_ref, ...), custom_call_target="tpu_custom_call" | custom-call | flops 1 | bytes 1 | tf_op jit(solution)/shard_map/edge/pallas_call | solution.py:185
  14.1 1.6 %collective-permute-start.7 = (bf16[448,512]{1,0:T(8,128)(2,1)}, bf16[448,512]{1,0:T(8,128)(2,1)}, u32[]{:S(2)}, u32[]{:S(2)}) collective-permute-start(bf16[448,512]{1,0:T(8,128)(2,1)} %edge.6), channel_id=1, source_target_pairs={{0,2},{1,3},{2,0},{3,1},{4,6},{5,7},{6,4},{7,5},{8,10},{9,11},{10,... | collective-permute-start | bytes 1376264 | tf_op jit(solution)/shard_map/ppermute | solution.py:698
  15.7 6.5 %collective-permute-done.1.refs_0_.refs_1_ = bf16[192,512]{1,0:T(8,128)(2,1)S(1)} collective-permute-done((bf16[192,512]{1,0:T(8,128)(2,1)S(1)}, bf16[192,512]{1,0:T(8,128)(2,1)S(1)}, u32[]{:S(2)}, u32[]{:S(2)}) %collective-permute-start.1) | collective-permute-done | bytes 196640 | tf_op jit(solution)/shard_map/ppermute | solution.py:698
  22.1 0.7 collective-permute-start.2
  22.8 1.4 %edge.7 = bf16[256,512]{1,0:T(8,128)(2,1)} custom-call(s32[2]{0:T(128)S(1)} %copy-done.6, f32[2,128]{1,0:T(2,128)S(1)} %pad_maximum_fusion.gain_ref, bf16[128,2048]{1,0:T(8,128)(2,1)S(1)} %bitcast.40, bf16[128,2048]{1,0:T(8,128)(2,1)S(1)} %bitcast.33, bf16[640,1024]{1,0:T(8,128)(2,1)S(1)} %collective-permute-done.mate_ref, ...), custom_call_target="tpu_custom_call" | custom-call | flops 1 | bytes 1 | tf_op jit(solution)/shard_map/edge/pallas_call | solution.py:185
  24.2 1.4 %collective-permute-start.8 = (bf16[256,512]{1,0:T(8,128)(2,1)}, bf16[256,512]{1,0:T(8,128)(2,1)}, u32[]{:S(2)}, u32[]{:S(2)}) collective-permute-start(bf16[256,512]{1,0:T(8,128)(2,1)} %edge.7), channel_id=1, source_target_pairs={{2,4},{3,5},{4,2},{5,3},{10,12},{11,13},{12,10},{13,11},{18,20},{1... | collective-permute-start | bytes 786440 | tf_op jit(solution)/shard_map/ppermute | solution.py:698
  25.5 0.7 pair_lyrics.3.refs_0_
  26.2 0.0 copy-start.7
  26.2 4.1 %collective-permute-start.4 = (bf16[192,512]{1,0:T(8,128)(2,1)S(1)}, bf16[192,512]{1,0:T(8,128)(2,1)S(1)}, u32[]{:S(2)}, u32[]{:S(2)}) collective-permute-start(bf16[192,512]{1,0:T(8,128)(2,1)S(1)} %pair_lyrics.3.refs_0_), channel_id=1, source_target_pairs={{0,4},{1,5},{2,6},{3,7},{4,0},{5,1},{6,2},{7,3},{8,12},{9,13},{10,... | collective-permute-start | bytes 589832 | tf_op jit(solution)/shard_map/ppermute | solution.py:698
  30.3 3.5 %collective-permute-done.2.refs_1_.refs_2_ = bf16[192,512]{1,0:T(8,128)(2,1)S(1)} collective-permute-done((bf16[192,512]{1,0:T(8,128)(2,1)S(1)}, bf16[192,512]{1,0:T(8,128)(2,1)S(1)}, u32[]{:S(2)}, u32[]{:S(2)}) %collective-permute-start.2) | collective-permute-done | bytes 196640 | tf_op jit(solution)/shard_map/ppermute | solution.py:698
  33.8 1.5 %edge.4 = bf16[448,512]{1,0:T(8,128)(2,1)} custom-call(s32[2]{0:T(128)S(1)} %copy-done.6, f32[2,128]{1,0:T(2,128)S(1)} %pad_maximum_fusion.gain_ref, bf16[128,2048]{1,0:T(8,128)(2,1)S(1)} %bitcast.41, bf16[128,2048]{1,0:T(8,128)(2,1)S(1)} %bitcast.34, bf16[640,1024]{1,0:T(8,128)(2,1)S(1)} %collective-permute-done.mate_ref, ...), custom_call_target="tpu_custom_call" | custom-call | flops 1 | bytes 1 | tf_op jit(solution)/shard_map/edge/pallas_call | solution.py:185
  35.3 0.6 collective-permute-start.3
  36.6 0.6 fusion
  37.2 1.4 %stack.74.meta_ref = s32[15]{0:T(128)S(1)} concatenate(s32[1]{0:T(128)} %bitcast, s32[1]{0:T(128)} %bitcast.1, s32[1]{0:T(128)} %bitcast.2, s32[1]{0:T(128)} %bitcast.3, s32[1]{0:T(128)S(6)} %copy.28, s32[1]{0:T(128)} %bitcast.4, s32[1]{0:T(128)} %bitcast.5, s32[1]{0:T(128)} %bitcast.6, s32[1]{0:T(128)} %bitcast.7, s32[1]{0:T(128)} %bitcast.8, s32[1]{0:T(128)} %bitcast.9, ...), dimensions={0} | concatenate | bytes 120 | tf_op jit(solution)/shard_map/stack | solution.py:727
  38.5 0.9 prepare_keys.1.key_ref
  39.5 0.0 copy-start.2
  39.5 0.0 copy-start.3
  39.5 4.9 %collective-permute-done.4.refs_0_.refs_1_ = bf16[192,512]{1,0:T(8,128)(2,1)S(1)} collective-permute-done((bf16[192,512]{1,0:T(8,128)(2,1)S(1)}, bf16[192,512]{1,0:T(8,128)(2,1)S(1)}, u32[]{:S(2)}, u32[]{:S(2)}) %collective-permute-start.4) | collective-permute-done | bytes 196640 | tf_op jit(solution)/shard_map/ppermute | solution.py:698
  44.4 0.7 edge.5
  45.1 0.7 collective-permute-start.5
  45.8 0.0 collective-permute-done.7.one_ref
  45.8 0.0 collective-permute-done.8.mid_ref
  45.9 5.2 %attention.2 = (bf16[128,512]{1,0:T(8,128)(2,1)S(1)}, bf16[128,512]{1,0:T(8,128)(2,1)S(1)}, bf16[256,512]{1,0:T(8,128)(2,1)S(1)}, f32[256,512]{1,0:T(8,128)S(1)}...) custom-call(s32[15]{0:T(128)S(1)} %stack.74.meta_ref, ...), custom_call_target="tpu_custom_call" | custom-call | flops 1207959552 | bytes 8388608 | tf_op jit(solution)/shard_map/attention/pallas_call | solution.py:415
  51.1 1.3 %collective-permute-start.9 = (bf16[192,512]{1,0:T(8,128)(2,1)S(1)}, bf16[192,512]{1,0:T(8,128)(2,1)S(1)}, u32[]{:S(2)}, u32[]{:S(2)}) collective-permute-start(bf16[192,512]{1,0:T(8,128)(2,1)S(1)} %get-tuple-element.49), channel_id=1, source_target_pairs={{0,2},{1,3},{2,0},{3,1},{4,6},{5,7},{6,4},{7,5},{8,10},{9,11},{10,... | collective-permute-start | bytes 589832 | tf_op jit(solution)/shard_map/ppermute | solution.py:698
  52.4 0.7 collective-permute-start.6
  53.2 1.3 %collective-permute-start.14 = (bf16[448,512]{1,0:T(8,128)(2,1)S(1)}, bf16[448,512]{1,0:T(8,128)(2,1)S(1)}, u32[]{:S(2)}, u32[]{:S(2)}) collective-permute-start(bf16[448,512]{1,0:T(8,128)(2,1)S(1)} %get-tuple-element.52), channel_id=1, source_target_pairs={{0,2},{1,3},{2,0},{3,1},{4,6},{5,7},{6,4},{7,5},{8,10},{9,11},{10,... | collective-permute-start | bytes 1376264 | tf_op jit(solution)/shard_map/ppermute | solution.py:698
  54.4 4.5 %collective-permute-done.9.arrived_ref = bf16[192,512]{1,0:T(8,128)(2,1)S(1)} collective-permute-done((bf16[192,512]{1,0:T(8,128)(2,1)S(1)}, bf16[192,512]{1,0:T(8,128)(2,1)S(1)}, u32[]{:S(2)}, u32[]{:S(2)}) %collective-permute-start.9) | collective-permute-done | bytes 196640 | tf_op jit(solution)/shard_map/ppermute | solution.py:698
  59.0 0.7 collective-permute-start.17
  59.7 5.6 %collective-permute-done.6.refs_2_ = bf16[192,512]{1,0:T(8,128)(2,1)S(1)} collective-permute-done((bf16[192,512]{1,0:T(8,128)(2,1)S(1)}, bf16[192,512]{1,0:T(8,128)(2,1)S(1)}, u32[]{:S(2)}, u32[]{:S(2)}) %collective-permute-start.6) | collective-permute-done | bytes 196640 | tf_op jit(solution)/shard_map/ppermute | solution.py:698
  65.3 0.7 collective-permute-start.15
  66.0 0.0 collective-permute-done.5.mid_ref
  66.0 0.0 collective-permute-done.3.one_ref
  66.0 5.1 %attention.3 = (bf16[128,512]{1,0:T(8,128)(2,1)S(1)}, bf16[128,512]{1,0:T(8,128)(2,1)S(1)}, bf16[256,512]{1,0:T(8,128)(2,1)S(1)}, f32[256,512]{1,0:T(8,128)S(1)}...) custom-call(s32[15]{0:T(128)S(1)} %stack.74.meta_ref, ...), custom_call_target="tpu_custom_call" | custom-call | flops 1207959552 | bytes 8388608 | tf_op jit(solution)/shard_map/attention/pallas_call | solution.py:415
  71.1 2.5 %collective-permute-start.16 = (bf16[192,512]{1,0:T(8,128)(2,1)S(1)}, bf16[192,512]{1,0:T(8,128)(2,1)S(1)}, u32[]{:S(2)}, u32[]{:S(2)}) collective-permute-start(bf16[192,512]{1,0:T(8,128)(2,1)S(1)} %get-tuple-element.55), channel_id=1, source_target_pairs={{0,2},{1,3},{2,0},{3,1},{4,6},{5,7},{6,4},{7,5},{8,10},{9,11},{10,... | collective-permute-start | bytes 589832 | tf_op jit(solution)/shard_map/ppermute | solution.py:698
  73.7 1.5 %collective-permute-start.10 = (f32[8,128]{1,0:T(8,128)S(1)}, f32[8,128]{1,0:T(8,128)S(1)}, u32[]{:S(2)}, u32[]{:S(2)}) collective-permute-start(f32[8,128]{1,0:T(8,128)S(1)} %get-tuple-element.50), channel_id=1, source_target_pairs={{0,8},{8,0},{16,24},{24,16},{1,9},{9,1},{17,25},{25,17},{2,10},{10... | collective-permute-start | bytes 12296 | tf_op jit(solution)/shard_map/ppermute | solution.py:667
  75.2 2.1 %collective-permute-done.10 = f32[8,128]{1,0:T(8,128)S(1)} collective-permute-done((f32[8,128]{1,0:T(8,128)S(1)}, f32[8,128]{1,0:T(8,128)S(1)}, u32[]{:S(2)}, u32[]{:S(2)}) %collective-permute-start.10) | collective-permute-done | bytes 4128 | tf_op jit(solution)/shard_map/ppermute | solution.py:667
  77.3 0.0 collective-permute-done.17.refs_1_.refs_6_
  77.3 0.0 collective-permute-done.15.refs_3_.refs_2_
  77.3 0.0 collective-permute-done.14.refs_2_.refs_1_.refs_5_
  77.3 2.1 %collective-permute-done.16.arrived_ref = bf16[192,512]{1,0:T(8,128)(2,1)S(1)} collective-permute-done((bf16[192,512]{1,0:T(8,128)(2,1)S(1)}, bf16[192,512]{1,0:T(8,128)(2,1)S(1)}, u32[]{:S(2)}, u32[]{:S(2)}) %collective-permute-start.16) | collective-permute-done | bytes 196640 | tf_op jit(solution)/shard_map/ppermute | solution.py:698
  79.5 1.1 %collective-permute-start.18 = (bf16[448,512]{1,0:T(8,128)(2,1)S(1)}, bf16[448,512]{1,0:T(8,128)(2,1)S(1)}, u32[]{:S(2)}, u32[]{:S(2)}) collective-permute-start(bf16[448,512]{1,0:T(8,128)(2,1)S(1)} %get-tuple-element.58), channel_id=1, source_target_pairs={{0,2},{1,3},{2,0},{3,1},{4,6},{5,7},{6,4},{7,5},{8,10},{9,11},{10,... | collective-permute-start | bytes 1376264 | tf_op jit(solution)/shard_map/ppermute | solution.py:698
  80.6 0.7 collective-permute-start.20
  81.3 3.7 %collective-permute-start.19 = (bf16[192,512]{1,0:T(8,128)(2,1)S(1)}, bf16[192,512]{1,0:T(8,128)(2,1)S(1)}, u32[]{:S(2)}, u32[]{:S(2)}) collective-permute-start(bf16[192,512]{1,0:T(8,128)(2,1)S(1)} %get-tuple-element.59), channel_id=1, source_target_pairs={{0,4},{1,5},{2,6},{3,7},{4,0},{5,1},{6,2},{7,3},{8,12},{9,13},{10,... | collective-permute-start | bytes 589832 | tf_op jit(solution)/shard_map/ppermute | solution.py:698
  85.0 1.5 %collective-permute-start.11 = (f32[8,128]{1,0:T(8,128)S(1)}, f32[8,128]{1,0:T(8,128)S(1)}, u32[]{:S(2)}, u32[]{:S(2)}) collective-permute-start(f32[8,128]{1,0:T(8,128)S(1)} %add.54.refs_4_), channel_id=1, source_target_pairs={{0,16},{8,24},{16,0},{24,8},{1,17},{9,25},{17,1},{25,9},{2,18},{10... | collective-permute-start | bytes 12296 | tf_op jit(solution)/shard_map/ppermute | solution.py:667
  86.6 2.1 %collective-permute-done.11 = f32[8,128]{1,0:T(8,128)S(1)} collective-permute-done((f32[8,128]{1,0:T(8,128)S(1)}, f32[8,128]{1,0:T(8,128)S(1)}, u32[]{:S(2)}, u32[]{:S(2)}) %collective-permute-start.11) | collective-permute-done | bytes 4128 | tf_op jit(solution)/shard_map/ppermute | solution.py:667
  88.6 0.0 collective-permute-start.12
  88.7 4.2 %collective-permute-done.12 = f32[8,128]{1,0:T(8,128)S(1)} collective-permute-done((f32[8,128]{1,0:T(8,128)S(1)}, f32[8,128]{1,0:T(8,128)S(1)}, u32[]{:S(2)}, u32[]{:S(2)}) %collective-permute-start.12) | collective-permute-done | bytes 4128 | tf_op jit(solution)/shard_map/ppermute | solution.py:667
  92.9 3.0 %collective-permute-start.13 = (f32[8,128]{1,0:T(8,128)S(1)}, f32[8,128]{1,0:T(8,128)S(1)}, u32[]{:S(2)}, u32[]{:S(2)}) collective-permute-start(f32[8,128]{1,0:T(8,128)S(1)} %add.56), channel_id=1, source_target_pairs={{0,4},{1,5},{2,6},{3,7},{4,0},{5,1},{6,2},{7,3},{8,12},{9,13},{10,... | collective-permute-start | bytes 12296 | tf_op jit(solution)/shard_map/ppermute | solution.py:667
  95.9 1.7 %collective-permute-done.13 = f32[8,128]{1,0:T(8,128)S(1)} collective-permute-done((f32[8,128]{1,0:T(8,128)S(1)}, f32[8,128]{1,0:T(8,128)S(1)}, u32[]{:S(2)}, u32[]{:S(2)}) %collective-permute-start.13) | collective-permute-done | bytes 4128 | tf_op jit(solution)/shard_map/ppermute | solution.py:667
  97.5 0.9 finish_lyric.1
  98.5 0.0 collective-permute-done.20.refs_13_
  98.5 2.3 %finish_audio.1 = (bf16[128,2048]{1,0:T(8,128)(2,1)}, bf16[128,2048]{1,0:T(8,128)(2,1)}, bf16[128,2048]{1,0:T(8,128)(2,1)}, bf16[128,2048]{1,0:T(8,128)(2,1)}, bf16[624,1024]{1,0:T(8,128)(2,1)S(1)}) custom-call(s32[2]{0:T(128)S(1)} %copy-done.6, f32[2,128]{1,0:T(2,128)S(1)} %pad_maximum_fusion.gain_ref, bf16[128,2048]{1,0:T(8,128)(2,1)S(1)} %bitcast.44, ...), custom_call_target="tpu_custom_call" | custom-call | flops 1 | bytes 1 | tf_op jit(solution)/shard_map/finish_audio/pallas_call | solution.py:494
  100.8 0.1 collective-permute-start.21
  100.9 3.0 %collective-permute-done.21.mate_ref = bf16[624,1024]{1,0:T(8,128)(2,1)S(1)} collective-permute-done((bf16[624,1024]{1,0:T(8,128)(2,1)S(1)}, bf16[624,1024]{1,0:T(8,128)(2,1)S(1)}, u32[]{:S(2)}, u32[]{:S(2)}) %collective-permute-start.21) | collective-permute-done | bytes 1277984 | tf_op jit(solution)/shard_map/ppermute | solution.py:792
  103.8 2.2 %join.1 = (bf16[128,2048]{1,0:T(8,128)(2,1)}, bf16[128,2048]{1,0:T(8,128)(2,1)}, bf16[128,2048]{1,0:T(8,128)(2,1)}, bf16[128,2048]{1,0:T(8,128)(2,1)}, bf16[48,2...) custom-call(s32[2]{0:T(128)S(1)} %copy-done.6, ...), custom_call_target="tpu_custom_call", output_to_operand_aliasing={{0}: (4, {}), {1}: (5, {}), {2}: (6, {}), {3}: (7, {})} | custom-call | flops 1 | bytes 1 | tf_op jit(solution)/shard_map/join/pallas_call | solution.py:595
  (23 shorter events, 0.2 us)
Async XLA Ops:
  1.3 3.7 %copy-start.8 = (f32[128]{0:T(128)S(1)}, f32[128]{0:T(128)}, u32[]{:S(2)}) copy-start(f32[128]{0:T(128)} %param.16) | copy-start | bytes 1540
  1.3 3.7 %copy-start.9 = (f32[128]{0:T(128)S(1)}, f32[128]{0:T(128)}, u32[]{:S(2)}) copy-start(f32[128]{0:T(128)} %param.15) | copy-start | bytes 1540
  1.3 6.6 %copy-start.4 = (bf16[1,48,2048]{2,1,0:T(8,128)(2,1)S(1)}, bf16[1,48,2048]{2,1,0:T(8,128)(2,1)}, u32[]{:S(2)}) copy-start(bf16[1,48,2048]{2,1,0:T(8,128)(2,1)} %param.13) | copy-start | bytes 589828
  1.3 6.6 %copy-start.5 = (bf16[1,48,2048]{2,1,0:T(8,128)(2,1)S(1)}, bf16[1,48,2048]{2,1,0:T(8,128)(2,1)}, u32[]{:S(2)}) copy-start(bf16[1,48,2048]{2,1,0:T(8,128)(2,1)} %param.14) | copy-start | bytes 589828
  1.3 6.6 %copy-start.6 = (s32[2]{0:T(128)S(1)}, s32[2]{0:T(128)}, u32[]{:S(2)}) copy-start(s32[2]{0:T(128)} %pad_add_fusion.state_ref) | copy-start | bytes 28
  4.5 8.1 %copy-start = (bf16[1,128,2048]{2,1,0:T(8,128)(2,1)S(1)}, bf16[1,128,2048]{2,1,0:T(8,128)(2,1)}, u32[]{:S(2)}) copy-start(bf16[1,128,2048]{2,1,0:T(8,128)(2,1)} %param.12) | copy-start | bytes 1572868
  4.5 8.1 %copy-start.1 = (bf16[1,128,2048]{2,1,0:T(8,128)(2,1)S(1)}, bf16[1,128,2048]{2,1,0:T(8,128)(2,1)}, u32[]{:S(2)}) copy-start(bf16[1,128,2048]{2,1,0:T(8,128)(2,1)} %param.11) | copy-start | bytes 1572868
  4.5 3.4 %collective-permute-start = (bf16[640,1024]{1,0:T(8,128)(2,1)}, bf16[640,1024]{1,0:T(8,128)(2,1)S(1)}, u32[]{:S(2)}, u32[]{:S(2)}) collective-permute-start(bf16[640,1024]{1,0:T(8,128)(2,1)} %pack.1), channel_id=1, source_target_pairs={{0,1},{1,0},{2,3},{3,2},{4,5},{5,4},{6,7},{7,6},{8,9},{9,8},{10,11... | collective-permute-start | bytes 3932168 | tf_op jit(solution)/shard_map/ppermute | solution.py:743
  8.6 13.5 %collective-permute-start.1 = (bf16[192,512]{1,0:T(8,128)(2,1)S(1)}, bf16[192,512]{1,0:T(8,128)(2,1)S(1)}, u32[]{:S(2)}, u32[]{:S(2)}) collective-permute-start(bf16[192,512]{1,0:T(8,128)(2,1)S(1)} %pair_lyrics.2.refs_0_), channel_id=1, source_target_pairs={{0,4},{1,5},{2,6},{3,7},{4,0},{5,1},{6,2},{7,3},{8,12},{9,13},{10,... | collective-permute-start | bytes 589832 | tf_op jit(solution)/shard_map/ppermute | solution.py:698
  14.1 31.8 %collective-permute-start.7 = (bf16[448,512]{1,0:T(8,128)(2,1)}, bf16[448,512]{1,0:T(8,128)(2,1)}, u32[]{:S(2)}, u32[]{:S(2)}) collective-permute-start(bf16[448,512]{1,0:T(8,128)(2,1)} %edge.6), channel_id=1, source_target_pairs={{0,2},{1,3},{2,0},{3,1},{4,6},{5,7},{6,4},{7,5},{8,10},{9,11},{10,... | collective-permute-start | bytes 1376264 | tf_op jit(solution)/shard_map/ppermute | solution.py:698
  22.1 11.7 %collective-permute-start.2 = (bf16[192,512]{1,0:T(8,128)(2,1)S(1)}, bf16[192,512]{1,0:T(8,128)(2,1)S(1)}, u32[]{:S(2)}, u32[]{:S(2)}) collective-permute-start(bf16[192,512]{1,0:T(8,128)(2,1)S(1)} %collective-permute-done.1.refs_0_.refs_1_), channel_id=1, source_target_pairs={{0,2},{1,3},{2,0},{3,1},{4,6},{5,7},{6,4},{7,5},{8,10},{9,11},{10,... | collective-permute-start | bytes 589832 | tf_op jit(solution)/shard_map/ppermute | solution.py:698
  24.2 21.7 %collective-permute-start.8 = (bf16[256,512]{1,0:T(8,128)(2,1)}, bf16[256,512]{1,0:T(8,128)(2,1)}, u32[]{:S(2)}, u32[]{:S(2)}) collective-permute-start(bf16[256,512]{1,0:T(8,128)(2,1)} %edge.7), channel_id=1, source_target_pairs={{2,4},{3,5},{4,2},{5,3},{10,12},{11,13},{12,10},{13,11},{18,20},{1... | collective-permute-start | bytes 786440 | tf_op jit(solution)/shard_map/ppermute | solution.py:698
  26.2 10.3 %copy-start.7 = (s32[1,1,2]{2,1,0:T(1,128)S(1)}, s32[1,1,2]{2,1,0:T(1,128)}, u32[]{:S(2)}) copy-start(s32[1,1,2]{2,1,0:T(1,128)} %param.18) | copy-start | bytes 28
  26.2 18.2 %collective-permute-start.4 = (bf16[192,512]{1,0:T(8,128)(2,1)S(1)}, bf16[192,512]{1,0:T(8,128)(2,1)S(1)}, u32[]{:S(2)}, u32[]{:S(2)}) collective-permute-start(bf16[192,512]{1,0:T(8,128)(2,1)S(1)} %pair_lyrics.3.refs_0_), channel_id=1, source_target_pairs={{0,4},{1,5},{2,6},{3,7},{4,0},{5,1},{6,2},{7,3},{8,12},{9,13},{10,... | collective-permute-start | bytes 589832 | tf_op jit(solution)/shard_map/ppermute | solution.py:698
  35.3 30.7 %collective-permute-start.3 = (bf16[448,512]{1,0:T(8,128)(2,1)}, bf16[448,512]{1,0:T(8,128)(2,1)}, u32[]{:S(2)}, u32[]{:S(2)}) collective-permute-start(bf16[448,512]{1,0:T(8,128)(2,1)} %edge.4), channel_id=1, source_target_pairs={{0,2},{1,3},{2,0},{3,1},{4,6},{5,7},{6,4},{7,5},{8,10},{9,11},{10,... | collective-permute-start | bytes 1376264 | tf_op jit(solution)/shard_map/ppermute | solution.py:698
  39.5 6.4 %copy-start.2 = (bf16[1,128,2048]{2,1,0:T(8,128)(2,1)S(1)}, bf16[1,128,2048]{2,1,0:T(8,128)(2,1)}, u32[]{:S(2)}) copy-start(bf16[1,128,2048]{2,1,0:T(8,128)(2,1)} %param.10) | copy-start | bytes 1572868
  39.5 6.4 %copy-start.3 = (bf16[1,128,2048]{2,1,0:T(8,128)(2,1)S(1)}, bf16[1,128,2048]{2,1,0:T(8,128)(2,1)}, u32[]{:S(2)}) copy-start(bf16[1,128,2048]{2,1,0:T(8,128)(2,1)} %param.17) | copy-start | bytes 1572868
  45.1 20.9 %collective-permute-start.5 = (bf16[256,512]{1,0:T(8,128)(2,1)S(1)}, bf16[256,512]{1,0:T(8,128)(2,1)S(1)}, u32[]{:S(2)}, u32[]{:S(2)}) collective-permute-start(bf16[256,512]{1,0:T(8,128)(2,1)S(1)} %edge.5), channel_id=1, source_target_pairs={{2,4},{3,5},{4,2},{5,3},{10,12},{11,13},{12,10},{13,11},{18,20},{1... | collective-permute-start | bytes 786440 | tf_op jit(solution)/shard_map/ppermute | solution.py:698
  51.1 7.9 %collective-permute-start.9 = (bf16[192,512]{1,0:T(8,128)(2,1)S(1)}, bf16[192,512]{1,0:T(8,128)(2,1)S(1)}, u32[]{:S(2)}, u32[]{:S(2)}) collective-permute-start(bf16[192,512]{1,0:T(8,128)(2,1)S(1)} %get-tuple-element.49), channel_id=1, source_target_pairs={{0,2},{1,3},{2,0},{3,1},{4,6},{5,7},{6,4},{7,5},{8,10},{9,11},{10,... | collective-permute-start | bytes 589832 | tf_op jit(solution)/shard_map/ppermute | solution.py:698
  52.4 12.9 %collective-permute-start.6 = (bf16[192,512]{1,0:T(8,128)(2,1)S(1)}, bf16[192,512]{1,0:T(8,128)(2,1)S(1)}, u32[]{:S(2)}, u32[]{:S(2)}) collective-permute-start(bf16[192,512]{1,0:T(8,128)(2,1)S(1)} %collective-permute-done.4.refs_0_.refs_1_), channel_id=1, source_target_pairs={{0,2},{1,3},{2,0},{3,1},{4,6},{5,7},{6,4},{7,5},{8,10},{9,11},{10,... | collective-permute-start | bytes 589832 | tf_op jit(solution)/shard_map/ppermute | solution.py:698
  53.2 24.2 %collective-permute-start.14 = (bf16[448,512]{1,0:T(8,128)(2,1)S(1)}, bf16[448,512]{1,0:T(8,128)(2,1)S(1)}, u32[]{:S(2)}, u32[]{:S(2)}) collective-permute-start(bf16[448,512]{1,0:T(8,128)(2,1)S(1)} %get-tuple-element.52), channel_id=1, source_target_pairs={{0,2},{1,3},{2,0},{3,1},{4,6},{5,7},{6,4},{7,5},{8,10},{9,11},{10,... | collective-permute-start | bytes 1376264 | tf_op jit(solution)/shard_map/ppermute | solution.py:698
  59.0 18.3 %collective-permute-start.17 = (bf16[256,512]{1,0:T(8,128)(2,1)S(1)}, bf16[256,512]{1,0:T(8,128)(2,1)S(1)}, u32[]{:S(2)}, u32[]{:S(2)}) collective-permute-start(bf16[256,512]{1,0:T(8,128)(2,1)S(1)} %get-tuple-element.57), channel_id=1, source_target_pairs={{2,4},{3,5},{4,2},{5,3},{10,12},{11,13},{12,10},{13,11},{18,20},{1... | collective-permute-start | bytes 786440 | tf_op jit(solution)/shard_map/ppermute | solution.py:698
  65.3 12.0 %collective-permute-start.15 = (bf16[192,512]{1,0:T(8,128)(2,1)S(1)}, bf16[192,512]{1,0:T(8,128)(2,1)S(1)}, u32[]{:S(2)}, u32[]{:S(2)}) collective-permute-start(bf16[192,512]{1,0:T(8,128)(2,1)S(1)} %relay.2.refs_4_), channel_id=1, source_target_pairs={{0,4},{1,5},{2,6},{3,7},{4,0},{5,1},{6,2},{7,3},{8,12},{9,13},{10,... | collective-permute-start | bytes 589832 | tf_op jit(solution)/shard_map/ppermute | solution.py:698
  71.1 8.3 %collective-permute-start.16 = (bf16[192,512]{1,0:T(8,128)(2,1)S(1)}, bf16[192,512]{1,0:T(8,128)(2,1)S(1)}, u32[]{:S(2)}, u32[]{:S(2)}) collective-permute-start(bf16[192,512]{1,0:T(8,128)(2,1)S(1)} %get-tuple-element.55), channel_id=1, source_target_pairs={{0,2},{1,3},{2,0},{3,1},{4,6},{5,7},{6,4},{7,5},{8,10},{9,11},{10,... | collective-permute-start | bytes 589832 | tf_op jit(solution)/shard_map/ppermute | solution.py:698
  73.7 3.6 %collective-permute-start.10 = (f32[8,128]{1,0:T(8,128)S(1)}, f32[8,128]{1,0:T(8,128)S(1)}, u32[]{:S(2)}, u32[]{:S(2)}) collective-permute-start(f32[8,128]{1,0:T(8,128)S(1)} %get-tuple-element.50), channel_id=1, source_target_pairs={{0,8},{8,0},{16,24},{24,16},{1,9},{9,1},{17,25},{25,17},{2,10},{10... | collective-permute-start | bytes 12296 | tf_op jit(solution)/shard_map/ppermute | solution.py:667
  79.5 18.0 %collective-permute-start.18 = (bf16[448,512]{1,0:T(8,128)(2,1)S(1)}, bf16[448,512]{1,0:T(8,128)(2,1)S(1)}, u32[]{:S(2)}, u32[]{:S(2)}) collective-permute-start(bf16[448,512]{1,0:T(8,128)(2,1)S(1)} %get-tuple-element.58), channel_id=1, source_target_pairs={{0,2},{1,3},{2,0},{3,1},{4,6},{5,7},{6,4},{7,5},{8,10},{9,11},{10,... | collective-permute-start | bytes 1376264 | tf_op jit(solution)/shard_map/ppermute | solution.py:698
  80.6 17.8 %collective-permute-start.20 = (bf16[256,512]{1,0:T(8,128)(2,1)S(1)}, bf16[256,512]{1,0:T(8,128)(2,1)S(1)}, u32[]{:S(2)}, u32[]{:S(2)}) collective-permute-start(bf16[256,512]{1,0:T(8,128)(2,1)S(1)} %get-tuple-element.71), channel_id=1, source_target_pairs={{2,4},{3,5},{4,2},{5,3},{10,12},{11,13},{12,10},{13,11},{18,20},{1... | collective-permute-start | bytes 786440 | tf_op jit(solution)/shard_map/ppermute | solution.py:698
  81.3 16.2 %collective-permute-start.19 = (bf16[192,512]{1,0:T(8,128)(2,1)S(1)}, bf16[192,512]{1,0:T(8,128)(2,1)S(1)}, u32[]{:S(2)}, u32[]{:S(2)}) collective-permute-start(bf16[192,512]{1,0:T(8,128)(2,1)S(1)} %get-tuple-element.59), channel_id=1, source_target_pairs={{0,4},{1,5},{2,6},{3,7},{4,0},{5,1},{6,2},{7,3},{8,12},{9,13},{10,... | collective-permute-start | bytes 589832 | tf_op jit(solution)/shard_map/ppermute | solution.py:698
  85.0 3.6 %collective-permute-start.11 = (f32[8,128]{1,0:T(8,128)S(1)}, f32[8,128]{1,0:T(8,128)S(1)}, u32[]{:S(2)}, u32[]{:S(2)}) collective-permute-start(f32[8,128]{1,0:T(8,128)S(1)} %add.54.refs_4_), channel_id=1, source_target_pairs={{0,16},{8,24},{16,0},{24,8},{1,17},{9,25},{17,1},{25,9},{2,18},{10... | collective-permute-start | bytes 12296 | tf_op jit(solution)/shard_map/ppermute | solution.py:667
  88.6 4.2 %collective-permute-start.12 = (f32[8,128]{1,0:T(8,128)S(1)}, f32[8,128]{1,0:T(8,128)S(1)}, u32[]{:S(2)}, u32[]{:S(2)}) collective-permute-start(f32[8,128]{1,0:T(8,128)S(1)} %add.55), channel_id=1, source_target_pairs={{0,2},{1,3},{2,0},{3,1},{4,6},{5,7},{6,4},{7,5},{8,10},{9,11},{10,... | collective-permute-start | bytes 12296 | tf_op jit(solution)/shard_map/ppermute | solution.py:667
  92.9 4.7 %collective-permute-start.13 = (f32[8,128]{1,0:T(8,128)S(1)}, f32[8,128]{1,0:T(8,128)S(1)}, u32[]{:S(2)}, u32[]{:S(2)}) collective-permute-start(f32[8,128]{1,0:T(8,128)S(1)} %add.56), channel_id=1, source_target_pairs={{0,4},{1,5},{2,6},{3,7},{4,0},{5,1},{6,2},{7,3},{8,12},{9,13},{10,... | collective-permute-start | bytes 12296 | tf_op jit(solution)/shard_map/ppermute | solution.py:667
  100.8 3.1 %collective-permute-start.21 = (bf16[624,1024]{1,0:T(8,128)(2,1)S(1)}, bf16[624,1024]{1,0:T(8,128)(2,1)S(1)}, u32[]{:S(2)}, u32[]{:S(2)}) collective-permute-start(bf16[624,1024]{1,0:T(8,128)(2,1)S(1)} %get-tuple-element.73), channel_id=1, source_target_pairs={{0,1},{1,0},{2,3},{3,2},{4,5},{5,4},{6,7},{7,6},{8,9},{9,8},{10,11... | collective-permute-start | bytes 3833864 | tf_op jit(solution)/shard_map/ppermute | solution.py:792
